TPU v7x, 32 devices: a whole 2x2x4 slice. The times are simulated.
32 devices in a mesh: dp: 8 (over y, x, core), tensor: 4 (over z).
Axes of the slice: x: 2, y: 2, z: 4, core: 2. Of those that a mesh axis runs over, the one named last changes fastest.
Arguments:
- tokens: bfloat16 [16384, 1024], P(('dp', 'tensor')), may hold values from -6 to 6
- doc_lengths: int32 [8, 4], P('dp'), may hold values from 1 to 2048, as said below
- qkv_weight: bfloat16 [2, 3, 1024, 1024], P(None, None, 'dp', 'tensor'), may hold values from -0.1875 to 0.1875
- qv_bias: bfloat16 [2, 2, 16, 64], P(None, None, 'tensor', 'dp'), may hold values from -3 to 3
- out_weight: bfloat16 [2, 1024, 1024], P(None, 'dp', 'tensor'), may hold values from -3 to 3
- up_weight: bfloat16 [2, 1024, 4096], P(None, 'dp', 'tensor'), may hold values from -0.1875 to 0.1875
- up_bias: bfloat16 [2, 64, 64], P(None, 'tensor', 'dp'), may hold values from -3 to 3
- down_weight: bfloat16 [2, 1024, 4096], P(None, 'dp', 'tensor'), may hold values from -0.09375 to 0.09375
- gains: bfloat16 [2, 2, 1024], P(None, None, ('dp', 'tensor')), may hold values from 0.4 to 1.8
- shifts: bfloat16 [2, 4, 1024], P(None, None, ('dp', 'tensor')), may hold values from -3 to 3
- cotangent: bfloat16 [16384, 1024], P(('dp', 'tensor')), may hold values from -6 to 6
Outputs:
- layer_output: bfloat16 [16384, 1024], P(('dp', 'tensor'))
- input_grad: bfloat16 [16384, 1024], P(('dp', 'tensor'))
- qkv_grad: float32 [2, 3, 1024, 1024], P(None, None, 'dp', 'tensor')
- qv_bias_grad: float32 [2, 2, 16, 64], P(None, None, 'tensor', 'dp')
- out_grad: float32 [2, 1024, 1024], P(None, 'dp', 'tensor')
- up_grad: float32 [2, 1024, 4096], P(None, 'dp', 'tensor')
- up_bias_grad: float32 [2, 64, 64], P(None, 'tensor', 'dp')
- down_grad: float32 [2, 1024, 4096], P(None, 'dp', 'tensor')
- gains_grad: float32 [2, 2, 1024], P(None, None, ('dp', 'tensor'))
- shifts_grad: float32 [2, 4, 1024], P(None, None, ('dp', 'tensor'))
- grad_rms: float32 [], replicated
Inputs may be any that keep to these rules, and one draw needn't show every extreme that they name: `doc_lengths`: each row lists the 4 lengths of the documents packed into one sequence, in order; they sum to 2048.
All inputs are finite; a program needn't handle non-finite values.
Results may differ from a plain program's by a relative error of at most 0.035.
Values may be sent and summed in bfloat16 or wider, within the bound.
No kernel may reach another device: no remote copies, remote signals or barrier semaphores. Data moves between devices by JAX's collectives and lax.ppermute only.
A program may use at most 256 MiB of HBM per device.

v0:
```python
import jax
import jax.numpy as jnp
from jax import lax
from jax.sharding import PartitionSpec as P

D = 1024
HD = 64
FF = 4096
LAYERS = 2
SEQLEN = 2048
WINDOW = 1024


epsilon = 1e-06
neg_fill = -1000000000.0


def norm_rows(values_in, gain_row, shift_row):
    row_mean = jnp.mean(values_in, -1, keepdims=True)
    centred = values_in - row_mean
    variance = jnp.mean(centred * centred, -1, keepdims=True)
    inverse = lax.rsqrt(variance + epsilon)
    normed = centred * inverse
    return (normed * gain_row + shift_row, normed, inverse)


def norm_back(grad_rows, normed, inverse, gain_row):
    scaled = grad_rows * gain_row
    centred = (
        scaled
        - jnp.mean(scaled, -1, keepdims=True)
        - normed * jnp.mean(scaled * normed, -1, keepdims=True)
    )
    return (centred * inverse, jnp.sum(grad_rows * normed, 0), jnp.sum(grad_rows, 0))


def segments(lengths):
    doc_ends = jnp.cumsum(lengths, axis=-1)
    places = jnp.arange(SEQLEN, dtype=jnp.int32)
    return jnp.sum((places[..., :, None] >= doc_ends[..., None, :]).astype(jnp.int32), axis=-1)


def block_scores(query_block, key_seq, segment, block_index):
    block_rows = query_block.shape[0]
    row_start = block_index * block_rows
    rows_here = row_start + jnp.arange(block_rows, dtype=jnp.int32)
    places = jnp.arange(SEQLEN, dtype=jnp.int32)
    seg_here = lax.dynamic_slice_in_dim(segment, row_start, block_rows, 0)
    allowed = (seg_here[:, None] == segment[None, :]) & (
        jnp.abs(rows_here[:, None] - places[None, :]) < WINDOW
    )
    scores = jnp.einsum(
        "qhd,khd->hqk", query_block, key_seq, preferred_element_type=jnp.float32
    ) * HD ** (-0.5)
    return jnp.where(allowed[None], scores, neg_fill)


def attend_forward(queries, key_rows, value_rows, segment_ids):
    heads_here = queries.shape[1] // HD
    block_rows = min(512, SEQLEN)
    block_count = SEQLEN // block_rows
    query_blocks = queries.reshape(-1, block_count, block_rows, heads_here, HD)
    key_seqs = key_rows.reshape(-1, SEQLEN, heads_here, HD)
    value_seqs = value_rows.reshape(-1, SEQLEN, heads_here, HD)

    def one_sequence(sequence_items):
        query_seq, key_seq, value_seq, segment = sequence_items

        def one_block(block_items):
            query_block, block_index = block_items
            scores = block_scores(query_block, key_seq, segment, block_index)
            row_max = jnp.max(scores, -1, keepdims=True)
            exponent = jnp.exp(scores - row_max)
            row_total = jnp.sum(exponent, -1, keepdims=True)
            probability = (exponent / row_total).astype(jnp.bfloat16)
            context = jnp.einsum(
                "hqk,khd->qhd", probability, value_seq, preferred_element_type=jnp.float32
            )
            return (context.astype(jnp.bfloat16), (row_max + jnp.log(row_total))[..., 0])

        return lax.map(one_block, (query_seq, jnp.arange(block_count, dtype=jnp.int32)))

    context, log_sums = lax.map(one_sequence, (query_blocks, key_seqs, value_seqs, segment_ids))
    return (context.reshape(-1, heads_here * HD), log_sums)


def attend_backward(queries, key_rows, value_rows, grad_context, log_sums, segment_ids):
    heads_here = queries.shape[1] // HD
    block_rows = min(512, SEQLEN)
    block_count = SEQLEN // block_rows
    query_blocks = queries.reshape(-1, block_count, block_rows, heads_here, HD)
    grad_blocks = grad_context.reshape(-1, block_count, block_rows, heads_here, HD)
    key_seqs = key_rows.reshape(-1, SEQLEN, heads_here, HD)
    value_seqs = value_rows.reshape(-1, SEQLEN, heads_here, HD)

    def one_sequence(sequence_items):
        query_seq, key_seq, value_seq, grad_seq, sum_seq, segment = sequence_items

        def one_block(carry, block_items):
            key_total, value_total = carry
            query_block, grad_block, sum_block, block_index = block_items
            scores = block_scores(query_block, key_seq, segment, block_index)
            probability = jnp.exp(scores - sum_block[..., None])
            value_total = value_total + jnp.einsum(
                "hqk,qhd->khd",
                probability.astype(jnp.bfloat16),
                grad_block,
                preferred_element_type=jnp.float32,
            )
            grad_prob = jnp.einsum(
                "qhd,khd->hqk", grad_block, value_seq, preferred_element_type=jnp.float32
            )
            inner = jnp.sum(probability * grad_prob, -1, keepdims=True)
            grad_score = (probability * (grad_prob - inner)).astype(jnp.bfloat16)
            grad_query = jnp.einsum(
                "hqk,khd->qhd", grad_score, key_seq, preferred_element_type=jnp.float32
            ) * HD ** (-0.5)
            key_total = key_total + jnp.einsum(
                "hqk,qhd->khd", grad_score, query_block, preferred_element_type=jnp.float32
            ) * HD ** (-0.5)
            return ((key_total, value_total), grad_query)

        empty = jnp.zeros((SEQLEN, heads_here, HD), jnp.float32)
        (key_total, value_total), grad_query = lax.scan(
            one_block,
            (empty, empty),
            (query_seq, grad_seq, sum_seq, jnp.arange(block_count, dtype=jnp.int32)),
        )
        return (grad_query, key_total, value_total)

    grad_query, grad_key, grad_value = lax.map(
        one_sequence, (query_blocks, key_seqs, value_seqs, grad_blocks, log_sums, segment_ids)
    )
    local_width = heads_here * HD
    return (
        grad_query.reshape(-1, local_width),
        grad_key.reshape(-1, local_width),
        grad_value.reshape(-1, local_width),
    )


def layer_forward(hidden, pieces, segment_ids, tensor_count, data_count):
    qkv_full, qv_full, out_full, up_full, up_bias_full, down_full, vector_part = pieces
    hidden_low = hidden.astype(jnp.bfloat16)
    gathered_rows, vector_all = (
        lax.all_gather(hidden_low, "tensor", axis=0, tiled=True),
        lax.all_gather(vector_part, "tensor", axis=1, tiled=True),
    )
    vectors = (
        vector_all.reshape(6, tensor_count, data_count, -1)
        .transpose(0, 2, 1, 3)
        .reshape(6, -1)
        .astype(jnp.float32)
    )
    projected = jnp.einsum(
        "gd,cde->cge", gathered_rows, qkv_full, preferred_element_type=jnp.float32
    )
    local_width = projected.shape[2]
    qv_rows = qv_full.reshape(2, local_width).astype(jnp.float32)
    queries = (projected[0] + qv_rows[0]).astype(jnp.bfloat16)
    key_rows = projected[1].astype(jnp.bfloat16)
    value_rows = (projected[2] + qv_rows[1]).astype(jnp.bfloat16)
    context, log_sums = attend_forward(queries, key_rows, value_rows, segment_ids)
    attention = (
        lax.psum_scatter(
            lax.dot_general(
                context, out_full, (((1,), (1,)), ((), ())), preferred_element_type=jnp.float32
            ).astype(jnp.bfloat16),
            "tensor",
            scatter_dimension=0,
            tiled=True,
        ).astype(jnp.float32)
        + vectors[2]
    )
    mid_state, normed_one, inverse_one = norm_rows(hidden + attention, vectors[0], vectors[3])
    units_in = lax.all_gather(mid_state.astype(jnp.bfloat16), "tensor", axis=0, tiled=True)
    pre_act = jnp.dot(units_in, up_full, preferred_element_type=jnp.float32) + up_bias_full.reshape(
        -1
    ).astype(jnp.float32)
    active = jax.nn.gelu(pre_act, approximate=False).astype(jnp.bfloat16)
    feedforward = (
        lax.psum_scatter(
            lax.dot_general(
                active, down_full, (((1,), (1,)), ((), ())), preferred_element_type=jnp.float32
            ).astype(jnp.bfloat16),
            "tensor",
            scatter_dimension=0,
            tiled=True,
        ).astype(jnp.float32)
        + vectors[4]
    )
    output, normed_two, inverse_two = norm_rows(mid_state + feedforward, vectors[1], vectors[5])
    kept_state = (
        gathered_rows,
        queries,
        key_rows,
        value_rows,
        context,
        log_sums,
        normed_one,
        inverse_one,
        units_in,
        pre_act,
        active,
        normed_two,
        inverse_two,
        vectors,
    )
    return (output, kept_state)


def layer_backward(grad_out, pieces, kept_state, segment_ids, tensor_count, data_count):
    qkv_full, qv_full, out_full, up_full, up_bias_full, down_full, vector_part = pieces
    (
        gathered_rows,
        queries,
        key_rows,
        value_rows,
        context,
        log_sums,
        normed_one,
        inverse_one,
        units_in,
        pre_act,
        active,
        normed_two,
        inverse_two,
        vectors,
    ) = kept_state
    grad_mid, grad_gain_two, grad_shift_two = norm_back(
        grad_out, normed_two, inverse_two, vectors[1]
    )
    grad_ffn_low = grad_mid.astype(jnp.bfloat16)
    grad_down_bias = jnp.sum(grad_ffn_low.astype(jnp.float32), 0)
    grad_units = lax.all_gather(grad_ffn_low, "tensor", axis=0, tiled=True)
    grad_down = lax.dot_general(
        grad_units, active, (((0,), (0,)), ((), ())), preferred_element_type=jnp.float32
    )
    grad_active = jnp.dot(grad_units, down_full, preferred_element_type=jnp.float32)
    unused_value, gelu_pull = jax.vjp(
        lambda argument: jax.nn.gelu(argument, approximate=False), pre_act
    )
    grad_pre = gelu_pull(grad_active)[0].astype(jnp.bfloat16)
    grad_up_bias = jnp.sum(grad_pre.astype(jnp.float32), 0).reshape(up_bias_full.shape)
    grad_up = lax.dot_general(
        units_in, grad_pre, (((0,), (0,)), ((), ())), preferred_element_type=jnp.float32
    )
    grad_first = grad_mid + lax.psum_scatter(
        lax.dot_general(
            grad_pre, up_full, (((1,), (1,)), ((), ())), preferred_element_type=jnp.float32
        ).astype(jnp.bfloat16),
        "tensor",
        scatter_dimension=0,
        tiled=True,
    ).astype(jnp.float32)
    grad_attn_pre, grad_gain_one, grad_shift_one = norm_back(
        grad_first, normed_one, inverse_one, vectors[0]
    )
    grad_attn_low = grad_attn_pre.astype(jnp.bfloat16)
    grad_out_bias = jnp.sum(grad_attn_low.astype(jnp.float32), 0)
    grad_heads = lax.all_gather(grad_attn_low, "tensor", axis=0, tiled=True)
    grad_out_weight = lax.dot_general(
        grad_heads, context, (((0,), (0,)), ((), ())), preferred_element_type=jnp.float32
    )
    grad_context = jnp.dot(grad_heads, out_full, preferred_element_type=jnp.float32).astype(
        jnp.bfloat16
    )
    grad_query, grad_key, grad_value = attend_backward(
        queries, key_rows, value_rows, grad_context, log_sums, segment_ids
    )
    grad_stack = jnp.stack([grad_query, grad_key, grad_value]).astype(jnp.bfloat16)
    grad_qkv = jnp.einsum(
        "gd,cge->cde", gathered_rows, grad_stack, preferred_element_type=jnp.float32
    )
    stack_sums = jnp.sum(grad_stack.astype(jnp.float32), 1)
    grad_qv = jnp.stack([stack_sums[0], stack_sums[2]]).reshape(qv_full.shape)
    grad_in_part = jnp.einsum(
        "cge,cde->gd", grad_stack, qkv_full, preferred_element_type=jnp.float32
    )
    vector_grad = jnp.stack(
        [
            grad_gain_one,
            grad_gain_two,
            grad_out_bias,
            grad_shift_one,
            grad_down_bias,
            grad_shift_two,
        ]
    )
    vector_order = (
        vector_grad.reshape(6, data_count, tensor_count, -1).transpose(0, 2, 1, 3).reshape(6, -1)
    )
    grad_in_sum, vector_tensor = (
        lax.psum_scatter(
            grad_in_part.astype(jnp.bfloat16), "tensor", scatter_dimension=0, tiled=True
        ).astype(jnp.float32),
        lax.psum_scatter(
            vector_order.astype(jnp.bfloat16), "tensor", scatter_dimension=1, tiled=True
        ).astype(jnp.float32),
    )
    grad_input = grad_attn_pre + grad_in_sum
    return (
        grad_input,
        (grad_qkv, grad_qv, grad_out_weight, grad_up, grad_up_bias, grad_down, vector_tensor),
    )


def on_device(
    tokens,
    doc_lengths,
    qkv_weight,
    qv_bias,
    out_weight,
    up_weight,
    up_bias,
    down_weight,
    gains,
    shifts,
    cotangent,
):
    tensor_count = lax.axis_size("tensor")
    data_count = lax.axis_size("dp")
    layer_total = qkv_weight.shape[0]
    segment_ids = segments(doc_lengths)
    hidden = tokens.astype(jnp.float32)
    stored = []
    for layer_index in range(layer_total):
        pieces = (
            lax.all_gather(qkv_weight[layer_index], "dp", axis=1, tiled=True),
            lax.all_gather(qv_bias[layer_index], "dp", axis=2, tiled=True),
            lax.all_gather(out_weight[layer_index], "dp", axis=0, tiled=True),
            lax.all_gather(up_weight[layer_index], "dp", axis=0, tiled=True),
            lax.all_gather(up_bias[layer_index], "dp", axis=1, tiled=True),
            lax.all_gather(down_weight[layer_index], "dp", axis=0, tiled=True),
            lax.all_gather(
                jnp.concatenate([gains[layer_index], shifts[layer_index]], axis=0),
                "dp",
                axis=1,
                tiled=True,
            ),
        )
        hidden, kept_state = layer_forward(hidden, pieces, segment_ids, tensor_count, data_count)
        stored.append((pieces, kept_state))
    layer_output = hidden.astype(jnp.bfloat16)
    grad_hidden = cotangent.astype(jnp.float32)
    results = [None] * layer_total
    for layer_index in reversed(range(layer_total)):
        pieces, kept_state = stored[layer_index]
        pieces = (
            lax.all_gather(qkv_weight[layer_index], "dp", axis=1, tiled=True),
            lax.all_gather(qv_bias[layer_index], "dp", axis=2, tiled=True),
            lax.all_gather(out_weight[layer_index], "dp", axis=0, tiled=True),
            lax.all_gather(up_weight[layer_index], "dp", axis=0, tiled=True),
            lax.all_gather(up_bias[layer_index], "dp", axis=1, tiled=True),
            lax.all_gather(down_weight[layer_index], "dp", axis=0, tiled=True),
            lax.all_gather(
                jnp.concatenate([gains[layer_index], shifts[layer_index]], axis=0),
                "dp",
                axis=1,
                tiled=True,
            ),
        )
        grad_hidden, terms = layer_backward(
            grad_hidden, pieces, kept_state, segment_ids, tensor_count, data_count
        )
        results[layer_index] = (
            lax.psum_scatter(terms[0], "dp", scatter_dimension=1, tiled=True),
            lax.psum_scatter(terms[1], "dp", scatter_dimension=2, tiled=True),
            lax.psum_scatter(terms[2], "dp", scatter_dimension=0, tiled=True),
            lax.psum_scatter(terms[3], "dp", scatter_dimension=0, tiled=True),
            lax.psum_scatter(terms[4], "dp", scatter_dimension=1, tiled=True),
            lax.psum_scatter(terms[5], "dp", scatter_dimension=0, tiled=True),
            lax.psum_scatter(terms[6], "dp", scatter_dimension=1, tiled=True),
        )
    qkv_grad = jnp.stack([entry_set[0] for entry_set in results])
    qv_bias_grad = jnp.stack([entry_set[1] for entry_set in results])
    out_grad = jnp.stack([entry_set[2] for entry_set in results])
    up_grad = jnp.stack([entry_set[3] for entry_set in results])
    up_bias_grad = jnp.stack([entry_set[4] for entry_set in results])
    down_grad = jnp.stack([entry_set[5] for entry_set in results])
    gains_grad = jnp.stack([entry_set[6][0:2] for entry_set in results])
    shifts_grad = jnp.stack([entry_set[6][2:6] for entry_set in results])
    all_grads = (
        qkv_grad,
        qv_bias_grad,
        out_grad,
        up_grad,
        up_bias_grad,
        down_grad,
        gains_grad,
        shifts_grad,
    )
    local_squares = sum((jnp.sum(member * member) for member in all_grads))
    total_squares = lax.psum(local_squares, ("dp", "tensor"))
    entry_count = LAYERS * (4 * D * D + 2 * D * FF + FF + 8 * D)
    grad_rms = jnp.sqrt(total_squares / entry_count)
    return (
        layer_output,
        grad_hidden.astype(jnp.bfloat16),
        qkv_grad,
        qv_bias_grad,
        out_grad,
        up_grad,
        up_bias_grad,
        down_grad,
        gains_grad,
        shifts_grad,
        grad_rms,
    )


def solution(mesh):
    in_specs = (
        P(("dp", "tensor"), None),
        P("dp", None),
        P(None, None, "dp", "tensor"),
        P(None, None, "tensor", "dp"),
        P(None, "dp", "tensor"),
        P(None, "dp", "tensor"),
        P(None, "tensor", "dp"),
        P(None, "dp", "tensor"),
        P(None, None, ("dp", "tensor")),
        P(None, None, ("dp", "tensor")),
        P(("dp", "tensor"), None),
    )
    out_specs = (
        P(("dp", "tensor"), None),
        P(("dp", "tensor"), None),
        P(None, None, "dp", "tensor"),
        P(None, None, "tensor", "dp"),
        P(None, "dp", "tensor"),
        P(None, "dp", "tensor"),
        P(None, "tensor", "dp"),
        P(None, "dp", "tensor"),
        P(None, None, ("dp", "tensor")),
        P(None, None, ("dp", "tensor")),
        P(),
    )
    return jax.shard_map(
        on_device, mesh=mesh, in_specs=in_specs, out_specs=out_specs, check_vma=False
    )
```

profile of v0, /device:TPU:1, one launch (start us, length us, event | category | flops | bytes accessed | tf_op | source)
XLA Modules:
  0.0 2476.1 jit_solution(15236296140519674970)
XLA Ops:
  39.6 82.2 %all-gather.29.cloned.1.call-done = bf16[2048,1024]{1,0:T(8,128)(2,1)} async-done(((bf16[512,1024]{1,0:T(8,128)(2,1)}), bf16[2048,1024]{1,0:T(8,128)(2,1)}) %all-gather.29.cloned.1.call-update) | async-done | bytes 4194320 | tf_op jit(solution)/shard_map/all_gather | solution.py:146
  136.0 66.0 %while.94 = (s32[]{:T(128)}, bf16[4,512,4,64]{1,3,2,0:T(8,128)(2,1)}, f32[4,4,512]{2,1,0:T(4,128)S(1)}, s32[4]{0:T(128)S(1)}, s32[2048]{0:T(1024)S(1)}, /*index=...) while((s32[]{:T(128)}, ...), condition=%wide.region_5.6_spmd, body=%wide.region_2.5_spmd.sunk | while | flops 1129445888 | bytes 57231560 | solution.py:81
  234.5 50.7 %reduce-scatter.29.cloned.1.call-done = bf16[512,1024]{1,0:T(8,128)(2,1)} async-done(((bf16[2048,1024]{1,0:T(8,128)(2,1)}), bf16[512,1024]{1,0:T(8,128)(2,1)}) %reduce-scatter.29.cloned.1.call-update) | async-done | bytes 1048592 | tf_op jit(solution)/shard_map/reduce_scatter | solution.py:165
  301.4 15.1 all-gather.47.cloned.1.call-done
  316.6 82.4 %all-gather.31.cloned.1.call-done = bf16[2048,1024]{1,0:T(8,128)(2,1)} async-done(((bf16[512,1024]{1,0:T(8,128)(2,1)}), bf16[2048,1024]{1,0:T(8,128)(2,1)}) %all-gather.31.cloned.1.call-update) | async-done | bytes 4194320 | tf_op jit(solution)/shard_map/all_gather | solution.py:176
  399.0 26.3 %multiply_convert_fusion.3 = (bf16[2048,1024]{1,0:T(8,128)(2,1)}, f32[2048,1024]{1,0:T(8,128)}, f32[2048,1024]{1,0:T(8,128)}) fusion(f32[1024]{0:T(1024)S(1)} %reshape.612, bf16[2048,1024]{1,0:T(8,128)(2,1)} %all-gather.31.cloned.1.call-done, bf16[1,1024,1024]{2,1,0:T(8,128)(2,1)} %all-gather.47.cloned.1.call-done), kind=kOutput, calls=%fused_computation.129 | convolution fusion | flops 4433379328 | bytes 27267072 | tf_op jit(solution)/shard_map/dot_general | solution.py:177
  439.9 74.5 %reduce-scatter.31.cloned.1.call-done = bf16[512,1024]{1,0:T(8,128)(2,1)} async-done(((bf16[2048,1024]{1,0:T(8,128)(2,1)}), bf16[512,1024]{1,0:T(8,128)(2,1)}) %reduce-scatter.31.cloned.1.call-update) | async-done | bytes 1048592 | tf_op jit(solution)/shard_map/reduce_scatter | solution.py:182
  544.4 82.3 %all-gather.33.cloned.1.call-done = bf16[2048,1024]{1,0:T(8,128)(2,1)} async-done(((bf16[512,1024]{1,0:T(8,128)(2,1)}), bf16[2048,1024]{1,0:T(8,128)(2,1)}) %all-gather.33.cloned.1.call-update) | async-done | bytes 4194320 | tf_op jit(solution)/shard_map/all_gather | solution.py:146
  626.7 16.7 fusion.111
  651.8 65.9 %while.95 = (s32[]{:T(128)}, bf16[4,512,4,64]{1,3,2,0:T(8,128)(2,1)}, f32[4,4,512]{2,1,0:T(4,128)S(1)}, s32[4]{0:T(128)S(1)}, s32[2048]{0:T(1024)S(1)}, /*index=...) while((s32[]{:T(128)}, ...), condition=%wide.region_15.16_spmd, body=%wide.region_12.15_spmd.sunk | while | flops 1129445888 | bytes 57231560 | solution.py:81
  747.3 53.6 %reduce-scatter.33.cloned.1.call-done = bf16[512,1024]{1,0:T(8,128)(2,1)} async-done(((bf16[2048,1024]{1,0:T(8,128)(2,1)}), bf16[512,1024]{1,0:T(8,128)(2,1)}) %reduce-scatter.33.cloned.1.call-update) | async-done | bytes 1048592 | tf_op jit(solution)/shard_map/reduce_scatter | solution.py:165
  816.0 16.3 all-gather.53.cloned.1.call-done
  832.3 82.5 %all-gather.35.cloned.1.call-done = bf16[2048,1024]{1,0:T(8,128)(2,1)} async-done(((bf16[512,1024]{1,0:T(8,128)(2,1)}), bf16[2048,1024]{1,0:T(8,128)(2,1)}) %all-gather.35.cloned.1.call-update) | async-done | bytes 4194320 | tf_op jit(solution)/shard_map/all_gather | solution.py:176
  914.7 26.7 %multiply_convert_fusion.2 = (bf16[2048,1024]{1,0:T(8,128)(2,1)}, f32[2048,1024]{1,0:T(8,128)}, f32[2048,1024]{1,0:T(8,128)}) fusion(f32[1024]{0:T(1024)S(1)} %reshape.613, bf16[2048,1024]{1,0:T(8,128)(2,1)} %all-gather.35.cloned.1.call-done, bf16[1,1024,1024]{2,1,0:T(8,128)(2,1)} %all-gather.53.cloned.1.call-done), kind=kOutput, calls=%fused_computation.116 | convolution fusion | flops 4433379328 | bytes 27267072 | tf_op jit(solution)/shard_map/dot_general | solution.py:177
  954.0 76.2 %reduce-scatter.35.cloned.1.call-done = bf16[512,1024]{1,0:T(8,128)(2,1)} async-done(((bf16[2048,1024]{1,0:T(8,128)(2,1)}), bf16[512,1024]{1,0:T(8,128)(2,1)}) %reduce-scatter.35.cloned.1.call-update) | async-done | bytes 1048592 | tf_op jit(solution)/shard_map/reduce_scatter | solution.py:182
  1038.1 81.4 %all-gather.37.cloned.1.call-done = bf16[2048,1024]{1,0:T(8,128)(2,1)} async-done(((bf16[512,1024]{1,0:T(8,128)(2,1)}), bf16[2048,1024]{1,0:T(8,128)(2,1)}) %all-gather.37.cloned.1.call-update) | async-done | bytes 4194320 | tf_op jit(solution)/shard_map/all_gather | solution.py:235
  1141.9 75.4 %reduce-scatter.37.cloned.1.call-done = bf16[512,1024]{1,0:T(8,128)(2,1)} async-done(((bf16[2048,1024]{1,0:T(8,128)(2,1)}), bf16[512,1024]{1,0:T(8,128)(2,1)}) %reduce-scatter.37.cloned.1.call-update) | async-done | bytes 1048592 | tf_op jit(solution)/shard_map/reduce_scatter | solution.py:248
  1223.9 81.3 %all-gather.39.cloned.1.call-done = bf16[2048,1024]{1,0:T(8,128)(2,1)} async-done(((bf16[512,1024]{1,0:T(8,128)(2,1)}), bf16[2048,1024]{1,0:T(8,128)(2,1)}) %all-gather.39.cloned.1.call-update) | async-done | bytes 4194320 | tf_op jit(solution)/shard_map/all_gather | solution.py:261
  1316.5 192.9 %while.96 = (s32[]{:T(128)}, f32[2048,4,64]{0,2,1:T(8,128)}, f32[2048,4,64]{0,2,1:T(8,128)}, bf16[4,512,4,64]{1,3,2,0:T(8,128)(2,1)}, bf16[4,512,4,64]{1,3,2,0:T...) while((s32[]{:T(128)}, f32[2048,4,64]{0,2,1:T(8,128)}, ...), condition=%wide.region_29.30_spmd.clone, body=%wide.region_27.29_spmd.clone.sunk | while | flops 2755262976 | bytes 181250448 | solution.py:124
  1530.7 75.4 %reduce-scatter.39.cloned.1.call-done = bf16[512,1024]{1,0:T(8,128)(2,1)} async-done(((bf16[2048,1024]{1,0:T(8,128)(2,1)}), bf16[512,1024]{1,0:T(8,128)(2,1)}) %reduce-scatter.39.cloned.1.call-update) | async-done | bytes 1048592 | tf_op jit(solution)/shard_map/reduce_scatter | solution.py:294
  1611.7 81.3 %all-gather.41.cloned.1.call-done = bf16[2048,1024]{1,0:T(8,128)(2,1)} async-done(((bf16[512,1024]{1,0:T(8,128)(2,1)}), bf16[2048,1024]{1,0:T(8,128)(2,1)}) %all-gather.41.cloned.1.call-update) | async-done | bytes 4194320 | tf_op jit(solution)/shard_map/all_gather | solution.py:235
  1693.0 14.0 convert_reduce_fusion.1
  1717.7 73.3 %reduce-scatter.41.cloned.1.call-done = bf16[512,1024]{1,0:T(8,128)(2,1)} async-done(((bf16[2048,1024]{1,0:T(8,128)(2,1)}), bf16[512,1024]{1,0:T(8,128)(2,1)}) %reduce-scatter.41.cloned.1.call-update) | async-done | bytes 1048592 | tf_op jit(solution)/shard_map/reduce_scatter | solution.py:248
  1860.2 54.3 %all-gather.43.cloned.1.call-done = bf16[2048,1024]{1,0:T(8,128)(2,1)} async-done(((bf16[512,1024]{1,0:T(8,128)(2,1)}), bf16[2048,1024]{1,0:T(8,128)(2,1)}) %all-gather.43.cloned.1.call-update) | async-done | bytes 4194320 | tf_op jit(solution)/shard_map/all_gather | solution.py:261
  1938.2 199.1 %while.97 = (s32[]{:T(128)}, f32[2048,4,64]{0,2,1:T(8,128)}, f32[2048,4,64]{0,2,1:T(8,128)}, bf16[4,512,4,64]{1,3,2,0:T(8,128)(2,1)}, bf16[4,512,4,64]{1,3,2,0:T...) while((s32[]{:T(128)}, f32[2048,4,64]{0,2,1:T(8,128)}, ...), condition=%wide.region_38.39_spmd.clone, body=%wide.region_36.38_spmd.clone.sunk | while | flops 2755262976 | bytes 180988240 | solution.py:124
  2177.1 28.7 %reduce-scatter.65.cloned.1.call-done = f32[32,6]{1,0:T(8,128)} async-done(((f32[256,6]{1,0:T(8,128)}), f32[32,6]{1,0:T(8,128)}) %reduce-scatter.65.cloned.1.call-update) | async-done | bytes 784
  2212.0 20.6 all-reduce.4
  2245.7 39.6 %reduce-scatter.49.cloned.1.call-done = f32[128,256]{1,0:T(8,128)} async-done(((f32[1024,256]{1,0:T(8,128)}), f32[128,256]{1,0:T(8,128)}) %reduce-scatter.49.cloned.1.call-update) | async-done | bytes 131088 | tf_op jit(solution)/shard_map/reduce_scatter | solution.py:369
  2287.5 47.9 %reduce-scatter.47.cloned.1.call-done = f32[3,128,256]{1,2,0:T(8,128)} async-done(((f32[3,1024,256]{1,2,0:T(8,128)}), f32[3,128,256]{1,2,0:T(8,128)}) %reduce-scatter.47.cloned.1.call-update) | async-done | bytes 393232 | tf_op jit(solution)/shard_map/reduce_scatter | solution.py:367
  2335.4 49.5 %reduce-scatter.45.cloned.1.call-done = f32[3,128,256]{1,2,0:T(8,128)} async-done(((f32[3,1024,256]{1,2,0:T(8,128)}), f32[3,128,256]{1,2,0:T(8,128)}) %reduce-scatter.45.cloned.1.call-update) | async-done | bytes 393232 | tf_op jit(solution)/shard_map/reduce_scatter | solution.py:367
  2391.7 43.4 %psum.7 = f32[]{:T(128)} all-reduce(f32[]{:T(128)S(6)} %add.439), channel_id=1, replica_groups=mesh['dp'=8,'tensor'=4] {'dp','tensor'}, use_global_device_ids=true, to_apply=%region_80.81 | all-reduce | flops 1 | bytes 8 | tf_op jit(solution)/shard_map/psum | solution.py:394
  2437.0 28.2 %reduce-scatter.43.cloned.1.call-done = bf16[512,1024]{1,0:T(8,128)(2,1)} async-done(((bf16[2048,1024]{1,0:T(8,128)(2,1)}), bf16[512,1024]{1,0:T(8,128)(2,1)}) %reduce-scatter.43.cloned.1.call-update) | async-done | bytes 1048592 | tf_op jit(solution)/shard_map/reduce_scatter | solution.py:294
  (691 shorter events, 960.4 us)
Async XLA Ops:
  9.8 112.1 %all-gather.29.cloned.1.call-start = ((), (), s32[]{:S(2)}) async-start(), calls=%async_computation.20 | async-start | bytes 5242880 | tf_op jit(solution)/shard_map/all_gather | solution.py:146
  10.5 274.7 %reduce-scatter.29.cloned.1.call-start = ((), (), s32[]{:S(2)}) async-start(), calls=%async_computation.21 | async-start | bytes 5242880 | tf_op jit(solution)/shard_map/reduce_scatter | solution.py:165
  209.5 107.1 %all-gather.47.cloned.1.call-start = ((), (), s32[]{:S(2)}) async-start(), calls=%async_computation.47 | async-start | bytes 2359296 | tf_op jit(solution)/shard_map/all_gather | solution.py:332
  211.5 187.6 %all-gather.31.cloned.1.call-start = ((), (), s32[]{:S(2)}) async-start(), calls=%async_computation.22 | async-start | bytes 5242880 | tf_op jit(solution)/shard_map/all_gather | solution.py:176
  290.4 137.9 %all-gather.49.cloned.1.call-start = ((), (), s32[]{:S(2)}) async-start(), calls=%async_computation.48 | async-start | bytes 2359296 | tf_op jit(solution)/shard_map/all_gather | solution.py:334
  291.3 223.0 %reduce-scatter.31.cloned.1.call-start = ((), (), s32[]{:S(2)}) async-start(), calls=%async_computation.23 | async-start | bytes 5242880 | tf_op jit(solution)/shard_map/reduce_scatter | solution.py:182
  437.9 106.5 %all-gather.51.cloned.1.call-start = ((), (), s32[]{:S(2)}) async-start(), calls=%async_computation.49 | async-start | bytes 1769472 | tf_op jit(solution)/shard_map/all_gather | solution.py:329
  439.6 187.1 %all-gather.33.cloned.1.call-start = ((), (), s32[]{:S(2)}) async-start(), calls=%async_computation.24 | async-start | bytes 5242880 | tf_op jit(solution)/shard_map/all_gather | solution.py:146
  519.4 281.5 %reduce-scatter.33.cloned.1.call-start = ((), (), s32[]{:S(2)}) async-start(), calls=%async_computation.25 | async-start | bytes 5242880 | tf_op jit(solution)/shard_map/reduce_scatter | solution.py:165
  725.2 107.1 %all-gather.53.cloned.1.call-start = ((), (), s32[]{:S(2)}) async-start(), calls=%async_computation.50 | async-start | bytes 2359296 | tf_op jit(solution)/shard_map/all_gather | solution.py:332
  725.9 188.8 %all-gather.35.cloned.1.call-start = ((), (), s32[]{:S(2)}) async-start(), calls=%async_computation.26 | async-start | bytes 5242880 | tf_op jit(solution)/shard_map/all_gather | solution.py:176
  805.7 138.5 %all-gather.55.cloned.1.call-start = ((), (), s32[]{:S(2)}) async-start(), calls=%async_computation.51 | async-start | bytes 2359296 | tf_op jit(solution)/shard_map/all_gather | solution.py:334
  806.4 223.8 %reduce-scatter.35.cloned.1.call-start = ((), (), s32[]{:S(2)}) async-start(), calls=%async_computation.27 | async-start | bytes 5242880 | tf_op jit(solution)/shard_map/reduce_scatter | solution.py:182
  953.7 165.7 %all-gather.37.cloned.1.call-start = ((), (), s32[]{:S(2)}) async-start(), calls=%async_computation.28 | async-start | bytes 5242880 | tf_op jit(solution)/shard_map/all_gather | solution.py:235
  1038.0 179.3 %reduce-scatter.37.cloned.1.call-start = ((), (), s32[]{:S(2)}) async-start(), calls=%async_computation.29 | async-start | bytes 5242880 | tf_op jit(solution)/shard_map/reduce_scatter | solution.py:248
  1141.8 163.4 %all-gather.39.cloned.1.call-start = ((), (), s32[]{:S(2)}) async-start(), calls=%async_computation.30 | async-start | bytes 5242880 | tf_op jit(solution)/shard_map/all_gather | solution.py:261
  1223.8 382.3 %reduce-scatter.39.cloned.1.call-start = ((), (), s32[]{:S(2)}) async-start(), calls=%async_computation.31 | async-start | bytes 5242880 | tf_op jit(solution)/shard_map/reduce_scatter | solution.py:294
  1530.6 162.4 %all-gather.41.cloned.1.call-start = ((), (), s32[]{:S(2)}) async-start(), calls=%async_computation.32 | async-start | bytes 5242880 | tf_op jit(solution)/shard_map/all_gather | solution.py:235
  1611.6 179.4 %reduce-scatter.41.cloned.1.call-start = ((), (), s32[]{:S(2)}) async-start(), calls=%async_computation.33 | async-start | bytes 5242880 | tf_op jit(solution)/shard_map/reduce_scatter | solution.py:248
  1717.5 136.4 %reduce-scatter.61.cloned.1.call-start = ((), (), s32[]{:S(2)}) async-start(), calls=%async_computation.44 | async-start | bytes 20480 | tf_op jit(solution)/shard_map/reduce_scatter | solution.py:297
  1798.2 116.3 %all-gather.43.cloned.1.call-start = ((), (), s32[]{:S(2)}) async-start(), calls=%async_computation.34 | async-start | bytes 5242880 | tf_op jit(solution)/shard_map/all_gather | solution.py:261
  1798.9 368.4 %reduce-scatter.67.cloned.1.call-start = ((), (), s32[]{:S(2)}) async-start(), calls=%async_computation.53 | async-start | bytes 147456
  1812.6 358.3 %reduce-scatter.59.cloned.1.call-start = ((), (), s32[]{:S(2)}) async-start(), calls=%async_computation.43 | async-start | bytes 4718592 | tf_op jit(solution)/shard_map/reduce_scatter | solution.py:372
  1822.9 348.0 %reduce-scatter.57.cloned.1.call-start = ((), (), s32[]{:S(2)}) async-start(), calls=%async_computation.42 | async-start | bytes 4718592 | tf_op jit(solution)/shard_map/reduce_scatter | solution.py:372
  1833.0 340.9 %reduce-scatter.55.cloned.1.call-start = ((), (), s32[]{:S(2)}) async-start(), calls=%async_computation.41 | async-start | bytes 4718592 | tf_op jit(solution)/shard_map/reduce_scatter | solution.py:370
  1843.6 330.3 %reduce-scatter.53.cloned.1.call-start = ((), (), s32[]{:S(2)}) async-start(), calls=%async_computation.40 | async-start | bytes 4718592 | tf_op jit(solution)/shard_map/reduce_scatter | solution.py:370
  1853.8 352.0 %reduce-scatter.65.cloned.1.call-start = ((), (), s32[]{:S(2)}) async-start(), calls=%async_computation.52 | async-start | bytes 147456
  1855.4 390.2 %reduce-scatter.51.cloned.1.call-start = ((), (), s32[]{:S(2)}) async-start(), calls=%async_computation.39 | async-start | bytes 1179648 | tf_op jit(solution)/shard_map/reduce_scatter | solution.py:369
  1860.1 425.1 %reduce-scatter.49.cloned.1.call-start = ((), (), s32[]{:S(2)}) async-start(), calls=%async_computation.38 | async-start | bytes 1179648 | tf_op jit(solution)/shard_map/reduce_scatter | solution.py:369
  1918.9 416.5 %reduce-scatter.47.cloned.1.call-start = ((), (), s32[]{:S(2)}) async-start(), calls=%async_computation.37 | async-start | bytes 3538944 | tf_op jit(solution)/shard_map/reduce_scatter | solution.py:367
  1926.9 458.0 %reduce-scatter.45.cloned.1.call-start = ((), (), s32[]{:S(2)}) async-start(), calls=%async_computation.36 | async-start | bytes 3538944 | tf_op jit(solution)/shard_map/reduce_scatter | solution.py:367
  2158.9 306.2 %reduce-scatter.43.cloned.1.call-start = ((), (), s32[]{:S(2)}) async-start(), calls=%async_computation.35 | async-start | bytes 5242880 | tf_op jit(solution)/shard_map/reduce_scatter | solution.py:294
  (122 other events, 3944.7 us)
Sparse Core Ops, SparseCore 0:
  10.5 29.1 all-gather.44
  41.2 80.6 all-gather.28
  209.6 75.5 reduce-scatter.28
  287.7 28.7 all-gather.46
  318.6 80.3 all-gather.30
  401.5 26.8 all-gather.48
  438.0 76.3 reduce-scatter.30
  516.8 27.4 all-gather.50
  546.5 80.1 all-gather.32
  725.3 75.5 reduce-scatter.32
  803.5 28.6 all-gather.52
  834.3 80.3 all-gather.34
  917.3 26.8 all-gather.54
  953.8 76.3 reduce-scatter.34
  1038.2 81.2 all-gather.36
  1141.9 75.2 reduce-scatter.36
  1224.0 81.2 all-gather.38
  1530.7 75.3 reduce-scatter.38
  1611.7 81.2 all-gather.40
  1715.7 75.3 reduce-scatter.40
  1833.2 81.1 all-gather.42
  1918.1 31.3 reduce-scatter.66
  1952.9 51.7 reduce-scatter.58
  2008.4 51.2 reduce-scatter.56
  2062.9 51.3 reduce-scatter.54
  2118.0 51.3 reduce-scatter.52
  2172.9 32.8 reduce-scatter.64
  2209.2 36.4 reduce-scatter.50
  2249.2 36.0 reduce-scatter.48
  2289.0 46.3 reduce-scatter.46
  2338.6 46.2 reduce-scatter.44
  2387.3 77.8 reduce-scatter.42
  (2 shorter events, 34.1 us)
where the time goes:
time: 2490 us; the launch traced here: 2480 us
  waiting for transfers between devices  1370 us (55%)
  matrix products  577 us (23%)
  other arithmetic  223 us (9%)
  blocking collectives  169 us (7%)
  local copies, waits for them, and re-layouts  99.8 us (4%)
    all_gather x2, waiting for transfers between devices, layer_forward(): lax.all_gather(mid_state.astype(jnp.bfloat16), 'tensor', axis=0, tiled=True)  165 us
    all_gather x2, waiting for transfers between devices, layer_forward(): lax.all_gather(hidden_low, 'tensor', axis=0, tiled=True)  165 us
    all_gather x2, waiting for transfers between devices, layer_backward(): grad_units = lax.all_gather(grad_ffn_low, 'tensor', axis=0, tiled=True)  163 us
    reduce_scatter x2, waiting for transfers between devices, layer_forward(): lax.psum_scatter(lax.dot_general(active, down_full, (((1,), (1,)), ((), (...  151 us
    reduce_scatter x2, waiting for transfers between devices, layer_backward(): lax.psum_scatter(lax.dot_general(grad_pre, up_full, (((1,), (1,)), ((), (...  149 us
    all_gather x2, waiting for transfers between devices, layer_backward(): grad_heads = lax.all_gather(grad_attn_low, 'tensor', axis=0, tiled=True)  136 us
    reduce_scatter x2, waiting for transfers between devices, layer_forward(): lax.psum_scatter(lax.dot_general(context, out_full, (((1,), (1,)), ((), (...  104 us
    reduce_scatter x2, waiting for transfers between devices, layer_backward(): lax.psum_scatter(grad_in_part.astype(jnp.bfloat16), 'tensor', scatter_dim...  104 us
  transfers between devices with their start and end apart: 34, of which 28 were waited for; matrix products, arithmetic and copies ran while one was open for 16% of the time, Pallas kernels for 0%

commit v1 on v0

v1 whole, which is shorter than its diff:
```python
import functools

import jax
import jax.numpy as jnp
from jax import lax
from jax.experimental import pallas as pl
from jax.experimental.pallas import tpu as pltpu
from jax.sharding import Mesh
from jax.sharding import PartitionSpec as P

D = 1024
HD = 64
HEADS = 16
FF = 4096
LAYERS = 2
SEQLEN = 2048
WINDOW = 1024
EPS = 1e-06
FILL = -1000000000.0

F32 = jnp.float32
BF16 = jnp.bfloat16
GROUP = ("c", "zl")
ALL = ("zh", "zl", "q", "c")
VMEM_LIMIT = 52 * 1024 * 1024
NT = (((1,), (1,)), ((), ()))
NN = (((1,), (0,)), ((), ()))


def mm(left, right, dims=NN):
    return lax.dot_general(left, right, dims, preferred_element_type=F32)


def full(shape):
    return pl.BlockSpec(shape, lambda *_: (0,) * len(shape))


def call(body, grid, in_specs, out_specs, out_shape, scratch, args, scalars=(), flops=0, traffic=0, name=None):
    return pl.pallas_call(
        body,
        grid_spec=pltpu.PrefetchScalarGridSpec(
            num_scalar_prefetch=len(scalars),
            grid=grid,
            in_specs=in_specs,
            out_specs=out_specs,
            scratch_shapes=scratch,
        ),
        out_shape=out_shape,
        compiler_params=pltpu.CompilerParams(
            dimension_semantics=("arbitrary",) * len(grid), vmem_limit_bytes=VMEM_LIMIT
        ),
        cost_estimate=pl.CostEstimate(flops=int(flops), bytes_accessed=int(traffic), transcendentals=0),
        name=name,
    )(*scalars, *args)


def sds(shape, kind):
    return jax.ShapeDtypeStruct(shape, kind)


def norm_rows(values_in):
    centred = values_in - jnp.mean(values_in, -1, keepdims=True)
    variance = jnp.mean(centred * centred, -1, keepdims=True)
    inverse = lax.rsqrt(variance + EPS)
    return centred * inverse, inverse


def norm_back_rows(grad, normed, inverse, gain):
    scaled = grad * gain
    centred = scaled - jnp.mean(scaled, -1, keepdims=True) - normed * jnp.mean(scaled * normed, -1, keepdims=True)
    return centred * inverse


def fold_rows(values_in):
    return jnp.sum(values_in.reshape(-1, 8, values_in.shape[-1]), 0)


CHUNK = 64


def norm_forward_epilogue(acc, prev, vec, n_ref, low_ref, inv_ref):
    def step(index, carry):
        rows = pl.ds(index * CHUNK, CHUNK)
        total = prev[rows, :] * vec[0:1, :] + vec[1:2, :] + (acc[rows, :] + vec[2:3, :])
        normed, inverse = norm_rows(total)
        n_ref[rows, :] = normed
        low_ref[rows, :] = (normed * vec[3:4, :] + vec[4:5, :]).astype(BF16)
        inv_ref[rows, :] = jnp.broadcast_to(inverse, (CHUNK, 128))
        return carry

    lax.fori_loop(0, acc.shape[0] // CHUNK, step, 0)


def norm_backward_epilogue(get_grad, rows_total, n_ref, inv_ref, gain_ref, g_ref, low_ref, sums_ref):
    def step(index, carry):
        rows = pl.ds(index * CHUNK, CHUNK)
        grad = get_grad(rows)
        normed = n_ref[rows, :]
        result = norm_back_rows(grad, normed, inv_ref[rows, 0:1], gain_ref[0:1, :])
        low = result.astype(BF16)
        g_ref[rows, :] = result
        low_ref[rows, :] = low
        return (
            carry[0] + fold_rows(grad * normed),
            carry[1] + fold_rows(grad),
            carry[2] + fold_rows(low.astype(F32)),
        )

    zero = jnp.zeros((8, D), F32)
    sums = lax.fori_loop(0, rows_total // CHUNK, step, (zero, zero, zero))
    sums_ref[...] = jnp.zeros(sums_ref.shape, F32)
    for row, member in enumerate(sums):
        sums_ref[row : row + 1, :] = jnp.sum(member, 0, keepdims=True)


def project_blocks(place, rows_in, weight, bias):
    count, depth, width = weight.shape
    tokens = rows_in.shape[0]

    def body(place_ref, x_ref, w_ref, *rest):
        if bias is None:
            outs = rest
        else:
            bias_ref, outs = rest[0], rest[1:]
        step = pl.program_id(0)
        value = mm(x_ref[...], w_ref[0])
        if bias is not None:
            value = value + bias_ref[0]
        value = value.astype(BF16)
        for index, out in enumerate(outs):

            @pl.when(step == index)
            def _(out=out):
                out[...] = value

    pick = lambda r, place_ref: (place_ref[0] ^ r, 0, 0)
    specs = [full((tokens, depth)), pl.BlockSpec((1, depth, width), pick)]
    args = [rows_in, weight]
    if bias is not None:
        specs.append(pl.BlockSpec((1, 1, width), pick))
        args.append(bias)
    return call(
        body, (count,), specs, [full((tokens, width))] * count, [sds((tokens, width), BF16)] * count, [], args,
        (place,), 2 * tokens * depth * width * count, 2 * (count * depth * width + tokens * (depth + count * width)),
        name="project_blocks",
    )


def gelu_parts(u):
    size = jnp.abs(u)
    t = 1.0 / (1.0 + 0.2316419 * size)
    poly = t * (0.127414796 + t * (-0.142248368 + t * (0.7107068705 + t * (-0.7265760135 + t * 0.5307027145))))
    bell = jnp.exp(-0.5 * (u * u))
    tail = poly * bell
    cdf = jnp.where(u >= 0, 1.0 - tail, tail)
    return u * cdf, cdf + u * (0.3989422804014327 * bell)


def up_gelu(rows_in, weight, bias, block=512):
    count, depth, width = weight.shape
    tokens = rows_in.shape[0]
    per = width // block
    half = tokens // 2

    def body(x_ref, w_ref, b_ref, act_ref, slope_ref):
        for index in range(2):
            rows = slice(index * half, (index + 1) * half)
            act, slope = gelu_parts(mm(x_ref[rows, :], w_ref[0]) + b_ref[...])
            act_ref[rows, :] = act.astype(BF16)
            slope_ref[rows, :] = slope.astype(BF16)

    column = pl.BlockSpec((tokens, block), lambda j: (0, j))
    return call(
        body, (count * per,),
        [full((tokens, depth)), pl.BlockSpec((1, depth, block), lambda j: (j // per, 0, j % per)),
         pl.BlockSpec((1, block), lambda j: (0, j))],
        [column, column], [sds((tokens, count * width), BF16)] * 2, [], [rows_in, weight, bias], (),
        2 * tokens * depth * width * count, 2 * (count * depth * width + tokens * (depth + 2 * count * width)),
        name="up_gelu",
    )


def units_back(rows_in, weight, slope, block=512):
    count, depth, width = weight.shape
    tokens = rows_in.shape[0]
    per = width // block
    half = tokens // 2

    def body(x_ref, w_ref, s_ref, out_ref, sum_ref):
        total = jnp.zeros((8, block), F32)
        for index in range(2):
            rows = slice(index * half, (index + 1) * half)
            low = (mm(x_ref[rows, :], w_ref[0]) * s_ref[rows, :].astype(F32)).astype(BF16)
            out_ref[rows, :] = low
            total = total + fold_rows(low.astype(F32))
        sum_ref[...] = jnp.sum(total, 0, keepdims=True)

    column = pl.BlockSpec((tokens, block), lambda j: (0, j))
    return call(
        body, (count * per,),
        [full((tokens, depth)), pl.BlockSpec((1, depth, block), lambda j: (j // per, 0, j % per)), column],
        [column, pl.BlockSpec((1, block), lambda j: (0, j))],
        [sds((tokens, count * width), BF16), sds((1, count * width), F32)], [], [rows_in, weight, slope], (),
        2 * tokens * depth * width * count, 2 * (count * depth * width + tokens * (depth + 2 * count * width)),
        name="units_back",
    )


def contract_blocks(place, left, weight, extra, extra_specs, out_specs, out_shape, finish, name):
    count, depth, width = weight.shape
    listed = isinstance(left, (list, tuple))
    lefts = list(left) if listed else [left]
    tokens = lefts[0].shape[0]

    def body(place_ref, *refs):
        left_refs = refs[: len(lefts)]
        w_ref = refs[len(lefts)]
        extra_refs = refs[len(lefts) + 1 : len(lefts) + 1 + len(extra)]
        out_refs = refs[len(lefts) + 1 + len(extra) : -1]
        acc = refs[-1]
        step = pl.program_id(0)
        if listed:
            for index, left_ref in enumerate(left_refs):

                @pl.when(step == index)
                def _(left_ref=left_ref, index=index):
                    value = mm(left_ref[...], w_ref[0], NT)
                    acc[...] = value if index == 0 else acc[...] + value

        else:

            @pl.when(step == 0)
            def _():
                acc[...] = mm(left_refs[0][...], w_ref[0], NT)

            @pl.when(step != 0)
            def _():
                acc[...] += mm(left_refs[0][...], w_ref[0], NT)

        @pl.when(step == count - 1)
        def _():
            finish(acc, extra_refs, out_refs)

    if listed:
        left_specs = [full((tokens, width))] * len(lefts)
        pick = lambda r, place_ref: (place_ref[0] ^ r, 0, 0)
    else:
        left_specs = [pl.BlockSpec((tokens, width), lambda r, place_ref: (0, r))]
        pick = lambda r, place_ref: (r, 0, 0)
    return call(
        body, (count,), left_specs + [pl.BlockSpec((1, depth, width), pick)] + extra_specs, out_specs, out_shape,
        [pltpu.VMEM((tokens, depth), F32)], lefts + [weight] + extra, (place,),
        2 * tokens * depth * width * count, 2 * (count * depth * width + tokens * (4 * depth + count * width)),
        name=name,
    )


def sublayer_norm(place, left, weight, prev, vec, name):
    tokens = prev.shape[0]

    def finish(acc, extra, outs):
        norm_forward_epilogue(acc, extra[0], extra[1], outs[0], outs[1], outs[2])

    return contract_blocks(
        place, left, weight, [prev, vec], [full((tokens, D)), full((8, D))],
        [full((tokens, D)), full((tokens, D)), full((tokens, 128))],
        [sds((tokens, D), F32), sds((tokens, D), BF16), sds((tokens, 128), F32)], finish, name,
    )


def sublayer_norm_back(place, left, weight, residual, normed, inverse, gain, name):
    tokens = residual.shape[0]

    def finish(acc, extra, outs):
        norm_backward_epilogue(
            lambda rows: extra[0][rows, :] + acc[rows, :], tokens, extra[1], extra[2], extra[3], outs[0], outs[1], outs[2]
        )

    return contract_blocks(
        place, left, weight, [residual, normed, inverse, gain],
        [full((tokens, D)), full((tokens, D)), full((tokens, 128)), full((8, D))],
        [full((tokens, D)), full((tokens, D)), full((8, D))],
        [sds((tokens, D), F32), sds((tokens, D), BF16), sds((8, D), F32)], finish, name,
    )


def sublayer_back_last(place, left, weight, residual, name):
    tokens = residual.shape[0]

    def finish(acc, extra, outs):
        outs[0][...] = (extra[0][...] + acc[...]).astype(BF16)

    return contract_blocks(
        place, left, weight, [residual], [full((tokens, D))], [full((tokens, D))], [sds((tokens, D), BF16)], finish, name
    )[0]


def norm_back(grad, normed, inverse, gain):
    tokens = grad.shape[0]

    def body(grad_ref, n_ref, inv_ref, gain_ref, g_ref, low_ref, sums_ref):
        norm_backward_epilogue(
            lambda rows: grad_ref[rows, :].astype(F32), tokens, n_ref, inv_ref, gain_ref, g_ref, low_ref, sums_ref
        )

    return call(
        body, (1,), [full((tokens, D)), full((tokens, D)), full((tokens, 128)), full((8, D))],
        [full((tokens, D)), full((tokens, D)), full((8, D))],
        [sds((tokens, D), F32), sds((tokens, D), BF16), sds((8, D), F32)], [], [grad, normed, inverse, gain], (),
        20 * tokens * D, 12 * tokens * D, name="norm_back",
    )


def weight_grad(left, right, count, block=512):
    tokens, depth = left.shape
    width = right.shape[1] // count
    per = width // block

    def body(x_ref, y_ref, out_ref, turned):
        @pl.when(pl.program_id(0) == 0)
        def _():
            turned[...] = x_ref[...].T

        out_ref[0] = mm(turned[...], y_ref[...]).astype(BF16)

    return call(
        body, (count * per,), [full((tokens, depth)), pl.BlockSpec((tokens, block), lambda j: (0, j))],
        pl.BlockSpec((1, depth, block), lambda j: (j // per, 0, j % per)), sds((count, depth, width), BF16),
        [pltpu.VMEM((depth, tokens), BF16)], [left, right], (),
        2 * tokens * depth * width * count, 2 * (count * depth * width + tokens * (depth + count * width)),
        name="weight_grad",
    )


def weight_grad_blocks(place, left, rights, with_sums):
    tokens, depth = left.shape
    count = len(rights)
    width = rights[0].shape[1]

    def body(place_ref, x_ref, *refs):
        parts = refs[:count]
        if with_sums:
            out_ref, sum_ref, turned = refs[count:]
        else:
            out_ref, turned = refs[count:]
        step = pl.program_id(0)

        @pl.when(step == 0)
        def _():
            turned[...] = x_ref[...].T

        for index, part in enumerate(parts):

            @pl.when(step == index)
            def _(part=part):
                out_ref[0] = mm(turned[...], part[...]).astype(BF16)
                if with_sums:
                    sum_ref[0] = jnp.sum(part[...].astype(F32), 0, keepdims=True)

    pick = lambda r, place_ref: (place_ref[0] ^ r, 0, 0)
    out_specs = [pl.BlockSpec((1, depth, width), pick)]
    out_shape = [sds((count, depth, width), BF16)]
    if with_sums:
        out_specs.append(pl.BlockSpec((1, 1, width), pick))
        out_shape.append(sds((count, 1, width), F32))
    return call(
        body, (count,), [full((tokens, depth))] + [full((tokens, width))] * count, out_specs, out_shape,
        [pltpu.VMEM((depth, tokens), BF16)], [left] + list(rights), (place,),
        2 * tokens * depth * width * count, 2 * (count * depth * width + tokens * (depth + count * width)),
        name="weight_grad_blocks",
    )


BQ = 256


def reach(ends_ref, row):
    first = jnp.zeros_like(row)
    for index in range(3):
        first = jnp.where(row >= ends_ref[index], ends_ref[index], first)
    last = jnp.full_like(row, SEQLEN)
    for index in (2, 1, 0):
        last = jnp.where(row < ends_ref[index], ends_ref[index], last)
    return jnp.maximum(first, row - (WINDOW - 1)), jnp.minimum(last, row + WINDOW)


def block_reach(ends_ref, start):
    low_first, high_first = reach(ends_ref, start)
    low_last, high_last = reach(ends_ref, start + BQ - 1)
    return low_first, low_last, high_first, high_last


def row_reach(ends_ref, start):
    return reach(ends_ref, start + lax.broadcasted_iota(jnp.int32, (1, BQ), 1))


def attend_forward(place, ends, parts):
    count = len(parts)
    chunk, width3 = parts[0].shape
    width = width3 // 3
    heads = width // HD
    steps = SEQLEN // BQ
    per = chunk // BQ

    def body(place_ref, ends_ref, *refs):
        part_refs = refs[:count]
        ctx_refs = refs[count : 2 * count]
        wide_ref, lse_ref = refs[2 * count : 2 * count + 2]
        qh, kh, vt, acc, stat, stage = refs[2 * count + 2 :]
        step = pl.program_id(0)
        me = place_ref[0]

        @pl.when(step == 0)
        def _():
            for r in range(count):
                j = me ^ r
                rows = pl.ds(pl.multiple_of(j * chunk, chunk), chunk)
                for h in range(heads):
                    cols = slice(h * HD, (h + 1) * HD)
                    qh[h, rows, :] = part_refs[r][:, cols] * BF16(HD**-0.5)
                    kh[h, rows, :] = part_refs[r][:, width + h * HD : width + (h + 1) * HD]
                vt[j] = part_refs[r][:, 2 * width :].T

        start = step * BQ
        low_first, low_last, high_first, high_last = block_reach(ends_ref, start)
        low_row, high_row = row_reach(ends_ref, start)
        rows = pl.ds(pl.multiple_of(start, BQ), BQ)
        acc[...] = jnp.zeros(acc.shape, F32)
        stat[0:heads, :] = jnp.full((heads, BQ), -3.0e38, F32)
        stat[heads : 2 * heads, :] = jnp.zeros((heads, BQ), F32)

        def block(b, masked):
            keys = pl.ds(pl.multiple_of(b * chunk, chunk), chunk)
            if masked:
                place_of = b * chunk + lax.broadcasted_iota(jnp.int32, (chunk, BQ), 0)
                allowed = (place_of >= low_row) & (place_of < high_row)
            for h in range(heads):
                score = mm(kh[h, keys, :], qh[h, rows, :], NT)
                if masked:
                    score = jnp.where(allowed, score, FILL)
                old = stat[h : h + 1, :]
                new = jnp.maximum(old, jnp.max(score, 0, keepdims=True))
                weight = jnp.exp(score - new)
                decay = jnp.exp(old - new)
                stat[h : h + 1, :] = new
                stat[heads + h : heads + h + 1, :] = stat[heads + h : heads + h + 1, :] * decay + jnp.sum(
                    weight, 0, keepdims=True
                )
                part = slice(h * HD, (h + 1) * HD)
                acc[part, :] = acc[part, :] * decay + mm(vt[b, part, :], weight.astype(BF16))

        def one(b, carry):
            open_all = (b * chunk >= low_last) & ((b + 1) * chunk <= high_first)

            @pl.when(open_all)
            def _():
                block(b, False)

            @pl.when(jnp.logical_not(open_all))
            def _():
                block(b, True)

            return carry

        lax.fori_loop(low_first // chunk, (high_last + chunk - 1) // chunk, one, 0)
        for h in range(heads):
            part = slice(h * HD, (h + 1) * HD)
            total = stat[heads + h : heads + h + 1, :]
            wide_ref[part, :] = acc[part, :] / total
            lse_ref[h : h + 1, :] = stat[h : h + 1, :] + jnp.log(total)
        lse_ref[heads:, :] = jnp.zeros((8 - heads, BQ), F32)
        stage[step // per, pl.ds(pl.multiple_of((step % per) * BQ, BQ), BQ), :] = wide_ref[...].T.astype(BF16)

        @pl.when(step == steps - 1)
        def _():
            for r in range(count):
                ctx_refs[r][...] = stage[me ^ r]

    pairs = SEQLEN * SEQLEN
    return call(
        body, (steps,), [full((chunk, width3))] * count,
        [full((chunk, width))] * count
        + [pl.BlockSpec((width, BQ), lambda i, *_: (0, i)), pl.BlockSpec((8, BQ), lambda i, *_: (0, i))],
        [sds((chunk, width), BF16)] * count + [sds((width, SEQLEN), F32), sds((8, SEQLEN), F32)],
        [
            pltpu.VMEM((heads, SEQLEN, HD), BF16),
            pltpu.VMEM((heads, SEQLEN, HD), BF16),
            pltpu.VMEM((count, width, chunk), BF16),
            pltpu.VMEM((width, BQ), F32),
            pltpu.VMEM((2 * heads, BQ), F32),
            pltpu.VMEM((count, chunk, width), BF16),
        ],
        list(parts), (place, ends), 6 * pairs * heads * HD, 6 * SEQLEN * width * 2, name="attend_forward",
    )


def attend_backward(place, ends, parts, grads, wide, lse):
    count = len(parts)
    chunk, width3 = parts[0].shape
    width = width3 // 3
    heads = width // HD
    steps = SEQLEN // BQ
    per = chunk // BQ

    def body(place_ref, ends_ref, *refs):
        part_refs = refs[:count]
        grad_refs = refs[count : 2 * count]
        wide_ref, lse_ref = refs[2 * count : 2 * count + 2]
        out_refs = refs[2 * count + 2 : 3 * count + 2]
        qh, kh, vh, gh, kt, qt, gt, gq, gk, gv, stage = refs[3 * count + 2 :]
        step = pl.program_id(0)
        me = place_ref[0]

        @pl.when(step == 0)
        def _():
            for r in range(count):
                j = me ^ r
                rows = pl.ds(pl.multiple_of(j * chunk, chunk), chunk)
                for h in range(heads):
                    cols = slice(h * HD, (h + 1) * HD)
                    qh[h, rows, :] = part_refs[r][:, cols] * BF16(HD**-0.5)
                    kh[h, rows, :] = part_refs[r][:, width + h * HD : width + (h + 1) * HD]
                    vh[h, rows, :] = part_refs[r][:, 2 * width + h * HD : 2 * width + (h + 1) * HD]
                    gh[h, rows, :] = grad_refs[r][:, cols]
                kt[j] = part_refs[r][:, width : 2 * width].T
                for s in range(per):
                    sub = slice(s * BQ, (s + 1) * BQ)
                    qt[j * per + s] = (part_refs[r][sub, :width] * BF16(HD**-0.5)).T
                    gt[j * per + s] = grad_refs[r][sub, :].T
            gk[...] = jnp.zeros(gk.shape, F32)
            gv[...] = jnp.zeros(gv.shape, F32)

        start = step * BQ
        low_first, low_last, high_first, high_last = block_reach(ends_ref, start)
        low_row, high_row = row_reach(ends_ref, start)
        rows = pl.ds(pl.multiple_of(start, BQ), BQ)
        gq[...] = jnp.zeros(gq.shape, F32)
        inner = []
        for h in range(heads):
            part = slice(h * HD, (h + 1) * HD)
            inner.append(jnp.sum(gt[step, part, :].astype(F32) * wide_ref[part, :], 0, keepdims=True))

        def block(b, masked):
            keys = pl.ds(pl.multiple_of(b * chunk, chunk), chunk)
            if masked:
                place_of = b * chunk + lax.broadcasted_iota(jnp.int32, (chunk, BQ), 0)
                allowed = (place_of >= low_row) & (place_of < high_row)
            for h in range(heads):
                part = slice(h * HD, (h + 1) * HD)
                score = mm(kh[h, keys, :], qh[h, rows, :], NT)
                if masked:
                    score = jnp.where(allowed, score, FILL)
                weight = jnp.exp(score - lse_ref[h : h + 1, :])
                grad_weight = mm(vh[h, keys, :], gh[h, rows, :], NT)
                grad_score = (weight * (grad_weight - inner[h])).astype(BF16)
                gv[b, part, :] += mm(gt[step, part, :], weight.astype(BF16), NT)
                gk[b, part, :] += mm(qt[step, part, :], grad_score, NT)
                gq[part, :] += mm(kt[b, part, :], grad_score)

        def one(b, carry):
            open_all = (b * chunk >= low_last) & ((b + 1) * chunk <= high_first)

            @pl.when(open_all)
            def _():
                block(b, False)

            @pl.when(jnp.logical_not(open_all))
            def _():
                block(b, True)

            return carry

        lax.fori_loop(low_first // chunk, (high_last + chunk - 1) // chunk, one, 0)
        stage[step // per, pl.ds(pl.multiple_of((step % per) * BQ, BQ), BQ), :] = (gq[...] * HD**-0.5).T.astype(BF16)

        @pl.when(step == steps - 1)
        def _():
            for r in range(count):
                j = me ^ r
                out_refs[r][:, :width] = stage[j]
                out_refs[r][:, width : 2 * width] = gk[j].T.astype(BF16)
                out_refs[r][:, 2 * width :] = gv[j].T.astype(BF16)

    pairs = SEQLEN * SEQLEN
    return call(
        body, (steps,),
        [full((chunk, width3))] * count + [full((chunk, width))] * count
        + [pl.BlockSpec((width, BQ), lambda i, *_: (0, i)), pl.BlockSpec((8, BQ), lambda i, *_: (0, i))],
        [full((chunk, width3))] * count, [sds((chunk, width3), BF16)] * count,
        [pltpu.VMEM((heads, SEQLEN, HD), BF16)] * 4
        + [
            pltpu.VMEM((count, width, chunk), BF16),
            pltpu.VMEM((steps, width, BQ), BF16),
            pltpu.VMEM((steps, width, BQ), BF16),
            pltpu.VMEM((width, BQ), F32),
            pltpu.VMEM((count, width, chunk), F32),
            pltpu.VMEM((count, width, chunk), F32),
            pltpu.VMEM((count, chunk, width), BF16),
        ],
        list(parts) + list(grads) + [wide, lse], (place, ends), 14 * pairs * heads * HD, 20 * SEQLEN * width,
        name="attend_backward",
    )


def regroup(values_in):
    count = lax.axis_size("zh")
    perm = [(a * count + b, b * count + a) for a in range(count) for b in range(count)]
    return lax.ppermute(values_in, ("c", "zh"), perm)


def swap_members(parts):
    count = len(parts)
    out = [parts[0]]
    for r in range(1, count):
        out.append(lax.ppermute(parts[r], GROUP, [(a, a ^ r) for a in range(count)]))
    return out


def gather_blocks(shard):
    members = lax.axis_size("zh") * lax.axis_size("zl")
    gathered = lax.all_gather(shard, ALL, axis=0, tiled=True)
    return gathered.reshape(members, -1, shard.shape[1])


def scatter_sum(blocks):
    return lax.psum_scatter(blocks.reshape(-1, blocks.shape[2]), ALL, scatter_dimension=0, tiled=True).astype(F32)


def on_device(
    tokens, doc_lengths, qkv_weight, qv_bias, out_weight, up_weight, up_bias, down_weight, gains, shifts, cotangent
):
    layers = qkv_weight.shape[0]
    tz = lax.axis_size("zh") * lax.axis_size("zl")
    dp = lax.axis_size("q") * lax.axis_size("c")
    place = lax.axis_index(GROUP).astype(jnp.int32).reshape(1)

    x_low = regroup(tokens)
    lengths = regroup(doc_lengths)
    ends = jnp.cumsum(lengths[0], dtype=jnp.int32)

    pieces = [qv_bias, up_bias, gains, shifts]
    sizes = [piece.size // layers for piece in pieces]
    small = jnp.concatenate([piece.reshape(layers, -1) for piece in pieces], axis=1)
    small_all = lax.all_gather(small, ALL, axis=0, tiled=False).reshape(tz, dp, layers, -1).astype(F32)
    cuts = [0]
    for size in sizes:
        cuts.append(cuts[-1] + size)
    parts = [small_all[..., cuts[i] : cuts[i + 1]] for i in range(4)]
    hz = qv_bias.shape[2]
    qv_full = parts[0].reshape(tz, dp, layers, 2, hz, -1).transpose(2, 3, 0, 4, 1, 5).reshape(layers, 2, tz, -1)
    bias_qkv = jnp.stack([qv_full[:, 0], jnp.zeros_like(qv_full[:, 0]), qv_full[:, 1]], axis=2)
    bias_qkv = bias_qkv.reshape(layers, tz, 1, -1)
    up_bias_full = (
        parts[1].reshape(tz, dp, layers, up_bias.shape[1], -1).transpose(2, 0, 3, 1, 4).reshape(layers, 1, FF)
    )
    gain_full = parts[2].reshape(tz, dp, layers, 2, -1).transpose(2, 3, 1, 0, 4).reshape(layers, 2, D)
    shift_full = parts[3].reshape(tz, dp, layers, 4, -1).transpose(2, 3, 1, 0, 4).reshape(layers, 4, D)

    weights = []
    for l in range(layers):
        qkv_cols = qkv_weight[l].transpose(1, 0, 2).reshape(qkv_weight.shape[2], -1)
        weights.append(
            (
                gather_blocks(qkv_cols),
                gather_blocks(out_weight[l]),
                gather_blocks(up_weight[l]),
                gather_blocks(down_weight[l]),
            )
        )
    grad_rows = regroup(cotangent)

    one, zero = jnp.ones((D,), F32), jnp.zeros((D,), F32)
    pad = [zero, zero, zero]
    prev = tokens_wide = x_low.astype(F32)
    prev_gain, prev_shift = one, zero
    kept = []
    for l in range(layers):
        w_qkv, w_out, w_up, w_down = weights[l]
        qkv = swap_members(project_blocks(place, x_low, w_qkv, bias_qkv[l]))
        *ctx, wide, lse = attend_forward(place, ends, qkv)
        ctx = swap_members(ctx)
        vec = jnp.stack([prev_gain, prev_shift, shift_full[l, 0], gain_full[l, 0], shift_full[l, 1]] + pad)
        n1, hs, r1 = sublayer_norm(place, ctx, w_out, prev, vec, "out_norm")
        act, slope = up_gelu(hs, w_up, up_bias_full[l])
        vec = jnp.stack([gain_full[l, 0], shift_full[l, 1], shift_full[l, 2], gain_full[l, 1], shift_full[l, 3]] + pad)
        n2, y_low, r2 = sublayer_norm(place, act, w_down, n1, vec, "down_norm")
        kept.append((x_low, qkv, ctx, wide, lse, n1, hs, r1, act, slope, n2, r2))
        x_low, prev, prev_gain, prev_shift = y_low, n2, gain_full[l, 1], shift_full[l, 3]
    layer_output = regroup(x_low)

    gain_rows = [[jnp.broadcast_to(gain_full[l, i], (8, D)) for i in range(2)] for l in range(layers)]
    g2, gf, sums2 = norm_back(grad_rows, kept[-1][10], kept[-1][11], gain_rows[-1][1])
    results = [None] * layers
    small_grads = [None] * layers
    for l in reversed(range(layers)):
        w_qkv, w_out, w_up, w_down = weights[l]
        x_in, qkv, ctx, wide, lse, n1, hs, r1, act, slope, n2, r2 = kept[l]
        gu, up_bias_sum = units_back(gf, w_down, slope)
        d_down = scatter_sum(weight_grad(gf, act, tz))
        g1, ga, sums1 = sublayer_norm_back(place, gu, w_up, g2, n1, r1, gain_rows[l][0], "up_back")
        d_up = scatter_sum(weight_grad(hs, gu, tz))
        gc = swap_members(project_blocks(place, ga, w_out, None))
        d_out = scatter_sum(weight_grad_blocks(place, ga, ctx, False)[0])
        gqkv = swap_members(attend_backward(place, ends, qkv, gc, wide, lse))
        d_qkv, qkv_sums = weight_grad_blocks(place, x_in, gqkv, True)
        d_qkv = scatter_sum(d_qkv)
        qv_sums = qkv_sums.reshape(tz, 3, hz, dp, -1)
        pieces = [
            jnp.stack([qv_sums[:, 0], qv_sums[:, 2]], axis=1).transpose(0, 3, 1, 2, 4).reshape(tz, dp, -1),
            up_bias_sum.reshape(tz, up_bias.shape[1], dp, -1).transpose(0, 2, 1, 3).reshape(tz, dp, -1),
            jnp.stack([sums1[0], sums2[0]]).reshape(2, dp, tz, -1).transpose(2, 1, 0, 3).reshape(tz, dp, -1),
            jnp.stack([sums1[2], sums1[1], sums2[2], sums2[1]])
            .reshape(4, dp, tz, -1)
            .transpose(2, 1, 0, 3)
            .reshape(tz, dp, -1),
        ]
        small_grads[l] = jnp.concatenate(pieces, axis=-1)
        if l > 0:
            g2, gf, sums2 = sublayer_norm_back(
                place, gqkv, w_qkv, g1, kept[l - 1][10], kept[l - 1][11], gain_rows[l - 1][1], "qkv_back"
            )
        else:
            input_grad = regroup(sublayer_back_last(place, gqkv, w_qkv, g1, "qkv_back"))
        results[l] = (d_qkv.reshape(d_qkv.shape[0], 3, -1).transpose(1, 0, 2), d_out, d_up, d_down)

    small_out = lax.psum_scatter(
        jnp.stack(small_grads, axis=2).reshape(tz * dp, -1), ALL, scatter_dimension=0, tiled=True
    ).reshape(layers, -1)
    qkv_grad, out_grad, up_grad, down_grad = (jnp.stack([entry[i] for entry in results]) for i in range(4))
    qv_bias_grad = small_out[:, cuts[0] : cuts[1]].reshape(qv_bias.shape)
    up_bias_grad = small_out[:, cuts[1] : cuts[2]].reshape(up_bias.shape)
    gains_grad = small_out[:, cuts[2] : cuts[3]].reshape(gains.shape)
    shifts_grad = small_out[:, cuts[3] : cuts[4]].reshape(shifts.shape)
    all_grads = (qkv_grad, qv_bias_grad, out_grad, up_grad, up_bias_grad, down_grad, gains_grad, shifts_grad)
    local_squares = sum(jnp.sum(member * member) for member in all_grads)
    entry_count = LAYERS * (4 * D * D + 2 * D * FF + FF + 8 * D)
    grad_rms = jnp.sqrt(lax.psum(local_squares, ALL) / entry_count)
    return (
        layer_output, input_grad, qkv_grad, qv_bias_grad, out_grad, up_grad, up_bias_grad, down_grad, gains_grad,
        shifts_grad, grad_rms,
    )


def solution(mesh):
    dp, tensor = mesh.shape["dp"], mesh.shape["tensor"]
    fine = Mesh(mesh.devices.reshape(dp // 2, 2, 2, tensor // 2), ("q", "c", "zh", "zl"))
    data, model = ("q", "c"), ("zh", "zl")
    both = data + model
    weight3, weight4 = P(None, data, model), P(None, None, data, model)
    in_specs = (
        P(both, None), P(data, None), weight4, P(None, None, model, data), weight3, weight3, P(None, model, data),
        weight3, P(None, None, both), P(None, None, both), P(both, None),
    )
    out_specs = (
        P(both, None), P(both, None), weight4, P(None, None, model, data), weight3, weight3, P(None, model, data),
        weight3, P(None, None, both), P(None, None, both), P(),
    )
    return jax.shard_map(on_device, mesh=fine, in_specs=in_specs, out_specs=out_specs, check_vma=False)
```

time: 2490 us -> 2260 us (0.908)
  matrix products: 577 us -> 0 us
  Pallas kernels: 0 us -> 448 us
  other arithmetic: 223 us -> 14.9 us
  waiting for transfers between devices: 1370 us -> 1570 us
  blocking collectives: 169 us -> 86.1 us
  starting transfers between devices: 2.26 us -> 35.6 us
  local copies, waits for them, and re-layouts: 99.8 us -> 66.8 us
    dot_general x80 -> x0, matrix products: 577 us -> none  [the longest x8 93.2 us: one_block(): jnp.einsum('qhd,khd->hqk', grad_block, value_seq, preferred_element_type=...]
    pallas_call x0 -> x29, Pallas kernels: none -> 448 us  [call(): pl.pallas_call(body, grid_spec=pltpu.PrefetchScalarGridSpec(num_scalar_pr...]
    all_gather x14 -> x8, waiting for transfers between devices: 671 us -> 225 us  [gather_blocks(): gathered = lax.all_gather(shard, ALL, axis=0, tiled=True)]
    unnamed x36 -> x20, waiting for transfers between devices: 32 us -> 276 us
    ppermute x0 -> x29, waiting for transfers between devices: none -> 224 us  [the longest x24 153 us: swap_members(): lax.ppermute(parts[r], GROUP, [(a, a ^ r) for a in range(count)])]
    reduce_scatter x18 -> x6, waiting for transfers between devices: 667 us -> 844 us  [scatter_sum(): lax.psum_scatter(blocks.reshape(-1, blocks.shape[2]), ALL, scatter_dimens...]
    convert_element_type x16 -> x1, other arithmetic: 103 us -> 2.79 us  [on_device(): prev = tokens_wide = x_low.astype(F32)]
    reduce_sum x27 -> x0, other arithmetic: 72.4 us -> none  [the longest x8 34.6 us: one_block(): row_total = jnp.sum(exponent, -1, keepdims=True)]
  transfers between devices with their start and end apart: 34 -> 46, of which waited for: 28 -> 29; matrix products, arithmetic and copies ran while one was open for 16% -> 3% of each run, Pallas kernels for 0% -> 11%
where the time goes in v1:
time: 2260 us; the launch traced here: 2240 us
  waiting for transfers between devices  1570 us (69%)
  Pallas kernels  448 us (20%)
  blocking collectives  86.1 us (4%)
  local copies, waits for them, and re-layouts  66.8 us (3%)
  starting transfers between devices  35.6 us (2%)
    reduce_scatter x6, waiting for transfers between devices, scatter_sum(): lax.psum_scatter(blocks.reshape(-1, blocks.shape[2]), ALL, scatter_dimens...  844 us
    pallas_call x29, Pallas kernels, call(): pl.pallas_call(body, grid_spec=pltpu.PrefetchScalarGridSpec(num_scalar_pr...  448 us
    unnamed x20, waiting for transfers between devices  276 us
    all_gather x8, waiting for transfers between devices, gather_blocks(): gathered = lax.all_gather(shard, ALL, axis=0, tiled=True)  225 us
    ppermute x24, waiting for transfers between devices, swap_members(): lax.ppermute(parts[r], GROUP, [(a, a ^ r) for a in range(count)])  153 us
    ppermute x5, waiting for transfers between devices, regroup(): return lax.ppermute(values_in, ('c', 'zh'), perm)  70.5 us
  transfers between devices with their start and end apart: 46, of which 29 were waited for; matrix products, arithmetic and copies ran while one was open for 3% of the time, Pallas kernels for 11%

profile of v1, /device:TPU:1, one launch (start us, length us, event | category | flops | bytes accessed | tf_op | source)
XLA Modules:
  0.0 2241.3 jit_solution(15251302224008389211)
XLA Ops:
  23.9 44.3 %all-gather.7 = bf16[32,2,384]{2,1,0:T(2,128)(2,1)S(1)} all-gather(bf16[1,2,384]{2,1,0:T(2,128)(2,1)S(1)} %maximum_bitcast_fusion.4), channel_id=2, replica_groups=mesh['q'=4,'c'=2,'zh'=2,'zl'=2] {'zh','zl','q','c'}, dimensions={0}, use_global_device_ids=true | all-gather | bytes 50688 | tf_op jit(solution)/shard_map/all_gather | solution.py:644
  68.9 27.5 %all-gather.17.cloned.1.call-done = bf16[4096,768]{0,1:T(8,128)(2,1)} async-done(((bf16[128,768]{0,1:T(8,128)(2,1)}), bf16[4096,768]{0,1:T(8,128)(2,1)}) %all-gather.17.cloned.1.call-update) | async-done | bytes 6291472 | tf_op jit(solution)/shard_map/all_gather | solution.py:621
  119.7 46.2 %collective-permute-done = s32[1,4]{1,0:T(1,128)S(1)} collective-permute-done((s32[1,4]{1,0:T(1,128)S(1)}, s32[1,4]{1,0:T(1,128)S(1)}, u32[]{:S(2)}, u32[]{:S(2)}) %collective-permute-start) | collective-permute-done | bytes 48 | tf_op jit(solution)/shard_map/ppermute | solution.py:608
  173.8 52.5 %attend_forward.2 = (bf16[512,256]{1,0:T(8,128)(2,1)S(1)}, bf16[512,256]{1,0:T(8,128)(2,1)S(1)}, bf16[512,256]{1,0:T(8,128)(2,1)S(1)}, bf16[512,256]{1,0:T(8,128...) custom-call(s32[1]{0:T(128)} %bitcast.2.place_ref, s32[4]{0:T(128)S(1)} %bitcast.146, ...), custom_call_target="tpu_custom_call" | custom-call | flops 6442450944 | bytes 6291456 | tf_op jit(solution)/shard_map/attend_forward/pallas_call | solution.py:39
  257.3 71.8 %all-gather.23.cloned.1.call-done = bf16[1,4096,1024]{2,1,0:T(8,128)(2,1)} async-done(((bf16[1,128,1024]{2,1,0:T(8,128)(2,1)}), bf16[1,4096,1024]{2,1,0:T(8,128)(2,1)}) %all-gather.23.cloned.1.call-update) | async-done | bytes 8388624 | tf_op jit(solution)/shard_map/all_gather | solution.py:621
  330.4 14.9 up_gelu.2
  345.3 63.2 %all-gather.25.cloned.1.call-done = bf16[1,4096,1024]{2,1,0:T(8,128)(2,1)} async-done(((bf16[1,128,1024]{2,1,0:T(8,128)(2,1)}), bf16[1,4096,1024]{2,1,0:T(8,128)(2,1)}) %all-gather.25.cloned.1.call-update) | async-done | bytes 8388624 | tf_op jit(solution)/shard_map/all_gather | solution.py:621
  408.6 11.7 down_norm.2
  430.8 19.8 collective-permute-done.8.refs_1_
  450.6 23.0 %collective-permute-done.10.refs_3_ = bf16[512,768]{1,0:T(8,128)(2,1)S(1)} collective-permute-done((bf16[512,768]{1,0:T(8,128)(2,1)}, bf16[512,768]{1,0:T(8,128)(2,1)S(1)}, u32[]{:S(2)}, u32[]{:S(2)}) %collective-permute-start.10) | collective-permute-done | bytes 786464 | tf_op jit(solution)/shard_map/ppermute | solution.py:615
  474.5 52.6 %attend_forward.3 = (bf16[512,256]{1,0:T(8,128)(2,1)S(1)}, bf16[512,256]{1,0:T(8,128)(2,1)}, bf16[512,256]{1,0:T(8,128)(2,1)}, bf16[512,256]{1,0:T(8,128)(2,1)S(...) custom-call(s32[1]{0:T(128)} %bitcast.2.place_ref, s32[4]{0:T(128)S(1)} %bitcast.147, ...), custom_call_target="tpu_custom_call" | custom-call | flops 6442450944 | bytes 6291456 | tf_op jit(solution)/shard_map/attend_forward/pallas_call | solution.py:39
  534.1 24.9 %collective-permute-done.11.refs_1_ = bf16[512,256]{1,0:T(8,128)(2,1)S(1)} collective-permute-done((bf16[512,256]{1,0:T(8,128)(2,1)}, bf16[512,256]{1,0:T(8,128)(2,1)S(1)}, u32[]{:S(2)}, u32[]{:S(2)}) %collective-permute-start.11) | collective-permute-done | bytes 262176 | tf_op jit(solution)/shard_map/ppermute | solution.py:615
  574.0 14.9 up_gelu.3
  588.9 53.6 %all-gather.31.cloned.1.call-done = bf16[1,4096,1024]{2,1,0:T(8,128)(2,1)} async-done(((bf16[1,128,1024]{2,1,0:T(8,128)(2,1)}), bf16[1,4096,1024]{2,1,0:T(8,128)(2,1)}) %all-gather.31.cloned.1.call-update) | async-done | bytes 8388624 | tf_op jit(solution)/shard_map/all_gather | solution.py:621
  642.5 11.8 down_norm.3
  671.7 12.4 up_back.2
  702.7 56.8 %attend_backward.2 = (bf16[512,768]{1,0:T(8,128)(2,1)S(1)}, bf16[512,768]{1,0:T(8,128)(2,1)}, bf16[512,768]{1,0:T(8,128)(2,1)}, bf16[512,768]{1,0:T(8,128)(2,1)}) custom-call(s32[1]{0:T(128)} %bitcast.2.place_ref, s32[4]{0:T(128)S(1)} %bitcast.148, bf16[512,768]{1,0:T(8,128)(2,1)} %copy-done.16, bf16[512,768]{1,0:T(8,128)(2,1)} %copy-done.26, ...), custom_call_target="tpu_custom_call" | custom-call | flops 15032385536 | bytes 10485760 | tf_op jit(solution)/shard_map/attend_backward/pallas_call | solution.py:39
  779.0 17.0 collective-permute-done.21.refs_3_
  820.5 12.6 up_back.3
  851.7 56.4 %attend_backward.3 = (bf16[512,768]{1,0:T(8,128)(2,1)S(1)}, bf16[512,768]{1,0:T(8,128)(2,1)}, bf16[512,768]{1,0:T(8,128)(2,1)}, bf16[512,768]{1,0:T(8,128)(2,1)}) custom-call(s32[1]{0:T(128)} %bitcast.2.place_ref, s32[4]{0:T(128)S(1)} %bitcast.149, bf16[512,768]{1,0:T(8,128)(2,1)} %copy-done.15, bf16[512,768]{1,0:T(8,128)(2,1)} %collective-permute-done.2.refs_1_, ...), custom_call_target="tpu_custom_call" | custom-call | flops 15032385536 | bytes 10485760 | tf_op jit(solution)/shard_map/attend_backward/pallas_call | solution.py:39
  927.6 16.9 collective-permute-done.27.refs_3_
  1025.6 24.3 %collective-permute-done.14 = bf16[512,1024]{1,0:T(8,128)(2,1)S(1)} collective-permute-done((bf16[512,1024]{1,0:T(8,128)(2,1)S(1)}, bf16[512,1024]{1,0:T(8,128)(2,1)S(1)}, u32[]{:S(2)}, u32[]{:S(2)}) %collective-permute-start.14) | collective-permute-done | bytes 1048608 | tf_op jit(solution)/shard_map/ppermute | solution.py:608
  1050.0 35.5 %all-reduce.3.cloned.1.call-done = f32[32,768]{1,0:T(8,128)} async-done(((f32[32,768]{1,0:T(8,128)}), f32[32,768]{1,0:T(8,128)}) %all-reduce.3.cloned.1.call-update) | async-done | bytes 98320
  1091.0 129.1 %reduce-scatter.15.cloned.1.call-done = bf16[128,256]{1,0:T(8,128)(2,1)} async-done(((bf16[4096,256]{1,0:T(8,128)(2,1)}), bf16[128,256]{1,0:T(8,128)(2,1)}) %reduce-scatter.15.cloned.1.call-update) | async-done | bytes 65552 | tf_op jit(solution)/shard_map/reduce_scatter | solution.py:626
  1220.1 135.0 %reduce-scatter.13.cloned.1.call-done = bf16[128,256]{1,0:T(8,128)(2,1)} async-done(((bf16[4096,256]{1,0:T(8,128)(2,1)}), bf16[128,256]{1,0:T(8,128)(2,1)}) %reduce-scatter.13.cloned.1.call-update) | async-done | bytes 65552 | tf_op jit(solution)/shard_map/reduce_scatter | solution.py:626
  1357.3 117.5 %reduce-scatter.27.cloned.1.call-done = bf16[128,768]{1,0:T(8,128)(2,1)} async-done(((bf16[4096,768]{1,0:T(8,128)(2,1)}), bf16[128,768]{1,0:T(8,128)(2,1)}) %reduce-scatter.27.cloned.1.call-update) | async-done | bytes 196624
  1475.9 119.3 %reduce-scatter.25.cloned.1.call-done = bf16[128,768]{1,0:T(8,128)(2,1)} async-done(((bf16[4096,768]{1,0:T(8,128)(2,1)}), bf16[128,768]{1,0:T(8,128)(2,1)}) %reduce-scatter.25.cloned.1.call-update) | async-done | bytes 196624
  1599.2 142.3 %reduce-scatter.19.cloned.1.call-done = bf16[128,1024]{1,0:T(8,128)(2,1)} async-done(((bf16[4096,1024]{1,0:T(8,128)(2,1)}), bf16[128,1024]{1,0:T(8,128)(2,1)}) %reduce-scatter.19.cloned.1.call-update) | async-done | bytes 262160 | tf_op jit(solution)/shard_map/reduce_scatter | solution.py:626
  1741.5 146.9 %reduce-scatter.17.cloned.1.call-done = bf16[128,1024]{1,0:T(8,128)(2,1)} async-done(((bf16[4096,1024]{1,0:T(8,128)(2,1)}), bf16[128,1024]{1,0:T(8,128)(2,1)}) %reduce-scatter.17.cloned.1.call-update) | async-done | bytes 262160 | tf_op jit(solution)/shard_map/reduce_scatter | solution.py:626
  1891.1 143.9 %reduce-scatter.23.cloned.1.call-done = bf16[128,1024]{1,0:T(8,128)(2,1)} async-done(((bf16[4096,1024]{1,0:T(8,128)(2,1)}), bf16[128,1024]{1,0:T(8,128)(2,1)}) %reduce-scatter.23.cloned.1.call-update) | async-done | bytes 262160 | tf_op jit(solution)/shard_map/reduce_scatter | solution.py:626
  2035.0 146.7 %reduce-scatter.21.cloned.1.call-done = bf16[128,1024]{1,0:T(8,128)(2,1)} async-done(((bf16[4096,1024]{1,0:T(8,128)(2,1)}), bf16[128,1024]{1,0:T(8,128)(2,1)}) %reduce-scatter.21.cloned.1.call-update) | async-done | bytes 262160 | tf_op jit(solution)/shard_map/reduce_scatter | solution.py:626
  2188.9 41.8 %psum.7 = f32[]{:T(128)} all-reduce(f32[]{:T(128)S(6)} %add.51), channel_id=1, replica_groups=mesh['q'=4,'c'=2,'zh'=2,'zl'=2] {'zh','zl','q','c'}, use_global_device_ids=true, to_apply=%region_18.19 | all-reduce | flops 1 | bytes 8 | tf_op jit(solution)/shard_map/psum | solution.py:737
  (295 shorter events, 332.4 us)
Async XLA Ops:
  7.2 89.2 %all-gather.17.cloned.1.call-start = ((), (), s32[]{:S(2)}) async-start(), calls=%async_computation.8 | async-start | bytes 6488064 | tf_op jit(solution)/shard_map/all_gather | solution.py:621
  9.2 223.1 %all-gather.19.cloned.1.call-start = ((), (), s32[]{:S(2)}) async-start(), calls=%async_computation.9 | async-start | bytes 6488064 | tf_op jit(solution)/shard_map/all_gather | solution.py:621
  10.1 239.3 %all-gather.21.cloned.1.call-start = ((), (), s32[]{:S(2)}) async-start(), calls=%async_computation.16 | async-start | bytes 2162688 | tf_op jit(solution)/shard_map/all_gather | solution.py:621
  11.7 317.5 %all-gather.23.cloned.1.call-start = ((), (), s32[]{:S(2)}) async-start(), calls=%async_computation.17 | async-start | bytes 8650752 | tf_op jit(solution)/shard_map/all_gather | solution.py:621
  13.7 394.9 %all-gather.25.cloned.1.call-start = ((), (), s32[]{:S(2)}) async-start(), calls=%async_computation.18 | async-start | bytes 8650752 | tf_op jit(solution)/shard_map/all_gather | solution.py:621
  15.6 518.5 %all-gather.27.cloned.1.call-start = ((), (), s32[]{:S(2)}) async-start(), calls=%async_computation.19 | async-start | bytes 2162688 | tf_op jit(solution)/shard_map/all_gather | solution.py:621
  16.2 556.6 %all-gather.29.cloned.1.call-start = ((), (), s32[]{:S(2)}) async-start(), calls=%async_computation.20 | async-start | bytes 8650752 | tf_op jit(solution)/shard_map/all_gather | solution.py:621
  16.9 625.5 %all-gather.31.cloned.1.call-start = ((), (), s32[]{:S(2)}) async-start(), calls=%async_computation.21 | async-start | bytes 8650752 | tf_op jit(solution)/shard_map/all_gather | solution.py:621
  17.7 1067.8 %all-reduce.3.cloned.1.call-start = ((), (), s32[]{:S(2)}) async-start(), calls=%async_computation.24 | async-start | bytes 196608
  17.7 87.3 %collective-permute-start.1 = (bf16[512,1024]{1,0:T(8,128)(2,1)S(1)}, bf16[512,1024]{1,0:T(8,128)(2,1)}, u32[]{:S(2)}, u32[]{:S(2)}) collective-permute-start(bf16[512,1024]{1,0:T(8,128)(2,1)S(1)} %copy-done.25), channel_id=1, source_target_pairs={{0,0},{2,4},{4,2},{6,6},{1,1},{3,5},{5,3},{7,7},{8,8},{10,12},{12,... | collective-permute-start | bytes 3145736 | tf_op jit(solution)/shard_map/ppermute | solution.py:608
  112.7 53.4 %collective-permute-start.2 = (bf16[512,768]{1,0:T(8,128)(2,1)S(1)}, bf16[512,768]{1,0:T(8,128)(2,1)}, u32[]{:S(2)}, u32[]{:S(2)}) collective-permute-start(bf16[512,768]{1,0:T(8,128)(2,1)S(1)} %get-tuple-element.84), channel_id=1, source_target_pairs={{0,1},{1,0},{4,5},{5,4},{2,3},{3,2},{6,7},{7,6},{8,9},{9,8},{12,13... | collective-permute-start | bytes 2359304 | tf_op jit(solution)/shard_map/ppermute | solution.py:615
  112.7 53.4 %collective-permute-start.3 = (bf16[512,768]{1,0:T(8,128)(2,1)}, bf16[512,768]{1,0:T(8,128)(2,1)}, u32[]{:S(2)}, u32[]{:S(2)}) collective-permute-start(bf16[512,768]{1,0:T(8,128)(2,1)} %get-tuple-element.85), channel_id=1, source_target_pairs={{0,4},{1,5},{4,0},{5,1},{2,6},{3,7},{6,2},{7,3},{8,12},{9,13},{12,... | collective-permute-start | bytes 2359304 | tf_op jit(solution)/shard_map/ppermute | solution.py:615
  112.9 60.8 %collective-permute-start.4 = (bf16[512,768]{1,0:T(8,128)(2,1)}, bf16[512,768]{1,0:T(8,128)(2,1)}, u32[]{:S(2)}, u32[]{:S(2)}) collective-permute-start(bf16[512,768]{1,0:T(8,128)(2,1)} %get-tuple-element.86), channel_id=1, source_target_pairs={{0,5},{1,4},{4,1},{5,0},{2,7},{3,6},{6,3},{7,2},{8,13},{9,12},{12,... | collective-permute-start | bytes 2359304 | tf_op jit(solution)/shard_map/ppermute | solution.py:615
  114.6 51.3 %collective-permute-start = (s32[1,4]{1,0:T(1,128)S(1)}, s32[1,4]{1,0:T(1,128)S(1)}, u32[]{:S(2)}, u32[]{:S(2)}) collective-permute-start(s32[1,4]{1,0:T(1,128)S(1)} %copy-done.30), channel_id=1, source_target_pairs={{0,0},{2,4},{4,2},{6,6},{1,1},{3,5},{5,3},{7,7},{8,8},{10,12},{12,... | collective-permute-start | bytes 56 | tf_op jit(solution)/shard_map/ppermute | solution.py:608
  226.3 23.2 %collective-permute-start.5 = (bf16[512,256]{1,0:T(8,128)(2,1)S(1)}, bf16[512,256]{1,0:T(8,128)(2,1)S(1)}, u32[]{:S(2)}, u32[]{:S(2)}) collective-permute-start(bf16[512,256]{1,0:T(8,128)(2,1)S(1)} %get-tuple-element.88), channel_id=1, source_target_pairs={{0,1},{1,0},{4,5},{5,4},{2,3},{3,2},{6,7},{7,6},{8,9},{9,8},{12,13... | collective-permute-start | bytes 786440 | tf_op jit(solution)/shard_map/ppermute | solution.py:615
  430.7 42.9 %collective-permute-start.10 = (bf16[512,768]{1,0:T(8,128)(2,1)}, bf16[512,768]{1,0:T(8,128)(2,1)S(1)}, u32[]{:S(2)}, u32[]{:S(2)}) collective-permute-start(bf16[512,768]{1,0:T(8,128)(2,1)} %get-tuple-element.98), channel_id=1, source_target_pairs={{0,5},{1,4},{4,1},{5,0},{2,7},{3,6},{6,3},{7,2},{8,13},{9,12},{12,... | collective-permute-start | bytes 2359304 | tf_op jit(solution)/shard_map/ppermute | solution.py:615
  527.7 31.2 %collective-permute-start.11 = (bf16[512,256]{1,0:T(8,128)(2,1)}, bf16[512,256]{1,0:T(8,128)(2,1)S(1)}, u32[]{:S(2)}, u32[]{:S(2)}) collective-permute-start(bf16[512,256]{1,0:T(8,128)(2,1)} %get-tuple-element.100), channel_id=1, source_target_pairs={{0,1},{1,0},{4,5},{5,4},{2,3},{3,2},{6,7},{7,6},{8,9},{9,8},{12,13... | collective-permute-start | bytes 786440 | tf_op jit(solution)/shard_map/ppermute | solution.py:615
  529.0 30.0 %collective-permute-start.12 = (bf16[512,256]{1,0:T(8,128)(2,1)}, bf16[512,256]{1,0:T(8,128)(2,1)S(1)}, u32[]{:S(2)}, u32[]{:S(2)}) collective-permute-start(bf16[512,256]{1,0:T(8,128)(2,1)} %get-tuple-element.101), channel_id=1, source_target_pairs={{0,4},{1,5},{4,0},{5,1},{2,6},{3,7},{6,2},{7,3},{8,12},{9,13},{12,... | collective-permute-start | bytes 786440 | tf_op jit(solution)/shard_map/ppermute | solution.py:615
  529.2 35.4 %collective-permute-start.13 = (bf16[512,256]{1,0:T(8,128)(2,1)S(1)}, bf16[512,256]{1,0:T(8,128)(2,1)S(1)}, u32[]{:S(2)}, u32[]{:S(2)}) collective-permute-start(bf16[512,256]{1,0:T(8,128)(2,1)S(1)} %get-tuple-element.102), channel_id=1, source_target_pairs={{0,5},{1,4},{4,1},{5,0},{2,7},{3,6},{6,3},{7,2},{8,13},{9,12},{12,... | collective-permute-start | bytes 786440 | tf_op jit(solution)/shard_map/ppermute | solution.py:615
  529.6 125.6 %collective-permute-start.15 = (bf16[512,1024]{1,0:T(8,128)(2,1)}, bf16[512,1024]{1,0:T(8,128)(2,1)}, u32[]{:S(2)}, u32[]{:S(2)}) collective-permute-start(bf16[512,1024]{1,0:T(8,128)(2,1)} %param.21), channel_id=1, source_target_pairs={{0,0},{2,4},{4,2},{6,6},{1,1},{3,5},{5,3},{7,7},{8,8},{10,12},{12,... | collective-permute-start | bytes 3145736 | tf_op jit(solution)/shard_map/ppermute | solution.py:608
  761.0 34.9 %collective-permute-start.21 = (bf16[512,768]{1,0:T(8,128)(2,1)}, bf16[512,768]{1,0:T(8,128)(2,1)}, u32[]{:S(2)}, u32[]{:S(2)}) collective-permute-start(bf16[512,768]{1,0:T(8,128)(2,1)} %get-tuple-element.125), channel_id=1, source_target_pairs={{0,5},{1,4},{4,1},{5,0},{2,7},{3,6},{6,3},{7,2},{8,13},{9,12},{12,... | collective-permute-start | bytes 2359304 | tf_op jit(solution)/shard_map/ppermute | solution.py:615
  909.5 35.0 %collective-permute-start.27 = (bf16[512,768]{1,0:T(8,128)(2,1)}, bf16[512,768]{1,0:T(8,128)(2,1)}, u32[]{:S(2)}, u32[]{:S(2)}) collective-permute-start(bf16[512,768]{1,0:T(8,128)(2,1)} %get-tuple-element.143), channel_id=1, source_target_pairs={{0,5},{1,4},{4,1},{5,0},{2,7},{3,6},{6,3},{7,2},{8,13},{9,12},{12,... | collective-permute-start | bytes 2359304 | tf_op jit(solution)/shard_map/ppermute | solution.py:615
  953.2 266.9 %reduce-scatter.15.cloned.1.call-start = ((), (), s32[]{:S(2)}) async-start(), calls=%async_computation.11 | async-start | bytes 2162688 | tf_op jit(solution)/shard_map/reduce_scatter | solution.py:626
  957.5 397.6 %reduce-scatter.13.cloned.1.call-start = ((), (), s32[]{:S(2)}) async-start(), calls=%async_computation.10 | async-start | bytes 2162688 | tf_op jit(solution)/shard_map/reduce_scatter | solution.py:626
  961.8 513.0 %reduce-scatter.27.cloned.1.call-start = ((), (), s32[]{:S(2)}) async-start(), calls=%async_computation.23 | async-start | bytes 6488064
  962.4 632.8 %reduce-scatter.25.cloned.1.call-start = ((), (), s32[]{:S(2)}) async-start(), calls=%async_computation.22 | async-start | bytes 6488064
  963.2 778.3 %reduce-scatter.19.cloned.1.call-start = ((), (), s32[]{:S(2)}) async-start(), calls=%async_computation.13 | async-start | bytes 8650752 | tf_op jit(solution)/shard_map/reduce_scatter | solution.py:626
  974.0 914.3 %reduce-scatter.17.cloned.1.call-start = ((), (), s32[]{:S(2)}) async-start(), calls=%async_computation.12 | async-start | bytes 8650752 | tf_op jit(solution)/shard_map/reduce_scatter | solution.py:626
  985.9 1049.2 %reduce-scatter.23.cloned.1.call-start = ((), (), s32[]{:S(2)}) async-start(), calls=%async_computation.15 | async-start | bytes 8650752 | tf_op jit(solution)/shard_map/reduce_scatter | solution.py:626
  997.4 1184.3 %reduce-scatter.21.cloned.1.call-start = ((), (), s32[]{:S(2)}) async-start(), calls=%async_computation.14 | async-start | bytes 8650752 | tf_op jit(solution)/shard_map/reduce_scatter | solution.py:626
  1010.2 39.8 %collective-permute-start.14 = (bf16[512,1024]{1,0:T(8,128)(2,1)S(1)}, bf16[512,1024]{1,0:T(8,128)(2,1)S(1)}, u32[]{:S(2)}, u32[]{:S(2)}) collective-permute-start(bf16[512,1024]{1,0:T(8,128)(2,1)S(1)} %copy-done.7), channel_id=1, source_target_pairs={{0,0},{2,4},{4,2},{6,6},{1,1},{3,5},{5,3},{7,7},{8,8},{10,12},{12,... | collective-permute-start | bytes 3145736 | tf_op jit(solution)/shard_map/ppermute | solution.py:608
  1022.9 68.1 %collective-permute-start.28 = (bf16[512,1024]{1,0:T(8,128)(2,1)}, bf16[512,1024]{1,0:T(8,128)(2,1)S(1)}, u32[]{:S(2)}, u32[]{:S(2)}) collective-permute-start(bf16[512,1024]{1,0:T(8,128)(2,1)} %qkv_back.3), channel_id=1, source_target_pairs={{0,0},{2,4},{4,2},{6,6},{1,1},{3,5},{5,3},{7,7},{8,8},{10,12},{12,... | collective-permute-start | bytes 3145736 | tf_op jit(solution)/shard_map/ppermute | solution.py:608
  (46 other events, 1798.3 us)
Sparse Core Ops, SparseCore 0:
  11.5 84.8 all-gather.16
  99.3 91.7 all-gather.18
  194.0 55.4 all-gather.20
  252.8 76.3 all-gather.22
  332.5 76.0 all-gather.24
  411.3 56.4 all-gather.26
  471.2 90.5 all-gather.28
  564.7 77.7 all-gather.30
  953.3 132.1 all-reduce.2
  1087.6 132.4 reduce-scatter.14
  1222.5 132.5 reduce-scatter.12
  1360.6 114.1 reduce-scatter.26
  1481.3 113.8 reduce-scatter.24
  1597.4 144.0 reduce-scatter.18
  1743.6 144.6 reduce-scatter.16
  1890.5 144.4 reduce-scatter.22
  2037.2 144.5 reduce-scatter.20

commit v2 on v1

v2 whole, which is shorter than its diff:
```python
import jax
import jax.numpy as jnp
from jax import lax
from jax.experimental import pallas as pl
from jax.experimental.pallas import tpu as pltpu
from jax.sharding import Mesh
from jax.sharding import PartitionSpec as P

D = 1024
HD = 64
HEADS = 16
FF = 4096
LAYERS = 2
SEQLEN = 2048
WINDOW = 1024
EPS = 1e-06
FILL = -1000000000.0

F32 = jnp.float32
BF16 = jnp.bfloat16
GROUP = ("c", "zl")
MODEL = ("zh", "zl")
ALL = ("zh", "zl", "q", "c")
VMEM_LIMIT = 56 * 1024 * 1024
NT = (((1,), (1,)), ((), ()))
NN = (((1,), (0,)), ((), ()))
ROWS = 128
CHUNK = 64
BQ = 256


def mm(left, right, dims=NN):
    return lax.dot_general(left, right, dims, preferred_element_type=F32)


def full(shape):
    return pl.BlockSpec(shape, lambda *_: (0,) * len(shape))


ANY = pl.BlockSpec(memory_space=pl.ANY)


def sds(shape, kind):
    return jax.ShapeDtypeStruct(shape, kind)


def call(body, grid, in_specs, out_specs, out_shape, scratch, args, scalars, flops, traffic, name):
    return pl.pallas_call(
        body,
        grid_spec=pltpu.PrefetchScalarGridSpec(
            num_scalar_prefetch=len(scalars),
            grid=grid,
            in_specs=in_specs,
            out_specs=out_specs,
            scratch_shapes=scratch,
        ),
        out_shape=out_shape,
        compiler_params=pltpu.CompilerParams(
            dimension_semantics=("arbitrary",) * len(grid), vmem_limit_bytes=VMEM_LIMIT
        ),
        cost_estimate=pl.CostEstimate(flops=int(flops), bytes_accessed=int(traffic), transcendentals=0),
        name=name,
    )(*scalars, *args)


S_P, S_Q, S_C, S_ZH, S_Z = range(5)


def norm_rows(values_in):
    centred = values_in - jnp.mean(values_in, -1, keepdims=True)
    variance = jnp.mean(centred * centred, -1, keepdims=True)
    inverse = lax.rsqrt(variance + EPS)
    return centred * inverse, inverse


def norm_back_rows(grad, normed, inverse, gain):
    scaled = grad * gain
    centred = scaled - jnp.mean(scaled, -1, keepdims=True) - normed * jnp.mean(scaled * normed, -1, keepdims=True)
    return centred * inverse


def fold_rows(values_in):
    return jnp.sum(values_in.reshape(-1, 8, values_in.shape[-1]), 0)


def norm_forward(get_total, tokens, vec, n_ref, low_ref, inv_ref):
    def step(index, carry):
        rows = pl.ds(pl.multiple_of(index * CHUNK, CHUNK), CHUNK)
        normed, inverse = norm_rows(get_total(rows))
        n_ref[rows, :] = normed
        low_ref[rows, :] = (normed * vec[3:4, :] + vec[4:5, :]).astype(BF16)
        inv_ref[rows, :] = jnp.broadcast_to(inverse, (CHUNK, 128))
        return carry

    lax.fori_loop(0, tokens // CHUNK, step, 0)


def norm_backward(get_grad, tokens, n_ref, inv_ref, gain_ref, g_ref, low_ref, sums_ref):
    def step(index, carry):
        rows = pl.ds(pl.multiple_of(index * CHUNK, CHUNK), CHUNK)
        grad = get_grad(rows)
        normed = n_ref[rows, :]
        result = norm_back_rows(grad, normed, inv_ref[rows, 0:1], gain_ref[0:1, :])
        low = result.astype(BF16)
        g_ref[rows, :] = result
        low_ref[rows, :] = low
        return (
            carry[0] + fold_rows(grad * normed),
            carry[1] + fold_rows(grad),
            carry[2] + fold_rows(low.astype(F32)),
        )

    zero = jnp.zeros((8, D), F32)
    sums = lax.fori_loop(0, tokens // CHUNK, step, (zero, zero, zero))
    sums_ref[...] = jnp.zeros(sums_ref.shape, F32)
    for row, member in enumerate(sums):
        sums_ref[row : row + 1, :] = jnp.sum(member, 0, keepdims=True)


class Streamed:
    def __init__(self, refs, matrix, buffer, sems, scal):
        self.refs, self.matrix, self.buffer, self.sems, self.scal = refs, matrix, buffer, sems, scal

    def copies(self, s):
        slot = lax.rem(s, 2)
        plain, early, late = [], [], []
        for k in range(2):
            own, near_x, near_y, far_a, far_b = self.refs[5 * k : 5 * k + 5]

            def copy(src, r, k=k):
                row = ((self.scal[S_Q] ^ r) * 2 + (self.scal[S_C] ^ k)) * ROWS
                return pltpu.make_async_copy(
                    src, self.buffer.at[slot, pl.ds(pl.multiple_of(row, ROWS), ROWS), :], self.sems.at[slot, 4 * k + r]
                )

            for r, ref in enumerate((own, near_x, near_y)):
                plain.append(copy(ref.at[s, self.matrix], r))
            early.append(copy(far_a.at[jnp.minimum(s, 1), self.matrix], 3))
            late.append(copy(far_b.at[jnp.maximum(s - 2, 0), self.matrix], 3))
        return plain, early, late

    def each(self, s, act):
        plain, early, late = self.copies(s)
        for copy in plain:
            act(copy)

        @pl.when(s < 2)
        def _():
            for copy in early:
                act(copy)

        @pl.when(s >= 2)
        def _():
            for copy in late:
                act(copy)

    def start(self, s):
        self.each(s, lambda copy: copy.start())

    def wait(self, s):
        self.each(s, lambda copy: copy.wait())

    def turn(self, s, count):
        @pl.when(s == 0)
        def _():
            self.start(s)

        @pl.when(s + 1 < count)
        def _():
            self.start(s + 1)


def piece_shapes(width):
    return [pltpu.VMEM((2, D, width), BF16), pltpu.SemaphoreType.DMA((2, 8))]


def gelu_parts(u):
    size = jnp.abs(u)
    t = 1.0 / (1.0 + 0.2316419 * size)
    poly = t * (0.127414796 + t * (-0.142248368 + t * (0.7107068705 + t * (-0.7265760135 + t * 0.5307027145))))
    bell = jnp.exp(-0.5 * (u * u))
    tail = poly * bell
    cdf = jnp.where(u >= 0, 1.0 - tail, tail)
    return u * cdf, cdf + u * (0.3989422804014327 * bell)


def tiles(tokens, width):
    for i in range(2):
        for j in range(2):
            yield slice(i * tokens // 2, (i + 1) * tokens // 2), slice(j * width // 2, (j + 1) * width // 2)


def norm_up(scal, prev, parts, vec, weight, matrix, bias, count):
    tokens = prev.shape[0]
    width = FF // count

    def body(scal_ref, prev_ref, *refs):
        part_refs, refs = refs[: len(parts)], refs[len(parts) :]
        vec_ref, bias_ref, refs = refs[0], refs[1], refs[2:]
        pieces, (n_ref, low_ref, inv_ref, act_ref, slope_ref, buffer, sems) = refs[:10], refs[10:]
        s = pl.program_id(0)
        stream = Streamed(pieces, matrix, buffer, sems, scal_ref)
        stream.turn(s, count)

        @pl.when(s == 0)
        def _():
            def total(rows):
                attn = part_refs[0][rows, :].astype(F32)
                for part in part_refs[1:]:
                    attn = attn + part[rows, :].astype(F32)
                return prev_ref[rows, :] * vec_ref[0:1, :] + vec_ref[1:2, :] + (attn + vec_ref[2:3, :])

            norm_forward(total, tokens, vec_ref, n_ref, low_ref, inv_ref)

        stream.wait(s)
        slot = lax.rem(s, 2)
        for rows, cols in tiles(tokens, width):
            act, slope = gelu_parts(mm(low_ref[rows, :], buffer[slot, :, cols]) + bias_ref[0, :, cols])
            act_ref[rows, cols] = act.astype(BF16)
            slope_ref[rows, cols] = slope.astype(BF16)

    column = pl.BlockSpec((tokens, width), lambda s, _: (0, s))
    return call(
        body, (count,),
        [full((tokens, D))] * (1 + len(parts))
        + [full((8, D)), pl.BlockSpec((1, 1, width), lambda s, scal_ref: (scal_ref[S_Z] ^ s, 0, 0))] + [ANY] * 10,
        [full((tokens, D)), full((tokens, D)), full((tokens, 128)), column, column],
        [sds((tokens, D), F32), sds((tokens, D), BF16), sds((tokens, 128), F32)] + [sds((tokens, FF), BF16)] * 2,
        piece_shapes(width), [prev, *parts, vec, bias, *weight], (scal,), 2 * tokens * D * FF,
        2 * (D * FF + tokens * (10 * D + 2 * FF)), "norm_up",
    )


def down_norm(scal, act, weight, matrix, prev, vec, count):
    tokens = prev.shape[0]
    width = FF // count

    def body(scal_ref, act_ref, prev_ref, vec_ref, *refs):
        pieces, (n_ref, low_ref, inv_ref, buffer, sems, acc) = refs[:10], refs[10:]
        s = pl.program_id(0)
        stream = Streamed(pieces, matrix, buffer, sems, scal_ref)
        stream.turn(s, count)
        stream.wait(s)
        value = mm(act_ref[...], buffer[lax.rem(s, 2)], NT)

        @pl.when(s == 0)
        def _():
            acc[...] = value

        @pl.when(s > 0)
        def _():
            acc[...] += value

        @pl.when(s == count - 1)
        def _():
            def total(rows):
                return prev_ref[rows, :] * vec_ref[0:1, :] + vec_ref[1:2, :] + (acc[rows, :] + vec_ref[2:3, :])

            norm_forward(total, tokens, vec_ref, n_ref, low_ref, inv_ref)

    return call(
        body, (count,),
        [pl.BlockSpec((tokens, width), lambda s, _: (0, s)), full((tokens, D)), full((8, D))] + [ANY] * 10,
        [full((tokens, D)), full((tokens, D)), full((tokens, 128))],
        [sds((tokens, D), F32), sds((tokens, D), BF16), sds((tokens, 128), F32)],
        piece_shapes(width) + [pltpu.VMEM((tokens, D), F32)], [act, prev, vec, *weight], (scal,), 2 * tokens * D * FF,
        2 * (D * FF + tokens * (5 * D + FF)), "down_norm",
    )


def units_back(scal, grad, weight, matrix, slope, count):
    tokens = grad.shape[0]
    width = FF // count

    def body(scal_ref, grad_ref, slope_ref, *refs):
        pieces, (out_ref, sum_ref, buffer, sems) = refs[:10], refs[10:]
        s = pl.program_id(0)
        stream = Streamed(pieces, matrix, buffer, sems, scal_ref)
        stream.turn(s, count)
        stream.wait(s)
        slot = lax.rem(s, 2)
        sums = {}
        for rows, cols in tiles(tokens, width):
            low = (mm(grad_ref[rows, :], buffer[slot, :, cols]) * slope_ref[rows, cols].astype(F32)).astype(BF16)
            out_ref[rows, cols] = low
            part = fold_rows(low.astype(F32))
            sums[cols.start] = sums[cols.start] + part if cols.start in sums else part
            if rows.start > 0:
                sum_ref[0, :, cols] = jnp.sum(sums[cols.start], 0, keepdims=True)

    column = pl.BlockSpec((tokens, width), lambda s, _: (0, s))
    return call(
        body, (count,), [full((tokens, D)), column] + [ANY] * 10,
        [column, pl.BlockSpec((1, 1, width), lambda s, scal_ref: (scal_ref[S_Z] ^ s, 0, 0))],
        [sds((tokens, FF), BF16), sds((count, 1, width), F32)], piece_shapes(width), [grad, slope, *weight], (scal,),
        2 * tokens * D * FF, 2 * (D * FF + tokens * (D + 2 * FF)), "units_back",
    )


def up_back(scal, gu, weight, matrix, residual, normed, inverse, gain, count):
    tokens = residual.shape[0]
    width = FF // count

    def body(scal_ref, gu_ref, res_ref, n_ref, inv_ref, gain_ref, *refs):
        pieces, (g_ref, low_ref, sums_ref, buffer, sems, acc) = refs[:10], refs[10:]
        s = pl.program_id(0)
        stream = Streamed(pieces, matrix, buffer, sems, scal_ref)
        stream.turn(s, count)
        stream.wait(s)
        value = mm(gu_ref[...], buffer[lax.rem(s, 2)], NT)

        @pl.when(s == 0)
        def _():
            acc[...] = value

        @pl.when(s > 0)
        def _():
            acc[...] += value

        @pl.when(s == count - 1)
        def _():
            norm_backward(
                lambda rows: res_ref[rows, :] + acc[rows, :], tokens, n_ref, inv_ref, gain_ref, g_ref, low_ref, sums_ref
            )

    return call(
        body, (count,),
        [pl.BlockSpec((tokens, width), lambda s, _: (0, s)), full((tokens, D)), full((tokens, D)), full((tokens, 128)),
         full((8, D))] + [ANY] * 10,
        [full((tokens, D)), full((tokens, D)), full((8, D))],
        [sds((tokens, D), F32), sds((tokens, D), BF16), sds((8, D), F32)],
        piece_shapes(width) + [pltpu.VMEM((tokens, D), F32)], [gu, residual, normed, inverse, gain, *weight], (scal,),
        2 * tokens * D * FF, 2 * (D * FF + tokens * (8 * D + FF)), "up_back",
    )


def norm_back(scal, grad, normed, inverse, gain):
    tokens = grad.shape[0]

    def body(scal_ref, grad_ref, n_ref, inv_ref, gain_ref, g_ref, low_ref, sums_ref):
        norm_backward(
            lambda rows: grad_ref[rows, :].astype(F32), tokens, n_ref, inv_ref, gain_ref, g_ref, low_ref, sums_ref
        )

    return call(
        body, (1,), [full((tokens, D)), full((tokens, D)), full((tokens, 128)), full((8, D))],
        [full((tokens, D)), full((tokens, D)), full((8, D))],
        [sds((tokens, D), F32), sds((tokens, D), BF16), sds((8, D), F32)], [], [grad, normed, inverse, gain], (scal,),
        20 * tokens * D, 12 * tokens * D, "norm_back",
    )


def sum_norm_back(scal, residual, parts, normed, inverse, gain):
    tokens = residual.shape[0]

    def body(scal_ref, res_ref, *refs):
        part_refs, (n_ref, inv_ref, gain_ref, g_ref, low_ref, sums_ref) = refs[: len(parts)], refs[len(parts) :]

        def grad(rows):
            total = part_refs[0][rows, :].astype(F32)
            for part in part_refs[1:]:
                total = total + part[rows, :].astype(F32)
            return res_ref[rows, :] + total

        norm_backward(grad, tokens, n_ref, inv_ref, gain_ref, g_ref, low_ref, sums_ref)

    return call(
        body, (1,), [full((tokens, D))] * (2 + len(parts)) + [full((tokens, 128)), full((8, D))],
        [full((tokens, D)), full((tokens, D)), full((8, D))],
        [sds((tokens, D), F32), sds((tokens, D), BF16), sds((8, D), F32)], [],
        [residual, *parts, normed, inverse, gain], (scal,), 20 * tokens * D, 22 * tokens * D, "sum_norm_back",
    )


def turn_rows(scal_ref, x_ref, turned, core):
    for r in range(4):
        row = ((scal_ref[S_Q] ^ r) * 2 + core) * ROWS
        turned[r * ROWS : (r + 1) * ROWS, :] = x_ref[:, pl.ds(pl.multiple_of(row, ROWS), ROWS)].T


def grad_theirs(scal, left, right, count):
    tokens = left.shape[0]
    width = right.shape[1] // count

    def body(scal_ref, x_ref, y_ref, out_ref, turned):
        @pl.when(pl.program_id(0) == 0)
        def _():
            turn_rows(scal_ref, x_ref, turned, scal_ref[S_C] ^ 1)

        out_ref[:, 0] = mm(turned[...], y_ref[...]).astype(BF16).reshape(4, ROWS, width)

    return call(
        body, (count,), [full((tokens, D)), pl.BlockSpec((tokens, width), lambda s, _: (0, s))],
        pl.BlockSpec((4, 1, ROWS, width), lambda s, _: (0, s, 0, 0)), sds((4, count, ROWS, width), BF16),
        [pltpu.VMEM((4 * ROWS, tokens), BF16)], [left, right], (scal,), tokens * D * width * count,
        D * width * count + 2 * tokens * (D + count * width), "grad_theirs",
    )


def grad_mine(scal, left, right, received, count):
    tokens = left.shape[0]
    width = right.shape[1] // count
    half = count // 2

    def body(scal_ref, x_ref, y_ref, *refs):
        if received is None:
            own, to_x, to_y, rest_x, rest_y, turned = refs
        else:
            got_ref, own, to_x, to_y, rest_x, rest_y, turned = refs
        s = pl.program_id(0)

        @pl.when(s == 0)
        def _():
            turn_rows(scal_ref, x_ref, turned, scal_ref[S_C])

        value = mm(turned[...], y_ref[...]).reshape(4, ROWS, width)
        if received is not None:
            value = value + got_ref[:, 0].astype(F32)
        value = value.astype(BF16)
        own[s] = value[0]

        @pl.when(s < half)
        def _():
            to_x[s] = value[1]
            to_x[half + s] = value[3]
            rest_y[s] = value[2]

        @pl.when(s >= half)
        def _():
            rest_x[s - half] = value[1]
            to_y[s - half] = value[2]
            to_y[s] = value[3]

    specs = [full((tokens, D)), pl.BlockSpec((tokens, width), lambda s, _: (0, s))]
    args = [left, right]
    if received is not None:
        specs.append(pl.BlockSpec((4, 1, ROWS, width), lambda s, _: (0, s, 0, 0)))
        args.append(received)
    shapes = [(count, ROWS, width)] * 3 + [(half, ROWS, width)] * 2
    return call(
        body, (count,), specs, [full(shape) for shape in shapes], [sds(shape, BF16) for shape in shapes],
        [pltpu.VMEM((4 * ROWS, tokens), BF16)], args, (scal,), tokens * D * width * count,
        2 * D * width * count + 2 * tokens * (D + count * width), "grad_mine",
    )


def fetch_heads_weight(scal_ref, pieces, cols, buffer, sems):
    copies = []
    for r in range(4):
        for k in range(2):
            row = ((scal_ref[S_Q] ^ r) * 2 + (scal_ref[S_ZH] ^ k)) * ROWS
            copies.append(
                pltpu.make_async_copy(
                    pieces[r].at[k, :, cols], buffer.at[pl.ds(pl.multiple_of(row, ROWS), ROWS), :], sems.at[2 * r + k]
                )
            )
    for copy in copies:
        copy.start()
    for copy in copies:
        copy.wait()


def by_member(shape):
    return pl.BlockSpec((1,) + shape, lambda r, scal_ref: (scal_ref[S_P] ^ r, 0, 0))


def heads_weight_scratch(width):
    return [pltpu.VMEM((D, width), BF16), pltpu.SemaphoreType.DMA((8,))]


def project_in(scal, lefts, weight, cols, bias, name):
    count = len(lefts)
    tokens = lefts[0].shape[0]
    width = cols.stop - cols.start

    def body(scal_ref, *refs):
        left_refs, refs = refs[:count], refs[count:]
        if bias is not None:
            bias_ref, refs = refs[0], refs[1:]
        pieces, (out_ref, buffer, sems) = refs[:4], refs[4:]
        step = pl.program_id(0)

        @pl.when(step == 0)
        def _():
            fetch_heads_weight(scal_ref, pieces, cols, buffer, sems)

        for r, left in enumerate(left_refs):

            @pl.when(step == r)
            def _(left=left):
                value = mm(left[...], buffer[...])
                if bias is not None:
                    value = value + bias_ref[...]
                out_ref[0] = value.astype(BF16)

    extra, extra_specs = ([], []) if bias is None else ([bias], [full((1, width))])
    return call(
        body, (count,), [full((tokens, D))] * count + extra_specs + [ANY] * 4, by_member((tokens, width)),
        sds((count, tokens, width), BF16), heads_weight_scratch(width), [*lefts, *extra, *weight], (scal,),
        2 * tokens * D * width * count, 2 * (D * width + count * tokens * (D + width)), name,
    )


def project_out(scal, blocks, weight, cols, name):
    count, tokens, width = blocks.shape

    def body(scal_ref, block_ref, *refs):
        pieces, outs, (buffer, sems) = refs[:4], refs[4 : 4 + count], refs[4 + count :]
        step = pl.program_id(0)

        @pl.when(step == 0)
        def _():
            fetch_heads_weight(scal_ref, pieces, cols, buffer, sems)

        for r, out in enumerate(outs):

            @pl.when(step == r)
            def _(out=out):
                out[...] = mm(block_ref[0], buffer[...], NT).astype(BF16)

    return call(
        body, (count,), [by_member((tokens, width))] + [ANY] * 4, [full((tokens, D))] * count,
        [sds((tokens, D), BF16)] * count, heads_weight_scratch(width), [blocks, *weight], (scal,),
        2 * tokens * D * width * count, 2 * (D * width + count * tokens * (D + width)), name,
    )


def heads_grad(scal, xs, gqkv, gas, ctx):
    count, tokens, width = gqkv.shape
    out_width = ctx.shape[2]

    def body(scal_ref, *refs):
        x_refs, refs = refs[:count], refs[count:]
        ga_refs, refs = refs[:count], refs[count:]
        g_ref, ctx_ref = refs[:2]
        outs, (sum_ref, acc, acc_out) = refs[2:6], refs[6:]
        step = pl.program_id(0)
        for r in range(count):

            @pl.when(step == r)
            def _(r=r):
                value = mm(x_refs[r][...].T, g_ref[0])
                value_out = mm(ga_refs[r][...].T, ctx_ref[0])
                sums = jnp.sum(g_ref[0].astype(F32), 0, keepdims=True)
                if r == 0:
                    acc[...] = value
                    acc_out[...] = value_out
                    sum_ref[...] = sums
                else:
                    acc[...] += value
                    acc_out[...] += value_out
                    sum_ref[...] += sums

        @pl.when(step == count - 1)
        def _():
            for r in range(4):
                for k in range(2):
                    row = ((scal_ref[S_Q] ^ r) * 2 + (scal_ref[S_ZH] ^ k)) * ROWS
                    rows = pl.ds(pl.multiple_of(row, ROWS), ROWS)
                    outs[r][k, :, :width] = acc[rows, :].astype(BF16)
                    outs[r][k, :, width:] = acc_out[rows, :].astype(BF16)

    shape = (2, ROWS, width + out_width)
    return call(
        body, (count,), [full((tokens, D))] * (2 * count) + [by_member((tokens, width)), by_member((tokens, out_width))],
        [full(shape)] * 4 + [full((1, width))], [sds(shape, BF16)] * 4 + [sds((1, width), F32)],
        [pltpu.VMEM((D, width), F32), pltpu.VMEM((D, out_width), F32)], [*xs, *gas, gqkv, ctx], (scal,),
        2 * tokens * D * (width + out_width) * count, 4 * count * tokens * (D + width), "heads_grad",
    )


def reach(ends_ref, row):
    first = jnp.zeros_like(row)
    for index in range(3):
        first = jnp.where(row >= ends_ref[index], ends_ref[index], first)
    last = jnp.full_like(row, SEQLEN)
    for index in (2, 1, 0):
        last = jnp.where(row < ends_ref[index], ends_ref[index], last)
    return jnp.maximum(first, row - (WINDOW - 1)), jnp.minimum(last, row + WINDOW)


def over_keys(ends_ref, start, chunk, block):
    low_first, high_first = reach(ends_ref, start)
    low_last, high_last = reach(ends_ref, start + BQ - 1)
    low_row, high_row = reach(ends_ref, start + lax.broadcasted_iota(jnp.int32, (1, BQ), 1))

    def one(b, carry):
        open_all = (b * chunk >= low_last) & ((b + 1) * chunk <= high_first)

        @pl.when(open_all)
        def _():
            block(b, None)

        @pl.when(jnp.logical_not(open_all))
        def _():
            key = b * chunk + lax.broadcasted_iota(jnp.int32, (chunk, BQ), 0)
            block(b, (key >= low_row) & (key < high_row))

        return carry

    lax.fori_loop(low_first // chunk, (high_last + chunk - 1) // chunk, one, 0)


def attend_forward(ends, qkv):
    count, chunk, width3 = qkv.shape
    width = width3 // 3
    heads = width // HD
    steps = SEQLEN // BQ
    per = chunk // BQ

    def body(ends_ref, qkv_ref, ctx_ref, wide_ref, lse_ref, qh, kh, vt, acc, tops, sums, scores):
        step = pl.program_id(0)

        @pl.when(step == 0)
        def _():
            for j in range(count):
                rows = slice(j * chunk, (j + 1) * chunk)
                for h in range(heads):
                    qh[h, rows, :] = qkv_ref[j, :, h * HD : (h + 1) * HD] * BF16(HD**-0.5)
                    kh[h, rows, :] = qkv_ref[j, :, width + h * HD : width + (h + 1) * HD]
                vt[j] = qkv_ref[j, :, 2 * width :].T

        start = step * BQ
        rows = pl.ds(pl.multiple_of(start, BQ), BQ)
        acc[...] = jnp.zeros(acc.shape, F32)
        tops[...] = jnp.full(tops.shape, -3.0e38, F32)
        sums[...] = jnp.zeros(sums.shape, F32)

        def score(b, allowed):
            keys = pl.ds(pl.multiple_of(b * chunk, chunk), chunk)
            for h in range(heads):
                value = mm(kh[h, keys, :], qh[h, rows, :], NT)
                if allowed is not None:
                    value = jnp.where(allowed, value, FILL)
                scores[h, b] = value
                tops[h] = jnp.maximum(tops[h], jnp.max(value.reshape(-1, 8, BQ), 0))

        over_keys(ends_ref, start, chunk, score)
        top = [jnp.max(tops[h], 0, keepdims=True) for h in range(heads)]

        def weigh(b, carry):
            for h in range(heads):
                part = slice(h * HD, (h + 1) * HD)
                weight = jnp.exp(scores[h, b] - top[h])
                sums[h] += fold_rows(weight)
                acc[part, :] += mm(vt[b, part, :], weight.astype(BF16))
            return carry

        low_first, _ = reach(ends_ref, start)
        _, high_last = reach(ends_ref, start + BQ - 1)
        lax.fori_loop(low_first // chunk, (high_last + chunk - 1) // chunk, weigh, 0)
        for h in range(heads):
            part = slice(h * HD, (h + 1) * HD)
            total = jnp.sum(sums[h], 0, keepdims=True)
            wide_ref[part, :] = acc[part, :] / total
            lse_ref[h : h + 1, :] = top[h] + jnp.log(total)
        lse_ref[heads:, :] = jnp.zeros((8 - heads, BQ), F32)
        ctx_ref[0] = wide_ref[...].T.astype(BF16)

    pairs = SEQLEN * SEQLEN
    return call(
        body, (steps,), [full((count, chunk, width3))],
        [pl.BlockSpec((1, BQ, width), lambda i, _: (i // per, i % per, 0)),
         pl.BlockSpec((width, BQ), lambda i, _: (0, i)), pl.BlockSpec((8, BQ), lambda i, _: (0, i))],
        [sds((count, chunk, width), BF16), sds((width, SEQLEN), F32), sds((8, SEQLEN), F32)],
        [
            pltpu.VMEM((heads, SEQLEN, HD), BF16),
            pltpu.VMEM((heads, SEQLEN, HD), BF16),
            pltpu.VMEM((count, width, chunk), BF16),
            pltpu.VMEM((width, BQ), F32),
            pltpu.VMEM((heads, 8, BQ), F32),
            pltpu.VMEM((heads, 8, BQ), F32),
            pltpu.VMEM((heads, count, chunk, BQ), F32),
        ],
        [qkv], (ends,), 16 * pairs * heads * HD, 6 * SEQLEN * width * 2, "attend_forward",
    )


def attend_backward(ends, qkv, grads, wide, lse):
    count, chunk, width3 = qkv.shape
    width = width3 // 3
    heads = width // HD
    steps = SEQLEN // BQ
    per = chunk // BQ

    def body(ends_ref, qkv_ref, grad_ref, wide_ref, lse_ref, out_ref, qh, kh, vh, gh, kt, qt, gt, gq, gk, gv):
        step = pl.program_id(0)

        @pl.when(step == 0)
        def _():
            for j in range(count):
                rows = slice(j * chunk, (j + 1) * chunk)
                for h in range(heads):
                    cols = slice(h * HD, (h + 1) * HD)
                    qh[h, rows, :] = qkv_ref[j, :, cols] * BF16(HD**-0.5)
                    kh[h, rows, :] = qkv_ref[j, :, width + h * HD : width + (h + 1) * HD]
                    vh[h, rows, :] = qkv_ref[j, :, 2 * width + h * HD : 2 * width + (h + 1) * HD]
                    gh[h, rows, :] = grad_ref[j, :, cols]
                kt[j] = qkv_ref[j, :, width : 2 * width].T
                for s in range(per):
                    sub = slice(s * BQ, (s + 1) * BQ)
                    qt[j * per + s] = (qkv_ref[j, sub, :width] * BF16(HD**-0.5)).T
                    gt[j * per + s] = grad_ref[j, sub, :].T
            gk[...] = jnp.zeros(gk.shape, F32)
            gv[...] = jnp.zeros(gv.shape, F32)

        start = step * BQ
        rows = pl.ds(pl.multiple_of(start, BQ), BQ)
        gq[...] = jnp.zeros(gq.shape, F32)
        inner = []
        for h in range(heads):
            part = slice(h * HD, (h + 1) * HD)
            inner.append(jnp.sum(gt[step, part, :].astype(F32) * wide_ref[part, :], 0, keepdims=True))

        def block(b, allowed):
            keys = pl.ds(pl.multiple_of(b * chunk, chunk), chunk)
            for h in range(heads):
                part = slice(h * HD, (h + 1) * HD)
                score = mm(kh[h, keys, :], qh[h, rows, :], NT)
                grad_weight = mm(vh[h, keys, :], gh[h, rows, :], NT)
                if allowed is not None:
                    score = jnp.where(allowed, score, FILL)
                weight = jnp.exp(score - lse_ref[h : h + 1, :])
                grad_score = (weight * (grad_weight - inner[h])).astype(BF16)
                gv[b, part, :] += mm(gt[step, part, :], weight.astype(BF16), NT)
                gk[b, part, :] += mm(qt[step, part, :], grad_score, NT)
                gq[part, :] += mm(kt[b, part, :], grad_score)

        over_keys(ends_ref, start, chunk, block)
        out_ref[step // per, pl.ds(pl.multiple_of((step % per) * BQ, BQ), BQ), :width] = (
            (gq[...] * HD**-0.5).T.astype(BF16)
        )

        @pl.when(step == steps - 1)
        def _():
            for j in range(count):
                out_ref[j, :, width : 2 * width] = gk[j].T.astype(BF16)
                out_ref[j, :, 2 * width :] = gv[j].T.astype(BF16)

    pairs = SEQLEN * SEQLEN
    return call(
        body, (steps,),
        [full((count, chunk, width3)), full((count, chunk, width)), pl.BlockSpec((width, BQ), lambda i, _: (0, i)),
         pl.BlockSpec((8, BQ), lambda i, _: (0, i))],
        full((count, chunk, width3)), sds((count, chunk, width3), BF16),
        [pltpu.VMEM((heads, SEQLEN, HD), BF16)] * 4
        + [
            pltpu.VMEM((count, width, chunk), BF16),
            pltpu.VMEM((steps, width, BQ), BF16),
            pltpu.VMEM((steps, width, BQ), BF16),
            pltpu.VMEM((width, BQ), F32),
            pltpu.VMEM((count, width, chunk), F32),
            pltpu.VMEM((count, width, chunk), F32),
        ],
        [qkv, grads, wide, lse], (ends,), 28 * pairs * heads * HD, 20 * SEQLEN * width, "attend_backward",
    )


def flip(values_in, axes, mask):
    return lax.ppermute(values_in, axes, [(a, a ^ mask) for a in range(lax.axis_size(axes))])


def turn(values_in):
    return lax.ppermute(values_in, ("c", "zh"), [(2 * a + b, 2 * b + a) for a in range(2) for b in range(2)])


def cross(values_in):
    return lax.ppermute(values_in, ("c", "zh"), [(2 * a + b, 2 * b + 1 - a) for a in range(2) for b in range(2)])


def uncross(values_in):
    return lax.ppermute(values_in, ("c", "zh"), [(2 * b + 1 - a, 2 * a + b) for a in range(2) for b in range(2)])


def from_members(values_in, axes):
    return [values_in] + [flip(values_in, axes, r) for r in range(1, lax.axis_size(axes))]


def to_members(parts, axes):
    return [parts[0]] + [flip(part, axes, r) for r, part in enumerate(parts) if r > 0]


def add(*parts):
    total = parts[0].astype(F32)
    for part in parts[1:]:
        total = total + part.astype(F32)
    return total


def is_small():
    return lax.axis_size("q") == 4


def order_by(values_in, axis, position, count):
    bit = 1
    while bit < count:
        shape = values_in.shape
        split = shape[:axis] + (count // (2 * bit), 2, bit) + shape[axis + 1 :]
        cut = values_in.reshape(split)
        values_in = jnp.where((position & bit) != 0, jnp.flip(cut, axis + 1), cut).reshape(shape)
        bit *= 2
    return values_in


def gather_heads_weight(shard, zh):
    pair = jnp.stack([turn(shard), cross(shard)])
    if is_small():
        return from_members(pair, "q")
    every = order_by(lax.all_gather(pair, "q"), 1, zh, 2).reshape(4, 2, ROWS, -1)
    return [every[r] for r in range(4)]


def scatter_heads_grad(buckets, zh):
    if is_small():
        got = to_members(buckets, "q")
        first, second = (add(*(member[k] for member in got)).astype(BF16) for k in range(2))
    else:
        every = jnp.stack(buckets).reshape(lax.axis_size("q"), 2, -1, buckets[0].shape[-1])
        rows = order_by(lax.psum_scatter(every, "q", scatter_dimension=0, tiled=False), 0, zh, 2)
        first, second = rows[0], rows[1]
    return add(turn(first), uncross(second))


def gather_units_weight(shard):
    if is_small():
        two = jnp.stack([shard, flip(shard, "zl", 1)])
        own = jnp.concatenate([two, flip(two, "zh", 1)])
        near_x, near_y = flip(own, "q", 1), flip(own, "q", 2)
        far_a, far_b = flip(near_y[:2], "q", 1), flip(near_x[2:], "q", 2)
        mine = [own, near_x, near_y, far_a, far_b]
        return mine + [flip(piece, "c", 1) for piece in mine]
    matrices, _, width = shard.shape
    members = lax.axis_size(MODEL)
    every = lax.all_gather(shard, ALL).reshape(members, -1, matrices, shard.shape[1], width).transpose(0, 2, 1, 3, 4)
    every = every.reshape(members, matrices, 4, 2, ROWS, width)
    pieces = []
    for k in range(2):
        pieces += [every[:, :, r, k] for r in range(3)] + [every[:2, :, 3, k], every[2:, :, 3, k]]
    return pieces


def scatter_units_grad(scal, left, right, count):
    if is_small():
        got = flip(grad_theirs(scal, left, right, count), "c", 1)
        own, to_x, to_y, rest_x, rest_y = grad_mine(scal, left, right, got, count)
        half = count // 2
        from_x, from_y = flip(to_x, "q", 1), flip(to_y, "q", 2)
        late_x = flip(add(rest_x, from_y[half:]).astype(BF16), "q", 1)
        late_y = flip(add(rest_y, from_x[half:]).astype(BF16), "q", 2)
        near = add(own[:half], from_x[:half], late_y)
        far = add(own[half:], late_x, from_y[:half]).astype(BF16)
        both = near + flip(far, "zh", 1).astype(F32)
        return both[0] + flip(both[1].astype(BF16), "zl", 1).astype(F32)
    theirs = grad_theirs(scal, left, right, count)
    own, to_x, to_y, rest_x, rest_y = grad_mine(scal, left, right, None, count)
    half = count // 2
    mine = jnp.stack(
        [own, jnp.concatenate([to_x[:half], rest_x]), jnp.concatenate([rest_y, to_y[:half]]),
         jnp.concatenate([to_x[half:], to_y[half:]])]
    )
    every = jnp.stack([mine, theirs], axis=1).transpose(2, 0, 1, 3, 4).reshape(-1, mine.shape[-1])
    return lax.psum_scatter(every, ALL, scatter_dimension=0, tiled=True).astype(F32)


SMALL_AXES = ("q", MODEL, "c")


def gather_small(shard, where):
    tz, dp = lax.axis_size(MODEL), lax.axis_size(("q", "c"))
    if not is_small():
        return lax.all_gather(shard, ALL).reshape(tz, dp, -1)
    every = shard.reshape(1, -1)
    for axes in SMALL_AXES:
        every = jnp.stack(from_members(every, axes))
    every = every.reshape(2, 4, 4, -1)
    for axis, position in enumerate(where[::-1]):
        every = order_by(every, axis, position, every.shape[axis])
    return every.transpose(1, 2, 0, 3).reshape(tz, dp, -1)


def scatter_small(values_in, where):
    if not is_small():
        return lax.psum_scatter(values_in.reshape(-1, values_in.shape[-1]), ALL, scatter_dimension=0, tiled=True)[0]
    every = values_in.reshape(4, 4, 2, -1).transpose(1, 0, 2, 3)
    for axis, position in enumerate(where):
        every = order_by(every, axis, position, every.shape[axis])
    for axes in SMALL_AXES:
        every = add(*to_members([every[r] for r in range(every.shape[0])], axes))
    return every


def sum_all(value):
    if not is_small():
        return lax.psum(value, ALL)
    value = jnp.broadcast_to(value, (8, 128))
    for axes in SMALL_AXES:
        parts = jnp.stack(from_members(value, axes))
        value = jnp.sum(order_by(parts, 0, lax.axis_index(axes), parts.shape[0]), 0)
    return value[0, 0]


def on_device(
    tokens, doc_lengths, qkv_weight, qv_bias, out_weight, up_weight, up_bias, down_weight, gains, shifts, cotangent
):
    layers = qkv_weight.shape[0]
    tz, dp = lax.axis_size(MODEL), lax.axis_size(("q", "c"))
    place, zh = lax.axis_index(GROUP), lax.axis_index("zh")
    where = (lax.axis_index("q"), lax.axis_index(MODEL), lax.axis_index("c"))
    if is_small():
        spots = [place, where[0], where[2], zh, where[1]]
    else:
        spots = [place] + [jnp.zeros((), jnp.int32)] * 4
    scal = jnp.stack([spot.astype(jnp.int32) for spot in spots])

    x_low = turn(tokens)
    ends = jnp.cumsum(turn(doc_lengths)[0], dtype=jnp.int32)

    pieces = [qv_bias, up_bias, gains, shifts]
    sizes = [piece.size // layers for piece in pieces]
    small = jnp.concatenate([piece.reshape(layers, -1) for piece in pieces], axis=1)
    small_all = gather_small(small.reshape(-1), where).reshape(tz, dp, layers, -1).astype(F32)
    cuts = [0]
    for size in sizes:
        cuts.append(cuts[-1] + size)
    parts = [small_all[..., cuts[i] : cuts[i + 1]] for i in range(4)]
    hz = qv_bias.shape[2]
    qv_here = lax.dynamic_index_in_dim(parts[0], place, 0, False)
    qv_here = qv_here.reshape(dp, layers, 2, hz, -1).transpose(1, 2, 3, 0, 4).reshape(layers, 2, -1)
    bias_qkv = jnp.concatenate([qv_here[:, :1], jnp.zeros_like(qv_here[:, :1]), qv_here[:, 1:]], axis=1)
    bias_qkv = bias_qkv.reshape(layers, 1, -1)
    up_bias_full = parts[1].reshape(tz, dp, layers, up_bias.shape[1], -1).transpose(2, 0, 3, 1, 4)
    up_bias_full = up_bias_full.reshape(layers, tz, 1, -1)
    gain_full = parts[2].reshape(tz, dp, layers, 2, -1).transpose(2, 3, 1, 0, 4).reshape(layers, 2, D)
    shift_full = parts[3].reshape(tz, dp, layers, 4, -1).transpose(2, 3, 1, 0, 4).reshape(layers, 4, D)

    qkv_cols = 3 * out_weight.shape[2]
    heads_weight, units_weight = [], []
    for l in range(layers):
        shard = jnp.concatenate([qkv_weight[l].transpose(1, 0, 2).reshape(-1, qkv_cols), out_weight[l]], axis=1)
        heads_weight.append(gather_heads_weight(shard, zh))
        if l == 0:
            up = (gather_units_weight(up_weight[l][None]), 0)
            down = (gather_units_weight(down_weight[l][None]), 0)
        else:
            both = gather_units_weight(jnp.stack([up_weight[l], down_weight[l]]))
            up, down = (both, 0), (both, 1)
        units_weight.append((up, down))
    top_grad = turn(cotangent)
    in_cols, out_cols = slice(0, qkv_cols), slice(qkv_cols, qkv_cols + out_weight.shape[2])

    one, zero = jnp.ones((D,), F32), jnp.zeros((D,), F32)
    pad = [zero, zero, zero]
    prev, prev_gain, prev_shift = x_low.astype(F32), one, zero
    kept = []
    for l in range(layers):
        w_heads, (w_up, w_down) = heads_weight[l], units_weight[l]
        xs = from_members(x_low, GROUP)
        qkv = project_in(scal, xs, w_heads, in_cols, bias_qkv[l], "project_qkv")
        ctx, wide, lse = attend_forward(ends, qkv)
        attn = to_members(project_out(scal, ctx, w_heads, out_cols, "project_attn"), GROUP)
        vec = jnp.stack([prev_gain, prev_shift, shift_full[l, 0], gain_full[l, 0], shift_full[l, 1]] + pad)
        n1, hs, r1, act, slope = norm_up(scal, prev, attn, vec, *w_up, up_bias_full[l], tz)
        vec = jnp.stack([gain_full[l, 0], shift_full[l, 1], shift_full[l, 2], gain_full[l, 1], shift_full[l, 3]] + pad)
        n2, y_low, r2 = down_norm(scal, act, *w_down, n1, vec, tz)
        kept.append((xs, qkv, ctx, wide, lse, n1, hs, r1, act, slope, n2, r2))
        x_low, prev, prev_gain, prev_shift = y_low, n2, gain_full[l, 1], shift_full[l, 3]
    layer_output = turn(x_low)

    gain_rows = [[jnp.broadcast_to(gain_full[l, i], (8, D)) for i in range(2)] for l in range(layers)]
    g2, gf, sums2 = norm_back(scal, top_grad, kept[-1][10], kept[-1][11], gain_rows[-1][1])
    results = [None] * layers
    small_grads = [None] * layers
    for l in reversed(range(layers)):
        w_heads, (w_up, w_down) = heads_weight[l], units_weight[l]
        xs, qkv, ctx, wide, lse, n1, hs, r1, act, slope, n2, r2 = kept[l]
        gu, up_bias_sum = units_back(scal, gf, *w_down, slope, tz)
        g1, ga, sums1 = up_back(scal, gu, *w_up, g2, n1, r1, gain_rows[l][0], tz)
        gas = from_members(ga, GROUP)
        d_down = scatter_units_grad(scal, gf, act, tz)
        d_up = scatter_units_grad(scal, hs, gu, tz)
        gc = project_in(scal, gas, w_heads, out_cols, None, "project_gc")
        gqkv = attend_backward(ends, qkv, gc, wide, lse)
        back = to_members(project_out(scal, gqkv, w_heads, in_cols, "project_gx"), GROUP)
        *buckets, qkv_sums = heads_grad(scal, xs, gqkv, gas, ctx)
        d_heads = scatter_heads_grad(buckets, zh)
        qv_sums = qkv_sums.reshape(3, hz, dp, -1)
        qv_sums = jnp.stack([qv_sums[0], qv_sums[2]]).transpose(2, 0, 1, 3).reshape(1, dp, -1)
        mine = (jnp.arange(tz) == place).astype(F32).reshape(tz, 1, 1)
        small_grads[l] = jnp.concatenate(
            [
                mine * qv_sums,
                up_bias_sum.reshape(tz, up_bias.shape[1], dp, -1).transpose(0, 2, 1, 3).reshape(tz, dp, -1),
                jnp.stack([sums1[0], sums2[0]]).reshape(2, dp, tz, -1).transpose(2, 1, 0, 3).reshape(tz, dp, -1),
                jnp.stack([sums1[2], sums1[1], sums2[2], sums2[1]])
                .reshape(4, dp, tz, -1).transpose(2, 1, 0, 3).reshape(tz, dp, -1),
            ],
            axis=-1,
        )
        if l > 0:
            g2, gf, sums2 = sum_norm_back(scal, g1, back, kept[l - 1][10], kept[l - 1][11], gain_rows[l - 1][1])
        else:
            input_grad = turn((g1 + add(*back)).astype(BF16))
        rows = d_heads.shape[0]
        results[l] = (
            d_heads[:, :qkv_cols].reshape(rows, 3, -1).transpose(1, 0, 2), d_heads[:, qkv_cols:], d_up, d_down
        )

    small_out = scatter_small(jnp.stack(small_grads, axis=2).reshape(tz, dp, -1), where).reshape(layers, -1)
    qkv_grad, out_grad, up_grad, down_grad = (jnp.stack([entry[i] for entry in results]) for i in range(4))
    qv_bias_grad = small_out[:, cuts[0] : cuts[1]].reshape(qv_bias.shape)
    up_bias_grad = small_out[:, cuts[1] : cuts[2]].reshape(up_bias.shape)
    gains_grad = small_out[:, cuts[2] : cuts[3]].reshape(gains.shape)
    shifts_grad = small_out[:, cuts[3] : cuts[4]].reshape(shifts.shape)
    all_grads = (qkv_grad, qv_bias_grad, out_grad, up_grad, up_bias_grad, down_grad, gains_grad, shifts_grad)
    local_squares = sum(jnp.sum(member * member) for member in all_grads)
    entry_count = LAYERS * (4 * D * D + 2 * D * FF + FF + 8 * D)
    grad_rms = jnp.sqrt(sum_all(local_squares) / entry_count)
    return (
        layer_output, input_grad, qkv_grad, qv_bias_grad, out_grad, up_grad, up_bias_grad, down_grad, gains_grad,
        shifts_grad, grad_rms,
    )


def solution(mesh):
    dp, tensor = mesh.shape["dp"], mesh.shape["tensor"]
    fine = Mesh(mesh.devices.reshape(dp // 2, 2, 2, tensor // 2), ("q", "c", "zh", "zl"))
    data, model = ("q", "c"), ("zh", "zl")
    both = data + model
    weight3, weight4 = P(None, data, model), P(None, None, data, model)
    in_specs = (
        P(both, None), P(data, None), weight4, P(None, None, model, data), weight3, weight3, P(None, model, data),
        weight3, P(None, None, both), P(None, None, both), P(both, None),
    )
    out_specs = (
        P(both, None), P(both, None), weight4, P(None, None, model, data), weight3, weight3, P(None, model, data),
        weight3, P(None, None, both), P(None, None, both), P(),
    )
    return jax.shard_map(on_device, mesh=fine, in_specs=in_specs, out_specs=out_specs, check_vma=False)
```

time: 2260 us -> 1270 us (0.56)
  waiting for transfers between devices: 1570 us -> 528 us
  starting transfers between devices: 35.6 us -> 173 us
  blocking collectives: 86.1 us -> 0 us
    reduce_scatter x6 -> x0, waiting for transfers between devices: 844 us -> none  [scatter_sum(): lax.psum_scatter(blocks.reshape(-1, blocks.shape[2]), ALL, scatter_dimens...]
    ppermute x29 -> x131, waiting for transfers between devices: 224 us -> 528 us  [the longest x118 458 us: flip(): lax.ppermute(values_in, axes, [(a, a ^ mask) for a in range(lax.axis_size...]
    unnamed x20 -> x0, waiting for transfers between devices: 276 us -> none
    all_gather x8 -> x0, waiting for transfers between devices: 225 us -> none  [gather_blocks(): gathered = lax.all_gather(shard, ALL, axis=0, tiled=True)]
    ppermute x29 -> x131, starting transfers between devices: 34.9 us -> 173 us  [the longest x118 132 us: flip(): lax.ppermute(values_in, axes, [(a, a ^ mask) for a in range(lax.axis_size...]
    all_gather x1 -> x0, blocking collectives: 44.3 us -> none  [on_device(): lax.all_gather(small, ALL, axis=0, tiled=False).reshape(tz, dp, layers, -1)]
    psum x1 -> x0, blocking collectives: 41.8 us -> none  [on_device(): grad_rms = jnp.sqrt(lax.psum(local_squares, ALL) / entry_count)]
    pallas_call x29 -> x32, Pallas kernels: 448 us -> 469 us  [call(): pl.pallas_call(body, grid_spec=pltpu.PrefetchScalarGridSpec(num_scalar_pr...]
  transfers between devices with their start and end apart: 46 -> 131, of which waited for: 29 -> 50; matrix products, arithmetic and copies ran while one was open for 3% -> 5% of each run, Pallas kernels for 11% -> 29%
where the time goes in v2:
time: 1270 us
  waiting for transfers between devices  528 us (42%)
  Pallas kernels  469 us (37%)
  starting transfers between devices  173 us (14%)
  local copies, waits for them, and re-layouts  50.7 us (4%)
  other arithmetic  35.8 us (3%)
    pallas_call x32, Pallas kernels, call(): pl.pallas_call(body, grid_spec=pltpu.PrefetchScalarGridSpec(num_scalar_pr...  469 us
    ppermute x118, waiting for transfers between devices, flip(): lax.ppermute(values_in, axes, [(a, a ^ mask) for a in range(lax.axis_size...  458 us
    ppermute x118, starting transfers between devices, flip(): lax.ppermute(values_in, axes, [(a, a ^ mask) for a in range(lax.axis_size...  132 us
    ppermute x9, waiting for transfers between devices, turn(): lax.ppermute(values_in, ('c', 'zh'), [(2 * a + b, 2 * b + a) for a in ran...  69.7 us
    ppermute x9, starting transfers between devices, turn(): lax.ppermute(values_in, ('c', 'zh'), [(2 * a + b, 2 * b + a) for a in ran...  39.1 us
  transfers between devices with their start and end apart: 131, of which 50 were waited for; matrix products, arithmetic and copies ran while one was open for 5% of the time, Pallas kernels for 29%

profile of v2, /device:TPU:1, one launch (start us, length us, event | category | flops | bytes accessed | tf_op | source)
XLA Modules:
  0.0 1265.6 jit_solution(17960949339814291605)
XLA Ops:
  16.4 12.1 collective-permute-done.10
  59.6 62.5 %collective-permute-done.45 = bf16[128,1024]{1,0:T(8,128)(2,1)S(1)} collective-permute-done((bf16[128,1024]{1,0:T(8,128)(2,1)S(1)}, bf16[128,1024]{1,0:T(8,128)(2,1)S(1)}, u32[]{:S(2)}, u32[]{:S(2)}) %collective-permute-start.45) | collective-permute-done | bytes 262176 | tf_op jit(solution)/shard_map/ppermute | solution.py:764
  139.3 35.3 %collective-permute-done.54 = bf16[2,2,128,1024]{3,2,1,0:T(8,128)(2,1)} collective-permute-done((bf16[2,2,128,1024]{3,2,1,0:T(8,128)(2,1)}, bf16[2,2,128,1024]{3,2,1,0:T(8,128)(2,1)}, u32[]{:S(2)}, u32[]{:S(2)}) %collective-permute-start.54) | collective-permute-done | bytes 1048608 | tf_op jit(solution)/shard_map/ppermute | solution.py:760
  182.6 17.3 %collective-permute-done.34.refs_2_ = bf16[4,1,128,1024]{3,2,1,0:T(8,128)(2,1)} collective-permute-done((bf16[4,1,128,1024]{3,2,1,0:T(8,128)(2,1)}, bf16[4,1,128,1024]{3,2,1,0:T(8,128)(2,1)}, u32[]{:S(2)}, u32[]{:S(2)}) %collective-permute-start.34) | collective-permute-done | bytes 1048608 | tf_op jit(solution)/shard_map/ppermute | solution.py:760
  205.3 18.8 %collective-permute-done.4.refs_3_ = bf16[512,1024]{1,0:T(8,128)(2,1)} collective-permute-done((bf16[512,1024]{1,0:T(8,128)(2,1)}, bf16[512,1024]{1,0:T(8,128)(2,1)}, u32[]{:S(2)}, u32[]{:S(2)}) %collective-permute-start.4) | collective-permute-done | bytes 1048608 | tf_op jit(solution)/shard_map/ppermute | solution.py:760
  238.6 31.6 %attend_forward.2 = (bf16[4,512,256]{2,1,0:T(8,128)(2,1)}, f32[256,2048]{1,0:T(8,128)}, f32[8,2048]{1,0:T(8,128)}) custom-call(s32[4]{0:T(128)} %bitcast.333, bf16[4,512,768]{2,1,0:T(8,128)(2,1)} %project_qkv.2.qkv_ref), custom_call_target="tpu_custom_call" | custom-call | flops 17179869184 | bytes 6291456 | tf_op jit(solution)/shard_map/attend_forward/pallas_call | solution.py:48
  290.1 13.0 %collective-permute-done.17.refs_1_ = bf16[512,1024]{1,0:T(8,128)(2,1)} collective-permute-done((bf16[512,1024]{1,0:T(8,128)(2,1)}, bf16[512,1024]{1,0:T(8,128)(2,1)}, u32[]{:S(2)}, u32[]{:S(2)}) %collective-permute-start.17) | collective-permute-done | bytes 1048608 | tf_op jit(solution)/shard_map/ppermute | solution.py:760
  312.4 14.1 %collective-permute-done.19.refs_3_ = bf16[512,1024]{1,0:T(8,128)(2,1)} collective-permute-done((bf16[512,1024]{1,0:T(8,128)(2,1)}, bf16[512,1024]{1,0:T(8,128)(2,1)}, u32[]{:S(2)}, u32[]{:S(2)}) %collective-permute-start.19) | collective-permute-done | bytes 1048608 | tf_op jit(solution)/shard_map/ppermute | solution.py:760
  328.6 19.8 %norm_up.2 = (f32[512,1024]{1,0:T(8,128)}, bf16[512,1024]{1,0:T(8,128)(2,1)}, f32[512,128]{1,0:T(8,128)}, bf16[512,4096]{1,0:T(8,128)(2,1)}, bf16[512,4096]{1,0:T(8,128)(2,1)}) custom-call(s32[5]{0:T(128)} %stack.212.scal_ref, f32[512,1024]{1,0:T(8,128)} %convert_element_type.314.prev_ref, bf16[512,1024]{1,0:T(8,128)(2,1)} %get-tuple-element.96.refs_0_, ...), custom_call_target="tpu_custom_call" | custom-call | flops 4294967296 | bytes 27262976 | tf_op jit(solution)/shard_map/norm_up/pallas_call | solution.py:48
  349.3 14.3 %down_norm.2 = (f32[512,1024]{1,0:T(8,128)}, bf16[512,1024]{1,0:T(8,128)(2,1)}, f32[512,128]{1,0:T(8,128)}) custom-call(s32[5]{0:T(128)} %stack.212.scal_ref, bf16[512,4096]{1,0:T(8,128)(2,1)} %get-tuple-element.100.act_ref.y_ref, f32[512,1024]{1,0:T(8,128)} %get-tuple-element.101.prev_ref.n_ref, f32[8,1024]{1,0:T(8,128)} %stack.231.vec_ref, ...), custom_call_target="tpu_custom_call" | custom-call | flops 4294967296 | bytes 17825792 | tf_op jit(solution)/shard_map/down_norm/pallas_call | solution.py:48
  390.7 20.9 %collective-permute-done.44.refs_3_ = bf16[512,1024]{1,0:T(8,128)(2,1)S(1)} collective-permute-done((bf16[512,1024]{1,0:T(8,128)(2,1)}, bf16[512,1024]{1,0:T(8,128)(2,1)S(1)}, u32[]{:S(2)}, u32[]{:S(2)}) %collective-permute-start.44) | collective-permute-done | bytes 1048608 | tf_op jit(solution)/shard_map/ppermute | solution.py:760
  422.1 31.7 %attend_forward.3 = (bf16[4,512,256]{2,1,0:T(8,128)(2,1)}, f32[256,2048]{1,0:T(8,128)}, f32[8,2048]{1,0:T(8,128)}) custom-call(s32[4]{0:T(128)} %bitcast.334, bf16[4,512,768]{2,1,0:T(8,128)(2,1)} %project_qkv.3.qkv_ref), custom_call_target="tpu_custom_call" | custom-call | flops 17179869184 | bytes 6291456 | tf_op jit(solution)/shard_map/attend_forward/pallas_call | solution.py:48
  464.8 22.4 %collective-permute-done.50.refs_1_ = bf16[512,1024]{1,0:T(8,128)(2,1)S(1)} collective-permute-done((bf16[512,1024]{1,0:T(8,128)(2,1)}, bf16[512,1024]{1,0:T(8,128)(2,1)S(1)}, u32[]{:S(2)}, u32[]{:S(2)}) %collective-permute-start.50) | collective-permute-done | bytes 1048608 | tf_op jit(solution)/shard_map/ppermute | solution.py:760
  490.3 20.0 %collective-permute-done.52.refs_3_ = bf16[512,1024]{1,0:T(8,128)(2,1)} collective-permute-done((bf16[512,1024]{1,0:T(8,128)(2,1)}, bf16[512,1024]{1,0:T(8,128)(2,1)}, u32[]{:S(2)}, u32[]{:S(2)}) %collective-permute-start.52) | collective-permute-done | bytes 1048608 | tf_op jit(solution)/shard_map/ppermute | solution.py:760
  515.7 19.4 %norm_up.3 = (f32[512,1024]{1,0:T(8,128)}, bf16[512,1024]{1,0:T(8,128)(2,1)}, f32[512,128]{1,0:T(8,128)}, bf16[512,4096]{1,0:T(8,128)(2,1)}, bf16[512,4096]{1,0:T(8,128)(2,1)}) custom-call(s32[5]{0:T(128)} %stack.212.scal_ref, f32[512,1024]{1,0:T(8,128)} %get-tuple-element.102.prev_ref.refs_4_, bf16[512,1024]{1,0:T(8,128)(2,1)} %get-tuple-element.105.refs_0_, ...), custom_call_target="tpu_custom_call" | custom-call | flops 4294967296 | bytes 27262976 | tf_op jit(solution)/shard_map/norm_up/pallas_call | solution.py:48
  535.2 14.4 %down_norm.3 = (f32[512,1024]{1,0:T(8,128)}, bf16[512,1024]{1,0:T(8,128)(2,1)}, f32[512,128]{1,0:T(8,128)}) custom-call(s32[5]{0:T(128)} %stack.212.scal_ref, bf16[512,4096]{1,0:T(8,128)(2,1)} %get-tuple-element.109.act_ref.y_ref, f32[512,1024]{1,0:T(8,128)} %get-tuple-element.110.prev_ref.n_ref, f32[8,1024]{1,0:T(8,128)} %stack.242.vec_ref, ...), custom_call_target="tpu_custom_call" | custom-call | flops 4294967296 | bytes 17825792 | tf_op jit(solution)/shard_map/down_norm/pallas_call | solution.py:48
  556.2 11.5 units_back.2
  568.3 15.0 %up_back.2 = (f32[512,1024]{1,0:T(8,128)}, bf16[512,1024]{1,0:T(8,128)(2,1)}, f32[8,1024]{1,0:T(8,128)}) custom-call(s32[5]{0:T(128)} %stack.212.scal_ref, bf16[512,4096]{1,0:T(8,128)(2,1)} %get-tuple-element.116.gu_ref.y_ref, f32[512,1024]{1,0:T(8,128)} %get-tuple-element.117.res_ref, f32[512,1024]{1,0:T(8,128)} %get-tuple-element.110.prev_ref.n_ref, ...), custom_call_target="tpu_custom_call" | custom-call | flops 4294967296 | bytes 20971520 | tf_op jit(solution)/shard_map/up_back/pallas_call | solution.py:48
  600.9 30.1 %collective-permute-done.68.refs_3_.refs_7_ = bf16[512,1024]{1,0:T(8,128)(2,1)S(1)} collective-permute-done((bf16[512,1024]{1,0:T(8,128)(2,1)}, bf16[512,1024]{1,0:T(8,128)(2,1)S(1)}, u32[]{:S(2)}, u32[]{:S(2)}) %collective-permute-start.68) | collective-permute-done | bytes 1048608 | tf_op jit(solution)/shard_map/ppermute | solution.py:760
  638.8 57.7 %attend_backward.2.block_ref.refs_8_ = bf16[4,512,768]{2,1,0:T(8,128)(2,1)} custom-call(s32[4]{0:T(128)} %bitcast.335, bf16[4,512,768]{2,1,0:T(8,128)(2,1)} %project_qkv.3.qkv_ref, bf16[4,512,256]{2,1,0:T(8,128)(2,1)} %project_gc.2.grad_ref, f32[256,2048]{1,0:T(8,128)} %get-tuple-element.121.wide_ref, f32[8,2048]{1,0:T(8,128)} %get-tuple-element.122.lse_ref), custom_call_target="tpu_custom_call" | custom-call | flops 30064771072 | bytes 10485760 | tf_op jit(solution)/shard_map/attend_backward/pallas_call | solution.py:48
  731.3 21.7 %collective-permute-done.71.refs_3_ = bf16[512,1024]{1,0:T(8,128)(2,1)S(1)} collective-permute-done((bf16[512,1024]{1,0:T(8,128)(2,1)}, bf16[512,1024]{1,0:T(8,128)(2,1)S(1)}, u32[]{:S(2)}, u32[]{:S(2)}) %collective-permute-start.71) | collective-permute-done | bytes 1048608 | tf_op jit(solution)/shard_map/ppermute | solution.py:760
  762.1 11.5 units_back.3
  774.2 14.9 %up_back.3 = (f32[512,1024]{1,0:T(8,128)}, bf16[512,1024]{1,0:T(8,128)(2,1)}, f32[8,1024]{1,0:T(8,128)}) custom-call(s32[5]{0:T(128)} %stack.212.scal_ref, bf16[512,4096]{1,0:T(8,128)(2,1)} %get-tuple-element.130.gu_ref.y_ref, f32[512,1024]{1,0:T(8,128)} %get-tuple-element.131.res_ref, f32[512,1024]{1,0:T(8,128)} %get-tuple-element.101.prev_ref.n_ref, ...), custom_call_target="tpu_custom_call" | custom-call | flops 4294967296 | bytes 20971520 | tf_op jit(solution)/shard_map/up_back/pallas_call | solution.py:48
  791.7 11.4 heads_grad.3
  820.5 16.6 %collective-permute-done.74.refs_3_.refs_7_ = bf16[512,1024]{1,0:T(8,128)(2,1)} collective-permute-done((bf16[512,1024]{1,0:T(8,128)(2,1)}, bf16[512,1024]{1,0:T(8,128)(2,1)}, u32[]{:S(2)}, u32[]{:S(2)}) %collective-permute-start.74) | collective-permute-done | bytes 1048608 | tf_op jit(solution)/shard_map/ppermute | solution.py:760
  850.1 57.5 %attend_backward.3.block_ref.refs_8_ = bf16[4,512,768]{2,1,0:T(8,128)(2,1)} custom-call(s32[4]{0:T(128)} %bitcast.336, bf16[4,512,768]{2,1,0:T(8,128)(2,1)} %project_qkv.2.qkv_ref, bf16[4,512,256]{2,1,0:T(8,128)(2,1)} %project_gc.3.grad_ref, f32[256,2048]{1,0:T(8,128)} %get-tuple-element.135.wide_ref, f32[8,2048]{1,0:T(8,128)} %get-tuple-element.136.lse_ref), custom_call_target="tpu_custom_call" | custom-call | flops 30064771072 | bytes 10485760 | tf_op jit(solution)/shard_map/attend_backward/pallas_call | solution.py:48
  907.6 11.6 heads_grad.2
  1033.8 12.9 %collective-permute-done.118 = bf16[4,128,1024]{2,1,0:T(8,128)(2,1)} collective-permute-done((bf16[4,128,1024]{2,1,0:T(8,128)(2,1)}, bf16[4,128,1024]{2,1,0:T(8,128)(2,1)}, u32[]{:S(2)}, u32[]{:S(2)}) %collective-permute-start.118) | collective-permute-done | bytes 1048608 | tf_op jit(solution)/shard_map/ppermute | solution.py:760
  1101.4 15.0 %collective-permute-done.122 = bf16[2,128,1024]{2,1,0:T(8,128)(2,1)S(1)} collective-permute-done((bf16[2,128,1024]{2,1,0:T(8,128)(2,1)}, bf16[2,128,1024]{2,1,0:T(8,128)(2,1)S(1)}, u32[]{:S(2)}, u32[]{:S(2)}) %collective-permute-start.122) | collective-permute-done | bytes 524320 | tf_op jit(solution)/shard_map/ppermute | solution.py:760
  1147.1 28.2 %collective-permute-done.100 = bf16[2,128,1024]{2,1,0:T(8,128)(2,1)S(1)} collective-permute-done((bf16[2,128,1024]{2,1,0:T(8,128)(2,1)S(1)}, bf16[2,128,1024]{2,1,0:T(8,128)(2,1)S(1)}, u32[]{:S(2)}, u32[]{:S(2)}) %collective-permute-start.100) | collective-permute-done | bytes 524320 | tf_op jit(solution)/shard_map/ppermute | solution.py:760
  1176.6 11.7 collective-permute-done.114
  1189.2 23.9 %collective-permute-done.101 = bf16[2,128,1024]{2,1,0:T(8,128)(2,1)S(1)} collective-permute-done((bf16[2,128,1024]{2,1,0:T(8,128)(2,1)S(1)}, bf16[2,128,1024]{2,1,0:T(8,128)(2,1)S(1)}, u32[]{:S(2)}, u32[]{:S(2)}) %collective-permute-start.101) | collective-permute-done | bytes 524320 | tf_op jit(solution)/shard_map/ppermute | solution.py:760
  (604 shorter events, 536.5 us)
Async XLA Ops:
  41.2 82.2 %collective-permute-start.53 = (bf16[2,128,1024]{2,1,0:T(8,128)(2,1)S(1)}, bf16[2,128,1024]{2,1,0:T(8,128)(2,1)S(1)}, u32[]{:S(2)}, u32[]{:S(2)}) collective-permute-start(bf16[2,128,1024]{2,1,0:T(8,128)(2,1)S(1)} %get-tuple-element.235), channel_id=1, source_target_pairs={{0,1},{1,0},{2,3},{3,2},{4,5},{5,4},{6,7},{7,6},{8,9},{9,8},{10,11... | collective-permute-start | bytes 1572872 | tf_op jit(solution)/shard_map/ppermute | solution.py:760
  41.2 83.4 %collective-permute-start.21 = (bf16[2,1,128,1024]{3,2,1,0:T(8,128)(2,1)S(1)}, bf16[2,1,128,1024]{3,2,1,0:T(8,128)(2,1)S(1)}, u32[]{:S(2)}, u32[]{:S(2)}) collective-permute-start(bf16[2,1,128,1024]{3,2,1,0:T(8,128)(2,1)S(1)} %pad_maximum_fusion.8), channel_id=1, source_target_pairs={{0,2},{2,0},{1,3},{3,1},{4,6},{6,4},{5,7},{7,5},{8,10},{10,8},{9,1... | collective-permute-start | bytes 1572872 | tf_op jit(solution)/shard_map/ppermute | solution.py:760
  43.6 95.4 %collective-permute-start = (bf16[512,1024]{1,0:T(8,128)(2,1)}, bf16[512,1024]{1,0:T(8,128)(2,1)}, u32[]{:S(2)}, u32[]{:S(2)}) collective-permute-start(bf16[512,1024]{1,0:T(8,128)(2,1)} %param.11), channel_id=1, source_target_pairs={{0,0},{2,4},{4,2},{6,6},{1,1},{3,5},{5,3},{7,7},{8,8},{10,12},{12,... | collective-permute-start | bytes 3145736 | tf_op jit(solution)/shard_map/ppermute | solution.py:764
  49.0 77.7 %collective-permute-start.32 = (bf16[2,1,128,1024]{3,2,1,0:T(8,128)(2,1)S(1)}, bf16[2,1,128,1024]{3,2,1,0:T(8,128)(2,1)S(1)}, u32[]{:S(2)}, u32[]{:S(2)}) collective-permute-start(bf16[2,1,128,1024]{3,2,1,0:T(8,128)(2,1)S(1)} %pad_maximum_fusion.9), channel_id=1, source_target_pairs={{0,2},{2,0},{1,3},{3,1},{4,6},{6,4},{5,7},{7,5},{8,10},{10,8},{9,1... | collective-permute-start | bytes 1572872 | tf_op jit(solution)/shard_map/ppermute | solution.py:760
  53.3 68.8 %collective-permute-start.45 = (bf16[128,1024]{1,0:T(8,128)(2,1)S(1)}, bf16[128,1024]{1,0:T(8,128)(2,1)S(1)}, u32[]{:S(2)}, u32[]{:S(2)}) collective-permute-start(bf16[128,1024]{1,0:T(8,128)(2,1)S(1)} %pad_maximum_fusion.13), channel_id=1, source_target_pairs={{0,0},{2,4},{4,2},{6,6},{1,1},{3,5},{5,3},{7,7},{8,8},{10,12},{12,... | collective-permute-start | bytes 786440 | tf_op jit(solution)/shard_map/ppermute | solution.py:764
  127.5 47.2 %collective-permute-start.54 = (bf16[2,2,128,1024]{3,2,1,0:T(8,128)(2,1)}, bf16[2,2,128,1024]{3,2,1,0:T(8,128)(2,1)}, u32[]{:S(2)}, u32[]{:S(2)}) collective-permute-start(bf16[2,2,128,1024]{3,2,1,0:T(8,128)(2,1)} %pad_maximum_fusion.3), channel_id=1, source_target_pairs={{0,2},{2,0},{1,3},{3,1},{4,6},{6,4},{5,7},{7,5},{8,10},{10,8},{9,1... | collective-permute-start | bytes 3145736 | tf_op jit(solution)/shard_map/ppermute | solution.py:760
  234.8 47.0 %collective-permute-start.38 = (bf16[4,1,128,1024]{3,2,1,0:T(8,128)(2,1)}, bf16[4,1,128,1024]{3,2,1,0:T(8,128)(2,1)}, u32[]{:S(2)}, u32[]{:S(2)}) collective-permute-start(bf16[4,1,128,1024]{3,2,1,0:T(8,128)(2,1)} %collective-permute-done.33.refs_1_), channel_id=1, source_target_pairs={{0,4},{4,0},{1,5},{5,1},{2,6},{6,2},{3,7},{7,3},{8,12},{12,8},{9,1... | collective-permute-start | bytes 3145736 | tf_op jit(solution)/shard_map/ppermute | solution.py:760
  235.3 48.6 %collective-permute-start.39 = (bf16[4,1,128,1024]{3,2,1,0:T(8,128)(2,1)}, bf16[4,1,128,1024]{3,2,1,0:T(8,128)(2,1)}, u32[]{:S(2)}, u32[]{:S(2)}) collective-permute-start(bf16[4,1,128,1024]{3,2,1,0:T(8,128)(2,1)} %collective-permute-done.34.refs_2_), channel_id=1, source_target_pairs={{0,4},{4,0},{1,5},{5,1},{2,6},{6,2},{3,7},{7,3},{8,12},{12,8},{9,1... | collective-permute-start | bytes 3145736 | tf_op jit(solution)/shard_map/ppermute | solution.py:760
  279.2 47.3 %collective-permute-start.19 = (bf16[512,1024]{1,0:T(8,128)(2,1)}, bf16[512,1024]{1,0:T(8,128)(2,1)}, u32[]{:S(2)}, u32[]{:S(2)}) collective-permute-start(bf16[512,1024]{1,0:T(8,128)(2,1)} %get-tuple-element.99), channel_id=1, source_target_pairs={{0,5},{1,4},{4,1},{5,0},{2,7},{3,6},{6,3},{7,2},{8,13},{9,12},{12,... | collective-permute-start | bytes 3145736 | tf_op jit(solution)/shard_map/ppermute | solution.py:760
  283.9 81.7 %collective-permute-start.55 = (bf16[4,2,128,1024]{3,2,1,0:T(8,128)(2,1)S(1)}, bf16[4,2,128,1024]{3,2,1,0:T(8,128)(2,1)}, u32[]{:S(2)}, u32[]{:S(2)}) collective-permute-start(bf16[4,2,128,1024]{3,2,1,0:T(8,128)(2,1)S(1)} %pad_maximum_fusion.refs_6_.refs_0_), channel_id=1, source_target_pairs={{0,8},{8,0},{16,24},{24,16},{1,9},{9,1},{17,25},{25,17},{2,10},{10... | collective-permute-start | bytes 6291464 | tf_op jit(solution)/shard_map/ppermute | solution.py:760
  288.7 79.0 %collective-permute-start.56 = (bf16[4,2,128,1024]{3,2,1,0:T(8,128)(2,1)S(1)}, bf16[4,2,128,1024]{3,2,1,0:T(8,128)(2,1)}, u32[]{:S(2)}, u32[]{:S(2)}) collective-permute-start(bf16[4,2,128,1024]{3,2,1,0:T(8,128)(2,1)S(1)} %pad_maximum_fusion.refs_6_.refs_0_), channel_id=1, source_target_pairs={{0,16},{8,24},{16,0},{24,8},{1,17},{9,25},{17,1},{25,9},{2,18},{10... | collective-permute-start | bytes 6291464 | tf_op jit(solution)/shard_map/ppermute | solution.py:760
  309.3 54.4 %collective-permute-start.47 = (bf16[2,128,1024]{2,1,0:T(8,128)(2,1)S(1)}, bf16[2,128,1024]{2,1,0:T(8,128)(2,1)S(1)}, u32[]{:S(2)}, u32[]{:S(2)}) collective-permute-start(bf16[2,128,1024]{2,1,0:T(8,128)(2,1)S(1)} %pad_maximum_fusion.10.refs_5_.refs_0_.refs_4_), channel_id=1, source_target_pairs={{0,8},{8,0},{16,24},{24,16},{1,9},{9,1},{17,25},{25,17},{2,10},{10... | collective-permute-start | bytes 1572872 | tf_op jit(solution)/shard_map/ppermute | solution.py:760
  363.9 47.7 %collective-permute-start.44 = (bf16[512,1024]{1,0:T(8,128)(2,1)}, bf16[512,1024]{1,0:T(8,128)(2,1)S(1)}, u32[]{:S(2)}, u32[]{:S(2)}) collective-permute-start(bf16[512,1024]{1,0:T(8,128)(2,1)} %get-tuple-element.103.refs_0_), channel_id=1, source_target_pairs={{0,5},{1,4},{4,1},{5,0},{2,7},{3,6},{6,3},{7,2},{8,13},{9,12},{12,... | collective-permute-start | bytes 3145736 | tf_op jit(solution)/shard_map/ppermute | solution.py:760
  367.7 93.6 %collective-permute-start.59 = (bf16[4,2,128,1024]{3,2,1,0:T(8,128)(2,1)S(1)}, bf16[4,2,128,1024]{3,2,1,0:T(8,128)(2,1)S(1)}, u32[]{:S(2)}, u32[]{:S(2)}) collective-permute-start(bf16[4,2,128,1024]{3,2,1,0:T(8,128)(2,1)S(1)} %pad_maximum_fusion.refs_6_.refs_0_), channel_id=1, source_target_pairs={{0,4},{4,0},{1,5},{5,1},{2,6},{6,2},{3,7},{7,3},{8,12},{12,8},{9,1... | collective-permute-start | bytes 6291464 | tf_op jit(solution)/shard_map/ppermute | solution.py:760
  379.8 82.8 %collective-permute-start.57 = (bf16[2,2,128,1024]{3,2,1,0:T(8,128)(2,1)S(1)}, bf16[2,2,128,1024]{3,2,1,0:T(8,128)(2,1)S(1)}, u32[]{:S(2)}, u32[]{:S(2)}) collective-permute-start(bf16[2,2,128,1024]{3,2,1,0:T(8,128)(2,1)S(1)} %slice.537), channel_id=1, source_target_pairs={{0,8},{8,0},{16,24},{24,16},{1,9},{9,1},{17,25},{25,17},{2,10},{10... | collective-permute-start | bytes 3145736 | tf_op jit(solution)/shard_map/ppermute | solution.py:760
  388.7 74.7 %collective-permute-start.58 = (bf16[2,2,128,1024]{3,2,1,0:T(8,128)(2,1)S(1)}, bf16[2,2,128,1024]{3,2,1,0:T(8,128)(2,1)}, u32[]{:S(2)}, u32[]{:S(2)}) collective-permute-start(bf16[2,2,128,1024]{3,2,1,0:T(8,128)(2,1)S(1)} %slice.538), channel_id=1, source_target_pairs={{0,16},{8,24},{16,0},{24,8},{1,17},{9,25},{17,1},{25,9},{2,18},{10... | collective-permute-start | bytes 3145736 | tf_op jit(solution)/shard_map/ppermute | solution.py:760
  389.7 124.7 %collective-permute-start.60 = (bf16[4,2,128,1024]{3,2,1,0:T(8,128)(2,1)}, bf16[4,2,128,1024]{3,2,1,0:T(8,128)(2,1)}, u32[]{:S(2)}, u32[]{:S(2)}) collective-permute-start(bf16[4,2,128,1024]{3,2,1,0:T(8,128)(2,1)} %collective-permute-done.55.refs_7_.refs_1_), channel_id=1, source_target_pairs={{0,4},{4,0},{1,5},{5,1},{2,6},{6,2},{3,7},{7,3},{8,12},{12,8},{9,1... | collective-permute-start | bytes 6291464 | tf_op jit(solution)/shard_map/ppermute | solution.py:760
  412.6 101.8 %collective-permute-start.61 = (bf16[4,2,128,1024]{3,2,1,0:T(8,128)(2,1)}, bf16[4,2,128,1024]{3,2,1,0:T(8,128)(2,1)}, u32[]{:S(2)}, u32[]{:S(2)}) collective-permute-start(bf16[4,2,128,1024]{3,2,1,0:T(8,128)(2,1)} %collective-permute-done.56.refs_8_.refs_2_), channel_id=1, source_target_pairs={{0,4},{4,0},{1,5},{5,1},{2,6},{6,2},{3,7},{7,3},{8,12},{12,8},{9,1... | collective-permute-start | bytes 6291464 | tf_op jit(solution)/shard_map/ppermute | solution.py:760
  463.4 46.9 %collective-permute-start.52 = (bf16[512,1024]{1,0:T(8,128)(2,1)}, bf16[512,1024]{1,0:T(8,128)(2,1)}, u32[]{:S(2)}, u32[]{:S(2)}) collective-permute-start(bf16[512,1024]{1,0:T(8,128)(2,1)} %get-tuple-element.108), channel_id=1, source_target_pairs={{0,5},{1,4},{4,1},{5,0},{2,7},{3,6},{6,3},{7,2},{8,13},{9,12},{12,... | collective-permute-start | bytes 3145736 | tf_op jit(solution)/shard_map/ppermute | solution.py:760
  706.6 46.4 %collective-permute-start.71 = (bf16[512,1024]{1,0:T(8,128)(2,1)}, bf16[512,1024]{1,0:T(8,128)(2,1)S(1)}, u32[]{:S(2)}, u32[]{:S(2)}) collective-permute-start(bf16[512,1024]{1,0:T(8,128)(2,1)} %get-tuple-element.126), channel_id=1, source_target_pairs={{0,5},{1,4},{4,1},{5,0},{2,7},{3,6},{6,3},{7,2},{8,13},{9,12},{12,... | collective-permute-start | bytes 3145736 | tf_op jit(solution)/shard_map/ppermute | solution.py:760
  719.7 253.7 %collective-permute-start.103 = (bf16[4,4,128,1024]{3,2,1,0:T(8,128)(2,1)}, bf16[4,4,128,1024]{3,2,1,0:T(8,128)(2,1)}, u32[]{:S(2)}, u32[]{:S(2)}) collective-permute-start(bf16[4,4,128,1024]{3,2,1,0:T(8,128)(2,1)} %grad_theirs.5), channel_id=1, source_target_pairs={{0,4},{4,0},{1,5},{5,1},{2,6},{6,2},{3,7},{7,3},{8,12},{12,8},{9,1... | collective-permute-start | bytes 12582920 | tf_op jit(solution)/shard_map/ppermute | solution.py:760
  727.4 271.4 %collective-permute-start.117 = (bf16[4,4,128,1024]{3,2,1,0:T(8,128)(2,1)}, bf16[4,4,128,1024]{3,2,1,0:T(8,128)(2,1)}, u32[]{:S(2)}, u32[]{:S(2)}) collective-permute-start(bf16[4,4,128,1024]{3,2,1,0:T(8,128)(2,1)} %grad_theirs.7), channel_id=1, source_target_pairs={{0,4},{4,0},{1,5},{5,1},{2,6},{6,2},{3,7},{7,3},{8,12},{12,8},{9,1... | collective-permute-start | bytes 12582920 | tf_op jit(solution)/shard_map/ppermute | solution.py:760
  791.1 46.0 %collective-permute-start.74 = (bf16[512,1024]{1,0:T(8,128)(2,1)}, bf16[512,1024]{1,0:T(8,128)(2,1)}, u32[]{:S(2)}, u32[]{:S(2)}) collective-permute-start(bf16[512,1024]{1,0:T(8,128)(2,1)} %get-tuple-element.134.refs_0_.refs_4_), channel_id=1, source_target_pairs={{0,5},{1,4},{4,1},{5,0},{2,7},{3,6},{6,3},{7,2},{8,13},{9,12},{12,... | collective-permute-start | bytes 3145736 | tf_op jit(solution)/shard_map/ppermute | solution.py:760
  813.1 108.3 %collective-permute-start.86 = (bf16[2,128,1024]{2,1,0:T(8,128)(2,1)}, bf16[2,128,1024]{2,1,0:T(8,128)(2,1)S(1)}, u32[]{:S(2)}, u32[]{:S(2)}) collective-permute-start(bf16[2,128,1024]{2,1,0:T(8,128)(2,1)} %get-tuple-element.148), channel_id=1, source_target_pairs={{0,24},{8,16},{16,8},{24,0},{1,25},{9,17},{17,9},{25,1},{2,26},{10... | collective-permute-start | bytes 1572872 | tf_op jit(solution)/shard_map/ppermute | solution.py:760
  816.0 105.5 %collective-permute-start.85 = (bf16[2,128,1024]{2,1,0:T(8,128)(2,1)}, bf16[2,128,1024]{2,1,0:T(8,128)(2,1)}, u32[]{:S(2)}, u32[]{:S(2)}) collective-permute-start(bf16[2,128,1024]{2,1,0:T(8,128)(2,1)} %get-tuple-element.147), channel_id=1, source_target_pairs={{0,16},{8,24},{16,0},{24,8},{1,17},{9,25},{17,1},{25,9},{2,18},{10... | collective-permute-start | bytes 1572872 | tf_op jit(solution)/shard_map/ppermute | solution.py:760
  837.1 89.1 %collective-permute-start.84 = (bf16[2,128,1024]{2,1,0:T(8,128)(2,1)}, bf16[2,128,1024]{2,1,0:T(8,128)(2,1)}, u32[]{:S(2)}, u32[]{:S(2)}) collective-permute-start(bf16[2,128,1024]{2,1,0:T(8,128)(2,1)} %get-tuple-element.146), channel_id=1, source_target_pairs={{0,8},{8,0},{16,24},{24,16},{1,9},{9,1},{17,25},{25,17},{2,10},{10... | collective-permute-start | bytes 1572872 | tf_op jit(solution)/shard_map/ppermute | solution.py:760
  955.0 113.2 %collective-permute-start.96 = (bf16[4,4,128,1024]{3,2,1,0:T(8,128)(2,1)}, bf16[4,4,128,1024]{3,2,1,0:T(8,128)(2,1)}, u32[]{:S(2)}, u32[]{:S(2)}) collective-permute-start(bf16[4,4,128,1024]{3,2,1,0:T(8,128)(2,1)} %grad_theirs.4), channel_id=1, source_target_pairs={{0,4},{4,0},{1,5},{5,1},{2,6},{6,2},{3,7},{7,3},{8,12},{12,8},{9,1... | collective-permute-start | bytes 12582920 | tf_op jit(solution)/shard_map/ppermute | solution.py:760
  967.4 109.6 %collective-permute-start.110 = (bf16[4,4,128,1024]{3,2,1,0:T(8,128)(2,1)}, bf16[4,4,128,1024]{3,2,1,0:T(8,128)(2,1)}, u32[]{:S(2)}, u32[]{:S(2)}) collective-permute-start(bf16[4,4,128,1024]{3,2,1,0:T(8,128)(2,1)} %grad_theirs.6), channel_id=1, source_target_pairs={{0,4},{4,0},{1,5},{5,1},{2,6},{6,2},{3,7},{7,3},{8,12},{12,8},{9,1... | collective-permute-start | bytes 12582920 | tf_op jit(solution)/shard_map/ppermute | solution.py:760
  1024.3 94.3 %collective-permute-start.77 = (bf16[512,1024]{1,0:T(8,128)(2,1)}, bf16[512,1024]{1,0:T(8,128)(2,1)S(1)}, u32[]{:S(2)}, u32[]{:S(2)}) collective-permute-start(bf16[512,1024]{1,0:T(8,128)(2,1)} %get-tuple-element.140), channel_id=1, source_target_pairs={{0,5},{1,4},{4,1},{5,0},{2,7},{3,6},{6,3},{7,2},{8,13},{9,12},{12,... | collective-permute-start | bytes 3145736 | tf_op jit(solution)/shard_map/ppermute | solution.py:760
  1068.1 52.0 %collective-permute-start.76 = (bf16[512,1024]{1,0:T(8,128)(2,1)}, bf16[512,1024]{1,0:T(8,128)(2,1)S(1)}, u32[]{:S(2)}, u32[]{:S(2)}) collective-permute-start(bf16[512,1024]{1,0:T(8,128)(2,1)} %get-tuple-element.139), channel_id=1, source_target_pairs={{0,4},{1,5},{4,0},{5,1},{2,6},{3,7},{6,2},{7,3},{8,12},{9,13},{12,... | collective-permute-start | bytes 3145736 | tf_op jit(solution)/shard_map/ppermute | solution.py:760
  1128.6 127.0 %collective-permute-start.64 = (bf16[512,1024]{1,0:T(8,128)(2,1)}, bf16[512,1024]{1,0:T(8,128)(2,1)S(1)}, u32[]{:S(2)}, u32[]{:S(2)}) collective-permute-start(bf16[512,1024]{1,0:T(8,128)(2,1)} %get-tuple-element.111), channel_id=1, source_target_pairs={{0,0},{2,4},{4,2},{6,6},{1,1},{3,5},{5,3},{7,7},{8,8},{10,12},{12,... | collective-permute-start | bytes 3145736 | tf_op jit(solution)/shard_map/ppermute | solution.py:764
  1134.2 125.3 %collective-permute-start.78 = (bf16[512,1024]{1,0:T(8,128)(2,1)S(1)}, bf16[512,1024]{1,0:T(8,128)(2,1)}, u32[]{:S(2)}, u32[]{:S(2)}) collective-permute-start(bf16[512,1024]{1,0:T(8,128)(2,1)S(1)} %add_convert_fusion), channel_id=1, source_target_pairs={{0,0},{2,4},{4,2},{6,6},{1,1},{3,5},{5,3},{7,7},{8,8},{10,12},{12,... | collective-permute-start | bytes 3145736 | tf_op jit(solution)/shard_map/ppermute | solution.py:764
  (165 other events, 3492.1 us)

commit v3 on v2

--- a/solution.py
+++ b/solution.py
@@ -22,6 +22,7 @@
 MODEL = ("zh", "zl")
 ALL = ("zh", "zl", "q", "c")
 VMEM_LIMIT = 56 * 1024 * 1024
+COST = 1000
 NT = (((1,), (1,)), ((), ()))
 NN = (((1,), (0,)), ((), ()))
 ROWS = 128
@@ -44,23 +45,57 @@
     return jax.ShapeDtypeStruct(shape, kind)
 
 
-def call(body, grid, in_specs, out_specs, out_shape, scratch, args, scalars, flops, traffic, name):
-    return pl.pallas_call(
-        body,
+class Flow:
+    def __init__(self, scal):
+        self.scal, self.before, self.held = scal, [], {}
+
+    def wait(self, *arrays):
+        self.before += arrays
+
+    def hold(self, **arrays):
+        self.held.update(arrays)
+
+    def free(self, name):
+        return self.held.pop(name)
+
+
+def call(flow, body, grid, in_specs, out_specs, out_shape, scratch, args, flops, traffic, name, scalars=None):
+    scalars = (flow.scal,) if scalars is None else scalars
+    single = not isinstance(out_specs, (list, tuple))
+    out_specs = [out_specs] if single else list(out_specs)
+    out_shape = [out_shape] if single else list(out_shape)
+    before, held = flow.before, list(flow.held.items())
+    ns, nb, nh, no = len(scalars), len(before), len(held), len(out_specs)
+    first, last = ns + nb + nh, ns + nb + nh + len(args) + no
+
+    def wrapped(*refs):
+        body(*refs[:ns], *refs[first:last], *refs[last + nh :])
+
+    result = pl.pallas_call(
+        wrapped,
         grid_spec=pltpu.PrefetchScalarGridSpec(
-            num_scalar_prefetch=len(scalars),
+            num_scalar_prefetch=ns,
             grid=grid,
-            in_specs=in_specs,
-            out_specs=out_specs,
+            in_specs=[ANY] * (nb + nh) + list(in_specs),
+            out_specs=out_specs + [ANY] * nh,
             scratch_shapes=scratch,
         ),
-        out_shape=out_shape,
+        out_shape=out_shape + [sds(array.shape, array.dtype) for _, array in held],
+        input_output_aliases={ns + nb + i: no + i for i in range(nh)},
         compiler_params=pltpu.CompilerParams(
             dimension_semantics=("arbitrary",) * len(grid), vmem_limit_bytes=VMEM_LIMIT
         ),
-        cost_estimate=pl.CostEstimate(flops=int(flops), bytes_accessed=int(traffic), transcendentals=0),
+        cost_estimate=pl.CostEstimate(flops=COST, bytes_accessed=COST, transcendentals=0),
         name=name,
-    )(*scalars, *args)
+    )(*scalars, *before, *[array for _, array in held], *args)
+    flow.before = []
+    flow.held = {key: value for (key, _), value in zip(held, result[no:])}
+    return result[0] if single else result[:no]
+
+
+def gate(flow):
+    if flow.held:
+        call(flow, lambda *refs: None, (1,), [], [], [], [], [], 0, 0, "gate")
 
 
 S_P, S_Q, S_C, S_ZH, S_Z = range(5)
@@ -117,6 +152,10 @@
         sums_ref[row : row + 1, :] = jnp.sum(member, 0, keepdims=True)
 
 
+def away(s):
+    return (s & 1) * 2 + s // 2
+
+
 class Streamed:
     def __init__(self, refs, matrix, buffer, sems, scal):
         self.refs, self.matrix, self.buffer, self.sems, self.scal = refs, matrix, buffer, sems, scal
@@ -190,7 +229,7 @@
             yield slice(i * tokens // 2, (i + 1) * tokens // 2), slice(j * width // 2, (j + 1) * width // 2)
 
 
-def norm_up(scal, prev, parts, vec, weight, matrix, bias, count):
+def norm_up(flow, prev, parts, vec, weight, matrix, bias, count):
     tokens = prev.shape[0]
     width = FF // count
 
@@ -221,17 +260,17 @@
 
     column = pl.BlockSpec((tokens, width), lambda s, _: (0, s))
     return call(
-        body, (count,),
+        flow, body, (count,),
         [full((tokens, D))] * (1 + len(parts))
-        + [full((8, D)), pl.BlockSpec((1, 1, width), lambda s, scal_ref: (scal_ref[S_Z] ^ s, 0, 0))] + [ANY] * 10,
+        + [full((8, D)), pl.BlockSpec((1, 1, width), lambda s, scal_ref: (scal_ref[S_Z] ^ away(s), 0, 0))] + [ANY] * 10,
         [full((tokens, D)), full((tokens, D)), full((tokens, 128)), column, column],
         [sds((tokens, D), F32), sds((tokens, D), BF16), sds((tokens, 128), F32)] + [sds((tokens, FF), BF16)] * 2,
-        piece_shapes(width), [prev, *parts, vec, bias, *weight], (scal,), 2 * tokens * D * FF,
+        piece_shapes(width), [prev, *parts, vec, bias, *weight], 2 * tokens * D * FF,
         2 * (D * FF + tokens * (10 * D + 2 * FF)), "norm_up",
     )
 
 
-def down_norm(scal, act, weight, matrix, prev, vec, count):
+def down_norm(flow, act, weight, matrix, prev, vec, count):
     tokens = prev.shape[0]
     width = FF // count
 
@@ -259,16 +298,16 @@
             norm_forward(total, tokens, vec_ref, n_ref, low_ref, inv_ref)
 
     return call(
-        body, (count,),
+        flow, body, (count,),
         [pl.BlockSpec((tokens, width), lambda s, _: (0, s)), full((tokens, D)), full((8, D))] + [ANY] * 10,
         [full((tokens, D)), full((tokens, D)), full((tokens, 128))],
         [sds((tokens, D), F32), sds((tokens, D), BF16), sds((tokens, 128), F32)],
-        piece_shapes(width) + [pltpu.VMEM((tokens, D), F32)], [act, prev, vec, *weight], (scal,), 2 * tokens * D * FF,
+        piece_shapes(width) + [pltpu.VMEM((tokens, D), F32)], [act, prev, vec, *weight], 2 * tokens * D * FF,
         2 * (D * FF + tokens * (5 * D + FF)), "down_norm",
     )
 
 
-def units_back(scal, grad, weight, matrix, slope, count):
+def units_back(flow, grad, weight, matrix, slope, count):
     tokens = grad.shape[0]
     width = FF // count
 
@@ -290,14 +329,14 @@
 
     column = pl.BlockSpec((tokens, width), lambda s, _: (0, s))
     return call(
-        body, (count,), [full((tokens, D)), column] + [ANY] * 10,
-        [column, pl.BlockSpec((1, 1, width), lambda s, scal_ref: (scal_ref[S_Z] ^ s, 0, 0))],
-        [sds((tokens, FF), BF16), sds((count, 1, width), F32)], piece_shapes(width), [grad, slope, *weight], (scal,),
+        flow, body, (count,), [full((tokens, D)), column] + [ANY] * 10,
+        [column, pl.BlockSpec((1, 1, width), lambda s, scal_ref: (scal_ref[S_Z] ^ away(s), 0, 0))],
+        [sds((tokens, FF), BF16), sds((count, 1, width), F32)], piece_shapes(width), [grad, slope, *weight],
         2 * tokens * D * FF, 2 * (D * FF + tokens * (D + 2 * FF)), "units_back",
     )
 
 
-def up_back(scal, gu, weight, matrix, residual, normed, inverse, gain, count):
+def up_back(flow, gu, weight, matrix, residual, normed, inverse, gain, count):
     tokens = residual.shape[0]
     width = FF // count
 
@@ -324,17 +363,17 @@
             )
 
     return call(
-        body, (count,),
+        flow, body, (count,),
         [pl.BlockSpec((tokens, width), lambda s, _: (0, s)), full((tokens, D)), full((tokens, D)), full((tokens, 128)),
          full((8, D))] + [ANY] * 10,
         [full((tokens, D)), full((tokens, D)), full((8, D))],
         [sds((tokens, D), F32), sds((tokens, D), BF16), sds((8, D), F32)],
-        piece_shapes(width) + [pltpu.VMEM((tokens, D), F32)], [gu, residual, normed, inverse, gain, *weight], (scal,),
+        piece_shapes(width) + [pltpu.VMEM((tokens, D), F32)], [gu, residual, normed, inverse, gain, *weight],
         2 * tokens * D * FF, 2 * (D * FF + tokens * (8 * D + FF)), "up_back",
     )
 
 
-def norm_back(scal, grad, normed, inverse, gain):
+def norm_back(flow, grad, normed, inverse, gain):
     tokens = grad.shape[0]
 
     def body(scal_ref, grad_ref, n_ref, inv_ref, gain_ref, g_ref, low_ref, sums_ref):
@@ -343,14 +382,14 @@
         )
 
     return call(
-        body, (1,), [full((tokens, D)), full((tokens, D)), full((tokens, 128)), full((8, D))],
+        flow, body, (1,), [full((tokens, D)), full((tokens, D)), full((tokens, 128)), full((8, D))],
         [full((tokens, D)), full((tokens, D)), full((8, D))],
-        [sds((tokens, D), F32), sds((tokens, D), BF16), sds((8, D), F32)], [], [grad, normed, inverse, gain], (scal,),
+        [sds((tokens, D), F32), sds((tokens, D), BF16), sds((8, D), F32)], [], [grad, normed, inverse, gain],
         20 * tokens * D, 12 * tokens * D, "norm_back",
     )
 
 
-def sum_norm_back(scal, residual, parts, normed, inverse, gain):
+def sum_norm_back(flow, residual, parts, normed, inverse, gain):
     tokens = residual.shape[0]
 
     def body(scal_ref, res_ref, *refs):
@@ -365,10 +404,10 @@
         norm_backward(grad, tokens, n_ref, inv_ref, gain_ref, g_ref, low_ref, sums_ref)
 
     return call(
-        body, (1,), [full((tokens, D))] * (2 + len(parts)) + [full((tokens, 128)), full((8, D))],
+        flow, body, (1,), [full((tokens, D))] * (2 + len(parts)) + [full((tokens, 128)), full((8, D))],
         [full((tokens, D)), full((tokens, D)), full((8, D))],
         [sds((tokens, D), F32), sds((tokens, D), BF16), sds((8, D), F32)], [],
-        [residual, *parts, normed, inverse, gain], (scal,), 20 * tokens * D, 22 * tokens * D, "sum_norm_back",
+        [residual, *parts, normed, inverse, gain], 20 * tokens * D, 22 * tokens * D, "sum_norm_back",
     )
 
 
@@ -378,69 +417,72 @@
         turned[r * ROWS : (r + 1) * ROWS, :] = x_ref[:, pl.ds(pl.multiple_of(row, ROWS), ROWS)].T
 
 
-def grad_theirs(scal, left, right, count):
-    tokens = left.shape[0]
-    width = right.shape[1] // count
-
-    def body(scal_ref, x_ref, y_ref, out_ref, turned):
-        @pl.when(pl.program_id(0) == 0)
-        def _():
-            turn_rows(scal_ref, x_ref, turned, scal_ref[S_C] ^ 1)
-
-        out_ref[:, 0] = mm(turned[...], y_ref[...]).astype(BF16).reshape(4, ROWS, width)
-
+def unit_grads(flow, down, up, received, count, sibling):
+    tokens = down[0].shape[0]
+    width = down[1].shape[1] // count
+    half = count // 2
+    steps = 2 * count
+
+    def body(scal_ref, x0_ref, y0_ref, x1_ref, y1_ref, *refs):
+        turned, t = refs[-1], pl.program_id(0)
+        m, s = t // count, lax.rem(t, count)
+        core = scal_ref[S_C] ^ 1 if sibling else scal_ref[S_C]
+
+        @pl.when(t == 0)
+        def _():
+            turn_rows(scal_ref, x0_ref, turned, core)
+
+        @pl.when(t == count)
+        def _():
+            turn_rows(scal_ref, x1_ref, turned, core)
+
+        def store(y_ref):
+            value = mm(turned[...], y_ref[...]).reshape(4, ROWS, width)
+            if sibling:
+                refs[0][:, 0] = value.astype(BF16)
+                return
+            if received is not None:
+                value = value + refs[0][:, 0].astype(F32)
+            value = value.astype(BF16)
+            own, to_x, to_y, rest_x, rest_y = refs[-6:-1]
+            own[t] = value[0]
+
+            @pl.when(s < half)
+            def _():
+                to_x[t] = value[1]
+                to_x[half + t] = value[3]
+                rest_y[m * half + s] = value[2]
+
+            @pl.when(s >= half)
+            def _():
+                rest_x[m * half + s - half] = value[1]
+                to_y[t - half] = value[2]
+                to_y[t] = value[3]
+
+        @pl.when(m == 0)
+        def _():
+            store(y0_ref)
+
+        @pl.when(m == 1)
+        def _():
+            store(y1_ref)
+
+    left = full((tokens, D))
+    specs = [left, pl.BlockSpec((tokens, width), lambda t, _: (0, jnp.minimum(t, count - 1))),
+             left, pl.BlockSpec((tokens, width), lambda t, _: (0, jnp.maximum(t - count, 0)))]
+    args = [*down, *up]
+    one = pl.BlockSpec((4, 1, ROWS, width), lambda t, _: (0, t, 0, 0))
+    if sibling:
+        out_specs, out_shape = one, sds((4, steps, ROWS, width), BF16)
+    else:
+        if received is not None:
+            specs.append(one)
+            args.append(received)
+        shapes = [(steps, ROWS, width)] * 3 + [(count, ROWS, width)] * 2
+        out_specs, out_shape = [full(shape) for shape in shapes], [sds(shape, BF16) for shape in shapes]
     return call(
-        body, (count,), [full((tokens, D)), pl.BlockSpec((tokens, width), lambda s, _: (0, s))],
-        pl.BlockSpec((4, 1, ROWS, width), lambda s, _: (0, s, 0, 0)), sds((4, count, ROWS, width), BF16),
-        [pltpu.VMEM((4 * ROWS, tokens), BF16)], [left, right], (scal,), tokens * D * width * count,
-        D * width * count + 2 * tokens * (D + count * width), "grad_theirs",
-    )
-
-
-def grad_mine(scal, left, right, received, count):
-    tokens = left.shape[0]
-    width = right.shape[1] // count
-    half = count // 2
-
-    def body(scal_ref, x_ref, y_ref, *refs):
-        if received is None:
-            own, to_x, to_y, rest_x, rest_y, turned = refs
-        else:
-            got_ref, own, to_x, to_y, rest_x, rest_y, turned = refs
-        s = pl.program_id(0)
-
-        @pl.when(s == 0)
-        def _():
-            turn_rows(scal_ref, x_ref, turned, scal_ref[S_C])
-
-        value = mm(turned[...], y_ref[...]).reshape(4, ROWS, width)
-        if received is not None:
-            value = value + got_ref[:, 0].astype(F32)
-        value = value.astype(BF16)
-        own[s] = value[0]
-
-        @pl.when(s < half)
-        def _():
-            to_x[s] = value[1]
-            to_x[half + s] = value[3]
-            rest_y[s] = value[2]
-
-        @pl.when(s >= half)
-        def _():
-            rest_x[s - half] = value[1]
-            to_y[s - half] = value[2]
-            to_y[s] = value[3]
-
-    specs = [full((tokens, D)), pl.BlockSpec((tokens, width), lambda s, _: (0, s))]
-    args = [left, right]
-    if received is not None:
-        specs.append(pl.BlockSpec((4, 1, ROWS, width), lambda s, _: (0, s, 0, 0)))
-        args.append(received)
-    shapes = [(count, ROWS, width)] * 3 + [(half, ROWS, width)] * 2
-    return call(
-        body, (count,), specs, [full(shape) for shape in shapes], [sds(shape, BF16) for shape in shapes],
-        [pltpu.VMEM((4 * ROWS, tokens), BF16)], args, (scal,), tokens * D * width * count,
-        2 * D * width * count + 2 * tokens * (D + count * width), "grad_mine",
+        flow, body, (steps,), specs, out_specs, out_shape, [pltpu.VMEM((4 * ROWS, tokens), BF16)], args,
+        0, 0, "grads_theirs" if sibling else "grads_mine",
     )
 
 
@@ -468,7 +510,7 @@
     return [pltpu.VMEM((D, width), BF16), pltpu.SemaphoreType.DMA((8,))]
 
 
-def project_in(scal, lefts, weight, cols, bias, name):
+def project_in(flow, lefts, weight, cols, bias, name):
     count = len(lefts)
     tokens = lefts[0].shape[0]
     width = cols.stop - cols.start
@@ -495,13 +537,13 @@
 
     extra, extra_specs = ([], []) if bias is None else ([bias], [full((1, width))])
     return call(
-        body, (count,), [full((tokens, D))] * count + extra_specs + [ANY] * 4, by_member((tokens, width)),
-        sds((count, tokens, width), BF16), heads_weight_scratch(width), [*lefts, *extra, *weight], (scal,),
+        flow, body, (count,), [full((tokens, D))] * count + extra_specs + [ANY] * 4, by_member((tokens, width)),
+        sds((count, tokens, width), BF16), heads_weight_scratch(width), [*lefts, *extra, *weight],
         2 * tokens * D * width * count, 2 * (D * width + count * tokens * (D + width)), name,
     )
 
 
-def project_out(scal, blocks, weight, cols, name):
+def project_out(flow, blocks, weight, cols, name):
     count, tokens, width = blocks.shape
 
     def body(scal_ref, block_ref, *refs):
@@ -519,13 +561,13 @@
                 out[...] = mm(block_ref[0], buffer[...], NT).astype(BF16)
 
     return call(
-        body, (count,), [by_member((tokens, width))] + [ANY] * 4, [full((tokens, D))] * count,
-        [sds((tokens, D), BF16)] * count, heads_weight_scratch(width), [blocks, *weight], (scal,),
+        flow, body, (count,), [by_member((tokens, width))] + [ANY] * 4, [full((tokens, D))] * count,
+        [sds((tokens, D), BF16)] * count, heads_weight_scratch(width), [blocks, *weight],
         2 * tokens * D * width * count, 2 * (D * width + count * tokens * (D + width)), name,
     )
 
 
-def heads_grad(scal, xs, gqkv, gas, ctx):
+def heads_grad(flow, xs, gqkv, gas, ctx):
     count, tokens, width = gqkv.shape
     out_width = ctx.shape[2]
 
@@ -562,9 +604,9 @@
 
     shape = (2, ROWS, width + out_width)
     return call(
-        body, (count,), [full((tokens, D))] * (2 * count) + [by_member((tokens, width)), by_member((tokens, out_width))],
+        flow, body, (count,), [full((tokens, D))] * (2 * count) + [by_member((tokens, width)), by_member((tokens, out_width))],
         [full(shape)] * 4 + [full((1, width))], [sds(shape, BF16)] * 4 + [sds((1, width), F32)],
-        [pltpu.VMEM((D, width), F32), pltpu.VMEM((D, out_width), F32)], [*xs, *gas, gqkv, ctx], (scal,),
+        [pltpu.VMEM((D, width), F32), pltpu.VMEM((D, out_width), F32)], [*xs, *gas, gqkv, ctx],
         2 * tokens * D * (width + out_width) * count, 4 * count * tokens * (D + width), "heads_grad",
     )
 
@@ -601,7 +643,7 @@
     lax.fori_loop(low_first // chunk, (high_last + chunk - 1) // chunk, one, 0)
 
 
-def attend_forward(ends, qkv):
+def attend_forward(flow, ends, qkv):
     count, chunk, width3 = qkv.shape
     width = width3 // 3
     heads = width // HD
@@ -659,7 +701,7 @@
 
     pairs = SEQLEN * SEQLEN
     return call(
-        body, (steps,), [full((count, chunk, width3))],
+        flow, body, (steps,), [full((count, chunk, width3))],
         [pl.BlockSpec((1, BQ, width), lambda i, _: (i // per, i % per, 0)),
          pl.BlockSpec((width, BQ), lambda i, _: (0, i)), pl.BlockSpec((8, BQ), lambda i, _: (0, i))],
         [sds((count, chunk, width), BF16), sds((width, SEQLEN), F32), sds((8, SEQLEN), F32)],
@@ -672,11 +714,11 @@
             pltpu.VMEM((heads, 8, BQ), F32),
             pltpu.VMEM((heads, count, chunk, BQ), F32),
         ],
-        [qkv], (ends,), 16 * pairs * heads * HD, 6 * SEQLEN * width * 2, "attend_forward",
-    )
-
-
-def attend_backward(ends, qkv, grads, wide, lse):
+        [qkv], 16 * pairs * heads * HD, 6 * SEQLEN * width * 2, "attend_forward", (ends,),
+    )
+
+
+def attend_backward(flow, ends, qkv, grads, wide, lse):
     count, chunk, width3 = qkv.shape
     width = width3 // 3
     heads = width // HD
@@ -739,7 +781,7 @@
 
     pairs = SEQLEN * SEQLEN
     return call(
-        body, (steps,),
+        flow, body, (steps,),
         [full((count, chunk, width3)), full((count, chunk, width)), pl.BlockSpec((width, BQ), lambda i, _: (0, i)),
          pl.BlockSpec((8, BQ), lambda i, _: (0, i))],
         full((count, chunk, width3)), sds((count, chunk, width3), BF16),
@@ -752,7 +794,7 @@
             pltpu.VMEM((count, width, chunk), F32),
             pltpu.VMEM((count, width, chunk), F32),
         ],
-        [qkv, grads, wide, lse], (ends,), 28 * pairs * heads * HD, 20 * SEQLEN * width, "attend_backward",
+        [qkv, grads, wide, lse], 28 * pairs * heads * HD, 20 * SEQLEN * width, "attend_backward", (ends,),
     )
 
 
@@ -802,64 +844,107 @@
     return values_in
 
 
-def gather_heads_weight(shard, zh):
+def all_heads_weight(shard, zh):
     pair = jnp.stack([turn(shard), cross(shard)])
-    if is_small():
-        return from_members(pair, "q")
     every = order_by(lax.all_gather(pair, "q"), 1, zh, 2).reshape(4, 2, ROWS, -1)
     return [every[r] for r in range(4)]
 
 
-def scatter_heads_grad(buckets, zh):
+def sum_heads_grad(buckets, zh):
     if is_small():
         got = to_members(buckets, "q")
-        first, second = (add(*(member[k] for member in got)).astype(BF16) for k in range(2))
-    else:
-        every = jnp.stack(buckets).reshape(lax.axis_size("q"), 2, -1, buckets[0].shape[-1])
-        rows = order_by(lax.psum_scatter(every, "q", scatter_dimension=0, tiled=False), 0, zh, 2)
-        first, second = rows[0], rows[1]
-    return add(turn(first), uncross(second))
-
-
-def gather_units_weight(shard):
-    if is_small():
-        two = jnp.stack([shard, flip(shard, "zl", 1)])
-        own = jnp.concatenate([two, flip(two, "zh", 1)])
-        near_x, near_y = flip(own, "q", 1), flip(own, "q", 2)
-        far_a, far_b = flip(near_y[:2], "q", 1), flip(near_x[2:], "q", 2)
-        mine = [own, near_x, near_y, far_a, far_b]
-        return mine + [flip(piece, "c", 1) for piece in mine]
+        return [add(*(member[k] for member in got)).astype(BF16) for k in range(2)]
+    every = jnp.stack(buckets).reshape(lax.axis_size("q"), 2, -1, buckets[0].shape[-1])
+    rows = order_by(lax.psum_scatter(every, "q", scatter_dimension=0, tiled=False), 0, zh, 2)
+    return [rows[0], rows[1]]
+
+
+SLOTS = (0, 2, 1, 3)
+
+
+def all_units_weight(shard):
     matrices, _, width = shard.shape
     members = lax.axis_size(MODEL)
     every = lax.all_gather(shard, ALL).reshape(members, -1, matrices, shard.shape[1], width).transpose(0, 2, 1, 3, 4)
     every = every.reshape(members, matrices, 4, 2, ROWS, width)
+    every = jnp.stack([every[slot] for slot in SLOTS])
     pieces = []
     for k in range(2):
         pieces += [every[:, :, r, k] for r in range(3)] + [every[:2, :, 3, k], every[2:, :, 3, k]]
     return pieces
 
 
-def scatter_units_grad(scal, left, right, count):
-    if is_small():
-        got = flip(grad_theirs(scal, left, right, count), "c", 1)
-        own, to_x, to_y, rest_x, rest_y = grad_mine(scal, left, right, got, count)
-        half = count // 2
-        from_x, from_y = flip(to_x, "q", 1), flip(to_y, "q", 2)
-        late_x = flip(add(rest_x, from_y[half:]).astype(BF16), "q", 1)
-        late_y = flip(add(rest_y, from_x[half:]).astype(BF16), "q", 2)
-        near = add(own[:half], from_x[:half], late_y)
-        far = add(own[half:], late_x, from_y[:half]).astype(BF16)
-        both = near + flip(far, "zh", 1).astype(F32)
-        return both[0] + flip(both[1].astype(BF16), "zl", 1).astype(F32)
-    theirs = grad_theirs(scal, left, right, count)
-    own, to_x, to_y, rest_x, rest_y = grad_mine(scal, left, right, None, count)
-    half = count // 2
-    mine = jnp.stack(
-        [own, jnp.concatenate([to_x[:half], rest_x]), jnp.concatenate([rest_y, to_y[:half]]),
-         jnp.concatenate([to_x[half:], to_y[half:]])]
-    )
-    every = jnp.stack([mine, theirs], axis=1).transpose(2, 0, 1, 3, 4).reshape(-1, mine.shape[-1])
-    return lax.psum_scatter(every, ALL, scatter_dimension=0, tiled=True).astype(F32)
+class UnitsWeight:
+    def __init__(self, shard):
+        self.shard = shard
+
+    def far_z(self):
+        self.two = jnp.stack([self.shard, flip(self.shard, "zh", 1)])
+
+    def near_z(self):
+        self.own = jnp.concatenate([self.two, flip(self.two, "zl", 1)])
+
+    def near(self):
+        self.near_x, self.near_y = flip(self.own, "q", 1), flip(self.own, "q", 2)
+
+    def far(self):
+        self.far_a, self.far_b = flip(self.near_y[:2], "q", 1), flip(self.near_x[2:], "q", 2)
+
+    def pieces(self):
+        mine = [self.own, self.near_x, self.near_y, self.far_a, self.far_b]
+        return mine + [flip(piece, "c", 1) for piece in mine]
+
+
+class UnitsGrads:
+    def __init__(self, flow, down, up, count):
+        self.flow, self.down, self.up, self.count = flow, down, up, count
+
+    def sibling(self):
+        self.theirs = unit_grads(self.flow, self.down, self.up, None, self.count, True)
+        self.got = flip(self.theirs, "c", 1) if is_small() else None
+
+    def mine(self):
+        made = unit_grads(self.flow, self.down, self.up, self.got, self.count, False)
+        self.made = made
+        self.own, self.to_x, self.to_y, self.rest_x, self.rest_y = (
+            part.reshape(2, -1, ROWS, part.shape[-1]) for part in made
+        )
+
+    def near(self):
+        self.from_x, self.from_y = flip(self.to_x, "q", 1), flip(self.to_y, "q", 2)
+        return [self.from_x, self.from_y]
+
+    def far(self):
+        half = self.count // 2
+        self.late_x = flip(add(self.rest_x, self.from_y[:, half:]).astype(BF16), "q", 1)
+        self.late_y = flip(add(self.rest_y, self.from_x[:, half:]).astype(BF16), "q", 2)
+        return [self.late_x, self.late_y]
+
+    def near_z(self):
+        half = self.count // 2
+        self.here = add(self.own[:, :half], self.from_x[:, :half], self.late_y)
+        self.there = flip(add(self.own[:, half:], self.late_x, self.from_y[:, :half]).astype(BF16), "zl", 1)
+        return [self.there]
+
+    def far_z(self):
+        both = self.here + self.there.astype(F32)
+        self.stays, self.last = both[:, 0], flip(both[:, 1].astype(BF16), "zh", 1)
+        return [self.last]
+
+    def total(self):
+        if is_small():
+            return self.stays + self.last.astype(F32)
+        half = self.count // 2
+        mine = jnp.stack(
+            [self.own, jnp.concatenate([self.to_x[:, :half], self.rest_x], 1),
+             jnp.concatenate([self.rest_y, self.to_y[:, :half]], 1),
+             jnp.concatenate([self.to_x[:, half:], self.to_y[:, half:]], 1)]
+        )
+        theirs = self.theirs.reshape(4, 2, self.count, ROWS, -1)
+        every = jnp.stack([mine, theirs], axis=2)
+        every = every.transpose(3, 0, 2, 4, 1, 5)
+        every = jnp.stack([every[slot] for slot in SLOTS]).reshape(-1, 2, mine.shape[-1])
+        return lax.psum_scatter(every, ALL, scatter_dimension=0, tiled=True).astype(F32).transpose(1, 0, 2)
 
 
 SMALL_AXES = ("q", MODEL, "c")
@@ -897,6 +982,17 @@
         parts = jnp.stack(from_members(value, axes))
         value = jnp.sum(order_by(parts, 0, lax.axis_index(axes), parts.shape[0]), 0)
     return value[0, 0]
+
+
+def finish(above, arrived, zh):
+    units, buckets = above
+    if arrived is None:
+        halves = sum_heads_grad(buckets, zh)
+        arrived = [turn(halves[0]), uncross(halves[1])]
+    d_heads = add(*arrived)
+    rows, cols = d_heads.shape[0], d_heads.shape[1] * 3 // 4
+    down_up = units.total()
+    return d_heads[:, :cols].reshape(rows, 3, -1).transpose(1, 0, 2), d_heads[:, cols:], down_up[1], down_up[0]
 
 
 def on_device(
@@ -912,8 +1008,32 @@
         spots = [place] + [jnp.zeros((), jnp.int32)] * 4
     scal = jnp.stack([spot.astype(jnp.int32) for spot in spots])
 
+    flow = Flow(scal)
+    small_slice = is_small()
+    qkv_cols = 3 * out_weight.shape[2]
+    heads_shard = [
+        jnp.concatenate([qkv_weight[l].transpose(1, 0, 2).reshape(-1, qkv_cols), out_weight[l]], axis=1)
+        for l in range(layers)
+    ]
     x_low = turn(tokens)
     ends = jnp.cumsum(turn(doc_lengths)[0], dtype=jnp.int32)
+    units_shard = [up_weight[0][None], down_weight[0][None], jnp.stack([up_weight[1], down_weight[1]])]
+    if small_slice:
+        pair = jnp.stack([turn(heads_shard[0]), cross(heads_shard[0])])
+        up0, down0, both1 = (UnitsWeight(shard) for shard in units_shard)
+        up0.far_z()
+        flow.wait(x_low, pair)
+        flow.hold(down0=down0.shard, both1=both1.shard, heads1=heads_shard[1], top=cotangent, low=x_low, two=up0.two)
+        gate(flow)
+        x_low, up0.two, down0.shard = flow.free("low"), flow.free("two"), flow.free("down0")
+        heads_weight = [from_members(pair, "q")]
+        up0.near_z()
+        down0.far_z()
+    else:
+        heads_weight = [all_heads_weight(shard, zh) for shard in heads_shard]
+        every = [all_units_weight(shard) for shard in units_shard]
+        units_weight = [((every[0], 0), (every[1], 0)), ((every[2], 0), (every[2], 1))]
+        top_grad = turn(cotangent)
 
     pieces = [qv_bias, up_bias, gains, shifts]
     sizes = [piece.size // layers for piece in pieces]
@@ -933,19 +1053,6 @@
     gain_full = parts[2].reshape(tz, dp, layers, 2, -1).transpose(2, 3, 1, 0, 4).reshape(layers, 2, D)
     shift_full = parts[3].reshape(tz, dp, layers, 4, -1).transpose(2, 3, 1, 0, 4).reshape(layers, 4, D)
 
-    qkv_cols = 3 * out_weight.shape[2]
-    heads_weight, units_weight = [], []
-    for l in range(layers):
-        shard = jnp.concatenate([qkv_weight[l].transpose(1, 0, 2).reshape(-1, qkv_cols), out_weight[l]], axis=1)
-        heads_weight.append(gather_heads_weight(shard, zh))
-        if l == 0:
-            up = (gather_units_weight(up_weight[l][None]), 0)
-            down = (gather_units_weight(down_weight[l][None]), 0)
-        else:
-            both = gather_units_weight(jnp.stack([up_weight[l], down_weight[l]]))
-            up, down = (both, 0), (both, 1)
-        units_weight.append((up, down))
-    top_grad = turn(cotangent)
     in_cols, out_cols = slice(0, qkv_cols), slice(qkv_cols, qkv_cols + out_weight.shape[2])
 
     one, zero = jnp.ones((D,), F32), jnp.zeros((D,), F32)
@@ -953,36 +1060,95 @@
     prev, prev_gain, prev_shift = x_low.astype(F32), one, zero
     kept = []
     for l in range(layers):
-        w_heads, (w_up, w_down) = heads_weight[l], units_weight[l]
         xs = from_members(x_low, GROUP)
-        qkv = project_in(scal, xs, w_heads, in_cols, bias_qkv[l], "project_qkv")
-        ctx, wide, lse = attend_forward(ends, qkv)
-        attn = to_members(project_out(scal, ctx, w_heads, out_cols, "project_attn"), GROUP)
+        if small_slice and l == 0:
+            flow.wait(up0.own)
+            flow.hold(down0=down0.two)
+        if small_slice and l == 1:
+            flow.wait(*xs, *heads_members)
+            gate(flow)
+            both1.own = flow.free("both1")
+            both1.near()
+            heads_weight.append(heads_members)
+        w_heads = heads_weight[l]
+        qkv = project_in(flow, xs, w_heads, in_cols, bias_qkv[l], "project_qkv")
+        if small_slice and l == 0:
+            up0.near()
+            down0.two, both1.shard = flow.free("down0"), flow.free("both1")
+            down0.near_z()
+            both1.far_z()
+        if small_slice and l == 1:
+            top_grad = turn(flow.free("top"))
+        ctx, wide, lse = attend_forward(flow, ends, qkv)
+        if small_slice and l == 0:
+            flow.wait(up0.near_x, up0.near_y, down0.own, both1.two)
+            flow.hold(both1=both1.two)
+            up0.far()
+            down0.near()
+        if small_slice and l == 1:
+            flow.wait(both1.near_x, both1.near_y, top_grad)
+            both1.far()
+        attn = to_members(project_out(flow, ctx, w_heads, out_cols, "project_attn"), GROUP)
+        if small_slice and l == 0:
+            w_up = (up0.pieces(), 0)
+            flow.wait(*attn[1:], *w_up[0], down0.near_x, down0.near_y)
+            gate(flow)
+            both1.two, shard = flow.free("both1"), flow.free("heads1")
+            both1.near_z()
+            down0.far()
+            pair = jnp.stack([turn(shard), cross(shard)])
+        elif small_slice:
+            every = both1.pieces()
+            w_up, w_down = (every, 0), (every, 1)
+        else:
+            w_up, w_down = units_weight[l]
         vec = jnp.stack([prev_gain, prev_shift, shift_full[l, 0], gain_full[l, 0], shift_full[l, 1]] + pad)
-        n1, hs, r1, act, slope = norm_up(scal, prev, attn, vec, *w_up, up_bias_full[l], tz)
+        n1, hs, r1, act, slope = norm_up(flow, prev, attn, vec, *w_up, up_bias_full[l], tz)
+        if small_slice and l == 0:
+            w_down = (down0.pieces(), 0)
+            flow.wait(both1.own, pair)
+            flow.hold(both1=both1.own)
+            heads_members = from_members(pair, "q")
         vec = jnp.stack([gain_full[l, 0], shift_full[l, 1], shift_full[l, 2], gain_full[l, 1], shift_full[l, 3]] + pad)
-        n2, y_low, r2 = down_norm(scal, act, *w_down, n1, vec, tz)
-        kept.append((xs, qkv, ctx, wide, lse, n1, hs, r1, act, slope, n2, r2))
+        n2, y_low, r2 = down_norm(flow, act, *w_down, n1, vec, tz)
+        kept.append((xs, qkv, ctx, wide, lse, n1, hs, r1, act, slope, n2, r2, w_heads, w_up, w_down))
         x_low, prev, prev_gain, prev_shift = y_low, n2, gain_full[l, 1], shift_full[l, 3]
     layer_output = turn(x_low)
 
     gain_rows = [[jnp.broadcast_to(gain_full[l, i], (8, D)) for i in range(2)] for l in range(layers)]
-    g2, gf, sums2 = norm_back(scal, top_grad, kept[-1][10], kept[-1][11], gain_rows[-1][1])
+    g2, gf, sums2 = norm_back(flow, top_grad, kept[-1][10], kept[-1][11], gain_rows[-1][1])
     results = [None] * layers
     small_grads = [None] * layers
+    above = None
     for l in reversed(range(layers)):
-        w_heads, (w_up, w_down) = heads_weight[l], units_weight[l]
-        xs, qkv, ctx, wide, lse, n1, hs, r1, act, slope, n2, r2 = kept[l]
-        gu, up_bias_sum = units_back(scal, gf, *w_down, slope, tz)
-        g1, ga, sums1 = up_back(scal, gu, *w_up, g2, n1, r1, gain_rows[l][0], tz)
+        xs, qkv, ctx, wide, lse, n1, hs, r1, act, slope, n2, r2, w_heads, w_up, w_down = kept[l]
+        gu, up_bias_sum = units_back(flow, gf, *w_down, slope, tz)
+        units = UnitsGrads(flow, (gf, act), (hs, gu), tz)
+        if small_slice and l == layers - 1:
+            flow.wait(layer_output)
+        units.sibling()
+        flow.wait(units.theirs)
+        if small_slice and above is not None:
+            flow.wait(*above[0].near_z())
+            halves = sum_heads_grad(above[1], zh)
+            flow.wait(*halves)
+        g1, ga, sums1 = up_back(flow, gu, *w_up, g2, n1, r1, gain_rows[l][0], tz)
         gas = from_members(ga, GROUP)
-        d_down = scatter_units_grad(scal, gf, act, tz)
-        d_up = scatter_units_grad(scal, hs, gu, tz)
-        gc = project_in(scal, gas, w_heads, out_cols, None, "project_gc")
-        gqkv = attend_backward(ends, qkv, gc, wide, lse)
-        back = to_members(project_out(scal, gqkv, w_heads, in_cols, "project_gx"), GROUP)
-        *buckets, qkv_sums = heads_grad(scal, xs, gqkv, gas, ctx)
-        d_heads = scatter_heads_grad(buckets, zh)
+        flow.wait(ga)
+        units.mine()
+        if small_slice:
+            flow.wait(*units.made)
+        if small_slice and above is not None:
+            arrived = [turn(halves[0]), uncross(halves[1])]
+            flow.wait(*above[0].far_z(), *arrived)
+        gc = project_in(flow, gas, w_heads, out_cols, None, "project_gc")
+        gqkv = attend_backward(flow, ends, qkv, gc, wide, lse)
+        if small_slice:
+            flow.wait(*units.near())
+        back = project_out(flow, gqkv, w_heads, in_cols, "project_gx")
+        flow.wait(back[0])
+        back = to_members(back, GROUP)
+        *buckets, qkv_sums = heads_grad(flow, xs, gqkv, gas, ctx)
         qv_sums = qkv_sums.reshape(3, hz, dp, -1)
         qv_sums = jnp.stack([qv_sums[0], qv_sums[2]]).transpose(2, 0, 1, 3).reshape(1, dp, -1)
         mine = (jnp.arange(tz) == place).astype(F32).reshape(tz, 1, 1)
@@ -996,16 +1162,35 @@
             ],
             axis=-1,
         )
+        if small_slice:
+            late = units.far()
+        if above is not None:
+            results[l + 1] = finish(above, arrived if small_slice else None, zh)
+        above = (units, buckets)
         if l > 0:
-            g2, gf, sums2 = sum_norm_back(scal, g1, back, kept[l - 1][10], kept[l - 1][11], gain_rows[l - 1][1])
+            flow.wait(buckets[0])
+            if small_slice:
+                flow.wait(*late)
+            g2, gf, sums2 = sum_norm_back(flow, g1, back, kept[l - 1][10], kept[l - 1][11], gain_rows[l - 1][1])
         else:
+            if small_slice:
+                flow.wait(*back)
+                flow.hold(small=jnp.stack(small_grads, axis=2).reshape(tz, dp, -1), **{f"b{r}": buckets[r] for r in (1, 2, 3)})
+                gate(flow)
+                small_sums = flow.free("small")
+                buckets = buckets[:1] + [flow.free(f"b{r}") for r in (1, 2, 3)]
+                above = (units, buckets)
+            else:
+                small_sums = jnp.stack(small_grads, axis=2).reshape(tz, dp, -1)
             input_grad = turn((g1 + add(*back)).astype(BF16))
-        rows = d_heads.shape[0]
-        results[l] = (
-            d_heads[:, :qkv_cols].reshape(rows, 3, -1).transpose(1, 0, 2), d_heads[:, qkv_cols:], d_up, d_down
-        )
-
-    small_out = scatter_small(jnp.stack(small_grads, axis=2).reshape(tz, dp, -1), where).reshape(layers, -1)
+            if small_slice:
+                units.near_z()
+                units.far_z()
+                halves = sum_heads_grad(buckets, zh)
+                arrived = [turn(halves[0]), uncross(halves[1])]
+            results[l] = finish(above, arrived if small_slice else None, zh)
+
+    small_out = scatter_small(small_sums, where).reshape(layers, -1)
     qkv_grad, out_grad, up_grad, down_grad = (jnp.stack([entry[i] for entry in results]) for i in range(4))
     qv_bias_grad = small_out[:, cuts[0] : cuts[1]].reshape(qv_bias.shape)
     up_bias_grad = small_out[:, cuts[1] : cuts[2]].reshape(up_bias.shape)

time: 1270 us -> 1250 us (0.984)
  waiting for transfers between devices: 528 us -> 457 us
  local copies, waits for them, and re-layouts: 50.7 us -> 92.2 us
    ppermute x118 -> x104, waiting for transfers between devices: 458 us -> 363 us  [flip(): lax.ppermute(values_in, axes, [(a, a ^ mask) for a in range(lax.axis_size...]
    ppermute x9, waiting for transfers between devices: 69.7 us -> 93.5 us  [turn(): lax.ppermute(values_in, ('c', 'zh'), [(2 * a + b, 2 * b + a) for a in ran...]
    unnamed x143 -> x209, local copies, waits for them, and re-layouts: 18.6 us -> 28 us
    ppermute x118 -> x104, starting transfers between devices: 132 us -> 127 us  [flip(): lax.ppermute(values_in, axes, [(a, a ^ mask) for a in range(lax.axis_size...]
  transfers between devices with their start and end apart: 131 -> 117, of which waited for: 50 -> 46; matrix products, arithmetic and copies ran while one was open for 5% -> 9% of each run, Pallas kernels for 29% -> 28%
where the time goes in v3:
time: 1250 us; the launch traced here: 1240 us
  Pallas kernels  464 us (37%)
  waiting for transfers between devices  457 us (37%)
  starting transfers between devices  169 us (14%)
  local copies, waits for them, and re-layouts  92.2 us (7%)
  other arithmetic  44.8 us (4%)
    pallas_call x32, Pallas kernels, call(): pl.pallas_call(wrapped, grid_spec=pltpu.PrefetchScalarGridSpec(num_scalar...  464 us
    ppermute x104, waiting for transfers between devices, flip(): lax.ppermute(values_in, axes, [(a, a ^ mask) for a in range(lax.axis_size...  363 us
    ppermute x104, starting transfers between devices, flip(): lax.ppermute(values_in, axes, [(a, a ^ mask) for a in range(lax.axis_size...  127 us
    ppermute x9, waiting for transfers between devices, turn(): lax.ppermute(values_in, ('c', 'zh'), [(2 * a + b, 2 * b + a) for a in ran...  93.5 us
    ppermute x9, starting transfers between devices, turn(): lax.ppermute(values_in, ('c', 'zh'), [(2 * a + b, 2 * b + a) for a in ran...  39.7 us
    unnamed x209, local copies, waits for them, and re-layouts  28 us
  transfers between devices with their start and end apart: 117, of which 46 were waited for; matrix products, arithmetic and copies ran while one was open for 9% of the time, Pallas kernels for 28%

profile of v3, /device:TPU:1, one launch (start us, length us, event | category | flops | bytes accessed | tf_op | source)
XLA Modules:
  0.0 1236.8 jit_solution(4553549615910948413)
XLA Ops:
  48.5 16.7 %collective-permute-start.4 = (bf16[2,1,128,1024]{3,2,1,0:T(8,128)(2,1)}, bf16[2,1,128,1024]{3,2,1,0:T(8,128)(2,1)}, u32[]{:S(2)}, u32[]{:S(2)}) collective-permute-start(bf16[2,1,128,1024]{3,2,1,0:T(8,128)(2,1)} %get-tuple-element.115), channel_id=1, source_target_pairs={{0,1},{1,0},{2,3},{3,2},{4,5},{5,4},{6,7},{7,6},{8,9},{9,8},{10,11... | collective-permute-start | bytes 1572872 | tf_op jit(solution)/shard_map/ppermute | solution.py:802
  78.5 43.7 %collective-permute-done.7 = bf16[1,128,1024]{2,1,0:T(8,128)(2,1)S(1)} collective-permute-done((bf16[1,128,1024]{2,1,0:T(8,128)(2,1)}, bf16[1,128,1024]{2,1,0:T(8,128)(2,1)S(1)}, u32[]{:S(2)}, u32[]{:S(2)}) %collective-permute-start.7) | collective-permute-done | bytes 262176 | tf_op jit(solution)/shard_map/ppermute | solution.py:802
  143.3 18.3 %collective-permute-done.23 = s32[1,4]{1,0:T(1,128)S(1)} collective-permute-done((s32[1,4]{1,0:T(1,128)S(1)}, s32[1,4]{1,0:T(1,128)S(1)}, u32[]{:S(2)}, u32[]{:S(2)}) %collective-permute-start.23) | collective-permute-done | bytes 48 | tf_op jit(solution)/shard_map/ppermute | solution.py:806
  162.4 31.8 %attend_forward.2 = (bf16[4,512,256]{2,1,0:T(8,128)(2,1)}, f32[256,2048]{1,0:T(8,128)}, f32[8,2048]{1,0:T(8,128)}, bf16[128,1024]{1,0:T(8,128)(2,1)}, bf16[512,1024]{1,0:T(8,128)(2,1)}) custom-call(s32[4]{0:T(128)} %bitcast.311, bf16[128,1024]{1,0:T(8,128)(2,1)} %get-tuple-element.123.refs_1_, ...), custom_call_target="tpu_custom_call", output_to_operand_aliasing={{3}: (1, {}), {4}: (2, {})} | custom-call | flops 1000 | bytes 1000 | tf_op jit(solution)/shard_map/attend_forward/pallas_call | solution.py:74
  214.3 11.8 collective-permute-done.28.refs_8_.refs_13_.refs_14_
  235.5 20.5 %collective-permute-done.26.refs_3_.refs_6_ = bf16[512,1024]{1,0:T(8,128)(2,1)} collective-permute-done((bf16[512,1024]{1,0:T(8,128)(2,1)}, bf16[512,1024]{1,0:T(8,128)(2,1)}, u32[]{:S(2)}, u32[]{:S(2)}) %collective-permute-start.26) | collective-permute-done | bytes 1048608 | tf_op jit(solution)/shard_map/ppermute | solution.py:802
  270.7 18.6 %collective-permute-done.37 = bf16[128,1024]{1,0:T(8,128)(2,1)S(1)} collective-permute-done((bf16[128,1024]{1,0:T(8,128)(2,1)}, bf16[128,1024]{1,0:T(8,128)(2,1)S(1)}, u32[]{:S(2)}, u32[]{:S(2)}) %collective-permute-start.37) | collective-permute-done | bytes 262176 | tf_op jit(solution)/shard_map/ppermute | solution.py:806
  302.3 19.6 %norm_up.2 = (f32[512,1024]{1,0:T(8,128)}, bf16[512,1024]{1,0:T(8,128)(2,1)}, f32[512,128]{1,0:T(8,128)}, bf16[512,4096]{1,0:T(8,128)(2,1)}, bf16[512,4096]{1,0:T(8,128)(2,1)}, /*index=5*/bf16[512,1024]{1,0:T(8,128)(2,1)}) custom-call(s32[5]{0:T(128)} %stack.203.refs_0_, ...), custom_call_target="tpu_custom_call", output_to_operand_aliasing={{5}: (1, {})} | custom-call | flops 1000 | bytes 1000 | tf_op jit(solution)/shard_map/norm_up/pallas_call | solution.py:74
  326.1 14.3 %down_norm.2 = (f32[512,1024]{1,0:T(8,128)}, bf16[512,1024]{1,0:T(8,128)(2,1)}, f32[512,128]{1,0:T(8,128)}, bf16[512,1024]{1,0:T(8,128)(2,1)}, bf16[4,2,128,1024]{3,2,1,0:T(8,128)(2,1)}) custom-call(s32[5]{0:T(128)} %stack.203.refs_0_, bf16[4,2,128,1024]{3,2,1,0:T(8,128)(2,1)} %copy-done.7, ...), custom_call_target="tpu_custom_call", output_to_operand_aliasing={{3}: (3, {}), {4}: (4, {})} | custom-call | flops 1000 | bytes 1000 | tf_op jit(solution)/shard_map/down_norm/pallas_call | solution.py:74
  348.3 22.6 %collective-permute-done.50.refs_7_.refs_9_.refs_12_.refs_6_ = bf16[2,128,1024]{2,1,0:T(8,128)(2,1)S(1)} collective-permute-done((bf16[2,128,1024]{2,1,0:T(8,128)(2,1)}, bf16[2,128,1024]{2,1,0:T(8,128)(2,1)S(1)}, u32[]{:S(2)}, u32[]{:S(2)}) %collective-permute-start.50) | collective-permute-done | bytes 524320 | tf_op jit(solution)/shard_map/ppermute | solution.py:802
  370.9 20.6 %collective-permute-done.48.refs_4_.refs_5_ = bf16[512,1024]{1,0:T(8,128)(2,1)S(1)} collective-permute-done((bf16[512,1024]{1,0:T(8,128)(2,1)}, bf16[512,1024]{1,0:T(8,128)(2,1)S(1)}, u32[]{:S(2)}, u32[]{:S(2)}) %collective-permute-start.48) | collective-permute-done | bytes 1048608 | tf_op jit(solution)/shard_map/ppermute | solution.py:802
  408.9 31.7 %attend_forward.3 = (bf16[4,512,256]{2,1,0:T(8,128)(2,1)}, f32[256,2048]{1,0:T(8,128)}, f32[8,2048]{1,0:T(8,128)}) custom-call(s32[4]{0:T(128)} %bitcast.312, bf16[4,512,768]{2,1,0:T(8,128)(2,1)} %get-tuple-element.149.refs_1_), custom_call_target="tpu_custom_call" | custom-call | flops 1000 | bytes 1000 | tf_op jit(solution)/shard_map/attend_forward/pallas_call | solution.py:74
  456.4 16.7 %collective-permute-done.55.refs_3_ = bf16[512,1024]{1,0:T(8,128)(2,1)S(1)} collective-permute-done((bf16[512,1024]{1,0:T(8,128)(2,1)}, bf16[512,1024]{1,0:T(8,128)(2,1)S(1)}, u32[]{:S(2)}, u32[]{:S(2)}) %collective-permute-start.55) | collective-permute-done | bytes 1048608 | tf_op jit(solution)/shard_map/ppermute | solution.py:802
  482.8 17.3 %collective-permute-done.57.refs_5_ = bf16[512,1024]{1,0:T(8,128)(2,1)} collective-permute-done((bf16[512,1024]{1,0:T(8,128)(2,1)}, bf16[512,1024]{1,0:T(8,128)(2,1)}, u32[]{:S(2)}, u32[]{:S(2)}) %collective-permute-start.57) | collective-permute-done | bytes 1048608 | tf_op jit(solution)/shard_map/ppermute | solution.py:802
  500.1 19.5 %norm_up.3 = (f32[512,1024]{1,0:T(8,128)}, bf16[512,1024]{1,0:T(8,128)(2,1)}, f32[512,128]{1,0:T(8,128)}, bf16[512,4096]{1,0:T(8,128)(2,1)}, bf16[512,4096]{1,0:T(8,128)(2,1)}) custom-call(s32[5]{0:T(128)} %stack.203.refs_0_, f32[512,1024]{1,0:T(8,128)} %get-tuple-element.142.refs_1_.refs_9_, bf16[512,1024]{1,0:T(8,128)(2,1)} %get-tuple-element.151.refs_2_, ...), custom_call_target="tpu_custom_call" | custom-call | flops 1000 | bytes 1000 | tf_op jit(solution)/shard_map/norm_up/pallas_call | solution.py:74
  519.6 14.4 %down_norm.3 = (f32[512,1024]{1,0:T(8,128)}, bf16[512,1024]{1,0:T(8,128)(2,1)}, f32[512,128]{1,0:T(8,128)}) custom-call(s32[5]{0:T(128)} %stack.203.refs_0_, bf16[512,4096]{1,0:T(8,128)(2,1)} %get-tuple-element.155.refs_1_.refs_3_, f32[512,1024]{1,0:T(8,128)} %get-tuple-element.156.refs_2_.refs_4_, f32[8,1024]{1,0:T(8,128)} %stack.234.refs_3_, ...), custom_call_target="tpu_custom_call" | custom-call | flops 1000 | bytes 1000 | tf_op jit(solution)/shard_map/down_norm/pallas_call | solution.py:74
  563.6 12.7 %grads_theirs.2.refs_1_ = bf16[4,8,128,1024]{3,2,1,0:T(8,128)(2,1)} custom-call(s32[5]{0:T(128)} %stack.203.refs_0_, bf16[512,1024]{1,0:T(8,128)(2,1)} %copy-done.49, bf16[512,1024]{1,0:T(8,128)(2,1)} %get-tuple-element.160.refs_1_.refs_2_, bf16[512,4096]{1,0:T(8,128)(2,1)} %get-tuple-element.155.refs_1_.refs_3_, ...), custom_call_target="tpu_custom_call" | custom-call | flops 1000 | bytes 1000 | tf_op jit(solution)/shard_map/grads_theirs/pallas_call | solution.py:74
  576.9 14.9 %up_back.2 = (f32[512,1024]{1,0:T(8,128)}, bf16[512,1024]{1,0:T(8,128)(2,1)}, f32[8,1024]{1,0:T(8,128)}) custom-call(s32[5]{0:T(128)} %stack.203.refs_0_, bf16[4,8,128,1024]{3,2,1,0:T(8,128)(2,1)} %grads_theirs.2.refs_1_, bf16[512,4096]{1,0:T(8,128)(2,1)} %get-tuple-element.163.refs_5_.refs_2_, f32[512,1024]{1,0:T(8,128)} %get-tuple-element.164.refs_3_, ...), custom_call_target="tpu_custom_call" | custom-call | flops 1000 | bytes 1000 | tf_op jit(solution)/shard_map/up_back/pallas_call | solution.py:74
  591.8 15.8 %grads_mine.2 = (bf16[8,128,1024]{2,1,0:T(8,128)(2,1)}, bf16[8,128,1024]{2,1,0:T(8,128)(2,1)}, bf16[8,128,1024]{2,1,0:T(8,128)(2,1)}, bf16[4,128,1024]{2,1,0:T(8,128)(2,1)}, bf16[4,128,1024]{2,1,0:T(8,128)(2,1)}) custom-call(s32[5]{0:T(128)} %stack.203.refs_0_, bf16[512,1024]{1,0:T(8,128)(2,1)} %get-tuple-element.166.refs_1_.refs_6_, ...), custom_call_target="tpu_custom_call" | custom-call | flops 1000 | bytes 1000 | tf_op jit(solution)/shard_map/grads_mine/pallas_call | solution.py:74
  617.3 21.0 %collective-permute-done.69.refs_7_ = bf16[512,1024]{1,0:T(8,128)(2,1)S(1)} collective-permute-done((bf16[512,1024]{1,0:T(8,128)(2,1)S(1)}, bf16[512,1024]{1,0:T(8,128)(2,1)S(1)}, u32[]{:S(2)}, u32[]{:S(2)}) %collective-permute-start.69) | collective-permute-done | bytes 1048608 | tf_op jit(solution)/shard_map/ppermute | solution.py:802
  638.3 23.7 %collective-permute-done.71.refs_9_ = bf16[512,1024]{1,0:T(8,128)(2,1)S(1)} collective-permute-done((bf16[512,1024]{1,0:T(8,128)(2,1)S(1)}, bf16[512,1024]{1,0:T(8,128)(2,1)S(1)}, u32[]{:S(2)}, u32[]{:S(2)}) %collective-permute-start.71) | collective-permute-done | bytes 1048608 | tf_op jit(solution)/shard_map/ppermute | solution.py:802
  669.8 58.0 %attend_backward.2.refs_3_.refs_10_ = bf16[4,512,768]{2,1,0:T(8,128)(2,1)} custom-call(s32[4]{0:T(128)} %bitcast.313, bf16[4,512,768]{2,1,0:T(8,128)(2,1)} %get-tuple-element.149.refs_1_, bf16[4,512,256]{2,1,0:T(8,128)(2,1)} %project_gc.2.refs_2_, f32[256,2048]{1,0:T(8,128)} %get-tuple-element.172.refs_3_, f32[8,2048]{1,0:T(8,128)} %get-tuple-element.173.refs_4_), custom_call_target="tpu_custom_call" | custom-call | flops 1000 | bytes 1000 | tf_op jit(solution)/shard_map/attend_backward/pallas_call | solution.py:74
  773.9 22.6 %collective-permute-done.76.refs_8_ = bf16[512,1024]{1,0:T(8,128)(2,1)} collective-permute-done((bf16[512,1024]{1,0:T(8,128)(2,1)}, bf16[512,1024]{1,0:T(8,128)(2,1)}, u32[]{:S(2)}, u32[]{:S(2)}) %collective-permute-start.76) | collective-permute-done | bytes 1048608 | tf_op jit(solution)/shard_map/ppermute | solution.py:802
  816.6 12.8 %grads_theirs.3.refs_1_ = bf16[4,8,128,1024]{3,2,1,0:T(8,128)(2,1)} custom-call(s32[5]{0:T(128)} %stack.203.refs_0_, bf16[512,1024]{1,0:T(8,128)(2,1)} %get-tuple-element.181.refs_1_.refs_2_, bf16[512,4096]{1,0:T(8,128)(2,1)} %get-tuple-element.140.refs_5_.refs_2_.refs_3_, bf16[512,1024]{1,0:T(8,128)(2,1)} %get-tuple-element.182.refs_3_.refs_4_, ...), custom_call_target="tpu_custom_call" | custom-call | flops 1000 | bytes 1000 | tf_op jit(solution)/shard_map/grads_theirs/pallas_call | solution.py:74
  864.1 15.1 %up_back.3 = (f32[512,1024]{1,0:T(8,128)}, bf16[512,1024]{1,0:T(8,128)(2,1)}, f32[8,1024]{1,0:T(8,128)}) custom-call(s32[5]{0:T(128)} %stack.203.refs_0_, bf16[4,8,128,1024]{3,2,1,0:T(8,128)(2,1)} %grads_theirs.3.refs_1_, bf16[2,2,128,1024]{3,2,1,0:T(8,128)(2,1)} %copy.190.refs_2_, bf16[128,1024]{1,0:T(8,128)(2,1)} %get-tuple-element.273.refs_3_, ...), custom_call_target="tpu_custom_call" | custom-call | flops 1000 | bytes 1000 | tf_op jit(solution)/shard_map/up_back/pallas_call | solution.py:74
  881.3 16.3 %grads_mine.3 = (bf16[8,128,1024]{2,1,0:T(8,128)(2,1)}, bf16[8,128,1024]{2,1,0:T(8,128)(2,1)}, bf16[8,128,1024]{2,1,0:T(8,128)(2,1)}, bf16[4,128,1024]{2,1,0:T(8,128)(2,1)}, bf16[4,128,1024]{2,1,0:T(8,128)(2,1)}) custom-call(s32[5]{0:T(128)} %stack.203.refs_0_, bf16[512,1024]{1,0:T(8,128)(2,1)} %get-tuple-element.191.refs_1_.refs_9_.refs_6_, ...), custom_call_target="tpu_custom_call" | custom-call | flops 1000 | bytes 1000 | tf_op jit(solution)/shard_map/grads_mine/pallas_call | solution.py:74
  910.6 24.1 %collective-permute-done.85.refs_7_ = bf16[128,1024]{1,0:T(8,128)(2,1)} collective-permute-done((bf16[128,1024]{1,0:T(8,128)(2,1)}, bf16[128,1024]{1,0:T(8,128)(2,1)}, u32[]{:S(2)}, u32[]{:S(2)}) %collective-permute-start.85) | collective-permute-done | bytes 262176 | tf_op jit(solution)/shard_map/ppermute | solution.py:806
  976.1 57.4 %attend_backward.3.refs_3_.refs_10_ = bf16[4,512,768]{2,1,0:T(8,128)(2,1)} custom-call(s32[4]{0:T(128)} %bitcast.314, bf16[4,512,768]{2,1,0:T(8,128)(2,1)} %get-tuple-element.125.refs_3_.refs_1_, bf16[4,512,256]{2,1,0:T(8,128)(2,1)} %project_gc.3.refs_2_, f32[256,2048]{1,0:T(8,128)} %get-tuple-element.197.refs_3_, f32[8,2048]{1,0:T(8,128)} %get-tuple-element.198.refs_4_), custom_call_target="tpu_custom_call" | custom-call | flops 1000 | bytes 1000 | tf_op jit(solution)/shard_map/attend_backward/pallas_call | solution.py:74
  1055.0 11.7 heads_grad.3
  1071.6 24.3 %collective-permute-done.92.refs_4_ = bf16[512,1024]{1,0:T(8,128)(2,1)S(1)} collective-permute-done((bf16[512,1024]{1,0:T(8,128)(2,1)}, bf16[512,1024]{1,0:T(8,128)(2,1)S(1)}, u32[]{:S(2)}, u32[]{:S(2)}) %collective-permute-start.92) | collective-permute-done | bytes 1048608 | tf_op jit(solution)/shard_map/ppermute | solution.py:802
  1116.9 14.4 %collective-permute-done.107 = bf16[2,2,128,1024]{3,2,1,0:T(8,128)(2,1)S(1)} collective-permute-done((bf16[2,2,128,1024]{3,2,1,0:T(8,128)(2,1)S(1)}, bf16[2,2,128,1024]{3,2,1,0:T(8,128)(2,1)S(1)}, u32[]{:S(2)}, u32[]{:S(2)}) %collective-permute-start.107) | collective-permute-done | bytes 1048608 | tf_op jit(solution)/shard_map/ppermute | solution.py:802
  1177.5 16.0 %collective-permute-done.97 = bf16[128,1024]{1,0:T(8,128)(2,1)S(1)} collective-permute-done((bf16[128,1024]{1,0:T(8,128)(2,1)S(1)}, bf16[128,1024]{1,0:T(8,128)(2,1)S(1)}, u32[]{:S(2)}, u32[]{:S(2)}) %collective-permute-start.97) | collective-permute-done | bytes 262176 | tf_op jit(solution)/shard_map/ppermute | solution.py:806
  (639 shorter events, 528.0 us)
Async XLA Ops:
  27.2 41.7 %collective-permute-start.18 = (bf16[2,128,1024]{2,1,0:T(8,128)(2,1)S(1)}, bf16[2,128,1024]{2,1,0:T(8,128)(2,1)S(1)}, u32[]{:S(2)}, u32[]{:S(2)}) collective-permute-start(bf16[2,128,1024]{2,1,0:T(8,128)(2,1)S(1)} %pad_maximum_fusion.5.refs_2_.refs_11_.refs_9_.refs_13_.refs_4_), channel_id=1, source_target_pairs={{0,8},{8,0},{16,24},{24,16},{1,9},{9,1},{17,25},{25,17},{2,10},{10... | collective-permute-start | bytes 1572872 | tf_op jit(solution)/shard_map/ppermute | solution.py:802
  28.4 40.5 %collective-permute-start.19 = (bf16[2,128,1024]{2,1,0:T(8,128)(2,1)S(1)}, bf16[2,128,1024]{2,1,0:T(8,128)(2,1)S(1)}, u32[]{:S(2)}, u32[]{:S(2)}) collective-permute-start(bf16[2,128,1024]{2,1,0:T(8,128)(2,1)S(1)} %pad_maximum_fusion.5.refs_2_.refs_11_.refs_9_.refs_13_.refs_4_), channel_id=1, source_target_pairs={{0,16},{8,24},{16,0},{24,8},{1,17},{9,25},{17,1},{25,9},{2,18},{10... | collective-permute-start | bytes 1572872 | tf_op jit(solution)/shard_map/ppermute | solution.py:802
  68.8 57.1 %collective-permute-start.10 = (bf16[512,1024]{1,0:T(8,128)(2,1)}, bf16[512,1024]{1,0:T(8,128)(2,1)S(1)}, u32[]{:S(2)}, u32[]{:S(2)}) collective-permute-start(bf16[512,1024]{1,0:T(8,128)(2,1)} %get-tuple-element.120.refs_6_.refs_2_), channel_id=1, source_target_pairs={{0,5},{1,4},{4,1},{5,0},{2,7},{3,6},{6,3},{7,2},{8,13},{9,12},{12,... | collective-permute-start | bytes 3145736 | tf_op jit(solution)/shard_map/ppermute | solution.py:802
  68.9 57.0 %collective-permute-start.8 = (bf16[512,1024]{1,0:T(8,128)(2,1)}, bf16[512,1024]{1,0:T(8,128)(2,1)S(1)}, u32[]{:S(2)}, u32[]{:S(2)}) collective-permute-start(bf16[512,1024]{1,0:T(8,128)(2,1)} %get-tuple-element.120.refs_6_.refs_2_), channel_id=1, source_target_pairs={{0,1},{1,0},{4,5},{5,4},{2,3},{3,2},{6,7},{7,6},{8,9},{9,8},{12,13... | collective-permute-start | bytes 3145736 | tf_op jit(solution)/shard_map/ppermute | solution.py:802
  69.0 56.9 %collective-permute-start.9 = (bf16[512,1024]{1,0:T(8,128)(2,1)}, bf16[512,1024]{1,0:T(8,128)(2,1)S(1)}, u32[]{:S(2)}, u32[]{:S(2)}) collective-permute-start(bf16[512,1024]{1,0:T(8,128)(2,1)} %get-tuple-element.120.refs_6_.refs_2_), channel_id=1, source_target_pairs={{0,4},{1,5},{4,0},{5,1},{2,6},{3,7},{6,2},{7,3},{8,12},{9,13},{12,... | collective-permute-start | bytes 3145736 | tf_op jit(solution)/shard_map/ppermute | solution.py:802
  73.0 49.2 %collective-permute-start.7 = (bf16[1,128,1024]{2,1,0:T(8,128)(2,1)}, bf16[1,128,1024]{2,1,0:T(8,128)(2,1)S(1)}, u32[]{:S(2)}, u32[]{:S(2)}) collective-permute-start(bf16[1,128,1024]{2,1,0:T(8,128)(2,1)} %get-tuple-element.119), channel_id=1, source_target_pairs={{0,2},{2,0},{1,3},{3,1},{4,6},{6,4},{5,7},{7,5},{8,10},{10,8},{9,1... | collective-permute-start | bytes 786440 | tf_op jit(solution)/shard_map/ppermute | solution.py:802
  75.3 121.8 %collective-permute-start.6 = (bf16[4,1,128,1024]{3,2,1,0:T(8,128)(2,1)S(1)}, bf16[4,1,128,1024]{3,2,1,0:T(8,128)(2,1)S(1)}, u32[]{:S(2)}, u32[]{:S(2)}) collective-permute-start(bf16[4,1,128,1024]{3,2,1,0:T(8,128)(2,1)S(1)} %constant_dynamic-update-slice_fusion.refs_1_.refs_4_.refs_9_.refs_10_), channel_id=1, source_target_pairs={{0,16},{8,24},{16,0},{24,8},{1,17},{9,25},{17,1},{25,9},{2,18},{10... | collective-permute-start | bytes 3145736 | tf_op jit(solution)/shard_map/ppermute | solution.py:802
  122.2 77.9 %collective-permute-start.5 = (bf16[4,1,128,1024]{3,2,1,0:T(8,128)(2,1)S(1)}, bf16[4,1,128,1024]{3,2,1,0:T(8,128)(2,1)S(1)}, u32[]{:S(2)}, u32[]{:S(2)}) collective-permute-start(bf16[4,1,128,1024]{3,2,1,0:T(8,128)(2,1)S(1)} %constant_dynamic-update-slice_fusion.refs_1_.refs_4_.refs_9_.refs_10_), channel_id=1, source_target_pairs={{0,8},{8,0},{16,24},{24,16},{1,9},{9,1},{17,25},{25,17},{2,10},{10... | collective-permute-start | bytes 3145736 | tf_op jit(solution)/shard_map/ppermute | solution.py:802
  137.1 57.9 %collective-permute-start.22 = (bf16[2,128,1024]{2,1,0:T(8,128)(2,1)}, bf16[2,128,1024]{2,1,0:T(8,128)(2,1)}, u32[]{:S(2)}, u32[]{:S(2)}) collective-permute-start(bf16[2,128,1024]{2,1,0:T(8,128)(2,1)} %get-tuple-element.122), channel_id=1, source_target_pairs={{0,2},{2,0},{1,3},{3,1},{4,6},{6,4},{5,7},{7,5},{8,10},{10,8},{9,1... | collective-permute-start | bytes 1572872 | tf_op jit(solution)/shard_map/ppermute | solution.py:802
  139.9 58.4 %collective-permute-start.21 = (bf16[2,1,128,1024]{3,2,1,0:T(8,128)(2,1)}, bf16[2,1,128,1024]{3,2,1,0:T(8,128)(2,1)}, u32[]{:S(2)}, u32[]{:S(2)}) collective-permute-start(bf16[2,1,128,1024]{3,2,1,0:T(8,128)(2,1)} %get-tuple-element.121), channel_id=1, source_target_pairs={{0,1},{1,0},{2,3},{3,2},{4,5},{5,4},{6,7},{7,6},{8,9},{9,8},{10,11... | collective-permute-start | bytes 1572872 | tf_op jit(solution)/shard_map/ppermute | solution.py:802
  161.7 50.2 %collective-permute-start.29 = (bf16[4,1,128,1024]{3,2,1,0:T(8,128)(2,1)}, bf16[4,1,128,1024]{3,2,1,0:T(8,128)(2,1)}, u32[]{:S(2)}, u32[]{:S(2)}) collective-permute-start(bf16[4,1,128,1024]{3,2,1,0:T(8,128)(2,1)} %copy-done.6), channel_id=1, source_target_pairs={{0,4},{4,0},{1,5},{5,1},{2,6},{6,2},{3,7},{7,3},{8,12},{12,8},{9,1... | collective-permute-start | bytes 3145736 | tf_op jit(solution)/shard_map/ppermute | solution.py:802
  209.4 46.6 %collective-permute-start.26 = (bf16[512,1024]{1,0:T(8,128)(2,1)}, bf16[512,1024]{1,0:T(8,128)(2,1)}, u32[]{:S(2)}, u32[]{:S(2)}) collective-permute-start(bf16[512,1024]{1,0:T(8,128)(2,1)} %get-tuple-element.131), channel_id=1, source_target_pairs={{0,5},{1,4},{4,1},{5,0},{2,7},{3,6},{6,3},{7,2},{8,13},{9,12},{12,... | collective-permute-start | bytes 3145736 | tf_op jit(solution)/shard_map/ppermute | solution.py:802
  214.3 41.8 %collective-permute-start.34 = (bf16[4,1,128,1024]{3,2,1,0:T(8,128)(2,1)}, bf16[4,1,128,1024]{3,2,1,0:T(8,128)(2,1)S(1)}, u32[]{:S(2)}, u32[]{:S(2)}) collective-permute-start(bf16[4,1,128,1024]{3,2,1,0:T(8,128)(2,1)} %constant_dynamic-update-slice_fusion.2.refs_3_.refs_8_), channel_id=1, source_target_pairs={{0,8},{8,0},{16,24},{24,16},{1,9},{9,1},{17,25},{25,17},{2,10},{10... | collective-permute-start | bytes 3145736 | tf_op jit(solution)/shard_map/ppermute | solution.py:802
  289.3 36.7 %collective-permute-start.42 = (bf16[4,1,128,1024]{3,2,1,0:T(8,128)(2,1)S(1)}, bf16[4,1,128,1024]{3,2,1,0:T(8,128)(2,1)}, u32[]{:S(2)}, u32[]{:S(2)}) collective-permute-start(bf16[4,1,128,1024]{3,2,1,0:T(8,128)(2,1)S(1)} %copy-done.15), channel_id=1, source_target_pairs={{0,4},{4,0},{1,5},{5,1},{2,6},{6,2},{3,7},{7,3},{8,12},{12,8},{9,1... | collective-permute-start | bytes 3145736 | tf_op jit(solution)/shard_map/ppermute | solution.py:802
  346.1 45.5 %collective-permute-start.48 = (bf16[512,1024]{1,0:T(8,128)(2,1)}, bf16[512,1024]{1,0:T(8,128)(2,1)S(1)}, u32[]{:S(2)}, u32[]{:S(2)}) collective-permute-start(bf16[512,1024]{1,0:T(8,128)(2,1)} %get-tuple-element.143.refs_1_.refs_2_), channel_id=1, source_target_pairs={{0,5},{1,4},{4,1},{5,0},{2,7},{3,6},{6,3},{7,2},{8,13},{9,12},{12,... | collective-permute-start | bytes 3145736 | tf_op jit(solution)/shard_map/ppermute | solution.py:802
  393.2 47.4 %collective-permute-start.52 = (bf16[4,2,128,1024]{3,2,1,0:T(8,128)(2,1)}, bf16[4,2,128,1024]{3,2,1,0:T(8,128)(2,1)}, u32[]{:S(2)}, u32[]{:S(2)}) collective-permute-start(bf16[4,2,128,1024]{3,2,1,0:T(8,128)(2,1)} %get-tuple-element.146.refs_8_.refs_4_.refs_3_.refs_7_), channel_id=1, source_target_pairs={{0,8},{8,0},{16,24},{24,16},{1,9},{9,1},{17,25},{25,17},{2,10},{10... | collective-permute-start | bytes 6291464 | tf_op jit(solution)/shard_map/ppermute | solution.py:802
  394.3 47.0 %collective-permute-start.53 = (bf16[4,2,128,1024]{3,2,1,0:T(8,128)(2,1)}, bf16[4,2,128,1024]{3,2,1,0:T(8,128)(2,1)}, u32[]{:S(2)}, u32[]{:S(2)}) collective-permute-start(bf16[4,2,128,1024]{3,2,1,0:T(8,128)(2,1)} %get-tuple-element.146.refs_8_.refs_4_.refs_3_.refs_7_), channel_id=1, source_target_pairs={{0,16},{8,24},{16,0},{24,8},{1,17},{9,25},{17,1},{25,9},{2,18},{10... | collective-permute-start | bytes 6291464 | tf_op jit(solution)/shard_map/ppermute | solution.py:802
  408.9 46.8 %collective-permute-start.60 = (bf16[4,2,128,1024]{3,2,1,0:T(8,128)(2,1)S(1)}, bf16[4,2,128,1024]{3,2,1,0:T(8,128)(2,1)S(1)}, u32[]{:S(2)}, u32[]{:S(2)}) collective-permute-start(bf16[4,2,128,1024]{3,2,1,0:T(8,128)(2,1)S(1)} %copy-done), channel_id=1, source_target_pairs={{0,4},{4,0},{1,5},{5,1},{2,6},{6,2},{3,7},{7,3},{8,12},{12,8},{9,1... | collective-permute-start | bytes 6291464 | tf_op jit(solution)/shard_map/ppermute | solution.py:802
  455.6 44.4 %collective-permute-start.61 = (bf16[4,2,128,1024]{3,2,1,0:T(8,128)(2,1)}, bf16[4,2,128,1024]{3,2,1,0:T(8,128)(2,1)}, u32[]{:S(2)}, u32[]{:S(2)}) collective-permute-start(bf16[4,2,128,1024]{3,2,1,0:T(8,128)(2,1)} %collective-permute-done.52.refs_1_.refs_9_.refs_5_.refs_4_.refs_8_), channel_id=1, source_target_pairs={{0,4},{4,0},{1,5},{5,1},{2,6},{6,2},{3,7},{7,3},{8,12},{12,8},{9,1... | collective-permute-start | bytes 6291464 | tf_op jit(solution)/shard_map/ppermute | solution.py:802
  610.9 117.0 %collective-permute-start.68 = (bf16[2,4,128,1024]{3,2,0,1:T(8,128)(2,1)}, bf16[2,4,128,1024]{3,2,0,1:T(8,128)(2,1)}, u32[]{:S(2)}, u32[]{:S(2)}) collective-permute-start(bf16[2,4,128,1024]{3,2,0,1:T(8,128)(2,1)} %copy.182), channel_id=1, source_target_pairs={{0,16},{8,24},{16,0},{24,8},{1,17},{9,25},{17,1},{25,9},{2,18},{10... | collective-permute-start | bytes 6291464 | tf_op jit(solution)/shard_map/ppermute | solution.py:802
  614.2 119.2 %collective-permute-start.67 = (bf16[2,4,128,1024]{3,2,0,1:T(8,128)(2,1)}, bf16[2,4,128,1024]{3,2,0,1:T(8,128)(2,1)S(1)}, u32[]{:S(2)}, u32[]{:S(2)}) collective-permute-start(bf16[2,4,128,1024]{3,2,0,1:T(8,128)(2,1)} %copy.181), channel_id=1, source_target_pairs={{0,8},{8,0},{16,24},{24,16},{1,9},{9,1},{17,25},{25,17},{2,10},{10... | collective-permute-start | bytes 6291464 | tf_op jit(solution)/shard_map/ppermute | solution.py:802
  615.7 46.3 %collective-permute-start.71 = (bf16[512,1024]{1,0:T(8,128)(2,1)S(1)}, bf16[512,1024]{1,0:T(8,128)(2,1)S(1)}, u32[]{:S(2)}, u32[]{:S(2)}) collective-permute-start(bf16[512,1024]{1,0:T(8,128)(2,1)S(1)} %copy-done.20), channel_id=1, source_target_pairs={{0,5},{1,4},{4,1},{5,0},{2,7},{3,6},{6,3},{7,2},{8,13},{9,12},{12,... | collective-permute-start | bytes 3145736 | tf_op jit(solution)/shard_map/ppermute | solution.py:802
  749.6 46.9 %collective-permute-start.76 = (bf16[512,1024]{1,0:T(8,128)(2,1)}, bf16[512,1024]{1,0:T(8,128)(2,1)}, u32[]{:S(2)}, u32[]{:S(2)}) collective-permute-start(bf16[512,1024]{1,0:T(8,128)(2,1)} %get-tuple-element.179), channel_id=1, source_target_pairs={{0,5},{1,4},{4,1},{5,0},{2,7},{3,6},{6,3},{7,2},{8,13},{9,12},{12,... | collective-permute-start | bytes 3145736 | tf_op jit(solution)/shard_map/ppermute | solution.py:802
  829.4 51.8 %collective-permute-start.81 = (bf16[4,8,128,1024]{3,2,1,0:T(8,128)(2,1)}, bf16[4,8,128,1024]{3,2,1,0:T(8,128)(2,1)}, u32[]{:S(2)}, u32[]{:S(2)}) collective-permute-start(bf16[4,8,128,1024]{3,2,1,0:T(8,128)(2,1)} %grads_theirs.3.refs_1_), channel_id=1, source_target_pairs={{0,4},{4,0},{1,5},{5,1},{2,6},{6,2},{3,7},{7,3},{8,12},{12,8},{9,1... | collective-permute-start | bytes 25165832 | tf_op jit(solution)/shard_map/ppermute | solution.py:802
  897.6 136.0 %collective-permute-start.82 = (bf16[2,4,128,1024]{3,2,1,0:T(8,128)(2,1)}, bf16[2,4,128,1024]{3,2,1,0:T(8,128)(2,1)S(1)}, u32[]{:S(2)}, u32[]{:S(2)}) collective-permute-start(bf16[2,4,128,1024]{3,2,1,0:T(8,128)(2,1)} %bitcast.259), channel_id=1, source_target_pairs={{0,8},{8,0},{16,24},{24,16},{1,9},{9,1},{17,25},{25,17},{2,10},{10... | collective-permute-start | bytes 6291464 | tf_op jit(solution)/shard_map/ppermute | solution.py:802
  898.2 135.3 %collective-permute-start.83 = (bf16[2,4,128,1024]{3,2,1,0:T(8,128)(2,1)}, bf16[2,4,128,1024]{3,2,1,0:T(8,128)(2,1)}, u32[]{:S(2)}, u32[]{:S(2)}) collective-permute-start(bf16[2,4,128,1024]{3,2,1,0:T(8,128)(2,1)} %bitcast.258), channel_id=1, source_target_pairs={{0,16},{8,24},{16,0},{24,8},{1,17},{9,25},{17,1},{25,9},{2,18},{10... | collective-permute-start | bytes 6291464 | tf_op jit(solution)/shard_map/ppermute | solution.py:802
  900.0 38.1 %collective-permute-start.84 = (bf16[2,128,1024]{2,1,0:T(8,128)(2,1)}, bf16[2,128,1024]{2,1,0:T(8,128)(2,1)}, u32[]{:S(2)}, u32[]{:S(2)}) collective-permute-start(bf16[2,128,1024]{2,1,0:T(8,128)(2,1)} %fusion.6), channel_id=1, source_target_pairs={{0,2},{2,0},{1,3},{3,1},{4,6},{6,4},{5,7},{7,5},{8,10},{10,8},{9,1... | collective-permute-start | bytes 1572872 | tf_op jit(solution)/shard_map/ppermute | solution.py:802
  1051.1 44.8 %collective-permute-start.92 = (bf16[512,1024]{1,0:T(8,128)(2,1)}, bf16[512,1024]{1,0:T(8,128)(2,1)S(1)}, u32[]{:S(2)}, u32[]{:S(2)}) collective-permute-start(bf16[512,1024]{1,0:T(8,128)(2,1)} %get-tuple-element.202), channel_id=1, source_target_pairs={{0,5},{1,4},{4,1},{5,0},{2,7},{3,6},{6,3},{7,2},{8,13},{9,12},{12,... | collective-permute-start | bytes 3145736 | tf_op jit(solution)/shard_map/ppermute | solution.py:802
  1112.9 52.5 %collective-permute-start.106 = (bf16[2,2,128,1024]{3,2,1,0:T(8,128)(2,1)}, bf16[2,2,128,1024]{3,2,1,0:T(8,128)(2,1)S(1)}, u32[]{:S(2)}, u32[]{:S(2)}) collective-permute-start(bf16[2,2,128,1024]{3,2,1,0:T(8,128)(2,1)} %fusion.1), channel_id=1, source_target_pairs={{0,16},{8,24},{16,0},{24,8},{1,17},{9,25},{17,1},{25,9},{2,18},{10... | collective-permute-start | bytes 3145736 | tf_op jit(solution)/shard_map/ppermute | solution.py:802
  1115.1 43.4 %collective-permute-start.95 = (bf16[2,128,1024]{2,1,0:T(8,128)(2,1)}, bf16[2,128,1024]{2,1,0:T(8,128)(2,1)}, u32[]{:S(2)}, u32[]{:S(2)}) collective-permute-start(bf16[2,128,1024]{2,1,0:T(8,128)(2,1)} %get-tuple-element.216), channel_id=1, source_target_pairs={{0,16},{8,24},{16,0},{24,8},{1,17},{9,25},{17,1},{25,9},{2,18},{10... | collective-permute-start | bytes 1572872 | tf_op jit(solution)/shard_map/ppermute | solution.py:802
  1115.2 43.3 %collective-permute-start.96 = (bf16[2,128,1024]{2,1,0:T(8,128)(2,1)}, bf16[2,128,1024]{2,1,0:T(8,128)(2,1)}, u32[]{:S(2)}, u32[]{:S(2)}) collective-permute-start(bf16[2,128,1024]{2,1,0:T(8,128)(2,1)} %get-tuple-element.217), channel_id=1, source_target_pairs={{0,24},{8,16},{16,8},{24,0},{1,25},{9,17},{17,9},{25,1},{2,26},{10... | collective-permute-start | bytes 1572872 | tf_op jit(solution)/shard_map/ppermute | solution.py:802
  1142.6 88.4 %collective-permute-start.93 = (bf16[512,1024]{1,0:T(8,128)(2,1)}, bf16[512,1024]{1,0:T(8,128)(2,1)}, u32[]{:S(2)}, u32[]{:S(2)}) collective-permute-start(bf16[512,1024]{1,0:T(8,128)(2,1)} %add_convert_fusion.1), channel_id=1, source_target_pairs={{0,0},{2,4},{4,2},{6,6},{1,1},{3,5},{5,3},{7,7},{8,8},{10,12},{12,... | collective-permute-start | bytes 3145736 | tf_op jit(solution)/shard_map/ppermute | solution.py:806
  (181 other events, 3089.6 us)

commit v4 on v3

v4 whole, which is shorter than its diff:
```python
import jax
import jax.numpy as jnp
from jax import lax
from jax.experimental import pallas as pl
from jax.experimental.pallas import tpu as pltpu
from jax.sharding import Mesh
from jax.sharding import PartitionSpec as P

D = 1024
HD = 64
HEADS = 16
FF = 4096
LAYERS = 2
SEQLEN = 2048
WINDOW = 1024
EPS = 1e-06
FILL = -1000000000.0

F32 = jnp.float32
BF16 = jnp.bfloat16
GROUP = ("c", "zl")
MODEL = ("zh", "zl")
ALL = ("zh", "zl", "q", "c")
VMEM_LIMIT = 56 * 1024 * 1024
TIMES = {
    "gate": 0.1, "norm_up": 20.0, "down_norm": 20.0, "units_back": 20.0, "up_back": 20.0, "norm_back": 6.0,
    "sum_norm_back": 20.0, "grads_theirs": 0.2, "grads_mine": 0.2, "project_qkv": 0.2, "project_gc": 0.2,
    "project_attn": 0.2, "project_gx": 0.2, "heads_grad": 0.2, "attend_forward": 40.0, "attend_backward": 60.0,
}
PEAK = 0.35e9
NT = (((1,), (1,)), ((), ()))
NN = (((1,), (0,)), ((), ()))
ROWS = 128
CHUNK = 64
BQ = 256


def mm(left, right, dims=NN):
    return lax.dot_general(left, right, dims, preferred_element_type=F32)


def full(shape):
    return pl.BlockSpec(shape, lambda *_: (0,) * len(shape))


ANY = pl.BlockSpec(memory_space=pl.ANY)


def sds(shape, kind):
    return jax.ShapeDtypeStruct(shape, kind)


class Flow:
    def __init__(self, scal):
        self.scal, self.before, self.held = scal, [], {}

    def wait(self, *arrays):
        self.before += arrays

    def hold(self, **arrays):
        self.held.update(arrays)

    def free(self, name):
        return self.held.pop(name)


def call(flow, body, grid, in_specs, out_specs, out_shape, scratch, args, flops, traffic, name, scalars=None):
    scalars = (flow.scal,) if scalars is None else scalars
    single = not isinstance(out_specs, (list, tuple))
    out_specs = [out_specs] if single else list(out_specs)
    out_shape = [out_shape] if single else list(out_shape)
    before, held = flow.before, list(flow.held.items())
    ns, nb, nh, no = len(scalars), len(before), len(held), len(out_specs)
    first, last = ns + nb + nh, ns + nb + nh + len(args) + no

    def wrapped(*refs):
        body(*refs[:ns], *refs[first:last], *refs[last + nh :])

    result = pl.pallas_call(
        wrapped,
        grid_spec=pltpu.PrefetchScalarGridSpec(
            num_scalar_prefetch=ns,
            grid=grid,
            in_specs=[ANY] * (nb + nh) + list(in_specs),
            out_specs=out_specs + [ANY] * nh,
            scratch_shapes=scratch,
        ),
        out_shape=out_shape + [sds(array.shape, array.dtype) for _, array in held],
        input_output_aliases={ns + nb + i: no + i for i in range(nh)},
        compiler_params=pltpu.CompilerParams(
            dimension_semantics=("arbitrary",) * len(grid), vmem_limit_bytes=VMEM_LIMIT
        ),
        cost_estimate=pl.CostEstimate(flops=int(TIMES[name] * PEAK), bytes_accessed=1024, transcendentals=0),
        name=name,
    )(*scalars, *before, *[array for _, array in held], *args)
    flow.before = []
    flow.held = {key: value for (key, _), value in zip(held, result[no:])}
    return result[0] if single else result[:no]


def gate(flow):
    if flow.held:
        call(flow, lambda *refs: None, (1,), [], [], [], [], [], 0, 0, "gate")


S_P, S_Q, S_C, S_ZH, S_Z = range(5)


def norm_rows(values_in):
    centred = values_in - jnp.mean(values_in, -1, keepdims=True)
    variance = jnp.mean(centred * centred, -1, keepdims=True)
    inverse = lax.rsqrt(variance + EPS)
    return centred * inverse, inverse


def norm_back_rows(grad, normed, inverse, gain):
    scaled = grad * gain
    centred = scaled - jnp.mean(scaled, -1, keepdims=True) - normed * jnp.mean(scaled * normed, -1, keepdims=True)
    return centred * inverse


def fold_rows(values_in):
    return jnp.sum(values_in.reshape(-1, 8, values_in.shape[-1]), 0)


def read(part, rows):
    return (part[0, rows, :] if len(part.shape) == 3 else part[rows, :]).astype(F32)


def part_spec(part):
    shape = part.shape
    return full(shape) if len(shape) == 2 else pl.BlockSpec((1,) + shape[1:], lambda *_: (0, 0, 0))


ONE, ZERO, TABLE = 0, 1, 16


def gain_row(layer, index):
    return 2 + 6 * layer + index


def shift_row(layer, index):
    return 4 + 6 * layer + index


def row_of(vec_ref, row):
    return vec_ref[row : row + 1, :]


def norm_forward(get_total, tokens, vec, gain, shift, n_ref, low_ref, inv_ref):

    def step(index, carry):
        rows = pl.ds(pl.multiple_of(index * CHUNK, CHUNK), CHUNK)
        normed, inverse = norm_rows(get_total(rows))
        n_ref[rows, :] = normed
        low_ref[rows, :] = (normed * row_of(vec, gain) + row_of(vec, shift)).astype(BF16)
        inv_ref[rows, :] = jnp.broadcast_to(inverse, (CHUNK, 128))
        return carry

    lax.fori_loop(0, tokens // CHUNK, step, 0)


def norm_backward(get_grad, tokens, n_ref, inv_ref, vec, gain, g_ref, low_ref, sums_ref):
    def step(index, carry):
        rows = pl.ds(pl.multiple_of(index * CHUNK, CHUNK), CHUNK)
        grad = get_grad(rows)
        normed = n_ref[rows, :]
        result = norm_back_rows(grad, normed, inv_ref[rows, 0:1], row_of(vec, gain))
        low = result.astype(BF16)
        g_ref[rows, :] = result
        low_ref[rows, :] = low
        return (
            carry[0] + fold_rows(grad * normed),
            carry[1] + fold_rows(grad),
            carry[2] + fold_rows(low.astype(F32)),
        )

    zero = jnp.zeros((8, D), F32)
    sums = lax.fori_loop(0, tokens // CHUNK, step, (zero, zero, zero))
    sums_ref[...] = jnp.zeros(sums_ref.shape, F32)
    for row, member in enumerate(sums):
        sums_ref[row : row + 1, :] = jnp.sum(member, 0, keepdims=True)


def away(s):
    return (s & 1) * 2 + s // 2


class Streamed:
    def __init__(self, refs, buffer, sems, scal):
        self.refs, self.buffer, self.sems, self.scal = refs, buffer, sems, scal

    def copies(self, s):
        slot = lax.rem(s, 2)
        for k, ref in enumerate(self.refs):
            for q in range(4):
                row = (2 * q + (self.scal[S_C] ^ k)) * ROWS
                yield pltpu.make_async_copy(
                    ref.at[s, q], self.buffer.at[slot, pl.ds(pl.multiple_of(row, ROWS), ROWS), :],
                    self.sems.at[slot, 4 * k + q],
                )

    def start(self, s):
        for copy in self.copies(s):
            copy.start()

    def wait(self, s):
        for copy in self.copies(s):
            copy.wait()

    def turn(self, s, count):
        @pl.when(s == 0)
        def _():
            self.start(s)

        @pl.when(s + 1 < count)
        def _():
            self.start(s + 1)


def piece_shapes(width):
    return [pltpu.VMEM((2, D, width), BF16), pltpu.SemaphoreType.DMA((2, 8))]


def gelu_parts(u):
    size = jnp.abs(u)
    t = 1.0 / (1.0 + 0.2316419 * size)
    poly = t * (0.127414796 + t * (-0.142248368 + t * (0.7107068705 + t * (-0.7265760135 + t * 0.5307027145))))
    bell = jnp.exp(-0.5 * (u * u))
    tail = poly * bell
    cdf = jnp.where(u >= 0, 1.0 - tail, tail)
    return u * cdf, cdf + u * (0.3989422804014327 * bell)


def tiles(tokens, width):
    for i in range(2):
        for j in range(2):
            yield slice(i * tokens // 2, (i + 1) * tokens // 2), slice(j * width // 2, (j + 1) * width // 2)


def norm_up(flow, prev, parts, vec, rows_used, weight, bias, count):
    tokens = prev.shape[0]
    width = FF // count

    def body(scal_ref, prev_ref, *refs):
        part_refs, refs = refs[: len(parts)], refs[len(parts) :]
        vec_ref, bias_ref, refs = refs[0], refs[1], refs[2:]
        pieces, (n_ref, low_ref, inv_ref, act_ref, slope_ref, buffer, sems) = refs[:2], refs[2:]
        s = pl.program_id(0)
        stream = Streamed(pieces, buffer, sems, scal_ref)
        stream.turn(s, count)

        @pl.when(s == 0)
        def _():
            def total(rows):
                attn = read(part_refs[0], rows)
                for part in part_refs[1:]:
                    attn = attn + read(part, rows)
                before = read(prev_ref, rows) * row_of(vec_ref, rows_used[0]) + row_of(vec_ref, rows_used[1])
                return before + (attn + row_of(vec_ref, rows_used[2]))

            norm_forward(total, tokens, vec_ref, *rows_used[3:], n_ref, low_ref, inv_ref)

        stream.wait(s)
        slot = lax.rem(s, 2)
        for rows, cols in tiles(tokens, width):
            act, slope = gelu_parts(mm(low_ref[rows, :], buffer[slot, :, cols]) + bias_ref[0, :, cols])
            act_ref[rows, cols] = act.astype(BF16)
            slope_ref[rows, cols] = slope.astype(BF16)

    column = pl.BlockSpec((tokens, width), lambda s, _: (0, s))
    return call(
        flow, body, (count,),
        [full((tokens, D))] + [part_spec(part) for part in parts]
        + [full((TABLE, D)), pl.BlockSpec((1, 1, width), lambda s, _: (s, 0, 0))] + [ANY] * 2,
        [full((tokens, D)), full((tokens, D)), full((tokens, 128)), column, column],
        [sds((tokens, D), F32), sds((tokens, D), BF16), sds((tokens, 128), F32)] + [sds((tokens, FF), BF16)] * 2,
        piece_shapes(width), [prev, *parts, vec, bias, *weight], 2 * tokens * D * FF,
        2 * (D * FF + tokens * (10 * D + 2 * FF)), "norm_up",
    )


def down_norm(flow, act, weight, prev, vec, rows_used, count):
    tokens = prev.shape[0]
    width = FF // count

    def body(scal_ref, act_ref, prev_ref, vec_ref, *refs):
        pieces, (n_ref, low_ref, inv_ref, buffer, sems, acc) = refs[:2], refs[2:]
        s = pl.program_id(0)
        stream = Streamed(pieces, buffer, sems, scal_ref)
        stream.turn(s, count)
        stream.wait(s)
        value = mm(act_ref[...], buffer[lax.rem(s, 2)], NT)

        @pl.when(s == 0)
        def _():
            acc[...] = value

        @pl.when(s > 0)
        def _():
            acc[...] += value

        @pl.when(s == count - 1)
        def _():
            def total(rows):
                before = prev_ref[rows, :] * row_of(vec_ref, rows_used[0]) + row_of(vec_ref, rows_used[1])
                return before + (acc[rows, :] + row_of(vec_ref, rows_used[2]))

            norm_forward(total, tokens, vec_ref, *rows_used[3:], n_ref, low_ref, inv_ref)

    return call(
        flow, body, (count,),
        [pl.BlockSpec((tokens, width), lambda s, _: (0, s)), full((tokens, D)), full((TABLE, D))] + [ANY] * 2,
        [full((tokens, D)), full((tokens, D)), full((tokens, 128))],
        [sds((tokens, D), F32), sds((tokens, D), BF16), sds((tokens, 128), F32)],
        piece_shapes(width) + [pltpu.VMEM((tokens, D), F32)], [act, prev, vec, *weight], 2 * tokens * D * FF,
        2 * (D * FF + tokens * (5 * D + FF)), "down_norm",
    )


def units_back(flow, grad, weight, slope, count):
    tokens = grad.shape[0]
    width = FF // count

    def body(scal_ref, grad_ref, slope_ref, *refs):
        pieces, (out_ref, sum_ref, buffer, sems) = refs[:2], refs[2:]
        s = pl.program_id(0)
        stream = Streamed(pieces, buffer, sems, scal_ref)
        stream.turn(s, count)
        stream.wait(s)
        slot = lax.rem(s, 2)
        sums = {}
        for rows, cols in tiles(tokens, width):
            low = (mm(grad_ref[rows, :], buffer[slot, :, cols]) * slope_ref[rows, cols].astype(F32)).astype(BF16)
            out_ref[rows, cols] = low
            part = fold_rows(low.astype(F32))
            sums[cols.start] = sums[cols.start] + part if cols.start in sums else part
            if rows.start > 0:
                sum_ref[0, :, cols] = jnp.sum(sums[cols.start], 0, keepdims=True)

    column = pl.BlockSpec((tokens, width), lambda s, _: (0, s))
    return call(
        flow, body, (count,), [full((tokens, D)), column] + [ANY] * 2,
        [column, pl.BlockSpec((1, 1, width), lambda s, _: (s, 0, 0))],
        [sds((tokens, FF), BF16), sds((count, 1, width), F32)], piece_shapes(width), [grad, slope, *weight],
        2 * tokens * D * FF, 2 * (D * FF + tokens * (D + 2 * FF)), "units_back",
    )


def up_back(flow, gu, weight, residual, normed, inverse, vec, gain, count):
    tokens = residual.shape[0]
    width = FF // count

    def body(scal_ref, gu_ref, res_ref, n_ref, inv_ref, vec_ref, *refs):
        pieces, (g_ref, low_ref, sums_ref, buffer, sems, acc) = refs[:2], refs[2:]
        s = pl.program_id(0)
        stream = Streamed(pieces, buffer, sems, scal_ref)
        stream.turn(s, count)
        stream.wait(s)
        value = mm(gu_ref[...], buffer[lax.rem(s, 2)], NT)

        @pl.when(s == 0)
        def _():
            acc[...] = value

        @pl.when(s > 0)
        def _():
            acc[...] += value

        @pl.when(s == count - 1)
        def _():
            norm_backward(
                lambda rows: res_ref[rows, :] + acc[rows, :], tokens, n_ref, inv_ref, vec_ref, gain, g_ref, low_ref,
                sums_ref,
            )

    return call(
        flow, body, (count,),
        [pl.BlockSpec((tokens, width), lambda s, _: (0, s)), full((tokens, D)), full((tokens, D)), full((tokens, 128)),
         full((TABLE, D))] + [ANY] * 2,
        [full((tokens, D)), full((tokens, D)), full((8, D))],
        [sds((tokens, D), F32), sds((tokens, D), BF16), sds((8, D), F32)],
        piece_shapes(width) + [pltpu.VMEM((tokens, D), F32)], [gu, residual, normed, inverse, vec, *weight],
        2 * tokens * D * FF, 2 * (D * FF + tokens * (8 * D + FF)), "up_back",
    )


def norm_back(flow, grad, normed, inverse, vec, gain):
    tokens = grad.shape[0]

    def body(scal_ref, grad_ref, n_ref, inv_ref, vec_ref, g_ref, low_ref, sums_ref):
        norm_backward(lambda rows: read(grad_ref, rows), tokens, n_ref, inv_ref, vec_ref, gain, g_ref, low_ref, sums_ref)

    return call(
        flow, body, (1,), [full((tokens, D)), full((tokens, D)), full((tokens, 128)), full((TABLE, D))],
        [full((tokens, D)), full((tokens, D)), full((8, D))],
        [sds((tokens, D), F32), sds((tokens, D), BF16), sds((8, D), F32)], [], [grad, normed, inverse, vec],
        20 * tokens * D, 12 * tokens * D, "norm_back",
    )


def sum_norm_back(flow, residual, parts, normed, inverse, vec, gain):
    tokens = residual.shape[0]

    def body(scal_ref, res_ref, *refs):
        part_refs, (n_ref, inv_ref, vec_ref, g_ref, low_ref, sums_ref) = refs[: len(parts)], refs[len(parts) :]

        def grad(rows):
            total = read(part_refs[0], rows)
            for part in part_refs[1:]:
                total = total + read(part, rows)
            return res_ref[rows, :] + total

        norm_backward(grad, tokens, n_ref, inv_ref, vec_ref, gain, g_ref, low_ref, sums_ref)

    return call(
        flow, body, (1,), [full((tokens, D))] + [part_spec(part) for part in parts]
        + [full((tokens, D)), full((tokens, 128)), full((TABLE, D))],
        [full((tokens, D)), full((tokens, D)), full((8, D))],
        [sds((tokens, D), F32), sds((tokens, D), BF16), sds((8, D), F32)], [],
        [residual, *parts, normed, inverse, vec], 20 * tokens * D, 22 * tokens * D, "sum_norm_back",
    )


def turn_rows(scal_ref, x_ref, turned, core):
    for r in range(4):
        row = ((scal_ref[S_Q] ^ r) * 2 + core) * ROWS
        turned[r * ROWS : (r + 1) * ROWS, :] = x_ref[:, pl.ds(pl.multiple_of(row, ROWS), ROWS)].T


def unit_grads(flow, down, up, received, count, sibling):
    tokens = down[0].shape[0]
    width = down[1].shape[1] // count
    half = count // 2
    steps = 2 * count

    def body(scal_ref, x0_ref, y0_ref, x1_ref, y1_ref, *refs):
        turned, t = refs[-1], pl.program_id(0)
        m, s = t // count, lax.rem(t, count)
        core = scal_ref[S_C] ^ 1 if sibling else scal_ref[S_C]

        @pl.when(t == 0)
        def _():
            turn_rows(scal_ref, x0_ref, turned, core)

        @pl.when(t == count)
        def _():
            turn_rows(scal_ref, x1_ref, turned, core)

        def store(y_ref):
            value = mm(turned[...], y_ref[...]).reshape(4, ROWS, width)
            if sibling:
                refs[0][:, 0] = value.astype(BF16)
                return
            if received is not None:
                value = value + refs[0][:, 0].astype(F32)
            value = value.astype(BF16)
            own, to_x, to_y, rest_x, rest_y = refs[-6:-1]
            spot = lax.rem(s, half) * 2 + m
            own[s // half * count + spot] = value[0]

            @pl.when(s < half)
            def _():
                to_x[spot] = value[1]
                to_x[count + spot] = value[3]
                rest_y[spot] = value[2]

            @pl.when(s >= half)
            def _():
                rest_x[spot] = value[1]
                to_y[spot] = value[2]
                to_y[count + spot] = value[3]

        @pl.when(m == 0)
        def _():
            store(y0_ref)

        @pl.when(m == 1)
        def _():
            store(y1_ref)

    left = full((tokens, D))
    pick_down = lambda t, scal_ref: (0, scal_ref[S_Z] ^ away(jnp.minimum(t, count - 1)))
    pick_up = lambda t, scal_ref: (0, scal_ref[S_Z] ^ away(jnp.maximum(t - count, 0)))
    specs = [left, pl.BlockSpec((tokens, width), pick_down), left, pl.BlockSpec((tokens, width), pick_up)]
    args = [*down, *up]
    one = pl.BlockSpec((4, 1, ROWS, width), lambda t, _: (0, t, 0, 0))
    if sibling:
        out_specs, out_shape = one, sds((4, steps, ROWS, width), BF16)
    else:
        if received is not None:
            specs.append(one)
            args.append(received)
        shapes = [(steps, ROWS, width)] * 3 + [(count, ROWS, width)] * 2
        out_specs, out_shape = [full(shape) for shape in shapes], [sds(shape, BF16) for shape in shapes]
    return call(
        flow, body, (steps,), specs, out_specs, out_shape, [pltpu.VMEM((4 * ROWS, tokens), BF16)], args,
        0, 0, "grads_theirs" if sibling else "grads_mine",
    )


def fetch_heads_weight(scal_ref, pieces, cols, buffer, sems):
    copies = []
    for r in range(4):
        for k in range(2):
            row = ((scal_ref[S_Q] ^ r) * 2 + (scal_ref[S_ZH] ^ k)) * ROWS
            copies.append(
                pltpu.make_async_copy(
                    pieces[r].at[k, pl.ds(0, ROWS), cols], buffer.at[pl.ds(pl.multiple_of(row, ROWS), ROWS), :],
                    sems.at[2 * r + k],
                )
            )
    for copy in copies:
        copy.start()
    for copy in copies:
        copy.wait()


def by_member(shape):
    return pl.BlockSpec((1,) + shape, lambda r, scal_ref: (scal_ref[S_P] ^ r, 0, 0))


def heads_weight_scratch(width):
    return [pltpu.VMEM((D, width), BF16), pltpu.SemaphoreType.DMA((8,))]


def project_in(flow, lefts, across, weight, cols, bias, name):
    tokens = lefts[0].shape[0]
    width = cols.stop - cols.start

    def body(scal_ref, left_ref, right_ref, *refs):
        if bias is not None:
            bias_ref, refs = refs[0], refs[1:]
        pieces, (out_ref, buffer, sems) = refs[:4], refs[4:]
        step = pl.program_id(0)

        @pl.when(step == 0)
        def _():
            fetch_heads_weight(scal_ref, pieces, cols, buffer, sems)

        for r, left in enumerate((left_ref, right_ref)):

            @pl.when(step == r)
            def _(left=left):
                value = mm(left[...], buffer[...])
                if bias is not None:
                    value = value + bias_ref[...]
                out_ref[0] = value.astype(BF16)

    extra, extra_specs = ([], []) if bias is None else ([bias], [full((1, width))])
    return call(
        flow, body, (2,), [full((tokens, D))] * 2 + extra_specs + [ANY] * 4,
        pl.BlockSpec((1, tokens, width), lambda r, scal_ref: ((scal_ref[S_P] >> 1) ^ r, 0, 0)),
        sds((2, tokens, width), BF16), heads_weight_scratch(width), [*lefts, *extra, *weight], 0, 0, name,
    )


def project_out(flow, blocks, members, weight, cols, stacked, name):
    count, tokens, width = blocks.shape

    def body(scal_ref, block_ref, *refs):
        pieces, outs, (buffer, sems) = refs[:4], refs[4:-2], refs[-2:]
        step = pl.program_id(0)

        @pl.when(step == 0)
        def _():
            fetch_heads_weight(scal_ref, pieces, cols, buffer, sems)

        value = mm(block_ref[0], buffer[...], NT).astype(BF16)
        if stacked:
            outs[0][0] = value
            return
        for r, out in enumerate(outs):

            @pl.when(step == r)
            def _(out=out):
                out[...] = value

    first, last = members
    pick = lambda r, scal_ref: (scal_ref[S_P] ^ (first + r * (last - first)), 0, 0)
    if stacked:
        out_specs, out_shape = pl.BlockSpec((1, tokens, D), lambda r, _: (r, 0, 0)), sds((2, tokens, D), BF16)
    else:
        out_specs, out_shape = [full((tokens, D))] * 2, [sds((tokens, D), BF16)] * 2
    return call(
        flow, body, (2,), [pl.BlockSpec((1, tokens, width), pick)] + [ANY] * 4, out_specs, out_shape,
        heads_weight_scratch(width), [blocks, *weight], 0, 0, name,
    )


def heads_grad(flow, xs, gqkv, gas, ctx):
    count, tokens, width = gqkv.shape
    out_width = ctx.shape[2]

    def body(scal_ref, *refs):
        x_refs, refs = refs[:count], refs[count:]
        ga_refs, refs = refs[:count], refs[count:]
        g_ref, ctx_ref = refs[:2]
        outs, (sum_ref, acc, acc_out) = refs[2:4], refs[4:]
        step = pl.program_id(0)
        for r in range(count):

            @pl.when(step == r)
            def _(r=r):
                value = mm(x_refs[r][...].T, g_ref[0])
                value_out = mm(ga_refs[r][...].T, ctx_ref[0])
                sums = jnp.sum(g_ref[0].astype(F32), 0, keepdims=True)
                if r == 0:
                    acc[...] = value
                    acc_out[...] = value_out
                    sum_ref[...] = sums
                else:
                    acc[...] += value
                    acc_out[...] += value_out
                    sum_ref[...] += sums

        @pl.when(step == count - 1)
        def _():
            for r in range(4):
                for k in range(2):
                    row = ((scal_ref[S_Q] ^ r) * 2 + (scal_ref[S_ZH] ^ k)) * ROWS
                    rows = pl.ds(pl.multiple_of(row, ROWS), ROWS)
                    outs[r % 2][r // 2, k, :, :width] = acc[rows, :].astype(BF16)
                    outs[r % 2][r // 2, k, :, width:] = acc_out[rows, :].astype(BF16)

    shape = (2, 2, ROWS, width + out_width)
    return call(
        flow, body, (count,), [full((tokens, D))] * (2 * count) + [by_member((tokens, width)), by_member((tokens, out_width))],
        [full(shape)] * 2 + [full((1, width))], [sds(shape, BF16)] * 2 + [sds((1, width), F32)],
        [pltpu.VMEM((D, width), F32), pltpu.VMEM((D, out_width), F32)], [*xs, *gas, gqkv, ctx],
        2 * tokens * D * (width + out_width) * count, 4 * count * tokens * (D + width), "heads_grad",
    )


def reach(ends_ref, row):
    first = jnp.zeros_like(row)
    for index in range(3):
        first = jnp.where(row >= ends_ref[index], ends_ref[index], first)
    last = jnp.full_like(row, SEQLEN)
    for index in (2, 1, 0):
        last = jnp.where(row < ends_ref[index], ends_ref[index], last)
    return jnp.maximum(first, row - (WINDOW - 1)), jnp.minimum(last, row + WINDOW)


def chunks_of(scal_ref, near_ref, far_ref):
    here = scal_ref[S_P] & 1
    for core in range(2):
        yield 2 * core + here, near_ref.at[core]
        yield 2 * core + 1 - here, far_ref.at[core]


def over_keys(ends_ref, start, chunk, block):
    low_first, high_first = reach(ends_ref, start)
    low_last, high_last = reach(ends_ref, start + BQ - 1)
    low_row, high_row = reach(ends_ref, start + lax.broadcasted_iota(jnp.int32, (1, BQ), 1))

    def one(b, carry):
        open_all = (b * chunk >= low_last) & ((b + 1) * chunk <= high_first)

        @pl.when(open_all)
        def _():
            block(b, None)

        @pl.when(jnp.logical_not(open_all))
        def _():
            key = b * chunk + lax.broadcasted_iota(jnp.int32, (chunk, BQ), 0)
            block(b, (key >= low_row) & (key < high_row))

        return carry

    lax.fori_loop(low_first // chunk, (high_last + chunk - 1) // chunk, one, 0)


def attend_forward(flow, ends, qkv):
    _, chunk, width3 = qkv[0].shape
    count = SEQLEN // chunk
    width = width3 // 3
    heads = width // HD
    steps = SEQLEN // BQ
    per = chunk // BQ

    def body(scal_ref, ends_ref, near_ref, far_ref, ctx_ref, wide_ref, lse_ref, qh, kh, vt, acc, tops, sums, scores):
        step = pl.program_id(0)

        @pl.when(step == 0)
        def _():
            for j, block in chunks_of(scal_ref, near_ref, far_ref):
                rows = pl.ds(pl.multiple_of(j * chunk, chunk), chunk)
                for h in range(heads):
                    qh[h, rows, :] = block[:, h * HD : (h + 1) * HD] * BF16(HD**-0.5)
                    kh[h, rows, :] = block[:, width + h * HD : width + (h + 1) * HD]
                vt[j] = block[:, 2 * width :].T

        start = step * BQ
        rows = pl.ds(pl.multiple_of(start, BQ), BQ)
        acc[...] = jnp.zeros(acc.shape, F32)
        tops[...] = jnp.full(tops.shape, -3.0e38, F32)
        sums[...] = jnp.zeros(sums.shape, F32)

        def score(b, allowed):
            keys = pl.ds(pl.multiple_of(b * chunk, chunk), chunk)
            for h in range(heads):
                value = mm(kh[h, keys, :], qh[h, rows, :], NT)
                if allowed is not None:
                    value = jnp.where(allowed, value, FILL)
                scores[h, b] = value
                tops[h] = jnp.maximum(tops[h], jnp.max(value.reshape(-1, 8, BQ), 0))

        over_keys(ends_ref, start, chunk, score)
        top = [jnp.max(tops[h], 0, keepdims=True) for h in range(heads)]

        def weigh(b, carry):
            for h in range(heads):
                part = slice(h * HD, (h + 1) * HD)
                weight = jnp.exp(scores[h, b] - top[h])
                sums[h] += fold_rows(weight)
                acc[part, :] += mm(vt[b, part, :], weight.astype(BF16))
            return carry

        low_first, _ = reach(ends_ref, start)
        _, high_last = reach(ends_ref, start + BQ - 1)
        lax.fori_loop(low_first // chunk, (high_last + chunk - 1) // chunk, weigh, 0)
        for h in range(heads):
            part = slice(h * HD, (h + 1) * HD)
            total = jnp.sum(sums[h], 0, keepdims=True)
            wide_ref[part, :] = acc[part, :] / total
            lse_ref[h : h + 1, :] = top[h] + jnp.log(total)
        lse_ref[heads:, :] = jnp.zeros((8 - heads, BQ), F32)
        ctx_ref[0] = wide_ref[...].T.astype(BF16)

    pairs = SEQLEN * SEQLEN
    return call(
        flow, body, (steps,), [full((2, chunk, width3))] * 2,
        [pl.BlockSpec((1, BQ, width), lambda i, *_: (i // per, i % per, 0)),
         pl.BlockSpec((width, BQ), lambda i, *_: (0, i)), pl.BlockSpec((8, BQ), lambda i, *_: (0, i))],
        [sds((count, chunk, width), BF16), sds((width, SEQLEN), F32), sds((8, SEQLEN), F32)],
        [
            pltpu.VMEM((heads, SEQLEN, HD), BF16),
            pltpu.VMEM((heads, SEQLEN, HD), BF16),
            pltpu.VMEM((count, width, chunk), BF16),
            pltpu.VMEM((width, BQ), F32),
            pltpu.VMEM((heads, 8, BQ), F32),
            pltpu.VMEM((heads, 8, BQ), F32),
            pltpu.VMEM((heads, count, chunk, BQ), F32),
        ],
        [*qkv], 16 * pairs * heads * HD, 6 * SEQLEN * width * 2, "attend_forward", (flow.scal, ends),
    )


def attend_backward(flow, ends, qkv, grads, wide, lse):
    _, chunk, width3 = qkv[0].shape
    count = SEQLEN // chunk
    width = width3 // 3
    heads = width // HD
    steps = SEQLEN // BQ
    per = chunk // BQ

    def body(
        scal_ref, ends_ref, near_ref, far_ref, grad_near, grad_far, wide_ref, lse_ref, out_ref, qh, kh, vh, gh, kt, qt, gt,
        gq, gk, gv,
    ):
        step = pl.program_id(0)

        @pl.when(step == 0)
        def _():
            blocks = chunks_of(scal_ref, near_ref, far_ref)
            grad_blocks = chunks_of(scal_ref, grad_near, grad_far)
            for (j, block), (_, grad_block) in zip(blocks, grad_blocks):
                rows = pl.ds(pl.multiple_of(j * chunk, chunk), chunk)
                for h in range(heads):
                    cols = slice(h * HD, (h + 1) * HD)
                    qh[h, rows, :] = block[:, cols] * BF16(HD**-0.5)
                    kh[h, rows, :] = block[:, width + h * HD : width + (h + 1) * HD]
                    vh[h, rows, :] = block[:, 2 * width + h * HD : 2 * width + (h + 1) * HD]
                    gh[h, rows, :] = grad_block[:, cols]
                kt[j] = block[:, width : 2 * width].T
                for s in range(per):
                    sub = slice(s * BQ, (s + 1) * BQ)
                    qt[j * per + s] = (block[sub, :width] * BF16(HD**-0.5)).T
                    gt[j * per + s] = grad_block[sub, :].T
            gk[...] = jnp.zeros(gk.shape, F32)
            gv[...] = jnp.zeros(gv.shape, F32)

        start = step * BQ
        rows = pl.ds(pl.multiple_of(start, BQ), BQ)
        gq[...] = jnp.zeros(gq.shape, F32)
        inner = []
        for h in range(heads):
            part = slice(h * HD, (h + 1) * HD)
            inner.append(jnp.sum(gt[step, part, :].astype(F32) * wide_ref[part, :], 0, keepdims=True))

        def block(b, allowed):
            keys = pl.ds(pl.multiple_of(b * chunk, chunk), chunk)
            for h in range(heads):
                part = slice(h * HD, (h + 1) * HD)
                score = mm(kh[h, keys, :], qh[h, rows, :], NT)
                grad_weight = mm(vh[h, keys, :], gh[h, rows, :], NT)
                if allowed is not None:
                    score = jnp.where(allowed, score, FILL)
                weight = jnp.exp(score - lse_ref[h : h + 1, :])
                grad_score = (weight * (grad_weight - inner[h])).astype(BF16)
                gv[b, part, :] += mm(gt[step, part, :], weight.astype(BF16), NT)
                gk[b, part, :] += mm(qt[step, part, :], grad_score, NT)
                gq[part, :] += mm(kt[b, part, :], grad_score)

        over_keys(ends_ref, start, chunk, block)
        out_ref[step // per, pl.ds(pl.multiple_of((step % per) * BQ, BQ), BQ), :width] = (
            (gq[...] * HD**-0.5).T.astype(BF16)
        )

        @pl.when(step == steps - 1)
        def _():
            for j in range(count):
                out_ref[j, :, width : 2 * width] = gk[j].T.astype(BF16)
                out_ref[j, :, 2 * width :] = gv[j].T.astype(BF16)

    pairs = SEQLEN * SEQLEN
    return call(
        flow, body, (steps,),
        [full((2, chunk, width3))] * 2 + [full((2, chunk, width))] * 2
        + [pl.BlockSpec((width, BQ), lambda i, *_: (0, i)), pl.BlockSpec((8, BQ), lambda i, *_: (0, i))],
        full((count, chunk, width3)), sds((count, chunk, width3), BF16),
        [pltpu.VMEM((heads, SEQLEN, HD), BF16)] * 4
        + [
            pltpu.VMEM((count, width, chunk), BF16),
            pltpu.VMEM((steps, width, BQ), BF16),
            pltpu.VMEM((steps, width, BQ), BF16),
            pltpu.VMEM((width, BQ), F32),
            pltpu.VMEM((count, width, chunk), F32),
            pltpu.VMEM((count, width, chunk), F32),
        ],
        [*qkv, *grads, wide, lse], 28 * pairs * heads * HD, 20 * SEQLEN * width, "attend_backward", (flow.scal, ends),
    )


def flip(values_in, axes, mask):
    return lax.ppermute(values_in, axes, [(a, a ^ mask) for a in range(lax.axis_size(axes))])


def turn(values_in):
    return lax.ppermute(values_in, ("c", "zh"), [(2 * a + b, 2 * b + a) for a in range(2) for b in range(2)])


def cross(values_in):
    return lax.ppermute(values_in, ("c", "zh"), [(2 * a + b, 2 * b + 1 - a) for a in range(2) for b in range(2)])


def uncross(values_in):
    return lax.ppermute(values_in, ("c", "zh"), [(2 * b + 1 - a, 2 * a + b) for a in range(2) for b in range(2)])


def from_members(values_in, axes):
    return [values_in] + [flip(values_in, axes, r) for r in range(1, lax.axis_size(axes))]


def to_members(parts, axes):
    return [parts[0]] + [flip(part, axes, r) for r, part in enumerate(parts) if r > 0]


def add(*parts):
    total = parts[0].astype(F32)
    for part in parts[1:]:
        total = total + part.astype(F32)
    return total


def is_small():
    return lax.axis_size("q") == 4


def order_by(values_in, axis, position, count):
    bit = 1
    while bit < count:
        shape = values_in.shape
        split = shape[:axis] + (count // (2 * bit), 2, bit) + shape[axis + 1 :]
        cut = values_in.reshape(split)
        values_in = jnp.where((position & bit) != 0, jnp.flip(cut, axis + 1), cut).reshape(shape)
        bit *= 2
    return values_in


def gather_group(values_in):
    across, sibling = flip(values_in, GROUP, 1), flip(values_in, GROUP, 2)
    return [values_in, across, sibling, flip(across, GROUP, 2)]


def sum_group(keep, send):
    got = flip(send, GROUP, 2)
    passed = add(keep[1], got[1]).astype(BF16)
    return [keep[0], got, flip(passed, GROUP, 1)], passed


EXTRA = 16


def heads_shard_of(qkv, out, bias):
    weights = jnp.concatenate([qkv.transpose(1, 0, 2).reshape(out.shape[0], -1), out], axis=1)
    below = jnp.pad(bias.reshape(1, -1), ((0, EXTRA - 1), (0, weights.shape[1] - bias.size)))
    return jnp.concatenate([weights, below])


def heads_bias(rows, heads):
    bias = rows.reshape(rows.shape[0], 2, heads, -1).transpose(1, 2, 0, 3).reshape(2, -1).astype(F32)
    return jnp.concatenate([bias[0], jnp.zeros_like(bias[0]), bias[1]])[None]


def heads_bias_near(members, size, heads, where, zh):
    rows = jnp.stack([member[:, ROWS, :size] for member in members])
    return heads_bias(order_by(order_by(rows, 0, where[0], 4), 1, zh, 2).reshape(8, size), heads)


def all_heads_weight(shard, size, heads, zh):
    pair = jnp.stack([turn(shard), cross(shard)])
    every = order_by(lax.all_gather(pair, "q"), 1, zh, 2)
    count = shard.shape[0] - EXTRA
    weights = every[:, :, :count].reshape(4, 2, ROWS, -1)
    return [weights[r] for r in range(4)], heads_bias(every[:, :, count, :size].reshape(-1, size), heads)


class HeadsGrad:
    def __init__(self, keep, send):
        self.keep, self.send = keep, send

    def along_x(self):
        self.got = flip(self.send, "q", 1)
        return self.got

    def along_y(self):
        self.here = add(self.keep[0], self.got[0])
        self.got = flip(add(self.keep[1], self.got[1]).astype(BF16), "q", 2)
        return self.got

    def halves(self, zh):
        if is_small():
            total = add(self.here, self.got).astype(BF16)
            return total[0], total[1]
        buckets = [self.keep[0], self.send[0], self.keep[1], self.send[1]]
        every = jnp.stack(buckets).reshape(lax.axis_size("q"), 2, -1, buckets[0].shape[-1])
        rows = order_by(lax.psum_scatter(every, "q", scatter_dimension=0, tiled=False), 0, zh, 2)
        return rows[0], rows[1]


SLOTS = (0, 2, 1, 3)


def units_weight(shard):
    if is_small():
        return lax.all_gather(shard, MODEL + ("q",)).reshape(-1, 4, ROWS, shard.shape[1]), None
    members = lax.axis_size(MODEL)
    every = lax.all_gather(shard, ALL, tiled=True).reshape(members, 4, 2, ROWS, shard.shape[1])
    return every[:, :, 0], every[:, :, 1]


class UnitsGrads:
    def __init__(self, flow, down, up, count):
        self.flow, self.down, self.up, self.count = flow, down, up, count

    def compute_theirs(self):
        self.theirs = unit_grads(self.flow, self.down, self.up, None, self.count, True)

    def send_theirs(self):
        self.got = flip(self.theirs, "c", 1) if is_small() else None

    def sibling(self):
        self.compute_theirs()
        self.send_theirs()

    def mine(self):
        self.made = unit_grads(self.flow, self.down, self.up, self.got, self.count, False)
        self.own, self.to_x, self.to_y, self.rest_x, self.rest_y = self.made

    def near(self):
        self.from_x, self.from_y = flip(self.to_x, "q", 1), flip(self.to_y, "q", 2)
        return [self.from_x, self.from_y]

    def far(self):
        half = self.count
        self.late_x = flip(add(self.rest_x, self.from_y[half:]).astype(BF16), "q", 1)
        self.late_y = flip(add(self.rest_y, self.from_x[half:]).astype(BF16), "q", 2)
        return [self.late_x, self.late_y]

    def near_z(self):
        half = self.count
        self.here = add(self.own[:half], self.from_x[:half], self.late_y)
        self.there = flip(add(self.own[half:], self.late_x, self.from_y[:half]).astype(BF16), "zl", 1)
        return [self.there]

    def far_z(self):
        half = self.count // 2
        self.stays = add(self.here[:half], self.there[:half])
        self.last = flip(add(self.here[half:], self.there[half:]).astype(BF16), "zh", 1)
        return [self.last]

    def total(self):
        if is_small():
            return self.stays + self.last.astype(F32)
        half = self.count
        mine = jnp.stack(
            [self.own, jnp.concatenate([self.to_x[:half], self.rest_x]), jnp.concatenate([self.rest_y, self.to_y[:half]]),
             jnp.concatenate([self.to_x[half:], self.to_y[half:]])]
        ).reshape(4, self.count, 2, ROWS, -1)
        theirs = self.theirs.reshape(4, 2, self.count, ROWS, -1).transpose(0, 2, 1, 3, 4)
        every = jnp.stack([mine, theirs], axis=1)
        every = every.transpose(2, 0, 1, 4, 3, 5)
        every = jnp.stack([every[slot] for slot in SLOTS]).reshape(-1, 2, mine.shape[-1])
        return lax.psum_scatter(every, ALL, scatter_dimension=0, tiled=True).astype(F32).transpose(1, 0, 2)


SMALL_AXES = ("q", MODEL, "c")
SMALL_STEPS = (("q", 1), ("q", 2), ("zl", 1), ("zh", 1), ("c", 1))


def small_step(values_in, step):
    axis, mask = SMALL_STEPS[step]
    return jnp.concatenate([values_in, flip(values_in, axis, mask)])


def order_small(every, where):
    every = every.reshape(2, 2, 2, 4, -1)
    every = every.reshape(2, 4, 4, -1)
    for axis, position in enumerate(where[::-1]):
        every = order_by(every, axis, position, every.shape[axis])
    return every.transpose(1, 2, 0, 3).reshape(16 // 4, 8, -1)


def scatter_small(values_in, where):
    if not is_small():
        return lax.psum_scatter(values_in.reshape(-1, values_in.shape[-1]), ALL, scatter_dimension=0, tiled=True)[0]
    every = values_in.reshape(4, 4, 2, -1).transpose(1, 0, 2, 3)
    for axis, position in enumerate(where):
        every = order_by(every, axis, position, every.shape[axis])
    every = every.transpose(2, 1, 0, 3).reshape(32, -1)
    for axis, mask in SMALL_STEPS[::-1]:
        half = every.shape[0] // 2
        every = every[:half] + flip(every[half:], axis, mask)
    return every[0]


def sum_all(value):
    if not is_small():
        return lax.psum(value, ALL)
    for axes in SMALL_AXES:
        parts = jnp.stack(from_members(value, axes))
        value = jnp.sum(order_by(parts, 0, lax.axis_index(axes), parts.shape[0]), 0)
    return value[0, 0]


def on_device(
    tokens, doc_lengths, qkv_weight, qv_bias, out_weight, up_weight, up_bias, down_weight, gains, shifts, cotangent
):
    layers = qkv_weight.shape[0]
    tz, dp = lax.axis_size(MODEL), lax.axis_size(("q", "c"))
    place, zh = lax.axis_index(GROUP), lax.axis_index("zh")
    where = (lax.axis_index("q"), lax.axis_index(MODEL), lax.axis_index("c"))
    if is_small():
        spots = [place, where[0], where[2], zh, where[1]]
    else:
        spots = [place] + [jnp.zeros((), jnp.int32)] * 4
    scal = jnp.stack([spot.astype(jnp.int32) for spot in spots])

    flow = Flow(scal)
    small_slice = is_small()
    qkv_cols, out_cols = 3 * out_weight.shape[2], out_weight.shape[2]
    in_cols, out_cols = slice(0, qkv_cols), slice(qkv_cols, qkv_cols + out_cols)
    hz, bias_size = qv_bias.shape[2], qv_bias.size // layers
    heads_shard = [heads_shard_of(qkv_weight[l], out_weight[l], qv_bias[l]) for l in range(layers)]
    pieces = [up_bias, gains, shifts]
    sizes = [piece.size // layers for piece in pieces]
    cuts = [0]
    for size in sizes:
        cuts.append(cuts[-1] + size)
    small = jnp.concatenate([piece.reshape(layers, -1) for piece in pieces], axis=1).reshape(1, -1)

    def spread_small(every):
        every = every.reshape(tz, dp, layers, -1).astype(F32)
        parts = [every[..., cuts[i] : cuts[i + 1]] for i in range(3)]
        biases = parts[0].reshape(tz, dp, layers, up_bias.shape[1], -1).transpose(2, 0, 3, 1, 4)
        gain = parts[1].reshape(tz, dp, layers, 2, -1).transpose(2, 3, 1, 0, 4).reshape(layers, 2, D)
        shift = parts[2].reshape(tz, dp, layers, 4, -1).transpose(2, 3, 1, 0, 4).reshape(layers, 4, D)
        table = jnp.concatenate([gain, shift], axis=1).reshape(layers * 6, D)
        head = jnp.concatenate([jnp.ones((1, D), F32), jnp.zeros((1, D), F32)])
        return biases.reshape(layers, tz, 1, -1), jnp.pad(jnp.concatenate([head, table]), ((0, TABLE - 2 - 6 * layers), (0, 0)))

    weights = [(units_weight(up_weight[l]), units_weight(down_weight[l])) for l in range(layers)]
    if small_slice:
        pair = jnp.stack([turn(heads_shard[0]), cross(heads_shard[0])])
        x_low = turn(tokens)
        ends = jnp.cumsum(turn(doc_lengths)[0], dtype=jnp.int32)
        members = from_members(pair, "q")
        small = small_step(small, 0)
        flow.wait(x_low, small)
        flow.hold(heads1=heads_shard[1], top=cotangent, low=x_low, small=small)
        gate(flow)
        x_low = flow.free("low")
        small = small_step(flow.free("small"), 1)
        weights_of = [(members, heads_bias_near(members, bias_size, hz, where, zh))]
    else:
        x_low = turn(tokens)
        ends = jnp.cumsum(turn(doc_lengths)[0], dtype=jnp.int32)
        weights_of = [all_heads_weight(shard, bias_size, hz, zh) for shard in heads_shard]
        top_grad = turn(cotangent)
        up_bias_full, table = spread_small(lax.all_gather(small, ALL))

    prev, prev_gain, prev_shift = x_low, ONE, ZERO
    kept = []
    for l in range(layers):
        first, last = small_slice and l == 0, small_slice and l == 1
        xs = gather_group(x_low)
        w_heads, bias = weights_of[l]
        w_up, w_down = weights[l]
        if first:
            flow.wait(small)
            flow.hold(small=small)
        qkv_near = project_in(flow, (xs[0], xs[2]), False, w_heads, in_cols, bias, "project_qkv")
        flow.wait(qkv_near)
        if first:
            small = small_step(flow.free("small"), 2)
            flow.wait(small)
            flow.hold(small=small)
        qkv_far = project_in(flow, (xs[1], xs[3]), True, w_heads, in_cols, bias, "project_qkv")
        qkv = (qkv_near, qkv_far)
        if first:
            small = small_step(flow.free("small"), 3)
        if last:
            top_grad = turn(flow.free("top"))
        if small_slice:
            flow.hold(up=w_up[0])
        ctx, wide, lse = attend_forward(flow, ends, qkv)
        if small_slice:
            mine = flow.free("up")
            w_up = mine, flip(mine, "c", 1)
        if first:
            flow.wait(small)
            flow.hold(small=small)
            shard = flow.free("heads1")
            pair = jnp.stack([turn(shard), cross(shard)])
        if last:
            flow.wait(top_grad)
        if small_slice:
            flow.hold(down=w_down[0])
        send = project_out(flow, ctx, (2, 3), w_heads, out_cols, True, "project_attn")
        flow.wait(send)
        if small_slice:
            mine = flow.free("down")
            w_down = mine, flip(mine, "c", 1)
        keep = project_out(flow, ctx, (0, 1), w_heads, out_cols, False, "project_attn")
        attn, _ = sum_group(keep, send)
        if first:
            up_bias_full, table = spread_small(order_small(small_step(flow.free("small"), 4), where))
            flow.wait(pair)
        used = (prev_gain, prev_shift, shift_row(l, 0), gain_row(l, 0), shift_row(l, 1))
        n1, hs, r1, act, slope = norm_up(flow, prev, attn, table, used, w_up, up_bias_full[l], tz)
        if first:
            members = from_members(pair, "q")
            weights_of.append((members, heads_bias_near(members, bias_size, hz, where, zh)))
        used = (gain_row(l, 0), shift_row(l, 1), shift_row(l, 2), gain_row(l, 1), shift_row(l, 3))
        n2, y_low, r2 = down_norm(flow, act, w_down, n1, table, used, tz)
        kept.append((xs, qkv, ctx, wide, lse, n1, hs, r1, act, slope, n2, r2, w_heads, w_up, w_down))
        x_low, prev, prev_gain, prev_shift = y_low, n2, gain_row(l, 1), shift_row(l, 3)
    layer_output = turn(x_low)

    g2, gf, sums2 = norm_back(flow, top_grad, kept[-1][10], kept[-1][11], table, gain_row(layers - 1, 1))
    small_grads = [None] * layers
    units_of, heads_of = [None] * layers, [None] * layers
    above = above_heads = None
    for l in reversed(range(layers)):
        top = l == layers - 1
        xs, qkv, ctx, wide, lse, n1, hs, r1, act, slope, n2, r2, w_heads, w_up, w_down = kept[l]
        beside = small_slice and not top
        gu, up_bias_sum = units_back(flow, gf, w_down, slope, tz)
        units = UnitsGrads(flow, (gf, act), (hs, gu), tz)
        if top:
            flow.wait(layer_output)
        else:
            if beside:
                flow.wait(*above.near())
                flow.hold(heads=above_heads.send)
            units.sibling()
            flow.wait(units.theirs)
            if beside:
                above_heads.send = flow.free("heads")
                above_heads.along_x()
                late = above.far()
        g1, ga, sums1 = up_back(flow, gu, w_up, g2, n1, r1, table, gain_row(l, 0), tz)
        gas = gather_group(ga)
        flow.wait(ga)
        if top:
            units.compute_theirs()
        else:
            units.mine()
            flow.wait(*units.made)
            if beside:
                flow.wait(*late, above_heads.got)
        gc_near = project_in(flow, (gas[0], gas[2]), False, w_heads, out_cols, None, "project_gc")
        flow.wait(gc_near)
        if top:
            flow.hold(theirs=units.theirs)
        gc_far = project_in(flow, (gas[1], gas[3]), True, w_heads, out_cols, None, "project_gc")
        if top:
            units.theirs = flow.free("theirs")
            units.send_theirs()
        gqkv = attend_backward(flow, ends, qkv, (gc_near, gc_far), wide, lse)
        if beside:
            flow.wait(*units.near(), *above.near_z(), above_heads.along_y())
        send = project_out(flow, gqkv, (2, 3), w_heads, in_cols, True, "project_gx")
        flow.wait(send)
        keep = project_out(flow, gqkv, (0, 1), w_heads, in_cols, False, "project_gx")
        back, passed = sum_group(keep, send)
        flow.wait(passed)
        if top:
            units.mine()
            flow.wait(*units.made)
        elif small_slice:
            flow.hold(there=above.there)
        *buckets, qkv_sums = heads_grad(flow, xs, gqkv, gas, ctx)
        heads = HeadsGrad(*buckets)
        units_of[l], heads_of[l] = units, heads
        qv_sums = qkv_sums.reshape(3, hz, dp, -1)
        qv_sums = jnp.stack([qv_sums[0], qv_sums[2]]).transpose(2, 0, 1, 3).reshape(1, dp, -1)
        mine = (jnp.arange(tz) == place).astype(F32).reshape(tz, 1, 1)
        small_grads[l] = jnp.concatenate(
            [
                mine * qv_sums,
                up_bias_sum.reshape(tz, up_bias.shape[1], dp, -1).transpose(0, 2, 1, 3).reshape(tz, dp, -1),
                jnp.stack([sums1[0], sums2[0]]).reshape(2, dp, tz, -1).transpose(2, 1, 0, 3).reshape(tz, dp, -1),
                jnp.stack([sums1[2], sums1[1], sums2[2], sums2[1]])
                .reshape(4, dp, tz, -1).transpose(2, 1, 0, 3).reshape(tz, dp, -1),
            ],
            axis=-1,
        )
        if l > 0:
            above, above_heads = units, heads
            flow.wait(heads.send)
            g2, gf, sums2 = sum_norm_back(flow, g1, back, kept[l - 1][10], kept[l - 1][11], table, gain_row(l - 1, 1))
    small_sums = jnp.stack(small_grads, axis=2).reshape(tz, dp, -1)
    if small_slice:
        units.far()
        above.there = flow.free("there")
        above.far_z()
        flow.hold(late_x=units.late_x, late_y=units.late_y, heads=heads.send)
        gate(flow)
        units.late_x, units.late_y, heads.send = flow.free("late_x"), flow.free("late_y"), flow.free("heads")
        heads.along_x()
        units.near_z()
        flow.wait(back[2])
        flow.hold(small=small_sums, there=units.there, got=heads.got)
        gate(flow)
        small_sums, units.there, heads.got = flow.free("small"), flow.free("there"), flow.free("got")
        heads.along_y()
        units.far_z()
    input_grad = turn(add(g1, back[0], back[1][0], back[2]).astype(BF16))
    halves = [member.halves(zh) for member in heads_of]
    d_heads = add(turn(jnp.stack([half[0] for half in halves])), uncross(jnp.stack([half[1] for half in halves])))
    qkv_grad = d_heads[:, :, : in_cols.stop].reshape(layers, d_heads.shape[1], 3, -1).transpose(0, 2, 1, 3)
    out_grad = d_heads[:, :, in_cols.stop :]
    totals = [member.total() for member in units_of]
    down_grad, up_grad = (jnp.stack([total[i] for total in totals]) for i in range(2))

    small_out = scatter_small(small_sums, where).reshape(layers, -1)
    rest = small_out[:, bias_size:]
    qv_bias_grad = small_out[:, :bias_size].reshape(qv_bias.shape)
    up_bias_grad = rest[:, cuts[0] : cuts[1]].reshape(up_bias.shape)
    gains_grad = rest[:, cuts[1] : cuts[2]].reshape(gains.shape)
    shifts_grad = rest[:, cuts[2] : cuts[3]].reshape(shifts.shape)
    all_grads = (qkv_grad, qv_bias_grad, out_grad, up_grad, up_bias_grad, down_grad, gains_grad, shifts_grad)
    local_squares = sum(jnp.sum(member * member) for member in all_grads)
    entry_count = LAYERS * (4 * D * D + 2 * D * FF + FF + 8 * D)
    if small_slice:
        flow.wait(input_grad)
        flow.hold(squares=jnp.broadcast_to(local_squares, (8, 128)))
        gate(flow)
        local_squares = flow.free("squares")
    grad_rms = jnp.sqrt(sum_all(local_squares) / entry_count)
    return (
        layer_output, input_grad, qkv_grad, qv_bias_grad, out_grad, up_grad, up_bias_grad, down_grad, gains_grad,
        shifts_grad, grad_rms,
    )


def solution(mesh):
    dp, tensor = mesh.shape["dp"], mesh.shape["tensor"]
    fine = Mesh(mesh.devices.reshape(dp // 2, 2, 2, tensor // 2), ("q", "c", "zh", "zl"))
    data, model = ("q", "c"), ("zh", "zl")
    both = data + model
    weight3, weight4 = P(None, data, model), P(None, None, data, model)
    in_specs = (
        P(both, None), P(data, None), weight4, P(None, None, model, data), weight3, weight3, P(None, model, data),
        weight3, P(None, None, both), P(None, None, both), P(both, None),
    )
    out_specs = (
        P(both, None), P(both, None), weight4, P(None, None, model, data), weight3, weight3, P(None, model, data),
        weight3, P(None, None, both), P(None, None, both), P(),
    )
    return jax.shard_map(on_device, mesh=fine, in_specs=in_specs, out_specs=out_specs, check_vma=False)
```

time: 1250 us -> 1080 us (0.86)
  waiting for transfers between devices: 457 us -> 344 us
  starting transfers between devices: 169 us -> 91.3 us
  local copies, waits for them, and re-layouts: 92.2 us -> 51.4 us
  Pallas kernels: 464 us -> 501 us
  other arithmetic: 44.8 us -> 61.1 us
  between operations: 9.73 us -> 22.8 us
    ppermute x104 -> x65, waiting for transfers between devices: 363 us -> 236 us  [flip(): lax.ppermute(values_in, axes, [(a, a ^ mask) for a in range(lax.axis_size...]
    ppermute x104 -> x65, starting transfers between devices: 127 us -> 53.2 us  [flip(): lax.ppermute(values_in, axes, [(a, a ^ mask) for a in range(lax.axis_size...]
    pallas_call x32 -> x40, Pallas kernels: 464 us -> 501 us  [call(): pl.pallas_call(wrapped, grid_spec=pltpu.PrefetchScalarGridSpec(num_scalar...]
    all_gather x0 -> x4, waiting for transfers between devices: none -> 35 us  [units_weight(): lax.all_gather(shard, MODEL + ('q',)).reshape(-1, 4, ROWS, shard.shape[1])]
    ppermute x9 -> x8, waiting for transfers between devices: 93.5 us -> 71.9 us  [turn(): lax.ppermute(values_in, ('c', 'zh'), [(2 * a + b, 2 * b + a) for a in ran...]
    convert_element_type x9 -> x18, other arithmetic: 15 us -> 31.5 us  [the longest x4 9.63 us: sum_group(): passed = add(keep[1], got[1]).astype(BF16)]
    unnamed x209 -> x163, local copies, waits for them, and re-layouts: 28 us -> 23.7 us
    ppermute x9 -> x8, starting transfers between devices: 39.7 us -> 36.6 us  [turn(): lax.ppermute(values_in, ('c', 'zh'), [(2 * a + b, 2 * b + a) for a in ran...]
  transfers between devices with their start and end apart: 117 -> 80, of which waited for: 46 -> 36; matrix products, arithmetic and copies ran while one was open for 9% -> 9% of each run, Pallas kernels for 28% -> 42%
where the time goes in v4:
time: 1080 us; the launch traced here: 1070 us
  Pallas kernels  501 us (46%)
  waiting for transfers between devices  344 us (32%)
  starting transfers between devices  91.3 us (8%)
  other arithmetic  61.1 us (6%)
  local copies, waits for them, and re-layouts  51.4 us (5%)
  between operations  22.8 us (2%)
    pallas_call x40, Pallas kernels, call(): pl.pallas_call(wrapped, grid_spec=pltpu.PrefetchScalarGridSpec(num_scalar...  501 us
    ppermute x65, waiting for transfers between devices, flip(): lax.ppermute(values_in, axes, [(a, a ^ mask) for a in range(lax.axis_size...  236 us
    ppermute x8, waiting for transfers between devices, turn(): lax.ppermute(values_in, ('c', 'zh'), [(2 * a + b, 2 * b + a) for a in ran...  71.9 us
    ppermute x65, starting transfers between devices, flip(): lax.ppermute(values_in, axes, [(a, a ^ mask) for a in range(lax.axis_size...  53.2 us
    ppermute x8, starting transfers between devices, turn(): lax.ppermute(values_in, ('c', 'zh'), [(2 * a + b, 2 * b + a) for a in ran...  36.6 us
    all_gather x4, waiting for transfers between devices, units_weight(): lax.all_gather(shard, MODEL + ('q',)).reshape(-1, 4, ROWS, shard.shape[1])  35 us
    unnamed x163, local copies, waits for them, and re-layouts  23.7 us
  transfers between devices with their start and end apart: 80, of which 36 were waited for; matrix products, arithmetic and copies ran while one was open for 9% of the time, Pallas kernels for 42%

profile of v4, /device:TPU:1, one launch (start us, length us, event | category | flops | bytes accessed | tf_op | source)
XLA Modules:
  0.0 1071.9 jit_solution(7346805520212663909)
XLA Ops:
  24.5 38.8 %collective-permute-done.1.refs_1_ = bf16[512,1024]{1,0:T(8,128)(2,1)S(1)} collective-permute-done((bf16[512,1024]{1,0:T(8,128)(2,1)S(1)}, bf16[512,1024]{1,0:T(8,128)(2,1)S(1)}, u32[]{:S(2)}, u32[]{:S(2)}) %collective-permute-start.1) | collective-permute-done | bytes 1048608 | tf_op jit(solution)/shard_map/ppermute | solution.py:841
  80.1 12.9 %collective-permute-done.8.refs_10_.refs_11_.refs_8_.refs_7_.refs_13_.refs_6_.refs_5_ = bf16[2,144,1024]{2,1,0:T(8,128)(2,1)S(1)} collective-permute-done((bf16[2,144,1024]{2,1,0:T(8,128)(2,1)S(1)}, bf16[2,144,1024]{2,1,0:T(8,128)(2,1)S(1)}, u32[]{:S(2)}, u32[]{:S(2)}) %collective-permute-start.8) | collective-permute-done | bytes 589856 | tf_op jit(solution)/shard_map/ppermute | solution.py:837
  125.8 33.7 %attend_forward.2 = (bf16[4,512,256]{2,1,0:T(8,128)(2,1)}, f32[256,2048]{1,0:T(8,128)}, f32[8,2048]{1,0:T(8,128)}, bf16[144,1024]{1,0:T(8,128)(2,1)}, bf16[512,1...) custom-call(s32[5]{0:T(128)} %stack.125.refs_0_, ...), custom_call_target="tpu_custom_call", output_to_operand_aliasing={{3}: (2, {}), {4}: (3, {}), {5}: (4, {})} | custom-call | flops 14000000000 | bytes 1024 | tf_op jit(solution)/shard_map/attend_forward/pallas_call | solution.py:79
  163.9 27.3 %all-gather.7.cloned.1.call-done = bf16[16,128,1024]{2,1,0:T(8,128)(2,1)} async-done(((bf16[1,128,1024]{2,1,0:T(8,128)(2,1)}), bf16[16,128,1024]{2,1,0:T(8,128)(2,1)}) %all-gather.7.cloned.1.call-update) | async-done | bytes 4194320 | tf_op jit(solution)/shard_map/all_gather | solution.py:948
  227.1 27.0 %collective-permute-done.17.refs_6_ = bf16[512,1024]{1,0:T(8,128)(2,1)} collective-permute-done((bf16[512,1024]{1,0:T(8,128)(2,1)S(1)}, bf16[512,1024]{1,0:T(8,128)(2,1)}, u32[]{:S(2)}, u32[]{:S(2)}) %collective-permute-start.17) | collective-permute-done | bytes 1048608 | tf_op jit(solution)/shard_map/ppermute | solution.py:837
  254.1 18.7 %norm_up.2 = (f32[512,1024]{1,0:T(8,128)}, bf16[512,1024]{1,0:T(8,128)(2,1)}, f32[512,128]{1,0:T(8,128)}, bf16[512,4096]{1,0:T(8,128)(2,1)}, bf16[512,4096]{1,0:T(8,128)(2,1)}, /*index=5*/bf16[512,1024]{1,0:T(8,128)(2,1)}) custom-call(s32[5]{0:T(128)} %stack.125.refs_0_, ...), custom_call_target="tpu_custom_call", output_to_operand_aliasing={{5}: (2, {})} | custom-call | flops 7000000000 | bytes 1024 | tf_op jit(solution)/shard_map/norm_up/pallas_call | solution.py:79
  272.7 14.4 %down_norm.2 = (f32[512,1024]{1,0:T(8,128)}, bf16[512,1024]{1,0:T(8,128)(2,1)}, f32[512,128]{1,0:T(8,128)}, bf16[512,1024]{1,0:T(8,128)(2,1)}) custom-call(s32[5]{0:T(128)} %stack.125.refs_0_, bf16[512,1024]{1,0:T(8,128)(2,1)} %get-tuple-element.137.refs_1_, ...), custom_call_target="tpu_custom_call", output_to_operand_aliasing={{3}: (1, {})} | custom-call | flops 7000000000 | bytes 1024 | tf_op jit(solution)/shard_map/down_norm/pallas_call | solution.py:79
  290.0 11.2 %collective-permute-done.24.refs_8_.refs_9_.refs_7_.refs_6_.refs_5_ = bf16[2,144,1024]{2,1,0:T(8,128)(2,1)S(1)} collective-permute-done((bf16[2,144,1024]{2,1,0:T(8,128)(2,1)S(1)}, bf16[2,144,1024]{2,1,0:T(8,128)(2,1)S(1)}, u32[]{:S(2)}, u32[]{:S(2)}) %collective-permute-start.24) | collective-permute-done | bytes 589856 | tf_op jit(solution)/shard_map/ppermute | solution.py:837
  301.2 16.8 %collective-permute-done.23.refs_7_.refs_8_.refs_6_.refs_5_.refs_4_ = bf16[2,144,1024]{2,1,0:T(8,128)(2,1)S(1)} collective-permute-done((bf16[2,144,1024]{2,1,0:T(8,128)(2,1)S(1)}, bf16[2,144,1024]{2,1,0:T(8,128)(2,1)S(1)}, u32[]{:S(2)}, u32[]{:S(2)}) %collective-permute-start.23) | collective-permute-done | bytes 589856 | tf_op jit(solution)/shard_map/ppermute | solution.py:837
  341.7 33.9 %attend_forward.3 = (bf16[4,512,256]{2,1,0:T(8,128)(2,1)}, f32[256,2048]{1,0:T(8,128)}, f32[8,2048]{1,0:T(8,128)}, bf16[4,4,128,1024]{3,2,1,0:T(8,128)(2,1)}) custom-call(s32[5]{0:T(128)} %stack.125.refs_0_, s32[4]{0:T(128)} %bitcast.257, bf16[4,4,128,1024]{3,2,1,0:T(8,128)(2,1)} %bitcast.253, ...), custom_call_target="tpu_custom_call", output_to_operand_aliasing={{3}: (2, {})} | custom-call | flops 14000000000 | bytes 1024 | tf_op jit(solution)/shard_map/attend_forward/pallas_call | solution.py:79
  407.0 23.6 %collective-permute-done.29.refs_4_ = bf16[512,1024]{1,0:T(8,128)(2,1)} collective-permute-done((bf16[512,1024]{1,0:T(8,128)(2,1)S(1)}, bf16[512,1024]{1,0:T(8,128)(2,1)}, u32[]{:S(2)}, u32[]{:S(2)}) %collective-permute-start.29) | collective-permute-done | bytes 1048608 | tf_op jit(solution)/shard_map/ppermute | solution.py:837
  430.6 18.9 %norm_up.3 = (f32[512,1024]{1,0:T(8,128)}, bf16[512,1024]{1,0:T(8,128)(2,1)}, f32[512,128]{1,0:T(8,128)}, bf16[512,4096]{1,0:T(8,128)(2,1)}, bf16[512,4096]{1,0:T(8,128)(2,1)}) custom-call(s32[5]{0:T(128)} %stack.125.refs_0_, f32[512,1024]{1,0:T(8,128)} %get-tuple-element.141.refs_1_.refs_6_, bf16[512,1024]{1,0:T(8,128)(2,1)} %get-tuple-element.150.refs_2_, ...), custom_call_target="tpu_custom_call" | custom-call | flops 7000000000 | bytes 1024 | tf_op jit(solution)/shard_map/norm_up/pallas_call | solution.py:79
  449.5 14.3 %down_norm.3 = (f32[512,1024]{1,0:T(8,128)}, bf16[512,1024]{1,0:T(8,128)(2,1)}, f32[512,128]{1,0:T(8,128)}) custom-call(s32[5]{0:T(128)} %stack.125.refs_0_, bf16[512,4096]{1,0:T(8,128)(2,1)} %get-tuple-element.153.refs_1_.refs_3_, f32[512,1024]{1,0:T(8,128)} %get-tuple-element.154.refs_2_.refs_4_, ...), custom_call_target="tpu_custom_call" | custom-call | flops 7000000000 | bytes 1024 | tf_op jit(solution)/shard_map/down_norm/pallas_call | solution.py:79
  474.3 11.4 %units_back.2 = (bf16[512,4096]{1,0:T(8,128)(2,1)}, f32[4,1,1024]{2,1,0:T(1,128)}) custom-call(s32[5]{0:T(128)} %stack.125.refs_0_, bf16[512,1024]{1,0:T(8,128)(2,1)} %get-tuple-element.159.refs_1_.refs_2_, bf16[512,4096]{1,0:T(8,128)(2,1)} %get-tuple-element.160.refs_2_, bf16[4,4,128,1024]{3,2,1,0:T(8,128)(2,1)} %get-tuple-element.155.refs_4_.refs_3_, ...), custom_call_target="tpu_custom_call" | custom-call | flops 7000000000 | bytes 1024 | tf_op jit(solution)/shard_map/units_back/pallas_call | solution.py:79
  493.3 15.0 %up_back.2 = (f32[512,1024]{1,0:T(8,128)}, bf16[512,1024]{1,0:T(8,128)(2,1)}, f32[8,1024]{1,0:T(8,128)}) custom-call(s32[5]{0:T(128)} %stack.125.refs_0_, bf16[512,1024]{1,0:T(8,128)(2,1)} %copy-done.45, bf16[512,4096]{1,0:T(8,128)(2,1)} %get-tuple-element.161.refs_2_.refs_5_, f32[512,1024]{1,0:T(8,128)} %get-tuple-element.162.refs_3_, ...), custom_call_target="tpu_custom_call" | custom-call | flops 7000000000 | bytes 1024 | tf_op jit(solution)/shard_map/up_back/pallas_call | solution.py:79
  508.8 17.3 %collective-permute-done.34.refs_3_.refs_11_ = bf16[512,1024]{1,0:T(8,128)(2,1)S(1)} collective-permute-done((bf16[512,1024]{1,0:T(8,128)(2,1)}, bf16[512,1024]{1,0:T(8,128)(2,1)S(1)}, u32[]{:S(2)}, u32[]{:S(2)}) %collective-permute-start.34) | collective-permute-done | bytes 1048608 | tf_op jit(solution)/shard_map/ppermute | solution.py:837
  526.1 12.8 %grads_theirs.2.refs_2_ = bf16[4,8,128,1024]{3,2,1,0:T(8,128)(2,1)} custom-call(s32[5]{0:T(128)} %stack.125.refs_0_, bf16[512,1024]{1,0:T(8,128)(2,1)} %get-tuple-element.164.refs_1_.refs_10_, bf16[512,1024]{1,0:T(8,128)(2,1)} %get-tuple-element.159.refs_1_.refs_2_, bf16[512,4096]{1,0:T(8,128)(2,1)} %get-tuple-element.153.refs_1_.refs_3_, ...), custom_call_target="tpu_custom_call" | custom-call | flops 70000000 | bytes 1024 | tf_op jit(solution)/shard_map/grads_theirs/pallas_call | solution.py:79
  551.4 61.4 %attend_backward.2.refs_1_.refs_2_.refs_14_ = bf16[4,512,768]{2,1,0:T(8,128)(2,1)} custom-call(s32[5]{0:T(128)} %stack.125.refs_0_, s32[4]{0:T(128)} %bitcast.258, bf16[2,512,768]{2,1,0:T(8,128)(2,1)} %get-tuple-element.144.refs_1_.refs_3_.refs_2_, bf16[2,512,768]{2,1,0:T(8,128)(2,1)} %get-tuple-element.147.refs_4_.refs_3_, ...), custom_call_target="tpu_custom_call" | custom-call | flops 20999999488 | bytes 1024 | tf_op jit(solution)/shard_map/attend_backward/pallas_call | solution.py:79
  629.5 16.0 %grads_mine.2 = (bf16[8,128,1024]{2,1,0:T(8,128)(2,1)}, bf16[8,128,1024]{2,1,0:T(8,128)(2,1)}, bf16[8,128,1024]{2,1,0:T(8,128)(2,1)}, bf16[4,128,1024]{2,1,0:T(8,128)(2,1)}, bf16[4,128,1024]{2,1,0:T(8,128)(2,1)}) custom-call(s32[5]{0:T(128)} %stack.125.refs_0_, bf16[512,1024]{1,0:T(8,128)(2,1)} %copy-done.27, ...), custom_call_target="tpu_custom_call" | custom-call | flops 70000000 | bytes 1024 | tf_op jit(solution)/shard_map/grads_mine/pallas_call | solution.py:79
  646.6 11.5 %heads_grad.2 = (bf16[2,2,128,1024]{3,2,1,0:T(8,128)(2,1)}, bf16[2,2,128,1024]{3,2,1,0:T(8,128)(2,1)}, f32[1,768]{1,0:T(1,128)}) custom-call(s32[5]{0:T(128)} %stack.125.refs_0_, bf16[8,128,1024]{2,1,0:T(8,128)(2,1)} %get-tuple-element.173.refs_1_, bf16[8,128,1024]{2,1,0:T(8,128)(2,1)} %get-tuple-element.171.refs_2_, ...), custom_call_target="tpu_custom_call" | custom-call | flops 70000000 | bytes 1024 | tf_op jit(solution)/shard_map/heads_grad/pallas_call | solution.py:79
  665.8 11.4 %units_back.3 = (bf16[512,4096]{1,0:T(8,128)(2,1)}, f32[4,1,1024]{2,1,0:T(1,128)}) custom-call(s32[5]{0:T(128)} %stack.125.refs_0_, bf16[512,1024]{1,0:T(8,128)(2,1)} %get-tuple-element.180.refs_1_.refs_4_.refs_2_, bf16[512,4096]{1,0:T(8,128)(2,1)} %get-tuple-element.182.refs_2_, bf16[4,4,128,1024]{3,2,1,0:T(8,128)(2,1)} %get-tuple-element.140.refs_5_.refs_3_, ...), custom_call_target="tpu_custom_call" | custom-call | flops 7000000000 | bytes 1024 | tf_op jit(solution)/shard_map/units_back/pallas_call | solution.py:79
  677.3 15.2 %collective-permute-done.38.refs_1_ = bf16[8,128,1024]{2,1,0:T(8,128)(2,1)S(1)} collective-permute-done((bf16[8,128,1024]{2,1,0:T(8,128)(2,1)}, bf16[8,128,1024]{2,1,0:T(8,128)(2,1)S(1)}, u32[]{:S(2)}, u32[]{:S(2)}) %collective-permute-start.38) | collective-permute-done | bytes 2097184 | tf_op jit(solution)/shard_map/ppermute | solution.py:837
  694.5 12.8 %grads_theirs.3 = (bf16[4,8,128,1024]{3,2,1,0:T(8,128)(2,1)}, bf16[2,2,128,1024]{3,2,1,0:T(8,128)(2,1)}) custom-call(s32[5]{0:T(128)} %stack.125.refs_0_, bf16[8,128,1024]{2,1,0:T(8,128)(2,1)} %copy-done.11, bf16[8,128,1024]{2,1,0:T(8,128)(2,1)} %copy-done.13, ...), custom_call_target="tpu_custom_call", output_to_operand_aliasing={{1}: (3, {})} | custom-call | flops 70000000 | bytes 1024 | tf_op jit(solution)/shard_map/grads_theirs/pallas_call | solution.py:79
  709.6 15.2 %up_back.3 = (f32[512,1024]{1,0:T(8,128)}, bf16[512,1024]{1,0:T(8,128)(2,1)}, f32[8,1024]{1,0:T(8,128)}) custom-call(s32[5]{0:T(128)} %stack.125.refs_0_, bf16[4,8,128,1024]{3,2,1,0:T(8,128)(2,1)} %get-tuple-element.184.refs_1_, bf16[512,4096]{1,0:T(8,128)(2,1)} %get-tuple-element.183.refs_7_.refs_2_.refs_5_, f32[512,1024]{1,0:T(8,128)} %get-tuple-element.185.refs_3_, ...), custom_call_target="tpu_custom_call" | custom-call | flops 7000000000 | bytes 1024 | tf_op jit(solution)/shard_map/up_back/pallas_call | solution.py:79
  735.3 14.4 %collective-permute-done.50.refs_2_.refs_8_ = bf16[512,1024]{1,0:T(8,128)(2,1)} collective-permute-done((bf16[512,1024]{1,0:T(8,128)(2,1)}, bf16[512,1024]{1,0:T(8,128)(2,1)}, u32[]{:S(2)}, u32[]{:S(2)}) %collective-permute-start.50) | collective-permute-done | bytes 1048608 | tf_op jit(solution)/shard_map/ppermute | solution.py:837
  756.5 16.1 %grads_mine.3 = (bf16[8,128,1024]{2,1,0:T(8,128)(2,1)}, bf16[8,128,1024]{2,1,0:T(8,128)(2,1)}, bf16[8,128,1024]{2,1,0:T(8,128)(2,1)}, bf16[4,128,1024]{2,1,0:T(8,128)(2,1)}, bf16[4,128,1024]{2,1,0:T(8,128)(2,1)}) custom-call(s32[5]{0:T(128)} %stack.125.refs_0_, bf16[512,1024]{1,0:T(8,128)(2,1)} %get-tuple-element.188.refs_1_.refs_9_.refs_7_, ...), custom_call_target="tpu_custom_call" | custom-call | flops 70000000 | bytes 1024 | tf_op jit(solution)/shard_map/grads_mine/pallas_call | solution.py:79
  790.6 61.4 %attend_backward.3.refs_5_.refs_2_.refs_11_ = bf16[4,512,768]{2,1,0:T(8,128)(2,1)} custom-call(s32[5]{0:T(128)} %stack.125.refs_0_, s32[4]{0:T(128)} %bitcast.259, bf16[2,512,768]{2,1,0:T(8,128)(2,1)} %get-tuple-element.118.refs_1_.refs_5_.refs_2_, bf16[2,512,768]{2,1,0:T(8,128)(2,1)} %get-tuple-element.124.refs_6_.refs_3_, ...), custom_call_target="tpu_custom_call" | custom-call | flops 20999999488 | bytes 1024 | tf_op jit(solution)/shard_map/attend_backward/pallas_call | solution.py:79
  884.8 11.5 %heads_grad.3 = (bf16[2,2,128,1024]{3,2,1,0:T(8,128)(2,1)}, bf16[2,2,128,1024]{3,2,1,0:T(8,128)(2,1)}, f32[1,768]{1,0:T(1,128)}, bf16[4,128,1024]{2,1,0:T(8,128)(2,1)}) custom-call(s32[5]{0:T(128)} %stack.125.refs_0_, bf16[512,1024]{1,0:T(8,128)(2,1)} %fusion.refs_1_, bf16[4,128,1024]{2,1,0:T(8,128)(2,1)} %copy-done.9, ...), custom_call_target="tpu_custom_call", output_to_operand_aliasing={{3}: (2, {})} | custom-call | flops 70000000 | bytes 1024 | tf_op jit(solution)/shard_map/heads_grad/pallas_call | solution.py:79
  910.2 32.2 %collective-permute-done.57.refs_3_ = bf16[4,128,1024]{2,1,0:T(8,128)(2,1)} collective-permute-done((bf16[4,128,1024]{2,1,0:T(8,128)(2,1)}, bf16[4,128,1024]{2,1,0:T(8,128)(2,1)}, u32[]{:S(2)}, u32[]{:S(2)}) %collective-permute-start.57) | collective-permute-done | bytes 1048608 | tf_op jit(solution)/shard_map/ppermute | solution.py:837
  959.3 8.5 collective-permute-done.65
  982.2 24.0 %collective-permute-done.67 = bf16[2,128,1024]{2,1,0:T(8,128)(2,1)} collective-permute-done((bf16[2,128,1024]{2,1,0:T(8,128)(2,1)}, bf16[2,128,1024]{2,1,0:T(8,128)(2,1)}, u32[]{:S(2)}, u32[]{:S(2)}) %collective-permute-start.67) | collective-permute-done | bytes 524320 | tf_op jit(solution)/shard_map/ppermute | solution.py:837
  1011.3 12.1 %collective-permute-done.60 = bf16[2,128,1024]{2,1,0:T(8,128)(2,1)S(1)} collective-permute-done((bf16[2,128,1024]{2,1,0:T(8,128)(2,1)S(1)}, bf16[2,128,1024]{2,1,0:T(8,128)(2,1)S(1)}, u32[]{:S(2)}, u32[]{:S(2)}) %collective-permute-start.60) | collective-permute-done | bytes 524320 | tf_op jit(solution)/shard_map/ppermute | solution.py:841
  (541 shorter events, 377.5 us)
Async XLA Ops:
  7.2 118.5 %all-gather.5.cloned.1.call-start = ((), (), s32[]{:S(2)}) async-start(), calls=%async_computation | async-start | bytes 4456448 | tf_op jit(solution)/shard_map/all_gather | solution.py:948
  10.6 180.5 %all-gather.7.cloned.1.call-start = ((), (), s32[]{:S(2)}) async-start(), calls=%async_computation.1 | async-start | bytes 4456448 | tf_op jit(solution)/shard_map/all_gather | solution.py:948
  11.5 330.2 %all-gather.11.cloned.1.call-start = ((), (), s32[]{:S(2)}) async-start(), calls=%async_computation.3 | async-start | bytes 4456448 | tf_op jit(solution)/shard_map/all_gather | solution.py:948
  12.2 371.1 %all-gather.9.cloned.1.call-start = ((), (), s32[]{:S(2)}) async-start(), calls=%async_computation.2 | async-start | bytes 4456448 | tf_op jit(solution)/shard_map/all_gather | solution.py:948
  12.3 51.1 %collective-permute-start.1 = (bf16[512,1024]{1,0:T(8,128)(2,1)S(1)}, bf16[512,1024]{1,0:T(8,128)(2,1)S(1)}, u32[]{:S(2)}, u32[]{:S(2)}) collective-permute-start(bf16[512,1024]{1,0:T(8,128)(2,1)S(1)} %copy-done.68), channel_id=1, source_target_pairs={{0,0},{2,4},{4,2},{6,6},{1,1},{3,5},{5,3},{7,7},{8,8},{10,12},{12,... | collective-permute-start | bytes 3145736 | tf_op jit(solution)/shard_map/ppermute | solution.py:841
  18.4 50.6 %collective-permute-start.5 = (bf16[144,1024]{1,0:T(8,128)(2,1)S(1)}, bf16[144,1024]{1,0:T(8,128)(2,1)S(1)}, u32[]{:S(2)}, u32[]{:S(2)}) collective-permute-start(bf16[144,1024]{1,0:T(8,128)(2,1)S(1)} %fusion.17), channel_id=1, source_target_pairs={{0,0},{2,4},{4,2},{6,6},{1,1},{3,5},{5,3},{7,7},{8,8},{10,12},{12,... | collective-permute-start | bytes 884744 | tf_op jit(solution)/shard_map/ppermute | solution.py:841
  20.3 48.7 %collective-permute-start.6 = (bf16[144,1024]{1,0:T(8,128)(2,1)S(1)}, bf16[144,1024]{1,0:T(8,128)(2,1)S(1)}, u32[]{:S(2)}, u32[]{:S(2)}) collective-permute-start(bf16[144,1024]{1,0:T(8,128)(2,1)S(1)} %fusion.17), channel_id=1, source_target_pairs={{0,2},{2,6},{4,0},{6,4},{1,3},{3,7},{5,1},{7,5},{8,10},{10,14},{12... | collective-permute-start | bytes 884744 | tf_op jit(solution)/shard_map/ppermute | solution.py:845
  159.4 94.6 %collective-permute-start.19 = (bf16[4,4,128,1024]{3,2,1,0:T(8,128)(2,1)}, bf16[4,4,128,1024]{3,2,1,0:T(8,128)(2,1)}, u32[]{:S(2)}, u32[]{:S(2)}) collective-permute-start(bf16[4,4,128,1024]{3,2,1,0:T(8,128)(2,1)} %get-tuple-element.136.refs_9_.refs_7_), channel_id=1, source_target_pairs={{0,4},{4,0},{1,5},{5,1},{2,6},{6,2},{3,7},{7,3},{8,12},{12,8},{9,1... | collective-permute-start | bytes 12582920 | tf_op jit(solution)/shard_map/ppermute | solution.py:837
  197.9 74.8 %collective-permute-start.20 = (bf16[4,4,128,1024]{3,2,1,0:T(8,128)(2,1)}, bf16[4,4,128,1024]{3,2,1,0:T(8,128)(2,1)}, u32[]{:S(2)}, u32[]{:S(2)}) collective-permute-start(bf16[4,4,128,1024]{3,2,1,0:T(8,128)(2,1)} %get-tuple-element.140.refs_5_.refs_3_), channel_id=1, source_target_pairs={{0,4},{4,0},{1,5},{5,1},{2,6},{6,2},{3,7},{7,3},{8,12},{12,8},{9,1... | collective-permute-start | bytes 12582920 | tf_op jit(solution)/shard_map/ppermute | solution.py:837
  213.0 41.0 %collective-permute-start.17 = (bf16[512,1024]{1,0:T(8,128)(2,1)S(1)}, bf16[512,1024]{1,0:T(8,128)(2,1)}, u32[]{:S(2)}, u32[]{:S(2)}) collective-permute-start(bf16[512,1024]{1,0:T(8,128)(2,1)S(1)} %fusion.5), channel_id=1, source_target_pairs={{0,1},{1,0},{4,5},{5,4},{2,3},{3,2},{6,7},{7,6},{8,9},{9,8},{12,13... | collective-permute-start | bytes 3145736 | tf_op jit(solution)/shard_map/ppermute | solution.py:837
  335.2 52.7 %collective-permute-start.27 = (bf16[512,1024]{1,0:T(8,128)(2,1)}, bf16[512,1024]{1,0:T(8,128)(2,1)S(1)}, u32[]{:S(2)}, u32[]{:S(2)}) collective-permute-start(bf16[512,1024]{1,0:T(8,128)(2,1)} %get-tuple-element.146), channel_id=1, source_target_pairs={{0,0},{2,4},{4,2},{6,6},{1,1},{3,5},{5,3},{7,7},{8,8},{10,12},{12,... | collective-permute-start | bytes 3145736 | tf_op jit(solution)/shard_map/ppermute | solution.py:841
  375.6 55.0 %collective-permute-start.30 = (bf16[4,4,128,1024]{3,2,1,0:T(8,128)(2,1)}, bf16[4,4,128,1024]{3,2,1,0:T(8,128)(2,1)}, u32[]{:S(2)}, u32[]{:S(2)}) collective-permute-start(bf16[4,4,128,1024]{3,2,1,0:T(8,128)(2,1)} %get-tuple-element.152.refs_7_), channel_id=1, source_target_pairs={{0,4},{4,0},{1,5},{5,1},{2,6},{6,2},{3,7},{7,3},{8,12},{12,8},{9,1... | collective-permute-start | bytes 12582920 | tf_op jit(solution)/shard_map/ppermute | solution.py:837
  393.6 55.9 %collective-permute-start.31 = (bf16[4,4,128,1024]{3,2,1,0:T(8,128)(2,1)}, bf16[4,4,128,1024]{3,2,1,0:T(8,128)(2,1)}, u32[]{:S(2)}, u32[]{:S(2)}) collective-permute-start(bf16[4,4,128,1024]{3,2,1,0:T(8,128)(2,1)} %get-tuple-element.155.refs_4_.refs_3_), channel_id=1, source_target_pairs={{0,4},{4,0},{1,5},{5,1},{2,6},{6,2},{3,7},{7,3},{8,12},{12,8},{9,1... | collective-permute-start | bytes 12582920 | tf_op jit(solution)/shard_map/ppermute | solution.py:837
  550.8 77.8 %collective-permute-start.37 = (bf16[4,8,128,1024]{3,2,1,0:T(8,128)(2,1)}, bf16[4,8,128,1024]{3,2,1,0:T(8,128)(2,1)}, u32[]{:S(2)}, u32[]{:S(2)}) collective-permute-start(bf16[4,8,128,1024]{3,2,1,0:T(8,128)(2,1)} %get-tuple-element.170), channel_id=1, source_target_pairs={{0,4},{4,0},{1,5},{5,1},{2,6},{6,2},{3,7},{7,3},{8,12},{12,8},{9,1... | collective-permute-start | bytes 25165832 | tf_op jit(solution)/shard_map/ppermute | solution.py:837
  645.6 46.9 %collective-permute-start.38 = (bf16[8,128,1024]{2,1,0:T(8,128)(2,1)}, bf16[8,128,1024]{2,1,0:T(8,128)(2,1)S(1)}, u32[]{:S(2)}, u32[]{:S(2)}) collective-permute-start(bf16[8,128,1024]{2,1,0:T(8,128)(2,1)} %get-tuple-element.171.refs_2_), channel_id=1, source_target_pairs={{0,8},{8,0},{16,24},{24,16},{1,9},{9,1},{17,25},{25,17},{2,10},{10... | collective-permute-start | bytes 6291464 | tf_op jit(solution)/shard_map/ppermute | solution.py:837
  646.6 46.6 %collective-permute-start.39 = (bf16[8,128,1024]{2,1,0:T(8,128)(2,1)}, bf16[8,128,1024]{2,1,0:T(8,128)(2,1)S(1)}, u32[]{:S(2)}, u32[]{:S(2)}) collective-permute-start(bf16[8,128,1024]{2,1,0:T(8,128)(2,1)} %get-tuple-element.172.refs_3_), channel_id=1, source_target_pairs={{0,16},{8,24},{16,0},{24,8},{1,17},{9,25},{17,1},{25,9},{2,18},{10... | collective-permute-start | bytes 6291464 | tf_op jit(solution)/shard_map/ppermute | solution.py:837
  707.3 49.1 %collective-permute-start.41 = (bf16[4,8,128,1024]{3,2,1,0:T(8,128)(2,1)}, bf16[4,8,128,1024]{3,2,1,0:T(8,128)(2,1)}, u32[]{:S(2)}, u32[]{:S(2)}) collective-permute-start(bf16[4,8,128,1024]{3,2,1,0:T(8,128)(2,1)} %get-tuple-element.184.refs_1_), channel_id=1, source_target_pairs={{0,4},{4,0},{1,5},{5,1},{2,6},{6,2},{3,7},{7,3},{8,12},{12,8},{9,1... | collective-permute-start | bytes 25165832 | tf_op jit(solution)/shard_map/ppermute | solution.py:837
  726.9 45.6 %collective-permute-start.44 = (bf16[4,128,1024]{2,1,0:T(8,128)(2,1)}, bf16[4,128,1024]{2,1,0:T(8,128)(2,1)}, u32[]{:S(2)}, u32[]{:S(2)}) collective-permute-start(bf16[4,128,1024]{2,1,0:T(8,128)(2,1)} %add_convert_fusion.5), channel_id=1, source_target_pairs={{0,8},{8,0},{16,24},{24,16},{1,9},{9,1},{17,25},{25,17},{2,10},{10... | collective-permute-start | bytes 3145736 | tf_op jit(solution)/shard_map/ppermute | solution.py:837
  729.2 44.2 %collective-permute-start.48 = (bf16[4,128,1024]{2,1,0:T(8,128)(2,1)}, bf16[4,128,1024]{2,1,0:T(8,128)(2,1)}, u32[]{:S(2)}, u32[]{:S(2)}) collective-permute-start(bf16[4,128,1024]{2,1,0:T(8,128)(2,1)} %add_convert_fusion.3), channel_id=1, source_target_pairs={{0,16},{8,24},{16,0},{24,8},{1,17},{9,25},{17,1},{25,9},{2,18},{10... | collective-permute-start | bytes 3145736 | tf_op jit(solution)/shard_map/ppermute | solution.py:837
  734.1 45.8 %collective-permute-start.49 = (bf16[512,1024]{1,0:T(8,128)(2,1)S(1)}, bf16[512,1024]{1,0:T(8,128)(2,1)}, u32[]{:S(2)}, u32[]{:S(2)}) collective-permute-start(bf16[512,1024]{1,0:T(8,128)(2,1)S(1)} %copy-done.8), channel_id=1, source_target_pairs={{0,4},{1,5},{4,0},{5,1},{2,6},{3,7},{6,2},{7,3},{8,12},{9,13},{12,... | collective-permute-start | bytes 3145736 | tf_op jit(solution)/shard_map/ppermute | solution.py:837
  756.5 95.6 %collective-permute-start.47 = (bf16[2,128,1024]{2,1,0:T(8,128)(2,1)}, bf16[2,128,1024]{2,1,0:T(8,128)(2,1)S(1)}, u32[]{:S(2)}, u32[]{:S(2)}) collective-permute-start(bf16[2,128,1024]{2,1,0:T(8,128)(2,1)} %fusion.14), channel_id=1, source_target_pairs={{0,16},{8,24},{16,0},{24,8},{1,17},{9,25},{17,1},{25,9},{2,18},{10... | collective-permute-start | bytes 1572872 | tf_op jit(solution)/shard_map/ppermute | solution.py:837
  772.5 79.5 %collective-permute-start.42 = (bf16[8,128,1024]{2,1,0:T(8,128)(2,1)}, bf16[8,128,1024]{2,1,0:T(8,128)(2,1)S(1)}, u32[]{:S(2)}, u32[]{:S(2)}) collective-permute-start(bf16[8,128,1024]{2,1,0:T(8,128)(2,1)} %get-tuple-element.189.refs_2_), channel_id=1, source_target_pairs={{0,8},{8,0},{16,24},{24,16},{1,9},{9,1},{17,25},{25,17},{2,10},{10... | collective-permute-start | bytes 6291464 | tf_op jit(solution)/shard_map/ppermute | solution.py:837
  773.4 78.7 %collective-permute-start.43 = (bf16[8,128,1024]{2,1,0:T(8,128)(2,1)}, bf16[8,128,1024]{2,1,0:T(8,128)(2,1)}, u32[]{:S(2)}, u32[]{:S(2)}) collective-permute-start(bf16[8,128,1024]{2,1,0:T(8,128)(2,1)} %get-tuple-element.190.refs_3_), channel_id=1, source_target_pairs={{0,16},{8,24},{16,0},{24,8},{1,17},{9,25},{17,1},{25,9},{2,18},{10... | collective-permute-start | bytes 6291464 | tf_op jit(solution)/shard_map/ppermute | solution.py:837
  779.9 72.1 %collective-permute-start.45 = (bf16[4,128,1024]{2,1,0:T(8,128)(2,1)}, bf16[4,128,1024]{2,1,0:T(8,128)(2,1)S(1)}, u32[]{:S(2)}, u32[]{:S(2)}) collective-permute-start(bf16[4,128,1024]{2,1,0:T(8,128)(2,1)} %get-tuple-element.278), channel_id=1, source_target_pairs={{0,1},{1,0},{2,3},{3,2},{4,5},{5,4},{6,7},{7,6},{8,9},{9,8},{10,11... | collective-permute-start | bytes 3145736 | tf_op jit(solution)/shard_map/ppermute | solution.py:837
  883.9 58.5 %collective-permute-start.53 = (bf16[512,1024]{1,0:T(8,128)(2,1)}, bf16[512,1024]{1,0:T(8,128)(2,1)}, u32[]{:S(2)}, u32[]{:S(2)}) collective-permute-start(bf16[512,1024]{1,0:T(8,128)(2,1)} %fusion.refs_1_), channel_id=1, source_target_pairs={{0,1},{1,0},{4,5},{5,4},{2,3},{3,2},{6,7},{7,6},{8,9},{9,8},{12,13... | collective-permute-start | bytes 3145736 | tf_op jit(solution)/shard_map/ppermute | solution.py:837
  903.8 38.6 %collective-permute-start.57 = (bf16[4,128,1024]{2,1,0:T(8,128)(2,1)}, bf16[4,128,1024]{2,1,0:T(8,128)(2,1)}, u32[]{:S(2)}, u32[]{:S(2)}) collective-permute-start(bf16[4,128,1024]{2,1,0:T(8,128)(2,1)} %get-tuple-element.276), channel_id=1, source_target_pairs={{0,1},{1,0},{2,3},{3,2},{4,5},{5,4},{6,7},{7,6},{8,9},{9,8},{10,11... | collective-permute-start | bytes 3145736 | tf_op jit(solution)/shard_map/ppermute | solution.py:837
  904.4 38.0 %collective-permute-start.58 = (bf16[2,2,128,1024]{3,2,1,0:T(8,128)(2,1)}, bf16[2,2,128,1024]{3,2,1,0:T(8,128)(2,1)}, u32[]{:S(2)}, u32[]{:S(2)}) collective-permute-start(bf16[2,2,128,1024]{3,2,1,0:T(8,128)(2,1)} %get-tuple-element.211), channel_id=1, source_target_pairs={{0,8},{8,0},{16,24},{24,16},{1,9},{9,1},{17,25},{25,17},{2,10},{10... | collective-permute-start | bytes 3145736 | tf_op jit(solution)/shard_map/ppermute | solution.py:837
  908.8 36.7 %collective-permute-start.68 = (bf16[2,128,1024]{2,1,0:T(8,128)(2,1)}, bf16[2,128,1024]{2,1,0:T(8,128)(2,1)}, u32[]{:S(2)}, u32[]{:S(2)}) collective-permute-start(bf16[2,128,1024]{2,1,0:T(8,128)(2,1)} %fusion.6), channel_id=1, source_target_pairs={{0,2},{2,0},{1,3},{3,1},{4,6},{6,4},{5,7},{7,5},{8,10},{10,8},{9,1... | collective-permute-start | bytes 1572872 | tf_op jit(solution)/shard_map/ppermute | solution.py:837
  958.0 48.1 %collective-permute-start.67 = (bf16[2,128,1024]{2,1,0:T(8,128)(2,1)}, bf16[2,128,1024]{2,1,0:T(8,128)(2,1)}, u32[]{:S(2)}, u32[]{:S(2)}) collective-permute-start(bf16[2,128,1024]{2,1,0:T(8,128)(2,1)} %fusion.8), channel_id=1, source_target_pairs={{0,2},{2,0},{1,3},{3,1},{4,6},{6,4},{5,7},{7,5},{8,10},{10,8},{9,1... | collective-permute-start | bytes 1572872 | tf_op jit(solution)/shard_map/ppermute | solution.py:837
  972.1 61.1 %collective-permute-start.54 = (bf16[512,1024]{1,0:T(8,128)(2,1)}, bf16[512,1024]{1,0:T(8,128)(2,1)S(1)}, u32[]{:S(2)}, u32[]{:S(2)}) collective-permute-start(bf16[512,1024]{1,0:T(8,128)(2,1)} %fusion.2), channel_id=1, source_target_pairs={{0,0},{2,4},{4,2},{6,6},{1,1},{3,5},{5,3},{7,7},{8,8},{10,12},{12,... | collective-permute-start | bytes 3145736 | tf_op jit(solution)/shard_map/ppermute | solution.py:841
  979.9 43.4 %collective-permute-start.60 = (bf16[2,128,1024]{2,1,0:T(8,128)(2,1)S(1)}, bf16[2,128,1024]{2,1,0:T(8,128)(2,1)S(1)}, u32[]{:S(2)}, u32[]{:S(2)}) collective-permute-start(bf16[2,128,1024]{2,1,0:T(8,128)(2,1)S(1)} %pad_maximum_fusion.4), channel_id=1, source_target_pairs={{0,0},{2,4},{4,2},{6,6},{1,1},{3,5},{5,3},{7,7},{8,8},{10,12},{12,... | collective-permute-start | bytes 1572872 | tf_op jit(solution)/shard_map/ppermute | solution.py:841
  981.9 41.4 %collective-permute-start.61 = (bf16[2,128,1024]{2,1,0:T(8,128)(2,1)S(1)}, bf16[2,128,1024]{2,1,0:T(8,128)(2,1)S(1)}, u32[]{:S(2)}, u32[]{:S(2)}) collective-permute-start(bf16[2,128,1024]{2,1,0:T(8,128)(2,1)S(1)} %pad_maximum_fusion.5), channel_id=1, source_target_pairs={{2,0},{6,2},{0,4},{4,6},{3,1},{7,3},{1,5},{5,7},{10,8},{14,10},{8,... | collective-permute-start | bytes 1572872 | tf_op jit(solution)/shard_map/ppermute | solution.py:849
  (119 other events, 1399.0 us)
Sparse Core Ops, SparseCore 0:
  10.8 101.5 all-gather.4
  115.1 75.9 all-gather.6
  194.5 90.1 all-gather.10
  287.3 95.9 all-gather.8

commit v5 on v4

--- a/solution.py
+++ b/solution.py
@@ -25,7 +25,7 @@
 TIMES = {
     "gate": 0.1, "norm_up": 20.0, "down_norm": 20.0, "units_back": 20.0, "up_back": 20.0, "norm_back": 6.0,
     "sum_norm_back": 20.0, "grads_theirs": 0.2, "grads_mine": 0.2, "project_qkv": 0.2, "project_gc": 0.2,
-    "project_attn": 0.2, "project_gx": 0.2, "heads_grad": 0.2, "attend_forward": 40.0, "attend_backward": 60.0,
+    "project_attn": 0.2, "project_gx": 0.2, "heads_grad": 0.2, "attend_forward": 40.0, "attend_backward": 30.0,
 }
 PEAK = 0.35e9
 NT = (((1,), (1,)), ((), ()))
@@ -33,6 +33,7 @@
 ROWS = 128
 CHUNK = 64
 BQ = 256
+PAIR = 2 * HD
 
 
 def mm(left, right, dims=NN):
@@ -187,17 +188,18 @@
 
 
 class Streamed:
-    def __init__(self, refs, buffer, sems, scal):
-        self.refs, self.buffer, self.sems, self.scal = refs, buffer, sems, scal
+    def __init__(self, refs, matrix, buffer, sems, scal):
+        self.refs, self.matrix, self.buffer, self.sems, self.scal = refs, matrix, buffer, sems, scal
 
     def copies(self, s):
         slot = lax.rem(s, 2)
-        for k, ref in enumerate(self.refs):
-            for q in range(4):
-                row = (2 * q + (self.scal[S_C] ^ k)) * ROWS
+        for k in range(2):
+            main, far = self.refs[2 * k : 2 * k + 2]
+            for r in range(4):
+                row = ((self.scal[S_Q] ^ r) * 2 + (self.scal[S_C] ^ k)) * ROWS
+                source = far.at[s, self.matrix] if r == 3 else main.at[r, s, self.matrix]
                 yield pltpu.make_async_copy(
-                    ref.at[s, q], self.buffer.at[slot, pl.ds(pl.multiple_of(row, ROWS), ROWS), :],
-                    self.sems.at[slot, 4 * k + q],
+                    source, self.buffer.at[slot, pl.ds(pl.multiple_of(row, ROWS), ROWS), :], self.sems.at[slot, 4 * k + r]
                 )
 
     def start(self, s):
@@ -238,16 +240,16 @@
             yield slice(i * tokens // 2, (i + 1) * tokens // 2), slice(j * width // 2, (j + 1) * width // 2)
 
 
-def norm_up(flow, prev, parts, vec, rows_used, weight, bias, count):
+def norm_up(flow, prev, parts, vec, rows_used, weight, matrix, bias, count):
     tokens = prev.shape[0]
     width = FF // count
 
     def body(scal_ref, prev_ref, *refs):
         part_refs, refs = refs[: len(parts)], refs[len(parts) :]
         vec_ref, bias_ref, refs = refs[0], refs[1], refs[2:]
-        pieces, (n_ref, low_ref, inv_ref, act_ref, slope_ref, buffer, sems) = refs[:2], refs[2:]
+        pieces, (n_ref, low_ref, inv_ref, act_ref, slope_ref, buffer, sems) = refs[:4], refs[4:]
         s = pl.program_id(0)
-        stream = Streamed(pieces, buffer, sems, scal_ref)
+        stream = Streamed(pieces, matrix, buffer, sems, scal_ref)
         stream.turn(s, count)
 
         @pl.when(s == 0)
@@ -272,7 +274,7 @@
     return call(
         flow, body, (count,),
         [full((tokens, D))] + [part_spec(part) for part in parts]
-        + [full((TABLE, D)), pl.BlockSpec((1, 1, width), lambda s, _: (s, 0, 0))] + [ANY] * 2,
+        + [full((TABLE, D)), pl.BlockSpec((1, 1, width), lambda s, scal_ref: (scal_ref[S_Z] ^ away(s), 0, 0))] + [ANY] * 4,
         [full((tokens, D)), full((tokens, D)), full((tokens, 128)), column, column],
         [sds((tokens, D), F32), sds((tokens, D), BF16), sds((tokens, 128), F32)] + [sds((tokens, FF), BF16)] * 2,
         piece_shapes(width), [prev, *parts, vec, bias, *weight], 2 * tokens * D * FF,
@@ -280,14 +282,14 @@
     )
 
 
-def down_norm(flow, act, weight, prev, vec, rows_used, count):
+def down_norm(flow, act, weight, matrix, prev, vec, rows_used, count):
     tokens = prev.shape[0]
     width = FF // count
 
     def body(scal_ref, act_ref, prev_ref, vec_ref, *refs):
-        pieces, (n_ref, low_ref, inv_ref, buffer, sems, acc) = refs[:2], refs[2:]
+        pieces, (n_ref, low_ref, inv_ref, buffer, sems, acc) = refs[:4], refs[4:]
         s = pl.program_id(0)
-        stream = Streamed(pieces, buffer, sems, scal_ref)
+        stream = Streamed(pieces, matrix, buffer, sems, scal_ref)
         stream.turn(s, count)
         stream.wait(s)
         value = mm(act_ref[...], buffer[lax.rem(s, 2)], NT)
@@ -310,7 +312,7 @@
 
     return call(
         flow, body, (count,),
-        [pl.BlockSpec((tokens, width), lambda s, _: (0, s)), full((tokens, D)), full((TABLE, D))] + [ANY] * 2,
+        [pl.BlockSpec((tokens, width), lambda s, _: (0, s)), full((tokens, D)), full((TABLE, D))] + [ANY] * 4,
         [full((tokens, D)), full((tokens, D)), full((tokens, 128))],
         [sds((tokens, D), F32), sds((tokens, D), BF16), sds((tokens, 128), F32)],
         piece_shapes(width) + [pltpu.VMEM((tokens, D), F32)], [act, prev, vec, *weight], 2 * tokens * D * FF,
@@ -318,14 +320,14 @@
     )
 
 
-def units_back(flow, grad, weight, slope, count):
+def units_back(flow, grad, weight, matrix, slope, count):
     tokens = grad.shape[0]
     width = FF // count
 
     def body(scal_ref, grad_ref, slope_ref, *refs):
-        pieces, (out_ref, sum_ref, buffer, sems) = refs[:2], refs[2:]
+        pieces, (out_ref, sum_ref, buffer, sems) = refs[:4], refs[4:]
         s = pl.program_id(0)
-        stream = Streamed(pieces, buffer, sems, scal_ref)
+        stream = Streamed(pieces, matrix, buffer, sems, scal_ref)
         stream.turn(s, count)
         stream.wait(s)
         slot = lax.rem(s, 2)
@@ -340,21 +342,21 @@
 
     column = pl.BlockSpec((tokens, width), lambda s, _: (0, s))
     return call(
-        flow, body, (count,), [full((tokens, D)), column] + [ANY] * 2,
-        [column, pl.BlockSpec((1, 1, width), lambda s, _: (s, 0, 0))],
+        flow, body, (count,), [full((tokens, D)), column] + [ANY] * 4,
+        [column, pl.BlockSpec((1, 1, width), lambda s, scal_ref: (scal_ref[S_Z] ^ away(s), 0, 0))],
         [sds((tokens, FF), BF16), sds((count, 1, width), F32)], piece_shapes(width), [grad, slope, *weight],
         2 * tokens * D * FF, 2 * (D * FF + tokens * (D + 2 * FF)), "units_back",
     )
 
 
-def up_back(flow, gu, weight, residual, normed, inverse, vec, gain, count):
+def up_back(flow, gu, weight, matrix, residual, normed, inverse, vec, gain, count):
     tokens = residual.shape[0]
     width = FF // count
 
     def body(scal_ref, gu_ref, res_ref, n_ref, inv_ref, vec_ref, *refs):
-        pieces, (g_ref, low_ref, sums_ref, buffer, sems, acc) = refs[:2], refs[2:]
+        pieces, (g_ref, low_ref, sums_ref, buffer, sems, acc) = refs[:4], refs[4:]
         s = pl.program_id(0)
-        stream = Streamed(pieces, buffer, sems, scal_ref)
+        stream = Streamed(pieces, matrix, buffer, sems, scal_ref)
         stream.turn(s, count)
         stream.wait(s)
         value = mm(gu_ref[...], buffer[lax.rem(s, 2)], NT)
@@ -377,7 +379,7 @@
     return call(
         flow, body, (count,),
         [pl.BlockSpec((tokens, width), lambda s, _: (0, s)), full((tokens, D)), full((tokens, D)), full((tokens, 128)),
-         full((TABLE, D))] + [ANY] * 2,
+         full((TABLE, D))] + [ANY] * 4,
         [full((tokens, D)), full((tokens, D)), full((8, D))],
         [sds((tokens, D), F32), sds((tokens, D), BF16), sds((8, D), F32)],
         piece_shapes(width) + [pltpu.VMEM((tokens, D), F32)], [gu, residual, normed, inverse, vec, *weight],
@@ -480,8 +482,8 @@
             store(y1_ref)
 
     left = full((tokens, D))
-    pick_down = lambda t, scal_ref: (0, scal_ref[S_Z] ^ away(jnp.minimum(t, count - 1)))
-    pick_up = lambda t, scal_ref: (0, scal_ref[S_Z] ^ away(jnp.maximum(t - count, 0)))
+    pick_down = lambda t, _: (0, jnp.minimum(t, count - 1))
+    pick_up = lambda t, _: (0, jnp.maximum(t - count, 0))
     specs = [left, pl.BlockSpec((tokens, width), pick_down), left, pl.BlockSpec((tokens, width), pick_up)]
     args = [*down, *up]
     one = pl.BlockSpec((4, 1, ROWS, width), lambda t, _: (0, t, 0, 0))
@@ -506,7 +508,7 @@
             row = ((scal_ref[S_Q] ^ r) * 2 + (scal_ref[S_ZH] ^ k)) * ROWS
             copies.append(
                 pltpu.make_async_copy(
-                    pieces[r].at[k, pl.ds(0, ROWS), cols], buffer.at[pl.ds(pl.multiple_of(row, ROWS), ROWS), :],
+                    pieces[r // 2].at[r % 2, k, pl.ds(0, ROWS), cols], buffer.at[pl.ds(pl.multiple_of(row, ROWS), ROWS), :],
                     sems.at[2 * r + k],
                 )
             )
@@ -531,7 +533,7 @@
     def body(scal_ref, left_ref, right_ref, *refs):
         if bias is not None:
             bias_ref, refs = refs[0], refs[1:]
-        pieces, (out_ref, buffer, sems) = refs[:4], refs[4:]
+        pieces, (out_ref, buffer, sems) = refs[:2], refs[2:]
         step = pl.program_id(0)
 
         @pl.when(step == 0)
@@ -549,24 +551,28 @@
 
     extra, extra_specs = ([], []) if bias is None else ([bias], [full((1, width))])
     return call(
-        flow, body, (2,), [full((tokens, D))] * 2 + extra_specs + [ANY] * 4,
+        flow, body, (2,), [full((tokens, D))] * 2 + extra_specs + [ANY] * 2,
         pl.BlockSpec((1, tokens, width), lambda r, scal_ref: ((scal_ref[S_P] >> 1) ^ r, 0, 0)),
         sds((2, tokens, width), BF16), heads_weight_scratch(width), [*lefts, *extra, *weight], 0, 0, name,
     )
 
 
 def project_out(flow, blocks, members, weight, cols, stacked, name):
-    count, tokens, width = blocks.shape
-
-    def body(scal_ref, block_ref, *refs):
-        pieces, outs, (buffer, sems) = refs[:4], refs[4:-2], refs[-2:]
+    count, tokens, width = blocks[0].shape
+
+    def body(scal_ref, *refs):
+        block_refs, refs = refs[: len(blocks)], refs[len(blocks) :]
+        pieces, outs, (buffer, sems) = refs[:2], refs[2:-2], refs[-2:]
         step = pl.program_id(0)
 
         @pl.when(step == 0)
         def _():
             fetch_heads_weight(scal_ref, pieces, cols, buffer, sems)
 
-        value = mm(block_ref[0], buffer[...], NT).astype(BF16)
+        value = mm(block_refs[0][0], buffer[:, :width], NT)
+        for index in range(1, len(blocks)):
+            value = value + mm(block_refs[index][0], buffer[:, index * width : (index + 1) * width], NT)
+        value = value.astype(BF16)
         if stacked:
             outs[0][0] = value
             return
@@ -583,36 +589,35 @@
     else:
         out_specs, out_shape = [full((tokens, D))] * 2, [sds((tokens, D), BF16)] * 2
     return call(
-        flow, body, (2,), [pl.BlockSpec((1, tokens, width), pick)] + [ANY] * 4, out_specs, out_shape,
-        heads_weight_scratch(width), [blocks, *weight], 0, 0, name,
+        flow, body, (2,), [pl.BlockSpec((1, tokens, width), pick)] * len(blocks) + [ANY] * 2, out_specs, out_shape,
+        heads_weight_scratch(width * len(blocks)), [*blocks, *weight], 0, 0, name,
     )
 
 
-def heads_grad(flow, xs, gqkv, gas, ctx):
-    count, tokens, width = gqkv.shape
+def heads_grad(flow, xs, parts, gas, ctx):
+    count, tokens, width = parts[0].shape
     out_width = ctx.shape[2]
+    cuts = [slice(i * width, (i + 1) * width) for i in range(len(parts))]
+    total = width * len(parts)
 
     def body(scal_ref, *refs):
         x_refs, refs = refs[:count], refs[count:]
         ga_refs, refs = refs[:count], refs[count:]
-        g_ref, ctx_ref = refs[:2]
-        outs, (sum_ref, acc, acc_out) = refs[2:4], refs[4:]
+        part_refs, refs = refs[: len(parts)], refs[len(parts) :]
+        ctx_ref, outs, (sum_ref, acc, acc_out) = refs[0], refs[1:3], refs[3:]
         step = pl.program_id(0)
         for r in range(count):
 
             @pl.when(step == r)
             def _(r=r):
-                value = mm(x_refs[r][...].T, g_ref[0])
+                turned = x_refs[r][...].T
                 value_out = mm(ga_refs[r][...].T, ctx_ref[0])
-                sums = jnp.sum(g_ref[0].astype(F32), 0, keepdims=True)
-                if r == 0:
-                    acc[...] = value
-                    acc_out[...] = value_out
-                    sum_ref[...] = sums
-                else:
-                    acc[...] += value
-                    acc_out[...] += value_out
-                    sum_ref[...] += sums
+                for cut, part in zip(cuts, part_refs):
+                    value = mm(turned, part[0])
+                    sums = jnp.sum(part[0].astype(F32), 0, keepdims=True)
+                    acc[:, cut] = value if r == 0 else acc[:, cut] + value
+                    sum_ref[:, cut] = sums if r == 0 else sum_ref[:, cut] + sums
+                acc_out[...] = value_out if r == 0 else acc_out[...] + value_out
 
         @pl.when(step == count - 1)
         def _():
@@ -620,15 +625,15 @@
                 for k in range(2):
                     row = ((scal_ref[S_Q] ^ r) * 2 + (scal_ref[S_ZH] ^ k)) * ROWS
                     rows = pl.ds(pl.multiple_of(row, ROWS), ROWS)
-                    outs[r % 2][r // 2, k, :, :width] = acc[rows, :].astype(BF16)
-                    outs[r % 2][r // 2, k, :, width:] = acc_out[rows, :].astype(BF16)
-
-    shape = (2, 2, ROWS, width + out_width)
+                    outs[r % 2][r // 2, k, :, :total] = acc[rows, :].astype(BF16)
+                    outs[r % 2][r // 2, k, :, total:] = acc_out[rows, :].astype(BF16)
+
+    shape = (2, 2, ROWS, total + out_width)
     return call(
-        flow, body, (count,), [full((tokens, D))] * (2 * count) + [by_member((tokens, width)), by_member((tokens, out_width))],
-        [full(shape)] * 2 + [full((1, width))], [sds(shape, BF16)] * 2 + [sds((1, width), F32)],
-        [pltpu.VMEM((D, width), F32), pltpu.VMEM((D, out_width), F32)], [*xs, *gas, gqkv, ctx],
-        2 * tokens * D * (width + out_width) * count, 4 * count * tokens * (D + width), "heads_grad",
+        flow, body, (count,),
+        [full((tokens, D))] * (2 * count) + [by_member((tokens, width))] * len(parts) + [by_member((tokens, out_width))],
+        [full(shape)] * 2 + [full((1, total))], [sds(shape, BF16)] * 2 + [sds((1, total), F32)],
+        [pltpu.VMEM((D, total), F32), pltpu.VMEM((D, out_width), F32)], [*xs, *gas, *parts, ctx], 0, 0, "heads_grad",
     )
 
 
@@ -649,10 +654,12 @@
         yield 2 * core + 1 - here, far_ref.at[core]
 
 
-def over_keys(ends_ref, start, chunk, block):
+def over_keys(ends_ref, start, chunk, keys_first, block):
     low_first, high_first = reach(ends_ref, start)
     low_last, high_last = reach(ends_ref, start + BQ - 1)
-    low_row, high_row = reach(ends_ref, start + lax.broadcasted_iota(jnp.int32, (1, BQ), 1))
+    axis = 1 if keys_first else 0
+    low_row, high_row = reach(ends_ref, start + lax.broadcasted_iota(jnp.int32, (1, BQ) if keys_first else (BQ, 1), axis))
+    shape = (chunk, BQ) if keys_first else (BQ, chunk)
 
     def one(b, carry):
         open_all = (b * chunk >= low_last) & ((b + 1) * chunk <= high_first)
@@ -663,7 +670,7 @@
 
         @pl.when(jnp.logical_not(open_all))
         def _():
-            key = b * chunk + lax.broadcasted_iota(jnp.int32, (chunk, BQ), 0)
+            key = b * chunk + lax.broadcasted_iota(jnp.int32, shape, 1 - axis)
             block(b, (key >= low_row) & (key < high_row))
 
         return carry
@@ -679,20 +686,24 @@
     steps = SEQLEN // BQ
     per = chunk // BQ
 
-    def body(scal_ref, ends_ref, near_ref, far_ref, ctx_ref, wide_ref, lse_ref, qh, kh, vt, acc, tops, sums, scores):
+    def body(scal_ref, ends_ref, near_ref, far_ref, ctx_ref, wide_ref, lse_ref, qt, kh, vt, acc, tops, sums, scores):
         step = pl.program_id(0)
 
         @pl.when(step == 0)
         def _():
             for j, block in chunks_of(scal_ref, near_ref, far_ref):
                 rows = pl.ds(pl.multiple_of(j * chunk, chunk), chunk)
-                for h in range(heads):
-                    qh[h, rows, :] = block[:, h * HD : (h + 1) * HD] * BF16(HD**-0.5)
-                    kh[h, rows, :] = block[:, width + h * HD : width + (h + 1) * HD]
-                vt[j] = block[:, 2 * width :].T
+                for pair in range(heads // 2):
+                    base = 3 * PAIR * pair
+                    part = slice(pair * PAIR, (pair + 1) * PAIR)
+                    vt[j, part, :] = block[:, base + 2 * PAIR : base + 3 * PAIR].T
+                    for s in range(per):
+                        queries = block[s * BQ : (s + 1) * BQ, base : base + PAIR] * BF16(HD**-0.5)
+                        qt[j * per + s, part, :] = queries.T
+                    for h in range(2):
+                        kh[2 * pair + h, rows, :] = block[:, base + PAIR + h * HD : base + PAIR + (h + 1) * HD]
 
         start = step * BQ
-        rows = pl.ds(pl.multiple_of(start, BQ), BQ)
         acc[...] = jnp.zeros(acc.shape, F32)
         tops[...] = jnp.full(tops.shape, -3.0e38, F32)
         sums[...] = jnp.zeros(sums.shape, F32)
@@ -700,13 +711,13 @@
         def score(b, allowed):
             keys = pl.ds(pl.multiple_of(b * chunk, chunk), chunk)
             for h in range(heads):
-                value = mm(kh[h, keys, :], qh[h, rows, :], NT)
+                value = mm(kh[h, keys, :], qt[step, h * HD : (h + 1) * HD, :])
                 if allowed is not None:
                     value = jnp.where(allowed, value, FILL)
                 scores[h, b] = value
                 tops[h] = jnp.maximum(tops[h], jnp.max(value.reshape(-1, 8, BQ), 0))
 
-        over_keys(ends_ref, start, chunk, score)
+        over_keys(ends_ref, start, chunk, True, score)
         top = [jnp.max(tops[h], 0, keepdims=True) for h in range(heads)]
 
         def weigh(b, carry):
@@ -720,22 +731,24 @@
         low_first, _ = reach(ends_ref, start)
         _, high_last = reach(ends_ref, start + BQ - 1)
         lax.fori_loop(low_first // chunk, (high_last + chunk - 1) // chunk, weigh, 0)
+        lse_ref[...] = jnp.zeros(lse_ref.shape, F32)
         for h in range(heads):
             part = slice(h * HD, (h + 1) * HD)
             total = jnp.sum(sums[h], 0, keepdims=True)
-            wide_ref[part, :] = acc[part, :] / total
-            lse_ref[h : h + 1, :] = top[h] + jnp.log(total)
-        lse_ref[heads:, :] = jnp.zeros((8 - heads, BQ), F32)
-        ctx_ref[0] = wide_ref[...].T.astype(BF16)
-
-    pairs = SEQLEN * SEQLEN
+            acc[part, :] = acc[part, :] / total
+            lse_ref[0, h : h + 1, :] = top[h] + jnp.log(total)
+        wide = acc[...].T
+        wide_ref[0] = wide
+        ctx_ref[0] = wide.astype(BF16)
+
+    row_block = lambda i, *_: (i // per, i % per, 0)
     return call(
         flow, body, (steps,), [full((2, chunk, width3))] * 2,
-        [pl.BlockSpec((1, BQ, width), lambda i, *_: (i // per, i % per, 0)),
-         pl.BlockSpec((width, BQ), lambda i, *_: (0, i)), pl.BlockSpec((8, BQ), lambda i, *_: (0, i))],
-        [sds((count, chunk, width), BF16), sds((width, SEQLEN), F32), sds((8, SEQLEN), F32)],
+        [pl.BlockSpec((1, BQ, width), row_block), pl.BlockSpec((1, BQ, width), row_block),
+         pl.BlockSpec((1, 8, BQ), lambda i, *_: (i, 0, 0))],
+        [sds((count, chunk, width), BF16), sds((count, chunk, width), F32), sds((steps, 8, BQ), F32)],
         [
-            pltpu.VMEM((heads, SEQLEN, HD), BF16),
+            pltpu.VMEM((steps, width, BQ), BF16),
             pltpu.VMEM((heads, SEQLEN, HD), BF16),
             pltpu.VMEM((count, width, chunk), BF16),
             pltpu.VMEM((width, BQ), F32),
@@ -743,20 +756,18 @@
             pltpu.VMEM((heads, 8, BQ), F32),
             pltpu.VMEM((heads, count, chunk, BQ), F32),
         ],
-        [*qkv], 16 * pairs * heads * HD, 6 * SEQLEN * width * 2, "attend_forward", (flow.scal, ends),
+        [*qkv], 0, 0, "attend_forward", (flow.scal, ends),
     )
 
 
-def attend_backward(flow, ends, qkv, grads, wide, lse):
-    _, chunk, width3 = qkv[0].shape
+def attend_backward(flow, ends, pair, qkv, grads, wide, lse):
+    chunk = qkv[0].shape[1]
     count = SEQLEN // chunk
-    width = width3 // 3
-    heads = width // HD
     steps = SEQLEN // BQ
     per = chunk // BQ
 
     def body(
-        scal_ref, ends_ref, near_ref, far_ref, grad_near, grad_far, wide_ref, lse_ref, out_ref, qh, kh, vh, gh, kt, qt, gt,
+        scal_ref, ends_ref, near_ref, far_ref, grad_near, grad_far, wide_ref, lse_ref, out_ref, qh, kh, gh, kt, vt, qt, gt,
         gq, gk, gv,
     ):
         step = pl.program_id(0)
@@ -767,69 +778,72 @@
             grad_blocks = chunks_of(scal_ref, grad_near, grad_far)
             for (j, block), (_, grad_block) in zip(blocks, grad_blocks):
                 rows = pl.ds(pl.multiple_of(j * chunk, chunk), chunk)
-                for h in range(heads):
+                queries = block[:, :PAIR] * BF16(HD**-0.5)
+                keys = block[:, PAIR : 2 * PAIR]
+                back = grad_block[...]
+                for h in range(2):
                     cols = slice(h * HD, (h + 1) * HD)
-                    qh[h, rows, :] = block[:, cols] * BF16(HD**-0.5)
-                    kh[h, rows, :] = block[:, width + h * HD : width + (h + 1) * HD]
-                    vh[h, rows, :] = block[:, 2 * width + h * HD : 2 * width + (h + 1) * HD]
-                    gh[h, rows, :] = grad_block[:, cols]
-                kt[j] = block[:, width : 2 * width].T
+                    qh[h, rows, :] = queries[:, cols]
+                    kh[h, rows, :] = keys[:, cols]
+                    gh[h, rows, :] = back[:, cols]
+                kt[j] = keys.T
+                vt[j] = block[:, 2 * PAIR :].T
                 for s in range(per):
                     sub = slice(s * BQ, (s + 1) * BQ)
-                    qt[j * per + s] = (block[sub, :width] * BF16(HD**-0.5)).T
-                    gt[j * per + s] = grad_block[sub, :].T
+                    qt[j * per + s] = queries[sub, :].T
+                    gt[j * per + s] = back[sub, :].T
             gk[...] = jnp.zeros(gk.shape, F32)
             gv[...] = jnp.zeros(gv.shape, F32)
 
         start = step * BQ
         rows = pl.ds(pl.multiple_of(start, BQ), BQ)
         gq[...] = jnp.zeros(gq.shape, F32)
-        inner = []
-        for h in range(heads):
-            part = slice(h * HD, (h + 1) * HD)
-            inner.append(jnp.sum(gt[step, part, :].astype(F32) * wide_ref[part, :], 0, keepdims=True))
+        sums = lse_ref[0].T
+        inner, logs = [], []
+        for h in range(2):
+            product = gh[h, rows, :].astype(F32) * wide_ref[0, :, h * HD : (h + 1) * HD]
+            inner.append(jnp.sum(product, 1, keepdims=True))
+            logs.append(sums[:, 2 * pair + h : 2 * pair + h + 1])
 
         def block(b, allowed):
             keys = pl.ds(pl.multiple_of(b * chunk, chunk), chunk)
-            for h in range(heads):
+            for h in range(2):
                 part = slice(h * HD, (h + 1) * HD)
-                score = mm(kh[h, keys, :], qh[h, rows, :], NT)
-                grad_weight = mm(vh[h, keys, :], gh[h, rows, :], NT)
+                score = mm(qh[h, rows, :], kt[b, part, :])
+                grad_weight = mm(gh[h, rows, :], vt[b, part, :])
                 if allowed is not None:
                     score = jnp.where(allowed, score, FILL)
-                weight = jnp.exp(score - lse_ref[h : h + 1, :])
+                weight = jnp.exp(score - logs[h])
                 grad_score = (weight * (grad_weight - inner[h])).astype(BF16)
-                gv[b, part, :] += mm(gt[step, part, :], weight.astype(BF16), NT)
-                gk[b, part, :] += mm(qt[step, part, :], grad_score, NT)
-                gq[part, :] += mm(kt[b, part, :], grad_score)
-
-        over_keys(ends_ref, start, chunk, block)
-        out_ref[step // per, pl.ds(pl.multiple_of((step % per) * BQ, BQ), BQ), :width] = (
-            (gq[...] * HD**-0.5).T.astype(BF16)
-        )
+                gv[b, part, :] += mm(gt[step, part, :], weight.astype(BF16))
+                gk[b, part, :] += mm(qt[step, part, :], grad_score)
+                gq[h] += mm(grad_score, kh[h, keys, :])
+
+        over_keys(ends_ref, start, chunk, False, block)
+        place = pl.ds(pl.multiple_of((step % per) * BQ, BQ), BQ)
+        for h in range(2):
+            out_ref[step // per, place, h * HD : (h + 1) * HD] = (gq[h] * HD**-0.5).astype(BF16)
 
         @pl.when(step == steps - 1)
         def _():
             for j in range(count):
-                out_ref[j, :, width : 2 * width] = gk[j].T.astype(BF16)
-                out_ref[j, :, 2 * width :] = gv[j].T.astype(BF16)
-
-    pairs = SEQLEN * SEQLEN
+                out_ref[j, :, PAIR : 2 * PAIR] = gk[j].T.astype(BF16)
+                out_ref[j, :, 2 * PAIR :] = gv[j].T.astype(BF16)
+
+    out = (count, chunk, 3 * PAIR)
     return call(
         flow, body, (steps,),
-        [full((2, chunk, width3))] * 2 + [full((2, chunk, width))] * 2
-        + [pl.BlockSpec((width, BQ), lambda i, *_: (0, i)), pl.BlockSpec((8, BQ), lambda i, *_: (0, i))],
-        full((count, chunk, width3)), sds((count, chunk, width3), BF16),
-        [pltpu.VMEM((heads, SEQLEN, HD), BF16)] * 4
-        + [
-            pltpu.VMEM((count, width, chunk), BF16),
-            pltpu.VMEM((steps, width, BQ), BF16),
-            pltpu.VMEM((steps, width, BQ), BF16),
-            pltpu.VMEM((width, BQ), F32),
-            pltpu.VMEM((count, width, chunk), F32),
-            pltpu.VMEM((count, width, chunk), F32),
-        ],
-        [*qkv, *grads, wide, lse], 28 * pairs * heads * HD, 20 * SEQLEN * width, "attend_backward", (flow.scal, ends),
+        [pl.BlockSpec((2, chunk, 3 * PAIR), lambda i, *_: (0, 0, pair))] * 2
+        + [pl.BlockSpec((2, chunk, PAIR), lambda i, *_: (0, 0, pair))] * 2
+        + [pl.BlockSpec((1, BQ, PAIR), lambda i, *_: (i // per, i % per, pair)),
+           pl.BlockSpec((1, 8, BQ), lambda i, *_: (i, 0, 0))],
+        full(out), sds(out, BF16),
+        [pltpu.VMEM((2, SEQLEN, HD), BF16)] * 3
+        + [pltpu.VMEM((count, PAIR, chunk), BF16)] * 2
+        + [pltpu.VMEM((steps, PAIR, BQ), BF16)] * 2
+        + [pltpu.VMEM((2, BQ, HD), F32)]
+        + [pltpu.VMEM((count, PAIR, chunk), F32)] * 2,
+        [*qkv, *grads, wide, lse], 0, 0, "attend_backward", (flow.scal, ends),
     )
 
 
@@ -881,7 +895,15 @@
 
 def gather_group(values_in):
     across, sibling = flip(values_in, GROUP, 1), flip(values_in, GROUP, 2)
-    return [values_in, across, sibling, flip(across, GROUP, 2)]
+    return [values_in, across, sibling]
+
+
+def forward(flow, members, *before):
+    flow.wait(*before)
+    flow.hold(across=members[1])
+    gate(flow)
+    members[1] = flow.free("across")
+    members.append(flip(members[1], GROUP, 2))
 
 
 def sum_group(keep, send):
@@ -894,19 +916,27 @@
 
 
 def heads_shard_of(qkv, out, bias):
-    weights = jnp.concatenate([qkv.transpose(1, 0, 2).reshape(out.shape[0], -1), out], axis=1)
+    rows = out.shape[0]
+    paired = qkv.reshape(3, rows, -1, PAIR).transpose(1, 2, 0, 3).reshape(rows, -1)
+    weights = jnp.concatenate([paired, out], axis=1)
     below = jnp.pad(bias.reshape(1, -1), ((0, EXTRA - 1), (0, weights.shape[1] - bias.size)))
     return jnp.concatenate([weights, below])
 
 
 def heads_bias(rows, heads):
     bias = rows.reshape(rows.shape[0], 2, heads, -1).transpose(1, 2, 0, 3).reshape(2, -1).astype(F32)
-    return jnp.concatenate([bias[0], jnp.zeros_like(bias[0]), bias[1]])[None]
-
-
-def heads_bias_near(members, size, heads, where, zh):
-    rows = jnp.stack([member[:, ROWS, :size] for member in members])
-    return heads_bias(order_by(order_by(rows, 0, where[0], 4), 1, zh, 2).reshape(8, size), heads)
+    bias = jnp.stack([bias[0], jnp.zeros_like(bias[0]), bias[1]])
+    return bias.reshape(3, -1, PAIR).transpose(1, 0, 2).reshape(1, -1)
+
+
+def heads_along_x(pair):
+    return jnp.stack([pair, flip(pair, "q", 1)])
+
+
+def heads_along_y(near, size, heads, where, zh):
+    far = flip(near, "q", 2)
+    rows = jnp.concatenate([near[:, :, ROWS, :size], far[:, :, ROWS, :size]])
+    return [near, far], heads_bias(order_by(order_by(rows, 0, where[0], 4), 1, zh, 2).reshape(8, size), heads)
 
 
 def all_heads_weight(shard, size, heads, zh):
@@ -914,7 +944,7 @@
     every = order_by(lax.all_gather(pair, "q"), 1, zh, 2)
     count = shard.shape[0] - EXTRA
     weights = every[:, :, :count].reshape(4, 2, ROWS, -1)
-    return [weights[r] for r in range(4)], heads_bias(every[:, :, count, :size].reshape(-1, size), heads)
+    return [weights[:2], weights[2:]], heads_bias(every[:, :, count, :size].reshape(-1, size), heads)
 
 
 class HeadsGrad:
@@ -943,12 +973,58 @@
 SLOTS = (0, 2, 1, 3)
 
 
-def units_weight(shard):
-    if is_small():
-        return lax.all_gather(shard, MODEL + ("q",)).reshape(-1, 4, ROWS, shard.shape[1]), None
+def all_units_weight(shard):
+    matrices, _, width = shard.shape
     members = lax.axis_size(MODEL)
-    every = lax.all_gather(shard, ALL, tiled=True).reshape(members, 4, 2, ROWS, shard.shape[1])
-    return every[:, :, 0], every[:, :, 1]
+    every = lax.all_gather(shard, ALL).reshape(members, -1, matrices, shard.shape[1], width).transpose(0, 2, 1, 3, 4)
+    every = every.reshape(members, matrices, 4, 2, ROWS, width)
+    every = jnp.stack([every[slot] for slot in SLOTS])
+    pieces = []
+    for k in range(2):
+        pieces += [jnp.stack([every[:, :, r, k] for r in range(3)]), every[:, :, 3, k]]
+    return pieces
+
+
+class UnitsWeight:
+    def __init__(self, shard):
+        self.shard = shard
+
+    def start_far_z(self):
+        self.other = flip(self.shard, "zh", 1)
+
+    def join_far_z(self, shard):
+        self.two = jnp.stack([shard, self.other])
+
+    def far_z(self):
+        self.start_far_z()
+        self.join_far_z(self.shard)
+
+    def start_z(self):
+        self.other = flip(self.two, "zl", 1)
+
+    def join_z(self, two):
+        self.own = jnp.concatenate([two, self.other])
+
+    def near_z(self):
+        self.start_z()
+        self.join_z(self.two)
+
+    def near(self):
+        self.near_x, self.near_y = flip(self.own, "q", 1), flip(self.own, "q", 2)
+
+    def corner(self):
+        self.far_a, self.far_b = flip(self.near_y[:2], "q", 1), flip(self.near_x[2:], "q", 2)
+
+    def swap_main(self):
+        self.main = jnp.stack([self.own, self.near_x, self.near_y])
+        self.main_sibling = flip(self.main, "c", 1)
+
+    def swap_corner(self):
+        self.far = jnp.concatenate([self.far_a, self.far_b])
+        self.far_sibling = flip(self.far, "c", 1)
+
+    def pieces(self):
+        return [self.main, self.far, self.main_sibling, self.far_sibling]
 
 
 class UnitsGrads:
@@ -1023,17 +1099,18 @@
     return every.transpose(1, 2, 0, 3).reshape(16 // 4, 8, -1)
 
 
-def scatter_small(values_in, where):
-    if not is_small():
-        return lax.psum_scatter(values_in.reshape(-1, values_in.shape[-1]), ALL, scatter_dimension=0, tiled=True)[0]
+def spread_by_distance(values_in, where):
     every = values_in.reshape(4, 4, 2, -1).transpose(1, 0, 2, 3)
     for axis, position in enumerate(where):
         every = order_by(every, axis, position, every.shape[axis])
-    every = every.transpose(2, 1, 0, 3).reshape(32, -1)
-    for axis, mask in SMALL_STEPS[::-1]:
+    return every.transpose(2, 1, 0, 3).reshape(32, -1)
+
+
+def fold_small(every, first, last):
+    for axis, mask in SMALL_STEPS[::-1][first:last]:
         half = every.shape[0] // 2
         every = every[:half] + flip(every[half:], axis, mask)
-    return every[0]
+    return every
 
 
 def sum_all(value):
@@ -1081,23 +1158,29 @@
         head = jnp.concatenate([jnp.ones((1, D), F32), jnp.zeros((1, D), F32)])
         return biases.reshape(layers, tz, 1, -1), jnp.pad(jnp.concatenate([head, table]), ((0, TABLE - 2 - 6 * layers), (0, 0)))
 
-    weights = [(units_weight(up_weight[l]), units_weight(down_weight[l])) for l in range(layers)]
     if small_slice:
         pair = jnp.stack([turn(heads_shard[0]), cross(heads_shard[0])])
         x_low = turn(tokens)
         ends = jnp.cumsum(turn(doc_lengths)[0], dtype=jnp.int32)
-        members = from_members(pair, "q")
+        near = heads_along_x(pair)
         small = small_step(small, 0)
+        up0, down0 = UnitsWeight(up_weight[0][None]), UnitsWeight(down_weight[0][None])
+        both1 = UnitsWeight(jnp.stack([up_weight[1], down_weight[1]]))
         flow.wait(x_low, small)
-        flow.hold(heads1=heads_shard[1], top=cotangent, low=x_low, small=small)
+        flow.hold(
+            up0=up0.shard, down0=down0.shard, down0_twin=down0.shard, both1=both1.shard, heads1=heads_shard[1], top=cotangent,
+            low=x_low, small=small,
+        )
         gate(flow)
-        x_low = flow.free("low")
+        x_low, up0.shard = flow.free("low"), flow.free("up0")
+        up0.far_z()
         small = small_step(flow.free("small"), 1)
-        weights_of = [(members, heads_bias_near(members, bias_size, hz, where, zh))]
+        weights_of = [heads_along_y(near, bias_size, hz, where, zh)]
     else:
         x_low = turn(tokens)
         ends = jnp.cumsum(turn(doc_lengths)[0], dtype=jnp.int32)
         weights_of = [all_heads_weight(shard, bias_size, hz, zh) for shard in heads_shard]
+        every = [all_units_weight(jnp.stack([up_weight[l], down_weight[l]])) for l in range(layers)]
         top_grad = turn(cotangent)
         up_bias_full, table = spread_small(lax.all_gather(small, ALL))
 
@@ -1107,55 +1190,96 @@
         first, last = small_slice and l == 0, small_slice and l == 1
         xs = gather_group(x_low)
         w_heads, bias = weights_of[l]
-        w_up, w_down = weights[l]
         if first:
-            flow.wait(small)
-            flow.hold(small=small)
+            flow.wait(up0.two, small)
+            flow.hold(small=small, two=up0.two, two_twin=up0.two)
+        if last:
+            flow.wait(both1.own)
+            flow.hold(own=both1.own)
         qkv_near = project_in(flow, (xs[0], xs[2]), False, w_heads, in_cols, bias, "project_qkv")
-        flow.wait(qkv_near)
         if first:
+            up0.two, down0.shard = flow.free("two"), flow.free("down0")
+            up0.start_z()
+            down0.start_far_z()
             small = small_step(flow.free("small"), 2)
-            flow.wait(small)
+        if last:
+            both1.own = flow.free("own")
+            both1.near()
+        forward(flow, xs, qkv_near)
+        if first:
             flow.hold(small=small)
         qkv_far = project_in(flow, (xs[1], xs[3]), True, w_heads, in_cols, bias, "project_qkv")
         qkv = (qkv_near, qkv_far)
         if first:
             small = small_step(flow.free("small"), 3)
+            both1.shard = flow.free("both1")
+            down0.join_far_z(flow.free("down0_twin"))
+            up0.join_z(flow.free("two_twin"))
+            up0.near()
+            down0.near_z()
+            both1.far_z()
         if last:
             top_grad = turn(flow.free("top"))
-        if small_slice:
-            flow.hold(up=w_up[0])
         ctx, wide, lse = attend_forward(flow, ends, qkv)
-        if small_slice:
-            mine = flow.free("up")
-            w_up = mine, flip(mine, "c", 1)
         if first:
-            flow.wait(small)
-            flow.hold(small=small)
+            flow.wait(up0.near_x, up0.near_y)
+            flow.hold(small=small, down0=down0.own, both1=both1.two)
+            up0.corner()
+        if last:
+            flow.wait(both1.near_x, both1.near_y, top_grad)
+            flow.hold(own=both1.own)
+            both1.corner()
+        send = project_out(flow, [ctx], (2, 3), w_heads, out_cols, True, "project_attn")
+        flow.wait(send)
+        if first:
             shard = flow.free("heads1")
             pair = jnp.stack([turn(shard), cross(shard)])
         if last:
-            flow.wait(top_grad)
-        if small_slice:
-            flow.hold(down=w_down[0])
-        send = project_out(flow, ctx, (2, 3), w_heads, out_cols, True, "project_attn")
-        flow.wait(send)
-        if small_slice:
-            mine = flow.free("down")
-            w_down = mine, flip(mine, "c", 1)
-        keep = project_out(flow, ctx, (0, 1), w_heads, out_cols, False, "project_attn")
-        attn, _ = sum_group(keep, send)
+            both1.own = flow.free("own")
+            both1.swap_main()
+        keep = project_out(flow, [ctx], (0, 1), w_heads, out_cols, False, "project_attn")
+        attn, passed = sum_group(keep, send)
         if first:
+            flow.wait(passed, up0.far_a, up0.far_b)
+            flow.hold(pair=pair, pair_twin=pair)
+            gate(flow)
+            up0.swap_main()
+            up0.swap_corner()
+            down0.own = flow.free("down0")
+            down0.near()
             up_bias_full, table = spread_small(order_small(small_step(flow.free("small"), 4), where))
-            flow.wait(pair)
+            flow.wait(down0.near_x, down0.near_y)
+            w_up = up0.pieces(), 0
+        elif last:
+            flow.wait(passed)
+            flow.hold(far_a=both1.far_a)
+            flow.wait(attn[2])
+            gate(flow)
+            both1.far_a = flow.free("far_a")
+            both1.swap_corner()
+            w_up, w_down = (both1.pieces(), 0), (both1.pieces(), 1)
+        else:
+            w_up, w_down = (every[l], 0), (every[l], 1)
         used = (prev_gain, prev_shift, shift_row(l, 0), gain_row(l, 0), shift_row(l, 1))
-        n1, hs, r1, act, slope = norm_up(flow, prev, attn, table, used, w_up, up_bias_full[l], tz)
+        n1, hs, r1, act, slope = norm_up(flow, prev, attn, table, used, *w_up, up_bias_full[l], tz)
         if first:
-            members = from_members(pair, "q")
-            weights_of.append((members, heads_bias_near(members, bias_size, hz, where, zh)))
+            down0.corner()
+            down0.swap_main()
+            flow.wait(n1)
+            flow.hold(far_a=down0.far_a)
+            gate(flow)
+            down0.far_a = flow.free("far_a")
+            down0.swap_corner()
+            both1.two, pair = flow.free("both1"), flow.free("pair")
+            both1.near_z()
+            beside = flip(pair, "q", 1)
+            w_down = down0.pieces(), 0
         used = (gain_row(l, 0), shift_row(l, 1), shift_row(l, 2), gain_row(l, 1), shift_row(l, 3))
-        n2, y_low, r2 = down_norm(flow, act, w_down, n1, table, used, tz)
+        n2, y_low, r2 = down_norm(flow, act, *w_down, n1, table, used, tz)
         kept.append((xs, qkv, ctx, wide, lse, n1, hs, r1, act, slope, n2, r2, w_heads, w_up, w_down))
+        if first:
+            near = jnp.stack([flow.free("pair_twin"), beside])
+            weights_of.append(heads_along_y(near, bias_size, hz, where, zh))
         x_low, prev, prev_gain, prev_shift = y_low, n2, gain_row(l, 1), shift_row(l, 3)
     layer_output = turn(x_low)
 
@@ -1167,10 +1291,10 @@
         top = l == layers - 1
         xs, qkv, ctx, wide, lse, n1, hs, r1, act, slope, n2, r2, w_heads, w_up, w_down = kept[l]
         beside = small_slice and not top
-        gu, up_bias_sum = units_back(flow, gf, w_down, slope, tz)
+        gu, up_bias_sum = units_back(flow, gf, *w_down, slope, tz)
         units = UnitsGrads(flow, (gf, act), (hs, gu), tz)
         if top:
-            flow.wait(layer_output)
+            flow.hold(output=layer_output)
         else:
             if beside:
                 flow.wait(*above.near())
@@ -1181,16 +1305,18 @@
                 above_heads.send = flow.free("heads")
                 above_heads.along_x()
                 late = above.far()
-        g1, ga, sums1 = up_back(flow, gu, w_up, g2, n1, r1, table, gain_row(l, 0), tz)
+        g1, ga, sums1 = up_back(flow, gu, *w_up, g2, n1, r1, table, gain_row(l, 0), tz)
         gas = gather_group(ga)
         flow.wait(ga)
         if top:
+            layer_output = flow.free("output")
             units.compute_theirs()
+            forward(flow, gas, units.theirs)
         else:
             units.mine()
-            flow.wait(*units.made)
             if beside:
                 flow.wait(*late, above_heads.got)
+            forward(flow, gas, *units.made)
         gc_near = project_in(flow, (gas[0], gas[2]), False, w_heads, out_cols, None, "project_gc")
         flow.wait(gc_near)
         if top:
@@ -1199,9 +1325,22 @@
         if top:
             units.theirs = flow.free("theirs")
             units.send_theirs()
-        gqkv = attend_backward(flow, ends, qkv, (gc_near, gc_far), wide, lse)
+        gcs = (gc_near, gc_far)
+        if beside:
+            flow.hold(rest_x=units.rest_x, rest_y=units.rest_y)
+        gqkv = [attend_backward(flow, ends, 0, qkv, gcs, wide, lse)]
+        if beside:
+            units.rest_x, units.rest_y = flow.free("rest_x"), flow.free("rest_y")
+        flow.wait(gqkv[0])
         if beside:
             flow.wait(*units.near(), *above.near_z(), above_heads.along_y())
+            above.far_z()
+            units.far()
+            above_halves = above_heads.halves(zh)
+        gqkv.append(attend_backward(flow, ends, 1, qkv, gcs, wide, lse))
+        if beside:
+            flow.wait(units.late_x, units.late_y)
+            units.near_z()
         send = project_out(flow, gqkv, (2, 3), w_heads, in_cols, True, "project_gx")
         flow.wait(send)
         keep = project_out(flow, gqkv, (0, 1), w_heads, in_cols, False, "project_gx")
@@ -1211,11 +1350,11 @@
             units.mine()
             flow.wait(*units.made)
         elif small_slice:
-            flow.hold(there=above.there)
+            flow.hold(h0=above_halves[0], h1=above_halves[1])
         *buckets, qkv_sums = heads_grad(flow, xs, gqkv, gas, ctx)
         heads = HeadsGrad(*buckets)
         units_of[l], heads_of[l] = units, heads
-        qv_sums = qkv_sums.reshape(3, hz, dp, -1)
+        qv_sums = qkv_sums.reshape(-1, 3, PAIR).transpose(1, 0, 2).reshape(3, hz, dp, -1)
         qv_sums = jnp.stack([qv_sums[0], qv_sums[2]]).transpose(2, 0, 1, 3).reshape(1, dp, -1)
         mine = (jnp.arange(tz) == place).astype(F32).reshape(tz, 1, 1)
         small_grads[l] = jnp.concatenate(
@@ -1234,29 +1373,40 @@
             g2, gf, sums2 = sum_norm_back(flow, g1, back, kept[l - 1][10], kept[l - 1][11], table, gain_row(l - 1, 1))
     small_sums = jnp.stack(small_grads, axis=2).reshape(tz, dp, -1)
     if small_slice:
-        units.far()
-        above.there = flow.free("there")
-        above.far_z()
-        flow.hold(late_x=units.late_x, late_y=units.late_y, heads=heads.send)
+        above_halves = flow.free("h0"), flow.free("h1")
+        done = turn(above_halves[0]), uncross(above_halves[1])
+        heads.along_x()
+        flow.wait(units.there)
+        flow.hold(small=small_sums)
         gate(flow)
-        units.late_x, units.late_y, heads.send = flow.free("late_x"), flow.free("late_y"), flow.free("heads")
-        heads.along_x()
-        units.near_z()
-        flow.wait(back[2])
-        flow.hold(small=small_sums, there=units.there, got=heads.got)
+        small_sums = flow.free("small")
+        units.far_z()
+        flow.wait(back[2], *done)
+        flow.hold(small=small_sums, got=heads.got)
         gate(flow)
-        small_sums, units.there, heads.got = flow.free("small"), flow.free("there"), flow.free("got")
+        small_sums, heads.got = flow.free("small"), flow.free("got")
+        input_grad = turn(add(g1, back[0], back[1][0], back[2]).astype(BF16))
         heads.along_y()
-        units.far_z()
-    input_grad = turn(add(g1, back[0], back[1][0], back[2]).astype(BF16))
-    halves = [member.halves(zh) for member in heads_of]
-    d_heads = add(turn(jnp.stack([half[0] for half in halves])), uncross(jnp.stack([half[1] for half in halves])))
-    qkv_grad = d_heads[:, :, : in_cols.stop].reshape(layers, d_heads.shape[1], 3, -1).transpose(0, 2, 1, 3)
+        small_sums = fold_small(spread_by_distance(small_sums, where), 0, 2)
+        flow.wait(heads.got)
+        flow.hold(small=small_sums, grad=input_grad, last=units.last)
+        gate(flow)
+        small_sums, input_grad, units.last = flow.free("small"), flow.free("grad"), flow.free("last")
+        halves = heads.halves(zh)
+        d_heads = jnp.stack([add(turn(halves[0]), uncross(halves[1])), add(*done)])
+        small_out = fold_small(small_sums, 2, 5).reshape(layers, -1)
+    else:
+        halves = [member.halves(zh) for member in heads_of]
+        d_heads = jnp.stack([add(turn(half[0]), uncross(half[1])) for half in halves])
+        input_grad = turn(add(g1, back[0], back[1][0], back[2]).astype(BF16))
+        small_out = lax.psum_scatter(small_sums.reshape(tz * dp, -1), ALL, scatter_dimension=0, tiled=True)
+        small_out = small_out.reshape(layers, -1)
+    qkv_grad = d_heads[:, :, : in_cols.stop].reshape(layers, d_heads.shape[1], -1, 3, PAIR)
+    qkv_grad = qkv_grad.transpose(0, 3, 1, 2, 4).reshape(qkv_weight.shape)
     out_grad = d_heads[:, :, in_cols.stop :]
     totals = [member.total() for member in units_of]
     down_grad, up_grad = (jnp.stack([total[i] for total in totals]) for i in range(2))
 
-    small_out = scatter_small(small_sums, where).reshape(layers, -1)
     rest = small_out[:, bias_size:]
     qv_bias_grad = small_out[:, :bias_size].reshape(qv_bias.shape)
     up_bias_grad = rest[:, cuts[0] : cuts[1]].reshape(up_bias.shape)
@@ -1266,10 +1416,7 @@
     local_squares = sum(jnp.sum(member * member) for member in all_grads)
     entry_count = LAYERS * (4 * D * D + 2 * D * FF + FF + 8 * D)
     if small_slice:
-        flow.wait(input_grad)
-        flow.hold(squares=jnp.broadcast_to(local_squares, (8, 128)))
-        gate(flow)
-        local_squares = flow.free("squares")
+        local_squares = jnp.broadcast_to(local_squares, (8, 128))
     grad_rms = jnp.sqrt(sum_all(local_squares) / entry_count)
     return (
         layer_output, input_grad, qkv_grad, qv_bias_grad, out_grad, up_grad, up_bias_grad, down_grad, gains_grad,

time: 1080 us -> 1070 us (level)
  waiting for transfers between devices: 344 us -> 233 us
  starting transfers between devices: 91.3 us -> 136 us
  other arithmetic: 61.1 us -> 89.6 us
  local copies, waits for them, and re-layouts: 51.4 us -> 78.3 us
  between operations: 22.8 us -> 10.3 us
  Pallas kernels: 501 us -> 512 us
    ppermute x65 -> x83, waiting for transfers between devices: 236 us -> 148 us  [flip(): lax.ppermute(values_in, axes, [(a, a ^ mask) for a in range(lax.axis_size...]
    ppermute x65 -> x83, starting transfers between devices: 53.2 us -> 99.8 us  [flip(): lax.ppermute(values_in, axes, [(a, a ^ mask) for a in range(lax.axis_size...]
    all_gather x4 -> x0, waiting for transfers between devices: 35 us -> none  [units_weight(): lax.all_gather(shard, MODEL + ('q',)).reshape(-1, 4, ROWS, shard.shape[1])]
    another operation x7 -> x17, other arithmetic: 1.57 us -> 25.1 us  [the longest x4 15.2 us: swap_main(): self.main = jnp.stack([self.own, self.near_x, self.near_y])]
    unnamed x163 -> x217, local copies, waits for them, and re-layouts: 23.7 us -> 42.2 us
    pallas_call x40 -> x49, Pallas kernels: 501 us -> 512 us  [call(): pl.pallas_call(wrapped, grid_spec=pltpu.PrefetchScalarGridSpec(num_scalar...]
    ppermute x8 -> x9, waiting for transfers between devices: 71.9 us -> 73.6 us  [turn(): lax.ppermute(values_in, ('c', 'zh'), [(2 * a + b, 2 * b + a) for a in ran...]
    ppermute x8 -> x9, starting transfers between devices: 36.6 us -> 35.7 us  [turn(): lax.ppermute(values_in, ('c', 'zh'), [(2 * a + b, 2 * b + a) for a in ran...]
  transfers between devices with their start and end apart: 80 -> 96, of which waited for: 36 -> 35; matrix products, arithmetic and copies ran while one was open for 9% -> 12% of each run, Pallas kernels for 42% -> 40%
where the time goes in v5:
time: 1070 us; the launch traced here: 1060 us
  Pallas kernels  512 us (48%)
  waiting for transfers between devices  233 us (22%)
  starting transfers between devices  136 us (13%)
  other arithmetic  89.6 us (8%)
  local copies, waits for them, and re-layouts  78.3 us (7%)
    pallas_call x49, Pallas kernels, call(): pl.pallas_call(wrapped, grid_spec=pltpu.PrefetchScalarGridSpec(num_scalar...  512 us
    ppermute x83, waiting for transfers between devices, flip(): lax.ppermute(values_in, axes, [(a, a ^ mask) for a in range(lax.axis_size...  148 us
    ppermute x83, starting transfers between devices, flip(): lax.ppermute(values_in, axes, [(a, a ^ mask) for a in range(lax.axis_size...  99.8 us
    ppermute x9, waiting for transfers between devices, turn(): lax.ppermute(values_in, ('c', 'zh'), [(2 * a + b, 2 * b + a) for a in ran...  73.6 us
    unnamed x217, local copies, waits for them, and re-layouts  42.2 us
    ppermute x9, starting transfers between devices, turn(): lax.ppermute(values_in, ('c', 'zh'), [(2 * a + b, 2 * b + a) for a in ran...  35.7 us
  transfers between devices with their start and end apart: 96, of which 35 were waited for; matrix products, arithmetic and copies ran while one was open for 12% of the time, Pallas kernels for 40%

profile of v5, /device:TPU:1, one launch (start us, length us, event | category | flops | bytes accessed | tf_op | source)
XLA Modules:
  0.0 1058.9 jit_solution(1106262568671672096)
XLA Ops:
  9.2 9.9 collective-permute-done.6
  39.8 10.6 collective-permute-done.refs_1_
  76.6 8.8 collective-permute-done.9.refs_7_
  95.2 10.6 collective-permute-done.15
  121.6 30.6 %attend_forward.2 = (bf16[4,512,256]{2,1,0:T(8,128)(2,1)}, f32[4,512,256]{2,1,0:T(8,128)}, f32[8,8,256]{2,1,0:T(8,128)}, bf16[144,1024]{1,0:T(8,128)(2,1)}, bf16[512,1024]{1,0:T(8,128)(2,1)}) custom-call(s32[5]{0:T(128)} %stack.209.refs_0_, s32[4]{0:T(128)} %bitcast.315, ...), custom_call_target="tpu_custom_call", output_to_operand_aliasing={{3}: (2, {}), {4}: (3, {})} | custom-call | flops 14000000000 | bytes 1024 | tf_op jit(solution)/shard_map/attend_forward/pallas_call | solution.py:80
  198.8 17.9 %collective-permute-done.26 = bf16[4,1,128,1024]{3,2,0,1:T(8,128)(2,1)} collective-permute-done((bf16[4,1,128,1024]{3,2,0,1:T(8,128)(2,1)}, bf16[4,1,128,1024]{3,2,0,1:T(8,128)(2,1)}, u32[]{:S(2)}, u32[]{:S(2)}) %collective-permute-start.26) | collective-permute-done | bytes 1048608 | tf_op jit(solution)/shard_map/ppermute | solution.py:851
  229.5 18.7 %norm_up.2 = (f32[512,1024]{1,0:T(8,128)}, bf16[512,1024]{1,0:T(8,128)(2,1)}, f32[512,128]{1,0:T(8,128)}, bf16[512,4096]{1,0:T(8,128)(2,1)}, bf16[512,4096]{1,0:...) custom-call(s32[5]{0:T(128)} %stack.209.refs_0_, ...), custom_call_target="tpu_custom_call", output_to_operand_aliasing={{5}: (3, {}), {6}: (4, {}), {7}: (5, {}), {8}: (6, {})} | custom-call | flops 7000000000 | bytes 1024 | tf_op jit(solution)/shard_map/norm_up/pallas_call | solution.py:80
  254.9 14.3 %down_norm.2 = (f32[512,1024]{1,0:T(8,128)}, bf16[512,1024]{1,0:T(8,128)(2,1)}, f32[512,128]{1,0:T(8,128)}, bf16[512,1024]{1,0:T(8,128)(2,1)}, bf16[2,144,1024]{2,1,0:T(8,128)(2,1)}) custom-call(s32[5]{0:T(128)} %stack.209.refs_0_, bf16[512,1024]{1,0:T(8,128)(2,1)} %get-tuple-element.212.refs_1_, ...), custom_call_target="tpu_custom_call", output_to_operand_aliasing={{3}: (1, {}), {4}: (2, {})} | custom-call | flops 7000000000 | bytes 1024 | tf_op jit(solution)/shard_map/down_norm/pallas_call | solution.py:80
  281.2 16.5 %collective-permute-done.38.refs_8_.refs_6_.refs_7_.refs_4_.refs_5_ = bf16[2,2,144,1024]{3,2,1,0:T(8,128)(2,1)S(1)} collective-permute-done((bf16[2,2,144,1024]{3,2,1,0:T(8,128)(2,1)S(1)}, bf16[2,2,144,1024]{3,2,1,0:T(8,128)(2,1)S(1)}, u32[]{:S(2)}, u32[]{:S(2)}) %collective-permute-start.38) | collective-permute-done | bytes 1179680 | tf_op jit(solution)/shard_map/ppermute | solution.py:851
  327.9 30.4 %attend_forward.3 = (bf16[4,512,256]{2,1,0:T(8,128)(2,1)}, f32[4,512,256]{2,1,0:T(8,128)}, f32[8,8,256]{2,1,0:T(8,128)}) custom-call(s32[5]{0:T(128)} %stack.209.refs_0_, s32[4]{0:T(128)} %bitcast.316, bf16[2,512,768]{2,1,0:T(8,128)(2,1)} %get-tuple-element.223.refs_1_.refs_2_.refs_3_, bf16[2,512,768]{2,1,0:T(8,128)(2,1)} %get-tuple-element.228.refs_3_.refs_4_), custom_call_target="tpu_custom_call" | custom-call | flops 14000000000 | bytes 1024 | tf_op jit(solution)/shard_map/attend_forward/pallas_call | solution.py:80
  390.5 8.1 collective-permute-done.46.refs_3_
  398.6 15.0 %collective-permute-done.45.refs_2_.refs_4_ = bf16[512,1024]{1,0:T(8,128)(2,1)S(1)} collective-permute-done((bf16[512,1024]{1,0:T(8,128)(2,1)S(1)}, bf16[512,1024]{1,0:T(8,128)(2,1)S(1)}, u32[]{:S(2)}, u32[]{:S(2)}) %collective-permute-start.45) | collective-permute-done | bytes 1048608 | tf_op jit(solution)/shard_map/ppermute | solution.py:851
  421.7 18.9 %norm_up.3 = (f32[512,1024]{1,0:T(8,128)}, bf16[512,1024]{1,0:T(8,128)(2,1)}, f32[512,128]{1,0:T(8,128)}, bf16[512,4096]{1,0:T(8,128)(2,1)}, bf16[512,4096]{1,0:T(8,128)(2,1)}) custom-call(s32[5]{0:T(128)} %stack.209.refs_0_, f32[512,1024]{1,0:T(8,128)} %get-tuple-element.216.refs_1_.refs_6_, bf16[512,1024]{1,0:T(8,128)(2,1)} %get-tuple-element.231.refs_2_, ...), custom_call_target="tpu_custom_call" | custom-call | flops 7000000000 | bytes 1024 | tf_op jit(solution)/shard_map/norm_up/pallas_call | solution.py:80
  440.6 14.4 %down_norm.3 = (f32[512,1024]{1,0:T(8,128)}, bf16[512,1024]{1,0:T(8,128)(2,1)}, f32[512,128]{1,0:T(8,128)}) custom-call(s32[5]{0:T(128)} %stack.209.refs_0_, bf16[512,4096]{1,0:T(8,128)(2,1)} %get-tuple-element.234.refs_1_.refs_3_, f32[512,1024]{1,0:T(8,128)} %get-tuple-element.235.refs_2_.refs_4_, ...), custom_call_target="tpu_custom_call" | custom-call | flops 7000000000 | bytes 1024 | tf_op jit(solution)/shard_map/down_norm/pallas_call | solution.py:80
  466.2 11.5 %units_back.2 = (bf16[512,4096]{1,0:T(8,128)(2,1)}, f32[4,1,1024]{2,1,0:T(1,128)}) custom-call(s32[5]{0:T(128)} %stack.209.refs_0_, bf16[512,1024]{1,0:T(8,128)(2,1)} %get-tuple-element.239.refs_1_.refs_2_, bf16[512,4096]{1,0:T(8,128)(2,1)} %get-tuple-element.240.refs_2_, bf16[3,4,2,128,1024]{4,3,2,1,0:T(8,128)(2,1)} %pad_maximum_fusion.refs_7_.refs_4_.refs_3_, ...), custom_call_target="tpu_custom_call" | custom-call | flops 7000000000 | bytes 1024 | tf_op jit(solution)/shard_map/units_back/pallas_call | solution.py:80
  484.9 14.9 %up_back.2 = (f32[512,1024]{1,0:T(8,128)}, bf16[512,1024]{1,0:T(8,128)(2,1)}, f32[8,1024]{1,0:T(8,128)}, bf16[512,1024]{1,0:T(8,128)(2,1)}) custom-call(s32[5]{0:T(128)} %stack.209.refs_0_, bf16[512,1024]{1,0:T(8,128)(2,1)} %copy-done.43, bf16[512,4096]{1,0:T(8,128)(2,1)} %get-tuple-element.241.refs_2_.refs_5_, ...), custom_call_target="tpu_custom_call", output_to_operand_aliasing={{3}: (1, {})} | custom-call | flops 7000000000 | bytes 1024 | tf_op jit(solution)/shard_map/up_back/pallas_call | solution.py:80
  500.4 12.7 %grads_theirs.2.refs_1_.refs_2_ = bf16[4,8,128,1024]{3,2,1,0:T(8,128)(2,1)} custom-call(s32[5]{0:T(128)} %stack.209.refs_0_, bf16[512,1024]{1,0:T(8,128)(2,1)} %get-tuple-element.245.refs_1_.refs_10_, bf16[512,1024]{1,0:T(8,128)(2,1)} %get-tuple-element.239.refs_1_.refs_2_, bf16[512,4096]{1,0:T(8,128)(2,1)} %get-tuple-element.234.refs_1_.refs_3_, ...), custom_call_target="tpu_custom_call" | custom-call | flops 70000000 | bytes 1024 | tf_op jit(solution)/shard_map/grads_theirs/pallas_call | solution.py:80
  530.8 32.7 %attend_backward.4.refs_2_.refs_1_.refs_14_ = bf16[4,512,384]{2,1,0:T(8,128)(2,1)} custom-call(s32[5]{0:T(128)} %stack.209.refs_0_, s32[4]{0:T(128)} %bitcast.317, bf16[2,512,768]{2,1,0:T(8,128)(2,1)} %get-tuple-element.223.refs_1_.refs_2_.refs_3_, bf16[2,512,768]{2,1,0:T(8,128)(2,1)} %get-tuple-element.228.refs_3_.refs_4_, ...), custom_call_target="tpu_custom_call" | custom-call | flops 10499999744 | bytes 1024 | tf_op jit(solution)/shard_map/attend_backward/pallas_call | solution.py:80
  563.5 33.0 %attend_backward.5.refs_2_.refs_3_.refs_15_ = bf16[4,512,384]{2,1,0:T(8,128)(2,1)} custom-call(s32[5]{0:T(128)} %stack.209.refs_0_, s32[4]{0:T(128)} %bitcast.318, bf16[4,512,384]{2,1,0:T(8,128)(2,1)} %attend_backward.4.refs_2_.refs_1_.refs_14_, bf16[2,512,768]{2,1,0:T(8,128)(2,1)} %get-tuple-element.223.refs_1_.refs_2_.refs_3_, ...), custom_call_target="tpu_custom_call" | custom-call | flops 10499999744 | bytes 1024 | tf_op jit(solution)/shard_map/attend_backward/pallas_call | solution.py:80
  614.6 15.8 %grads_mine.2 = (bf16[8,128,1024]{2,1,0:T(8,128)(2,1)}, bf16[8,128,1024]{2,1,0:T(8,128)(2,1)}, bf16[8,128,1024]{2,1,0:T(8,128)(2,1)}, bf16[4,128,1024]{2,1,0:T(8,128)(2,1)}, bf16[4,128,1024]{2,1,0:T(8,128)(2,1)}) custom-call(s32[5]{0:T(128)} %stack.209.refs_0_, bf16[512,1024]{1,0:T(8,128)(2,1)} %copy-done.41, ...), custom_call_target="tpu_custom_call" | custom-call | flops 70000000 | bytes 1024 | tf_op jit(solution)/shard_map/grads_mine/pallas_call | solution.py:80
  634.9 13.1 %heads_grad.2 = (bf16[2,2,128,1024]{3,2,1,0:T(8,128)(2,1)}, bf16[2,2,128,1024]{3,2,1,0:T(8,128)(2,1)}, f32[1,768]{1,0:T(1,128)}) custom-call(s32[5]{0:T(128)} %stack.209.refs_0_, bf16[8,128,1024]{2,1,0:T(8,128)(2,1)} %get-tuple-element.254.refs_1_, bf16[8,128,1024]{2,1,0:T(8,128)(2,1)} %get-tuple-element.252.refs_2_, ...), custom_call_target="tpu_custom_call" | custom-call | flops 70000000 | bytes 1024 | tf_op jit(solution)/shard_map/heads_grad/pallas_call | solution.py:80
  655.8 11.4 %units_back.3 = (bf16[512,4096]{1,0:T(8,128)(2,1)}, f32[4,1,1024]{2,1,0:T(1,128)}) custom-call(s32[5]{0:T(128)} %stack.209.refs_0_, bf16[512,1024]{1,0:T(8,128)(2,1)} %get-tuple-element.261.refs_1_.refs_4_.refs_2_, bf16[512,4096]{1,0:T(8,128)(2,1)} %get-tuple-element.263.refs_2_, bf16[3,4,1,128,1024]{4,3,2,1,0:T(8,128)(2,1)} %get-tuple-element.349.refs_6_.refs_3_, ...), custom_call_target="tpu_custom_call" | custom-call | flops 7000000000 | bytes 1024 | tf_op jit(solution)/shard_map/units_back/pallas_call | solution.py:80
  667.2 9.8 collective-permute-done.56.refs_1_
  682.0 12.8 %grads_theirs.3 = (bf16[4,8,128,1024]{3,2,1,0:T(8,128)(2,1)}, bf16[2,2,128,1024]{3,2,1,0:T(8,128)(2,1)}) custom-call(s32[5]{0:T(128)} %stack.209.refs_0_, bf16[8,128,1024]{2,1,0:T(8,128)(2,1)} %copy-done.21, bf16[8,128,1024]{2,1,0:T(8,128)(2,1)} %copy-done.23, ...), custom_call_target="tpu_custom_call", output_to_operand_aliasing={{1}: (3, {})} | custom-call | flops 70000000 | bytes 1024 | tf_op jit(solution)/shard_map/grads_theirs/pallas_call | solution.py:80
  702.9 15.3 %up_back.3 = (f32[512,1024]{1,0:T(8,128)}, bf16[512,1024]{1,0:T(8,128)(2,1)}, f32[8,1024]{1,0:T(8,128)}) custom-call(s32[5]{0:T(128)} %stack.209.refs_0_, bf16[4,8,128,1024]{3,2,1,0:T(8,128)(2,1)} %get-tuple-element.265.refs_1_, bf16[512,4096]{1,0:T(8,128)(2,1)} %get-tuple-element.264.refs_7_.refs_2_.refs_5_, f32[512,1024]{1,0:T(8,128)} %get-tuple-element.266.refs_3_, ...), custom_call_target="tpu_custom_call" | custom-call | flops 7000000000 | bytes 1024 | tf_op jit(solution)/shard_map/up_back/pallas_call | solution.py:80
  725.1 15.8 %grads_mine.3 = (bf16[8,128,1024]{2,1,0:T(8,128)(2,1)}, bf16[8,128,1024]{2,1,0:T(8,128)(2,1)}, bf16[8,128,1024]{2,1,0:T(8,128)(2,1)}, bf16[4,128,1024]{2,1,0:T(8,128)(2,1)}, bf16[4,128,1024]{2,1,0:T(8,128)(2,1)}) custom-call(s32[5]{0:T(128)} %stack.209.refs_0_, bf16[512,1024]{1,0:T(8,128)(2,1)} %get-tuple-element.268.refs_1_.refs_8_, ...), custom_call_target="tpu_custom_call" | custom-call | flops 70000000 | bytes 1024 | tf_op jit(solution)/shard_map/grads_mine/pallas_call | solution.py:80
  774.7 32.7 %attend_backward.6 = (bf16[4,512,384]{2,1,0:T(8,128)(2,1)}, bf16[4,128,1024]{2,1,0:T(8,128)(2,1)}, bf16[4,128,1024]{2,1,0:T(8,128)(2,1)}) custom-call(s32[5]{0:T(128)} %stack.209.refs_0_, s32[4]{0:T(128)} %bitcast.319, bf16[4,128,1024]{2,1,0:T(8,128)(2,1)} %get-tuple-element.269.refs_7_.refs_2_, ...), custom_call_target="tpu_custom_call", output_to_operand_aliasing={{1}: (2, {}), {2}: (3, {})} | custom-call | flops 10499999744 | bytes 1024 | tf_op jit(solution)/shard_map/attend_backward/pallas_call | solution.py:80
  816.9 33.0 %attend_backward.7.refs_4_.refs_3_.refs_13_ = bf16[4,512,384]{2,1,0:T(8,128)(2,1)} custom-call(s32[5]{0:T(128)} %stack.209.refs_0_, s32[4]{0:T(128)} %bitcast.320, bf16[4,512,384]{2,1,0:T(8,128)(2,1)} %get-tuple-element.279.refs_2_.refs_3_.refs_12_, bf16[8,128,1024]{2,1,0:T(8,128)(2,1)} %collective-permute-done.68.refs_3_, ...), custom_call_target="tpu_custom_call" | custom-call | flops 10499999744 | bytes 1024 | tf_op jit(solution)/shard_map/attend_backward/pallas_call | solution.py:80
  872.9 18.5 %collective-permute-done.88 = bf16[2,128,1024]{2,1,0:T(8,128)(2,1)S(1)} collective-permute-done((bf16[2,128,1024]{2,1,0:T(8,128)(2,1)S(1)}, bf16[2,128,1024]{2,1,0:T(8,128)(2,1)S(1)}, u32[]{:S(2)}, u32[]{:S(2)}) %collective-permute-start.88) | collective-permute-done | bytes 524320 | tf_op jit(solution)/shard_map/ppermute | solution.py:851
  904.0 12.9 %heads_grad.3 = (bf16[2,2,128,1024]{3,2,1,0:T(8,128)(2,1)}, bf16[2,2,128,1024]{3,2,1,0:T(8,128)(2,1)}, f32[1,768]{1,0:T(1,128)}, bf16[128,1024]{1,0:T(8,128)(2,1)}, bf16[128,1024]{1,0:T(8,128)(2,1)}) custom-call(s32[5]{0:T(128)} %stack.209.refs_0_, bf16[512,1024]{1,0:T(8,128)(2,1)} %fusion.2.refs_1_, ...), custom_call_target="tpu_custom_call", output_to_operand_aliasing={{3}: (2, {}), {4}: (3, {})} | custom-call | flops 70000000 | bytes 1024 | tf_op jit(solution)/shard_map/heads_grad/pallas_call | solution.py:80
  929.5 26.1 %collective-permute-done.74.refs_2_ = bf16[128,1024]{1,0:T(8,128)(2,1)S(1)} collective-permute-done((bf16[128,1024]{1,0:T(8,128)(2,1)}, bf16[128,1024]{1,0:T(8,128)(2,1)S(1)}, u32[]{:S(2)}, u32[]{:S(2)}) %collective-permute-start.74) | collective-permute-done | bytes 262176 | tf_op jit(solution)/shard_map/ppermute | solution.py:855
  987.9 18.9 %collective-permute-done.83 = bf16[128,1024]{1,0:T(8,128)(2,1)S(1)} collective-permute-done((bf16[128,1024]{1,0:T(8,128)(2,1)S(1)}, bf16[128,1024]{1,0:T(8,128)(2,1)S(1)}, u32[]{:S(2)}, u32[]{:S(2)}) %collective-permute-start.83) | collective-permute-done | bytes 262176 | tf_op jit(solution)/shard_map/ppermute | solution.py:855
  (655 shorter events, 482.9 us)
Async XLA Ops:
  30.7 38.1 %collective-permute-start.8 = (bf16[2,2,144,1024]{3,2,1,0:T(8,128)(2,1)S(1)}, bf16[2,2,144,1024]{3,2,1,0:T(8,128)(2,1)S(1)}, u32[]{:S(2)}, u32[]{:S(2)}) collective-permute-start(bf16[2,2,144,1024]{3,2,1,0:T(8,128)(2,1)S(1)} %pad_maximum_fusion.5.refs_14_.refs_10_.refs_9_.refs_7_.refs_3_.refs_4_.refs_5_), channel_id=1, source_target_pairs={{0,16},{8,24},{16,0},{24,8},{1,17},{9,25},{17,1},{25,9},{2,18},{10... | collective-permute-start | bytes 3538952 | tf_op jit(solution)/shard_map/ppermute | solution.py:851
  116.1 36.1 %collective-permute-start.16 = (bf16[8,640]{1,0:T(8,128)(2,1)}, bf16[8,640]{1,0:T(8,128)(2,1)S(1)}, u32[]{:S(2)}, u32[]{:S(2)}) collective-permute-start(bf16[8,640]{1,0:T(8,128)(2,1)} %get-tuple-element.184), channel_id=1, source_target_pairs={{0,2},{2,0},{1,3},{3,1},{4,6},{6,4},{5,7},{7,5},{8,10},{10,8},{9,1... | collective-permute-start | bytes 30728 | tf_op jit(solution)/shard_map/ppermute | solution.py:851
  117.2 37.7 %collective-permute-start.18 = (bf16[2,1,128,1024]{3,2,1,0:T(8,128)(2,1)S(1)}, bf16[2,1,128,1024]{3,2,1,0:T(8,128)(2,1)S(1)}, u32[]{:S(2)}, u32[]{:S(2)}) collective-permute-start(bf16[2,1,128,1024]{3,2,1,0:T(8,128)(2,1)S(1)} %pad_maximum_fusion.17), channel_id=1, source_target_pairs={{0,1},{1,0},{2,3},{3,2},{4,5},{5,4},{6,7},{7,6},{8,9},{9,8},{10,11... | collective-permute-start | bytes 1572872 | tf_op jit(solution)/shard_map/ppermute | solution.py:851
  117.2 35.5 %collective-permute-start.19 = (bf16[2,128,1024]{2,1,0:T(8,128)(2,1)}, bf16[2,128,1024]{2,1,0:T(8,128)(2,1)}, u32[]{:S(2)}, u32[]{:S(2)}) collective-permute-start(bf16[2,128,1024]{2,1,0:T(8,128)(2,1)} %get-tuple-element.187), channel_id=1, source_target_pairs={{0,2},{2,0},{1,3},{3,1},{4,6},{6,4},{5,7},{7,5},{8,10},{10,8},{9,1... | collective-permute-start | bytes 1572872 | tf_op jit(solution)/shard_map/ppermute | solution.py:851
  121.1 34.9 %collective-permute-start.13 = (bf16[4,1,128,1024]{3,2,1,0:T(8,128)(2,1)S(1)}, bf16[4,1,128,1024]{3,2,1,0:T(8,128)(2,1)S(1)}, u32[]{:S(2)}, u32[]{:S(2)}) collective-permute-start(bf16[4,1,128,1024]{3,2,1,0:T(8,128)(2,1)S(1)} %get-tuple-element.361), channel_id=1, source_target_pairs={{0,8},{8,0},{16,24},{24,16},{1,9},{9,1},{17,25},{25,17},{2,10},{10... | collective-permute-start | bytes 3145736 | tf_op jit(solution)/shard_map/ppermute | solution.py:851
  121.4 34.6 %collective-permute-start.14 = (bf16[4,1,128,1024]{3,2,0,1:T(8,128)(2,1)S(1)}, bf16[4,1,128,1024]{3,2,0,1:T(8,128)(2,1)S(1)}, u32[]{:S(2)}, u32[]{:S(2)}) collective-permute-start(bf16[4,1,128,1024]{3,2,0,1:T(8,128)(2,1)S(1)} %get-tuple-element.362), channel_id=1, source_target_pairs={{0,16},{8,24},{16,0},{24,8},{1,17},{9,25},{17,1},{25,9},{2,18},{10... | collective-permute-start | bytes 3145736 | tf_op jit(solution)/shard_map/ppermute | solution.py:851
  179.0 50.5 %collective-permute-start.29 = (bf16[3,4,1,128,1024]{4,3,1,2,0:T(8,128)(2,1)}, bf16[3,4,1,128,1024]{4,3,1,2,0:T(8,128)(2,1)}, u32[]{:S(2)}, u32[]{:S(2)}) collective-permute-start(bf16[3,4,1,128,1024]{4,3,1,2,0:T(8,128)(2,1)} %get-tuple-element.350), channel_id=1, source_target_pairs={{0,4},{4,0},{1,5},{5,1},{2,6},{6,2},{3,7},{7,3},{8,12},{12,8},{9,1... | collective-permute-start | bytes 9437192 | tf_op jit(solution)/shard_map/ppermute | solution.py:851
  196.3 33.2 %collective-permute-start.27 = (bf16[512,1024]{1,0:T(8,128)(2,1)S(1)}, bf16[512,1024]{1,0:T(8,128)(2,1)}, u32[]{:S(2)}, u32[]{:S(2)}) collective-permute-start(bf16[512,1024]{1,0:T(8,128)(2,1)S(1)} %copy-done.46), channel_id=1, source_target_pairs={{0,1},{1,0},{4,5},{5,4},{2,3},{3,2},{6,7},{7,6},{8,9},{9,8},{12,13... | collective-permute-start | bytes 3145736 | tf_op jit(solution)/shard_map/ppermute | solution.py:851
  221.0 32.9 %collective-permute-start.33 = (bf16[3,4,1,128,1024]{4,3,1,2,0:T(8,128)(2,1)}, bf16[3,4,1,128,1024]{4,3,1,2,0:T(8,128)(2,1)}, u32[]{:S(2)}, u32[]{:S(2)}) collective-permute-start(bf16[3,4,1,128,1024]{4,3,1,2,0:T(8,128)(2,1)} %get-tuple-element.348), channel_id=1, source_target_pairs={{0,4},{4,0},{1,5},{5,1},{2,6},{6,2},{3,7},{7,3},{8,12},{12,8},{9,1... | collective-permute-start | bytes 9437192 | tf_op jit(solution)/shard_map/ppermute | solution.py:851
  313.0 47.0 %collective-permute-start.40 = (bf16[4,2,128,1024]{3,2,1,0:T(8,128)(2,1)S(1)}, bf16[4,2,128,1024]{3,2,1,0:T(8,128)(2,1)S(1)}, u32[]{:S(2)}, u32[]{:S(2)}) collective-permute-start(bf16[4,2,128,1024]{3,2,1,0:T(8,128)(2,1)S(1)} %copy-done.5), channel_id=1, source_target_pairs={{0,16},{8,24},{16,0},{24,8},{1,17},{9,25},{17,1},{25,9},{2,18},{10... | collective-permute-start | bytes 6291464 | tf_op jit(solution)/shard_map/ppermute | solution.py:851
  313.1 47.0 %collective-permute-start.39 = (bf16[4,2,128,1024]{3,2,1,0:T(8,128)(2,1)S(1)}, bf16[4,2,128,1024]{3,2,1,0:T(8,128)(2,1)S(1)}, u32[]{:S(2)}, u32[]{:S(2)}) collective-permute-start(bf16[4,2,128,1024]{3,2,1,0:T(8,128)(2,1)S(1)} %copy-done.5), channel_id=1, source_target_pairs={{0,8},{8,0},{16,24},{24,16},{1,9},{9,1},{17,25},{25,17},{2,10},{10... | collective-permute-start | bytes 6291464 | tf_op jit(solution)/shard_map/ppermute | solution.py:851
  323.6 34.7 %collective-permute-start.43 = (bf16[512,1024]{1,0:T(8,128)(2,1)}, bf16[512,1024]{1,0:T(8,128)(2,1)S(1)}, u32[]{:S(2)}, u32[]{:S(2)}) collective-permute-start(bf16[512,1024]{1,0:T(8,128)(2,1)} %get-tuple-element.227), channel_id=1, source_target_pairs={{0,0},{2,4},{4,2},{6,6},{1,1},{3,5},{5,3},{7,7},{8,8},{10,12},{12,... | collective-permute-start | bytes 3145736 | tf_op jit(solution)/shard_map/ppermute | solution.py:855
  373.2 48.5 %collective-permute-start.48 = (bf16[3,4,2,128,1024]{4,3,2,1,0:T(8,128)(2,1)}, bf16[3,4,2,128,1024]{4,3,2,1,0:T(8,128)(2,1)}, u32[]{:S(2)}, u32[]{:S(2)}) collective-permute-start(bf16[3,4,2,128,1024]{4,3,2,1,0:T(8,128)(2,1)} %pad_maximum_fusion.refs_7_.refs_4_.refs_3_), channel_id=1, source_target_pairs={{0,4},{4,0},{1,5},{5,1},{2,6},{6,2},{3,7},{7,3},{8,12},{12,8},{9,1... | collective-permute-start | bytes 18874376 | tf_op jit(solution)/shard_map/ppermute | solution.py:851
  530.3 84.4 %collective-permute-start.55 = (bf16[4,8,128,1024]{3,2,1,0:T(8,128)(2,1)}, bf16[4,8,128,1024]{3,2,1,0:T(8,128)(2,1)}, u32[]{:S(2)}, u32[]{:S(2)}) collective-permute-start(bf16[4,8,128,1024]{3,2,1,0:T(8,128)(2,1)} %get-tuple-element.251), channel_id=1, source_target_pairs={{0,4},{4,0},{1,5},{5,1},{2,6},{6,2},{3,7},{7,3},{8,12},{12,8},{9,1... | collective-permute-start | bytes 25165832 | tf_op jit(solution)/shard_map/ppermute | solution.py:851
  613.3 34.7 %collective-permute-start.58 = (bf16[512,1024]{1,0:T(8,128)(2,1)S(1)}, bf16[512,1024]{1,0:T(8,128)(2,1)}, u32[]{:S(2)}, u32[]{:S(2)}) collective-permute-start(bf16[512,1024]{1,0:T(8,128)(2,1)S(1)} %fusion.3.refs_1_), channel_id=1, source_target_pairs={{0,1},{1,0},{4,5},{5,4},{2,3},{3,2},{6,7},{7,6},{8,9},{9,8},{12,13... | collective-permute-start | bytes 3145736 | tf_op jit(solution)/shard_map/ppermute | solution.py:851
  630.4 46.6 %collective-permute-start.56 = (bf16[8,128,1024]{2,1,0:T(8,128)(2,1)}, bf16[8,128,1024]{2,1,0:T(8,128)(2,1)S(1)}, u32[]{:S(2)}, u32[]{:S(2)}) collective-permute-start(bf16[8,128,1024]{2,1,0:T(8,128)(2,1)} %get-tuple-element.252.refs_2_), channel_id=1, source_target_pairs={{0,8},{8,0},{16,24},{24,16},{1,9},{9,1},{17,25},{25,17},{2,10},{10... | collective-permute-start | bytes 6291464 | tf_op jit(solution)/shard_map/ppermute | solution.py:851
  630.6 50.1 %collective-permute-start.57 = (bf16[8,128,1024]{2,1,0:T(8,128)(2,1)}, bf16[8,128,1024]{2,1,0:T(8,128)(2,1)S(1)}, u32[]{:S(2)}, u32[]{:S(2)}) collective-permute-start(bf16[8,128,1024]{2,1,0:T(8,128)(2,1)} %get-tuple-element.253.refs_3_), channel_id=1, source_target_pairs={{0,16},{8,24},{16,0},{24,8},{1,17},{9,25},{17,1},{25,9},{2,18},{10... | collective-permute-start | bytes 6291464 | tf_op jit(solution)/shard_map/ppermute | solution.py:851
  698.6 42.4 %collective-permute-start.62 = (bf16[4,128,1024]{2,1,0:T(8,128)(2,1)}, bf16[4,128,1024]{2,1,0:T(8,128)(2,1)S(1)}, u32[]{:S(2)}, u32[]{:S(2)}) collective-permute-start(bf16[4,128,1024]{2,1,0:T(8,128)(2,1)} %add_convert_fusion.4), channel_id=1, source_target_pairs={{0,16},{8,24},{16,0},{24,8},{1,17},{9,25},{17,1},{25,9},{2,18},{10... | collective-permute-start | bytes 3145736 | tf_op jit(solution)/shard_map/ppermute | solution.py:851
  702.1 39.7 %collective-permute-start.61 = (bf16[4,128,1024]{2,1,0:T(8,128)(2,1)}, bf16[4,128,1024]{2,1,0:T(8,128)(2,1)S(1)}, u32[]{:S(2)}, u32[]{:S(2)}) collective-permute-start(bf16[4,128,1024]{2,1,0:T(8,128)(2,1)} %add_convert_fusion.5), channel_id=1, source_target_pairs={{0,8},{8,0},{16,24},{24,16},{1,9},{9,1},{17,25},{25,17},{2,10},{10... | collective-permute-start | bytes 3145736 | tf_op jit(solution)/shard_map/ppermute | solution.py:851
  723.8 38.5 %collective-permute-start.60 = (bf16[512,1024]{1,0:T(8,128)(2,1)}, bf16[512,1024]{1,0:T(8,128)(2,1)}, u32[]{:S(2)}, u32[]{:S(2)}) collective-permute-start(bf16[512,1024]{1,0:T(8,128)(2,1)} %get-tuple-element.268.refs_1_.refs_8_), channel_id=1, source_target_pairs={{0,4},{1,5},{4,0},{5,1},{2,6},{3,7},{6,2},{7,3},{8,12},{9,13},{12,... | collective-permute-start | bytes 3145736 | tf_op jit(solution)/shard_map/ppermute | solution.py:851
  740.9 66.5 %collective-permute-start.68 = (bf16[8,128,1024]{2,1,0:T(8,128)(2,1)}, bf16[8,128,1024]{2,1,0:T(8,128)(2,1)}, u32[]{:S(2)}, u32[]{:S(2)}) collective-permute-start(bf16[8,128,1024]{2,1,0:T(8,128)(2,1)} %get-tuple-element.273.refs_5_), channel_id=1, source_target_pairs={{0,8},{8,0},{16,24},{24,16},{1,9},{9,1},{17,25},{25,17},{2,10},{10... | collective-permute-start | bytes 6291464 | tf_op jit(solution)/shard_map/ppermute | solution.py:851
  753.7 57.9 %collective-permute-start.66 = (bf16[8,128,1024]{2,1,0:T(8,128)(2,1)}, bf16[8,128,1024]{2,1,0:T(8,128)(2,1)}, u32[]{:S(2)}, u32[]{:S(2)}) collective-permute-start(bf16[8,128,1024]{2,1,0:T(8,128)(2,1)} %get-tuple-element.274.refs_6_), channel_id=1, source_target_pairs={{0,16},{8,24},{16,0},{24,8},{1,17},{9,25},{17,1},{25,9},{2,18},{10... | collective-permute-start | bytes 6291464 | tf_op jit(solution)/shard_map/ppermute | solution.py:851
  759.7 57.2 %collective-permute-start.70 = (bf16[4,128,1024]{2,1,0:T(8,128)(2,1)}, bf16[4,128,1024]{2,1,0:T(8,128)(2,1)}, u32[]{:S(2)}, u32[]{:S(2)}) collective-permute-start(bf16[4,128,1024]{2,1,0:T(8,128)(2,1)} %get-tuple-element.353), channel_id=1, source_target_pairs={{0,1},{1,0},{2,3},{3,2},{4,5},{5,4},{6,7},{7,6},{8,9},{9,8},{10,11... | collective-permute-start | bytes 3145736 | tf_op jit(solution)/shard_map/ppermute | solution.py:851
  762.2 54.7 %collective-permute-start.71 = (bf16[2,128,1024]{2,1,0:T(8,128)(2,1)}, bf16[2,128,1024]{2,1,0:T(8,128)(2,1)}, u32[]{:S(2)}, u32[]{:S(2)}) collective-permute-start(bf16[2,128,1024]{2,1,0:T(8,128)(2,1)} %fusion.15), channel_id=1, source_target_pairs={{0,16},{8,24},{16,0},{24,8},{1,17},{9,25},{17,1},{25,9},{2,18},{10... | collective-permute-start | bytes 1572872 | tf_op jit(solution)/shard_map/ppermute | solution.py:851
  809.5 40.5 %collective-permute-start.69 = (bf16[4,128,1024]{2,1,0:T(8,128)(2,1)S(1)}, bf16[4,128,1024]{2,1,0:T(8,128)(2,1)S(1)}, u32[]{:S(2)}, u32[]{:S(2)}) collective-permute-start(bf16[4,128,1024]{2,1,0:T(8,128)(2,1)S(1)} %add_convert_fusion.2), channel_id=1, source_target_pairs={{0,16},{8,24},{16,0},{24,8},{1,17},{9,25},{17,1},{25,9},{2,18},{10... | collective-permute-start | bytes 3145736 | tf_op jit(solution)/shard_map/ppermute | solution.py:851
  814.2 35.7 %collective-permute-start.67 = (bf16[4,128,1024]{2,1,0:T(8,128)(2,1)}, bf16[4,128,1024]{2,1,0:T(8,128)(2,1)S(1)}, u32[]{:S(2)}, u32[]{:S(2)}) collective-permute-start(bf16[4,128,1024]{2,1,0:T(8,128)(2,1)} %add_convert_fusion.3), channel_id=1, source_target_pairs={{0,8},{8,0},{16,24},{24,16},{1,9},{9,1},{17,25},{25,17},{2,10},{10... | collective-permute-start | bytes 3145736 | tf_op jit(solution)/shard_map/ppermute | solution.py:851
  858.8 42.3 %collective-permute-start.72 = (bf16[2,512,1024]{2,1,0:T(8,128)(2,1)}, bf16[2,512,1024]{2,1,0:T(8,128)(2,1)}, u32[]{:S(2)}, u32[]{:S(2)}) collective-permute-start(bf16[2,512,1024]{2,1,0:T(8,128)(2,1)} %project_gx.6.refs_1_), channel_id=1, source_target_pairs={{0,4},{1,5},{4,0},{5,1},{2,6},{3,7},{6,2},{7,3},{8,12},{9,13},{12,... | collective-permute-start | bytes 6291464 | tf_op jit(solution)/shard_map/ppermute | solution.py:851
  871.5 47.4 %collective-permute-start.76 = (bf16[4,128,1024]{2,1,0:T(8,128)(2,1)S(1)}, bf16[4,128,1024]{2,1,0:T(8,128)(2,1)S(1)}, u32[]{:S(2)}, u32[]{:S(2)}) collective-permute-start(bf16[4,128,1024]{2,1,0:T(8,128)(2,1)S(1)} %get-tuple-element.355), channel_id=1, source_target_pairs={{0,1},{1,0},{2,3},{3,2},{4,5},{5,4},{6,7},{7,6},{8,9},{9,8},{10,11... | collective-permute-start | bytes 3145736 | tf_op jit(solution)/shard_map/ppermute | solution.py:851
  904.0 51.6 %collective-permute-start.73 = (bf16[512,1024]{1,0:T(8,128)(2,1)}, bf16[512,1024]{1,0:T(8,128)(2,1)}, u32[]{:S(2)}, u32[]{:S(2)}) collective-permute-start(bf16[512,1024]{1,0:T(8,128)(2,1)} %fusion.2.refs_1_), channel_id=1, source_target_pairs={{0,1},{1,0},{4,5},{5,4},{2,3},{3,2},{6,7},{7,6},{8,9},{9,8},{12,13... | collective-permute-start | bytes 3145736 | tf_op jit(solution)/shard_map/ppermute | solution.py:851
  916.9 38.7 %collective-permute-start.77 = (bf16[2,2,128,1024]{3,2,1,0:T(8,128)(2,1)}, bf16[2,2,128,1024]{3,2,1,0:T(8,128)(2,1)S(1)}, u32[]{:S(2)}, u32[]{:S(2)}) collective-permute-start(bf16[2,2,128,1024]{3,2,1,0:T(8,128)(2,1)} %get-tuple-element.293), channel_id=1, source_target_pairs={{0,8},{8,0},{16,24},{24,16},{1,9},{9,1},{17,25},{25,17},{2,10},{10... | collective-permute-start | bytes 3145736 | tf_op jit(solution)/shard_map/ppermute | solution.py:851
  920.9 92.3 %collective-permute-start.82 = (bf16[2,128,1024]{2,1,0:T(8,128)(2,1)}, bf16[2,128,1024]{2,1,0:T(8,128)(2,1)}, u32[]{:S(2)}, u32[]{:S(2)}) collective-permute-start(bf16[2,128,1024]{2,1,0:T(8,128)(2,1)} %fusion.9), channel_id=1, source_target_pairs={{0,2},{2,0},{1,3},{3,1},{4,6},{6,4},{5,7},{7,5},{8,10},{10,8},{9,1... | collective-permute-start | bytes 1572872 | tf_op jit(solution)/shard_map/ppermute | solution.py:851
  970.0 43.2 %collective-permute-start.81 = (bf16[512,1024]{1,0:T(8,128)(2,1)}, bf16[512,1024]{1,0:T(8,128)(2,1)}, u32[]{:S(2)}, u32[]{:S(2)}) collective-permute-start(bf16[512,1024]{1,0:T(8,128)(2,1)} %fusion.1), channel_id=1, source_target_pairs={{0,0},{2,4},{4,2},{6,6},{1,1},{3,5},{5,3},{7,7},{8,8},{10,12},{12,... | collective-permute-start | bytes 3145736 | tf_op jit(solution)/shard_map/ppermute | solution.py:855
  (162 other events, 1763.2 us)

commit v6 on v5

--- a/solution.py
+++ b/solution.py
@@ -32,7 +32,7 @@
 NN = (((1,), (0,)), ((), ()))
 ROWS = 128
 CHUNK = 64
-BQ = 256
+BQ = 512
 PAIR = 2 * HD
 
 
@@ -956,14 +956,13 @@
         return self.got
 
     def along_y(self):
-        self.here = add(self.keep[0], self.got[0])
+        self.got_x = self.got
         self.got = flip(add(self.keep[1], self.got[1]).astype(BF16), "q", 2)
         return self.got
 
     def halves(self, zh):
         if is_small():
-            total = add(self.here, self.got).astype(BF16)
-            return total[0], total[1]
+            return tuple(add(self.keep[0, k], self.got_x[0, k], self.got[k]).astype(BF16) for k in range(2))
         buckets = [self.keep[0], self.send[0], self.keep[1], self.send[1]]
         every = jnp.stack(buckets).reshape(lax.axis_size("q"), 2, -1, buckets[0].shape[-1])
         rows = order_by(lax.psum_scatter(every, "q", scatter_dimension=0, tiled=False), 0, zh, 2)
@@ -1057,19 +1056,19 @@
 
     def near_z(self):
         half = self.count
-        self.here = add(self.own[:half], self.from_x[:half], self.late_y)
         self.there = flip(add(self.own[half:], self.late_x, self.from_y[:half]).astype(BF16), "zl", 1)
         return [self.there]
 
     def far_z(self):
-        half = self.count // 2
-        self.stays = add(self.here[:half], self.there[:half])
-        self.last = flip(add(self.here[half:], self.there[half:]).astype(BF16), "zh", 1)
+        self.last = flip(self.near_sum(slice(self.count // 2, self.count)).astype(BF16), "zh", 1)
         return [self.last]
+
+    def near_sum(self, blocks):
+        return add(self.own[blocks], self.from_x[blocks], self.late_y[blocks], self.there[blocks])
 
     def total(self):
         if is_small():
-            return self.stays + self.last.astype(F32)
+            return self.near_sum(slice(0, self.count // 2)) + self.last.astype(F32)
         half = self.count
         mine = jnp.stack(
             [self.own, jnp.concatenate([self.to_x[:half], self.rest_x]), jnp.concatenate([self.rest_y, self.to_y[:half]]),
@@ -1166,15 +1165,14 @@
         small = small_step(small, 0)
         up0, down0 = UnitsWeight(up_weight[0][None]), UnitsWeight(down_weight[0][None])
         both1 = UnitsWeight(jnp.stack([up_weight[1], down_weight[1]]))
-        flow.wait(x_low, small)
         flow.hold(
-            up0=up0.shard, down0=down0.shard, down0_twin=down0.shard, both1=both1.shard, heads1=heads_shard[1], top=cotangent,
-            low=x_low, small=small,
+            up0=up0.shard, down0=down0.shard, down0_twin=down0.shard, both1=both1.shard, heads1=heads_shard[1], low=x_low,
+            small=small,
         )
         gate(flow)
         x_low, up0.shard = flow.free("low"), flow.free("up0")
         up0.far_z()
-        small = small_step(flow.free("small"), 1)
+        small = small_step(small_step(flow.free("small"), 1), 2)
         weights_of = [heads_along_y(near, bias_size, hz, where, zh)]
     else:
         x_low = turn(tokens)
@@ -1201,57 +1199,59 @@
             up0.two, down0.shard = flow.free("two"), flow.free("down0")
             up0.start_z()
             down0.start_far_z()
-            small = small_step(flow.free("small"), 2)
+            small = small_step(flow.free("small"), 3)
         if last:
             both1.own = flow.free("own")
             both1.near()
+        if last:
+            flow.hold(top=cotangent)
         forward(flow, xs, qkv_near)
         if first:
             flow.hold(small=small)
         qkv_far = project_in(flow, (xs[1], xs[3]), True, w_heads, in_cols, bias, "project_qkv")
         qkv = (qkv_near, qkv_far)
         if first:
-            small = small_step(flow.free("small"), 3)
-            both1.shard = flow.free("both1")
             down0.join_far_z(flow.free("down0_twin"))
             up0.join_z(flow.free("two_twin"))
             up0.near()
             down0.near_z()
+            both1.shard = flow.free("both1")
             both1.far_z()
         if last:
             top_grad = turn(flow.free("top"))
         ctx, wide, lse = attend_forward(flow, ends, qkv)
         if first:
-            flow.wait(up0.near_x, up0.near_y)
-            flow.hold(small=small, down0=down0.own, both1=both1.two)
+            flow.wait(up0.near_x, up0.near_y, down0.own, both1.two)
+            flow.hold(both1=both1.two)
             up0.corner()
+            down0.near()
         if last:
             flow.wait(both1.near_x, both1.near_y, top_grad)
             flow.hold(own=both1.own)
             both1.corner()
         send = project_out(flow, [ctx], (2, 3), w_heads, out_cols, True, "project_attn")
         flow.wait(send)
-        if first:
-            shard = flow.free("heads1")
-            pair = jnp.stack([turn(shard), cross(shard)])
-        if last:
-            both1.own = flow.free("own")
-            both1.swap_main()
         keep = project_out(flow, [ctx], (0, 1), w_heads, out_cols, False, "project_attn")
         attn, passed = sum_group(keep, send)
         if first:
             flow.wait(passed, up0.far_a, up0.far_b)
-            flow.hold(pair=pair, pair_twin=pair)
+            flow.hold(own=up0.own)
             gate(flow)
+            up0.own = flow.free("own")
             up0.swap_main()
             up0.swap_corner()
-            down0.own = flow.free("down0")
-            down0.near()
             up_bias_full, table = spread_small(order_small(small_step(flow.free("small"), 4), where))
             flow.wait(down0.near_x, down0.near_y)
+            down0.corner()
+            down0.swap_main()
+            shard = flow.free("heads1")
+            pair = jnp.stack([turn(shard), cross(shard)])
             w_up = up0.pieces(), 0
         elif last:
             flow.wait(passed)
+            gate(flow)
+            both1.own = flow.free("own")
+            both1.swap_main()
             flow.hold(far_a=both1.far_a)
             flow.wait(attn[2])
             gate(flow)
@@ -1263,16 +1263,14 @@
         used = (prev_gain, prev_shift, shift_row(l, 0), gain_row(l, 0), shift_row(l, 1))
         n1, hs, r1, act, slope = norm_up(flow, prev, attn, table, used, *w_up, up_bias_full[l], tz)
         if first:
-            down0.corner()
-            down0.swap_main()
+            both1.two = flow.free("both1")
             flow.wait(n1)
-            flow.hold(far_a=down0.far_a)
+            flow.hold(far_a=down0.far_a, pair=pair, pair_twin=pair)
             gate(flow)
             down0.far_a = flow.free("far_a")
             down0.swap_corner()
-            both1.two, pair = flow.free("both1"), flow.free("pair")
+            beside = flip(flow.free("pair"), "q", 1)
             both1.near_z()
-            beside = flip(pair, "q", 1)
             w_down = down0.pieces(), 0
         used = (gain_row(l, 0), shift_row(l, 1), shift_row(l, 2), gain_row(l, 1), shift_row(l, 3))
         n2, y_low, r2 = down_norm(flow, act, *w_down, n1, table, used, tz)
@@ -1337,12 +1335,17 @@
             above.far_z()
             units.far()
             above_halves = above_heads.halves(zh)
+            done = turn(above_halves[0]), uncross(above_halves[1])
+            flow.hold(own=units.own)
         gqkv.append(attend_backward(flow, ends, 1, qkv, gcs, wide, lse))
         if beside:
-            flow.wait(units.late_x, units.late_y)
+            units.own = flow.free("own")
+            flow.wait(units.late_x, units.late_y, above.last, *done)
             units.near_z()
         send = project_out(flow, gqkv, (2, 3), w_heads, in_cols, True, "project_gx")
         flow.wait(send)
+        if beside:
+            flow.hold(own=units.own)
         keep = project_out(flow, gqkv, (0, 1), w_heads, in_cols, False, "project_gx")
         back, passed = sum_group(keep, send)
         flow.wait(passed)
@@ -1350,7 +1353,8 @@
             units.mine()
             flow.wait(*units.made)
         elif small_slice:
-            flow.hold(h0=above_halves[0], h1=above_halves[1])
+            units.own = flow.free("own")
+            units.far_z()
         *buckets, qkv_sums = heads_grad(flow, xs, gqkv, gas, ctx)
         heads = HeadsGrad(*buckets)
         units_of[l], heads_of[l] = units, heads
@@ -1373,25 +1377,18 @@
             g2, gf, sums2 = sum_norm_back(flow, g1, back, kept[l - 1][10], kept[l - 1][11], table, gain_row(l - 1, 1))
     small_sums = jnp.stack(small_grads, axis=2).reshape(tz, dp, -1)
     if small_slice:
-        above_halves = flow.free("h0"), flow.free("h1")
-        done = turn(above_halves[0]), uncross(above_halves[1])
         heads.along_x()
-        flow.wait(units.there)
-        flow.hold(small=small_sums)
+        flow.wait(back[2], units.last)
+        flow.hold(small=small_sums, got=heads.got, own=units.own)
         gate(flow)
-        small_sums = flow.free("small")
-        units.far_z()
-        flow.wait(back[2], *done)
-        flow.hold(small=small_sums, got=heads.got)
-        gate(flow)
-        small_sums, heads.got = flow.free("small"), flow.free("got")
+        small_sums, heads.got, units.own = flow.free("small"), flow.free("got"), flow.free("own")
         input_grad = turn(add(g1, back[0], back[1][0], back[2]).astype(BF16))
         heads.along_y()
         small_sums = fold_small(spread_by_distance(small_sums, where), 0, 2)
         flow.wait(heads.got)
-        flow.hold(small=small_sums, grad=input_grad, last=units.last)
+        flow.hold(small=small_sums, grad=input_grad)
         gate(flow)
-        small_sums, input_grad, units.last = flow.free("small"), flow.free("grad"), flow.free("last")
+        small_sums, input_grad = flow.free("small"), flow.free("grad")
         halves = heads.halves(zh)
         d_heads = jnp.stack([add(turn(halves[0]), uncross(halves[1])), add(*done)])
         small_out = fold_small(small_sums, 2, 5).reshape(layers, -1)

time: 1070 us -> 1040 us (0.972)
  waiting for transfers between devices: 233 us -> 212 us
  Pallas kernels: 512 us -> 496 us
    ppermute x9, waiting for transfers between devices: 73.6 us -> 41.6 us  [turn(): lax.ppermute(values_in, ('c', 'zh'), [(2 * a + b, 2 * b + a) for a in ran...]
    ppermute x9, starting transfers between devices: 35.7 us -> 58.2 us  [turn(): lax.ppermute(values_in, ('c', 'zh'), [(2 * a + b, 2 * b + a) for a in ran...]
    pallas_call x49, Pallas kernels: 512 us -> 496 us  [call(): pl.pallas_call(wrapped, grid_spec=pltpu.PrefetchScalarGridSpec(num_scalar...]
    ppermute x83, starting transfers between devices: 99.8 us -> 86.1 us  [flip(): lax.ppermute(values_in, axes, [(a, a ^ mask) for a in range(lax.axis_size...]
    unnamed x217 -> x250, local copies, waits for them, and re-layouts: 42.2 us -> 43.5 us
  transfers between devices with their start and end apart: 96 -> 96, of which waited for: 35 -> 41; matrix products, arithmetic and copies ran while one was open for 12% -> 11% of each run, Pallas kernels for 40% -> 40%
where the time goes in v6:
time: 1040 us; the launch traced here: 1030 us
  Pallas kernels  496 us (48%)
  waiting for transfers between devices  212 us (20%)
  starting transfers between devices  145 us (14%)
  other arithmetic  86.6 us (8%)
  local copies, waits for them, and re-layouts  80.4 us (8%)
    pallas_call x49, Pallas kernels, call(): pl.pallas_call(wrapped, grid_spec=pltpu.PrefetchScalarGridSpec(num_scalar...  496 us
    ppermute x83, waiting for transfers between devices, flip(): lax.ppermute(values_in, axes, [(a, a ^ mask) for a in range(lax.axis_size...  156 us
    ppermute x83, starting transfers between devices, flip(): lax.ppermute(values_in, axes, [(a, a ^ mask) for a in range(lax.axis_size...  86.1 us
    ppermute x9, starting transfers between devices, turn(): lax.ppermute(values_in, ('c', 'zh'), [(2 * a + b, 2 * b + a) for a in ran...  58.2 us
    unnamed x250, local copies, waits for them, and re-layouts  43.5 us
    ppermute x9, waiting for transfers between devices, turn(): lax.ppermute(values_in, ('c', 'zh'), [(2 * a + b, 2 * b + a) for a in ran...  41.6 us
  transfers between devices with their start and end apart: 96, of which 41 were waited for; matrix products, arithmetic and copies ran while one was open for 11% of the time, Pallas kernels for 40%

profile of v6, /device:TPU:1, one launch (start us, length us, event | category | flops | bytes accessed | tf_op | source)
XLA Modules:
  0.0 1030.1 jit_solution(14192657648247803851)
XLA Ops:
  10.0 9.9 collective-permute-done.7
  56.0 10.2 collective-permute-start.4
  81.0 8.6 collective-permute-done.10.refs_6_
  100.3 11.4 %collective-permute-done.21 = s32[1,4]{1,0:T(1,128)S(1)} collective-permute-done((s32[1,4]{1,0:T(1,128)S(1)}, s32[1,4]{1,0:T(1,128)S(1)}, u32[]{:S(2)}, u32[]{:S(2)}) %collective-permute-start.21) | collective-permute-done | bytes 48 | tf_op jit(solution)/shard_map/ppermute | solution.py:855
  127.9 28.5 %attend_forward.2 = (bf16[4,512,256]{2,1,0:T(8,128)(2,1)}, f32[4,512,256]{2,1,0:T(8,128)}, f32[4,8,512]{2,1,0:T(8,128)}, bf16[144,1024]{1,0:T(8,128)(2,1)}, bf16[16,640]{1,0:T(8,128)(2,1)}) custom-call(s32[5]{0:T(128)} %stack.209.refs_0_, s32[4]{0:T(128)} %bitcast.329, ...), custom_call_target="tpu_custom_call", output_to_operand_aliasing={{3}: (2, {}), {4}: (3, {})} | custom-call | flops 14000000000 | bytes 1024 | tf_op jit(solution)/shard_map/attend_forward/pallas_call | solution.py:80
  193.7 11.6 %collective-permute-done.16 = bf16[4,1,128,1024]{3,2,0,1:T(8,128)(2,1)} collective-permute-done((bf16[4,1,128,1024]{3,2,0,1:T(8,128)(2,1)}, bf16[4,1,128,1024]{3,2,0,1:T(8,128)(2,1)}, u32[]{:S(2)}, u32[]{:S(2)}) %collective-permute-start.16) | collective-permute-done | bytes 1048608 | tf_op jit(solution)/shard_map/ppermute | solution.py:851
  221.7 25.0 %collective-permute-start.30 = (bf16[144,1024]{1,0:T(8,128)(2,1)S(1)}, bf16[144,1024]{1,0:T(8,128)(2,1)}, u32[]{:S(2)}, u32[]{:S(2)}) collective-permute-start(bf16[144,1024]{1,0:T(8,128)(2,1)S(1)} %copy-done.7), channel_id=1, source_target_pairs={{0,0},{2,4},{4,2},{6,6},{1,1},{3,5},{5,3},{7,7},{8,8},{10,12},{12,... | collective-permute-start | bytes 884744 | tf_op jit(solution)/shard_map/ppermute | solution.py:855
  257.0 18.7 %norm_up.2 = (f32[512,1024]{1,0:T(8,128)}, bf16[512,1024]{1,0:T(8,128)(2,1)}, f32[512,128]{1,0:T(8,128)}, bf16[512,4096]{1,0:T(8,128)(2,1)}, bf16[512,4096]{1,0:...) custom-call(s32[5]{0:T(128)} %stack.209.refs_0_, ...), custom_call_target="tpu_custom_call", output_to_operand_aliasing={{5}: (3, {})} | custom-call | flops 7000000000 | bytes 1024 | tf_op jit(solution)/shard_map/norm_up/pallas_call | solution.py:80
  282.2 14.3 %down_norm.2 = (f32[512,1024]{1,0:T(8,128)}, bf16[512,1024]{1,0:T(8,128)(2,1)}, f32[512,128]{1,0:T(8,128)}, bf16[2,144,1024]{2,1,0:T(8,128)(2,1)}) custom-call(s32[5]{0:T(128)} %stack.209.refs_0_, bf16[2,144,1024]{2,1,0:T(8,128)(2,1)} %get-tuple-element.185.refs_1_, ...), custom_call_target="tpu_custom_call", output_to_operand_aliasing={{3}: (1, {})} | custom-call | flops 7000000000 | bytes 1024 | tf_op jit(solution)/shard_map/down_norm/pallas_call | solution.py:80
  306.8 18.8 %collective-permute-done.38.refs_7_.refs_6_.refs_5_.refs_4_ = bf16[2,2,144,1024]{3,2,1,0:T(8,128)(2,1)S(1)} collective-permute-done((bf16[2,2,144,1024]{3,2,1,0:T(8,128)(2,1)S(1)}, bf16[2,2,144,1024]{3,2,1,0:T(8,128)(2,1)S(1)}, u32[]{:S(2)}, u32[]{:S(2)}) %collective-permute-start.38) | collective-permute-done | bytes 1179680 | tf_op jit(solution)/shard_map/ppermute | solution.py:851
  354.2 28.4 %attend_forward.3 = (bf16[4,512,256]{2,1,0:T(8,128)(2,1)}, f32[4,512,256]{2,1,0:T(8,128)}, f32[4,8,512]{2,1,0:T(8,128)}) custom-call(s32[5]{0:T(128)} %stack.209.refs_0_, s32[4]{0:T(128)} %bitcast.330, bf16[2,512,768]{2,1,0:T(8,128)(2,1)} %get-tuple-element.194.refs_1_.refs_2_.refs_3_, bf16[2,512,768]{2,1,0:T(8,128)(2,1)} %get-tuple-element.198.refs_3_.refs_4_), custom_call_target="tpu_custom_call" | custom-call | flops 14000000000 | bytes 1024 | tf_op jit(solution)/shard_map/attend_forward/pallas_call | solution.py:80
  414.1 22.3 %collective-permute-done.46.refs_2_ = bf16[2,2,128,1024]{3,2,1,0:T(8,128)(2,1)S(1)} collective-permute-done((bf16[2,2,128,1024]{3,2,1,0:T(8,128)(2,1)S(1)}, bf16[2,2,128,1024]{3,2,1,0:T(8,128)(2,1)S(1)}, u32[]{:S(2)}, u32[]{:S(2)}) %collective-permute-start.46) | collective-permute-done | bytes 1048608 | tf_op jit(solution)/shard_map/ppermute | solution.py:851
  445.9 18.9 %norm_up.3 = (f32[512,1024]{1,0:T(8,128)}, bf16[512,1024]{1,0:T(8,128)(2,1)}, f32[512,128]{1,0:T(8,128)}, bf16[512,4096]{1,0:T(8,128)(2,1)}, bf16[512,4096]{1,0:T(8,128)(2,1)}) custom-call(s32[5]{0:T(128)} %stack.209.refs_0_, f32[512,1024]{1,0:T(8,128)} %get-tuple-element.188.refs_1_.refs_6_, bf16[512,1024]{1,0:T(8,128)(2,1)} %get-tuple-element.202.refs_2_, ...), custom_call_target="tpu_custom_call" | custom-call | flops 7000000000 | bytes 1024 | tf_op jit(solution)/shard_map/norm_up/pallas_call | solution.py:80
  464.8 14.3 %down_norm.3 = (f32[512,1024]{1,0:T(8,128)}, bf16[512,1024]{1,0:T(8,128)(2,1)}, f32[512,128]{1,0:T(8,128)}) custom-call(s32[5]{0:T(128)} %stack.209.refs_0_, bf16[512,4096]{1,0:T(8,128)(2,1)} %get-tuple-element.205.refs_1_.refs_3_, f32[512,1024]{1,0:T(8,128)} %get-tuple-element.206.refs_2_.refs_4_, f32[16,1024]{1,0:T(8,128)} %pad.13.refs_8_.refs_4_.refs_5_.refs_3_.refs_6_, ...), custom_call_target="tpu_custom_call" | custom-call | flops 7000000000 | bytes 1024 | tf_op jit(solution)/shard_map/down_norm/pallas_call | solution.py:80
  488.2 11.5 %units_back.2 = (bf16[512,4096]{1,0:T(8,128)(2,1)}, f32[4,1,1024]{2,1,0:T(1,128)}) custom-call(s32[5]{0:T(128)} %stack.209.refs_0_, bf16[512,1024]{1,0:T(8,128)(2,1)} %get-tuple-element.210.refs_1_.refs_2_, bf16[512,4096]{1,0:T(8,128)(2,1)} %get-tuple-element.211.refs_2_, bf16[3,4,2,128,1024]{4,3,2,1,0:T(8,128)(2,1)} %pad_maximum_fusion.refs_7_.refs_4_.refs_3_, ...), custom_call_target="tpu_custom_call" | custom-call | flops 7000000000 | bytes 1024 | tf_op jit(solution)/shard_map/units_back/pallas_call | solution.py:80
  508.3 15.0 %up_back.2 = (f32[512,1024]{1,0:T(8,128)}, bf16[512,1024]{1,0:T(8,128)(2,1)}, f32[8,1024]{1,0:T(8,128)}, bf16[512,1024]{1,0:T(8,128)(2,1)}) custom-call(s32[5]{0:T(128)} %stack.209.refs_0_, bf16[512,1024]{1,0:T(8,128)(2,1)} %copy-done.41, bf16[512,4096]{1,0:T(8,128)(2,1)} %get-tuple-element.212.refs_2_.refs_5_, ...), custom_call_target="tpu_custom_call", output_to_operand_aliasing={{3}: (1, {})} | custom-call | flops 7000000000 | bytes 1024 | tf_op jit(solution)/shard_map/up_back/pallas_call | solution.py:80
  523.4 12.7 %grads_theirs.2.refs_1_.refs_2_ = bf16[4,8,128,1024]{3,2,1,0:T(8,128)(2,1)} custom-call(s32[5]{0:T(128)} %stack.209.refs_0_, bf16[512,1024]{1,0:T(8,128)(2,1)} %get-tuple-element.216.refs_1_.refs_10_, bf16[512,1024]{1,0:T(8,128)(2,1)} %get-tuple-element.210.refs_1_.refs_2_, bf16[512,4096]{1,0:T(8,128)(2,1)} %get-tuple-element.205.refs_1_.refs_3_, ...), custom_call_target="tpu_custom_call" | custom-call | flops 70000000 | bytes 1024 | tf_op jit(solution)/shard_map/grads_theirs/pallas_call | solution.py:80
  554.9 29.5 %attend_backward.4.refs_2_.refs_1_.refs_14_ = bf16[4,512,384]{2,1,0:T(8,128)(2,1)} custom-call(s32[5]{0:T(128)} %stack.209.refs_0_, s32[4]{0:T(128)} %bitcast.331, bf16[2,512,768]{2,1,0:T(8,128)(2,1)} %get-tuple-element.194.refs_1_.refs_2_.refs_3_, bf16[2,512,768]{2,1,0:T(8,128)(2,1)} %get-tuple-element.198.refs_3_.refs_4_, ...), custom_call_target="tpu_custom_call" | custom-call | flops 10499999744 | bytes 1024 | tf_op jit(solution)/shard_map/attend_backward/pallas_call | solution.py:80
  584.5 29.7 %attend_backward.5.refs_2_.refs_3_.refs_15_ = bf16[4,512,384]{2,1,0:T(8,128)(2,1)} custom-call(s32[5]{0:T(128)} %stack.209.refs_0_, s32[4]{0:T(128)} %bitcast.332, bf16[4,512,384]{2,1,0:T(8,128)(2,1)} %attend_backward.4.refs_2_.refs_1_.refs_14_, bf16[2,512,768]{2,1,0:T(8,128)(2,1)} %get-tuple-element.194.refs_1_.refs_2_.refs_3_, ...), custom_call_target="tpu_custom_call" | custom-call | flops 10499999744 | bytes 1024 | tf_op jit(solution)/shard_map/attend_backward/pallas_call | solution.py:80
  632.0 15.9 %grads_mine.2 = (bf16[8,128,1024]{2,1,0:T(8,128)(2,1)}, bf16[8,128,1024]{2,1,0:T(8,128)(2,1)}, bf16[8,128,1024]{2,1,0:T(8,128)(2,1)}, bf16[4,128,1024]{2,1,0:T(8,128)(2,1)}, bf16[4,128,1024]{2,1,0:T(8,128)(2,1)}) custom-call(s32[5]{0:T(128)} %stack.209.refs_0_, bf16[512,1024]{1,0:T(8,128)(2,1)} %copy-done.38, ...), custom_call_target="tpu_custom_call" | custom-call | flops 70000000 | bytes 1024 | tf_op jit(solution)/shard_map/grads_mine/pallas_call | solution.py:80
  648.7 13.1 %heads_grad.2 = (bf16[2,2,128,1024]{3,2,1,0:T(8,128)(2,1)}, bf16[2,2,128,1024]{3,2,1,0:T(8,128)(2,1)}, f32[1,768]{1,0:T(1,128)}) custom-call(s32[5]{0:T(128)} %stack.209.refs_0_, bf16[8,128,1024]{2,1,0:T(8,128)(2,1)} %get-tuple-element.225.refs_1_, bf16[8,128,1024]{2,1,0:T(8,128)(2,1)} %get-tuple-element.223.refs_2_, ...), custom_call_target="tpu_custom_call" | custom-call | flops 70000000 | bytes 1024 | tf_op jit(solution)/shard_map/heads_grad/pallas_call | solution.py:80
  662.7 7.7 sum_norm_back.1
  670.4 11.5 %units_back.3 = (bf16[512,4096]{1,0:T(8,128)(2,1)}, f32[4,1,1024]{2,1,0:T(1,128)}) custom-call(s32[5]{0:T(128)} %stack.209.refs_0_, bf16[512,1024]{1,0:T(8,128)(2,1)} %get-tuple-element.232.refs_1_.refs_4_.refs_2_, bf16[512,4096]{1,0:T(8,128)(2,1)} %get-tuple-element.234.refs_2_, bf16[3,4,1,128,1024]{4,3,2,1,0:T(8,128)(2,1)} %get-tuple-element.321.refs_5_.refs_3_, ...), custom_call_target="tpu_custom_call" | custom-call | flops 7000000000 | bytes 1024 | tf_op jit(solution)/shard_map/units_back/pallas_call | solution.py:80
  681.9 12.9 %collective-permute-done.56.refs_1_ = bf16[8,128,1024]{2,1,0:T(8,128)(2,1)S(1)} collective-permute-done((bf16[8,128,1024]{2,1,0:T(8,128)(2,1)}, bf16[8,128,1024]{2,1,0:T(8,128)(2,1)S(1)}, u32[]{:S(2)}, u32[]{:S(2)}) %collective-permute-start.56) | collective-permute-done | bytes 2097184 | tf_op jit(solution)/shard_map/ppermute | solution.py:851
  696.9 12.8 %grads_theirs.3 = (bf16[4,8,128,1024]{3,2,1,0:T(8,128)(2,1)}, bf16[2,2,128,1024]{3,2,1,0:T(8,128)(2,1)}) custom-call(s32[5]{0:T(128)} %stack.209.refs_0_, bf16[8,128,1024]{2,1,0:T(8,128)(2,1)} %copy-done.22, bf16[8,128,1024]{2,1,0:T(8,128)(2,1)} %copy-done.24, ...), custom_call_target="tpu_custom_call", output_to_operand_aliasing={{1}: (3, {})} | custom-call | flops 70000000 | bytes 1024 | tf_op jit(solution)/shard_map/grads_theirs/pallas_call | solution.py:80
  716.5 15.2 %up_back.3 = (f32[512,1024]{1,0:T(8,128)}, bf16[512,1024]{1,0:T(8,128)(2,1)}, f32[8,1024]{1,0:T(8,128)}) custom-call(s32[5]{0:T(128)} %stack.209.refs_0_, bf16[4,8,128,1024]{3,2,1,0:T(8,128)(2,1)} %get-tuple-element.236.refs_1_, bf16[512,4096]{1,0:T(8,128)(2,1)} %get-tuple-element.235.refs_7_.refs_2_.refs_5_, f32[512,1024]{1,0:T(8,128)} %get-tuple-element.237.refs_3_, ...), custom_call_target="tpu_custom_call" | custom-call | flops 7000000000 | bytes 1024 | tf_op jit(solution)/shard_map/up_back/pallas_call | solution.py:80
  737.4 15.8 %grads_mine.3 = (bf16[8,128,1024]{2,1,0:T(8,128)(2,1)}, bf16[8,128,1024]{2,1,0:T(8,128)(2,1)}, bf16[8,128,1024]{2,1,0:T(8,128)(2,1)}, bf16[4,128,1024]{2,1,0:T(8,128)(2,1)}, bf16[4,128,1024]{2,1,0:T(8,128)(2,1)}) custom-call(s32[5]{0:T(128)} %stack.209.refs_0_, bf16[512,1024]{1,0:T(8,128)(2,1)} %get-tuple-element.239.refs_1_.refs_6_, ...), custom_call_target="tpu_custom_call" | custom-call | flops 70000000 | bytes 1024 | tf_op jit(solution)/shard_map/grads_mine/pallas_call | solution.py:80
  794.3 29.5 %attend_backward.6 = (bf16[4,512,384]{2,1,0:T(8,128)(2,1)}, bf16[4,128,1024]{2,1,0:T(8,128)(2,1)}, bf16[4,128,1024]{2,1,0:T(8,128)(2,1)}) custom-call(s32[5]{0:T(128)} %stack.209.refs_0_, s32[4]{0:T(128)} %bitcast.333, bf16[4,128,1024]{2,1,0:T(8,128)(2,1)} %get-tuple-element.240.refs_7_.refs_2_, ...), custom_call_target="tpu_custom_call", output_to_operand_aliasing={{1}: (2, {}), {2}: (3, {})} | custom-call | flops 10499999744 | bytes 1024 | tf_op jit(solution)/shard_map/attend_backward/pallas_call | solution.py:80
  831.2 30.0 %attend_backward.7 = (bf16[4,512,384]{2,1,0:T(8,128)(2,1)}, bf16[8,128,1024]{2,1,0:T(8,128)(2,1)}) custom-call(s32[5]{0:T(128)} %stack.209.refs_0_, s32[4]{0:T(128)} %bitcast.334, bf16[4,512,384]{2,1,0:T(8,128)(2,1)} %get-tuple-element.251.refs_2_.refs_6_.refs_3_.refs_10_, ...), custom_call_target="tpu_custom_call", output_to_operand_aliasing={{1}: (7, {})} | custom-call | flops 10499999744 | bytes 1024 | tf_op jit(solution)/shard_map/attend_backward/pallas_call | solution.py:80
  893.2 12.8 %heads_grad.3 = (bf16[2,2,128,1024]{3,2,1,0:T(8,128)(2,1)}, bf16[2,2,128,1024]{3,2,1,0:T(8,128)(2,1)}, f32[1,768]{1,0:T(1,128)}) custom-call(s32[5]{0:T(128)} %stack.209.refs_0_, bf16[512,1024]{1,0:T(8,128)(2,1)} %fusion.2.refs_1_, bf16[512,1024]{1,0:T(8,128)(2,1)} %get-tuple-element.148.refs_10_.refs_4_.refs_2_, ...), custom_call_target="tpu_custom_call" | custom-call | flops 70000000 | bytes 1024 | tf_op jit(solution)/shard_map/heads_grad/pallas_call | solution.py:80
  912.0 23.4 %collective-permute-done.78.refs_2_ = bf16[2,128,1024]{2,1,0:T(8,128)(2,1)S(1)} collective-permute-done((bf16[2,128,1024]{2,1,0:T(8,128)(2,1)}, bf16[2,128,1024]{2,1,0:T(8,128)(2,1)S(1)}, u32[]{:S(2)}, u32[]{:S(2)}) %collective-permute-start.78) | collective-permute-done | bytes 524320 | tf_op jit(solution)/shard_map/ppermute | solution.py:851
  973.8 12.3 %collective-permute-done.84 = bf16[128,1024]{1,0:T(8,128)(2,1)S(1)} collective-permute-done((bf16[128,1024]{1,0:T(8,128)(2,1)S(1)}, bf16[128,1024]{1,0:T(8,128)(2,1)S(1)}, u32[]{:S(2)}, u32[]{:S(2)}) %collective-permute-start.84) | collective-permute-done | bytes 262176 | tf_op jit(solution)/shard_map/ppermute | solution.py:855
  (686 shorter events, 467.6 us)
Async XLA Ops:
  31.5 41.7 %collective-permute-start.9 = (bf16[2,2,144,1024]{3,2,1,0:T(8,128)(2,1)S(1)}, bf16[2,2,144,1024]{3,2,1,0:T(8,128)(2,1)S(1)}, u32[]{:S(2)}, u32[]{:S(2)}) collective-permute-start(bf16[2,2,144,1024]{3,2,1,0:T(8,128)(2,1)S(1)} %pad_maximum_fusion.5.refs_13_.refs_9_.refs_6_.refs_3_.refs_4_.refs_8_.refs_5_), channel_id=1, source_target_pairs={{0,16},{8,24},{16,0},{24,8},{1,17},{9,25},{17,1},{25,9},{2,18},{10... | collective-permute-start | bytes 3538952 | tf_op jit(solution)/shard_map/ppermute | solution.py:851
  121.7 35.9 %collective-permute-start.14 = (bf16[2,1,128,1024]{3,2,0,1:T(8,128)(2,1)S(1)}, bf16[2,1,128,1024]{3,2,0,1:T(8,128)(2,1)S(1)}, u32[]{:S(2)}, u32[]{:S(2)}) collective-permute-start(bf16[2,1,128,1024]{3,2,0,1:T(8,128)(2,1)S(1)} %pad_maximum_fusion.17), channel_id=1, source_target_pairs={{0,1},{1,0},{2,3},{3,2},{4,5},{5,4},{6,7},{7,6},{8,9},{9,8},{10,11... | collective-permute-start | bytes 1572872 | tf_op jit(solution)/shard_map/ppermute | solution.py:851
  123.3 33.2 %collective-permute-start.20 = (bf16[2,128,1024]{2,1,0:T(8,128)(2,1)}, bf16[2,128,1024]{2,1,0:T(8,128)(2,1)S(1)}, u32[]{:S(2)}, u32[]{:S(2)}) collective-permute-start(bf16[2,128,1024]{2,1,0:T(8,128)(2,1)} %get-tuple-element.164), channel_id=1, source_target_pairs={{0,2},{2,0},{1,3},{3,1},{4,6},{6,4},{5,7},{7,5},{8,10},{10,8},{9,1... | collective-permute-start | bytes 1572872 | tf_op jit(solution)/shard_map/ppermute | solution.py:851
  125.4 33.8 %collective-permute-start.19 = (bf16[4,1,128,1024]{3,2,0,1:T(8,128)(2,1)S(1)}, bf16[4,1,128,1024]{3,2,0,1:T(8,128)(2,1)S(1)}, u32[]{:S(2)}, u32[]{:S(2)}) collective-permute-start(bf16[4,1,128,1024]{3,2,0,1:T(8,128)(2,1)S(1)} %get-tuple-element.335), channel_id=1, source_target_pairs={{0,16},{8,24},{16,0},{24,8},{1,17},{9,25},{17,1},{25,9},{2,18},{10... | collective-permute-start | bytes 3145736 | tf_op jit(solution)/shard_map/ppermute | solution.py:851
  126.7 32.5 %collective-permute-start.18 = (bf16[4,1,128,1024]{3,2,1,0:T(8,128)(2,1)S(1)}, bf16[4,1,128,1024]{3,2,1,0:T(8,128)(2,1)S(1)}, u32[]{:S(2)}, u32[]{:S(2)}) collective-permute-start(bf16[4,1,128,1024]{3,2,1,0:T(8,128)(2,1)S(1)} %get-tuple-element.336.refs_7_), channel_id=1, source_target_pairs={{0,8},{8,0},{16,24},{24,16},{1,9},{9,1},{17,25},{25,17},{2,10},{10... | collective-permute-start | bytes 3145736 | tf_op jit(solution)/shard_map/ppermute | solution.py:851
  169.8 35.5 %collective-permute-start.15 = (bf16[4,1,128,1024]{3,2,1,0:T(8,128)(2,1)S(1)}, bf16[4,1,128,1024]{3,2,1,0:T(8,128)(2,1)S(1)}, u32[]{:S(2)}, u32[]{:S(2)}) collective-permute-start(bf16[4,1,128,1024]{3,2,1,0:T(8,128)(2,1)S(1)} %copy-done.61), channel_id=1, source_target_pairs={{0,8},{8,0},{16,24},{24,16},{1,9},{9,1},{17,25},{25,17},{2,10},{10... | collective-permute-start | bytes 3145736 | tf_op jit(solution)/shard_map/ppermute | solution.py:851
  171.2 34.0 %collective-permute-start.16 = (bf16[4,1,128,1024]{3,2,0,1:T(8,128)(2,1)}, bf16[4,1,128,1024]{3,2,0,1:T(8,128)(2,1)}, u32[]{:S(2)}, u32[]{:S(2)}) collective-permute-start(bf16[4,1,128,1024]{3,2,0,1:T(8,128)(2,1)} %get-tuple-element.334), channel_id=1, source_target_pairs={{0,16},{8,24},{16,0},{24,8},{1,17},{9,25},{17,1},{25,9},{2,18},{10... | collective-permute-start | bytes 3145736 | tf_op jit(solution)/shard_map/ppermute | solution.py:851
  188.9 68.1 %collective-permute-start.27 = (bf16[3,4,1,128,1024]{4,3,1,2,0:T(8,128)(2,1)}, bf16[3,4,1,128,1024]{4,3,1,2,0:T(8,128)(2,1)}, u32[]{:S(2)}, u32[]{:S(2)}) collective-permute-start(bf16[3,4,1,128,1024]{4,3,1,2,0:T(8,128)(2,1)} %get-tuple-element.322), channel_id=1, source_target_pairs={{0,4},{4,0},{1,5},{5,1},{2,6},{6,2},{3,7},{7,3},{8,12},{12,8},{9,1... | collective-permute-start | bytes 9437192 | tf_op jit(solution)/shard_map/ppermute | solution.py:851
  193.2 63.6 %collective-permute-start.28 = (bf16[4,1,128,1024]{3,2,1,0:T(8,128)(2,1)}, bf16[4,1,128,1024]{3,2,1,0:T(8,128)(2,1)}, u32[]{:S(2)}, u32[]{:S(2)}) collective-permute-start(bf16[4,1,128,1024]{3,2,1,0:T(8,128)(2,1)} %pad_maximum_fusion.10.refs_11_.refs_8_), channel_id=1, source_target_pairs={{0,4},{4,0},{1,5},{5,1},{2,6},{6,2},{3,7},{7,3},{8,12},{12,8},{9,1... | collective-permute-start | bytes 3145736 | tf_op jit(solution)/shard_map/ppermute | solution.py:851
  209.5 69.6 %collective-permute-start.33 = (bf16[3,4,1,128,1024]{4,3,1,2,0:T(8,128)(2,1)}, bf16[3,4,1,128,1024]{4,3,1,2,0:T(8,128)(2,1)}, u32[]{:S(2)}, u32[]{:S(2)}) collective-permute-start(bf16[3,4,1,128,1024]{4,3,1,2,0:T(8,128)(2,1)} %get-tuple-element.320), channel_id=1, source_target_pairs={{0,4},{4,0},{1,5},{5,1},{2,6},{6,2},{3,7},{7,3},{8,12},{12,8},{9,1... | collective-permute-start | bytes 9437192 | tf_op jit(solution)/shard_map/ppermute | solution.py:851
  213.4 43.6 %collective-permute-start.25 = (bf16[512,1024]{1,0:T(8,128)(2,1)S(1)}, bf16[512,1024]{1,0:T(8,128)(2,1)}, u32[]{:S(2)}, u32[]{:S(2)}) collective-permute-start(bf16[512,1024]{1,0:T(8,128)(2,1)S(1)} %copy-done.44), channel_id=1, source_target_pairs={{0,1},{1,0},{4,5},{5,4},{2,3},{3,2},{6,7},{7,6},{8,9},{9,8},{12,13... | collective-permute-start | bytes 3145736 | tf_op jit(solution)/shard_map/ppermute | solution.py:851
  221.7 31.9 %collective-permute-start.30 = (bf16[144,1024]{1,0:T(8,128)(2,1)S(1)}, bf16[144,1024]{1,0:T(8,128)(2,1)}, u32[]{:S(2)}, u32[]{:S(2)}) collective-permute-start(bf16[144,1024]{1,0:T(8,128)(2,1)S(1)} %copy-done.7), channel_id=1, source_target_pairs={{0,0},{2,4},{4,2},{6,6},{1,1},{3,5},{5,3},{7,7},{8,8},{10,12},{12,... | collective-permute-start | bytes 884744 | tf_op jit(solution)/shard_map/ppermute | solution.py:855
  299.3 39.7 %collective-permute-start.41 = (bf16[512,1024]{1,0:T(8,128)(2,1)S(1)}, bf16[512,1024]{1,0:T(8,128)(2,1)}, u32[]{:S(2)}, u32[]{:S(2)}) collective-permute-start(bf16[512,1024]{1,0:T(8,128)(2,1)S(1)} %copy-done.51), channel_id=1, source_target_pairs={{0,1},{1,0},{4,5},{5,4},{2,3},{3,2},{6,7},{7,6},{8,9},{9,8},{12,13... | collective-permute-start | bytes 3145736 | tf_op jit(solution)/shard_map/ppermute | solution.py:851
  299.3 32.0 %collective-permute-start.36 = (bf16[512,1024]{1,0:T(8,128)(2,1)S(1)}, bf16[512,1024]{1,0:T(8,128)(2,1)S(1)}, u32[]{:S(2)}, u32[]{:S(2)}) collective-permute-start(bf16[512,1024]{1,0:T(8,128)(2,1)S(1)} %copy-done.51), channel_id=1, source_target_pairs={{0,4},{1,5},{4,0},{5,1},{2,6},{3,7},{6,2},{7,3},{8,12},{9,13},{12,... | collective-permute-start | bytes 3145736 | tf_op jit(solution)/shard_map/ppermute | solution.py:851
  340.8 46.5 %collective-permute-start.40 = (bf16[4,2,128,1024]{3,2,1,0:T(8,128)(2,1)S(1)}, bf16[4,2,128,1024]{3,2,1,0:T(8,128)(2,1)S(1)}, u32[]{:S(2)}, u32[]{:S(2)}) collective-permute-start(bf16[4,2,128,1024]{3,2,1,0:T(8,128)(2,1)S(1)} %copy-done.4), channel_id=1, source_target_pairs={{0,16},{8,24},{16,0},{24,8},{1,17},{9,25},{17,1},{25,9},{2,18},{10... | collective-permute-start | bytes 6291464 | tf_op jit(solution)/shard_map/ppermute | solution.py:851
  342.0 46.1 %collective-permute-start.39 = (bf16[4,2,128,1024]{3,2,1,0:T(8,128)(2,1)S(1)}, bf16[4,2,128,1024]{3,2,1,0:T(8,128)(2,1)S(1)}, u32[]{:S(2)}, u32[]{:S(2)}) collective-permute-start(bf16[4,2,128,1024]{3,2,1,0:T(8,128)(2,1)S(1)} %copy-done.4), channel_id=1, source_target_pairs={{0,8},{8,0},{16,24},{24,16},{1,9},{9,1},{17,25},{25,17},{2,10},{10... | collective-permute-start | bytes 6291464 | tf_op jit(solution)/shard_map/ppermute | solution.py:851
  412.0 33.9 %collective-permute-start.48 = (bf16[3,4,2,128,1024]{4,3,2,1,0:T(8,128)(2,1)}, bf16[3,4,2,128,1024]{4,3,2,1,0:T(8,128)(2,1)}, u32[]{:S(2)}, u32[]{:S(2)}) collective-permute-start(bf16[3,4,2,128,1024]{4,3,2,1,0:T(8,128)(2,1)} %pad_maximum_fusion.refs_7_.refs_4_.refs_3_), channel_id=1, source_target_pairs={{0,4},{4,0},{1,5},{5,1},{2,6},{6,2},{3,7},{7,3},{8,12},{12,8},{9,1... | collective-permute-start | bytes 18874376 | tf_op jit(solution)/shard_map/ppermute | solution.py:851
  554.4 76.7 %collective-permute-start.55 = (bf16[4,8,128,1024]{3,2,1,0:T(8,128)(2,1)}, bf16[4,8,128,1024]{3,2,1,0:T(8,128)(2,1)}, u32[]{:S(2)}, u32[]{:S(2)}) collective-permute-start(bf16[4,8,128,1024]{3,2,1,0:T(8,128)(2,1)} %get-tuple-element.222), channel_id=1, source_target_pairs={{0,4},{4,0},{1,5},{5,1},{2,6},{6,2},{3,7},{7,3},{8,12},{12,8},{9,1... | collective-permute-start | bytes 25165832 | tf_op jit(solution)/shard_map/ppermute | solution.py:851
  647.9 46.9 %collective-permute-start.56 = (bf16[8,128,1024]{2,1,0:T(8,128)(2,1)}, bf16[8,128,1024]{2,1,0:T(8,128)(2,1)S(1)}, u32[]{:S(2)}, u32[]{:S(2)}) collective-permute-start(bf16[8,128,1024]{2,1,0:T(8,128)(2,1)} %get-tuple-element.223.refs_2_), channel_id=1, source_target_pairs={{0,8},{8,0},{16,24},{24,16},{1,9},{9,1},{17,25},{25,17},{2,10},{10... | collective-permute-start | bytes 6291464 | tf_op jit(solution)/shard_map/ppermute | solution.py:851
  647.9 47.0 %collective-permute-start.57 = (bf16[8,128,1024]{2,1,0:T(8,128)(2,1)}, bf16[8,128,1024]{2,1,0:T(8,128)(2,1)S(1)}, u32[]{:S(2)}, u32[]{:S(2)}) collective-permute-start(bf16[8,128,1024]{2,1,0:T(8,128)(2,1)} %get-tuple-element.224.refs_3_), channel_id=1, source_target_pairs={{0,16},{8,24},{16,0},{24,8},{1,17},{9,25},{17,1},{25,9},{2,18},{10... | collective-permute-start | bytes 6291464 | tf_op jit(solution)/shard_map/ppermute | solution.py:851
  713.7 39.5 %collective-permute-start.62 = (bf16[4,128,1024]{2,1,0:T(8,128)(2,1)}, bf16[4,128,1024]{2,1,0:T(8,128)(2,1)}, u32[]{:S(2)}, u32[]{:S(2)}) collective-permute-start(bf16[4,128,1024]{2,1,0:T(8,128)(2,1)} %add_convert_fusion.4), channel_id=1, source_target_pairs={{0,16},{8,24},{16,0},{24,8},{1,17},{9,25},{17,1},{25,9},{2,18},{10... | collective-permute-start | bytes 3145736 | tf_op jit(solution)/shard_map/ppermute | solution.py:851
  715.8 38.1 %collective-permute-start.61 = (bf16[4,128,1024]{2,1,0:T(8,128)(2,1)}, bf16[4,128,1024]{2,1,0:T(8,128)(2,1)}, u32[]{:S(2)}, u32[]{:S(2)}) collective-permute-start(bf16[4,128,1024]{2,1,0:T(8,128)(2,1)} %add_convert_fusion.5), channel_id=1, source_target_pairs={{0,8},{8,0},{16,24},{24,16},{1,9},{9,1},{17,25},{25,17},{2,10},{10... | collective-permute-start | bytes 3145736 | tf_op jit(solution)/shard_map/ppermute | solution.py:851
  733.2 39.3 %collective-permute-start.60 = (bf16[512,1024]{1,0:T(8,128)(2,1)}, bf16[512,1024]{1,0:T(8,128)(2,1)}, u32[]{:S(2)}, u32[]{:S(2)}) collective-permute-start(bf16[512,1024]{1,0:T(8,128)(2,1)} %get-tuple-element.239.refs_1_.refs_6_), channel_id=1, source_target_pairs={{0,4},{1,5},{4,0},{5,1},{2,6},{3,7},{6,2},{7,3},{8,12},{9,13},{12,... | collective-permute-start | bytes 3145736 | tf_op jit(solution)/shard_map/ppermute | solution.py:851
  753.2 70.5 %collective-permute-start.68 = (bf16[8,128,1024]{2,1,0:T(8,128)(2,1)}, bf16[8,128,1024]{2,1,0:T(8,128)(2,1)}, u32[]{:S(2)}, u32[]{:S(2)}) collective-permute-start(bf16[8,128,1024]{2,1,0:T(8,128)(2,1)} %get-tuple-element.244.refs_5_), channel_id=1, source_target_pairs={{0,8},{8,0},{16,24},{24,16},{1,9},{9,1},{17,25},{25,17},{2,10},{10... | collective-permute-start | bytes 6291464 | tf_op jit(solution)/shard_map/ppermute | solution.py:851
  768.0 58.6 %collective-permute-start.66 = (bf16[8,128,1024]{2,1,0:T(8,128)(2,1)}, bf16[8,128,1024]{2,1,0:T(8,128)(2,1)}, u32[]{:S(2)}, u32[]{:S(2)}) collective-permute-start(bf16[8,128,1024]{2,1,0:T(8,128)(2,1)} %get-tuple-element.245.refs_6_), channel_id=1, source_target_pairs={{0,16},{8,24},{16,0},{24,8},{1,17},{9,25},{17,1},{25,9},{2,18},{10... | collective-permute-start | bytes 6291464 | tf_op jit(solution)/shard_map/ppermute | solution.py:851
  772.5 56.0 %collective-permute-start.70 = (bf16[4,128,1024]{2,1,0:T(8,128)(2,1)}, bf16[4,128,1024]{2,1,0:T(8,128)(2,1)S(1)}, u32[]{:S(2)}, u32[]{:S(2)}) collective-permute-start(bf16[4,128,1024]{2,1,0:T(8,128)(2,1)} %add_convert_fusion.1), channel_id=1, source_target_pairs={{0,1},{1,0},{2,3},{3,2},{4,5},{5,4},{6,7},{7,6},{8,9},{9,8},{10,11... | collective-permute-start | bytes 3145736 | tf_op jit(solution)/shard_map/ppermute | solution.py:851
  782.7 78.5 %collective-permute-start.74 = (bf16[128,1024]{1,0:T(8,128)(2,1)}, bf16[128,1024]{1,0:T(8,128)(2,1)S(1)}, u32[]{:S(2)}, u32[]{:S(2)}) collective-permute-start(bf16[128,1024]{1,0:T(8,128)(2,1)} %get-tuple-element.326), channel_id=1, source_target_pairs={{2,0},{6,2},{0,4},{4,6},{3,1},{7,3},{1,5},{5,7},{10,8},{14,10},{8,... | collective-permute-start | bytes 786440 | tf_op jit(solution)/shard_map/ppermute | solution.py:863
  783.2 78.0 %collective-permute-start.73 = (bf16[128,1024]{1,0:T(8,128)(2,1)S(1)}, bf16[128,1024]{1,0:T(8,128)(2,1)S(1)}, u32[]{:S(2)}, u32[]{:S(2)}) collective-permute-start(bf16[128,1024]{1,0:T(8,128)(2,1)S(1)} %get-tuple-element.327), channel_id=1, source_target_pairs={{0,0},{2,4},{4,2},{6,6},{1,1},{3,5},{5,3},{7,7},{8,8},{10,12},{12,... | collective-permute-start | bytes 786440 | tf_op jit(solution)/shard_map/ppermute | solution.py:855
  825.8 35.5 %collective-permute-start.69 = (bf16[4,128,1024]{2,1,0:T(8,128)(2,1)S(1)}, bf16[4,128,1024]{2,1,0:T(8,128)(2,1)S(1)}, u32[]{:S(2)}, u32[]{:S(2)}) collective-permute-start(bf16[4,128,1024]{2,1,0:T(8,128)(2,1)S(1)} %add_convert_fusion.2), channel_id=1, source_target_pairs={{0,16},{8,24},{16,0},{24,8},{1,17},{9,25},{17,1},{25,9},{2,18},{10... | collective-permute-start | bytes 3145736 | tf_op jit(solution)/shard_map/ppermute | solution.py:851
  828.3 33.0 %collective-permute-start.67 = (bf16[4,128,1024]{2,1,0:T(8,128)(2,1)S(1)}, bf16[4,128,1024]{2,1,0:T(8,128)(2,1)S(1)}, u32[]{:S(2)}, u32[]{:S(2)}) collective-permute-start(bf16[4,128,1024]{2,1,0:T(8,128)(2,1)S(1)} %add_convert_fusion.3), channel_id=1, source_target_pairs={{0,8},{8,0},{16,24},{24,16},{1,9},{9,1},{17,25},{25,17},{2,10},{10... | collective-permute-start | bytes 3145736 | tf_op jit(solution)/shard_map/ppermute | solution.py:851
  892.3 44.6 %collective-permute-start.76 = (bf16[512,1024]{1,0:T(8,128)(2,1)}, bf16[512,1024]{1,0:T(8,128)(2,1)S(1)}, u32[]{:S(2)}, u32[]{:S(2)}) collective-permute-start(bf16[512,1024]{1,0:T(8,128)(2,1)} %fusion.2.refs_1_), channel_id=1, source_target_pairs={{0,1},{1,0},{4,5},{5,4},{2,3},{3,2},{6,7},{7,6},{8,9},{9,8},{12,13... | collective-permute-start | bytes 3145736 | tf_op jit(solution)/shard_map/ppermute | solution.py:851
  947.9 38.3 %collective-permute-start.83 = (bf16[512,1024]{1,0:T(8,128)(2,1)}, bf16[512,1024]{1,0:T(8,128)(2,1)S(1)}, u32[]{:S(2)}, u32[]{:S(2)}) collective-permute-start(bf16[512,1024]{1,0:T(8,128)(2,1)} %fusion.1), channel_id=1, source_target_pairs={{0,0},{2,4},{4,2},{6,6},{1,1},{3,5},{5,3},{7,7},{8,8},{10,12},{12,... | collective-permute-start | bytes 3145736 | tf_op jit(solution)/shard_map/ppermute | solution.py:855
  (179 other events, 1703.6 us)

commit v7 on v6

--- a/solution.py
+++ b/solution.py
@@ -193,22 +193,42 @@
 
     def copies(self, s):
         slot = lax.rem(s, 2)
+        plain, early, late = [], [], []
         for k in range(2):
-            main, far = self.refs[2 * k : 2 * k + 2]
-            for r in range(4):
+            own, near_x, near_y, far_a, far_b = self.refs[5 * k : 5 * k + 5]
+
+            def copy(source, r, k=k):
                 row = ((self.scal[S_Q] ^ r) * 2 + (self.scal[S_C] ^ k)) * ROWS
-                source = far.at[s, self.matrix] if r == 3 else main.at[r, s, self.matrix]
-                yield pltpu.make_async_copy(
+                return pltpu.make_async_copy(
                     source, self.buffer.at[slot, pl.ds(pl.multiple_of(row, ROWS), ROWS), :], self.sems.at[slot, 4 * k + r]
                 )
 
+            for r, ref in enumerate((own, near_x, near_y)):
+                plain.append(copy(ref.at[s, self.matrix], r))
+            early.append(copy(far_a.at[jnp.minimum(s, 1), self.matrix], 3))
+            late.append(copy(far_b.at[jnp.maximum(s - 2, 0), self.matrix], 3))
+        return plain, early, late
+
+    def each(self, s, act):
+        plain, early, late = self.copies(s)
+        for copy in plain:
+            act(copy)
+
+        @pl.when(s < 2)
+        def _():
+            for copy in early:
+                act(copy)
+
+        @pl.when(s >= 2)
+        def _():
+            for copy in late:
+                act(copy)
+
     def start(self, s):
-        for copy in self.copies(s):
-            copy.start()
+        self.each(s, lambda copy: copy.start())
 
     def wait(self, s):
-        for copy in self.copies(s):
-            copy.wait()
+        self.each(s, lambda copy: copy.wait())
 
     def turn(self, s, count):
         @pl.when(s == 0)
@@ -247,7 +267,7 @@
     def body(scal_ref, prev_ref, *refs):
         part_refs, refs = refs[: len(parts)], refs[len(parts) :]
         vec_ref, bias_ref, refs = refs[0], refs[1], refs[2:]
-        pieces, (n_ref, low_ref, inv_ref, act_ref, slope_ref, buffer, sems) = refs[:4], refs[4:]
+        pieces, (n_ref, low_ref, inv_ref, act_ref, slope_ref, buffer, sems) = refs[:10], refs[10:]
         s = pl.program_id(0)
         stream = Streamed(pieces, matrix, buffer, sems, scal_ref)
         stream.turn(s, count)
@@ -274,7 +294,7 @@
     return call(
         flow, body, (count,),
         [full((tokens, D))] + [part_spec(part) for part in parts]
-        + [full((TABLE, D)), pl.BlockSpec((1, 1, width), lambda s, scal_ref: (scal_ref[S_Z] ^ away(s), 0, 0))] + [ANY] * 4,
+        + [full((TABLE, D)), pl.BlockSpec((1, 1, width), lambda s, scal_ref: (scal_ref[S_Z] ^ away(s), 0, 0))] + [ANY] * 10,
         [full((tokens, D)), full((tokens, D)), full((tokens, 128)), column, column],
         [sds((tokens, D), F32), sds((tokens, D), BF16), sds((tokens, 128), F32)] + [sds((tokens, FF), BF16)] * 2,
         piece_shapes(width), [prev, *parts, vec, bias, *weight], 2 * tokens * D * FF,
@@ -287,7 +307,7 @@
     width = FF // count
 
     def body(scal_ref, act_ref, prev_ref, vec_ref, *refs):
-        pieces, (n_ref, low_ref, inv_ref, buffer, sems, acc) = refs[:4], refs[4:]
+        pieces, (n_ref, low_ref, inv_ref, buffer, sems, acc) = refs[:10], refs[10:]
         s = pl.program_id(0)
         stream = Streamed(pieces, matrix, buffer, sems, scal_ref)
         stream.turn(s, count)
@@ -312,7 +332,7 @@
 
     return call(
         flow, body, (count,),
-        [pl.BlockSpec((tokens, width), lambda s, _: (0, s)), full((tokens, D)), full((TABLE, D))] + [ANY] * 4,
+        [pl.BlockSpec((tokens, width), lambda s, _: (0, s)), full((tokens, D)), full((TABLE, D))] + [ANY] * 10,
         [full((tokens, D)), full((tokens, D)), full((tokens, 128))],
         [sds((tokens, D), F32), sds((tokens, D), BF16), sds((tokens, 128), F32)],
         piece_shapes(width) + [pltpu.VMEM((tokens, D), F32)], [act, prev, vec, *weight], 2 * tokens * D * FF,
@@ -325,7 +345,7 @@
     width = FF // count
 
     def body(scal_ref, grad_ref, slope_ref, *refs):
-        pieces, (out_ref, sum_ref, buffer, sems) = refs[:4], refs[4:]
+        pieces, (out_ref, sum_ref, buffer, sems) = refs[:10], refs[10:]
         s = pl.program_id(0)
         stream = Streamed(pieces, matrix, buffer, sems, scal_ref)
         stream.turn(s, count)
@@ -342,7 +362,7 @@
 
     column = pl.BlockSpec((tokens, width), lambda s, _: (0, s))
     return call(
-        flow, body, (count,), [full((tokens, D)), column] + [ANY] * 4,
+        flow, body, (count,), [full((tokens, D)), column] + [ANY] * 10,
         [column, pl.BlockSpec((1, 1, width), lambda s, scal_ref: (scal_ref[S_Z] ^ away(s), 0, 0))],
         [sds((tokens, FF), BF16), sds((count, 1, width), F32)], piece_shapes(width), [grad, slope, *weight],
         2 * tokens * D * FF, 2 * (D * FF + tokens * (D + 2 * FF)), "units_back",
@@ -354,7 +374,7 @@
     width = FF // count
 
     def body(scal_ref, gu_ref, res_ref, n_ref, inv_ref, vec_ref, *refs):
-        pieces, (g_ref, low_ref, sums_ref, buffer, sems, acc) = refs[:4], refs[4:]
+        pieces, (g_ref, low_ref, sums_ref, buffer, sems, acc) = refs[:10], refs[10:]
         s = pl.program_id(0)
         stream = Streamed(pieces, matrix, buffer, sems, scal_ref)
         stream.turn(s, count)
@@ -379,7 +399,7 @@
     return call(
         flow, body, (count,),
         [pl.BlockSpec((tokens, width), lambda s, _: (0, s)), full((tokens, D)), full((tokens, D)), full((tokens, 128)),
-         full((TABLE, D))] + [ANY] * 4,
+         full((TABLE, D))] + [ANY] * 10,
         [full((tokens, D)), full((tokens, D)), full((8, D))],
         [sds((tokens, D), F32), sds((tokens, D), BF16), sds((8, D), F32)],
         piece_shapes(width) + [pltpu.VMEM((tokens, D), F32)], [gu, residual, normed, inverse, vec, *weight],
@@ -855,10 +875,6 @@
     return lax.ppermute(values_in, ("c", "zh"), [(2 * a + b, 2 * b + a) for a in range(2) for b in range(2)])
 
 
-def cross(values_in):
-    return lax.ppermute(values_in, ("c", "zh"), [(2 * a + b, 2 * b + 1 - a) for a in range(2) for b in range(2)])
-
-
 def uncross(values_in):
     return lax.ppermute(values_in, ("c", "zh"), [(2 * b + 1 - a, 2 * a + b) for a in range(2) for b in range(2)])
 
@@ -929,6 +945,10 @@
     return bias.reshape(3, -1, PAIR).transpose(1, 0, 2).reshape(1, -1)
 
 
+def with_sibling(shard):
+    return jnp.stack([shard, flip(shard, "c", 1)])
+
+
 def heads_along_x(pair):
     return jnp.stack([pair, flip(pair, "q", 1)])
 
@@ -940,7 +960,7 @@
 
 
 def all_heads_weight(shard, size, heads, zh):
-    pair = jnp.stack([turn(shard), cross(shard)])
+    pair = turn(with_sibling(shard))
     every = order_by(lax.all_gather(pair, "q"), 1, zh, 2)
     count = shard.shape[0] - EXTRA
     weights = every[:, :, :count].reshape(4, 2, ROWS, -1)
@@ -980,13 +1000,13 @@
     every = jnp.stack([every[slot] for slot in SLOTS])
     pieces = []
     for k in range(2):
-        pieces += [jnp.stack([every[:, :, r, k] for r in range(3)]), every[:, :, 3, k]]
+        pieces += [every[:, :, r, k] for r in range(3)] + [every[:2, :, 3, k], every[2:, :, 3, k]]
     return pieces
 
 
 class UnitsWeight:
     def __init__(self, shard):
-        self.shard = shard
+        self.shard, self.theirs = shard, {}
 
     def start_far_z(self):
         self.other = flip(self.shard, "zh", 1)
@@ -1014,16 +1034,13 @@
     def corner(self):
         self.far_a, self.far_b = flip(self.near_y[:2], "q", 1), flip(self.near_x[2:], "q", 2)
 
-    def swap_main(self):
-        self.main = jnp.stack([self.own, self.near_x, self.near_y])
-        self.main_sibling = flip(self.main, "c", 1)
-
-    def swap_corner(self):
-        self.far = jnp.concatenate([self.far_a, self.far_b])
-        self.far_sibling = flip(self.far, "c", 1)
+    def swap(self, *names):
+        for name in names:
+            self.theirs[name] = flip(getattr(self, name), "c", 1)
 
     def pieces(self):
-        return [self.main, self.far, self.main_sibling, self.far_sibling]
+        names = ("own", "near_x", "near_y", "far_a", "far_b")
+        return [getattr(self, name) for name in names] + [self.theirs[name] for name in names]
 
 
 class UnitsGrads:
@@ -1083,19 +1100,7 @@
 
 SMALL_AXES = ("q", MODEL, "c")
 SMALL_STEPS = (("q", 1), ("q", 2), ("zl", 1), ("zh", 1), ("c", 1))
-
-
-def small_step(values_in, step):
-    axis, mask = SMALL_STEPS[step]
-    return jnp.concatenate([values_in, flip(values_in, axis, mask)])
-
-
-def order_small(every, where):
-    every = every.reshape(2, 2, 2, 4, -1)
-    every = every.reshape(2, 4, 4, -1)
-    for axis, position in enumerate(where[::-1]):
-        every = order_by(every, axis, position, every.shape[axis])
-    return every.transpose(1, 2, 0, 3).reshape(16 // 4, 8, -1)
+SMALL_SHAPE = (128, 256)
 
 
 def spread_by_distance(values_in, where):
@@ -1145,10 +1150,13 @@
     cuts = [0]
     for size in sizes:
         cuts.append(cuts[-1] + size)
-    small = jnp.concatenate([piece.reshape(layers, -1) for piece in pieces], axis=1).reshape(1, -1)
-
-    def spread_small(every):
-        every = every.reshape(tz, dp, layers, -1).astype(F32)
+    small = jnp.concatenate([piece.reshape(layers, -1) for piece in pieces], axis=1).reshape(-1)
+    padded = jnp.pad(small, (0, SMALL_SHAPE[0] * SMALL_SHAPE[1] - small.size)).reshape(SMALL_SHAPE)
+    gathered = lax.all_gather(padded, ALL)
+    small_all = gathered.reshape(tz * dp, -1)[:, : small.size]
+
+    def spread_small():
+        every = small_all.reshape(tz, dp, layers, -1).astype(F32)
         parts = [every[..., cuts[i] : cuts[i + 1]] for i in range(3)]
         biases = parts[0].reshape(tz, dp, layers, up_bias.shape[1], -1).transpose(2, 0, 3, 1, 4)
         gain = parts[1].reshape(tz, dp, layers, 2, -1).transpose(2, 3, 1, 0, 4).reshape(layers, 2, D)
@@ -1157,22 +1165,21 @@
         head = jnp.concatenate([jnp.ones((1, D), F32), jnp.zeros((1, D), F32)])
         return biases.reshape(layers, tz, 1, -1), jnp.pad(jnp.concatenate([head, table]), ((0, TABLE - 2 - 6 * layers), (0, 0)))
 
+    up_bias_full, table = spread_small()
     if small_slice:
-        pair = jnp.stack([turn(heads_shard[0]), cross(heads_shard[0])])
+        pair = turn(with_sibling(heads_shard[0]))
         x_low = turn(tokens)
         ends = jnp.cumsum(turn(doc_lengths)[0], dtype=jnp.int32)
         near = heads_along_x(pair)
-        small = small_step(small, 0)
         up0, down0 = UnitsWeight(up_weight[0][None]), UnitsWeight(down_weight[0][None])
         both1 = UnitsWeight(jnp.stack([up_weight[1], down_weight[1]]))
         flow.hold(
-            up0=up0.shard, down0=down0.shard, down0_twin=down0.shard, both1=both1.shard, heads1=heads_shard[1], low=x_low,
-            small=small,
+            up0=up0.shard, down0=down0.shard, down0_twin=down0.shard, both1=both1.shard,
+            heads1=with_sibling(heads_shard[1]), low=x_low,
         )
         gate(flow)
         x_low, up0.shard = flow.free("low"), flow.free("up0")
         up0.far_z()
-        small = small_step(small_step(flow.free("small"), 1), 2)
         weights_of = [heads_along_y(near, bias_size, hz, where, zh)]
     else:
         x_low = turn(tokens)
@@ -1180,7 +1187,6 @@
         weights_of = [all_heads_weight(shard, bias_size, hz, zh) for shard in heads_shard]
         every = [all_units_weight(jnp.stack([up_weight[l], down_weight[l]])) for l in range(layers)]
         top_grad = turn(cotangent)
-        up_bias_full, table = spread_small(lax.all_gather(small, ALL))
 
     prev, prev_gain, prev_shift = x_low, ONE, ZERO
     kept = []
@@ -1189,25 +1195,19 @@
         xs = gather_group(x_low)
         w_heads, bias = weights_of[l]
         if first:
-            flow.wait(up0.two, small)
-            flow.hold(small=small, two=up0.two, two_twin=up0.two)
-        if last:
-            flow.wait(both1.own)
-            flow.hold(own=both1.own)
+            flow.wait(up0.two)
+            flow.hold(two=up0.two, two_twin=up0.two)
         qkv_near = project_in(flow, (xs[0], xs[2]), False, w_heads, in_cols, bias, "project_qkv")
         if first:
             up0.two, down0.shard = flow.free("two"), flow.free("down0")
             up0.start_z()
             down0.start_far_z()
-            small = small_step(flow.free("small"), 3)
+        if last:
+            flow.hold(top=cotangent, own=both1.own)
+        forward(flow, xs, qkv_near)
         if last:
             both1.own = flow.free("own")
             both1.near()
-        if last:
-            flow.hold(top=cotangent)
-        forward(flow, xs, qkv_near)
-        if first:
-            flow.hold(small=small)
         qkv_far = project_in(flow, (xs[1], xs[3]), True, w_heads, in_cols, bias, "project_qkv")
         qkv = (qkv_near, qkv_far)
         if first:
@@ -1217,67 +1217,65 @@
             down0.near_z()
             both1.shard = flow.free("both1")
             both1.far_z()
+            pair = turn(flow.free("heads1"))
         if last:
             top_grad = turn(flow.free("top"))
+            both1.swap("own")
         ctx, wide, lse = attend_forward(flow, ends, qkv)
         if first:
-            flow.wait(up0.near_x, up0.near_y, down0.own, both1.two)
-            flow.hold(both1=both1.two)
+            flow.wait(up0.near_x, up0.near_y)
+            flow.hold(both1=both1.two, down0=down0.own, pair=pair, pair_twin=pair)
             up0.corner()
-            down0.near()
+            up0.swap("own", "near_x", "near_y")
         if last:
             flow.wait(both1.near_x, both1.near_y, top_grad)
-            flow.hold(own=both1.own)
             both1.corner()
+            both1.swap("near_x", "near_y")
         send = project_out(flow, [ctx], (2, 3), w_heads, out_cols, True, "project_attn")
         flow.wait(send)
         keep = project_out(flow, [ctx], (0, 1), w_heads, out_cols, False, "project_attn")
         attn, passed = sum_group(keep, send)
         if first:
-            flow.wait(passed, up0.far_a, up0.far_b)
-            flow.hold(own=up0.own)
+            flow.wait(passed, up0.far_a, up0.far_b, gathered)
             gate(flow)
-            up0.own = flow.free("own")
-            up0.swap_main()
-            up0.swap_corner()
-            up_bias_full, table = spread_small(order_small(small_step(flow.free("small"), 4), where))
+            down0.own = flow.free("down0")
+            up0.swap("far_a", "far_b")
+            down0.near()
+            down0.swap("own")
             flow.wait(down0.near_x, down0.near_y)
             down0.corner()
-            down0.swap_main()
-            shard = flow.free("heads1")
-            pair = jnp.stack([turn(shard), cross(shard)])
+            down0.swap("near_x", "near_y")
+            beside = flip(flow.free("pair"), "q", 1)
             w_up = up0.pieces(), 0
         elif last:
             flow.wait(passed)
+            flow.hold(ends=ends)
             gate(flow)
-            both1.own = flow.free("own")
-            both1.swap_main()
-            flow.hold(far_a=both1.far_a)
+            ends = flow.free("ends")
+            flow.hold(far_a=both1.far_a, far_b=both1.far_b)
             flow.wait(attn[2])
             gate(flow)
-            both1.far_a = flow.free("far_a")
-            both1.swap_corner()
+            both1.far_a, both1.far_b = flow.free("far_a"), flow.free("far_b")
+            both1.swap("far_a", "far_b")
             w_up, w_down = (both1.pieces(), 0), (both1.pieces(), 1)
         else:
             w_up, w_down = (every[l], 0), (every[l], 1)
         used = (prev_gain, prev_shift, shift_row(l, 0), gain_row(l, 0), shift_row(l, 1))
         n1, hs, r1, act, slope = norm_up(flow, prev, attn, table, used, *w_up, up_bias_full[l], tz)
         if first:
+            flow.wait(n1, beside)
+            flow.hold(far_a=down0.far_a, far_b=down0.far_b)
+            gate(flow)
+            down0.far_a, down0.far_b = flow.free("far_a"), flow.free("far_b")
+            down0.swap("far_a", "far_b")
             both1.two = flow.free("both1")
-            flow.wait(n1)
-            flow.hold(far_a=down0.far_a, pair=pair, pair_twin=pair)
-            gate(flow)
-            down0.far_a = flow.free("far_a")
-            down0.swap_corner()
-            beside = flip(flow.free("pair"), "q", 1)
             both1.near_z()
+            near = jnp.stack([flow.free("pair_twin"), beside])
+            weights_of.append(heads_along_y(near, bias_size, hz, where, zh))
             w_down = down0.pieces(), 0
         used = (gain_row(l, 0), shift_row(l, 1), shift_row(l, 2), gain_row(l, 1), shift_row(l, 3))
         n2, y_low, r2 = down_norm(flow, act, *w_down, n1, table, used, tz)
         kept.append((xs, qkv, ctx, wide, lse, n1, hs, r1, act, slope, n2, r2, w_heads, w_up, w_down))
-        if first:
-            near = jnp.stack([flow.free("pair_twin"), beside])
-            weights_of.append(heads_along_y(near, bias_size, hz, where, zh))
         x_low, prev, prev_gain, prev_shift = y_low, n2, gain_row(l, 1), shift_row(l, 3)
     layer_output = turn(x_low)
 
@@ -1378,20 +1376,22 @@
     small_sums = jnp.stack(small_grads, axis=2).reshape(tz, dp, -1)
     if small_slice:
         heads.along_x()
-        flow.wait(back[2], units.last)
+        small_sums = fold_small(spread_by_distance(small_sums, where), 0, 1)
+        flow.wait(back[2])
         flow.hold(small=small_sums, got=heads.got, own=units.own)
         gate(flow)
         small_sums, heads.got, units.own = flow.free("small"), flow.free("got"), flow.free("own")
         input_grad = turn(add(g1, back[0], back[1][0], back[2]).astype(BF16))
         heads.along_y()
-        small_sums = fold_small(spread_by_distance(small_sums, where), 0, 2)
+        small_sums = fold_small(small_sums, 1, 2)
         flow.wait(heads.got)
-        flow.hold(small=small_sums, grad=input_grad)
+        flow.hold(small=small_sums, own=units.own)
         gate(flow)
-        small_sums, input_grad = flow.free("small"), flow.free("grad")
+        units.own = flow.free("own")
+        small_sums = fold_small(flow.free("small"), 2, 3)
         halves = heads.halves(zh)
         d_heads = jnp.stack([add(turn(halves[0]), uncross(halves[1])), add(*done)])
-        small_out = fold_small(small_sums, 2, 5).reshape(layers, -1)
+        small_out = fold_small(small_sums, 3, 5).reshape(layers, -1)
     else:
         halves = [member.halves(zh) for member in heads_of]
         d_heads = jnp.stack([add(turn(half[0]), uncross(half[1])) for half in halves])
@@ -1413,12 +1413,13 @@
     local_squares = sum(jnp.sum(member * member) for member in all_grads)
     entry_count = LAYERS * (4 * D * D + 2 * D * FF + FF + 8 * D)
     if small_slice:
-        local_squares = jnp.broadcast_to(local_squares, (8, 128))
+        flow.hold(squares=jnp.broadcast_to(local_squares, (8, 128)), grad=input_grad, output=layer_output)
+        flow.hold(**{f"out{i}": member for i, member in enumerate(all_grads)})
+        gate(flow)
+        local_squares, input_grad, layer_output = flow.free("squares"), flow.free("grad"), flow.free("output")
+        all_grads = [flow.free(f"out{i}") for i in range(len(all_grads))]
     grad_rms = jnp.sqrt(sum_all(local_squares) / entry_count)
-    return (
-        layer_output, input_grad, qkv_grad, qv_bias_grad, out_grad, up_grad, up_bias_grad, down_grad, gains_grad,
-        shifts_grad, grad_rms,
-    )
+    return (layer_output, input_grad, *all_grads, grad_rms)
 
 
 def solution(mesh):

time: 1040 us -> 1000 us (0.962)
  starting transfers between devices: 145 us -> 103 us
  other arithmetic: 86.6 us -> 68.4 us
  between operations: 10 us -> 23.2 us
    ppermute x9, starting transfers between devices: 58.2 us -> 34.9 us  [turn(): lax.ppermute(values_in, ('c', 'zh'), [(2 * a + b, 2 * b + a) for a in ran...]
    ppermute x83 -> x89, starting transfers between devices: 86.1 us -> 67.7 us  [flip(): lax.ppermute(values_in, axes, [(a, a ^ mask) for a in range(lax.axis_size...]
    ppermute x2 -> x0, waiting for transfers between devices: 14.8 us -> none  [cross(): lax.ppermute(values_in, ('c', 'zh'), [(2 * a + b, 2 * b + 1 - a) for a in...]
    ppermute x83 -> x89, waiting for transfers between devices: 156 us -> 169 us  [flip(): lax.ppermute(values_in, axes, [(a, a ^ mask) for a in range(lax.axis_size...]
    unnamed x250 -> x211, local copies, waits for them, and re-layouts: 43.5 us -> 39.2 us
    pallas_call x49 -> x50, Pallas kernels: 496 us -> 497 us  [call(): pl.pallas_call(wrapped, grid_spec=pltpu.PrefetchScalarGridSpec(num_scalar...]
  transfers between devices with their start and end apart: 96 -> 101, of which waited for: 41 -> 42; matrix products, arithmetic and copies ran while one was open for 11% -> 12% of each run, Pallas kernels for 40% -> 42%
where the time goes in v7:
time: 1000 us; the launch traced here: 990 us
  Pallas kernels  497 us (50%)
  waiting for transfers between devices  217 us (22%)
  starting transfers between devices  103 us (10%)
  local copies, waits for them, and re-layouts  81 us (8%)
  other arithmetic  68.4 us (7%)
  between operations  23.2 us (2%)
    pallas_call x50, Pallas kernels, call(): pl.pallas_call(wrapped, grid_spec=pltpu.PrefetchScalarGridSpec(num_scalar...  497 us
    ppermute x89, waiting for transfers between devices, flip(): lax.ppermute(values_in, axes, [(a, a ^ mask) for a in range(lax.axis_size...  169 us
    ppermute x89, starting transfers between devices, flip(): lax.ppermute(values_in, axes, [(a, a ^ mask) for a in range(lax.axis_size...  67.7 us
    ppermute x9, waiting for transfers between devices, turn(): lax.ppermute(values_in, ('c', 'zh'), [(2 * a + b, 2 * b + a) for a in ran...  48.4 us
    unnamed x211, local copies, waits for them, and re-layouts  39.2 us
    ppermute x9, starting transfers between devices, turn(): lax.ppermute(values_in, ('c', 'zh'), [(2 * a + b, 2 * b + a) for a in ran...  34.9 us
  transfers between devices with their start and end apart: 101, of which 42 were waited for; matrix products, arithmetic and copies ran while one was open for 12% of the time, Pallas kernels for 42%

profile of v7, /device:TPU:1, one launch (start us, length us, event | category | flops | bytes accessed | tf_op | source)
XLA Modules:
  0.0 990.0 jit_solution(6035436466551540812)
XLA Ops:
  18.2 13.9 %collective-permute-done.5 = bf16[2,144,1024]{2,1,0:T(8,128)(2,1)S(1)} collective-permute-done((bf16[2,144,1024]{2,1,0:T(8,128)(2,1)S(1)}, bf16[2,144,1024]{2,1,0:T(8,128)(2,1)S(1)}, u32[]{:S(2)}, u32[]{:S(2)}) %collective-permute-start.5) | collective-permute-done | bytes 589856 | tf_op jit(solution)/shard_map/ppermute | solution.py:875
  65.5 10.8 %collective-permute-done.2 = bf16[1,128,1024]{2,1,0:T(8,128)(2,1)} collective-permute-done((bf16[1,128,1024]{2,1,0:T(8,128)(2,1)}, bf16[1,128,1024]{2,1,0:T(8,128)(2,1)}, u32[]{:S(2)}, u32[]{:S(2)}) %collective-permute-start.2) | collective-permute-done | bytes 262176 | tf_op jit(solution)/shard_map/ppermute | solution.py:871
  127.0 28.4 %attend_forward.2 = (bf16[4,512,256]{2,1,0:T(8,128)(2,1)}, f32[4,512,256]{2,1,0:T(8,128)}, f32[4,8,512]{2,1,0:T(8,128)}) custom-call(s32[5]{0:T(128)} %stack.176.refs_0_, s32[4]{0:T(128)} %bitcast.285, bf16[2,512,768]{2,1,0:T(8,128)(2,1)} %get-tuple-element.155.refs_1_.refs_2_.refs_4_.refs_8_, bf16[2,512,768]{2,1,0:T(8,128)(2,1)} %get-tuple-element.171.refs_3_.refs_5_.refs_9_), custom_call_target="tpu_custom_call" | custom-call | flops 14000000000 | bytes 1024 | tf_op jit(solution)/shard_map/attend_forward/pallas_call | solution.py:80
  200.0 19.5 %collective-permute-done.22.refs_2_.refs_6_.refs_5_ = bf16[4,1,128,1024]{3,2,1,0:T(8,128)(2,1)} collective-permute-done((bf16[4,1,128,1024]{3,2,1,0:T(8,128)(2,1)}, bf16[4,1,128,1024]{3,2,1,0:T(8,128)(2,1)}, u32[]{:S(2)}, u32[]{:S(2)}) %collective-permute-start.22) | collective-permute-done | bytes 1048608 | tf_op jit(solution)/shard_map/ppermute | solution.py:871
  235.4 18.9 %norm_up.2 = (f32[512,1024]{1,0:T(8,128)}, bf16[512,1024]{1,0:T(8,128)(2,1)}, f32[512,128]{1,0:T(8,128)}, bf16[512,4096]{1,0:T(8,128)(2,1)}, bf16[512,4096]{1,0:...) custom-call(s32[5]{0:T(128)} %stack.176.refs_0_, ...), custom_call_target="tpu_custom_call", output_to_operand_aliasing={{5}: (3, {}), {6}: (4, {})} | custom-call | flops 7000000000 | bytes 1024 | tf_op jit(solution)/shard_map/norm_up/pallas_call | solution.py:80
  259.9 14.4 %down_norm.2 = (f32[512,1024]{1,0:T(8,128)}, bf16[512,1024]{1,0:T(8,128)(2,1)}, f32[512,128]{1,0:T(8,128)}) custom-call(s32[5]{0:T(128)} %stack.176.refs_0_, bf16[512,4096]{1,0:T(8,128)(2,1)} %get-tuple-element.187.refs_1_.refs_5_.refs_3_, f32[512,1024]{1,0:T(8,128)} %get-tuple-element.188.refs_1_.refs_2_.refs_4_, ...), custom_call_target="tpu_custom_call" | custom-call | flops 7000000000 | bytes 1024 | tf_op jit(solution)/shard_map/down_norm/pallas_call | solution.py:80
  294.3 9.8 collective-permute-done.40.refs_4_
  318.9 28.8 %attend_forward.3 = (bf16[4,512,256]{2,1,0:T(8,128)(2,1)}, f32[4,512,256]{2,1,0:T(8,128)}, f32[4,8,512]{2,1,0:T(8,128)}) custom-call(s32[5]{0:T(128)} %stack.176.refs_0_, s32[4]{0:T(128)} %bitcast.286, bf16[2,512,768]{2,1,0:T(8,128)(2,1)} %project_qkv.6.refs_1_.refs_2_.refs_3_, bf16[2,512,768]{2,1,0:T(8,128)(2,1)} %get-tuple-element.201.refs_3_.refs_4_), custom_call_target="tpu_custom_call" | custom-call | flops 14000000000 | bytes 1024 | tf_op jit(solution)/shard_map/attend_forward/pallas_call | solution.py:80
  374.0 13.2 %collective-permute-done.47.refs_2_ = bf16[2,2,128,1024]{3,2,1,0:T(8,128)(2,1)S(1)} collective-permute-done((bf16[2,2,128,1024]{3,2,1,0:T(8,128)(2,1)}, bf16[2,2,128,1024]{3,2,1,0:T(8,128)(2,1)S(1)}, u32[]{:S(2)}, u32[]{:S(2)}) %collective-permute-start.47) | collective-permute-done | bytes 1048608 | tf_op jit(solution)/shard_map/ppermute | solution.py:871
  388.7 8.6 collective-permute-done.46.refs_1_.refs_4_
  404.6 19.1 %norm_up.3 = (f32[512,1024]{1,0:T(8,128)}, bf16[512,1024]{1,0:T(8,128)(2,1)}, f32[512,128]{1,0:T(8,128)}, bf16[512,4096]{1,0:T(8,128)(2,1)}, bf16[512,4096]{1,0:T(8,128)(2,1)}) custom-call(s32[5]{0:T(128)} %stack.176.refs_0_, f32[512,1024]{1,0:T(8,128)} %get-tuple-element.204.refs_1_.refs_6_, bf16[512,1024]{1,0:T(8,128)(2,1)} %get-tuple-element.205.refs_2_, ...), custom_call_target="tpu_custom_call" | custom-call | flops 7000000000 | bytes 1024 | tf_op jit(solution)/shard_map/norm_up/pallas_call | solution.py:80
  423.7 14.3 %down_norm.3 = (f32[512,1024]{1,0:T(8,128)}, bf16[512,1024]{1,0:T(8,128)(2,1)}, f32[512,128]{1,0:T(8,128)}) custom-call(s32[5]{0:T(128)} %stack.176.refs_0_, bf16[512,4096]{1,0:T(8,128)(2,1)} %get-tuple-element.208.refs_1_.refs_3_, f32[512,1024]{1,0:T(8,128)} %get-tuple-element.209.refs_2_.refs_4_, ...), custom_call_target="tpu_custom_call" | custom-call | flops 7000000000 | bytes 1024 | tf_op jit(solution)/shard_map/down_norm/pallas_call | solution.py:80
  446.1 11.5 %units_back.2 = (bf16[512,4096]{1,0:T(8,128)(2,1)}, f32[4,1,1024]{2,1,0:T(1,128)}) custom-call(s32[5]{0:T(128)} %stack.176.refs_0_, bf16[512,1024]{1,0:T(8,128)(2,1)} %get-tuple-element.213.refs_1_.refs_2_, bf16[512,4096]{1,0:T(8,128)(2,1)} %get-tuple-element.214.refs_2_, bf16[4,2,128,1024]{3,2,1,0:T(8,128)(2,1)} %get-tuple-element.197.refs_7_.refs_4_.refs_3_, ...), custom_call_target="tpu_custom_call" | custom-call | flops 7000000000 | bytes 1024 | tf_op jit(solution)/shard_map/units_back/pallas_call | solution.py:80
  457.6 8.5 collective-permute-done.54.refs_1_
  467.2 15.0 %up_back.2 = (f32[512,1024]{1,0:T(8,128)}, bf16[512,1024]{1,0:T(8,128)(2,1)}, f32[8,1024]{1,0:T(8,128)}, bf16[512,1024]{1,0:T(8,128)(2,1)}) custom-call(s32[5]{0:T(128)} %stack.176.refs_0_, bf16[512,1024]{1,0:T(8,128)(2,1)} %copy-done.12, bf16[512,4096]{1,0:T(8,128)(2,1)} %get-tuple-element.215.refs_2_.refs_5_, ...), custom_call_target="tpu_custom_call", output_to_operand_aliasing={{3}: (1, {})} | custom-call | flops 7000000000 | bytes 1024 | tf_op jit(solution)/shard_map/up_back/pallas_call | solution.py:80
  482.3 12.7 %grads_theirs.2.refs_1_.refs_2_ = bf16[4,8,128,1024]{3,2,1,0:T(8,128)(2,1)} custom-call(s32[5]{0:T(128)} %stack.176.refs_0_, bf16[512,1024]{1,0:T(8,128)(2,1)} %get-tuple-element.218.refs_1_.refs_10_, bf16[512,1024]{1,0:T(8,128)(2,1)} %get-tuple-element.213.refs_1_.refs_2_, bf16[512,4096]{1,0:T(8,128)(2,1)} %get-tuple-element.208.refs_1_.refs_3_, ...), custom_call_target="tpu_custom_call" | custom-call | flops 70000000 | bytes 1024 | tf_op jit(solution)/shard_map/grads_theirs/pallas_call | solution.py:80
  514.5 29.6 %attend_backward.4.refs_2_.refs_1_.refs_14_ = bf16[4,512,384]{2,1,0:T(8,128)(2,1)} custom-call(s32[5]{0:T(128)} %stack.176.refs_0_, s32[4]{0:T(128)} %gate.17.refs_1_, bf16[2,512,768]{2,1,0:T(8,128)(2,1)} %project_qkv.6.refs_1_.refs_2_.refs_3_, bf16[2,512,768]{2,1,0:T(8,128)(2,1)} %get-tuple-element.201.refs_3_.refs_4_, ...), custom_call_target="tpu_custom_call" | custom-call | flops 10499999744 | bytes 1024 | tf_op jit(solution)/shard_map/attend_backward/pallas_call | solution.py:80
  544.0 29.8 %attend_backward.5.refs_2_.refs_3_.refs_15_ = bf16[4,512,384]{2,1,0:T(8,128)(2,1)} custom-call(s32[5]{0:T(128)} %stack.176.refs_0_, s32[4]{0:T(128)} %gate.17.refs_1_, bf16[4,512,384]{2,1,0:T(8,128)(2,1)} %attend_backward.4.refs_2_.refs_1_.refs_14_, bf16[2,512,768]{2,1,0:T(8,128)(2,1)} %project_qkv.6.refs_1_.refs_2_.refs_3_, ...), custom_call_target="tpu_custom_call" | custom-call | flops 10499999744 | bytes 1024 | tf_op jit(solution)/shard_map/attend_backward/pallas_call | solution.py:80
  591.6 15.8 %grads_mine.2 = (bf16[8,128,1024]{2,1,0:T(8,128)(2,1)}, bf16[8,128,1024]{2,1,0:T(8,128)(2,1)}, bf16[8,128,1024]{2,1,0:T(8,128)(2,1)}, bf16[4,128,1024]{2,1,0:T(8,128)(2,1)}, bf16[4,128,1024]{2,1,0:T(8,128)(2,1)}) custom-call(s32[5]{0:T(128)} %stack.176.refs_0_, bf16[512,1024]{1,0:T(8,128)(2,1)} %copy-done.33, ...), custom_call_target="tpu_custom_call" | custom-call | flops 70000000 | bytes 1024 | tf_op jit(solution)/shard_map/grads_mine/pallas_call | solution.py:80
  608.2 13.1 %heads_grad.2 = (bf16[2,2,128,1024]{3,2,1,0:T(8,128)(2,1)}, bf16[2,2,128,1024]{3,2,1,0:T(8,128)(2,1)}, f32[1,768]{1,0:T(1,128)}) custom-call(s32[5]{0:T(128)} %stack.176.refs_0_, bf16[8,128,1024]{2,1,0:T(8,128)(2,1)} %get-tuple-element.227.refs_1_, bf16[8,128,1024]{2,1,0:T(8,128)(2,1)} %get-tuple-element.225.refs_2_, ...), custom_call_target="tpu_custom_call" | custom-call | flops 70000000 | bytes 1024 | tf_op jit(solution)/shard_map/heads_grad/pallas_call | solution.py:80
  621.3 7.7 sum_norm_back.1
  629.0 11.5 %units_back.3 = (bf16[512,4096]{1,0:T(8,128)(2,1)}, f32[4,1,1024]{2,1,0:T(1,128)}) custom-call(s32[5]{0:T(128)} %stack.176.refs_0_, bf16[512,1024]{1,0:T(8,128)(2,1)} %get-tuple-element.234.refs_1_.refs_4_.refs_2_, bf16[512,4096]{1,0:T(8,128)(2,1)} %get-tuple-element.236.refs_2_, bf16[4,1,128,1024]{3,2,1,0:T(8,128)(2,1)} %get-tuple-element.183.refs_4_.refs_3_, ...), custom_call_target="tpu_custom_call" | custom-call | flops 7000000000 | bytes 1024 | tf_op jit(solution)/shard_map/units_back/pallas_call | solution.py:80
  640.5 13.8 %collective-permute-done.60.refs_1_ = bf16[8,128,1024]{2,1,0:T(8,128)(2,1)S(1)} collective-permute-done((bf16[8,128,1024]{2,1,0:T(8,128)(2,1)}, bf16[8,128,1024]{2,1,0:T(8,128)(2,1)S(1)}, u32[]{:S(2)}, u32[]{:S(2)}) %collective-permute-start.60) | collective-permute-done | bytes 2097184 | tf_op jit(solution)/shard_map/ppermute | solution.py:871
  656.4 12.8 %grads_theirs.3 = (bf16[4,8,128,1024]{3,2,1,0:T(8,128)(2,1)}, bf16[2,2,128,1024]{3,2,1,0:T(8,128)(2,1)}) custom-call(s32[5]{0:T(128)} %stack.176.refs_0_, bf16[8,128,1024]{2,1,0:T(8,128)(2,1)} %copy-done.20, bf16[8,128,1024]{2,1,0:T(8,128)(2,1)} %copy-done.23, ...), custom_call_target="tpu_custom_call", output_to_operand_aliasing={{1}: (3, {})} | custom-call | flops 70000000 | bytes 1024 | tf_op jit(solution)/shard_map/grads_theirs/pallas_call | solution.py:80
  675.4 15.3 %up_back.3 = (f32[512,1024]{1,0:T(8,128)}, bf16[512,1024]{1,0:T(8,128)(2,1)}, f32[8,1024]{1,0:T(8,128)}) custom-call(s32[5]{0:T(128)} %stack.176.refs_0_, bf16[4,8,128,1024]{3,2,1,0:T(8,128)(2,1)} %get-tuple-element.238.refs_1_, bf16[512,4096]{1,0:T(8,128)(2,1)} %get-tuple-element.237.refs_7_.refs_2_.refs_5_, f32[512,1024]{1,0:T(8,128)} %get-tuple-element.239.refs_3_, ...), custom_call_target="tpu_custom_call" | custom-call | flops 7000000000 | bytes 1024 | tf_op jit(solution)/shard_map/up_back/pallas_call | solution.py:80
  696.2 15.9 %grads_mine.3 = (bf16[8,128,1024]{2,1,0:T(8,128)(2,1)}, bf16[8,128,1024]{2,1,0:T(8,128)(2,1)}, bf16[8,128,1024]{2,1,0:T(8,128)(2,1)}, bf16[4,128,1024]{2,1,0:T(8,128)(2,1)}, bf16[4,128,1024]{2,1,0:T(8,128)(2,1)}) custom-call(s32[5]{0:T(128)} %stack.176.refs_0_, bf16[512,1024]{1,0:T(8,128)(2,1)} %get-tuple-element.241.refs_1_.refs_6_, ...), custom_call_target="tpu_custom_call" | custom-call | flops 70000000 | bytes 1024 | tf_op jit(solution)/shard_map/grads_mine/pallas_call | solution.py:80
  753.0 29.5 %attend_backward.6 = (bf16[4,512,384]{2,1,0:T(8,128)(2,1)}, bf16[4,128,1024]{2,1,0:T(8,128)(2,1)}, bf16[4,128,1024]{2,1,0:T(8,128)(2,1)}) custom-call(s32[5]{0:T(128)} %stack.176.refs_0_, s32[4]{0:T(128)} %gate.17.refs_1_, bf16[4,128,1024]{2,1,0:T(8,128)(2,1)} %get-tuple-element.242.refs_7_.refs_2_, ...), custom_call_target="tpu_custom_call", output_to_operand_aliasing={{1}: (2, {}), {2}: (3, {})} | custom-call | flops 10499999744 | bytes 1024 | tf_op jit(solution)/shard_map/attend_backward/pallas_call | solution.py:80
  793.5 30.0 %attend_backward.7 = (bf16[4,512,384]{2,1,0:T(8,128)(2,1)}, bf16[8,128,1024]{2,1,0:T(8,128)(2,1)}) custom-call(s32[5]{0:T(128)} %stack.176.refs_0_, s32[4]{0:T(128)} %gate.17.refs_1_, bf16[4,512,384]{2,1,0:T(8,128)(2,1)} %get-tuple-element.253.refs_2_.refs_6_.refs_3_.refs_10_, ...), custom_call_target="tpu_custom_call", output_to_operand_aliasing={{1}: (7, {})} | custom-call | flops 10499999744 | bytes 1024 | tf_op jit(solution)/shard_map/attend_backward/pallas_call | solution.py:80
  854.8 13.0 %heads_grad.3 = (bf16[2,2,128,1024]{3,2,1,0:T(8,128)(2,1)}, bf16[2,2,128,1024]{3,2,1,0:T(8,128)(2,1)}, f32[1,768]{1,0:T(1,128)}) custom-call(s32[5]{0:T(128)} %stack.176.refs_0_, bf16[512,1024]{1,0:T(8,128)(2,1)} %fusion.2.refs_1_, bf16[512,1024]{1,0:T(8,128)(2,1)} %get-tuple-element.154.refs_8_.refs_5_.refs_2_, ...), custom_call_target="tpu_custom_call" | custom-call | flops 70000000 | bytes 1024 | tf_op jit(solution)/shard_map/heads_grad/pallas_call | solution.py:80
  876.4 17.4 %collective-permute-done.82.refs_3_ = bf16[2,2,128,1024]{3,2,1,0:T(8,128)(2,1)S(1)} collective-permute-done((bf16[2,2,128,1024]{3,2,1,0:T(8,128)(2,1)}, bf16[2,2,128,1024]{3,2,1,0:T(8,128)(2,1)S(1)}, u32[]{:S(2)}, u32[]{:S(2)}) %collective-permute-start.82) | collective-permute-done | bytes 1048608 | tf_op jit(solution)/shard_map/ppermute | solution.py:871
  893.8 7.7 collective-permute-done.80.refs_1_
  937.4 9.4 collective-permute-done.84
  (644 shorter events, 447.4 us)
Async XLA Ops:
  7.2 186.3 %all-gather.2.cloned.1.call-start = ((), (), s32[]{:S(2)}) async-start(), calls=%async_computation | async-start | bytes 2162688 | tf_op jit(solution)/shard_map/all_gather | solution.py:1155
  41.7 38.1 %collective-permute-start.7 = (bf16[2,2,144,1024]{3,2,1,0:T(8,128)(2,1)S(1)}, bf16[2,2,144,1024]{3,2,1,0:T(8,128)(2,1)S(1)}, u32[]{:S(2)}, u32[]{:S(2)}) collective-permute-start(bf16[2,2,144,1024]{3,2,1,0:T(8,128)(2,1)S(1)} %pad_maximum_fusion.1.refs_11_.refs_8_.refs_7_.refs_3_.refs_4_.refs_5_), channel_id=1, source_target_pairs={{0,16},{8,24},{16,0},{24,8},{1,17},{9,25},{17,1},{25,9},{2,18},{10... | collective-permute-start | bytes 3538952 | tf_op jit(solution)/shard_map/ppermute | solution.py:871
  119.2 47.9 %collective-permute-start.12 = (bf16[4,1,128,1024]{3,2,1,0:T(8,128)(2,1)}, bf16[4,1,128,1024]{3,2,1,0:T(8,128)(2,1)}, u32[]{:S(2)}, u32[]{:S(2)}) collective-permute-start(bf16[4,1,128,1024]{3,2,1,0:T(8,128)(2,1)} %constant_dynamic-update-slice_fusion.refs_11_.refs_7_), channel_id=1, source_target_pairs={{0,16},{8,24},{16,0},{24,8},{1,17},{9,25},{17,1},{25,9},{2,18},{10... | collective-permute-start | bytes 3145736 | tf_op jit(solution)/shard_map/ppermute | solution.py:871
  120.5 46.6 %collective-permute-start.11 = (bf16[4,1,128,1024]{3,2,1,0:T(8,128)(2,1)}, bf16[4,1,128,1024]{3,2,1,0:T(8,128)(2,1)}, u32[]{:S(2)}, u32[]{:S(2)}) collective-permute-start(bf16[4,1,128,1024]{3,2,1,0:T(8,128)(2,1)} %constant_dynamic-update-slice_fusion.refs_11_.refs_7_), channel_id=1, source_target_pairs={{0,8},{8,0},{16,24},{24,16},{1,9},{9,1},{17,25},{25,17},{2,10},{10... | collective-permute-start | bytes 3145736 | tf_op jit(solution)/shard_map/ppermute | solution.py:871
  120.8 38.4 %collective-permute-start.15 = (bf16[2,1,128,1024]{3,2,1,0:T(8,128)(2,1)S(1)}, bf16[2,1,128,1024]{3,2,1,0:T(8,128)(2,1)S(1)}, u32[]{:S(2)}, u32[]{:S(2)}) collective-permute-start(bf16[2,1,128,1024]{3,2,1,0:T(8,128)(2,1)S(1)} %pad_maximum_fusion.11), channel_id=1, source_target_pairs={{0,1},{1,0},{2,3},{3,2},{4,5},{5,4},{6,7},{7,6},{8,9},{9,8},{10,11... | collective-permute-start | bytes 1572872 | tf_op jit(solution)/shard_map/ppermute | solution.py:871
  123.3 34.8 %collective-permute-start.13 = (bf16[2,128,1024]{2,1,0:T(8,128)(2,1)S(1)}, bf16[2,128,1024]{2,1,0:T(8,128)(2,1)S(1)}, u32[]{:S(2)}, u32[]{:S(2)}) collective-permute-start(bf16[2,128,1024]{2,1,0:T(8,128)(2,1)S(1)} %copy-done.8), channel_id=1, source_target_pairs={{0,2},{2,0},{1,3},{3,1},{4,6},{6,4},{5,7},{7,5},{8,10},{10,8},{9,1... | collective-permute-start | bytes 1572872 | tf_op jit(solution)/shard_map/ppermute | solution.py:871
  123.4 42.9 %collective-permute-start.16 = (bf16[2,144,1024]{2,1,0:T(8,128)(2,1)S(1)}, bf16[2,144,1024]{2,1,0:T(8,128)(2,1)S(1)}, u32[]{:S(2)}, u32[]{:S(2)}) collective-permute-start(bf16[2,144,1024]{2,1,0:T(8,128)(2,1)S(1)} %copy-done.10), channel_id=1, source_target_pairs={{0,0},{2,4},{4,2},{6,6},{1,1},{3,5},{5,3},{7,7},{8,8},{10,12},{12,... | collective-permute-start | bytes 1769480 | tf_op jit(solution)/shard_map/ppermute | solution.py:875
  195.2 33.1 %collective-permute-start.25 = (bf16[4,1,128,1024]{3,2,1,0:T(8,128)(2,1)}, bf16[4,1,128,1024]{3,2,1,0:T(8,128)(2,1)}, u32[]{:S(2)}, u32[]{:S(2)}) collective-permute-start(bf16[4,1,128,1024]{3,2,1,0:T(8,128)(2,1)} %collective-permute-done.11.refs_1_.refs_12_.refs_8_), channel_id=1, source_target_pairs={{0,4},{4,0},{1,5},{5,1},{2,6},{6,2},{3,7},{7,3},{8,12},{12,8},{9,1... | collective-permute-start | bytes 3145736 | tf_op jit(solution)/shard_map/ppermute | solution.py:871
  195.8 37.4 %collective-permute-start.23 = (bf16[512,1024]{1,0:T(8,128)(2,1)S(1)}, bf16[512,1024]{1,0:T(8,128)(2,1)}, u32[]{:S(2)}, u32[]{:S(2)}) collective-permute-start(bf16[512,1024]{1,0:T(8,128)(2,1)S(1)} %copy-done.46), channel_id=1, source_target_pairs={{0,1},{1,0},{4,5},{5,4},{2,3},{3,2},{6,7},{7,6},{8,9},{9,8},{12,13... | collective-permute-start | bytes 3145736 | tf_op jit(solution)/shard_map/ppermute | solution.py:871
  197.7 34.2 %collective-permute-start.29 = (bf16[2,144,1024]{2,1,0:T(8,128)(2,1)S(1)}, bf16[2,144,1024]{2,1,0:T(8,128)(2,1)S(1)}, u32[]{:S(2)}, u32[]{:S(2)}) collective-permute-start(bf16[2,144,1024]{2,1,0:T(8,128)(2,1)S(1)} %copy-done.14), channel_id=1, source_target_pairs={{0,8},{8,0},{16,24},{24,16},{1,9},{9,1},{17,25},{25,17},{2,10},{10... | collective-permute-start | bytes 1769480 | tf_op jit(solution)/shard_map/ppermute | solution.py:871
  219.5 37.2 %collective-permute-start.32 = (bf16[4,1,128,1024]{3,2,1,0:T(8,128)(2,1)S(1)}, bf16[4,1,128,1024]{3,2,1,0:T(8,128)(2,1)}, u32[]{:S(2)}, u32[]{:S(2)}) collective-permute-start(bf16[4,1,128,1024]{3,2,1,0:T(8,128)(2,1)S(1)} %copy-done.9), channel_id=1, source_target_pairs={{0,4},{4,0},{1,5},{5,1},{2,6},{6,2},{3,7},{7,3},{8,12},{12,8},{9,1... | collective-permute-start | bytes 3145736 | tf_op jit(solution)/shard_map/ppermute | solution.py:871
  223.5 34.4 %collective-permute-start.34 = (bf16[4,1,128,1024]{3,2,1,0:T(8,128)(2,1)}, bf16[4,1,128,1024]{3,2,1,0:T(8,128)(2,1)}, u32[]{:S(2)}, u32[]{:S(2)}) collective-permute-start(bf16[4,1,128,1024]{3,2,1,0:T(8,128)(2,1)} %collective-permute-done.22.refs_2_.refs_6_.refs_5_), channel_id=1, source_target_pairs={{0,4},{4,0},{1,5},{5,1},{2,6},{6,2},{3,7},{7,3},{8,12},{12,8},{9,1... | collective-permute-start | bytes 3145736 | tf_op jit(solution)/shard_map/ppermute | solution.py:871
  306.7 47.5 %collective-permute-start.42 = (bf16[4,2,128,1024]{3,2,1,0:T(8,128)(2,1)}, bf16[4,2,128,1024]{3,2,1,0:T(8,128)(2,1)}, u32[]{:S(2)}, u32[]{:S(2)}) collective-permute-start(bf16[4,2,128,1024]{3,2,1,0:T(8,128)(2,1)} %get-tuple-element.197.refs_7_.refs_4_.refs_3_), channel_id=1, source_target_pairs={{0,16},{8,24},{16,0},{24,8},{1,17},{9,25},{17,1},{25,9},{2,18},{10... | collective-permute-start | bytes 6291464 | tf_op jit(solution)/shard_map/ppermute | solution.py:871
  306.7 47.5 %collective-permute-start.41 = (bf16[4,2,128,1024]{3,2,1,0:T(8,128)(2,1)}, bf16[4,2,128,1024]{3,2,1,0:T(8,128)(2,1)}, u32[]{:S(2)}, u32[]{:S(2)}) collective-permute-start(bf16[4,2,128,1024]{3,2,1,0:T(8,128)(2,1)} %get-tuple-element.197.refs_7_.refs_4_.refs_3_), channel_id=1, source_target_pairs={{0,8},{8,0},{16,24},{24,16},{1,9},{9,1},{17,25},{25,17},{2,10},{10... | collective-permute-start | bytes 6291464 | tf_op jit(solution)/shard_map/ppermute | solution.py:871
  317.0 30.7 %collective-permute-start.44 = (bf16[512,1024]{1,0:T(8,128)(2,1)}, bf16[512,1024]{1,0:T(8,128)(2,1)S(1)}, u32[]{:S(2)}, u32[]{:S(2)}) collective-permute-start(bf16[512,1024]{1,0:T(8,128)(2,1)} %get-tuple-element.200), channel_id=1, source_target_pairs={{0,0},{2,4},{4,2},{6,6},{1,1},{3,5},{5,3},{7,7},{8,8},{10,12},{12,... | collective-permute-start | bytes 3145736 | tf_op jit(solution)/shard_map/ppermute | solution.py:875
  513.3 77.4 %collective-permute-start.59 = (bf16[4,8,128,1024]{3,2,1,0:T(8,128)(2,1)}, bf16[4,8,128,1024]{3,2,1,0:T(8,128)(2,1)}, u32[]{:S(2)}, u32[]{:S(2)}) collective-permute-start(bf16[4,8,128,1024]{3,2,1,0:T(8,128)(2,1)} %get-tuple-element.224), channel_id=1, source_target_pairs={{0,4},{4,0},{1,5},{5,1},{2,6},{6,2},{3,7},{7,3},{8,12},{12,8},{9,1... | collective-permute-start | bytes 25165832 | tf_op jit(solution)/shard_map/ppermute | solution.py:871
  590.6 30.7 %collective-permute-start.62 = (bf16[512,1024]{1,0:T(8,128)(2,1)S(1)}, bf16[512,1024]{1,0:T(8,128)(2,1)}, u32[]{:S(2)}, u32[]{:S(2)}) collective-permute-start(bf16[512,1024]{1,0:T(8,128)(2,1)S(1)} %fusion.3.refs_1_), channel_id=1, source_target_pairs={{0,1},{1,0},{4,5},{5,4},{2,3},{3,2},{6,7},{7,6},{8,9},{9,8},{12,13... | collective-permute-start | bytes 3145736 | tf_op jit(solution)/shard_map/ppermute | solution.py:871
  607.4 46.9 %collective-permute-start.60 = (bf16[8,128,1024]{2,1,0:T(8,128)(2,1)}, bf16[8,128,1024]{2,1,0:T(8,128)(2,1)S(1)}, u32[]{:S(2)}, u32[]{:S(2)}) collective-permute-start(bf16[8,128,1024]{2,1,0:T(8,128)(2,1)} %get-tuple-element.225.refs_2_), channel_id=1, source_target_pairs={{0,8},{8,0},{16,24},{24,16},{1,9},{9,1},{17,25},{25,17},{2,10},{10... | collective-permute-start | bytes 6291464 | tf_op jit(solution)/shard_map/ppermute | solution.py:871
  607.4 47.0 %collective-permute-start.61 = (bf16[8,128,1024]{2,1,0:T(8,128)(2,1)}, bf16[8,128,1024]{2,1,0:T(8,128)(2,1)S(1)}, u32[]{:S(2)}, u32[]{:S(2)}) collective-permute-start(bf16[8,128,1024]{2,1,0:T(8,128)(2,1)} %get-tuple-element.226.refs_3_), channel_id=1, source_target_pairs={{0,16},{8,24},{16,0},{24,8},{1,17},{9,25},{17,1},{25,9},{2,18},{10... | collective-permute-start | bytes 6291464 | tf_op jit(solution)/shard_map/ppermute | solution.py:871
  673.2 38.9 %collective-permute-start.66 = (bf16[4,128,1024]{2,1,0:T(8,128)(2,1)}, bf16[4,128,1024]{2,1,0:T(8,128)(2,1)}, u32[]{:S(2)}, u32[]{:S(2)}) collective-permute-start(bf16[4,128,1024]{2,1,0:T(8,128)(2,1)} %add_convert_fusion.4), channel_id=1, source_target_pairs={{0,16},{8,24},{16,0},{24,8},{1,17},{9,25},{17,1},{25,9},{2,18},{10... | collective-permute-start | bytes 3145736 | tf_op jit(solution)/shard_map/ppermute | solution.py:871
  674.6 38.3 %collective-permute-start.65 = (bf16[4,128,1024]{2,1,0:T(8,128)(2,1)}, bf16[4,128,1024]{2,1,0:T(8,128)(2,1)}, u32[]{:S(2)}, u32[]{:S(2)}) collective-permute-start(bf16[4,128,1024]{2,1,0:T(8,128)(2,1)} %add_convert_fusion.5), channel_id=1, source_target_pairs={{0,8},{8,0},{16,24},{24,16},{1,9},{9,1},{17,25},{25,17},{2,10},{10... | collective-permute-start | bytes 3145736 | tf_op jit(solution)/shard_map/ppermute | solution.py:871
  692.0 39.3 %collective-permute-start.64 = (bf16[512,1024]{1,0:T(8,128)(2,1)}, bf16[512,1024]{1,0:T(8,128)(2,1)}, u32[]{:S(2)}, u32[]{:S(2)}) collective-permute-start(bf16[512,1024]{1,0:T(8,128)(2,1)} %get-tuple-element.241.refs_1_.refs_6_), channel_id=1, source_target_pairs={{0,4},{1,5},{4,0},{5,1},{2,6},{3,7},{6,2},{7,3},{8,12},{9,13},{12,... | collective-permute-start | bytes 3145736 | tf_op jit(solution)/shard_map/ppermute | solution.py:871
  712.1 70.5 %collective-permute-start.72 = (bf16[8,128,1024]{2,1,0:T(8,128)(2,1)}, bf16[8,128,1024]{2,1,0:T(8,128)(2,1)}, u32[]{:S(2)}, u32[]{:S(2)}) collective-permute-start(bf16[8,128,1024]{2,1,0:T(8,128)(2,1)} %get-tuple-element.246.refs_5_), channel_id=1, source_target_pairs={{0,8},{8,0},{16,24},{24,16},{1,9},{9,1},{17,25},{25,17},{2,10},{10... | collective-permute-start | bytes 6291464 | tf_op jit(solution)/shard_map/ppermute | solution.py:871
  727.5 59.6 %collective-permute-start.70 = (bf16[8,128,1024]{2,1,0:T(8,128)(2,1)}, bf16[8,128,1024]{2,1,0:T(8,128)(2,1)}, u32[]{:S(2)}, u32[]{:S(2)}) collective-permute-start(bf16[8,128,1024]{2,1,0:T(8,128)(2,1)} %get-tuple-element.247.refs_6_), channel_id=1, source_target_pairs={{0,16},{8,24},{16,0},{24,8},{1,17},{9,25},{17,1},{25,9},{2,18},{10... | collective-permute-start | bytes 6291464 | tf_op jit(solution)/shard_map/ppermute | solution.py:871
  731.3 59.0 %collective-permute-start.74 = (bf16[4,128,1024]{2,1,0:T(8,128)(2,1)}, bf16[4,128,1024]{2,1,0:T(8,128)(2,1)S(1)}, u32[]{:S(2)}, u32[]{:S(2)}) collective-permute-start(bf16[4,128,1024]{2,1,0:T(8,128)(2,1)} %add_convert_fusion.1), channel_id=1, source_target_pairs={{0,1},{1,0},{2,3},{3,2},{4,5},{5,4},{6,7},{7,6},{8,9},{9,8},{10,11... | collective-permute-start | bytes 3145736 | tf_op jit(solution)/shard_map/ppermute | solution.py:871
  741.5 82.0 %collective-permute-start.78 = (bf16[128,1024]{1,0:T(8,128)(2,1)}, bf16[128,1024]{1,0:T(8,128)(2,1)S(1)}, u32[]{:S(2)}, u32[]{:S(2)}) collective-permute-start(bf16[128,1024]{1,0:T(8,128)(2,1)} %get-tuple-element.354), channel_id=1, source_target_pairs={{2,0},{6,2},{0,4},{4,6},{3,1},{7,3},{1,5},{5,7},{10,8},{14,10},{8,... | collective-permute-start | bytes 786440 | tf_op jit(solution)/shard_map/ppermute | solution.py:879
  741.8 81.7 %collective-permute-start.77 = (bf16[128,1024]{1,0:T(8,128)(2,1)S(1)}, bf16[128,1024]{1,0:T(8,128)(2,1)S(1)}, u32[]{:S(2)}, u32[]{:S(2)}) collective-permute-start(bf16[128,1024]{1,0:T(8,128)(2,1)S(1)} %get-tuple-element.355), channel_id=1, source_target_pairs={{0,0},{2,4},{4,2},{6,6},{1,1},{3,5},{5,3},{7,7},{8,8},{10,12},{12,... | collective-permute-start | bytes 786440 | tf_op jit(solution)/shard_map/ppermute | solution.py:875
  785.6 37.9 %collective-permute-start.73 = (bf16[4,128,1024]{2,1,0:T(8,128)(2,1)}, bf16[4,128,1024]{2,1,0:T(8,128)(2,1)S(1)}, u32[]{:S(2)}, u32[]{:S(2)}) collective-permute-start(bf16[4,128,1024]{2,1,0:T(8,128)(2,1)} %add_convert_fusion.2), channel_id=1, source_target_pairs={{0,16},{8,24},{16,0},{24,8},{1,17},{9,25},{17,1},{25,9},{2,18},{10... | collective-permute-start | bytes 3145736 | tf_op jit(solution)/shard_map/ppermute | solution.py:871
  789.6 33.9 %collective-permute-start.71 = (bf16[4,128,1024]{2,1,0:T(8,128)(2,1)}, bf16[4,128,1024]{2,1,0:T(8,128)(2,1)S(1)}, u32[]{:S(2)}, u32[]{:S(2)}) collective-permute-start(bf16[4,128,1024]{2,1,0:T(8,128)(2,1)} %add_convert_fusion.3), channel_id=1, source_target_pairs={{0,8},{8,0},{16,24},{24,16},{1,9},{9,1},{17,25},{25,17},{2,10},{10... | collective-permute-start | bytes 3145736 | tf_op jit(solution)/shard_map/ppermute | solution.py:871
  853.9 47.6 %collective-permute-start.80 = (bf16[512,1024]{1,0:T(8,128)(2,1)}, bf16[512,1024]{1,0:T(8,128)(2,1)S(1)}, u32[]{:S(2)}, u32[]{:S(2)}) collective-permute-start(bf16[512,1024]{1,0:T(8,128)(2,1)} %fusion.2.refs_1_), channel_id=1, source_target_pairs={{0,1},{1,0},{4,5},{5,4},{2,3},{3,2},{6,7},{7,6},{8,9},{9,8},{12,13... | collective-permute-start | bytes 3145736 | tf_op jit(solution)/shard_map/ppermute | solution.py:871
  873.4 45.2 %collective-permute-start.91 = (bf16[2,128,1024]{2,1,0:T(8,128)(2,1)}, bf16[2,128,1024]{2,1,0:T(8,128)(2,1)}, u32[]{:S(2)}, u32[]{:S(2)}) collective-permute-start(bf16[2,128,1024]{2,1,0:T(8,128)(2,1)} %add_convert_fusion.6), channel_id=1, source_target_pairs={{0,2},{2,0},{1,3},{3,1},{4,6},{6,4},{5,7},{7,5},{8,10},{10,8},{9,1... | collective-permute-start | bytes 1572872 | tf_op jit(solution)/shard_map/ppermute | solution.py:871
  908.8 47.6 %collective-permute-start.92 = (bf16[512,1024]{1,0:T(8,128)(2,1)}, bf16[512,1024]{1,0:T(8,128)(2,1)}, u32[]{:S(2)}, u32[]{:S(2)}) collective-permute-start(bf16[512,1024]{1,0:T(8,128)(2,1)} %fusion.1), channel_id=1, source_target_pairs={{0,0},{2,4},{4,2},{6,6},{1,1},{3,5},{5,3},{7,7},{8,8},{10,12},{12,... | collective-permute-start | bytes 3145736 | tf_op jit(solution)/shard_map/ppermute | solution.py:875
  (166 other events, 1707.5 us)
Sparse Core Ops, SparseCore 0:
  101.8 75.3 all-gather.1

commit v8 on v7

--- a/solution.py
+++ b/solution.py
@@ -23,7 +23,7 @@
 ALL = ("zh", "zl", "q", "c")
 VMEM_LIMIT = 56 * 1024 * 1024
 TIMES = {
-    "gate": 0.1, "norm_up": 20.0, "down_norm": 20.0, "units_back": 20.0, "up_back": 20.0, "norm_back": 6.0,
+    "gate": 0.1, "norm_up": 20.0, "down_norm": 20.0, "units_back": 45.0, "up_back": 20.0, "norm_back": 6.0,
     "sum_norm_back": 20.0, "grads_theirs": 0.2, "grads_mine": 0.2, "project_qkv": 0.2, "project_gc": 0.2,
     "project_attn": 0.2, "project_gx": 0.2, "heads_grad": 0.2, "attend_forward": 40.0, "attend_backward": 30.0,
 }
@@ -340,20 +340,33 @@
     )
 
 
-def units_back(flow, grad, weight, matrix, slope, count):
-    tokens = grad.shape[0]
+def units_back(flow, residual, parts, normed, inverse, vec, gain, weight, matrix, slope, count):
+    tokens = residual.shape[0]
     width = FF // count
 
-    def body(scal_ref, grad_ref, slope_ref, *refs):
-        pieces, (out_ref, sum_ref, buffer, sems) = refs[:10], refs[10:]
+    def body(scal_ref, res_ref, *refs):
+        part_refs, refs = refs[: len(parts)], refs[len(parts) :]
+        n_ref, inv_ref, vec_ref, slope_ref, refs = refs[0], refs[1], refs[2], refs[3], refs[4:]
+        pieces, (g_ref, low_ref, sums_ref, out_ref, sum_ref, buffer, sems) = refs[:10], refs[10:]
         s = pl.program_id(0)
         stream = Streamed(pieces, matrix, buffer, sems, scal_ref)
         stream.turn(s, count)
+
+        @pl.when(s == 0)
+        def _():
+            def grad(rows):
+                total = read(res_ref, rows)
+                for part in part_refs:
+                    total = total + read(part, rows)
+                return total
+
+            norm_backward(grad, tokens, n_ref, inv_ref, vec_ref, gain, g_ref, low_ref, sums_ref)
+
         stream.wait(s)
         slot = lax.rem(s, 2)
         sums = {}
         for rows, cols in tiles(tokens, width):
-            low = (mm(grad_ref[rows, :], buffer[slot, :, cols]) * slope_ref[rows, cols].astype(F32)).astype(BF16)
+            low = (mm(low_ref[rows, :], buffer[slot, :, cols]) * slope_ref[rows, cols].astype(F32)).astype(BF16)
             out_ref[rows, cols] = low
             part = fold_rows(low.astype(F32))
             sums[cols.start] = sums[cols.start] + part if cols.start in sums else part
@@ -362,10 +375,14 @@
 
     column = pl.BlockSpec((tokens, width), lambda s, _: (0, s))
     return call(
-        flow, body, (count,), [full((tokens, D)), column] + [ANY] * 10,
-        [column, pl.BlockSpec((1, 1, width), lambda s, scal_ref: (scal_ref[S_Z] ^ away(s), 0, 0))],
-        [sds((tokens, FF), BF16), sds((count, 1, width), F32)], piece_shapes(width), [grad, slope, *weight],
-        2 * tokens * D * FF, 2 * (D * FF + tokens * (D + 2 * FF)), "units_back",
+        flow, body, (count,),
+        [full((tokens, D))] + [part_spec(part) for part in parts]
+        + [full((tokens, D)), full((tokens, 128)), full((TABLE, D)), column] + [ANY] * 10,
+        [full((tokens, D)), full((tokens, D)), full((8, D)), column,
+         pl.BlockSpec((1, 1, width), lambda s, scal_ref: (scal_ref[S_Z] ^ away(s), 0, 0))],
+        [sds((tokens, D), F32), sds((tokens, D), BF16), sds((8, D), F32), sds((tokens, FF), BF16),
+         sds((count, 1, width), F32)],
+        piece_shapes(width), [residual, *parts, normed, inverse, vec, slope, *weight], 0, 0, "units_back",
     )
 
 
@@ -404,43 +421,6 @@
         [sds((tokens, D), F32), sds((tokens, D), BF16), sds((8, D), F32)],
         piece_shapes(width) + [pltpu.VMEM((tokens, D), F32)], [gu, residual, normed, inverse, vec, *weight],
         2 * tokens * D * FF, 2 * (D * FF + tokens * (8 * D + FF)), "up_back",
-    )
-
-
-def norm_back(flow, grad, normed, inverse, vec, gain):
-    tokens = grad.shape[0]
-
-    def body(scal_ref, grad_ref, n_ref, inv_ref, vec_ref, g_ref, low_ref, sums_ref):
-        norm_backward(lambda rows: read(grad_ref, rows), tokens, n_ref, inv_ref, vec_ref, gain, g_ref, low_ref, sums_ref)
-
-    return call(
-        flow, body, (1,), [full((tokens, D)), full((tokens, D)), full((tokens, 128)), full((TABLE, D))],
-        [full((tokens, D)), full((tokens, D)), full((8, D))],
-        [sds((tokens, D), F32), sds((tokens, D), BF16), sds((8, D), F32)], [], [grad, normed, inverse, vec],
-        20 * tokens * D, 12 * tokens * D, "norm_back",
-    )
-
-
-def sum_norm_back(flow, residual, parts, normed, inverse, vec, gain):
-    tokens = residual.shape[0]
-
-    def body(scal_ref, res_ref, *refs):
-        part_refs, (n_ref, inv_ref, vec_ref, g_ref, low_ref, sums_ref) = refs[: len(parts)], refs[len(parts) :]
-
-        def grad(rows):
-            total = read(part_refs[0], rows)
-            for part in part_refs[1:]:
-                total = total + read(part, rows)
-            return res_ref[rows, :] + total
-
-        norm_backward(grad, tokens, n_ref, inv_ref, vec_ref, gain, g_ref, low_ref, sums_ref)
-
-    return call(
-        flow, body, (1,), [full((tokens, D))] + [part_spec(part) for part in parts]
-        + [full((tokens, D)), full((tokens, 128)), full((TABLE, D))],
-        [full((tokens, D)), full((tokens, D)), full((8, D))],
-        [sds((tokens, D), F32), sds((tokens, D), BF16), sds((8, D), F32)], [],
-        [residual, *parts, normed, inverse, vec], 20 * tokens * D, 22 * tokens * D, "sum_norm_back",
     )
 
 
@@ -787,7 +767,7 @@
     per = chunk // BQ
 
     def body(
-        scal_ref, ends_ref, near_ref, far_ref, grad_near, grad_far, wide_ref, lse_ref, out_ref, qh, kh, gh, kt, vt, qt, gt,
+        scal_ref, ends_ref, near_ref, far_ref, grad_near, grad_far, wide_ref, lse_ref, out_ref, qh, gh, kt, vt, qt, gt,
         gq, gk, gv,
     ):
         step = pl.program_id(0)
@@ -804,7 +784,6 @@
                 for h in range(2):
                     cols = slice(h * HD, (h + 1) * HD)
                     qh[h, rows, :] = queries[:, cols]
-                    kh[h, rows, :] = keys[:, cols]
                     gh[h, rows, :] = back[:, cols]
                 kt[j] = keys.T
                 vt[j] = block[:, 2 * PAIR :].T
@@ -826,7 +805,6 @@
             logs.append(sums[:, 2 * pair + h : 2 * pair + h + 1])
 
         def block(b, allowed):
-            keys = pl.ds(pl.multiple_of(b * chunk, chunk), chunk)
             for h in range(2):
                 part = slice(h * HD, (h + 1) * HD)
                 score = mm(qh[h, rows, :], kt[b, part, :])
@@ -837,12 +815,11 @@
                 grad_score = (weight * (grad_weight - inner[h])).astype(BF16)
                 gv[b, part, :] += mm(gt[step, part, :], weight.astype(BF16))
                 gk[b, part, :] += mm(qt[step, part, :], grad_score)
-                gq[h] += mm(grad_score, kh[h, keys, :])
+                gq[part, :] += mm(kt[b, part, :], grad_score, NT)
 
         over_keys(ends_ref, start, chunk, False, block)
         place = pl.ds(pl.multiple_of((step % per) * BQ, BQ), BQ)
-        for h in range(2):
-            out_ref[step // per, place, h * HD : (h + 1) * HD] = (gq[h] * HD**-0.5).astype(BF16)
+        out_ref[step // per, place, :PAIR] = (gq[...] * HD**-0.5).T.astype(BF16)
 
         @pl.when(step == steps - 1)
         def _():
@@ -858,10 +835,10 @@
         + [pl.BlockSpec((1, BQ, PAIR), lambda i, *_: (i // per, i % per, pair)),
            pl.BlockSpec((1, 8, BQ), lambda i, *_: (i, 0, 0))],
         full(out), sds(out, BF16),
-        [pltpu.VMEM((2, SEQLEN, HD), BF16)] * 3
+        [pltpu.VMEM((2, SEQLEN, HD), BF16)] * 2
         + [pltpu.VMEM((count, PAIR, chunk), BF16)] * 2
         + [pltpu.VMEM((steps, PAIR, BQ), BF16)] * 2
-        + [pltpu.VMEM((2, BQ, HD), F32)]
+        + [pltpu.VMEM((PAIR, BQ), F32)]
         + [pltpu.VMEM((count, PAIR, chunk), F32)] * 2,
         [*qkv, *grads, wide, lse], 0, 0, "attend_backward", (flow.scal, ends),
     )
@@ -1073,7 +1050,8 @@
 
     def near_z(self):
         half = self.count
-        self.there = flip(add(self.own[half:], self.late_x, self.from_y[:half]).astype(BF16), "zl", 1)
+        self.passing = add(self.own[half:], self.late_x, self.from_y[:half]).astype(BF16)
+        self.there = flip(self.passing, "zl", 1)
         return [self.there]
 
     def far_z(self):
@@ -1175,7 +1153,7 @@
         both1 = UnitsWeight(jnp.stack([up_weight[1], down_weight[1]]))
         flow.hold(
             up0=up0.shard, down0=down0.shard, down0_twin=down0.shard, both1=both1.shard,
-            heads1=with_sibling(heads_shard[1]), low=x_low,
+            heads1=heads_shard[1], low=x_low,
         )
         gate(flow)
         x_low, up0.shard = flow.free("low"), flow.free("up0")
@@ -1205,6 +1183,8 @@
         if last:
             flow.hold(top=cotangent, own=both1.own)
         forward(flow, xs, qkv_near)
+        if first:
+            pair = with_sibling(flow.free("heads1"))
         if last:
             both1.own = flow.free("own")
             both1.near()
@@ -1217,16 +1197,18 @@
             down0.near_z()
             both1.shard = flow.free("both1")
             both1.far_z()
-            pair = turn(flow.free("heads1"))
+            pair = turn(pair)
         if last:
             top_grad = turn(flow.free("top"))
             both1.swap("own")
         ctx, wide, lse = attend_forward(flow, ends, qkv)
         if first:
             flow.wait(up0.near_x, up0.near_y)
-            flow.hold(both1=both1.two, down0=down0.own, pair=pair, pair_twin=pair)
+            flow.hold(both1=both1.two, down0=down0.own, pair_twin=pair)
+            flow.wait(pair)
+            beside = flip(pair, "q", 1)
             up0.corner()
-            up0.swap("own", "near_x", "near_y")
+            up0.swap("own")
         if last:
             flow.wait(both1.near_x, both1.near_y, top_grad)
             both1.corner()
@@ -1236,16 +1218,16 @@
         keep = project_out(flow, [ctx], (0, 1), w_heads, out_cols, False, "project_attn")
         attn, passed = sum_group(keep, send)
         if first:
-            flow.wait(passed, up0.far_a, up0.far_b, gathered)
+            flow.wait(passed, gathered)
+            flow.hold(near_x=up0.near_x, near_y=up0.near_y)
             gate(flow)
-            down0.own = flow.free("down0")
-            up0.swap("far_a", "far_b")
+            down0.own, up0.near_x, up0.near_y = flow.free("down0"), flow.free("near_x"), flow.free("near_y")
+            up0.swap("near_x", "near_y", "far_a", "far_b")
             down0.near()
             down0.swap("own")
             flow.wait(down0.near_x, down0.near_y)
             down0.corner()
             down0.swap("near_x", "near_y")
-            beside = flip(flow.free("pair"), "q", 1)
             w_up = up0.pieces(), 0
         elif last:
             flow.wait(passed)
@@ -1279,7 +1261,7 @@
         x_low, prev, prev_gain, prev_shift = y_low, n2, gain_row(l, 1), shift_row(l, 3)
     layer_output = turn(x_low)
 
-    g2, gf, sums2 = norm_back(flow, top_grad, kept[-1][10], kept[-1][11], table, gain_row(layers - 1, 1))
+    residual, back = top_grad, []
     small_grads = [None] * layers
     units_of, heads_of = [None] * layers, [None] * layers
     above = above_heads = None
@@ -1287,7 +1269,9 @@
         top = l == layers - 1
         xs, qkv, ctx, wide, lse, n1, hs, r1, act, slope, n2, r2, w_heads, w_up, w_down = kept[l]
         beside = small_slice and not top
-        gu, up_bias_sum = units_back(flow, gf, *w_down, slope, tz)
+        g2, gf, sums2, gu, up_bias_sum = units_back(
+            flow, residual, back, n2, r2, table, gain_row(l, 1), *w_down, slope, tz
+        )
         units = UnitsGrads(flow, (gf, act), (hs, gu), tz)
         if top:
             flow.hold(output=layer_output)
@@ -1338,8 +1322,8 @@
         gqkv.append(attend_backward(flow, ends, 1, qkv, gcs, wide, lse))
         if beside:
             units.own = flow.free("own")
-            flow.wait(units.late_x, units.late_y, above.last, *done)
             units.near_z()
+            flow.wait(units.passing, units.late_y, above.last, *done)
         send = project_out(flow, gqkv, (2, 3), w_heads, in_cols, True, "project_gx")
         flow.wait(send)
         if beside:
@@ -1352,6 +1336,7 @@
             flow.wait(*units.made)
         elif small_slice:
             units.own = flow.free("own")
+            flow.wait(units.there)
             units.far_z()
         *buckets, qkv_sums = heads_grad(flow, xs, gqkv, gas, ctx)
         heads = HeadsGrad(*buckets)
@@ -1372,7 +1357,7 @@
         if l > 0:
             above, above_heads = units, heads
             flow.wait(heads.send)
-            g2, gf, sums2 = sum_norm_back(flow, g1, back, kept[l - 1][10], kept[l - 1][11], table, gain_row(l - 1, 1))
+            residual = g1
     small_sums = jnp.stack(small_grads, axis=2).reshape(tz, dp, -1)
     if small_slice:
         heads.along_x()

time: 1000 us -> 1040 us (1.040)
  waiting for transfers between devices: 217 us -> 256 us
  starting transfers between devices: 103 us -> 120 us
  Pallas kernels: 497 us -> 481 us
    ppermute x89, waiting for transfers between devices: 169 us -> 199 us  [flip(): lax.ppermute(values_in, axes, [(a, a ^ mask) for a in range(lax.axis_size...]
    pallas_call x50 -> x48, Pallas kernels: 497 us -> 481 us  [call(): pl.pallas_call(wrapped, grid_spec=pltpu.PrefetchScalarGridSpec(num_scalar...]
    unnamed x211 -> x195, local copies, waits for them, and re-layouts: 39.2 us -> 40.6 us
  transfers between devices with their start and end apart: 101 -> 101, of which waited for: 42 -> 36; matrix products, arithmetic and copies ran while one was open for 12% -> 11% of each run, Pallas kernels for 42% -> 39%
where the time goes in v8:
time: 1040 us; the launch traced here: 1030 us
  Pallas kernels  481 us (46%)
  waiting for transfers between devices  256 us (25%)
  starting transfers between devices  120 us (12%)
  local copies, waits for them, and re-layouts  81.1 us (8%)
  other arithmetic  65.9 us (6%)
  between operations  23.3 us (2%)
    pallas_call x48, Pallas kernels, call(): pl.pallas_call(wrapped, grid_spec=pltpu.PrefetchScalarGridSpec(num_scalar...  481 us
    ppermute x89, waiting for transfers between devices, flip(): lax.ppermute(values_in, axes, [(a, a ^ mask) for a in range(lax.axis_size...  199 us
    ppermute x89, starting transfers between devices, flip(): lax.ppermute(values_in, axes, [(a, a ^ mask) for a in range(lax.axis_size...  77.9 us
    ppermute x9, waiting for transfers between devices, turn(): lax.ppermute(values_in, ('c', 'zh'), [(2 * a + b, 2 * b + a) for a in ran...  57.7 us
    unnamed x195, local copies, waits for them, and re-layouts  40.6 us
    ppermute x9, starting transfers between devices, turn(): lax.ppermute(values_in, ('c', 'zh'), [(2 * a + b, 2 * b + a) for a in ran...  36.9 us
  transfers between devices with their start and end apart: 101, of which 36 were waited for; matrix products, arithmetic and copies ran while one was open for 11% of the time, Pallas kernels for 39%

profile of v8, /device:TPU:1, one launch (start us, length us, event | category | flops | bytes accessed | tf_op | source)
XLA Modules:
  0.0 1028.0 jit_solution(16412455110806163319)
XLA Ops:
  18.1 13.9 %collective-permute-done.4 = bf16[2,144,1024]{2,1,0:T(8,128)(2,1)S(1)} collective-permute-done((bf16[2,144,1024]{2,1,0:T(8,128)(2,1)S(1)}, bf16[2,144,1024]{2,1,0:T(8,128)(2,1)S(1)}, u32[]{:S(2)}, u32[]{:S(2)}) %collective-permute-start.4) | collective-permute-done | bytes 589856 | tf_op jit(solution)/shard_map/ppermute | solution.py:852
  65.2 11.1 %collective-permute-done.1 = bf16[1,128,1024]{2,1,0:T(8,128)(2,1)} collective-permute-done((bf16[1,128,1024]{2,1,0:T(8,128)(2,1)}, bf16[1,128,1024]{2,1,0:T(8,128)(2,1)}, u32[]{:S(2)}, u32[]{:S(2)}) %collective-permute-start.1) | collective-permute-done | bytes 262176 | tf_op jit(solution)/shard_map/ppermute | solution.py:848
  109.0 19.6 %collective-permute-done.17 = s32[1,4]{1,0:T(1,128)S(1)} collective-permute-done((s32[1,4]{1,0:T(1,128)S(1)}, s32[1,4]{1,0:T(1,128)S(1)}, u32[]{:S(2)}, u32[]{:S(2)}) %collective-permute-start.17) | collective-permute-done | bytes 48 | tf_op jit(solution)/shard_map/ppermute | solution.py:852
  143.4 28.2 %attend_forward.2 = (bf16[4,512,256]{2,1,0:T(8,128)(2,1)}, f32[4,512,256]{2,1,0:T(8,128)}, f32[4,8,512]{2,1,0:T(8,128)}) custom-call(s32[5]{0:T(128)} %stack.176.refs_0_, s32[4]{0:T(128)} %bitcast.286, bf16[2,512,768]{2,1,0:T(8,128)(2,1)} %get-tuple-element.153.refs_1_.refs_2_.refs_4_.refs_8_, bf16[2,512,768]{2,1,0:T(8,128)(2,1)} %get-tuple-element.168.refs_3_.refs_5_.refs_9_), custom_call_target="tpu_custom_call" | custom-call | flops 14000000000 | bytes 1024 | tf_op jit(solution)/shard_map/attend_forward/pallas_call | solution.py:80
  214.7 15.9 %collective-permute-done.19.refs_1_.refs_5_.refs_11_ = bf16[4,1,128,1024]{3,2,1,0:T(8,128)(2,1)} collective-permute-done((bf16[4,1,128,1024]{3,2,1,0:T(8,128)(2,1)}, bf16[4,1,128,1024]{3,2,1,0:T(8,128)(2,1)}, u32[]{:S(2)}, u32[]{:S(2)}) %collective-permute-start.19) | collective-permute-done | bytes 1048608 | tf_op jit(solution)/shard_map/ppermute | solution.py:848
  239.9 19.0 %norm_up.2 = (f32[512,1024]{1,0:T(8,128)}, bf16[512,1024]{1,0:T(8,128)(2,1)}, f32[512,128]{1,0:T(8,128)}, bf16[512,4096]{1,0:T(8,128)(2,1)}, bf16[512,4096]{1,0:...) custom-call(s32[5]{0:T(128)} %stack.176.refs_0_, ...), custom_call_target="tpu_custom_call", output_to_operand_aliasing={{5}: (3, {}), {6}: (4, {})} | custom-call | flops 7000000000 | bytes 1024 | tf_op jit(solution)/shard_map/norm_up/pallas_call | solution.py:80
  267.0 14.5 %down_norm.2 = (f32[512,1024]{1,0:T(8,128)}, bf16[512,1024]{1,0:T(8,128)(2,1)}, f32[512,128]{1,0:T(8,128)}) custom-call(s32[5]{0:T(128)} %stack.176.refs_0_, bf16[512,4096]{1,0:T(8,128)(2,1)} %get-tuple-element.184.refs_1_.refs_5_.refs_3_, f32[512,1024]{1,0:T(8,128)} %get-tuple-element.185.refs_1_.refs_2_.refs_4_, ...), custom_call_target="tpu_custom_call" | custom-call | flops 7000000000 | bytes 1024 | tf_op jit(solution)/shard_map/down_norm/pallas_call | solution.py:80
  300.3 8.9 collective-permute-done.40.refs_4_
  324.6 28.6 %attend_forward.3 = (bf16[4,512,256]{2,1,0:T(8,128)(2,1)}, f32[4,512,256]{2,1,0:T(8,128)}, f32[4,8,512]{2,1,0:T(8,128)}) custom-call(s32[5]{0:T(128)} %stack.176.refs_0_, s32[4]{0:T(128)} %bitcast.287, bf16[2,512,768]{2,1,0:T(8,128)(2,1)} %project_qkv.6.refs_1_.refs_2_.refs_3_, bf16[2,512,768]{2,1,0:T(8,128)(2,1)} %get-tuple-element.197.refs_3_.refs_4_), custom_call_target="tpu_custom_call" | custom-call | flops 14000000000 | bytes 1024 | tf_op jit(solution)/shard_map/attend_forward/pallas_call | solution.py:80
  381.1 11.1 %collective-permute-done.47.refs_2_ = bf16[2,2,128,1024]{3,2,1,0:T(8,128)(2,1)S(1)} collective-permute-done((bf16[2,2,128,1024]{3,2,1,0:T(8,128)(2,1)}, bf16[2,2,128,1024]{3,2,1,0:T(8,128)(2,1)S(1)}, u32[]{:S(2)}, u32[]{:S(2)}) %collective-permute-start.47) | collective-permute-done | bytes 1048608 | tf_op jit(solution)/shard_map/ppermute | solution.py:848
  394.5 8.5 collective-permute-done.46.refs_1_.refs_4_
  410.2 19.0 %norm_up.3 = (f32[512,1024]{1,0:T(8,128)}, bf16[512,1024]{1,0:T(8,128)(2,1)}, f32[512,128]{1,0:T(8,128)}, bf16[512,4096]{1,0:T(8,128)(2,1)}, bf16[512,4096]{1,0:T(8,128)(2,1)}) custom-call(s32[5]{0:T(128)} %stack.176.refs_0_, f32[512,1024]{1,0:T(8,128)} %get-tuple-element.200.refs_1_.refs_6_, bf16[512,1024]{1,0:T(8,128)(2,1)} %get-tuple-element.201.refs_2_, ...), custom_call_target="tpu_custom_call" | custom-call | flops 7000000000 | bytes 1024 | tf_op jit(solution)/shard_map/norm_up/pallas_call | solution.py:80
  429.2 14.3 %down_norm.3 = (f32[512,1024]{1,0:T(8,128)}, bf16[512,1024]{1,0:T(8,128)(2,1)}, f32[512,128]{1,0:T(8,128)}) custom-call(s32[5]{0:T(128)} %stack.176.refs_0_, bf16[512,4096]{1,0:T(8,128)(2,1)} %get-tuple-element.204.refs_1_.refs_3_, f32[512,1024]{1,0:T(8,128)} %get-tuple-element.205.refs_2_.refs_4_, ...), custom_call_target="tpu_custom_call" | custom-call | flops 7000000000 | bytes 1024 | tf_op jit(solution)/shard_map/down_norm/pallas_call | solution.py:80
  446.3 12.6 %units_back.2 = (f32[512,1024]{1,0:T(8,128)}, bf16[512,1024]{1,0:T(8,128)(2,1)}, f32[8,1024]{1,0:T(8,128)}, bf16[512,4096]{1,0:T(8,128)(2,1)}, f32[4,1,1024]{2,1,0:T(1,128)}) custom-call(s32[5]{0:T(128)} %stack.176.refs_0_, bf16[512,1024]{1,0:T(8,128)(2,1)} %copy-done.66, f32[512,1024]{1,0:T(8,128)} %get-tuple-element.207.refs_2_, ...), custom_call_target="tpu_custom_call" | custom-call | flops 15749999616 | bytes 1024 | tf_op jit(solution)/shard_map/units_back/pallas_call | solution.py:80
  458.9 13.0 %collective-permute-done.54.refs_1_ = bf16[512,1024]{1,0:T(8,128)(2,1)S(1)} collective-permute-done((bf16[512,1024]{1,0:T(8,128)(2,1)}, bf16[512,1024]{1,0:T(8,128)(2,1)S(1)}, u32[]{:S(2)}, u32[]{:S(2)}) %collective-permute-start.54) | collective-permute-done | bytes 1048608 | tf_op jit(solution)/shard_map/ppermute | solution.py:852
  472.9 14.9 %up_back.2 = (f32[512,1024]{1,0:T(8,128)}, bf16[512,1024]{1,0:T(8,128)(2,1)}, f32[8,1024]{1,0:T(8,128)}, bf16[512,1024]{1,0:T(8,128)(2,1)}) custom-call(s32[5]{0:T(128)} %stack.176.refs_0_, bf16[512,1024]{1,0:T(8,128)(2,1)} %copy-done.10, bf16[512,4096]{1,0:T(8,128)(2,1)} %get-tuple-element.210.refs_2_.refs_5_, ...), custom_call_target="tpu_custom_call", output_to_operand_aliasing={{3}: (1, {})} | custom-call | flops 7000000000 | bytes 1024 | tf_op jit(solution)/shard_map/up_back/pallas_call | solution.py:80
  488.0 12.7 %grads_theirs.2.refs_1_.refs_2_ = bf16[4,8,128,1024]{3,2,1,0:T(8,128)(2,1)} custom-call(s32[5]{0:T(128)} %stack.176.refs_0_, bf16[512,1024]{1,0:T(8,128)(2,1)} %get-tuple-element.213.refs_1_.refs_10_, bf16[512,1024]{1,0:T(8,128)(2,1)} %get-tuple-element.214.refs_2_, bf16[512,4096]{1,0:T(8,128)(2,1)} %get-tuple-element.204.refs_1_.refs_3_, ...), custom_call_target="tpu_custom_call" | custom-call | flops 70000000 | bytes 1024 | tf_op jit(solution)/shard_map/grads_theirs/pallas_call | solution.py:80
  516.8 28.2 %attend_backward.4.refs_2_.refs_1_.refs_14_ = bf16[4,512,384]{2,1,0:T(8,128)(2,1)} custom-call(s32[5]{0:T(128)} %stack.176.refs_0_, s32[4]{0:T(128)} %gate.17.refs_1_, bf16[2,512,768]{2,1,0:T(8,128)(2,1)} %project_qkv.6.refs_1_.refs_2_.refs_3_, bf16[2,512,768]{2,1,0:T(8,128)(2,1)} %get-tuple-element.197.refs_3_.refs_4_, ...), custom_call_target="tpu_custom_call" | custom-call | flops 10499999744 | bytes 1024 | tf_op jit(solution)/shard_map/attend_backward/pallas_call | solution.py:80
  544.9 28.5 %attend_backward.5.refs_2_.refs_3_.refs_15_ = bf16[4,512,384]{2,1,0:T(8,128)(2,1)} custom-call(s32[5]{0:T(128)} %stack.176.refs_0_, s32[4]{0:T(128)} %gate.17.refs_1_, bf16[4,512,384]{2,1,0:T(8,128)(2,1)} %attend_backward.4.refs_2_.refs_1_.refs_14_, bf16[2,512,768]{2,1,0:T(8,128)(2,1)} %project_qkv.6.refs_1_.refs_2_.refs_3_, ...), custom_call_target="tpu_custom_call" | custom-call | flops 10499999744 | bytes 1024 | tf_op jit(solution)/shard_map/attend_backward/pallas_call | solution.py:80
  591.2 15.8 %grads_mine.2 = (bf16[8,128,1024]{2,1,0:T(8,128)(2,1)}, bf16[8,128,1024]{2,1,0:T(8,128)(2,1)}, bf16[8,128,1024]{2,1,0:T(8,128)(2,1)}, bf16[4,128,1024]{2,1,0:T(8,128)(2,1)}, bf16[4,128,1024]{2,1,0:T(8,128)(2,1)}) custom-call(s32[5]{0:T(128)} %stack.176.refs_0_, bf16[512,1024]{1,0:T(8,128)(2,1)} %copy-done.35, bf16[512,1024]{1,0:T(8,128)(2,1)} %get-tuple-element.214.refs_2_, ...), custom_call_target="tpu_custom_call" | custom-call | flops 70000000 | bytes 1024 | tf_op jit(solution)/shard_map/grads_mine/pallas_call | solution.py:80
  608.4 13.1 %heads_grad.2 = (bf16[2,2,128,1024]{3,2,1,0:T(8,128)(2,1)}, bf16[2,2,128,1024]{3,2,1,0:T(8,128)(2,1)}, f32[1,768]{1,0:T(1,128)}) custom-call(s32[5]{0:T(128)} %stack.176.refs_0_, bf16[8,128,1024]{2,1,0:T(8,128)(2,1)} %get-tuple-element.223.refs_1_, bf16[8,128,1024]{2,1,0:T(8,128)(2,1)} %get-tuple-element.221.refs_2_, ...), custom_call_target="tpu_custom_call" | custom-call | flops 70000000 | bytes 1024 | tf_op jit(solution)/shard_map/heads_grad/pallas_call | solution.py:80
  622.5 14.1 %units_back.3 = (f32[512,1024]{1,0:T(8,128)}, bf16[512,1024]{1,0:T(8,128)(2,1)}, f32[8,1024]{1,0:T(8,128)}, bf16[512,4096]{1,0:T(8,128)(2,1)}, f32[4,1,1024]{2,1,0:T(1,128)}) custom-call(s32[5]{0:T(128)} %stack.176.refs_0_, bf16[2,2,128,1024]{3,2,1,0:T(8,128)(2,1)} %get-tuple-element.226.refs_1_.refs_3_, f32[512,1024]{1,0:T(8,128)} %get-tuple-element.227.refs_2_, ...), custom_call_target="tpu_custom_call" | custom-call | flops 15749999616 | bytes 1024 | tf_op jit(solution)/shard_map/units_back/pallas_call | solution.py:80
  636.6 17.4 %collective-permute-done.60.refs_1_ = bf16[8,128,1024]{2,1,0:T(8,128)(2,1)S(1)} collective-permute-done((bf16[8,128,1024]{2,1,0:T(8,128)(2,1)}, bf16[8,128,1024]{2,1,0:T(8,128)(2,1)S(1)}, u32[]{:S(2)}, u32[]{:S(2)}) %collective-permute-start.60) | collective-permute-done | bytes 2097184 | tf_op jit(solution)/shard_map/ppermute | solution.py:848
  656.2 12.8 %grads_theirs.3 = (bf16[4,8,128,1024]{3,2,1,0:T(8,128)(2,1)}, bf16[2,2,128,1024]{3,2,1,0:T(8,128)(2,1)}) custom-call(s32[5]{0:T(128)} %stack.176.refs_0_, bf16[8,128,1024]{2,1,0:T(8,128)(2,1)} %copy-done.16, bf16[8,128,1024]{2,1,0:T(8,128)(2,1)} %copy-done.19, ...), custom_call_target="tpu_custom_call", output_to_operand_aliasing={{1}: (3, {})} | custom-call | flops 70000000 | bytes 1024 | tf_op jit(solution)/shard_map/grads_theirs/pallas_call | solution.py:80
  675.4 15.2 %up_back.3 = (f32[512,1024]{1,0:T(8,128)}, bf16[512,1024]{1,0:T(8,128)(2,1)}, f32[8,1024]{1,0:T(8,128)}) custom-call(s32[5]{0:T(128)} %stack.176.refs_0_, bf16[4,8,128,1024]{3,2,1,0:T(8,128)(2,1)} %get-tuple-element.234.refs_1_, bf16[512,4096]{1,0:T(8,128)(2,1)} %get-tuple-element.233.refs_7_.refs_2_.refs_5_, f32[512,1024]{1,0:T(8,128)} %get-tuple-element.235.refs_3_, ...), custom_call_target="tpu_custom_call" | custom-call | flops 7000000000 | bytes 1024 | tf_op jit(solution)/shard_map/up_back/pallas_call | solution.py:80
  702.7 15.9 %grads_mine.3 = (bf16[8,128,1024]{2,1,0:T(8,128)(2,1)}, bf16[8,128,1024]{2,1,0:T(8,128)(2,1)}, bf16[8,128,1024]{2,1,0:T(8,128)(2,1)}, bf16[4,128,1024]{2,1,0:T(8,128)(2,1)}, bf16[4,128,1024]{2,1,0:T(8,128)(2,1)}) custom-call(s32[5]{0:T(128)} %stack.176.refs_0_, bf16[512,1024]{1,0:T(8,128)(2,1)} %get-tuple-element.237.refs_1_.refs_7_, ...), custom_call_target="tpu_custom_call" | custom-call | flops 70000000 | bytes 1024 | tf_op jit(solution)/shard_map/grads_mine/pallas_call | solution.py:80
  735.4 42.0 %collective-permute-done.73.refs_6_ = bf16[2,128,1024]{2,1,0:T(8,128)(2,1)} collective-permute-done((bf16[2,128,1024]{2,1,0:T(8,128)(2,1)}, bf16[2,128,1024]{2,1,0:T(8,128)(2,1)}, u32[]{:S(2)}, u32[]{:S(2)}) %collective-permute-start.73) | collective-permute-done | bytes 524320 | tf_op jit(solution)/shard_map/ppermute | solution.py:848
  792.2 28.2 %attend_backward.6 = (bf16[4,512,384]{2,1,0:T(8,128)(2,1)}, bf16[4,128,1024]{2,1,0:T(8,128)(2,1)}, bf16[4,128,1024]{2,1,0:T(8,128)(2,1)}) custom-call(s32[5]{0:T(128)} %stack.176.refs_0_, s32[4]{0:T(128)} %gate.17.refs_1_, bf16[4,128,1024]{2,1,0:T(8,128)(2,1)} %get-tuple-element.238.refs_7_.refs_2_, ...), custom_call_target="tpu_custom_call", output_to_operand_aliasing={{1}: (2, {}), {2}: (3, {})} | custom-call | flops 10499999744 | bytes 1024 | tf_op jit(solution)/shard_map/attend_backward/pallas_call | solution.py:80
  826.9 28.2 %attend_backward.7 = (bf16[4,512,384]{2,1,0:T(8,128)(2,1)}, bf16[8,128,1024]{2,1,0:T(8,128)(2,1)}) custom-call(s32[5]{0:T(128)} %stack.176.refs_0_, s32[4]{0:T(128)} %gate.17.refs_1_, bf16[4,512,384]{2,1,0:T(8,128)(2,1)} %get-tuple-element.246.refs_2_.refs_6_.refs_3_.refs_11_, ...), custom_call_target="tpu_custom_call", output_to_operand_aliasing={{1}: (7, {})} | custom-call | flops 10499999744 | bytes 1024 | tf_op jit(solution)/shard_map/attend_backward/pallas_call | solution.py:80
  886.9 10.3 %collective-permute-done.80.refs_2_ = bf16[4,128,1024]{2,1,0:T(8,128)(2,1)S(1)} collective-permute-done((bf16[4,128,1024]{2,1,0:T(8,128)(2,1)}, bf16[4,128,1024]{2,1,0:T(8,128)(2,1)S(1)}, u32[]{:S(2)}, u32[]{:S(2)}) %collective-permute-start.80) | collective-permute-done | bytes 1048608 | tf_op jit(solution)/shard_map/ppermute | solution.py:848
  898.2 13.0 %heads_grad.3 = (bf16[2,2,128,1024]{3,2,1,0:T(8,128)(2,1)}, bf16[2,2,128,1024]{3,2,1,0:T(8,128)(2,1)}, f32[1,768]{1,0:T(1,128)}) custom-call(s32[5]{0:T(128)} %stack.176.refs_0_, bf16[512,1024]{1,0:T(8,128)(2,1)} %copy-done.31, bf16[4,128,1024]{2,1,0:T(8,128)(2,1)} %copy-done.28, bf16[512,1024]{1,0:T(8,128)(2,1)} %get-tuple-element.152.refs_8_.refs_5_.refs_3_, ...), custom_call_target="tpu_custom_call" | custom-call | flops 70000000 | bytes 1024 | tf_op jit(solution)/shard_map/heads_grad/pallas_call | solution.py:80
  921.1 15.7 %collective-permute-done.83.refs_3_ = bf16[2,2,128,1024]{3,2,1,0:T(8,128)(2,1)} collective-permute-done((bf16[2,2,128,1024]{3,2,1,0:T(8,128)(2,1)}, bf16[2,2,128,1024]{3,2,1,0:T(8,128)(2,1)}, u32[]{:S(2)}, u32[]{:S(2)}) %collective-permute-start.83) | collective-permute-done | bytes 1048608 | tf_op jit(solution)/shard_map/ppermute | solution.py:848
  (626 shorter events, 440.5 us)
Async XLA Ops:
  7.2 195.7 %all-gather.2.cloned.1.call-start = ((), (), s32[]{:S(2)}) async-start(), calls=%async_computation | async-start | bytes 2162688 | tf_op jit(solution)/shard_map/all_gather | solution.py:1133
  41.6 38.1 %collective-permute-start.6 = (bf16[2,2,144,1024]{3,2,1,0:T(8,128)(2,1)S(1)}, bf16[2,2,144,1024]{3,2,1,0:T(8,128)(2,1)S(1)}, u32[]{:S(2)}, u32[]{:S(2)}) collective-permute-start(bf16[2,2,144,1024]{3,2,1,0:T(8,128)(2,1)S(1)} %pad_maximum_fusion.1.refs_11_.refs_7_.refs_8_.refs_6_.refs_3_.refs_4_.refs_5_), channel_id=1, source_target_pairs={{0,16},{8,24},{16,0},{24,8},{1,17},{9,25},{17,1},{25,9},{2,18},{10... | collective-permute-start | bytes 3538952 | tf_op jit(solution)/shard_map/ppermute | solution.py:848
  96.0 34.2 %collective-permute-start.8 = (bf16[512,1024]{1,0:T(8,128)(2,1)}, bf16[512,1024]{1,0:T(8,128)(2,1)S(1)}, u32[]{:S(2)}, u32[]{:S(2)}) collective-permute-start(bf16[512,1024]{1,0:T(8,128)(2,1)} %get-tuple-element.161.refs_4_), channel_id=1, source_target_pairs={{0,4},{1,5},{4,0},{5,1},{2,6},{3,7},{6,2},{7,3},{8,12},{9,13},{12,... | collective-permute-start | bytes 3145736 | tf_op jit(solution)/shard_map/ppermute | solution.py:848
  102.9 36.9 %collective-permute-start.9 = (bf16[2,1,128,1024]{3,2,1,0:T(8,128)(2,1)S(1)}, bf16[2,1,128,1024]{3,2,1,0:T(8,128)(2,1)}, u32[]{:S(2)}, u32[]{:S(2)}) collective-permute-start(bf16[2,1,128,1024]{3,2,1,0:T(8,128)(2,1)S(1)} %copy-done.52), channel_id=1, source_target_pairs={{0,1},{1,0},{2,3},{3,2},{4,5},{5,4},{6,7},{7,6},{8,9},{9,8},{10,11... | collective-permute-start | bytes 1572872 | tf_op jit(solution)/shard_map/ppermute | solution.py:848
  108.1 35.1 %collective-permute-start.15 = (bf16[1,128,1024]{2,1,0:T(8,128)(2,1)}, bf16[1,128,1024]{2,1,0:T(8,128)(2,1)S(1)}, u32[]{:S(2)}, u32[]{:S(2)}) collective-permute-start(bf16[1,128,1024]{2,1,0:T(8,128)(2,1)} %get-tuple-element.167), channel_id=1, source_target_pairs={{0,2},{2,0},{1,3},{3,1},{4,6},{6,4},{5,7},{7,5},{8,10},{10,8},{9,1... | collective-permute-start | bytes 786440 | tf_op jit(solution)/shard_map/ppermute | solution.py:848
  141.7 32.1 %collective-permute-start.11 = (bf16[4,1,128,1024]{3,2,1,0:T(8,128)(2,1)}, bf16[4,1,128,1024]{3,2,1,0:T(8,128)(2,1)S(1)}, u32[]{:S(2)}, u32[]{:S(2)}) collective-permute-start(bf16[4,1,128,1024]{3,2,1,0:T(8,128)(2,1)} %constant_dynamic-update-slice_fusion.refs_11_.refs_7_), channel_id=1, source_target_pairs={{0,16},{8,24},{16,0},{24,8},{1,17},{9,25},{17,1},{25,9},{2,18},{10... | collective-permute-start | bytes 3145736 | tf_op jit(solution)/shard_map/ppermute | solution.py:848
  143.0 30.8 %collective-permute-start.10 = (bf16[4,1,128,1024]{3,2,1,0:T(8,128)(2,1)}, bf16[4,1,128,1024]{3,2,1,0:T(8,128)(2,1)S(1)}, u32[]{:S(2)}, u32[]{:S(2)}) collective-permute-start(bf16[4,1,128,1024]{3,2,1,0:T(8,128)(2,1)} %constant_dynamic-update-slice_fusion.refs_11_.refs_7_), channel_id=1, source_target_pairs={{0,8},{8,0},{16,24},{24,16},{1,9},{9,1},{17,25},{25,17},{2,10},{10... | collective-permute-start | bytes 3145736 | tf_op jit(solution)/shard_map/ppermute | solution.py:848
  232.4 31.8 %collective-permute-start.33 = (bf16[4,1,128,1024]{3,2,1,0:T(8,128)(2,1)}, bf16[4,1,128,1024]{3,2,1,0:T(8,128)(2,1)}, u32[]{:S(2)}, u32[]{:S(2)}) collective-permute-start(bf16[4,1,128,1024]{3,2,1,0:T(8,128)(2,1)} %collective-permute-done.19.refs_1_.refs_5_.refs_11_), channel_id=1, source_target_pairs={{0,4},{4,0},{1,5},{5,1},{2,6},{6,2},{3,7},{7,3},{8,12},{12,8},{9,1... | collective-permute-start | bytes 3145736 | tf_op jit(solution)/shard_map/ppermute | solution.py:848
  311.6 47.5 %collective-permute-start.41 = (bf16[4,2,128,1024]{3,2,1,0:T(8,128)(2,1)}, bf16[4,2,128,1024]{3,2,1,0:T(8,128)(2,1)}, u32[]{:S(2)}, u32[]{:S(2)}) collective-permute-start(bf16[4,2,128,1024]{3,2,1,0:T(8,128)(2,1)} %get-tuple-element.193.refs_7_.refs_4_.refs_6_), channel_id=1, source_target_pairs={{0,8},{8,0},{16,24},{24,16},{1,9},{9,1},{17,25},{25,17},{2,10},{10... | collective-permute-start | bytes 6291464 | tf_op jit(solution)/shard_map/ppermute | solution.py:848
  311.6 47.5 %collective-permute-start.42 = (bf16[4,2,128,1024]{3,2,1,0:T(8,128)(2,1)}, bf16[4,2,128,1024]{3,2,1,0:T(8,128)(2,1)}, u32[]{:S(2)}, u32[]{:S(2)}) collective-permute-start(bf16[4,2,128,1024]{3,2,1,0:T(8,128)(2,1)} %get-tuple-element.193.refs_7_.refs_4_.refs_6_), channel_id=1, source_target_pairs={{0,16},{8,24},{16,0},{24,8},{1,17},{9,25},{17,1},{25,9},{2,18},{10... | collective-permute-start | bytes 6291464 | tf_op jit(solution)/shard_map/ppermute | solution.py:848
  321.8 31.4 %collective-permute-start.44 = (bf16[512,1024]{1,0:T(8,128)(2,1)}, bf16[512,1024]{1,0:T(8,128)(2,1)S(1)}, u32[]{:S(2)}, u32[]{:S(2)}) collective-permute-start(bf16[512,1024]{1,0:T(8,128)(2,1)} %get-tuple-element.196), channel_id=1, source_target_pairs={{0,0},{2,4},{4,2},{6,6},{1,1},{3,5},{5,3},{7,7},{8,8},{10,12},{12,... | collective-permute-start | bytes 3145736 | tf_op jit(solution)/shard_map/ppermute | solution.py:852
  515.5 75.6 %collective-permute-start.59 = (bf16[4,8,128,1024]{3,2,1,0:T(8,128)(2,1)}, bf16[4,8,128,1024]{3,2,1,0:T(8,128)(2,1)}, u32[]{:S(2)}, u32[]{:S(2)}) collective-permute-start(bf16[4,8,128,1024]{3,2,1,0:T(8,128)(2,1)} %get-tuple-element.220), channel_id=1, source_target_pairs={{0,4},{4,0},{1,5},{5,1},{2,6},{6,2},{3,7},{7,3},{8,12},{12,8},{9,1... | collective-permute-start | bytes 25165832 | tf_op jit(solution)/shard_map/ppermute | solution.py:848
  590.2 31.2 %collective-permute-start.62 = (bf16[512,1024]{1,0:T(8,128)(2,1)S(1)}, bf16[512,1024]{1,0:T(8,128)(2,1)S(1)}, u32[]{:S(2)}, u32[]{:S(2)}) collective-permute-start(bf16[512,1024]{1,0:T(8,128)(2,1)S(1)} %fusion.3.refs_1_), channel_id=1, source_target_pairs={{0,1},{1,0},{4,5},{5,4},{2,3},{3,2},{6,7},{7,6},{8,9},{9,8},{12,13... | collective-permute-start | bytes 3145736 | tf_op jit(solution)/shard_map/ppermute | solution.py:848
  607.0 46.9 %collective-permute-start.60 = (bf16[8,128,1024]{2,1,0:T(8,128)(2,1)}, bf16[8,128,1024]{2,1,0:T(8,128)(2,1)S(1)}, u32[]{:S(2)}, u32[]{:S(2)}) collective-permute-start(bf16[8,128,1024]{2,1,0:T(8,128)(2,1)} %get-tuple-element.221.refs_2_), channel_id=1, source_target_pairs={{0,8},{8,0},{16,24},{24,16},{1,9},{9,1},{17,25},{25,17},{2,10},{10... | collective-permute-start | bytes 6291464 | tf_op jit(solution)/shard_map/ppermute | solution.py:848
  608.2 46.6 %collective-permute-start.61 = (bf16[8,128,1024]{2,1,0:T(8,128)(2,1)}, bf16[8,128,1024]{2,1,0:T(8,128)(2,1)S(1)}, u32[]{:S(2)}, u32[]{:S(2)}) collective-permute-start(bf16[8,128,1024]{2,1,0:T(8,128)(2,1)} %get-tuple-element.222.refs_3_), channel_id=1, source_target_pairs={{0,16},{8,24},{16,0},{24,8},{1,17},{9,25},{17,1},{25,9},{2,18},{10... | collective-permute-start | bytes 6291464 | tf_op jit(solution)/shard_map/ppermute | solution.py:848
  669.0 32.9 %collective-permute-start.63 = (bf16[4,8,128,1024]{3,2,1,0:T(8,128)(2,1)}, bf16[4,8,128,1024]{3,2,1,0:T(8,128)(2,1)}, u32[]{:S(2)}, u32[]{:S(2)}) collective-permute-start(bf16[4,8,128,1024]{3,2,1,0:T(8,128)(2,1)} %get-tuple-element.234.refs_1_), channel_id=1, source_target_pairs={{0,4},{4,0},{1,5},{5,1},{2,6},{6,2},{3,7},{7,3},{8,12},{12,8},{9,1... | collective-permute-start | bytes 25165832 | tf_op jit(solution)/shard_map/ppermute | solution.py:848
  674.5 47.3 %collective-permute-start.66 = (bf16[4,128,1024]{2,1,0:T(8,128)(2,1)}, bf16[4,128,1024]{2,1,0:T(8,128)(2,1)S(1)}, u32[]{:S(2)}, u32[]{:S(2)}) collective-permute-start(bf16[4,128,1024]{2,1,0:T(8,128)(2,1)} %add_convert_fusion.4), channel_id=1, source_target_pairs={{0,16},{8,24},{16,0},{24,8},{1,17},{9,25},{17,1},{25,9},{2,18},{10... | collective-permute-start | bytes 3145736 | tf_op jit(solution)/shard_map/ppermute | solution.py:848
  674.7 44.9 %collective-permute-start.67 = (bf16[2,2,128,1024]{3,2,1,0:T(8,128)(2,1)}, bf16[2,2,128,1024]{3,2,1,0:T(8,128)(2,1)}, u32[]{:S(2)}, u32[]{:S(2)}) collective-permute-start(bf16[2,2,128,1024]{3,2,1,0:T(8,128)(2,1)} %get-tuple-element.240), channel_id=1, source_target_pairs={{0,8},{8,0},{16,24},{24,16},{1,9},{9,1},{17,25},{25,17},{2,10},{10... | collective-permute-start | bytes 3145736 | tf_op jit(solution)/shard_map/ppermute | solution.py:848
  690.7 32.4 %collective-permute-start.68 = (bf16[512,1024]{1,0:T(8,128)(2,1)}, bf16[512,1024]{1,0:T(8,128)(2,1)S(1)}, u32[]{:S(2)}, u32[]{:S(2)}) collective-permute-start(bf16[512,1024]{1,0:T(8,128)(2,1)} %get-tuple-element.237.refs_1_.refs_7_), channel_id=1, source_target_pairs={{0,1},{1,0},{4,5},{5,4},{2,3},{3,2},{6,7},{7,6},{8,9},{9,8},{12,13... | collective-permute-start | bytes 3145736 | tf_op jit(solution)/shard_map/ppermute | solution.py:848
  701.9 83.2 %collective-permute-start.72 = (bf16[4,128,1024]{2,1,0:T(8,128)(2,1)}, bf16[4,128,1024]{2,1,0:T(8,128)(2,1)}, u32[]{:S(2)}, u32[]{:S(2)}) collective-permute-start(bf16[4,128,1024]{2,1,0:T(8,128)(2,1)} %add_convert_fusion.3), channel_id=1, source_target_pairs={{0,1},{1,0},{2,3},{3,2},{4,5},{5,4},{6,7},{7,6},{8,9},{9,8},{10,11... | collective-permute-start | bytes 3145736 | tf_op jit(solution)/shard_map/ppermute | solution.py:848
  719.6 100.8 %collective-permute-start.71 = (bf16[8,128,1024]{2,1,0:T(8,128)(2,1)}, bf16[8,128,1024]{2,1,0:T(8,128)(2,1)}, u32[]{:S(2)}, u32[]{:S(2)}) collective-permute-start(bf16[8,128,1024]{2,1,0:T(8,128)(2,1)} %get-tuple-element.243.refs_6_), channel_id=1, source_target_pairs={{0,16},{8,24},{16,0},{24,8},{1,17},{9,25},{17,1},{25,9},{2,18},{10... | collective-permute-start | bytes 6291464 | tf_op jit(solution)/shard_map/ppermute | solution.py:848
  721.8 55.5 %collective-permute-start.73 = (bf16[2,128,1024]{2,1,0:T(8,128)(2,1)}, bf16[2,128,1024]{2,1,0:T(8,128)(2,1)}, u32[]{:S(2)}, u32[]{:S(2)}) collective-permute-start(bf16[2,128,1024]{2,1,0:T(8,128)(2,1)} %fusion.9), channel_id=1, source_target_pairs={{0,16},{8,24},{16,0},{24,8},{1,17},{9,25},{17,1},{25,9},{2,18},{10... | collective-permute-start | bytes 1572872 | tf_op jit(solution)/shard_map/ppermute | solution.py:848
  724.9 61.8 %collective-permute-start.69 = (bf16[512,1024]{1,0:T(8,128)(2,1)}, bf16[512,1024]{1,0:T(8,128)(2,1)}, u32[]{:S(2)}, u32[]{:S(2)}) collective-permute-start(bf16[512,1024]{1,0:T(8,128)(2,1)} %gate.20.refs_2_.refs_8_), channel_id=1, source_target_pairs={{0,4},{1,5},{4,0},{5,1},{2,6},{3,7},{6,2},{7,3},{8,12},{9,13},{12,... | collective-permute-start | bytes 3145736 | tf_op jit(solution)/shard_map/ppermute | solution.py:848
  726.5 97.3 %collective-permute-start.70 = (bf16[8,128,1024]{2,1,0:T(8,128)(2,1)}, bf16[8,128,1024]{2,1,0:T(8,128)(2,1)}, u32[]{:S(2)}, u32[]{:S(2)}) collective-permute-start(bf16[8,128,1024]{2,1,0:T(8,128)(2,1)} %get-tuple-element.242.refs_5_), channel_id=1, source_target_pairs={{0,8},{8,0},{16,24},{24,16},{1,9},{9,1},{17,25},{25,17},{2,10},{10... | collective-permute-start | bytes 6291464 | tf_op jit(solution)/shard_map/ppermute | solution.py:848
  779.5 78.7 %collective-permute-start.77 = (bf16[128,1024]{1,0:T(8,128)(2,1)}, bf16[128,1024]{1,0:T(8,128)(2,1)S(1)}, u32[]{:S(2)}, u32[]{:S(2)}) collective-permute-start(bf16[128,1024]{1,0:T(8,128)(2,1)} %get-tuple-element.351), channel_id=1, source_target_pairs={{0,0},{2,4},{4,2},{6,6},{1,1},{3,5},{5,3},{7,7},{8,8},{10,12},{12,... | collective-permute-start | bytes 786440 | tf_op jit(solution)/shard_map/ppermute | solution.py:852
  785.1 73.1 %collective-permute-start.78 = (bf16[128,1024]{1,0:T(8,128)(2,1)S(1)}, bf16[128,1024]{1,0:T(8,128)(2,1)S(1)}, u32[]{:S(2)}, u32[]{:S(2)}) collective-permute-start(bf16[128,1024]{1,0:T(8,128)(2,1)S(1)} %get-tuple-element.350), channel_id=1, source_target_pairs={{2,0},{6,2},{0,4},{4,6},{3,1},{7,3},{1,5},{5,7},{10,8},{14,10},{8,... | collective-permute-start | bytes 786440 | tf_op jit(solution)/shard_map/ppermute | solution.py:856
  786.8 71.5 %collective-permute-start.76 = (bf16[2,128,1024]{2,1,0:T(8,128)(2,1)S(1)}, bf16[2,128,1024]{2,1,0:T(8,128)(2,1)S(1)}, u32[]{:S(2)}, u32[]{:S(2)}) collective-permute-start(bf16[2,128,1024]{2,1,0:T(8,128)(2,1)S(1)} %add_convert_fusion.8), channel_id=1, source_target_pairs={{0,2},{2,0},{1,3},{3,1},{4,6},{6,4},{5,7},{7,5},{8,10},{10,8},{9,1... | collective-permute-start | bytes 1572872 | tf_op jit(solution)/shard_map/ppermute | solution.py:848
  822.5 32.6 %collective-permute-start.74 = (bf16[4,128,1024]{2,1,0:T(8,128)(2,1)S(1)}, bf16[4,128,1024]{2,1,0:T(8,128)(2,1)S(1)}, u32[]{:S(2)}, u32[]{:S(2)}) collective-permute-start(bf16[4,128,1024]{2,1,0:T(8,128)(2,1)S(1)} %add_convert_fusion.2), channel_id=1, source_target_pairs={{0,8},{8,0},{16,24},{24,16},{1,9},{9,1},{17,25},{25,17},{2,10},{10... | collective-permute-start | bytes 3145736 | tf_op jit(solution)/shard_map/ppermute | solution.py:848
  825.5 32.8 %collective-permute-start.75 = (bf16[4,128,1024]{2,1,0:T(8,128)(2,1)S(1)}, bf16[4,128,1024]{2,1,0:T(8,128)(2,1)S(1)}, u32[]{:S(2)}, u32[]{:S(2)}) collective-permute-start(bf16[4,128,1024]{2,1,0:T(8,128)(2,1)S(1)} %add_convert_fusion), channel_id=1, source_target_pairs={{0,16},{8,24},{16,0},{24,8},{1,17},{9,25},{17,1},{25,9},{2,18},{10... | collective-permute-start | bytes 3145736 | tf_op jit(solution)/shard_map/ppermute | solution.py:848
  886.3 34.8 %collective-permute-start.81 = (bf16[512,1024]{1,0:T(8,128)(2,1)S(1)}, bf16[512,1024]{1,0:T(8,128)(2,1)}, u32[]{:S(2)}, u32[]{:S(2)}) collective-permute-start(bf16[512,1024]{1,0:T(8,128)(2,1)S(1)} %fusion.2.refs_1_), channel_id=1, source_target_pairs={{0,1},{1,0},{4,5},{5,4},{2,3},{3,2},{6,7},{7,6},{8,9},{9,8},{12,13... | collective-permute-start | bytes 3145736 | tf_op jit(solution)/shard_map/ppermute | solution.py:848
  917.9 49.6 %collective-permute-start.91 = (bf16[2,128,1024]{2,1,0:T(8,128)(2,1)}, bf16[2,128,1024]{2,1,0:T(8,128)(2,1)}, u32[]{:S(2)}, u32[]{:S(2)}) collective-permute-start(bf16[2,128,1024]{2,1,0:T(8,128)(2,1)} %add_convert_fusion.6), channel_id=1, source_target_pairs={{0,2},{2,0},{1,3},{3,1},{4,6},{6,4},{5,7},{7,5},{8,10},{10,8},{9,1... | collective-permute-start | bytes 1572872 | tf_op jit(solution)/shard_map/ppermute | solution.py:848
  945.6 50.3 %collective-permute-start.92 = (bf16[512,1024]{1,0:T(8,128)(2,1)}, bf16[512,1024]{1,0:T(8,128)(2,1)}, u32[]{:S(2)}, u32[]{:S(2)}) collective-permute-start(bf16[512,1024]{1,0:T(8,128)(2,1)} %fusion.1), channel_id=1, source_target_pairs={{0,0},{2,4},{4,2},{6,6},{1,1},{3,5},{5,3},{7,7},{8,8},{10,12},{12,... | collective-permute-start | bytes 3145736 | tf_op jit(solution)/shard_map/ppermute | solution.py:852
  (158 other events, 1862.4 us)
Sparse Core Ops, SparseCore 0:
  109.2 71.5 all-gather.1

commit v9 on v8

--- a/solution.py
+++ b/solution.py
@@ -23,7 +23,7 @@
 ALL = ("zh", "zl", "q", "c")
 VMEM_LIMIT = 56 * 1024 * 1024
 TIMES = {
-    "gate": 0.1, "norm_up": 20.0, "down_norm": 20.0, "units_back": 45.0, "up_back": 20.0, "norm_back": 6.0,
+    "gate": 0.1, "finish": 0.2, "norm_up": 20.0, "down_norm": 20.0, "units_back": 45.0, "up_back": 20.0, "norm_back": 6.0,
     "sum_norm_back": 20.0, "grads_theirs": 0.2, "grads_mine": 0.2, "project_qkv": 0.2, "project_gc": 0.2,
     "project_attn": 0.2, "project_gx": 0.2, "heads_grad": 0.2, "attend_forward": 40.0, "attend_backward": 30.0,
 }
@@ -501,21 +501,56 @@
     )
 
 
-def fetch_heads_weight(scal_ref, pieces, cols, buffer, sems):
-    copies = []
+def finish(flow, units, heads, small):
+    layers = len(units)
+    rows, cols = heads[0][0].shape
+    in_width = cols * 3 // 4
+    pairs = in_width // (3 * PAIR)
+    width = units[0][0].shape[2]
+
+    def body(scal_ref, *refs):
+        qkv_ref, out_ref, up_ref, down_ref, square_ref = refs[-5:]
+        small_ref, refs = refs[-6], refs[:-6]
+        squares = jnp.sum(small_ref[...] * small_ref[...], keepdims=True)
+        for l in range(layers):
+            unit_refs, (first, second) = refs[7 * l : 7 * l + 5], refs[7 * l + 5 : 7 * l + 7]
+            for m, target in enumerate((down_ref, up_ref)):
+                total = unit_refs[0][m].astype(F32)
+                for part in unit_refs[1:]:
+                    total = total + part[m].astype(F32)
+                target[l] = total
+                squares = squares + jnp.sum(jnp.sum(total * total, 0, keepdims=True), 1, keepdims=True)
+            total = first[...].astype(F32) + second[...].astype(F32)
+            squares = squares + jnp.sum(jnp.sum(total * total, 0, keepdims=True), 1, keepdims=True)
+            out_ref[l] = total[:, in_width:]
+            for pair in range(pairs):
+                for which in range(3):
+                    base = (3 * pair + which) * PAIR
+                    qkv_ref[l, which, :, pair * PAIR : (pair + 1) * PAIR] = total[:, base : base + PAIR]
+        square_ref[...] = jnp.broadcast_to(squares, (8, 128))
+
+    specs, args = [], []
+    for l in range(layers):
+        specs += [pl.BlockSpec((2, rows, width), lambda *_: (0, 0, 0))] * 5 + [full((rows, cols))] * 2
+        args += [*units[l], *heads[l]]
+    shapes = [(layers, 3, rows, in_width // 3), (layers, rows, cols - in_width), (layers, rows, width), (layers, rows, width),
+              (8, 128)]
+    return call(
+        flow, body, (1,), specs + [full(small.shape)], [full(shape) for shape in shapes],
+        [sds(shape, F32) for shape in shapes], [], args + [small], 0, 0, "finish",
+    )
+
+
+def place_heads_weight(scal_ref, pieces, buffer):
     for r in range(4):
         for k in range(2):
             row = ((scal_ref[S_Q] ^ r) * 2 + (scal_ref[S_ZH] ^ k)) * ROWS
-            copies.append(
-                pltpu.make_async_copy(
-                    pieces[r // 2].at[r % 2, k, pl.ds(0, ROWS), cols], buffer.at[pl.ds(pl.multiple_of(row, ROWS), ROWS), :],
-                    sems.at[2 * r + k],
-                )
-            )
-    for copy in copies:
-        copy.start()
-    for copy in copies:
-        copy.wait()
+            buffer[pl.ds(pl.multiple_of(row, ROWS), ROWS), :] = pieces[r // 2][r % 2, k, :ROWS, :]
+
+
+def heads_weight_specs(weight, cols):
+    width = cols.stop - cols.start
+    return [pl.BlockSpec((2, 2, piece.shape[2], width), lambda *_: (0, 0, 0, cols.start // width)) for piece in weight]
 
 
 def by_member(shape):
@@ -523,7 +558,7 @@
 
 
 def heads_weight_scratch(width):
-    return [pltpu.VMEM((D, width), BF16), pltpu.SemaphoreType.DMA((8,))]
+    return [pltpu.VMEM((D, width), BF16)]
 
 
 def project_in(flow, lefts, across, weight, cols, bias, name):
@@ -533,12 +568,12 @@
     def body(scal_ref, left_ref, right_ref, *refs):
         if bias is not None:
             bias_ref, refs = refs[0], refs[1:]
-        pieces, (out_ref, buffer, sems) = refs[:2], refs[2:]
+        pieces, (out_ref, buffer) = refs[:2], refs[2:]
         step = pl.program_id(0)
 
         @pl.when(step == 0)
         def _():
-            fetch_heads_weight(scal_ref, pieces, cols, buffer, sems)
+            place_heads_weight(scal_ref, pieces, buffer)
 
         for r, left in enumerate((left_ref, right_ref)):
 
@@ -551,7 +586,7 @@
 
     extra, extra_specs = ([], []) if bias is None else ([bias], [full((1, width))])
     return call(
-        flow, body, (2,), [full((tokens, D))] * 2 + extra_specs + [ANY] * 2,
+        flow, body, (2,), [full((tokens, D))] * 2 + extra_specs + heads_weight_specs(weight, cols),
         pl.BlockSpec((1, tokens, width), lambda r, scal_ref: ((scal_ref[S_P] >> 1) ^ r, 0, 0)),
         sds((2, tokens, width), BF16), heads_weight_scratch(width), [*lefts, *extra, *weight], 0, 0, name,
     )
@@ -562,12 +597,12 @@
 
     def body(scal_ref, *refs):
         block_refs, refs = refs[: len(blocks)], refs[len(blocks) :]
-        pieces, outs, (buffer, sems) = refs[:2], refs[2:-2], refs[-2:]
+        pieces, outs, buffer = refs[:2], refs[2:-1], refs[-1]
         step = pl.program_id(0)
 
         @pl.when(step == 0)
         def _():
-            fetch_heads_weight(scal_ref, pieces, cols, buffer, sems)
+            place_heads_weight(scal_ref, pieces, buffer)
 
         value = mm(block_refs[0][0], buffer[:, :width], NT)
         for index in range(1, len(blocks)):
@@ -589,7 +624,8 @@
     else:
         out_specs, out_shape = [full((tokens, D))] * 2, [sds((tokens, D), BF16)] * 2
     return call(
-        flow, body, (2,), [pl.BlockSpec((1, tokens, width), pick)] * len(blocks) + [ANY] * 2, out_specs, out_shape,
+        flow, body, (2,), [pl.BlockSpec((1, tokens, width), pick)] * len(blocks) + heads_weight_specs(weight, cols), out_specs,
+        out_shape,
         heads_weight_scratch(width * len(blocks)), [*blocks, *weight], 0, 0, name,
     )
 
@@ -931,7 +967,10 @@
 
 
 def heads_along_y(near, size, heads, where, zh):
-    far = flip(near, "q", 2)
+    return heads_pieces(near, flip(near, "q", 2), size, heads, where, zh)
+
+
+def heads_pieces(near, far, size, heads, where, zh):
     rows = jnp.concatenate([near[:, :, ROWS, :size], far[:, :, ROWS, :size]])
     return [near, far], heads_bias(order_by(order_by(rows, 0, where[0], 4), 1, zh, 2).reshape(8, size), heads)
 
@@ -1061,9 +1100,10 @@
     def near_sum(self, blocks):
         return add(self.own[blocks], self.from_x[blocks], self.late_y[blocks], self.there[blocks])
 
+    def parts(self):
+        return self.own, self.from_x, self.late_y, self.there, self.last
+
     def total(self):
-        if is_small():
-            return self.near_sum(slice(0, self.count // 2)) + self.last.astype(F32)
         half = self.count
         mine = jnp.stack(
             [self.own, jnp.concatenate([self.to_x[:half], self.rest_x]), jnp.concatenate([self.rest_y, self.to_y[:half]]),
@@ -1145,20 +1185,19 @@
 
     up_bias_full, table = spread_small()
     if small_slice:
-        pair = turn(with_sibling(heads_shard[0]))
-        x_low = turn(tokens)
+        pair = with_sibling(heads_shard[0])
+        bundle = turn(jnp.concatenate([tokens, pair.reshape(-1, D)]))
+        x_low, pair = bundle[: tokens.shape[0]], bundle[tokens.shape[0] :].reshape(pair.shape)
         ends = jnp.cumsum(turn(doc_lengths)[0], dtype=jnp.int32)
-        near = heads_along_x(pair)
+        members = from_members(pair, "q")
+        weights_of = [heads_pieces(jnp.stack(members[:2]), jnp.stack(members[2:]), bias_size, hz, where, zh)]
         up0, down0 = UnitsWeight(up_weight[0][None]), UnitsWeight(down_weight[0][None])
         both1 = UnitsWeight(jnp.stack([up_weight[1], down_weight[1]]))
         flow.hold(
-            up0=up0.shard, down0=down0.shard, down0_twin=down0.shard, both1=both1.shard,
-            heads1=heads_shard[1], low=x_low,
+            up0=up0.shard, down0=down0.shard, down0_twin=down0.shard, both1=both1.shard, heads1=heads_shard[1], low=x_low
         )
         gate(flow)
-        x_low, up0.shard = flow.free("low"), flow.free("up0")
-        up0.far_z()
-        weights_of = [heads_along_y(near, bias_size, hz, where, zh)]
+        x_low = flow.free("low")
     else:
         x_low = turn(tokens)
         ends = jnp.cumsum(turn(doc_lengths)[0], dtype=jnp.int32)
@@ -1172,18 +1211,18 @@
         first, last = small_slice and l == 0, small_slice and l == 1
         xs = gather_group(x_low)
         w_heads, bias = weights_of[l]
+        qkv_near = project_in(flow, (xs[0], xs[2]), False, w_heads, in_cols, bias, "project_qkv")
         if first:
-            flow.wait(up0.two)
+            up0.shard = flow.free("up0")
+            up0.far_z()
             flow.hold(two=up0.two, two_twin=up0.two)
-        qkv_near = project_in(flow, (xs[0], xs[2]), False, w_heads, in_cols, bias, "project_qkv")
+        if last:
+            flow.hold(top=cotangent, own=both1.own)
+        forward(flow, xs, qkv_near)
         if first:
             up0.two, down0.shard = flow.free("two"), flow.free("down0")
             up0.start_z()
             down0.start_far_z()
-        if last:
-            flow.hold(top=cotangent, own=both1.own)
-        forward(flow, xs, qkv_near)
-        if first:
             pair = with_sibling(flow.free("heads1"))
         if last:
             both1.own = flow.free("own")
@@ -1307,13 +1346,15 @@
             units.send_theirs()
         gcs = (gc_near, gc_far)
         if beside:
-            flow.hold(rest_x=units.rest_x, rest_y=units.rest_y)
+            early = [above_heads.along_y(), *above.near_z()]
+            flow.hold(rest_x=units.rest_x, rest_y=units.rest_y, keep=above_heads.keep, above=above.own)
         gqkv = [attend_backward(flow, ends, 0, qkv, gcs, wide, lse)]
         if beside:
             units.rest_x, units.rest_y = flow.free("rest_x"), flow.free("rest_y")
+            above_heads.keep, above.own = flow.free("keep"), flow.free("above")
         flow.wait(gqkv[0])
         if beside:
-            flow.wait(*units.near(), *above.near_z(), above_heads.along_y())
+            flow.wait(*units.near(), *early)
             above.far_z()
             units.far()
             above_halves = above_heads.halves(zh)
@@ -1336,7 +1377,6 @@
             flow.wait(*units.made)
         elif small_slice:
             units.own = flow.free("own")
-            flow.wait(units.there)
             units.far_z()
         *buckets, qkv_sums = heads_grad(flow, xs, gqkv, gas, ctx)
         heads = HeadsGrad(*buckets)
@@ -1363,48 +1403,48 @@
         heads.along_x()
         small_sums = fold_small(spread_by_distance(small_sums, where), 0, 1)
         flow.wait(back[2])
-        flow.hold(small=small_sums, got=heads.got, own=units.own)
+        flow.hold(small=small_sums, got=heads.got)
         gate(flow)
-        small_sums, heads.got, units.own = flow.free("small"), flow.free("got"), flow.free("own")
+        small_sums, heads.got = flow.free("small"), flow.free("got")
         input_grad = turn(add(g1, back[0], back[1][0], back[2]).astype(BF16))
         heads.along_y()
         small_sums = fold_small(small_sums, 1, 2)
-        flow.wait(heads.got)
-        flow.hold(small=small_sums, own=units.own)
+        flow.wait(heads.got, units.last)
+        flow.hold(small=small_sums)
         gate(flow)
-        units.own = flow.free("own")
         small_sums = fold_small(flow.free("small"), 2, 3)
         halves = heads.halves(zh)
-        d_heads = jnp.stack([add(turn(halves[0]), uncross(halves[1])), add(*done)])
         small_out = fold_small(small_sums, 3, 5).reshape(layers, -1)
+        parts = [(turn(halves[0]), uncross(halves[1])), done]
+        flow.hold(grad=input_grad, output=layer_output)
+        qkv_grad, out_grad, up_grad, down_grad, squares = finish(
+            flow, [member.parts() for member in units_of], parts, small_out
+        )
+        input_grad, layer_output = flow.free("grad"), flow.free("output")
     else:
         halves = [member.halves(zh) for member in heads_of]
         d_heads = jnp.stack([add(turn(half[0]), uncross(half[1])) for half in halves])
         input_grad = turn(add(g1, back[0], back[1][0], back[2]).astype(BF16))
         small_out = lax.psum_scatter(small_sums.reshape(tz * dp, -1), ALL, scatter_dimension=0, tiled=True)
         small_out = small_out.reshape(layers, -1)
-    qkv_grad = d_heads[:, :, : in_cols.stop].reshape(layers, d_heads.shape[1], -1, 3, PAIR)
-    qkv_grad = qkv_grad.transpose(0, 3, 1, 2, 4).reshape(qkv_weight.shape)
-    out_grad = d_heads[:, :, in_cols.stop :]
-    totals = [member.total() for member in units_of]
-    down_grad, up_grad = (jnp.stack([total[i] for total in totals]) for i in range(2))
+        qkv_grad = d_heads[:, :, : in_cols.stop].reshape(layers, d_heads.shape[1], -1, 3, PAIR)
+        qkv_grad = qkv_grad.transpose(0, 3, 1, 2, 4).reshape(qkv_weight.shape)
+        out_grad = d_heads[:, :, in_cols.stop :]
+        totals = [member.total() for member in units_of]
+        down_grad, up_grad = (jnp.stack([total[i] for total in totals]) for i in range(2))
+        squares = sum(jnp.sum(member * member) for member in (qkv_grad, out_grad, up_grad, down_grad, small_out))
 
     rest = small_out[:, bias_size:]
     qv_bias_grad = small_out[:, :bias_size].reshape(qv_bias.shape)
     up_bias_grad = rest[:, cuts[0] : cuts[1]].reshape(up_bias.shape)
     gains_grad = rest[:, cuts[1] : cuts[2]].reshape(gains.shape)
     shifts_grad = rest[:, cuts[2] : cuts[3]].reshape(shifts.shape)
-    all_grads = (qkv_grad, qv_bias_grad, out_grad, up_grad, up_bias_grad, down_grad, gains_grad, shifts_grad)
-    local_squares = sum(jnp.sum(member * member) for member in all_grads)
     entry_count = LAYERS * (4 * D * D + 2 * D * FF + FF + 8 * D)
-    if small_slice:
-        flow.hold(squares=jnp.broadcast_to(local_squares, (8, 128)), grad=input_grad, output=layer_output)
-        flow.hold(**{f"out{i}": member for i, member in enumerate(all_grads)})
-        gate(flow)
-        local_squares, input_grad, layer_output = flow.free("squares"), flow.free("grad"), flow.free("output")
-        all_grads = [flow.free(f"out{i}") for i in range(len(all_grads))]
-    grad_rms = jnp.sqrt(sum_all(local_squares) / entry_count)
-    return (layer_output, input_grad, *all_grads, grad_rms)
+    grad_rms = jnp.sqrt(sum_all(squares) / entry_count)
+    return (
+        layer_output, input_grad, qkv_grad, qv_bias_grad, out_grad, up_grad, up_bias_grad, down_grad, gains_grad,
+        shifts_grad, grad_rms,
+    )
 
 
 def solution(mesh):

time: 1040 us -> 989 us (0.951)
    ppermute x89 -> x90, waiting for transfers between devices: 199 us -> 179 us  [flip(): lax.ppermute(values_in, axes, [(a, a ^ mask) for a in range(lax.axis_size...]
    ppermute x9 -> x8, waiting for transfers between devices: 57.7 us -> 72.9 us  [turn(): lax.ppermute(values_in, ('c', 'zh'), [(2 * a + b, 2 * b + a) for a in ran...]
    ppermute x9 -> x8, starting transfers between devices: 36.9 us -> 33.5 us  [turn(): lax.ppermute(values_in, ('c', 'zh'), [(2 * a + b, 2 * b + a) for a in ran...]
    unnamed x195 -> x206, local copies, waits for them, and re-layouts: 40.6 us -> 38.6 us
    ppermute x89 -> x90, starting transfers between devices: 77.9 us -> 78.1 us  [flip(): lax.ppermute(values_in, axes, [(a, a ^ mask) for a in range(lax.axis_size...]
  transfers between devices with their start and end apart: 101 -> 101, of which waited for: 36 -> 35; matrix products, arithmetic and copies ran while one was open for 11% -> 9% of each run, Pallas kernels for 39% -> 40%
where the time goes in v9:
time: 989 us; the launch traced here: 981 us
  Pallas kernels  472 us (48%)
  waiting for transfers between devices  252 us (25%)
  starting transfers between devices  112 us (11%)
  local copies, waits for them, and re-layouts  70.9 us (7%)
  other arithmetic  56.2 us (6%)
  between operations  18.1 us (2%)
    pallas_call x48, Pallas kernels, call(): pl.pallas_call(wrapped, grid_spec=pltpu.PrefetchScalarGridSpec(num_scalar...  472 us
    ppermute x90, waiting for transfers between devices, flip(): lax.ppermute(values_in, axes, [(a, a ^ mask) for a in range(lax.axis_size...  179 us
    ppermute x90, starting transfers between devices, flip(): lax.ppermute(values_in, axes, [(a, a ^ mask) for a in range(lax.axis_size...  78.1 us
    ppermute x8, waiting for transfers between devices, turn(): lax.ppermute(values_in, ('c', 'zh'), [(2 * a + b, 2 * b + a) for a in ran...  72.9 us
    unnamed x206, local copies, waits for them, and re-layouts  38.6 us
    ppermute x8, starting transfers between devices, turn(): lax.ppermute(values_in, ('c', 'zh'), [(2 * a + b, 2 * b + a) for a in ran...  33.5 us
  transfers between devices with their start and end apart: 101, of which 35 were waited for; matrix products, arithmetic and copies ran while one was open for 9% of the time, Pallas kernels for 40%

profile of v9, /device:TPU:1, one launch (start us, length us, event | category | flops | bytes accessed | tf_op | source)
XLA Modules:
  0.0 980.8 jit_solution(8027342131628089453)
XLA Ops:
  18.8 36.3 %collective-permute-done.1 = bf16[800,1024]{1,0:T(8,128)(2,1)S(1)} collective-permute-done((bf16[800,1024]{1,0:T(8,128)(2,1)S(1)}, bf16[800,1024]{1,0:T(8,128)(2,1)S(1)}, u32[]{:S(2)}, u32[]{:S(2)}) %collective-permute-start.1) | collective-permute-done | bytes 1638432 | tf_op jit(solution)/shard_map/ppermute | solution.py:888
  86.1 9.8 collective-permute-done.6
  117.9 13.5 %collective-permute-done.17 = s32[1,4]{1,0:T(1,128)S(1)} collective-permute-done((s32[1,4]{1,0:T(1,128)S(1)}, s32[1,4]{1,0:T(1,128)S(1)}, u32[]{:S(2)}, u32[]{:S(2)}) %collective-permute-start.17) | collective-permute-done | bytes 48 | tf_op jit(solution)/shard_map/ppermute | solution.py:888
  148.7 28.2 %attend_forward.2 = (bf16[4,512,256]{2,1,0:T(8,128)(2,1)}, f32[4,512,256]{2,1,0:T(8,128)}, f32[4,8,512]{2,1,0:T(8,128)}) custom-call(s32[5]{0:T(128)} %stack.167.refs_0_, s32[4]{0:T(128)} %bitcast.280, bf16[2,512,768]{2,1,0:T(8,128)(2,1)} %get-tuple-element.149.refs_1_.refs_2_.refs_6_.refs_8_, bf16[2,512,768]{2,1,0:T(8,128)(2,1)} %get-tuple-element.165.refs_3_.refs_7_.refs_9_), custom_call_target="tpu_custom_call" | custom-call | flops 14000000000 | bytes 1024 | tf_op jit(solution)/shard_map/attend_forward/pallas_call | solution.py:80
  219.1 15.6 %collective-permute-done.19.refs_1_.refs_5_.refs_11_ = bf16[4,1,128,1024]{3,2,1,0:T(8,128)(2,1)} collective-permute-done((bf16[4,1,128,1024]{3,2,1,0:T(8,128)(2,1)}, bf16[4,1,128,1024]{3,2,1,0:T(8,128)(2,1)}, u32[]{:S(2)}, u32[]{:S(2)}) %collective-permute-start.19) | collective-permute-done | bytes 1048608 | tf_op jit(solution)/shard_map/ppermute | solution.py:884
  242.8 19.0 %norm_up.2 = (f32[512,1024]{1,0:T(8,128)}, bf16[512,1024]{1,0:T(8,128)(2,1)}, f32[512,128]{1,0:T(8,128)}, bf16[512,4096]{1,0:T(8,128)(2,1)}, bf16[512,4096]{1,0:...) custom-call(s32[5]{0:T(128)} %stack.167.refs_0_, ...), custom_call_target="tpu_custom_call", output_to_operand_aliasing={{5}: (3, {}), {6}: (4, {})} | custom-call | flops 7000000000 | bytes 1024 | tf_op jit(solution)/shard_map/norm_up/pallas_call | solution.py:80
  269.8 14.4 %down_norm.2 = (f32[512,1024]{1,0:T(8,128)}, bf16[512,1024]{1,0:T(8,128)(2,1)}, f32[512,128]{1,0:T(8,128)}) custom-call(s32[5]{0:T(128)} %stack.167.refs_0_, bf16[512,4096]{1,0:T(8,128)(2,1)} %get-tuple-element.181.refs_1_.refs_5_.refs_3_, f32[512,1024]{1,0:T(8,128)} %get-tuple-element.182.refs_1_.refs_2_.refs_4_, ...), custom_call_target="tpu_custom_call" | custom-call | flops 7000000000 | bytes 1024 | tf_op jit(solution)/shard_map/down_norm/pallas_call | solution.py:80
  302.4 9.7 collective-permute-done.40.refs_4_
  327.2 28.6 %attend_forward.3 = (bf16[4,512,256]{2,1,0:T(8,128)(2,1)}, f32[4,512,256]{2,1,0:T(8,128)}, f32[4,8,512]{2,1,0:T(8,128)}) custom-call(s32[5]{0:T(128)} %stack.167.refs_0_, s32[4]{0:T(128)} %bitcast.281, bf16[2,512,768]{2,1,0:T(8,128)(2,1)} %project_qkv.6.refs_1_.refs_2_.refs_3_, bf16[2,512,768]{2,1,0:T(8,128)(2,1)} %get-tuple-element.194.refs_3_.refs_4_), custom_call_target="tpu_custom_call" | custom-call | flops 14000000000 | bytes 1024 | tf_op jit(solution)/shard_map/attend_forward/pallas_call | solution.py:80
  381.9 13.5 %collective-permute-done.47.refs_2_ = bf16[2,2,128,1024]{3,2,1,0:T(8,128)(2,1)S(1)} collective-permute-done((bf16[2,2,128,1024]{3,2,1,0:T(8,128)(2,1)}, bf16[2,2,128,1024]{3,2,1,0:T(8,128)(2,1)S(1)}, u32[]{:S(2)}, u32[]{:S(2)}) %collective-permute-start.47) | collective-permute-done | bytes 1048608 | tf_op jit(solution)/shard_map/ppermute | solution.py:884
  411.0 19.0 %norm_up.3 = (f32[512,1024]{1,0:T(8,128)}, bf16[512,1024]{1,0:T(8,128)(2,1)}, f32[512,128]{1,0:T(8,128)}, bf16[512,4096]{1,0:T(8,128)(2,1)}, bf16[512,4096]{1,0:T(8,128)(2,1)}) custom-call(s32[5]{0:T(128)} %stack.167.refs_0_, f32[512,1024]{1,0:T(8,128)} %get-tuple-element.197.refs_1_.refs_6_, bf16[512,1024]{1,0:T(8,128)(2,1)} %get-tuple-element.198.refs_2_, ...), custom_call_target="tpu_custom_call" | custom-call | flops 7000000000 | bytes 1024 | tf_op jit(solution)/shard_map/norm_up/pallas_call | solution.py:80
  430.0 14.3 %down_norm.3 = (f32[512,1024]{1,0:T(8,128)}, bf16[512,1024]{1,0:T(8,128)(2,1)}, f32[512,128]{1,0:T(8,128)}) custom-call(s32[5]{0:T(128)} %stack.167.refs_0_, bf16[512,4096]{1,0:T(8,128)(2,1)} %get-tuple-element.201.refs_1_.refs_3_, f32[512,1024]{1,0:T(8,128)} %get-tuple-element.202.refs_2_.refs_4_, ...), custom_call_target="tpu_custom_call" | custom-call | flops 7000000000 | bytes 1024 | tf_op jit(solution)/shard_map/down_norm/pallas_call | solution.py:80
  447.3 12.7 %units_back.2 = (f32[512,1024]{1,0:T(8,128)}, bf16[512,1024]{1,0:T(8,128)(2,1)}, f32[8,1024]{1,0:T(8,128)}, bf16[512,4096]{1,0:T(8,128)(2,1)}, f32[4,1,1024]{2,1,0:T(1,128)}) custom-call(s32[5]{0:T(128)} %stack.167.refs_0_, bf16[512,1024]{1,0:T(8,128)(2,1)} %copy-done.70, f32[512,1024]{1,0:T(8,128)} %get-tuple-element.204.refs_2_, ...), custom_call_target="tpu_custom_call" | custom-call | flops 15749999616 | bytes 1024 | tf_op jit(solution)/shard_map/units_back/pallas_call | solution.py:80
  460.0 12.8 %collective-permute-done.54.refs_1_ = bf16[512,1024]{1,0:T(8,128)(2,1)S(1)} collective-permute-done((bf16[512,1024]{1,0:T(8,128)(2,1)}, bf16[512,1024]{1,0:T(8,128)(2,1)S(1)}, u32[]{:S(2)}, u32[]{:S(2)}) %collective-permute-start.54) | collective-permute-done | bytes 1048608 | tf_op jit(solution)/shard_map/ppermute | solution.py:888
  473.7 15.0 %up_back.2 = (f32[512,1024]{1,0:T(8,128)}, bf16[512,1024]{1,0:T(8,128)(2,1)}, f32[8,1024]{1,0:T(8,128)}, bf16[512,1024]{1,0:T(8,128)(2,1)}) custom-call(s32[5]{0:T(128)} %stack.167.refs_0_, bf16[512,1024]{1,0:T(8,128)(2,1)} %copy-done.14, bf16[512,4096]{1,0:T(8,128)(2,1)} %get-tuple-element.207.refs_2_.refs_5_, ...), custom_call_target="tpu_custom_call", output_to_operand_aliasing={{3}: (1, {})} | custom-call | flops 7000000000 | bytes 1024 | tf_op jit(solution)/shard_map/up_back/pallas_call | solution.py:80
  488.9 12.8 %grads_theirs.2.refs_1_.refs_2_ = bf16[4,8,128,1024]{3,2,1,0:T(8,128)(2,1)} custom-call(s32[5]{0:T(128)} %stack.167.refs_0_, bf16[512,1024]{1,0:T(8,128)(2,1)} %get-tuple-element.210.refs_1_.refs_10_, bf16[512,1024]{1,0:T(8,128)(2,1)} %get-tuple-element.211.refs_2_, bf16[512,4096]{1,0:T(8,128)(2,1)} %get-tuple-element.201.refs_1_.refs_3_, ...), custom_call_target="tpu_custom_call" | custom-call | flops 70000000 | bytes 1024 | tf_op jit(solution)/shard_map/grads_theirs/pallas_call | solution.py:80
  515.6 28.2 %attend_backward.4.refs_2_.refs_1_.refs_14_ = bf16[4,512,384]{2,1,0:T(8,128)(2,1)} custom-call(s32[5]{0:T(128)} %stack.167.refs_0_, s32[4]{0:T(128)} %gate.16.refs_1_, bf16[2,512,768]{2,1,0:T(8,128)(2,1)} %project_qkv.6.refs_1_.refs_2_.refs_3_, bf16[2,512,768]{2,1,0:T(8,128)(2,1)} %get-tuple-element.194.refs_3_.refs_4_, ...), custom_call_target="tpu_custom_call" | custom-call | flops 10499999744 | bytes 1024 | tf_op jit(solution)/shard_map/attend_backward/pallas_call | solution.py:80
  543.8 28.5 %attend_backward.5.refs_2_.refs_3_.refs_15_ = bf16[4,512,384]{2,1,0:T(8,128)(2,1)} custom-call(s32[5]{0:T(128)} %stack.167.refs_0_, s32[4]{0:T(128)} %gate.16.refs_1_, bf16[4,512,384]{2,1,0:T(8,128)(2,1)} %attend_backward.4.refs_2_.refs_1_.refs_14_, bf16[2,512,768]{2,1,0:T(8,128)(2,1)} %project_qkv.6.refs_1_.refs_2_.refs_3_, ...), custom_call_target="tpu_custom_call" | custom-call | flops 10499999744 | bytes 1024 | tf_op jit(solution)/shard_map/attend_backward/pallas_call | solution.py:80
  588.2 15.8 %grads_mine.2 = (bf16[8,128,1024]{2,1,0:T(8,128)(2,1)}, bf16[8,128,1024]{2,1,0:T(8,128)(2,1)}, bf16[8,128,1024]{2,1,0:T(8,128)(2,1)}, bf16[4,128,1024]{2,1,0:T(8,128)(2,1)}, bf16[4,128,1024]{2,1,0:T(8,128)(2,1)}) custom-call(s32[5]{0:T(128)} %stack.167.refs_0_, bf16[512,1024]{1,0:T(8,128)(2,1)} %copy-done.35, bf16[512,1024]{1,0:T(8,128)(2,1)} %get-tuple-element.211.refs_2_, ...), custom_call_target="tpu_custom_call" | custom-call | flops 70000000 | bytes 1024 | tf_op jit(solution)/shard_map/grads_mine/pallas_call | solution.py:80
  605.7 13.1 %heads_grad.2 = (bf16[2,2,128,1024]{3,2,1,0:T(8,128)(2,1)}, bf16[2,2,128,1024]{3,2,1,0:T(8,128)(2,1)}, f32[1,768]{1,0:T(1,128)}) custom-call(s32[5]{0:T(128)} %stack.167.refs_0_, bf16[8,128,1024]{2,1,0:T(8,128)(2,1)} %get-tuple-element.220.refs_1_.refs_5_, bf16[8,128,1024]{2,1,0:T(8,128)(2,1)} %get-tuple-element.218.refs_2_, ...), custom_call_target="tpu_custom_call" | custom-call | flops 70000000 | bytes 1024 | tf_op jit(solution)/shard_map/heads_grad/pallas_call | solution.py:80
  618.8 14.2 %units_back.3 = (f32[512,1024]{1,0:T(8,128)}, bf16[512,1024]{1,0:T(8,128)(2,1)}, f32[8,1024]{1,0:T(8,128)}, bf16[512,4096]{1,0:T(8,128)(2,1)}, f32[4,1,1024]{2,1,0:T(1,128)}) custom-call(s32[5]{0:T(128)} %stack.167.refs_0_, bf16[2,2,128,1024]{3,2,1,0:T(8,128)(2,1)} %get-tuple-element.223.refs_1_.refs_3_, f32[512,1024]{1,0:T(8,128)} %get-tuple-element.224.refs_2_, ...), custom_call_target="tpu_custom_call" | custom-call | flops 15749999616 | bytes 1024 | tf_op jit(solution)/shard_map/units_back/pallas_call | solution.py:80
  633.0 18.0 %collective-permute-done.61.refs_2_ = bf16[8,128,1024]{2,1,0:T(8,128)(2,1)S(1)} collective-permute-done((bf16[8,128,1024]{2,1,0:T(8,128)(2,1)}, bf16[8,128,1024]{2,1,0:T(8,128)(2,1)S(1)}, u32[]{:S(2)}, u32[]{:S(2)}) %collective-permute-start.61) | collective-permute-done | bytes 2097184 | tf_op jit(solution)/shard_map/ppermute | solution.py:884
  653.4 12.8 %grads_theirs.3 = (bf16[4,8,128,1024]{3,2,1,0:T(8,128)(2,1)}, bf16[2,2,128,1024]{3,2,1,0:T(8,128)(2,1)}) custom-call(s32[5]{0:T(128)} %stack.167.refs_0_, bf16[8,128,1024]{2,1,0:T(8,128)(2,1)} %copy-done.7, bf16[8,128,1024]{2,1,0:T(8,128)(2,1)} %copy-done.16, ...), custom_call_target="tpu_custom_call", output_to_operand_aliasing={{1}: (3, {})} | custom-call | flops 70000000 | bytes 1024 | tf_op jit(solution)/shard_map/grads_theirs/pallas_call | solution.py:80
  673.3 15.1 %up_back.3 = (f32[512,1024]{1,0:T(8,128)}, bf16[512,1024]{1,0:T(8,128)(2,1)}, f32[8,1024]{1,0:T(8,128)}) custom-call(s32[5]{0:T(128)} %stack.167.refs_0_, bf16[4,8,128,1024]{3,2,1,0:T(8,128)(2,1)} %get-tuple-element.231.refs_1_, bf16[512,4096]{1,0:T(8,128)(2,1)} %get-tuple-element.230.refs_7_.refs_2_.refs_5_, f32[512,1024]{1,0:T(8,128)} %get-tuple-element.232.refs_3_, ...), custom_call_target="tpu_custom_call" | custom-call | flops 7000000000 | bytes 1024 | tf_op jit(solution)/shard_map/up_back/pallas_call | solution.py:80
  690.6 15.8 %grads_mine.3 = (bf16[8,128,1024]{2,1,0:T(8,128)(2,1)}, bf16[8,128,1024]{2,1,0:T(8,128)(2,1)}, bf16[8,128,1024]{2,1,0:T(8,128)(2,1)}, bf16[4,128,1024]{2,1,0:T(8,128)(2,1)}, bf16[4,128,1024]{2,1,0:T(8,128)(2,1)}) custom-call(s32[5]{0:T(128)} %stack.167.refs_0_, bf16[512,1024]{1,0:T(8,128)(2,1)} %get-tuple-element.235.refs_1_.refs_6_, ...), custom_call_target="tpu_custom_call" | custom-call | flops 70000000 | bytes 1024 | tf_op jit(solution)/shard_map/grads_mine/pallas_call | solution.py:80
  706.4 10.4 %collective-permute-done.67.refs_3_ = bf16[2,2,128,1024]{3,2,1,0:T(8,128)(2,1)S(1)} collective-permute-done((bf16[2,2,128,1024]{3,2,1,0:T(8,128)(2,1)}, bf16[2,2,128,1024]{3,2,1,0:T(8,128)(2,1)S(1)}, u32[]{:S(2)}, u32[]{:S(2)}) %collective-permute-start.67) | collective-permute-done | bytes 1048608 | tf_op jit(solution)/shard_map/ppermute | solution.py:884
  735.1 28.3 %attend_backward.6 = (bf16[4,512,384]{2,1,0:T(8,128)(2,1)}, bf16[4,128,1024]{2,1,0:T(8,128)(2,1)}, bf16[4,128,1024]{2,1,0:T(8,128)(2,1)}, bf16[2,2,128,1024]{3,2,1,0:T(8,128)(2,1)}, bf16[8,128,1024]{2,1,0:T(8,128)(2,1)}) custom-call(s32[5]{0:T(128)} %stack.167.refs_0_, ...), custom_call_target="tpu_custom_call", output_to_operand_aliasing={{1}: (2, {}), {2}: (3, {}), {3}: (4, {}), {4}: (5, {})} | custom-call | flops 10499999744 | bytes 1024 | tf_op jit(solution)/shard_map/attend_backward/pallas_call | solution.py:80
  768.7 10.3 %collective-permute-done.72.refs_5_ = bf16[2,128,1024]{2,1,0:T(8,128)(2,1)} collective-permute-done((bf16[2,128,1024]{2,1,0:T(8,128)(2,1)}, bf16[2,128,1024]{2,1,0:T(8,128)(2,1)}, u32[]{:S(2)}, u32[]{:S(2)}) %collective-permute-start.72) | collective-permute-done | bytes 524320 | tf_op jit(solution)/shard_map/ppermute | solution.py:884
  791.4 28.2 %attend_backward.7 = (bf16[4,512,384]{2,1,0:T(8,128)(2,1)}, bf16[8,128,1024]{2,1,0:T(8,128)(2,1)}) custom-call(s32[5]{0:T(128)} %stack.167.refs_0_, s32[4]{0:T(128)} %gate.16.refs_1_, bf16[4,512,384]{2,1,0:T(8,128)(2,1)} %get-tuple-element.245.refs_2_.refs_6_.refs_3_.refs_10_, bf16[8,128,1024]{2,1,0:T(8,128)(2,1)} %copy-done.26, ...), custom_call_target="tpu_custom_call", output_to_operand_aliasing={{1}: (7, {})} | custom-call | flops 10499999744 | bytes 1024 | tf_op jit(solution)/shard_map/attend_backward/pallas_call | solution.py:80
  848.6 12.9 %heads_grad.3 = (bf16[2,2,128,1024]{3,2,1,0:T(8,128)(2,1)}, bf16[2,2,128,1024]{3,2,1,0:T(8,128)(2,1)}, f32[1,768]{1,0:T(1,128)}) custom-call(s32[5]{0:T(128)} %stack.167.refs_0_, bf16[512,1024]{1,0:T(8,128)(2,1)} %fusion.refs_1_, bf16[512,1024]{1,0:T(8,128)(2,1)} %get-tuple-element.148.refs_6_.refs_5_.refs_2_, ...), custom_call_target="tpu_custom_call" | custom-call | flops 70000000 | bytes 1024 | tf_op jit(solution)/shard_map/heads_grad/pallas_call | solution.py:80
  867.6 28.3 %collective-permute-done.80.refs_1_ = bf16[512,1024]{1,0:T(8,128)(2,1)S(1)} collective-permute-done((bf16[512,1024]{1,0:T(8,128)(2,1)}, bf16[512,1024]{1,0:T(8,128)(2,1)S(1)}, u32[]{:S(2)}, u32[]{:S(2)}) %collective-permute-start.80) | collective-permute-done | bytes 1048608 | tf_op jit(solution)/shard_map/ppermute | solution.py:884
  931.1 10.3 %collective-permute-done.87.refs_8_ = bf16[128,1024]{1,0:T(8,128)(2,1)S(1)} collective-permute-done((bf16[128,1024]{1,0:T(8,128)(2,1)S(1)}, bf16[128,1024]{1,0:T(8,128)(2,1)S(1)}, u32[]{:S(2)}, u32[]{:S(2)}) %collective-permute-start.87) | collective-permute-done | bytes 262176 | tf_op jit(solution)/shard_map/ppermute | solution.py:888
  (626 shorter events, 397.6 us)
Async XLA Ops:
  7.2 198.6 %all-gather.2.cloned.1.call-start = ((), (), s32[]{:S(2)}) async-start(), calls=%async_computation | async-start | bytes 2162688 | tf_op jit(solution)/shard_map/all_gather | solution.py:1173
  13.0 42.1 %collective-permute-start.1 = (bf16[800,1024]{1,0:T(8,128)(2,1)S(1)}, bf16[800,1024]{1,0:T(8,128)(2,1)S(1)}, u32[]{:S(2)}, u32[]{:S(2)}) collective-permute-start(bf16[800,1024]{1,0:T(8,128)(2,1)S(1)} %pad_maximum_fusion.1), channel_id=1, source_target_pairs={{0,0},{2,4},{4,2},{6,6},{1,1},{3,5},{5,3},{7,7},{8,8},{10,12},{12,... | collective-permute-start | bytes 4915208 | tf_op jit(solution)/shard_map/ppermute | solution.py:888
  99.5 33.5 %collective-permute-start.8 = (bf16[512,1024]{1,0:T(8,128)(2,1)}, bf16[512,1024]{1,0:T(8,128)(2,1)S(1)}, u32[]{:S(2)}, u32[]{:S(2)}) collective-permute-start(bf16[512,1024]{1,0:T(8,128)(2,1)} %get-tuple-element.158.refs_4_.refs_3_), channel_id=1, source_target_pairs={{0,4},{1,5},{4,0},{5,1},{2,6},{3,7},{6,2},{7,3},{8,12},{9,13},{12,... | collective-permute-start | bytes 3145736 | tf_op jit(solution)/shard_map/ppermute | solution.py:884
  110.0 31.7 %collective-permute-start.9 = (bf16[2,1,128,1024]{3,2,1,0:T(8,128)(2,1)}, bf16[2,1,128,1024]{3,2,1,0:T(8,128)(2,1)S(1)}, u32[]{:S(2)}, u32[]{:S(2)}) collective-permute-start(bf16[2,1,128,1024]{3,2,1,0:T(8,128)(2,1)} %get-tuple-element.160), channel_id=1, source_target_pairs={{0,1},{1,0},{2,3},{3,2},{4,5},{5,4},{6,7},{7,6},{8,9},{9,8},{10,11... | collective-permute-start | bytes 1572872 | tf_op jit(solution)/shard_map/ppermute | solution.py:884
  142.5 36.5 %collective-permute-start.11 = (bf16[4,1,128,1024]{3,2,1,0:T(8,128)(2,1)}, bf16[4,1,128,1024]{3,2,1,0:T(8,128)(2,1)S(1)}, u32[]{:S(2)}, u32[]{:S(2)}) collective-permute-start(bf16[4,1,128,1024]{3,2,1,0:T(8,128)(2,1)} %constant_dynamic-update-slice_fusion.refs_11_.refs_7_), channel_id=1, source_target_pairs={{0,16},{8,24},{16,0},{24,8},{1,17},{9,25},{17,1},{25,9},{2,18},{10... | collective-permute-start | bytes 3145736 | tf_op jit(solution)/shard_map/ppermute | solution.py:884
  143.8 35.2 %collective-permute-start.10 = (bf16[4,1,128,1024]{3,2,1,0:T(8,128)(2,1)}, bf16[4,1,128,1024]{3,2,1,0:T(8,128)(2,1)S(1)}, u32[]{:S(2)}, u32[]{:S(2)}) collective-permute-start(bf16[4,1,128,1024]{3,2,1,0:T(8,128)(2,1)} %constant_dynamic-update-slice_fusion.refs_11_.refs_7_), channel_id=1, source_target_pairs={{0,8},{8,0},{16,24},{24,16},{1,9},{9,1},{17,25},{25,17},{2,10},{10... | collective-permute-start | bytes 3145736 | tf_op jit(solution)/shard_map/ppermute | solution.py:884
  145.0 31.9 %collective-permute-start.14 = (bf16[2,128,1024]{2,1,0:T(8,128)(2,1)S(1)}, bf16[2,128,1024]{2,1,0:T(8,128)(2,1)S(1)}, u32[]{:S(2)}, u32[]{:S(2)}) collective-permute-start(bf16[2,128,1024]{2,1,0:T(8,128)(2,1)S(1)} %copy-done.5), channel_id=1, source_target_pairs={{0,2},{2,0},{1,3},{3,1},{4,6},{6,4},{5,7},{7,5},{8,10},{10,8},{9,1... | collective-permute-start | bytes 1572872 | tf_op jit(solution)/shard_map/ppermute | solution.py:884
  145.1 32.8 %collective-permute-start.16 = (bf16[2,1,128,1024]{3,2,1,0:T(8,128)(2,1)S(1)}, bf16[2,1,128,1024]{3,2,1,0:T(8,128)(2,1)S(1)}, u32[]{:S(2)}, u32[]{:S(2)}) collective-permute-start(bf16[2,1,128,1024]{3,2,1,0:T(8,128)(2,1)S(1)} %pad_maximum_fusion.11), channel_id=1, source_target_pairs={{0,1},{1,0},{2,3},{3,2},{4,5},{5,4},{6,7},{7,6},{8,9},{9,8},{10,11... | collective-permute-start | bytes 1572872 | tf_op jit(solution)/shard_map/ppermute | solution.py:884
  314.5 47.5 %collective-permute-start.41 = (bf16[4,2,128,1024]{3,2,1,0:T(8,128)(2,1)}, bf16[4,2,128,1024]{3,2,1,0:T(8,128)(2,1)}, u32[]{:S(2)}, u32[]{:S(2)}) collective-permute-start(bf16[4,2,128,1024]{3,2,1,0:T(8,128)(2,1)} %get-tuple-element.190.refs_7_.refs_4_.refs_6_), channel_id=1, source_target_pairs={{0,8},{8,0},{16,24},{24,16},{1,9},{9,1},{17,25},{25,17},{2,10},{10... | collective-permute-start | bytes 6291464 | tf_op jit(solution)/shard_map/ppermute | solution.py:884
  315.9 47.2 %collective-permute-start.42 = (bf16[4,2,128,1024]{3,2,1,0:T(8,128)(2,1)}, bf16[4,2,128,1024]{3,2,1,0:T(8,128)(2,1)}, u32[]{:S(2)}, u32[]{:S(2)}) collective-permute-start(bf16[4,2,128,1024]{3,2,1,0:T(8,128)(2,1)} %get-tuple-element.190.refs_7_.refs_4_.refs_6_), channel_id=1, source_target_pairs={{0,16},{8,24},{16,0},{24,8},{1,17},{9,25},{17,1},{25,9},{2,18},{10... | collective-permute-start | bytes 6291464 | tf_op jit(solution)/shard_map/ppermute | solution.py:884
  323.8 31.9 %collective-permute-start.44 = (bf16[512,1024]{1,0:T(8,128)(2,1)}, bf16[512,1024]{1,0:T(8,128)(2,1)S(1)}, u32[]{:S(2)}, u32[]{:S(2)}) collective-permute-start(bf16[512,1024]{1,0:T(8,128)(2,1)} %get-tuple-element.193), channel_id=1, source_target_pairs={{0,0},{2,4},{4,2},{6,6},{1,1},{3,5},{5,3},{7,7},{8,8},{10,12},{12,... | collective-permute-start | bytes 3145736 | tf_op jit(solution)/shard_map/ppermute | solution.py:888
  514.4 73.8 %collective-permute-start.59 = (bf16[4,8,128,1024]{3,2,1,0:T(8,128)(2,1)}, bf16[4,8,128,1024]{3,2,1,0:T(8,128)(2,1)}, u32[]{:S(2)}, u32[]{:S(2)}) collective-permute-start(bf16[4,8,128,1024]{3,2,1,0:T(8,128)(2,1)} %get-tuple-element.217), channel_id=1, source_target_pairs={{0,4},{4,0},{1,5},{5,1},{2,6},{6,2},{3,7},{7,3},{8,12},{12,8},{9,1... | collective-permute-start | bytes 25165832 | tf_op jit(solution)/shard_map/ppermute | solution.py:884
  587.3 31.5 %collective-permute-start.62 = (bf16[512,1024]{1,0:T(8,128)(2,1)S(1)}, bf16[512,1024]{1,0:T(8,128)(2,1)}, u32[]{:S(2)}, u32[]{:S(2)}) collective-permute-start(bf16[512,1024]{1,0:T(8,128)(2,1)S(1)} %fusion.3.refs_1_), channel_id=1, source_target_pairs={{0,1},{1,0},{4,5},{5,4},{2,3},{3,2},{6,7},{7,6},{8,9},{9,8},{12,13... | collective-permute-start | bytes 3145736 | tf_op jit(solution)/shard_map/ppermute | solution.py:884
  604.1 46.9 %collective-permute-start.61 = (bf16[8,128,1024]{2,1,0:T(8,128)(2,1)}, bf16[8,128,1024]{2,1,0:T(8,128)(2,1)S(1)}, u32[]{:S(2)}, u32[]{:S(2)}) collective-permute-start(bf16[8,128,1024]{2,1,0:T(8,128)(2,1)} %get-tuple-element.219.refs_3_), channel_id=1, source_target_pairs={{0,16},{8,24},{16,0},{24,8},{1,17},{9,25},{17,1},{25,9},{2,18},{10... | collective-permute-start | bytes 6291464 | tf_op jit(solution)/shard_map/ppermute | solution.py:884
  605.4 46.6 %collective-permute-start.60 = (bf16[8,128,1024]{2,1,0:T(8,128)(2,1)}, bf16[8,128,1024]{2,1,0:T(8,128)(2,1)S(1)}, u32[]{:S(2)}, u32[]{:S(2)}) collective-permute-start(bf16[8,128,1024]{2,1,0:T(8,128)(2,1)} %get-tuple-element.218.refs_2_), channel_id=1, source_target_pairs={{0,8},{8,0},{16,24},{24,16},{1,9},{9,1},{17,25},{25,17},{2,10},{10... | collective-permute-start | bytes 6291464 | tf_op jit(solution)/shard_map/ppermute | solution.py:884
  669.6 36.8 %collective-permute-start.65 = (bf16[4,128,1024]{2,1,0:T(8,128)(2,1)S(1)}, bf16[4,128,1024]{2,1,0:T(8,128)(2,1)S(1)}, u32[]{:S(2)}, u32[]{:S(2)}) collective-permute-start(bf16[4,128,1024]{2,1,0:T(8,128)(2,1)S(1)} %add_convert_fusion.5), channel_id=1, source_target_pairs={{0,8},{8,0},{16,24},{24,16},{1,9},{9,1},{17,25},{25,17},{2,10},{10... | collective-permute-start | bytes 3145736 | tf_op jit(solution)/shard_map/ppermute | solution.py:884
  670.2 46.6 %collective-permute-start.67 = (bf16[2,2,128,1024]{3,2,1,0:T(8,128)(2,1)}, bf16[2,2,128,1024]{3,2,1,0:T(8,128)(2,1)S(1)}, u32[]{:S(2)}, u32[]{:S(2)}) collective-permute-start(bf16[2,2,128,1024]{3,2,1,0:T(8,128)(2,1)} %get-tuple-element.239), channel_id=1, source_target_pairs={{0,8},{8,0},{16,24},{24,16},{1,9},{9,1},{17,25},{25,17},{2,10},{10... | collective-permute-start | bytes 3145736 | tf_op jit(solution)/shard_map/ppermute | solution.py:884
  672.6 44.1 %collective-permute-start.66 = (bf16[4,128,1024]{2,1,0:T(8,128)(2,1)}, bf16[4,128,1024]{2,1,0:T(8,128)(2,1)S(1)}, u32[]{:S(2)}, u32[]{:S(2)}) collective-permute-start(bf16[4,128,1024]{2,1,0:T(8,128)(2,1)} %add_convert_fusion.4), channel_id=1, source_target_pairs={{0,16},{8,24},{16,0},{24,8},{1,17},{9,25},{17,1},{25,9},{2,18},{10... | collective-permute-start | bytes 3145736 | tf_op jit(solution)/shard_map/ppermute | solution.py:884
  689.3 37.0 %collective-permute-start.64 = (bf16[512,1024]{1,0:T(8,128)(2,1)}, bf16[512,1024]{1,0:T(8,128)(2,1)}, u32[]{:S(2)}, u32[]{:S(2)}) collective-permute-start(bf16[512,1024]{1,0:T(8,128)(2,1)} %get-tuple-element.235.refs_1_.refs_6_), channel_id=1, source_target_pairs={{0,4},{1,5},{4,0},{5,1},{2,6},{3,7},{6,2},{7,3},{8,12},{9,13},{12,... | collective-permute-start | bytes 3145736 | tf_op jit(solution)/shard_map/ppermute | solution.py:884
  720.3 65.8 %collective-permute-start.71 = (bf16[8,128,1024]{2,1,0:T(8,128)(2,1)}, bf16[8,128,1024]{2,1,0:T(8,128)(2,1)}, u32[]{:S(2)}, u32[]{:S(2)}) collective-permute-start(bf16[8,128,1024]{2,1,0:T(8,128)(2,1)} %get-tuple-element.242.refs_6_), channel_id=1, source_target_pairs={{0,16},{8,24},{16,0},{24,8},{1,17},{9,25},{17,1},{25,9},{2,18},{10... | collective-permute-start | bytes 6291464 | tf_op jit(solution)/shard_map/ppermute | solution.py:884
  723.8 39.6 %collective-permute-start.73 = (bf16[4,128,1024]{2,1,0:T(8,128)(2,1)}, bf16[4,128,1024]{2,1,0:T(8,128)(2,1)}, u32[]{:S(2)}, u32[]{:S(2)}) collective-permute-start(bf16[4,128,1024]{2,1,0:T(8,128)(2,1)} %add_convert_fusion.3), channel_id=1, source_target_pairs={{0,1},{1,0},{2,3},{3,2},{4,5},{5,4},{6,7},{7,6},{8,9},{9,8},{10,11... | collective-permute-start | bytes 3145736 | tf_op jit(solution)/shard_map/ppermute | solution.py:884
  724.7 65.4 %collective-permute-start.70 = (bf16[8,128,1024]{2,1,0:T(8,128)(2,1)}, bf16[8,128,1024]{2,1,0:T(8,128)(2,1)S(1)}, u32[]{:S(2)}, u32[]{:S(2)}) collective-permute-start(bf16[8,128,1024]{2,1,0:T(8,128)(2,1)} %get-tuple-element.241.refs_5_), channel_id=1, source_target_pairs={{0,8},{8,0},{16,24},{24,16},{1,9},{9,1},{17,25},{25,17},{2,10},{10... | collective-permute-start | bytes 6291464 | tf_op jit(solution)/shard_map/ppermute | solution.py:884
  726.4 52.7 %collective-permute-start.72 = (bf16[2,128,1024]{2,1,0:T(8,128)(2,1)}, bf16[2,128,1024]{2,1,0:T(8,128)(2,1)}, u32[]{:S(2)}, u32[]{:S(2)}) collective-permute-start(bf16[2,128,1024]{2,1,0:T(8,128)(2,1)} %fusion.9), channel_id=1, source_target_pairs={{0,16},{8,24},{16,0},{24,8},{1,17},{9,25},{17,1},{25,9},{2,18},{10... | collective-permute-start | bytes 1572872 | tf_op jit(solution)/shard_map/ppermute | solution.py:884
  765.9 57.0 %collective-permute-start.76 = (bf16[2,128,1024]{2,1,0:T(8,128)(2,1)}, bf16[2,128,1024]{2,1,0:T(8,128)(2,1)S(1)}, u32[]{:S(2)}, u32[]{:S(2)}) collective-permute-start(bf16[2,128,1024]{2,1,0:T(8,128)(2,1)} %add_convert_fusion.8), channel_id=1, source_target_pairs={{0,2},{2,0},{1,3},{3,1},{4,6},{6,4},{5,7},{7,5},{8,10},{10,8},{9,1... | collective-permute-start | bytes 1572872 | tf_op jit(solution)/shard_map/ppermute | solution.py:884
  781.2 41.7 %collective-permute-start.77 = (bf16[128,1024]{1,0:T(8,128)(2,1)}, bf16[128,1024]{1,0:T(8,128)(2,1)S(1)}, u32[]{:S(2)}, u32[]{:S(2)}) collective-permute-start(bf16[128,1024]{1,0:T(8,128)(2,1)} %get-tuple-element.337), channel_id=1, source_target_pairs={{0,0},{2,4},{4,2},{6,6},{1,1},{3,5},{5,3},{7,7},{8,8},{10,12},{12,... | collective-permute-start | bytes 786440 | tf_op jit(solution)/shard_map/ppermute | solution.py:888
  785.8 37.1 %collective-permute-start.78 = (bf16[128,1024]{1,0:T(8,128)(2,1)}, bf16[128,1024]{1,0:T(8,128)(2,1)S(1)}, u32[]{:S(2)}, u32[]{:S(2)}) collective-permute-start(bf16[128,1024]{1,0:T(8,128)(2,1)} %get-tuple-element.336), channel_id=1, source_target_pairs={{2,0},{6,2},{0,4},{4,6},{3,1},{7,3},{1,5},{5,7},{10,8},{14,10},{8,... | collective-permute-start | bytes 786440 | tf_op jit(solution)/shard_map/ppermute | solution.py:892
  788.7 31.0 %collective-permute-start.74 = (bf16[4,128,1024]{2,1,0:T(8,128)(2,1)}, bf16[4,128,1024]{2,1,0:T(8,128)(2,1)S(1)}, u32[]{:S(2)}, u32[]{:S(2)}) collective-permute-start(bf16[4,128,1024]{2,1,0:T(8,128)(2,1)} %add_convert_fusion.2), channel_id=1, source_target_pairs={{0,8},{8,0},{16,24},{24,16},{1,9},{9,1},{17,25},{25,17},{2,10},{10... | collective-permute-start | bytes 3145736 | tf_op jit(solution)/shard_map/ppermute | solution.py:884
  790.5 32.4 %collective-permute-start.75 = (bf16[4,128,1024]{2,1,0:T(8,128)(2,1)S(1)}, bf16[4,128,1024]{2,1,0:T(8,128)(2,1)S(1)}, u32[]{:S(2)}, u32[]{:S(2)}) collective-permute-start(bf16[4,128,1024]{2,1,0:T(8,128)(2,1)S(1)} %add_convert_fusion), channel_id=1, source_target_pairs={{0,16},{8,24},{16,0},{24,8},{1,17},{9,25},{17,1},{25,9},{2,18},{10... | collective-permute-start | bytes 3145736 | tf_op jit(solution)/shard_map/ppermute | solution.py:884
  848.1 47.8 %collective-permute-start.80 = (bf16[512,1024]{1,0:T(8,128)(2,1)}, bf16[512,1024]{1,0:T(8,128)(2,1)S(1)}, u32[]{:S(2)}, u32[]{:S(2)}) collective-permute-start(bf16[512,1024]{1,0:T(8,128)(2,1)} %fusion.refs_1_), channel_id=1, source_target_pairs={{0,1},{1,0},{4,5},{5,4},{2,3},{3,2},{6,7},{7,6},{8,9},{9,8},{12,13... | collective-permute-start | bytes 3145736 | tf_op jit(solution)/shard_map/ppermute | solution.py:884
  863.2 32.6 %collective-permute-start.85 = (bf16[2,2,128,1024]{3,2,1,0:T(8,128)(2,1)}, bf16[2,2,128,1024]{3,2,1,0:T(8,128)(2,1)S(1)}, u32[]{:S(2)}, u32[]{:S(2)}) collective-permute-start(bf16[2,2,128,1024]{3,2,1,0:T(8,128)(2,1)} %get-tuple-element.265), channel_id=1, source_target_pairs={{0,8},{8,0},{16,24},{24,16},{1,9},{9,1},{17,25},{25,17},{2,10},{10... | collective-permute-start | bytes 3145736 | tf_op jit(solution)/shard_map/ppermute | solution.py:884
  866.8 43.9 %collective-permute-start.83 = (bf16[2,128,1024]{2,1,0:T(8,128)(2,1)}, bf16[2,128,1024]{2,1,0:T(8,128)(2,1)}, u32[]{:S(2)}, u32[]{:S(2)}) collective-permute-start(bf16[2,128,1024]{2,1,0:T(8,128)(2,1)} %add_convert_fusion.7), channel_id=1, source_target_pairs={{0,2},{2,0},{1,3},{3,1},{4,6},{6,4},{5,7},{7,5},{8,10},{10,8},{9,1... | collective-permute-start | bytes 1572872 | tf_op jit(solution)/shard_map/ppermute | solution.py:884
  904.6 36.7 %collective-permute-start.81 = (bf16[512,1024]{1,0:T(8,128)(2,1)S(1)}, bf16[512,1024]{1,0:T(8,128)(2,1)S(1)}, u32[]{:S(2)}, u32[]{:S(2)}) collective-permute-start(bf16[512,1024]{1,0:T(8,128)(2,1)S(1)} %fusion.2), channel_id=1, source_target_pairs={{0,0},{2,4},{4,2},{6,6},{1,1},{3,5},{5,3},{7,7},{8,8},{10,12},{12,... | collective-permute-start | bytes 3145736 | tf_op jit(solution)/shard_map/ppermute | solution.py:888
  (164 other events, 1821.9 us)
Sparse Core Ops, SparseCore 0:
  118.0 74.0 all-gather.1

commit v10 on v9

--- a/solution.py
+++ b/solution.py
@@ -502,8 +502,7 @@
 
 
 def finish(flow, units, heads, small):
-    layers = len(units)
-    rows, cols = heads[0][0].shape
+    layers, rows, cols = heads[0].shape
     in_width = cols * 3 // 4
     pairs = in_width // (3 * PAIR)
     width = units[0][0].shape[2]
@@ -511,16 +510,17 @@
     def body(scal_ref, *refs):
         qkv_ref, out_ref, up_ref, down_ref, square_ref = refs[-5:]
         small_ref, refs = refs[-6], refs[:-6]
+        first, second, refs = refs[0], refs[1], refs[2:]
         squares = jnp.sum(small_ref[...] * small_ref[...], keepdims=True)
         for l in range(layers):
-            unit_refs, (first, second) = refs[7 * l : 7 * l + 5], refs[7 * l + 5 : 7 * l + 7]
+            unit_refs = refs[5 * l : 5 * l + 5]
             for m, target in enumerate((down_ref, up_ref)):
                 total = unit_refs[0][m].astype(F32)
                 for part in unit_refs[1:]:
                     total = total + part[m].astype(F32)
                 target[l] = total
                 squares = squares + jnp.sum(jnp.sum(total * total, 0, keepdims=True), 1, keepdims=True)
-            total = first[...].astype(F32) + second[...].astype(F32)
+            total = first[l].astype(F32) + second[l].astype(F32)
             squares = squares + jnp.sum(jnp.sum(total * total, 0, keepdims=True), 1, keepdims=True)
             out_ref[l] = total[:, in_width:]
             for pair in range(pairs):
@@ -529,10 +529,10 @@
                     qkv_ref[l, which, :, pair * PAIR : (pair + 1) * PAIR] = total[:, base : base + PAIR]
         square_ref[...] = jnp.broadcast_to(squares, (8, 128))
 
-    specs, args = [], []
+    specs, args = [full((layers, rows, cols))] * 2, list(heads)
     for l in range(layers):
-        specs += [pl.BlockSpec((2, rows, width), lambda *_: (0, 0, 0))] * 5 + [full((rows, cols))] * 2
-        args += [*units[l], *heads[l]]
+        specs += [pl.BlockSpec((2, rows, width), lambda *_: (0, 0, 0))] * 5
+        args += units[l]
     shapes = [(layers, 3, rows, in_width // 3), (layers, rows, cols - in_width), (layers, rows, width), (layers, rows, width),
               (8, 128)]
     return call(
@@ -1194,7 +1194,8 @@
         up0, down0 = UnitsWeight(up_weight[0][None]), UnitsWeight(down_weight[0][None])
         both1 = UnitsWeight(jnp.stack([up_weight[1], down_weight[1]]))
         flow.hold(
-            up0=up0.shard, down0=down0.shard, down0_twin=down0.shard, both1=both1.shard, heads1=heads_shard[1], low=x_low
+            up0=up0.shard, up0_twin=up0.shard, up0_last=up0.shard, down0=down0.shard, down0_twin=down0.shard, both1=both1.shard,
+            heads1=heads_shard[1], low=x_low,
         )
         gate(flow)
         x_low = flow.free("low")
@@ -1214,16 +1215,17 @@
         qkv_near = project_in(flow, (xs[0], xs[2]), False, w_heads, in_cols, bias, "project_qkv")
         if first:
             up0.shard = flow.free("up0")
-            up0.far_z()
-            flow.hold(two=up0.two, two_twin=up0.two)
+            up0.start_far_z()
+            flow.wait(up0.other)
         if last:
             flow.hold(top=cotangent, own=both1.own)
         forward(flow, xs, qkv_near)
         if first:
-            up0.two, down0.shard = flow.free("two"), flow.free("down0")
+            twin, down0.shard = flow.free("up0_twin"), flow.free("down0")
+            up0.join_far_z(twin)
+            across = up0.other
             up0.start_z()
             down0.start_far_z()
-            pair = with_sibling(flow.free("heads1"))
         if last:
             both1.own = flow.free("own")
             both1.near()
@@ -1231,21 +1233,18 @@
         qkv = (qkv_near, qkv_far)
         if first:
             down0.join_far_z(flow.free("down0_twin"))
-            up0.join_z(flow.free("two_twin"))
+            up0.join_z(jnp.stack([flow.free("up0_last"), across]))
             up0.near()
             down0.near_z()
             both1.shard = flow.free("both1")
             both1.far_z()
-            pair = turn(pair)
         if last:
             top_grad = turn(flow.free("top"))
             both1.swap("own")
         ctx, wide, lse = attend_forward(flow, ends, qkv)
         if first:
             flow.wait(up0.near_x, up0.near_y)
-            flow.hold(both1=both1.two, down0=down0.own, pair_twin=pair)
-            flow.wait(pair)
-            beside = flip(pair, "q", 1)
+            flow.hold(both1=both1.two, down0=down0.own)
             up0.corner()
             up0.swap("own")
         if last:
@@ -1267,6 +1266,8 @@
             flow.wait(down0.near_x, down0.near_y)
             down0.corner()
             down0.swap("near_x", "near_y")
+            pair = with_sibling(flow.free("heads1"))
+            flow.hold(pair=pair)
             w_up = up0.pieces(), 0
         elif last:
             flow.wait(passed)
@@ -1284,18 +1285,21 @@
         used = (prev_gain, prev_shift, shift_row(l, 0), gain_row(l, 0), shift_row(l, 1))
         n1, hs, r1, act, slope = norm_up(flow, prev, attn, table, used, *w_up, up_bias_full[l], tz)
         if first:
-            flow.wait(n1, beside)
+            pair = turn(flow.free("pair"))
+            flow.wait(n1)
             flow.hold(far_a=down0.far_a, far_b=down0.far_b)
             gate(flow)
             down0.far_a, down0.far_b = flow.free("far_a"), flow.free("far_b")
             down0.swap("far_a", "far_b")
             both1.two = flow.free("both1")
             both1.near_z()
-            near = jnp.stack([flow.free("pair_twin"), beside])
-            weights_of.append(heads_along_y(near, bias_size, hz, where, zh))
+            flow.wait(pair)
             w_down = down0.pieces(), 0
         used = (gain_row(l, 0), shift_row(l, 1), shift_row(l, 2), gain_row(l, 1), shift_row(l, 3))
         n2, y_low, r2 = down_norm(flow, act, *w_down, n1, table, used, tz)
+        if first:
+            members = from_members(pair, "q")
+            weights_of.append(heads_pieces(jnp.stack(members[:2]), jnp.stack(members[2:]), bias_size, hz, where, zh))
         kept.append((xs, qkv, ctx, wide, lse, n1, hs, r1, act, slope, n2, r2, w_heads, w_up, w_down))
         x_low, prev, prev_gain, prev_shift = y_low, n2, gain_row(l, 1), shift_row(l, 3)
     layer_output = turn(x_low)
@@ -1334,7 +1338,7 @@
         else:
             units.mine()
             if beside:
-                flow.wait(*late, above_heads.got)
+                flow.wait(*late)
             forward(flow, gas, *units.made)
         gc_near = project_in(flow, (gas[0], gas[2]), False, w_heads, out_cols, None, "project_gc")
         flow.wait(gc_near)
@@ -1346,7 +1350,7 @@
             units.send_theirs()
         gcs = (gc_near, gc_far)
         if beside:
-            early = [above_heads.along_y(), *above.near_z()]
+            early = above.near_z()
             flow.hold(rest_x=units.rest_x, rest_y=units.rest_y, keep=above_heads.keep, above=above.own)
         gqkv = [attend_backward(flow, ends, 0, qkv, gcs, wide, lse)]
         if beside:
@@ -1354,17 +1358,17 @@
             above_heads.keep, above.own = flow.free("keep"), flow.free("above")
         flow.wait(gqkv[0])
         if beside:
-            flow.wait(*units.near(), *early)
+            flow.wait(*units.near(), *early, above_heads.got)
             above.far_z()
             units.far()
-            above_halves = above_heads.halves(zh)
-            done = turn(above_halves[0]), uncross(above_halves[1])
-            flow.hold(own=units.own)
+            above_heads.along_y()
+            flow.hold(own=units.own, keep=above_heads.keep)
         gqkv.append(attend_backward(flow, ends, 1, qkv, gcs, wide, lse))
         if beside:
-            units.own = flow.free("own")
+            units.own, above_heads.keep = flow.free("own"), flow.free("keep")
             units.near_z()
-            flow.wait(units.passing, units.late_y, above.last, *done)
+            flow.wait(units.passing, units.late_y, above.last, above_heads.got)
+            above_halves = above_heads.halves(zh)
         send = project_out(flow, gqkv, (2, 3), w_heads, in_cols, True, "project_gx")
         flow.wait(send)
         if beside:
@@ -1415,10 +1419,11 @@
         small_sums = fold_small(flow.free("small"), 2, 3)
         halves = heads.halves(zh)
         small_out = fold_small(small_sums, 3, 5).reshape(layers, -1)
-        parts = [(turn(halves[0]), uncross(halves[1])), done]
+        stacked = [jnp.stack([half, above_half]) for half, above_half in zip(halves, above_halves)]
+        arrived = turn(stacked[0]), uncross(stacked[1])
         flow.hold(grad=input_grad, output=layer_output)
         qkv_grad, out_grad, up_grad, down_grad, squares = finish(
-            flow, [member.parts() for member in units_of], parts, small_out
+            flow, [member.parts() for member in units_of], arrived, small_out
         )
         input_grad, layer_output = flow.free("grad"), flow.free("output")
     else:

time: 989 us -> 1010 us (1.021)
    ppermute x90 -> x91, waiting for transfers between devices: 179 us -> 164 us  [flip(): lax.ppermute(values_in, axes, [(a, a ^ mask) for a in range(lax.axis_size...]
    ppermute x8 -> x7, waiting for transfers between devices: 72.9 us -> 86.4 us  [turn(): lax.ppermute(values_in, ('c', 'zh'), [(2 * a + b, 2 * b + a) for a in ran...]
    ppermute x90 -> x91, starting transfers between devices: 78.1 us -> 84.4 us  [flip(): lax.ppermute(values_in, axes, [(a, a ^ mask) for a in range(lax.axis_size...]
    ppermute x8 -> x7, starting transfers between devices: 33.5 us -> 30.5 us  [turn(): lax.ppermute(values_in, ('c', 'zh'), [(2 * a + b, 2 * b + a) for a in ran...]
    unnamed x206 -> x213, local copies, waits for them, and re-layouts: 38.6 us -> 37.7 us
  transfers between devices with their start and end apart: 101 -> 100, of which waited for: 35 -> 36; matrix products, arithmetic and copies ran while one was open for 9% -> 11% of each run, Pallas kernels for 40% -> 39%
where the time goes in v10:
time: 1010 us; the launch traced here: 1000 us
  Pallas kernels  475 us (47%)
  waiting for transfers between devices  250 us (25%)
  starting transfers between devices  115 us (11%)
  local copies, waits for them, and re-layouts  79.6 us (8%)
  other arithmetic  62.3 us (6%)
  between operations  18 us (2%)
    pallas_call x48, Pallas kernels, call(): pl.pallas_call(wrapped, grid_spec=pltpu.PrefetchScalarGridSpec(num_scalar...  475 us
    ppermute x91, waiting for transfers between devices, flip(): lax.ppermute(values_in, axes, [(a, a ^ mask) for a in range(lax.axis_size...  164 us
    ppermute x7, waiting for transfers between devices, turn(): lax.ppermute(values_in, ('c', 'zh'), [(2 * a + b, 2 * b + a) for a in ran...  86.4 us
    ppermute x91, starting transfers between devices, flip(): lax.ppermute(values_in, axes, [(a, a ^ mask) for a in range(lax.axis_size...  84.4 us
    unnamed x213, local copies, waits for them, and re-layouts  37.7 us
    ppermute x7, starting transfers between devices, turn(): lax.ppermute(values_in, ('c', 'zh'), [(2 * a + b, 2 * b + a) for a in ran...  30.5 us
  transfers between devices with their start and end apart: 100, of which 36 were waited for; matrix products, arithmetic and copies ran while one was open for 11% of the time, Pallas kernels for 39%

profile of v10, /device:TPU:1, one launch (start us, length us, event | category | flops | bytes accessed | tf_op | source)
XLA Modules:
  0.0 999.7 jit_solution(9920909139557580806)
XLA Ops:
  18.8 36.3 %collective-permute-done.1 = bf16[800,1024]{1,0:T(8,128)(2,1)S(1)} collective-permute-done((bf16[800,1024]{1,0:T(8,128)(2,1)S(1)}, bf16[800,1024]{1,0:T(8,128)(2,1)S(1)}, u32[]{:S(2)}, u32[]{:S(2)}) %collective-permute-start.1) | collective-permute-done | bytes 1638432 | tf_op jit(solution)/shard_map/ppermute | solution.py:888
  86.1 11.1 %collective-permute-done.7.refs_9_ = bf16[512,1024]{1,0:T(8,128)(2,1)S(1)} collective-permute-done((bf16[512,1024]{1,0:T(8,128)(2,1)}, bf16[512,1024]{1,0:T(8,128)(2,1)S(1)}, u32[]{:S(2)}, u32[]{:S(2)}) %collective-permute-start.7) | collective-permute-done | bytes 1048608 | tf_op jit(solution)/shard_map/ppermute | solution.py:884
  110.6 11.4 %collective-permute-done.12 = s32[1,4]{1,0:T(1,128)S(1)} collective-permute-done((s32[1,4]{1,0:T(1,128)S(1)}, s32[1,4]{1,0:T(1,128)S(1)}, u32[]{:S(2)}, u32[]{:S(2)}) %collective-permute-start.12) | collective-permute-done | bytes 48 | tf_op jit(solution)/shard_map/ppermute | solution.py:888
  136.3 28.4 %attend_forward.2 = (bf16[4,512,256]{2,1,0:T(8,128)(2,1)}, f32[4,512,256]{2,1,0:T(8,128)}, f32[4,8,512]{2,1,0:T(8,128)}, bf16[144,1024]{1,0:T(8,128)(2,1)}) custom-call(s32[5]{0:T(128)} %stack.190.refs_0_, s32[4]{0:T(128)} %bitcast.275, bf16[144,1024]{1,0:T(8,128)(2,1)} %get-tuple-element.172.refs_2_, ...), custom_call_target="tpu_custom_call", output_to_operand_aliasing={{3}: (2, {})} | custom-call | flops 14000000000 | bytes 1024 | tf_op jit(solution)/shard_map/attend_forward/pallas_call | solution.py:80
  207.5 11.4 %collective-permute-done.17.refs_1_.refs_6_.refs_11_ = bf16[4,1,128,1024]{3,2,1,0:T(8,128)(2,1)} collective-permute-done((bf16[4,1,128,1024]{3,2,1,0:T(8,128)(2,1)}, bf16[4,1,128,1024]{3,2,1,0:T(8,128)(2,1)}, u32[]{:S(2)}, u32[]{:S(2)}) %collective-permute-start.17) | collective-permute-done | bytes 1048608 | tf_op jit(solution)/shard_map/ppermute | solution.py:884
  232.8 19.0 %norm_up.2 = (f32[512,1024]{1,0:T(8,128)}, bf16[512,1024]{1,0:T(8,128)(2,1)}, f32[512,128]{1,0:T(8,128)}, bf16[512,4096]{1,0:T(8,128)(2,1)}, bf16[512,4096]{1,0:...) custom-call(s32[5]{0:T(128)} %stack.190.refs_0_, ...), custom_call_target="tpu_custom_call", output_to_operand_aliasing={{5}: (3, {}), {6}: (4, {})} | custom-call | flops 7000000000 | bytes 1024 | tf_op jit(solution)/shard_map/norm_up/pallas_call | solution.py:80
  259.8 10.9 %collective-permute-done.28.refs_1_ = bf16[2,144,1024]{2,1,0:T(8,128)(2,1)} collective-permute-done((bf16[2,144,1024]{2,1,0:T(8,128)(2,1)}, bf16[2,144,1024]{2,1,0:T(8,128)(2,1)}, u32[]{:S(2)}, u32[]{:S(2)}) %collective-permute-start.28) | collective-permute-done | bytes 589856 | tf_op jit(solution)/shard_map/ppermute | solution.py:888
  274.5 14.3 %down_norm.2 = (f32[512,1024]{1,0:T(8,128)}, bf16[512,1024]{1,0:T(8,128)(2,1)}, f32[512,128]{1,0:T(8,128)}) custom-call(s32[5]{0:T(128)} %stack.190.refs_0_, bf16[2,144,1024]{2,1,0:T(8,128)(2,1)} %collective-permute-done.28.refs_1_, bf16[512,4096]{1,0:T(8,128)(2,1)} %get-tuple-element.194.refs_2_.refs_5_.refs_3_, ...), custom_call_target="tpu_custom_call" | custom-call | flops 7000000000 | bytes 1024 | tf_op jit(solution)/shard_map/down_norm/pallas_call | solution.py:80
  330.8 28.8 %attend_forward.3 = (bf16[4,512,256]{2,1,0:T(8,128)(2,1)}, f32[4,512,256]{2,1,0:T(8,128)}, f32[4,8,512]{2,1,0:T(8,128)}) custom-call(s32[5]{0:T(128)} %stack.190.refs_0_, s32[4]{0:T(128)} %bitcast.276, bf16[2,512,768]{2,1,0:T(8,128)(2,1)} %project_qkv.6.refs_1_.refs_2_.refs_3_, bf16[2,512,768]{2,1,0:T(8,128)(2,1)} %get-tuple-element.205.refs_3_.refs_4_), custom_call_target="tpu_custom_call" | custom-call | flops 14000000000 | bytes 1024 | tf_op jit(solution)/shard_map/attend_forward/pallas_call | solution.py:80
  384.1 13.5 %collective-permute-done.48.refs_2_ = bf16[2,2,128,1024]{3,2,1,0:T(8,128)(2,1)S(1)} collective-permute-done((bf16[2,2,128,1024]{3,2,1,0:T(8,128)(2,1)}, bf16[2,2,128,1024]{3,2,1,0:T(8,128)(2,1)S(1)}, u32[]{:S(2)}, u32[]{:S(2)}) %collective-permute-start.48) | collective-permute-done | bytes 1048608 | tf_op jit(solution)/shard_map/ppermute | solution.py:884
  398.5 7.6 collective-permute-done.47.refs_1_.refs_4_
  413.5 19.0 %norm_up.3 = (f32[512,1024]{1,0:T(8,128)}, bf16[512,1024]{1,0:T(8,128)(2,1)}, f32[512,128]{1,0:T(8,128)}, bf16[512,4096]{1,0:T(8,128)(2,1)}, bf16[512,4096]{1,0:T(8,128)(2,1)}) custom-call(s32[5]{0:T(128)} %stack.190.refs_0_, f32[512,1024]{1,0:T(8,128)} %get-tuple-element.208.refs_1_.refs_6_, bf16[512,1024]{1,0:T(8,128)(2,1)} %get-tuple-element.209.refs_2_, ...), custom_call_target="tpu_custom_call" | custom-call | flops 7000000000 | bytes 1024 | tf_op jit(solution)/shard_map/norm_up/pallas_call | solution.py:80
  432.5 14.3 %down_norm.3 = (f32[512,1024]{1,0:T(8,128)}, bf16[512,1024]{1,0:T(8,128)(2,1)}, f32[512,128]{1,0:T(8,128)}) custom-call(s32[5]{0:T(128)} %stack.190.refs_0_, bf16[512,4096]{1,0:T(8,128)(2,1)} %get-tuple-element.212.refs_1_.refs_3_, f32[512,1024]{1,0:T(8,128)} %get-tuple-element.213.refs_2_.refs_4_, ...), custom_call_target="tpu_custom_call" | custom-call | flops 7000000000 | bytes 1024 | tf_op jit(solution)/shard_map/down_norm/pallas_call | solution.py:80
  451.4 12.6 %units_back.2 = (f32[512,1024]{1,0:T(8,128)}, bf16[512,1024]{1,0:T(8,128)(2,1)}, f32[8,1024]{1,0:T(8,128)}, bf16[512,4096]{1,0:T(8,128)(2,1)}, f32[4,1,1024]{2,1,0:T(1,128)}) custom-call(s32[5]{0:T(128)} %stack.190.refs_0_, bf16[512,1024]{1,0:T(8,128)(2,1)} %copy-done.70, f32[512,1024]{1,0:T(8,128)} %get-tuple-element.215.refs_2_, ...), custom_call_target="tpu_custom_call" | custom-call | flops 15749999616 | bytes 1024 | tf_op jit(solution)/shard_map/units_back/pallas_call | solution.py:80
  464.0 11.3 %collective-permute-done.55.refs_1_ = bf16[512,1024]{1,0:T(8,128)(2,1)S(1)} collective-permute-done((bf16[512,1024]{1,0:T(8,128)(2,1)}, bf16[512,1024]{1,0:T(8,128)(2,1)S(1)}, u32[]{:S(2)}, u32[]{:S(2)}) %collective-permute-start.55) | collective-permute-done | bytes 1048608 | tf_op jit(solution)/shard_map/ppermute | solution.py:888
  476.3 14.9 %up_back.2 = (f32[512,1024]{1,0:T(8,128)}, bf16[512,1024]{1,0:T(8,128)(2,1)}, f32[8,1024]{1,0:T(8,128)}, bf16[512,1024]{1,0:T(8,128)(2,1)}) custom-call(s32[5]{0:T(128)} %stack.190.refs_0_, bf16[512,1024]{1,0:T(8,128)(2,1)} %copy-done.13, bf16[512,4096]{1,0:T(8,128)(2,1)} %get-tuple-element.218.refs_2_.refs_5_, ...), custom_call_target="tpu_custom_call", output_to_operand_aliasing={{3}: (1, {})} | custom-call | flops 7000000000 | bytes 1024 | tf_op jit(solution)/shard_map/up_back/pallas_call | solution.py:80
  491.4 12.7 %grads_theirs.2.refs_1_.refs_2_ = bf16[4,8,128,1024]{3,2,1,0:T(8,128)(2,1)} custom-call(s32[5]{0:T(128)} %stack.190.refs_0_, bf16[512,1024]{1,0:T(8,128)(2,1)} %get-tuple-element.221.refs_1_.refs_10_, bf16[512,1024]{1,0:T(8,128)(2,1)} %get-tuple-element.222.refs_2_, bf16[512,4096]{1,0:T(8,128)(2,1)} %get-tuple-element.212.refs_1_.refs_3_, ...), custom_call_target="tpu_custom_call" | custom-call | flops 70000000 | bytes 1024 | tf_op jit(solution)/shard_map/grads_theirs/pallas_call | solution.py:80
  518.1 28.8 %attend_backward.4.refs_2_.refs_1_.refs_14_ = bf16[4,512,384]{2,1,0:T(8,128)(2,1)} custom-call(s32[5]{0:T(128)} %stack.190.refs_0_, s32[4]{0:T(128)} %gate.16.refs_1_, bf16[2,512,768]{2,1,0:T(8,128)(2,1)} %project_qkv.6.refs_1_.refs_2_.refs_3_, bf16[2,512,768]{2,1,0:T(8,128)(2,1)} %get-tuple-element.205.refs_3_.refs_4_, ...), custom_call_target="tpu_custom_call" | custom-call | flops 10499999744 | bytes 1024 | tf_op jit(solution)/shard_map/attend_backward/pallas_call | solution.py:80
  546.9 29.0 %attend_backward.5.refs_2_.refs_3_.refs_15_ = bf16[4,512,384]{2,1,0:T(8,128)(2,1)} custom-call(s32[5]{0:T(128)} %stack.190.refs_0_, s32[4]{0:T(128)} %gate.16.refs_1_, bf16[4,512,384]{2,1,0:T(8,128)(2,1)} %attend_backward.4.refs_2_.refs_1_.refs_14_, bf16[2,512,768]{2,1,0:T(8,128)(2,1)} %project_qkv.6.refs_1_.refs_2_.refs_3_, ...), custom_call_target="tpu_custom_call" | custom-call | flops 10499999744 | bytes 1024 | tf_op jit(solution)/shard_map/attend_backward/pallas_call | solution.py:80
  591.9 15.8 %grads_mine.2 = (bf16[8,128,1024]{2,1,0:T(8,128)(2,1)}, bf16[8,128,1024]{2,1,0:T(8,128)(2,1)}, bf16[8,128,1024]{2,1,0:T(8,128)(2,1)}, bf16[4,128,1024]{2,1,0:T(8,128)(2,1)}, bf16[4,128,1024]{2,1,0:T(8,128)(2,1)}) custom-call(s32[5]{0:T(128)} %stack.190.refs_0_, bf16[512,1024]{1,0:T(8,128)(2,1)} %copy-done.33, bf16[512,1024]{1,0:T(8,128)(2,1)} %get-tuple-element.222.refs_2_, ...), custom_call_target="tpu_custom_call" | custom-call | flops 70000000 | bytes 1024 | tf_op jit(solution)/shard_map/grads_mine/pallas_call | solution.py:80
  608.0 13.1 %heads_grad.2 = (bf16[2,2,128,1024]{3,2,1,0:T(8,128)(2,1)}, bf16[2,2,128,1024]{3,2,1,0:T(8,128)(2,1)}, f32[1,768]{1,0:T(1,128)}) custom-call(s32[5]{0:T(128)} %stack.190.refs_0_, bf16[8,128,1024]{2,1,0:T(8,128)(2,1)} %get-tuple-element.231.refs_1_.refs_5_, bf16[8,128,1024]{2,1,0:T(8,128)(2,1)} %get-tuple-element.229.refs_2_, ...), custom_call_target="tpu_custom_call" | custom-call | flops 70000000 | bytes 1024 | tf_op jit(solution)/shard_map/heads_grad/pallas_call | solution.py:80
  621.0 14.2 %units_back.3 = (f32[512,1024]{1,0:T(8,128)}, bf16[512,1024]{1,0:T(8,128)(2,1)}, f32[8,1024]{1,0:T(8,128)}, bf16[512,4096]{1,0:T(8,128)(2,1)}, f32[4,1,1024]{2,1,0:T(1,128)}) custom-call(s32[5]{0:T(128)} %stack.190.refs_0_, bf16[2,2,128,1024]{3,2,1,0:T(8,128)(2,1)} %get-tuple-element.234.refs_1_.refs_3_, f32[512,1024]{1,0:T(8,128)} %get-tuple-element.235.refs_2_, ...), custom_call_target="tpu_custom_call" | custom-call | flops 15749999616 | bytes 1024 | tf_op jit(solution)/shard_map/units_back/pallas_call | solution.py:80
  635.2 19.4 %collective-permute-done.62.refs_2_ = bf16[8,128,1024]{2,1,0:T(8,128)(2,1)S(1)} collective-permute-done((bf16[8,128,1024]{2,1,0:T(8,128)(2,1)}, bf16[8,128,1024]{2,1,0:T(8,128)(2,1)S(1)}, u32[]{:S(2)}, u32[]{:S(2)}) %collective-permute-start.62) | collective-permute-done | bytes 2097184 | tf_op jit(solution)/shard_map/ppermute | solution.py:884
  656.6 12.8 %grads_theirs.3 = (bf16[4,8,128,1024]{3,2,1,0:T(8,128)(2,1)}, bf16[2,2,128,1024]{3,2,1,0:T(8,128)(2,1)}) custom-call(s32[5]{0:T(128)} %stack.190.refs_0_, bf16[8,128,1024]{2,1,0:T(8,128)(2,1)} %copy-done.5, bf16[8,128,1024]{2,1,0:T(8,128)(2,1)} %copy-done.14, ...), custom_call_target="tpu_custom_call", output_to_operand_aliasing={{1}: (3, {})} | custom-call | flops 70000000 | bytes 1024 | tf_op jit(solution)/shard_map/grads_theirs/pallas_call | solution.py:80
  674.0 15.1 %up_back.3 = (f32[512,1024]{1,0:T(8,128)}, bf16[512,1024]{1,0:T(8,128)(2,1)}, f32[8,1024]{1,0:T(8,128)}) custom-call(s32[5]{0:T(128)} %stack.190.refs_0_, bf16[4,8,128,1024]{3,2,1,0:T(8,128)(2,1)} %get-tuple-element.242.refs_1_, bf16[512,4096]{1,0:T(8,128)(2,1)} %get-tuple-element.241.refs_7_.refs_2_.refs_5_, f32[512,1024]{1,0:T(8,128)} %get-tuple-element.243.refs_3_, ...), custom_call_target="tpu_custom_call" | custom-call | flops 7000000000 | bytes 1024 | tf_op jit(solution)/shard_map/up_back/pallas_call | solution.py:80
  691.0 15.9 %grads_mine.3 = (bf16[8,128,1024]{2,1,0:T(8,128)(2,1)}, bf16[8,128,1024]{2,1,0:T(8,128)(2,1)}, bf16[8,128,1024]{2,1,0:T(8,128)(2,1)}, bf16[4,128,1024]{2,1,0:T(8,128)(2,1)}, bf16[4,128,1024]{2,1,0:T(8,128)(2,1)}) custom-call(s32[5]{0:T(128)} %stack.190.refs_0_, bf16[512,1024]{1,0:T(8,128)(2,1)} %get-tuple-element.246.refs_1_.refs_6_, ...), custom_call_target="tpu_custom_call" | custom-call | flops 70000000 | bytes 1024 | tf_op jit(solution)/shard_map/grads_mine/pallas_call | solution.py:80
  731.6 29.0 %attend_backward.6 = (bf16[4,512,384]{2,1,0:T(8,128)(2,1)}, bf16[4,128,1024]{2,1,0:T(8,128)(2,1)}, bf16[4,128,1024]{2,1,0:T(8,128)(2,1)}, bf16[2,2,128,1024]{3,2,1,0:T(8,128)(2,1)}, bf16[8,128,1024]{2,1,0:T(8,128)(2,1)}) custom-call(s32[5]{0:T(128)} %stack.190.refs_0_, ...), custom_call_target="tpu_custom_call", output_to_operand_aliasing={{1}: (2, {}), {2}: (3, {}), {3}: (4, {}), {4}: (5, {})} | custom-call | flops 10499999744 | bytes 1024 | tf_op jit(solution)/shard_map/attend_backward/pallas_call | solution.py:80
  766.2 20.8 %collective-permute-done.73.refs_6_ = bf16[2,2,128,1024]{3,2,1,0:T(8,128)(2,1)S(1)} collective-permute-done((bf16[2,2,128,1024]{3,2,1,0:T(8,128)(2,1)}, bf16[2,2,128,1024]{3,2,1,0:T(8,128)(2,1)S(1)}, u32[]{:S(2)}, u32[]{:S(2)}) %collective-permute-start.73) | collective-permute-done | bytes 1048608 | tf_op jit(solution)/shard_map/ppermute | solution.py:884
  793.5 28.8 %attend_backward.7 = (bf16[4,512,384]{2,1,0:T(8,128)(2,1)}, bf16[8,128,1024]{2,1,0:T(8,128)(2,1)}, bf16[2,2,128,1024]{3,2,1,0:T(8,128)(2,1)}) custom-call(s32[5]{0:T(128)} %stack.190.refs_0_, s32[4]{0:T(128)} %gate.16.refs_1_, bf16[4,512,384]{2,1,0:T(8,128)(2,1)} %get-tuple-element.255.refs_2_.refs_5_.refs_3_.refs_10_, ...), custom_call_target="tpu_custom_call", output_to_operand_aliasing={{1}: (7, {}), {2}: (8, {})} | custom-call | flops 10499999744 | bytes 1024 | tf_op jit(solution)/shard_map/attend_backward/pallas_call | solution.py:80
  854.5 12.9 %heads_grad.3 = (bf16[2,2,128,1024]{3,2,1,0:T(8,128)(2,1)}, bf16[2,2,128,1024]{3,2,1,0:T(8,128)(2,1)}, f32[1,768]{1,0:T(1,128)}) custom-call(s32[5]{0:T(128)} %stack.190.refs_0_, bf16[512,1024]{1,0:T(8,128)(2,1)} %fusion.refs_1_, bf16[512,1024]{1,0:T(8,128)(2,1)} %get-tuple-element.156.refs_8_.refs_5_.refs_2_, ...), custom_call_target="tpu_custom_call" | custom-call | flops 70000000 | bytes 1024 | tf_op jit(solution)/shard_map/heads_grad/pallas_call | solution.py:80
  877.5 24.1 %collective-permute-done.79.refs_1_ = bf16[512,1024]{1,0:T(8,128)(2,1)S(1)} collective-permute-done((bf16[512,1024]{1,0:T(8,128)(2,1)}, bf16[512,1024]{1,0:T(8,128)(2,1)S(1)}, u32[]{:S(2)}, u32[]{:S(2)}) %collective-permute-start.79) | collective-permute-done | bytes 1048608 | tf_op jit(solution)/shard_map/ppermute | solution.py:884
  939.7 10.9 %collective-permute-done.80.refs_1_ = bf16[512,1024]{1,0:T(8,128)(2,1)S(1)} collective-permute-done((bf16[512,1024]{1,0:T(8,128)(2,1)S(1)}, bf16[512,1024]{1,0:T(8,128)(2,1)S(1)}, u32[]{:S(2)}, u32[]{:S(2)}) %collective-permute-start.80) | collective-permute-done | bytes 1048608 | tf_op jit(solution)/shard_map/ppermute | solution.py:888
  (634 shorter events, 413.6 us)
Async XLA Ops:
  7.2 185.7 %all-gather.2.cloned.1.call-start = ((), (), s32[]{:S(2)}) async-start(), calls=%async_computation | async-start | bytes 2162688 | tf_op jit(solution)/shard_map/all_gather | solution.py:1173
  13.0 42.1 %collective-permute-start.1 = (bf16[800,1024]{1,0:T(8,128)(2,1)S(1)}, bf16[800,1024]{1,0:T(8,128)(2,1)S(1)}, u32[]{:S(2)}, u32[]{:S(2)}) collective-permute-start(bf16[800,1024]{1,0:T(8,128)(2,1)S(1)} %pad_maximum_fusion.1), channel_id=1, source_target_pairs={{0,0},{2,4},{4,2},{6,6},{1,1},{3,5},{5,3},{7,7},{8,8},{10,12},{12,... | collective-permute-start | bytes 4915208 | tf_op jit(solution)/shard_map/ppermute | solution.py:888
  130.7 36.2 %collective-permute-start.11 = (bf16[4,1,128,1024]{3,2,1,0:T(8,128)(2,1)S(1)}, bf16[4,1,128,1024]{3,2,1,0:T(8,128)(2,1)S(1)}, u32[]{:S(2)}, u32[]{:S(2)}) collective-permute-start(bf16[4,1,128,1024]{3,2,1,0:T(8,128)(2,1)S(1)} %pad_maximum_fusion.7.refs_11_.refs_7_), channel_id=1, source_target_pairs={{0,16},{8,24},{16,0},{24,8},{1,17},{9,25},{17,1},{25,9},{2,18},{10... | collective-permute-start | bytes 3145736 | tf_op jit(solution)/shard_map/ppermute | solution.py:884
  132.0 34.9 %collective-permute-start.10 = (bf16[4,1,128,1024]{3,2,1,0:T(8,128)(2,1)S(1)}, bf16[4,1,128,1024]{3,2,1,0:T(8,128)(2,1)S(1)}, u32[]{:S(2)}, u32[]{:S(2)}) collective-permute-start(bf16[4,1,128,1024]{3,2,1,0:T(8,128)(2,1)S(1)} %pad_maximum_fusion.7.refs_11_.refs_7_), channel_id=1, source_target_pairs={{0,8},{8,0},{16,24},{24,16},{1,9},{9,1},{17,25},{25,17},{2,10},{10... | collective-permute-start | bytes 3145736 | tf_op jit(solution)/shard_map/ppermute | solution.py:884
  133.3 32.5 %collective-permute-start.15 = (bf16[2,1,128,1024]{3,2,1,0:T(8,128)(2,1)S(1)}, bf16[2,1,128,1024]{3,2,1,0:T(8,128)(2,1)S(1)}, u32[]{:S(2)}, u32[]{:S(2)}) collective-permute-start(bf16[2,1,128,1024]{3,2,1,0:T(8,128)(2,1)S(1)} %pad_maximum_fusion.13), channel_id=1, source_target_pairs={{0,1},{1,0},{2,3},{3,2},{4,5},{5,4},{6,7},{7,6},{8,9},{9,8},{10,11... | collective-permute-start | bytes 1572872 | tf_op jit(solution)/shard_map/ppermute | solution.py:884
  196.2 35.2 %collective-permute-start.20 = (bf16[512,1024]{1,0:T(8,128)(2,1)}, bf16[512,1024]{1,0:T(8,128)(2,1)}, u32[]{:S(2)}, u32[]{:S(2)}) collective-permute-start(bf16[512,1024]{1,0:T(8,128)(2,1)} %fusion.5.refs_1_), channel_id=1, source_target_pairs={{0,1},{1,0},{4,5},{5,4},{2,3},{3,2},{6,7},{7,6},{8,9},{9,8},{12,13... | collective-permute-start | bytes 3145736 | tf_op jit(solution)/shard_map/ppermute | solution.py:884
  198.0 33.7 %collective-permute-start.24 = (bf16[4,1,128,1024]{3,2,1,0:T(8,128)(2,1)S(1)}, bf16[4,1,128,1024]{3,2,1,0:T(8,128)(2,1)}, u32[]{:S(2)}, u32[]{:S(2)}) collective-permute-start(bf16[4,1,128,1024]{3,2,1,0:T(8,128)(2,1)S(1)} %copy-done.20), channel_id=1, source_target_pairs={{0,4},{4,0},{1,5},{5,1},{2,6},{6,2},{3,7},{7,3},{8,12},{12,8},{9,1... | collective-permute-start | bytes 3145736 | tf_op jit(solution)/shard_map/ppermute | solution.py:884
  198.8 33.9 %collective-permute-start.25 = (bf16[4,1,128,1024]{3,2,1,0:T(8,128)(2,1)S(1)}, bf16[4,1,128,1024]{3,2,1,0:T(8,128)(2,1)}, u32[]{:S(2)}, u32[]{:S(2)}) collective-permute-start(bf16[4,1,128,1024]{3,2,1,0:T(8,128)(2,1)S(1)} %copy-done.18), channel_id=1, source_target_pairs={{0,4},{4,0},{1,5},{5,1},{2,6},{6,2},{3,7},{7,3},{8,12},{12,8},{9,1... | collective-permute-start | bytes 3145736 | tf_op jit(solution)/shard_map/ppermute | solution.py:884
  223.0 36.7 %collective-permute-start.31 = (bf16[4,1,128,1024]{3,2,1,0:T(8,128)(2,1)S(1)}, bf16[4,1,128,1024]{3,2,1,0:T(8,128)(2,1)}, u32[]{:S(2)}, u32[]{:S(2)}) collective-permute-start(bf16[4,1,128,1024]{3,2,1,0:T(8,128)(2,1)S(1)} %copy-done.4), channel_id=1, source_target_pairs={{0,4},{4,0},{1,5},{5,1},{2,6},{6,2},{3,7},{7,3},{8,12},{12,8},{9,1... | collective-permute-start | bytes 3145736 | tf_op jit(solution)/shard_map/ppermute | solution.py:884
  231.7 39.0 %collective-permute-start.32 = (bf16[4,1,128,1024]{3,2,1,0:T(8,128)(2,1)}, bf16[4,1,128,1024]{3,2,1,0:T(8,128)(2,1)S(1)}, u32[]{:S(2)}, u32[]{:S(2)}) collective-permute-start(bf16[4,1,128,1024]{3,2,1,0:T(8,128)(2,1)} %collective-permute-done.17.refs_1_.refs_6_.refs_11_), channel_id=1, source_target_pairs={{0,4},{4,0},{1,5},{5,1},{2,6},{6,2},{3,7},{7,3},{8,12},{12,8},{9,1... | collective-permute-start | bytes 3145736 | tf_op jit(solution)/shard_map/ppermute | solution.py:884
  232.7 39.4 %collective-permute-start.33 = (bf16[4,1,128,1024]{3,2,1,0:T(8,128)(2,1)}, bf16[4,1,128,1024]{3,2,1,0:T(8,128)(2,1)S(1)}, u32[]{:S(2)}, u32[]{:S(2)}) collective-permute-start(bf16[4,1,128,1024]{3,2,1,0:T(8,128)(2,1)} %collective-permute-done.18.refs_2_.refs_7_.refs_12_), channel_id=1, source_target_pairs={{0,4},{4,0},{1,5},{5,1},{2,6},{6,2},{3,7},{7,3},{8,12},{12,8},{9,1... | collective-permute-start | bytes 3145736 | tf_op jit(solution)/shard_map/ppermute | solution.py:884
  316.6 47.2 %collective-permute-start.42 = (bf16[4,2,128,1024]{3,2,1,0:T(8,128)(2,1)}, bf16[4,2,128,1024]{3,2,1,0:T(8,128)(2,1)}, u32[]{:S(2)}, u32[]{:S(2)}) collective-permute-start(bf16[4,2,128,1024]{3,2,1,0:T(8,128)(2,1)} %get-tuple-element.201.refs_7_.refs_4_.refs_6_), channel_id=1, source_target_pairs={{0,8},{8,0},{16,24},{24,16},{1,9},{9,1},{17,25},{25,17},{2,10},{10... | collective-permute-start | bytes 6291464 | tf_op jit(solution)/shard_map/ppermute | solution.py:884
  318.0 47.1 %collective-permute-start.43 = (bf16[4,2,128,1024]{3,2,1,0:T(8,128)(2,1)}, bf16[4,2,128,1024]{3,2,1,0:T(8,128)(2,1)}, u32[]{:S(2)}, u32[]{:S(2)}) collective-permute-start(bf16[4,2,128,1024]{3,2,1,0:T(8,128)(2,1)} %get-tuple-element.201.refs_7_.refs_4_.refs_6_), channel_id=1, source_target_pairs={{0,16},{8,24},{16,0},{24,8},{1,17},{9,25},{17,1},{25,9},{2,18},{10... | collective-permute-start | bytes 6291464 | tf_op jit(solution)/shard_map/ppermute | solution.py:884
  326.4 33.3 %collective-permute-start.45 = (bf16[512,1024]{1,0:T(8,128)(2,1)}, bf16[512,1024]{1,0:T(8,128)(2,1)S(1)}, u32[]{:S(2)}, u32[]{:S(2)}) collective-permute-start(bf16[512,1024]{1,0:T(8,128)(2,1)} %get-tuple-element.204), channel_id=1, source_target_pairs={{0,0},{2,4},{4,2},{6,6},{1,1},{3,5},{5,3},{7,7},{8,8},{10,12},{12,... | collective-permute-start | bytes 3145736 | tf_op jit(solution)/shard_map/ppermute | solution.py:888
  517.0 74.8 %collective-permute-start.60 = (bf16[4,8,128,1024]{3,2,1,0:T(8,128)(2,1)}, bf16[4,8,128,1024]{3,2,1,0:T(8,128)(2,1)}, u32[]{:S(2)}, u32[]{:S(2)}) collective-permute-start(bf16[4,8,128,1024]{3,2,1,0:T(8,128)(2,1)} %get-tuple-element.228), channel_id=1, source_target_pairs={{0,4},{4,0},{1,5},{5,1},{2,6},{6,2},{3,7},{7,3},{8,12},{12,8},{9,1... | collective-permute-start | bytes 25165832 | tf_op jit(solution)/shard_map/ppermute | solution.py:884
  607.7 46.9 %collective-permute-start.62 = (bf16[8,128,1024]{2,1,0:T(8,128)(2,1)}, bf16[8,128,1024]{2,1,0:T(8,128)(2,1)S(1)}, u32[]{:S(2)}, u32[]{:S(2)}) collective-permute-start(bf16[8,128,1024]{2,1,0:T(8,128)(2,1)} %get-tuple-element.230.refs_3_), channel_id=1, source_target_pairs={{0,16},{8,24},{16,0},{24,8},{1,17},{9,25},{17,1},{25,9},{2,18},{10... | collective-permute-start | bytes 6291464 | tf_op jit(solution)/shard_map/ppermute | solution.py:884
  607.8 46.7 %collective-permute-start.61 = (bf16[8,128,1024]{2,1,0:T(8,128)(2,1)}, bf16[8,128,1024]{2,1,0:T(8,128)(2,1)S(1)}, u32[]{:S(2)}, u32[]{:S(2)}) collective-permute-start(bf16[8,128,1024]{2,1,0:T(8,128)(2,1)} %get-tuple-element.229.refs_2_), channel_id=1, source_target_pairs={{0,8},{8,0},{16,24},{24,16},{1,9},{9,1},{17,25},{25,17},{2,10},{10... | collective-permute-start | bytes 6291464 | tf_op jit(solution)/shard_map/ppermute | solution.py:884
  672.5 34.4 %collective-permute-start.66 = (bf16[4,128,1024]{2,1,0:T(8,128)(2,1)S(1)}, bf16[4,128,1024]{2,1,0:T(8,128)(2,1)S(1)}, u32[]{:S(2)}, u32[]{:S(2)}) collective-permute-start(bf16[4,128,1024]{2,1,0:T(8,128)(2,1)S(1)} %add_convert_fusion.5), channel_id=1, source_target_pairs={{0,8},{8,0},{16,24},{24,16},{1,9},{9,1},{17,25},{25,17},{2,10},{10... | collective-permute-start | bytes 3145736 | tf_op jit(solution)/shard_map/ppermute | solution.py:884
  673.1 33.7 %collective-permute-start.67 = (bf16[4,128,1024]{2,1,0:T(8,128)(2,1)S(1)}, bf16[4,128,1024]{2,1,0:T(8,128)(2,1)S(1)}, u32[]{:S(2)}, u32[]{:S(2)}) collective-permute-start(bf16[4,128,1024]{2,1,0:T(8,128)(2,1)S(1)} %add_convert_fusion.4), channel_id=1, source_target_pairs={{0,16},{8,24},{16,0},{24,8},{1,17},{9,25},{17,1},{25,9},{2,18},{10... | collective-permute-start | bytes 3145736 | tf_op jit(solution)/shard_map/ppermute | solution.py:884
  716.8 71.3 %collective-permute-start.71 = (bf16[8,128,1024]{2,1,0:T(8,128)(2,1)}, bf16[8,128,1024]{2,1,0:T(8,128)(2,1)}, u32[]{:S(2)}, u32[]{:S(2)}) collective-permute-start(bf16[8,128,1024]{2,1,0:T(8,128)(2,1)} %get-tuple-element.252.refs_5_), channel_id=1, source_target_pairs={{0,16},{8,24},{16,0},{24,8},{1,17},{9,25},{17,1},{25,9},{2,18},{10... | collective-permute-start | bytes 6291464 | tf_op jit(solution)/shard_map/ppermute | solution.py:884
  717.5 73.7 %collective-permute-start.70 = (bf16[8,128,1024]{2,1,0:T(8,128)(2,1)}, bf16[8,128,1024]{2,1,0:T(8,128)(2,1)}, u32[]{:S(2)}, u32[]{:S(2)}) collective-permute-start(bf16[8,128,1024]{2,1,0:T(8,128)(2,1)} %get-tuple-element.251.refs_4_), channel_id=1, source_target_pairs={{0,8},{8,0},{16,24},{24,16},{1,9},{9,1},{17,25},{25,17},{2,10},{10... | collective-permute-start | bytes 6291464 | tf_op jit(solution)/shard_map/ppermute | solution.py:884
  721.6 39.1 %collective-permute-start.72 = (bf16[4,128,1024]{2,1,0:T(8,128)(2,1)}, bf16[4,128,1024]{2,1,0:T(8,128)(2,1)S(1)}, u32[]{:S(2)}, u32[]{:S(2)}) collective-permute-start(bf16[4,128,1024]{2,1,0:T(8,128)(2,1)} %add_convert_fusion.3), channel_id=1, source_target_pairs={{0,1},{1,0},{2,3},{3,2},{4,5},{5,4},{6,7},{7,6},{8,9},{9,8},{10,11... | collective-permute-start | bytes 3145736 | tf_op jit(solution)/shard_map/ppermute | solution.py:884
  722.4 64.6 %collective-permute-start.73 = (bf16[2,2,128,1024]{3,2,1,0:T(8,128)(2,1)}, bf16[2,2,128,1024]{3,2,1,0:T(8,128)(2,1)S(1)}, u32[]{:S(2)}, u32[]{:S(2)}) collective-permute-start(bf16[2,2,128,1024]{3,2,1,0:T(8,128)(2,1)} %get-tuple-element.256), channel_id=1, source_target_pairs={{0,8},{8,0},{16,24},{24,16},{1,9},{9,1},{17,25},{25,17},{2,10},{10... | collective-permute-start | bytes 3145736 | tf_op jit(solution)/shard_map/ppermute | solution.py:884
  762.6 62.9 %collective-permute-start.76 = (bf16[2,128,1024]{2,1,0:T(8,128)(2,1)S(1)}, bf16[2,128,1024]{2,1,0:T(8,128)(2,1)S(1)}, u32[]{:S(2)}, u32[]{:S(2)}) collective-permute-start(bf16[2,128,1024]{2,1,0:T(8,128)(2,1)S(1)} %add_convert_fusion.9), channel_id=1, source_target_pairs={{0,2},{2,0},{1,3},{3,1},{4,6},{6,4},{5,7},{7,5},{8,10},{10,8},{9,1... | collective-permute-start | bytes 1572872 | tf_op jit(solution)/shard_map/ppermute | solution.py:884
  787.2 38.3 %collective-permute-start.77 = (bf16[2,128,1024]{2,1,0:T(8,128)(2,1)S(1)}, bf16[2,128,1024]{2,1,0:T(8,128)(2,1)S(1)}, u32[]{:S(2)}, u32[]{:S(2)}) collective-permute-start(bf16[2,128,1024]{2,1,0:T(8,128)(2,1)S(1)} %fusion.9), channel_id=1, source_target_pairs={{0,16},{8,24},{16,0},{24,8},{1,17},{9,25},{17,1},{25,9},{2,18},{10... | collective-permute-start | bytes 1572872 | tf_op jit(solution)/shard_map/ppermute | solution.py:884
  789.8 32.6 %collective-permute-start.74 = (bf16[4,128,1024]{2,1,0:T(8,128)(2,1)S(1)}, bf16[4,128,1024]{2,1,0:T(8,128)(2,1)S(1)}, u32[]{:S(2)}, u32[]{:S(2)}) collective-permute-start(bf16[4,128,1024]{2,1,0:T(8,128)(2,1)S(1)} %add_convert_fusion.2), channel_id=1, source_target_pairs={{0,8},{8,0},{16,24},{24,16},{1,9},{9,1},{17,25},{25,17},{2,10},{10... | collective-permute-start | bytes 3145736 | tf_op jit(solution)/shard_map/ppermute | solution.py:884
  792.8 32.7 %collective-permute-start.75 = (bf16[4,128,1024]{2,1,0:T(8,128)(2,1)S(1)}, bf16[4,128,1024]{2,1,0:T(8,128)(2,1)S(1)}, u32[]{:S(2)}, u32[]{:S(2)}) collective-permute-start(bf16[4,128,1024]{2,1,0:T(8,128)(2,1)S(1)} %add_convert_fusion), channel_id=1, source_target_pairs={{0,16},{8,24},{16,0},{24,8},{1,17},{9,25},{17,1},{25,9},{2,18},{10... | collective-permute-start | bytes 3145736 | tf_op jit(solution)/shard_map/ppermute | solution.py:884
  853.8 47.9 %collective-permute-start.79 = (bf16[512,1024]{1,0:T(8,128)(2,1)}, bf16[512,1024]{1,0:T(8,128)(2,1)S(1)}, u32[]{:S(2)}, u32[]{:S(2)}) collective-permute-start(bf16[512,1024]{1,0:T(8,128)(2,1)} %fusion.refs_1_), channel_id=1, source_target_pairs={{0,1},{1,0},{4,5},{5,4},{2,3},{3,2},{6,7},{7,6},{8,9},{9,8},{12,13... | collective-permute-start | bytes 3145736 | tf_op jit(solution)/shard_map/ppermute | solution.py:884
  869.1 32.5 %collective-permute-start.82 = (bf16[2,2,128,1024]{3,2,1,0:T(8,128)(2,1)}, bf16[2,2,128,1024]{3,2,1,0:T(8,128)(2,1)S(1)}, u32[]{:S(2)}, u32[]{:S(2)}) collective-permute-start(bf16[2,2,128,1024]{3,2,1,0:T(8,128)(2,1)} %get-tuple-element.275), channel_id=1, source_target_pairs={{0,8},{8,0},{16,24},{24,16},{1,9},{9,1},{17,25},{25,17},{2,10},{10... | collective-permute-start | bytes 3145736 | tf_op jit(solution)/shard_map/ppermute | solution.py:884
  872.5 51.5 %collective-permute-start.87 = (bf16[2,128,1024]{2,1,0:T(8,128)(2,1)}, bf16[2,128,1024]{2,1,0:T(8,128)(2,1)}, u32[]{:S(2)}, u32[]{:S(2)}) collective-permute-start(bf16[2,128,1024]{2,1,0:T(8,128)(2,1)} %add_convert_fusion.6), channel_id=1, source_target_pairs={{0,2},{2,0},{1,3},{3,1},{4,6},{6,4},{5,7},{7,5},{8,10},{10,8},{9,1... | collective-permute-start | bytes 1572872 | tf_op jit(solution)/shard_map/ppermute | solution.py:884
  910.9 39.7 %collective-permute-start.80 = (bf16[512,1024]{1,0:T(8,128)(2,1)S(1)}, bf16[512,1024]{1,0:T(8,128)(2,1)S(1)}, u32[]{:S(2)}, u32[]{:S(2)}) collective-permute-start(bf16[512,1024]{1,0:T(8,128)(2,1)S(1)} %fusion.2), channel_id=1, source_target_pairs={{0,0},{2,4},{4,2},{6,6},{1,1},{3,5},{5,3},{7,7},{8,8},{10,12},{12,... | collective-permute-start | bytes 3145736 | tf_op jit(solution)/shard_map/ppermute | solution.py:888
  919.6 36.5 %collective-permute-start.84 = (bf16[2,128,1024]{2,1,0:T(8,128)(2,1)}, bf16[2,128,1024]{2,1,0:T(8,128)(2,1)S(1)}, u32[]{:S(2)}, u32[]{:S(2)}) collective-permute-start(bf16[2,128,1024]{2,1,0:T(8,128)(2,1)} %pad_maximum_fusion.14), channel_id=1, source_target_pairs={{0,0},{2,4},{4,2},{6,6},{1,1},{3,5},{5,3},{7,7},{8,8},{10,12},{12,... | collective-permute-start | bytes 1572872 | tf_op jit(solution)/shard_map/ppermute | solution.py:888
  (167 other events, 1884.0 us)
Sparse Core Ops, SparseCore 0:
  110.7 69.5 all-gather.1

commit v11 on v10

--- a/solution.py
+++ b/solution.py
@@ -502,7 +502,8 @@
 
 
 def finish(flow, units, heads, small):
-    layers, rows, cols = heads[0].shape
+    layers = len(units)
+    rows, cols = heads[0][0].shape
     in_width = cols * 3 // 4
     pairs = in_width // (3 * PAIR)
     width = units[0][0].shape[2]
@@ -510,17 +511,16 @@
     def body(scal_ref, *refs):
         qkv_ref, out_ref, up_ref, down_ref, square_ref = refs[-5:]
         small_ref, refs = refs[-6], refs[:-6]
-        first, second, refs = refs[0], refs[1], refs[2:]
         squares = jnp.sum(small_ref[...] * small_ref[...], keepdims=True)
         for l in range(layers):
-            unit_refs = refs[5 * l : 5 * l + 5]
+            unit_refs, (first, second) = refs[7 * l : 7 * l + 5], refs[7 * l + 5 : 7 * l + 7]
             for m, target in enumerate((down_ref, up_ref)):
                 total = unit_refs[0][m].astype(F32)
                 for part in unit_refs[1:]:
                     total = total + part[m].astype(F32)
                 target[l] = total
                 squares = squares + jnp.sum(jnp.sum(total * total, 0, keepdims=True), 1, keepdims=True)
-            total = first[l].astype(F32) + second[l].astype(F32)
+            total = first[...].astype(F32) + second[...].astype(F32)
             squares = squares + jnp.sum(jnp.sum(total * total, 0, keepdims=True), 1, keepdims=True)
             out_ref[l] = total[:, in_width:]
             for pair in range(pairs):
@@ -529,10 +529,10 @@
                     qkv_ref[l, which, :, pair * PAIR : (pair + 1) * PAIR] = total[:, base : base + PAIR]
         square_ref[...] = jnp.broadcast_to(squares, (8, 128))
 
-    specs, args = [full((layers, rows, cols))] * 2, list(heads)
+    specs, args = [], []
     for l in range(layers):
-        specs += [pl.BlockSpec((2, rows, width), lambda *_: (0, 0, 0))] * 5
-        args += units[l]
+        specs += [pl.BlockSpec((2, rows, width), lambda *_: (0, 0, 0))] * 5 + [full((rows, cols))] * 2
+        args += [*units[l], *heads[l]]
     shapes = [(layers, 3, rows, in_width // 3), (layers, rows, cols - in_width), (layers, rows, width), (layers, rows, width),
               (8, 128)]
     return call(
@@ -1245,28 +1245,29 @@
         if first:
             flow.wait(up0.near_x, up0.near_y)
             flow.hold(both1=both1.two, down0=down0.own)
-            up0.corner()
-            up0.swap("own")
+            up0.swap("own", "near_x", "near_y")
         if last:
             flow.wait(both1.near_x, both1.near_y, top_grad)
             both1.corner()
             both1.swap("near_x", "near_y")
         send = project_out(flow, [ctx], (2, 3), w_heads, out_cols, True, "project_attn")
         flow.wait(send)
+        if first:
+            pair = with_sibling(flow.free("heads1"))
         keep = project_out(flow, [ctx], (0, 1), w_heads, out_cols, False, "project_attn")
         attn, passed = sum_group(keep, send)
         if first:
-            flow.wait(passed, gathered)
+            flow.wait(passed, gathered, pair, *up0.theirs.values())
             flow.hold(near_x=up0.near_x, near_y=up0.near_y)
             gate(flow)
             down0.own, up0.near_x, up0.near_y = flow.free("down0"), flow.free("near_x"), flow.free("near_y")
-            up0.swap("near_x", "near_y", "far_a", "far_b")
+            up0.corner()
+            up0.swap("far_a", "far_b")
             down0.near()
             down0.swap("own")
             flow.wait(down0.near_x, down0.near_y)
             down0.corner()
             down0.swap("near_x", "near_y")
-            pair = with_sibling(flow.free("heads1"))
             flow.hold(pair=pair)
             w_up = up0.pieces(), 0
         elif last:
@@ -1286,20 +1287,22 @@
         n1, hs, r1, act, slope = norm_up(flow, prev, attn, table, used, *w_up, up_bias_full[l], tz)
         if first:
             pair = turn(flow.free("pair"))
-            flow.wait(n1)
+            flow.wait(n1, *down0.theirs.values())
             flow.hold(far_a=down0.far_a, far_b=down0.far_b)
             gate(flow)
             down0.far_a, down0.far_b = flow.free("far_a"), flow.free("far_b")
             down0.swap("far_a", "far_b")
             both1.two = flow.free("both1")
             both1.near_z()
-            flow.wait(pair)
+            flow.hold(pair=pair, pair_twin=pair)
+            gate(flow)
+            across = flip(flow.free("pair"), "q", 1)
             w_down = down0.pieces(), 0
         used = (gain_row(l, 0), shift_row(l, 1), shift_row(l, 2), gain_row(l, 1), shift_row(l, 3))
         n2, y_low, r2 = down_norm(flow, act, *w_down, n1, table, used, tz)
         if first:
-            members = from_members(pair, "q")
-            weights_of.append(heads_pieces(jnp.stack(members[:2]), jnp.stack(members[2:]), bias_size, hz, where, zh))
+            near = jnp.stack([flow.free("pair_twin"), across])
+            weights_of.append(heads_along_y(near, bias_size, hz, where, zh))
         kept.append((xs, qkv, ctx, wide, lse, n1, hs, r1, act, slope, n2, r2, w_heads, w_up, w_down))
         x_low, prev, prev_gain, prev_shift = y_low, n2, gain_row(l, 1), shift_row(l, 3)
     layer_output = turn(x_low)
@@ -1338,7 +1341,7 @@
         else:
             units.mine()
             if beside:
-                flow.wait(*late)
+                flow.wait(*late, above_heads.got)
             forward(flow, gas, *units.made)
         gc_near = project_in(flow, (gas[0], gas[2]), False, w_heads, out_cols, None, "project_gc")
         flow.wait(gc_near)
@@ -1358,7 +1361,7 @@
             above_heads.keep, above.own = flow.free("keep"), flow.free("above")
         flow.wait(gqkv[0])
         if beside:
-            flow.wait(*units.near(), *early, above_heads.got)
+            flow.wait(*units.near(), *early)
             above.far_z()
             units.far()
             above_heads.along_y()
@@ -1369,6 +1372,7 @@
             units.near_z()
             flow.wait(units.passing, units.late_y, above.last, above_heads.got)
             above_halves = above_heads.halves(zh)
+            done = turn(above_halves[0]), uncross(above_halves[1])
         send = project_out(flow, gqkv, (2, 3), w_heads, in_cols, True, "project_gx")
         flow.wait(send)
         if beside:
@@ -1382,6 +1386,7 @@
         elif small_slice:
             units.own = flow.free("own")
             units.far_z()
+            flow.wait(*done)
         *buckets, qkv_sums = heads_grad(flow, xs, gqkv, gas, ctx)
         heads = HeadsGrad(*buckets)
         units_of[l], heads_of[l] = units, heads
@@ -1419,8 +1424,7 @@
         small_sums = fold_small(flow.free("small"), 2, 3)
         halves = heads.halves(zh)
         small_out = fold_small(small_sums, 3, 5).reshape(layers, -1)
-        stacked = [jnp.stack([half, above_half]) for half, above_half in zip(halves, above_halves)]
-        arrived = turn(stacked[0]), uncross(stacked[1])
+        arrived = [(turn(halves[0]), uncross(halves[1])), done]
         flow.hold(grad=input_grad, output=layer_output)
         qkv_grad, out_grad, up_grad, down_grad, squares = finish(
             flow, [member.parts() for member in units_of], arrived, small_out

time: 1010 us -> 991 us (0.981)
    ppermute x7 -> x8, waiting for transfers between devices: 86.4 us -> 80 us  [turn(): lax.ppermute(values_in, ('c', 'zh'), [(2 * a + b, 2 * b + a) for a in ran...]
    ppermute x7 -> x8, starting transfers between devices: 30.5 us -> 35.9 us  [turn(): lax.ppermute(values_in, ('c', 'zh'), [(2 * a + b, 2 * b + a) for a in ran...]
    ppermute x91 -> x90, starting transfers between devices: 84.4 us -> 79.9 us  [flip(): lax.ppermute(values_in, axes, [(a, a ^ mask) for a in range(lax.axis_size...]
    ppermute x91 -> x90, waiting for transfers between devices: 164 us -> 168 us  [flip(): lax.ppermute(values_in, axes, [(a, a ^ mask) for a in range(lax.axis_size...]
    unnamed x213 -> x210, local copies, waits for them, and re-layouts: 37.7 us -> 40.2 us
    pallas_call x48 -> x49, Pallas kernels: 475 us -> 475 us  [call(): pl.pallas_call(wrapped, grid_spec=pltpu.PrefetchScalarGridSpec(num_scalar...]
  transfers between devices with their start and end apart: 100 -> 101, of which waited for: 36 -> 34; matrix products, arithmetic and copies ran while one was open for 11% -> 9% of each run, Pallas kernels for 39% -> 40%
where the time goes in v11:
time: 991 us; the launch traced here: 983 us
  Pallas kernels  475 us (48%)
  waiting for transfers between devices  248 us (25%)
  starting transfers between devices  116 us (12%)
  local copies, waits for them, and re-layouts  71 us (7%)
  other arithmetic  54.4 us (5%)
  between operations  18.1 us (2%)
    pallas_call x49, Pallas kernels, call(): pl.pallas_call(wrapped, grid_spec=pltpu.PrefetchScalarGridSpec(num_scalar...  475 us
    ppermute x90, waiting for transfers between devices, flip(): lax.ppermute(values_in, axes, [(a, a ^ mask) for a in range(lax.axis_size...  168 us
    ppermute x8, waiting for transfers between devices, turn(): lax.ppermute(values_in, ('c', 'zh'), [(2 * a + b, 2 * b + a) for a in ran...  80 us
    ppermute x90, starting transfers between devices, flip(): lax.ppermute(values_in, axes, [(a, a ^ mask) for a in range(lax.axis_size...  79.9 us
    unnamed x210, local copies, waits for them, and re-layouts  40.2 us
    ppermute x8, starting transfers between devices, turn(): lax.ppermute(values_in, ('c', 'zh'), [(2 * a + b, 2 * b + a) for a in ran...  35.9 us
  transfers between devices with their start and end apart: 101, of which 34 were waited for; matrix products, arithmetic and copies ran while one was open for 9% of the time, Pallas kernels for 40%

profile of v11, /device:TPU:1, one launch (start us, length us, event | category | flops | bytes accessed | tf_op | source)
XLA Modules:
  0.0 983.2 jit_solution(2987296080840488663)
XLA Ops:
  18.8 36.3 %collective-permute-done.1 = bf16[800,1024]{1,0:T(8,128)(2,1)S(1)} collective-permute-done((bf16[800,1024]{1,0:T(8,128)(2,1)S(1)}, bf16[800,1024]{1,0:T(8,128)(2,1)S(1)}, u32[]{:S(2)}, u32[]{:S(2)}) %collective-permute-start.1) | collective-permute-done | bytes 1638432 | tf_op jit(solution)/shard_map/ppermute | solution.py:888
  86.7 11.6 %collective-permute-done.7.refs_9_ = bf16[512,1024]{1,0:T(8,128)(2,1)S(1)} collective-permute-done((bf16[512,1024]{1,0:T(8,128)(2,1)}, bf16[512,1024]{1,0:T(8,128)(2,1)S(1)}, u32[]{:S(2)}, u32[]{:S(2)}) %collective-permute-start.7) | collective-permute-done | bytes 1048608 | tf_op jit(solution)/shard_map/ppermute | solution.py:884
  111.6 11.4 %collective-permute-done.12 = s32[1,4]{1,0:T(1,128)S(1)} collective-permute-done((s32[1,4]{1,0:T(1,128)S(1)}, s32[1,4]{1,0:T(1,128)S(1)}, u32[]{:S(2)}, u32[]{:S(2)}) %collective-permute-start.12) | collective-permute-done | bytes 48 | tf_op jit(solution)/shard_map/ppermute | solution.py:888
  136.9 28.4 %attend_forward.2 = (bf16[4,512,256]{2,1,0:T(8,128)(2,1)}, f32[4,512,256]{2,1,0:T(8,128)}, f32[4,8,512]{2,1,0:T(8,128)}, bf16[144,1024]{1,0:T(8,128)(2,1)}) custom-call(s32[5]{0:T(128)} %stack.171.refs_0_, s32[4]{0:T(128)} %bitcast.283, bf16[144,1024]{1,0:T(8,128)(2,1)} %get-tuple-element.173.refs_2_, ...), custom_call_target="tpu_custom_call", output_to_operand_aliasing={{3}: (2, {})} | custom-call | flops 14000000000 | bytes 1024 | tf_op jit(solution)/shard_map/attend_forward/pallas_call | solution.py:80
  200.2 26.8 %collective-permute-done.24.refs_14_.refs_10_ = bf16[2,1,128,1024]{3,2,1,0:T(8,128)(2,1)} collective-permute-done((bf16[2,1,128,1024]{3,2,1,0:T(8,128)(2,1)S(1)}, bf16[2,1,128,1024]{3,2,1,0:T(8,128)(2,1)}, u32[]{:S(2)}, u32[]{:S(2)}) %collective-permute-start.24) | collective-permute-done | bytes 524320 | tf_op jit(solution)/shard_map/ppermute | solution.py:884
  235.4 19.0 %norm_up.2 = (f32[512,1024]{1,0:T(8,128)}, bf16[512,1024]{1,0:T(8,128)(2,1)}, f32[512,128]{1,0:T(8,128)}, bf16[512,4096]{1,0:T(8,128)(2,1)}, bf16[512,4096]{1,0:...) custom-call(s32[5]{0:T(128)} %stack.171.refs_0_, ...), custom_call_target="tpu_custom_call", output_to_operand_aliasing={{5}: (3, {}), {6}: (4, {})} | custom-call | flops 7000000000 | bytes 1024 | tf_op jit(solution)/shard_map/norm_up/pallas_call | solution.py:80
  260.6 12.5 %collective-permute-done.28.refs_1_ = bf16[2,144,1024]{2,1,0:T(8,128)(2,1)S(1)} collective-permute-done((bf16[2,144,1024]{2,1,0:T(8,128)(2,1)}, bf16[2,144,1024]{2,1,0:T(8,128)(2,1)S(1)}, u32[]{:S(2)}, u32[]{:S(2)}) %collective-permute-start.28) | collective-permute-done | bytes 589856 | tf_op jit(solution)/shard_map/ppermute | solution.py:888
  276.3 14.4 %down_norm.2 = (f32[512,1024]{1,0:T(8,128)}, bf16[512,1024]{1,0:T(8,128)(2,1)}, f32[512,128]{1,0:T(8,128)}, bf16[2,144,1024]{2,1,0:T(8,128)(2,1)}) custom-call(s32[5]{0:T(128)} %stack.171.refs_0_, bf16[2,144,1024]{2,1,0:T(8,128)(2,1)} %get-tuple-element.193.refs_1_, ...), custom_call_target="tpu_custom_call", output_to_operand_aliasing={{3}: (1, {})} | custom-call | flops 7000000000 | bytes 1024 | tf_op jit(solution)/shard_map/down_norm/pallas_call | solution.py:80
  296.4 12.6 %collective-permute-done.38.refs_5_.refs_6_.refs_4_ = bf16[2,2,144,1024]{3,2,1,0:T(8,128)(2,1)S(1)} collective-permute-done((bf16[2,2,144,1024]{3,2,1,0:T(8,128)(2,1)S(1)}, bf16[2,2,144,1024]{3,2,1,0:T(8,128)(2,1)S(1)}, u32[]{:S(2)}, u32[]{:S(2)}) %collective-permute-start.38) | collective-permute-done | bytes 1179680 | tf_op jit(solution)/shard_map/ppermute | solution.py:884
  335.3 28.8 %attend_forward.3 = (bf16[4,512,256]{2,1,0:T(8,128)(2,1)}, f32[4,512,256]{2,1,0:T(8,128)}, f32[4,8,512]{2,1,0:T(8,128)}) custom-call(s32[5]{0:T(128)} %stack.171.refs_0_, s32[4]{0:T(128)} %bitcast.284, bf16[2,512,768]{2,1,0:T(8,128)(2,1)} %project_qkv.6.refs_1_.refs_2_.refs_3_, bf16[2,512,768]{2,1,0:T(8,128)(2,1)} %get-tuple-element.207.refs_3_.refs_4_), custom_call_target="tpu_custom_call" | custom-call | flops 14000000000 | bytes 1024 | tf_op jit(solution)/shard_map/attend_forward/pallas_call | solution.py:80
  388.2 14.1 %collective-permute-done.47.refs_2_ = bf16[2,2,128,1024]{3,2,1,0:T(8,128)(2,1)S(1)} collective-permute-done((bf16[2,2,128,1024]{3,2,1,0:T(8,128)(2,1)}, bf16[2,2,128,1024]{3,2,1,0:T(8,128)(2,1)S(1)}, u32[]{:S(2)}, u32[]{:S(2)}) %collective-permute-start.47) | collective-permute-done | bytes 1048608 | tf_op jit(solution)/shard_map/ppermute | solution.py:884
  417.3 19.0 %norm_up.3 = (f32[512,1024]{1,0:T(8,128)}, bf16[512,1024]{1,0:T(8,128)(2,1)}, f32[512,128]{1,0:T(8,128)}, bf16[512,4096]{1,0:T(8,128)(2,1)}, bf16[512,4096]{1,0:T(8,128)(2,1)}) custom-call(s32[5]{0:T(128)} %stack.171.refs_0_, f32[512,1024]{1,0:T(8,128)} %get-tuple-element.210.refs_1_.refs_6_, bf16[512,1024]{1,0:T(8,128)(2,1)} %get-tuple-element.211.refs_2_, ...), custom_call_target="tpu_custom_call" | custom-call | flops 7000000000 | bytes 1024 | tf_op jit(solution)/shard_map/norm_up/pallas_call | solution.py:80
  436.3 14.3 %down_norm.3 = (f32[512,1024]{1,0:T(8,128)}, bf16[512,1024]{1,0:T(8,128)(2,1)}, f32[512,128]{1,0:T(8,128)}) custom-call(s32[5]{0:T(128)} %stack.171.refs_0_, bf16[512,4096]{1,0:T(8,128)(2,1)} %get-tuple-element.214.refs_1_.refs_3_, f32[512,1024]{1,0:T(8,128)} %get-tuple-element.215.refs_2_.refs_4_, ...), custom_call_target="tpu_custom_call" | custom-call | flops 7000000000 | bytes 1024 | tf_op jit(solution)/shard_map/down_norm/pallas_call | solution.py:80
  456.0 12.6 %units_back.2 = (f32[512,1024]{1,0:T(8,128)}, bf16[512,1024]{1,0:T(8,128)(2,1)}, f32[8,1024]{1,0:T(8,128)}, bf16[512,4096]{1,0:T(8,128)(2,1)}, f32[4,1,1024]{2,1,0:T(1,128)}) custom-call(s32[5]{0:T(128)} %stack.171.refs_0_, bf16[512,1024]{1,0:T(8,128)(2,1)} %copy-done.75, f32[512,1024]{1,0:T(8,128)} %get-tuple-element.217.refs_2_, ...), custom_call_target="tpu_custom_call" | custom-call | flops 15749999616 | bytes 1024 | tf_op jit(solution)/shard_map/units_back/pallas_call | solution.py:80
  468.6 11.3 %collective-permute-done.54.refs_1_ = bf16[512,1024]{1,0:T(8,128)(2,1)S(1)} collective-permute-done((bf16[512,1024]{1,0:T(8,128)(2,1)}, bf16[512,1024]{1,0:T(8,128)(2,1)S(1)}, u32[]{:S(2)}, u32[]{:S(2)}) %collective-permute-start.54) | collective-permute-done | bytes 1048608 | tf_op jit(solution)/shard_map/ppermute | solution.py:888
  480.9 14.9 %up_back.2 = (f32[512,1024]{1,0:T(8,128)}, bf16[512,1024]{1,0:T(8,128)(2,1)}, f32[8,1024]{1,0:T(8,128)}, bf16[512,1024]{1,0:T(8,128)(2,1)}) custom-call(s32[5]{0:T(128)} %stack.171.refs_0_, bf16[512,1024]{1,0:T(8,128)(2,1)} %copy-done.15, bf16[512,4096]{1,0:T(8,128)(2,1)} %get-tuple-element.220.refs_2_.refs_5_, ...), custom_call_target="tpu_custom_call", output_to_operand_aliasing={{3}: (1, {})} | custom-call | flops 7000000000 | bytes 1024 | tf_op jit(solution)/shard_map/up_back/pallas_call | solution.py:80
  496.1 12.7 %grads_theirs.2.refs_1_.refs_2_ = bf16[4,8,128,1024]{3,2,1,0:T(8,128)(2,1)} custom-call(s32[5]{0:T(128)} %stack.171.refs_0_, bf16[512,1024]{1,0:T(8,128)(2,1)} %get-tuple-element.223.refs_1_.refs_10_, bf16[512,1024]{1,0:T(8,128)(2,1)} %get-tuple-element.224.refs_2_, bf16[512,4096]{1,0:T(8,128)(2,1)} %get-tuple-element.214.refs_1_.refs_3_, ...), custom_call_target="tpu_custom_call" | custom-call | flops 70000000 | bytes 1024 | tf_op jit(solution)/shard_map/grads_theirs/pallas_call | solution.py:80
  522.8 28.8 %attend_backward.4.refs_2_.refs_1_.refs_14_ = bf16[4,512,384]{2,1,0:T(8,128)(2,1)} custom-call(s32[5]{0:T(128)} %stack.171.refs_0_, s32[4]{0:T(128)} %gate.18.refs_1_, bf16[2,512,768]{2,1,0:T(8,128)(2,1)} %project_qkv.6.refs_1_.refs_2_.refs_3_, bf16[2,512,768]{2,1,0:T(8,128)(2,1)} %get-tuple-element.207.refs_3_.refs_4_, ...), custom_call_target="tpu_custom_call" | custom-call | flops 10499999744 | bytes 1024 | tf_op jit(solution)/shard_map/attend_backward/pallas_call | solution.py:80
  551.6 29.0 %attend_backward.5.refs_2_.refs_3_.refs_15_ = bf16[4,512,384]{2,1,0:T(8,128)(2,1)} custom-call(s32[5]{0:T(128)} %stack.171.refs_0_, s32[4]{0:T(128)} %gate.18.refs_1_, bf16[4,512,384]{2,1,0:T(8,128)(2,1)} %attend_backward.4.refs_2_.refs_1_.refs_14_, bf16[2,512,768]{2,1,0:T(8,128)(2,1)} %project_qkv.6.refs_1_.refs_2_.refs_3_, ...), custom_call_target="tpu_custom_call" | custom-call | flops 10499999744 | bytes 1024 | tf_op jit(solution)/shard_map/attend_backward/pallas_call | solution.py:80
  596.6 15.8 %grads_mine.2 = (bf16[8,128,1024]{2,1,0:T(8,128)(2,1)}, bf16[8,128,1024]{2,1,0:T(8,128)(2,1)}, bf16[8,128,1024]{2,1,0:T(8,128)(2,1)}, bf16[4,128,1024]{2,1,0:T(8,128)(2,1)}, bf16[4,128,1024]{2,1,0:T(8,128)(2,1)}) custom-call(s32[5]{0:T(128)} %stack.171.refs_0_, bf16[512,1024]{1,0:T(8,128)(2,1)} %copy-done.32, bf16[512,1024]{1,0:T(8,128)(2,1)} %get-tuple-element.224.refs_2_, ...), custom_call_target="tpu_custom_call" | custom-call | flops 70000000 | bytes 1024 | tf_op jit(solution)/shard_map/grads_mine/pallas_call | solution.py:80
  614.8 13.1 %heads_grad.2 = (bf16[2,2,128,1024]{3,2,1,0:T(8,128)(2,1)}, bf16[2,2,128,1024]{3,2,1,0:T(8,128)(2,1)}, f32[1,768]{1,0:T(1,128)}) custom-call(s32[5]{0:T(128)} %stack.171.refs_0_, bf16[8,128,1024]{2,1,0:T(8,128)(2,1)} %get-tuple-element.233.refs_1_.refs_5_, bf16[8,128,1024]{2,1,0:T(8,128)(2,1)} %get-tuple-element.231.refs_2_, ...), custom_call_target="tpu_custom_call" | custom-call | flops 70000000 | bytes 1024 | tf_op jit(solution)/shard_map/heads_grad/pallas_call | solution.py:80
  627.8 14.2 %units_back.3 = (f32[512,1024]{1,0:T(8,128)}, bf16[512,1024]{1,0:T(8,128)(2,1)}, f32[8,1024]{1,0:T(8,128)}, bf16[512,4096]{1,0:T(8,128)(2,1)}, f32[4,1,1024]{2,1,0:T(1,128)}) custom-call(s32[5]{0:T(128)} %stack.171.refs_0_, bf16[2,2,128,1024]{3,2,1,0:T(8,128)(2,1)} %get-tuple-element.236.refs_1_.refs_3_, f32[512,1024]{1,0:T(8,128)} %get-tuple-element.237.refs_2_, ...), custom_call_target="tpu_custom_call" | custom-call | flops 15749999616 | bytes 1024 | tf_op jit(solution)/shard_map/units_back/pallas_call | solution.py:80
  642.0 17.3 %collective-permute-done.61.refs_2_ = bf16[8,128,1024]{2,1,0:T(8,128)(2,1)S(1)} collective-permute-done((bf16[8,128,1024]{2,1,0:T(8,128)(2,1)}, bf16[8,128,1024]{2,1,0:T(8,128)(2,1)S(1)}, u32[]{:S(2)}, u32[]{:S(2)}) %collective-permute-start.61) | collective-permute-done | bytes 2097184 | tf_op jit(solution)/shard_map/ppermute | solution.py:884
  661.6 12.8 %grads_theirs.3 = (bf16[4,8,128,1024]{3,2,1,0:T(8,128)(2,1)}, bf16[2,2,128,1024]{3,2,1,0:T(8,128)(2,1)}) custom-call(s32[5]{0:T(128)} %stack.171.refs_0_, bf16[8,128,1024]{2,1,0:T(8,128)(2,1)} %copy-done.6, bf16[8,128,1024]{2,1,0:T(8,128)(2,1)} %copy-done.17, ...), custom_call_target="tpu_custom_call", output_to_operand_aliasing={{1}: (3, {})} | custom-call | flops 70000000 | bytes 1024 | tf_op jit(solution)/shard_map/grads_theirs/pallas_call | solution.py:80
  681.4 15.1 %up_back.3 = (f32[512,1024]{1,0:T(8,128)}, bf16[512,1024]{1,0:T(8,128)(2,1)}, f32[8,1024]{1,0:T(8,128)}) custom-call(s32[5]{0:T(128)} %stack.171.refs_0_, bf16[4,8,128,1024]{3,2,1,0:T(8,128)(2,1)} %get-tuple-element.244.refs_1_, bf16[512,4096]{1,0:T(8,128)(2,1)} %get-tuple-element.243.refs_7_.refs_2_.refs_5_, f32[512,1024]{1,0:T(8,128)} %get-tuple-element.245.refs_3_, ...), custom_call_target="tpu_custom_call" | custom-call | flops 7000000000 | bytes 1024 | tf_op jit(solution)/shard_map/up_back/pallas_call | solution.py:80
  698.6 15.9 %grads_mine.3 = (bf16[8,128,1024]{2,1,0:T(8,128)(2,1)}, bf16[8,128,1024]{2,1,0:T(8,128)(2,1)}, bf16[8,128,1024]{2,1,0:T(8,128)(2,1)}, bf16[4,128,1024]{2,1,0:T(8,128)(2,1)}, bf16[4,128,1024]{2,1,0:T(8,128)(2,1)}) custom-call(s32[5]{0:T(128)} %stack.171.refs_0_, bf16[512,1024]{1,0:T(8,128)(2,1)} %get-tuple-element.248.refs_1_.refs_8_, ...), custom_call_target="tpu_custom_call" | custom-call | flops 70000000 | bytes 1024 | tf_op jit(solution)/shard_map/grads_mine/pallas_call | solution.py:80
  714.5 10.5 %collective-permute-done.67.refs_3_ = bf16[2,2,128,1024]{3,2,1,0:T(8,128)(2,1)S(1)} collective-permute-done((bf16[2,2,128,1024]{3,2,1,0:T(8,128)(2,1)}, bf16[2,2,128,1024]{3,2,1,0:T(8,128)(2,1)S(1)}, u32[]{:S(2)}, u32[]{:S(2)}) %collective-permute-start.67) | collective-permute-done | bytes 1048608 | tf_op jit(solution)/shard_map/ppermute | solution.py:884
  742.6 29.1 %attend_backward.6 = (bf16[4,512,384]{2,1,0:T(8,128)(2,1)}, bf16[4,128,1024]{2,1,0:T(8,128)(2,1)}, bf16[4,128,1024]{2,1,0:T(8,128)(2,1)}, bf16[2,2,128,1024]{3,2,1,0:T(8,128)(2,1)}, bf16[8,128,1024]{2,1,0:T(8,128)(2,1)}) custom-call(s32[5]{0:T(128)} %stack.171.refs_0_, ...), custom_call_target="tpu_custom_call", output_to_operand_aliasing={{1}: (2, {}), {2}: (3, {}), {3}: (4, {}), {4}: (5, {})} | custom-call | flops 10499999744 | bytes 1024 | tf_op jit(solution)/shard_map/attend_backward/pallas_call | solution.py:80
  783.1 28.7 %attend_backward.7 = (bf16[4,512,384]{2,1,0:T(8,128)(2,1)}, bf16[8,128,1024]{2,1,0:T(8,128)(2,1)}, bf16[2,2,128,1024]{3,2,1,0:T(8,128)(2,1)}) custom-call(s32[5]{0:T(128)} %stack.171.refs_0_, s32[4]{0:T(128)} %gate.18.refs_1_, bf16[4,512,384]{2,1,0:T(8,128)(2,1)} %get-tuple-element.258.refs_2_.refs_5_.refs_3_.refs_12_, ...), custom_call_target="tpu_custom_call", output_to_operand_aliasing={{1}: (6, {}), {2}: (7, {})} | custom-call | flops 10499999744 | bytes 1024 | tf_op jit(solution)/shard_map/attend_backward/pallas_call | solution.py:80
  845.5 12.7 %heads_grad.3 = (bf16[2,2,128,1024]{3,2,1,0:T(8,128)(2,1)}, bf16[2,2,128,1024]{3,2,1,0:T(8,128)(2,1)}, f32[1,768]{1,0:T(1,128)}) custom-call(s32[5]{0:T(128)} %stack.171.refs_0_, bf16[512,1024]{1,0:T(8,128)(2,1)} %fusion.refs_1_, bf16[128,1024]{1,0:T(8,128)(2,1)} %copy-done.63, bf16[128,1024]{1,0:T(8,128)(2,1)} %copy-done.64, ...), custom_call_target="tpu_custom_call" | custom-call | flops 70000000 | bytes 1024 | tf_op jit(solution)/shard_map/heads_grad/pallas_call | solution.py:80
  868.0 28.7 %collective-permute-done.78.refs_1_ = bf16[512,1024]{1,0:T(8,128)(2,1)S(1)} collective-permute-done((bf16[512,1024]{1,0:T(8,128)(2,1)}, bf16[512,1024]{1,0:T(8,128)(2,1)S(1)}, u32[]{:S(2)}, u32[]{:S(2)}) %collective-permute-start.78) | collective-permute-done | bytes 1048608 | tf_op jit(solution)/shard_map/ppermute | solution.py:884
  934.5 8.5 collective-permute-done.87.refs_8_
  (631 shorter events, 384.3 us)
Async XLA Ops:
  7.2 181.6 %all-gather.2.cloned.1.call-start = ((), (), s32[]{:S(2)}) async-start(), calls=%async_computation | async-start | bytes 2162688 | tf_op jit(solution)/shard_map/all_gather | solution.py:1173
  13.0 42.1 %collective-permute-start.1 = (bf16[800,1024]{1,0:T(8,128)(2,1)S(1)}, bf16[800,1024]{1,0:T(8,128)(2,1)S(1)}, u32[]{:S(2)}, u32[]{:S(2)}) collective-permute-start(bf16[800,1024]{1,0:T(8,128)(2,1)S(1)} %pad_maximum_fusion.1), channel_id=1, source_target_pairs={{0,0},{2,4},{4,2},{6,6},{1,1},{3,5},{5,3},{7,7},{8,8},{10,12},{12,... | collective-permute-start | bytes 4915208 | tf_op jit(solution)/shard_map/ppermute | solution.py:888
  131.7 35.7 %collective-permute-start.10 = (bf16[4,1,128,1024]{3,2,1,0:T(8,128)(2,1)S(1)}, bf16[4,1,128,1024]{3,2,1,0:T(8,128)(2,1)S(1)}, u32[]{:S(2)}, u32[]{:S(2)}) collective-permute-start(bf16[4,1,128,1024]{3,2,1,0:T(8,128)(2,1)S(1)} %pad_maximum_fusion.6.refs_11_.refs_7_), channel_id=1, source_target_pairs={{0,8},{8,0},{16,24},{24,16},{1,9},{9,1},{17,25},{25,17},{2,10},{10... | collective-permute-start | bytes 3145736 | tf_op jit(solution)/shard_map/ppermute | solution.py:884
  133.0 34.5 %collective-permute-start.11 = (bf16[4,1,128,1024]{3,2,1,0:T(8,128)(2,1)S(1)}, bf16[4,1,128,1024]{3,2,1,0:T(8,128)(2,1)S(1)}, u32[]{:S(2)}, u32[]{:S(2)}) collective-permute-start(bf16[4,1,128,1024]{3,2,1,0:T(8,128)(2,1)S(1)} %pad_maximum_fusion.6.refs_11_.refs_7_), channel_id=1, source_target_pairs={{0,16},{8,24},{16,0},{24,8},{1,17},{9,25},{17,1},{25,9},{2,18},{10... | collective-permute-start | bytes 3145736 | tf_op jit(solution)/shard_map/ppermute | solution.py:884
  134.3 32.1 %collective-permute-start.15 = (bf16[2,1,128,1024]{3,2,1,0:T(8,128)(2,1)S(1)}, bf16[2,1,128,1024]{3,2,1,0:T(8,128)(2,1)S(1)}, u32[]{:S(2)}, u32[]{:S(2)}) collective-permute-start(bf16[2,1,128,1024]{3,2,1,0:T(8,128)(2,1)S(1)} %pad_maximum_fusion.12), channel_id=1, source_target_pairs={{0,1},{1,0},{2,3},{3,2},{4,5},{5,4},{6,7},{7,6},{8,9},{9,8},{10,11... | collective-permute-start | bytes 1572872 | tf_op jit(solution)/shard_map/ppermute | solution.py:884
  191.0 37.3 %collective-permute-start.21 = (bf16[4,1,128,1024]{3,2,1,0:T(8,128)(2,1)}, bf16[4,1,128,1024]{3,2,1,0:T(8,128)(2,1)}, u32[]{:S(2)}, u32[]{:S(2)}) collective-permute-start(bf16[4,1,128,1024]{3,2,1,0:T(8,128)(2,1)} %get-tuple-element.187.refs_5_.refs_10_), channel_id=1, source_target_pairs={{0,8},{8,0},{16,24},{24,16},{1,9},{9,1},{17,25},{25,17},{2,10},{10... | collective-permute-start | bytes 3145736 | tf_op jit(solution)/shard_map/ppermute | solution.py:884
  191.0 37.7 %collective-permute-start.22 = (bf16[4,1,128,1024]{3,2,1,0:T(8,128)(2,1)}, bf16[4,1,128,1024]{3,2,1,0:T(8,128)(2,1)}, u32[]{:S(2)}, u32[]{:S(2)}) collective-permute-start(bf16[4,1,128,1024]{3,2,1,0:T(8,128)(2,1)} %get-tuple-element.187.refs_5_.refs_10_), channel_id=1, source_target_pairs={{0,16},{8,24},{16,0},{24,8},{1,17},{9,25},{17,1},{25,9},{2,18},{10... | collective-permute-start | bytes 3145736 | tf_op jit(solution)/shard_map/ppermute | solution.py:884
  191.5 37.3 %collective-permute-start.23 = (bf16[512,1024]{1,0:T(8,128)(2,1)S(1)}, bf16[512,1024]{1,0:T(8,128)(2,1)}, u32[]{:S(2)}, u32[]{:S(2)}) collective-permute-start(bf16[512,1024]{1,0:T(8,128)(2,1)S(1)} %copy-done.41), channel_id=1, source_target_pairs={{0,1},{1,0},{4,5},{5,4},{2,3},{3,2},{6,7},{7,6},{8,9},{9,8},{12,13... | collective-permute-start | bytes 3145736 | tf_op jit(solution)/shard_map/ppermute | solution.py:884
  194.3 32.6 %collective-permute-start.24 = (bf16[2,1,128,1024]{3,2,1,0:T(8,128)(2,1)S(1)}, bf16[2,1,128,1024]{3,2,1,0:T(8,128)(2,1)}, u32[]{:S(2)}, u32[]{:S(2)}) collective-permute-start(bf16[2,1,128,1024]{3,2,1,0:T(8,128)(2,1)S(1)} %slice.360), channel_id=1, source_target_pairs={{0,8},{8,0},{16,24},{24,16},{1,9},{9,1},{17,25},{25,17},{2,10},{10... | collective-permute-start | bytes 1572872 | tf_op jit(solution)/shard_map/ppermute | solution.py:884
  320.7 47.5 %collective-permute-start.41 = (bf16[4,2,128,1024]{3,2,1,0:T(8,128)(2,1)}, bf16[4,2,128,1024]{3,2,1,0:T(8,128)(2,1)}, u32[]{:S(2)}, u32[]{:S(2)}) collective-permute-start(bf16[4,2,128,1024]{3,2,1,0:T(8,128)(2,1)} %get-tuple-element.203.refs_7_.refs_4_.refs_6_), channel_id=1, source_target_pairs={{0,8},{8,0},{16,24},{24,16},{1,9},{9,1},{17,25},{25,17},{2,10},{10... | collective-permute-start | bytes 6291464 | tf_op jit(solution)/shard_map/ppermute | solution.py:884
  321.7 47.2 %collective-permute-start.42 = (bf16[4,2,128,1024]{3,2,1,0:T(8,128)(2,1)}, bf16[4,2,128,1024]{3,2,1,0:T(8,128)(2,1)}, u32[]{:S(2)}, u32[]{:S(2)}) collective-permute-start(bf16[4,2,128,1024]{3,2,1,0:T(8,128)(2,1)} %get-tuple-element.203.refs_7_.refs_4_.refs_6_), channel_id=1, source_target_pairs={{0,16},{8,24},{16,0},{24,8},{1,17},{9,25},{17,1},{25,9},{2,18},{10... | collective-permute-start | bytes 6291464 | tf_op jit(solution)/shard_map/ppermute | solution.py:884
  330.0 38.9 %collective-permute-start.44 = (bf16[512,1024]{1,0:T(8,128)(2,1)}, bf16[512,1024]{1,0:T(8,128)(2,1)S(1)}, u32[]{:S(2)}, u32[]{:S(2)}) collective-permute-start(bf16[512,1024]{1,0:T(8,128)(2,1)} %get-tuple-element.206), channel_id=1, source_target_pairs={{0,0},{2,4},{4,2},{6,6},{1,1},{3,5},{5,3},{7,7},{8,8},{10,12},{12,... | collective-permute-start | bytes 3145736 | tf_op jit(solution)/shard_map/ppermute | solution.py:888
  521.7 74.8 %collective-permute-start.59 = (bf16[4,8,128,1024]{3,2,1,0:T(8,128)(2,1)}, bf16[4,8,128,1024]{3,2,1,0:T(8,128)(2,1)}, u32[]{:S(2)}, u32[]{:S(2)}) collective-permute-start(bf16[4,8,128,1024]{3,2,1,0:T(8,128)(2,1)} %get-tuple-element.230), channel_id=1, source_target_pairs={{0,4},{4,0},{1,5},{5,1},{2,6},{6,2},{3,7},{7,3},{8,12},{12,8},{9,1... | collective-permute-start | bytes 25165832 | tf_op jit(solution)/shard_map/ppermute | solution.py:884
  595.6 32.2 %collective-permute-start.62 = (bf16[512,1024]{1,0:T(8,128)(2,1)S(1)}, bf16[512,1024]{1,0:T(8,128)(2,1)}, u32[]{:S(2)}, u32[]{:S(2)}) collective-permute-start(bf16[512,1024]{1,0:T(8,128)(2,1)S(1)} %fusion.3.refs_1_), channel_id=1, source_target_pairs={{0,1},{1,0},{4,5},{5,4},{2,3},{3,2},{6,7},{7,6},{8,9},{9,8},{12,13... | collective-permute-start | bytes 3145736 | tf_op jit(solution)/shard_map/ppermute | solution.py:884
  612.4 46.9 %collective-permute-start.61 = (bf16[8,128,1024]{2,1,0:T(8,128)(2,1)}, bf16[8,128,1024]{2,1,0:T(8,128)(2,1)S(1)}, u32[]{:S(2)}, u32[]{:S(2)}) collective-permute-start(bf16[8,128,1024]{2,1,0:T(8,128)(2,1)} %get-tuple-element.232.refs_3_), channel_id=1, source_target_pairs={{0,16},{8,24},{16,0},{24,8},{1,17},{9,25},{17,1},{25,9},{2,18},{10... | collective-permute-start | bytes 6291464 | tf_op jit(solution)/shard_map/ppermute | solution.py:884
  613.6 46.6 %collective-permute-start.60 = (bf16[8,128,1024]{2,1,0:T(8,128)(2,1)}, bf16[8,128,1024]{2,1,0:T(8,128)(2,1)S(1)}, u32[]{:S(2)}, u32[]{:S(2)}) collective-permute-start(bf16[8,128,1024]{2,1,0:T(8,128)(2,1)} %get-tuple-element.231.refs_2_), channel_id=1, source_target_pairs={{0,8},{8,0},{16,24},{24,16},{1,9},{9,1},{17,25},{25,17},{2,10},{10... | collective-permute-start | bytes 6291464 | tf_op jit(solution)/shard_map/ppermute | solution.py:884
  677.8 36.6 %collective-permute-start.65 = (bf16[4,128,1024]{2,1,0:T(8,128)(2,1)S(1)}, bf16[4,128,1024]{2,1,0:T(8,128)(2,1)S(1)}, u32[]{:S(2)}, u32[]{:S(2)}) collective-permute-start(bf16[4,128,1024]{2,1,0:T(8,128)(2,1)S(1)} %add_convert_fusion.5), channel_id=1, source_target_pairs={{0,8},{8,0},{16,24},{24,16},{1,9},{9,1},{17,25},{25,17},{2,10},{10... | collective-permute-start | bytes 3145736 | tf_op jit(solution)/shard_map/ppermute | solution.py:884
  680.4 34.0 %collective-permute-start.66 = (bf16[4,128,1024]{2,1,0:T(8,128)(2,1)}, bf16[4,128,1024]{2,1,0:T(8,128)(2,1)S(1)}, u32[]{:S(2)}, u32[]{:S(2)}) collective-permute-start(bf16[4,128,1024]{2,1,0:T(8,128)(2,1)} %add_convert_fusion.4), channel_id=1, source_target_pairs={{0,16},{8,24},{16,0},{24,8},{1,17},{9,25},{17,1},{25,9},{2,18},{10... | collective-permute-start | bytes 3145736 | tf_op jit(solution)/shard_map/ppermute | solution.py:884
  681.0 43.9 %collective-permute-start.67 = (bf16[2,2,128,1024]{3,2,1,0:T(8,128)(2,1)}, bf16[2,2,128,1024]{3,2,1,0:T(8,128)(2,1)S(1)}, u32[]{:S(2)}, u32[]{:S(2)}) collective-permute-start(bf16[2,2,128,1024]{3,2,1,0:T(8,128)(2,1)} %get-tuple-element.252), channel_id=1, source_target_pairs={{0,8},{8,0},{16,24},{24,16},{1,9},{9,1},{17,25},{25,17},{2,10},{10... | collective-permute-start | bytes 3145736 | tf_op jit(solution)/shard_map/ppermute | solution.py:884
  697.3 36.2 %collective-permute-start.64 = (bf16[512,1024]{1,0:T(8,128)(2,1)}, bf16[512,1024]{1,0:T(8,128)(2,1)}, u32[]{:S(2)}, u32[]{:S(2)}) collective-permute-start(bf16[512,1024]{1,0:T(8,128)(2,1)} %get-tuple-element.248.refs_1_.refs_8_), channel_id=1, source_target_pairs={{0,4},{1,5},{4,0},{5,1},{2,6},{3,7},{6,2},{7,3},{8,12},{9,13},{12,... | collective-permute-start | bytes 3145736 | tf_op jit(solution)/shard_map/ppermute | solution.py:884
  728.1 50.5 %collective-permute-start.71 = (bf16[8,128,1024]{2,1,0:T(8,128)(2,1)}, bf16[8,128,1024]{2,1,0:T(8,128)(2,1)}, u32[]{:S(2)}, u32[]{:S(2)}) collective-permute-start(bf16[8,128,1024]{2,1,0:T(8,128)(2,1)} %get-tuple-element.255.refs_6_), channel_id=1, source_target_pairs={{0,16},{8,24},{16,0},{24,8},{1,17},{9,25},{17,1},{25,9},{2,18},{10... | collective-permute-start | bytes 6291464 | tf_op jit(solution)/shard_map/ppermute | solution.py:884
  728.8 51.9 %collective-permute-start.70 = (bf16[8,128,1024]{2,1,0:T(8,128)(2,1)}, bf16[8,128,1024]{2,1,0:T(8,128)(2,1)}, u32[]{:S(2)}, u32[]{:S(2)}) collective-permute-start(bf16[8,128,1024]{2,1,0:T(8,128)(2,1)} %get-tuple-element.254.refs_5_), channel_id=1, source_target_pairs={{0,8},{8,0},{16,24},{24,16},{1,9},{9,1},{17,25},{25,17},{2,10},{10... | collective-permute-start | bytes 6291464 | tf_op jit(solution)/shard_map/ppermute | solution.py:884
  732.7 39.0 %collective-permute-start.72 = (bf16[4,128,1024]{2,1,0:T(8,128)(2,1)}, bf16[4,128,1024]{2,1,0:T(8,128)(2,1)S(1)}, u32[]{:S(2)}, u32[]{:S(2)}) collective-permute-start(bf16[4,128,1024]{2,1,0:T(8,128)(2,1)} %add_convert_fusion.3), channel_id=1, source_target_pairs={{0,1},{1,0},{2,3},{3,2},{4,5},{5,4},{6,7},{7,6},{8,9},{9,8},{10,11... | collective-permute-start | bytes 3145736 | tf_op jit(solution)/shard_map/ppermute | solution.py:884
  773.6 41.4 %collective-permute-start.75 = (bf16[2,128,1024]{2,1,0:T(8,128)(2,1)S(1)}, bf16[2,128,1024]{2,1,0:T(8,128)(2,1)S(1)}, u32[]{:S(2)}, u32[]{:S(2)}) collective-permute-start(bf16[2,128,1024]{2,1,0:T(8,128)(2,1)S(1)} %add_convert_fusion.9), channel_id=1, source_target_pairs={{0,2},{2,0},{1,3},{3,1},{4,6},{6,4},{5,7},{7,5},{8,10},{10,8},{9,1... | collective-permute-start | bytes 1572872 | tf_op jit(solution)/shard_map/ppermute | solution.py:884
  777.9 37.1 %collective-permute-start.76 = (bf16[2,128,1024]{2,1,0:T(8,128)(2,1)}, bf16[2,128,1024]{2,1,0:T(8,128)(2,1)S(1)}, u32[]{:S(2)}, u32[]{:S(2)}) collective-permute-start(bf16[2,128,1024]{2,1,0:T(8,128)(2,1)} %fusion.9), channel_id=1, source_target_pairs={{0,16},{8,24},{16,0},{24,8},{1,17},{9,25},{17,1},{25,9},{2,18},{10... | collective-permute-start | bytes 1572872 | tf_op jit(solution)/shard_map/ppermute | solution.py:884
  780.3 31.6 %collective-permute-start.73 = (bf16[4,128,1024]{2,1,0:T(8,128)(2,1)S(1)}, bf16[4,128,1024]{2,1,0:T(8,128)(2,1)S(1)}, u32[]{:S(2)}, u32[]{:S(2)}) collective-permute-start(bf16[4,128,1024]{2,1,0:T(8,128)(2,1)S(1)} %add_convert_fusion.2), channel_id=1, source_target_pairs={{0,8},{8,0},{16,24},{24,16},{1,9},{9,1},{17,25},{25,17},{2,10},{10... | collective-permute-start | bytes 3145736 | tf_op jit(solution)/shard_map/ppermute | solution.py:884
  782.3 32.7 %collective-permute-start.74 = (bf16[4,128,1024]{2,1,0:T(8,128)(2,1)S(1)}, bf16[4,128,1024]{2,1,0:T(8,128)(2,1)S(1)}, u32[]{:S(2)}, u32[]{:S(2)}) collective-permute-start(bf16[4,128,1024]{2,1,0:T(8,128)(2,1)S(1)} %add_convert_fusion), channel_id=1, source_target_pairs={{0,16},{8,24},{16,0},{24,8},{1,17},{9,25},{17,1},{25,9},{2,18},{10... | collective-permute-start | bytes 3145736 | tf_op jit(solution)/shard_map/ppermute | solution.py:884
  832.7 32.0 %collective-permute-start.80 = (bf16[4,128,1024]{2,1,0:T(8,128)(2,1)}, bf16[4,128,1024]{2,1,0:T(8,128)(2,1)}, u32[]{:S(2)}, u32[]{:S(2)}) collective-permute-start(bf16[4,128,1024]{2,1,0:T(8,128)(2,1)} %add_convert_fusion.1.refs_1_), channel_id=1, source_target_pairs={{0,1},{1,0},{2,3},{3,2},{4,5},{5,4},{6,7},{7,6},{8,9},{9,8},{10,11... | collective-permute-start | bytes 3145736 | tf_op jit(solution)/shard_map/ppermute | solution.py:884
  843.6 53.0 %collective-permute-start.78 = (bf16[512,1024]{1,0:T(8,128)(2,1)}, bf16[512,1024]{1,0:T(8,128)(2,1)S(1)}, u32[]{:S(2)}, u32[]{:S(2)}) collective-permute-start(bf16[512,1024]{1,0:T(8,128)(2,1)} %fusion.refs_1_), channel_id=1, source_target_pairs={{0,1},{1,0},{4,5},{5,4},{2,3},{3,2},{6,7},{7,6},{8,9},{9,8},{12,13... | collective-permute-start | bytes 3145736 | tf_op jit(solution)/shard_map/ppermute | solution.py:884
  859.9 36.7 %collective-permute-start.85 = (bf16[2,2,128,1024]{3,2,1,0:T(8,128)(2,1)}, bf16[2,2,128,1024]{3,2,1,0:T(8,128)(2,1)S(1)}, u32[]{:S(2)}, u32[]{:S(2)}) collective-permute-start(bf16[2,2,128,1024]{3,2,1,0:T(8,128)(2,1)} %get-tuple-element.279), channel_id=1, source_target_pairs={{0,8},{8,0},{16,24},{24,16},{1,9},{9,1},{17,25},{25,17},{2,10},{10... | collective-permute-start | bytes 3145736 | tf_op jit(solution)/shard_map/ppermute | solution.py:884
  867.3 44.2 %collective-permute-start.81 = (bf16[2,128,1024]{2,1,0:T(8,128)(2,1)}, bf16[2,128,1024]{2,1,0:T(8,128)(2,1)}, u32[]{:S(2)}, u32[]{:S(2)}) collective-permute-start(bf16[2,128,1024]{2,1,0:T(8,128)(2,1)} %add_convert_fusion.7), channel_id=1, source_target_pairs={{0,2},{2,0},{1,3},{3,1},{4,6},{6,4},{5,7},{7,5},{8,10},{10,8},{9,1... | collective-permute-start | bytes 1572872 | tf_op jit(solution)/shard_map/ppermute | solution.py:884
  906.0 37.0 %collective-permute-start.79 = (bf16[512,1024]{1,0:T(8,128)(2,1)S(1)}, bf16[512,1024]{1,0:T(8,128)(2,1)S(1)}, u32[]{:S(2)}, u32[]{:S(2)}) collective-permute-start(bf16[512,1024]{1,0:T(8,128)(2,1)S(1)} %fusion.2), channel_id=1, source_target_pairs={{0,0},{2,4},{4,2},{6,6},{1,1},{3,5},{5,3},{7,7},{8,8},{10,12},{12,... | collective-permute-start | bytes 3145736 | tf_op jit(solution)/shard_map/ppermute | solution.py:888
  (166 other events, 1737.1 us)
Sparse Core Ops, SparseCore 0:
  111.7 70.8 all-gather.1

commit v12 on v11

--- a/solution.py
+++ b/solution.py
@@ -1226,6 +1226,7 @@
             across = up0.other
             up0.start_z()
             down0.start_far_z()
+            flow.hold(pair=with_sibling(flow.free("heads1")))
         if last:
             both1.own = flow.free("own")
             both1.near()
@@ -1238,26 +1239,31 @@
             down0.near_z()
             both1.shard = flow.free("both1")
             both1.far_z()
+            pair = turn(flow.free("pair"))
         if last:
             top_grad = turn(flow.free("top"))
             both1.swap("own")
         ctx, wide, lse = attend_forward(flow, ends, qkv)
         if first:
             flow.wait(up0.near_x, up0.near_y)
-            flow.hold(both1=both1.two, down0=down0.own)
+            flow.hold(both1=both1.two, down0=down0.own, pair_twin=pair)
+            flow.wait(pair)
+            beside = flip(pair, "q", 1)
             up0.swap("own", "near_x", "near_y")
         if last:
             flow.wait(both1.near_x, both1.near_y, top_grad)
+        send = project_out(flow, [ctx], (2, 3), w_heads, out_cols, True, "project_attn")
+        flow.wait(send)
+        if last:
+            flow.hold(near_x=both1.near_x, near_y=both1.near_y)
+        keep = project_out(flow, [ctx], (0, 1), w_heads, out_cols, False, "project_attn")
+        if last:
+            both1.near_x, both1.near_y = flow.free("near_x"), flow.free("near_y")
             both1.corner()
             both1.swap("near_x", "near_y")
-        send = project_out(flow, [ctx], (2, 3), w_heads, out_cols, True, "project_attn")
-        flow.wait(send)
-        if first:
-            pair = with_sibling(flow.free("heads1"))
-        keep = project_out(flow, [ctx], (0, 1), w_heads, out_cols, False, "project_attn")
         attn, passed = sum_group(keep, send)
         if first:
-            flow.wait(passed, gathered, pair, *up0.theirs.values())
+            flow.wait(passed, gathered, *up0.theirs.values())
             flow.hold(near_x=up0.near_x, near_y=up0.near_y)
             gate(flow)
             down0.own, up0.near_x, up0.near_y = flow.free("down0"), flow.free("near_x"), flow.free("near_y")
@@ -1268,7 +1274,6 @@
             flow.wait(down0.near_x, down0.near_y)
             down0.corner()
             down0.swap("near_x", "near_y")
-            flow.hold(pair=pair)
             w_up = up0.pieces(), 0
         elif last:
             flow.wait(passed)
@@ -1286,23 +1291,18 @@
         used = (prev_gain, prev_shift, shift_row(l, 0), gain_row(l, 0), shift_row(l, 1))
         n1, hs, r1, act, slope = norm_up(flow, prev, attn, table, used, *w_up, up_bias_full[l], tz)
         if first:
-            pair = turn(flow.free("pair"))
-            flow.wait(n1, *down0.theirs.values())
+            flow.wait(n1, beside, *down0.theirs.values())
             flow.hold(far_a=down0.far_a, far_b=down0.far_b)
             gate(flow)
             down0.far_a, down0.far_b = flow.free("far_a"), flow.free("far_b")
             down0.swap("far_a", "far_b")
             both1.two = flow.free("both1")
             both1.near_z()
-            flow.hold(pair=pair, pair_twin=pair)
-            gate(flow)
-            across = flip(flow.free("pair"), "q", 1)
+            near = jnp.stack([flow.free("pair_twin"), beside])
+            weights_of.append(heads_along_y(near, bias_size, hz, where, zh))
             w_down = down0.pieces(), 0
         used = (gain_row(l, 0), shift_row(l, 1), shift_row(l, 2), gain_row(l, 1), shift_row(l, 3))
         n2, y_low, r2 = down_norm(flow, act, *w_down, n1, table, used, tz)
-        if first:
-            near = jnp.stack([flow.free("pair_twin"), across])
-            weights_of.append(heads_along_y(near, bias_size, hz, where, zh))
         kept.append((xs, qkv, ctx, wide, lse, n1, hs, r1, act, slope, n2, r2, w_heads, w_up, w_down))
         x_low, prev, prev_gain, prev_shift = y_low, n2, gain_row(l, 1), shift_row(l, 3)
     layer_output = turn(x_low)
@@ -1369,14 +1369,11 @@
         gqkv.append(attend_backward(flow, ends, 1, qkv, gcs, wide, lse))
         if beside:
             units.own, above_heads.keep = flow.free("own"), flow.free("keep")
-            units.near_z()
-            flow.wait(units.passing, units.late_y, above.last, above_heads.got)
+            flow.wait(units.late_x, units.late_y, above.last, above_heads.got)
             above_halves = above_heads.halves(zh)
             done = turn(above_halves[0]), uncross(above_halves[1])
         send = project_out(flow, gqkv, (2, 3), w_heads, in_cols, True, "project_gx")
         flow.wait(send)
-        if beside:
-            flow.hold(own=units.own)
         keep = project_out(flow, gqkv, (0, 1), w_heads, in_cols, False, "project_gx")
         back, passed = sum_group(keep, send)
         flow.wait(passed)
@@ -1384,8 +1381,6 @@
             units.mine()
             flow.wait(*units.made)
         elif small_slice:
-            units.own = flow.free("own")
-            units.far_z()
             flow.wait(*done)
         *buckets, qkv_sums = heads_grad(flow, xs, gqkv, gas, ctx)
         heads = HeadsGrad(*buckets)
@@ -1412,15 +1407,18 @@
         heads.along_x()
         small_sums = fold_small(spread_by_distance(small_sums, where), 0, 1)
         flow.wait(back[2])
-        flow.hold(small=small_sums, got=heads.got)
+        flow.hold(small=small_sums, got=heads.got, own=units.own)
         gate(flow)
-        small_sums, heads.got = flow.free("small"), flow.free("got")
+        small_sums, heads.got, units.own = flow.free("small"), flow.free("got"), flow.free("own")
         input_grad = turn(add(g1, back[0], back[1][0], back[2]).astype(BF16))
         heads.along_y()
+        units.near_z()
         small_sums = fold_small(small_sums, 1, 2)
-        flow.wait(heads.got, units.last)
-        flow.hold(small=small_sums)
+        flow.wait(heads.got)
+        flow.hold(small=small_sums, there=units.there)
         gate(flow)
+        units.there = flow.free("there")
+        units.far_z()
         small_sums = fold_small(flow.free("small"), 2, 3)
         halves = heads.halves(zh)
         small_out = fold_small(small_sums, 3, 5).reshape(layers, -1)

time: 991 us -> 1010 us (1.019)
  waiting for transfers between devices: 248 us -> 268 us
    ppermute x90, waiting for transfers between devices: 168 us -> 188 us  [flip(): lax.ppermute(values_in, axes, [(a, a ^ mask) for a in range(lax.axis_size...]
    unnamed x210 -> x232, local copies, waits for them, and re-layouts: 40.2 us -> 43 us
    pallas_call x49 -> x48, Pallas kernels: 475 us -> 475 us  [call(): pl.pallas_call(wrapped, grid_spec=pltpu.PrefetchScalarGridSpec(num_scalar...]
  transfers between devices with their start and end apart: 101 -> 101, of which waited for: 34 -> 38; matrix products, arithmetic and copies ran while one was open for 9% -> 9% of each run, Pallas kernels for 40% -> 39%
where the time goes in v12:
time: 1010 us
  Pallas kernels  475 us (47%)
  waiting for transfers between devices  268 us (27%)
  starting transfers between devices  116 us (11%)
  local copies, waits for them, and re-layouts  75.1 us (7%)
  other arithmetic  52.9 us (5%)
  between operations  18.2 us (2%)
    pallas_call x48, Pallas kernels, call(): pl.pallas_call(wrapped, grid_spec=pltpu.PrefetchScalarGridSpec(num_scalar...  475 us
    ppermute x90, waiting for transfers between devices, flip(): lax.ppermute(values_in, axes, [(a, a ^ mask) for a in range(lax.axis_size...  188 us
    ppermute x90, starting transfers between devices, flip(): lax.ppermute(values_in, axes, [(a, a ^ mask) for a in range(lax.axis_size...  86.5 us
    ppermute x8, waiting for transfers between devices, turn(): lax.ppermute(values_in, ('c', 'zh'), [(2 * a + b, 2 * b + a) for a in ran...  80 us
    unnamed x232, local copies, waits for them, and re-layouts  43 us
    ppermute x8, starting transfers between devices, turn(): lax.ppermute(values_in, ('c', 'zh'), [(2 * a + b, 2 * b + a) for a in ran...  29.4 us
  transfers between devices with their start and end apart: 101, of which 38 were waited for; matrix products, arithmetic and copies ran while one was open for 9% of the time, Pallas kernels for 39%

profile of v12, /device:TPU:1, one launch (start us, length us, event | category | flops | bytes accessed | tf_op | source)
XLA Modules:
  0.0 1005.5 jit_solution(7926854752401457026)
XLA Ops:
  18.8 36.3 %collective-permute-done.1 = bf16[800,1024]{1,0:T(8,128)(2,1)S(1)} collective-permute-done((bf16[800,1024]{1,0:T(8,128)(2,1)S(1)}, bf16[800,1024]{1,0:T(8,128)(2,1)S(1)}, u32[]{:S(2)}, u32[]{:S(2)}) %collective-permute-start.1) | collective-permute-done | bytes 1638432 | tf_op jit(solution)/shard_map/ppermute | solution.py:888
  86.6 11.6 %collective-permute-done.7.refs_9_ = bf16[512,1024]{1,0:T(8,128)(2,1)S(1)} collective-permute-done((bf16[512,1024]{1,0:T(8,128)(2,1)}, bf16[512,1024]{1,0:T(8,128)(2,1)S(1)}, u32[]{:S(2)}, u32[]{:S(2)}) %collective-permute-start.7) | collective-permute-done | bytes 1048608 | tf_op jit(solution)/shard_map/ppermute | solution.py:884
  137.0 28.4 %attend_forward.2 = (bf16[4,512,256]{2,1,0:T(8,128)(2,1)}, f32[4,512,256]{2,1,0:T(8,128)}, f32[4,8,512]{2,1,0:T(8,128)}) custom-call(s32[5]{0:T(128)} %stack.171.refs_0_, s32[4]{0:T(128)} %bitcast.283, bf16[2,512,768]{2,1,0:T(8,128)(2,1)} %get-tuple-element.162.refs_2_.refs_6_.refs_8_, bf16[2,512,768]{2,1,0:T(8,128)(2,1)} %get-tuple-element.180.refs_3_.refs_7_.refs_9_), custom_call_target="tpu_custom_call" | custom-call | flops 14000000000 | bytes 1024 | tf_op jit(solution)/shard_map/attend_forward/pallas_call | solution.py:80
  209.9 29.3 %collective-permute-done.25.refs_14_.refs_10_ = bf16[2,1,128,1024]{3,2,1,0:T(8,128)(2,1)} collective-permute-done((bf16[2,1,128,1024]{3,2,1,0:T(8,128)(2,1)}, bf16[2,1,128,1024]{3,2,1,0:T(8,128)(2,1)}, u32[]{:S(2)}, u32[]{:S(2)}) %collective-permute-start.25) | collective-permute-done | bytes 524320 | tf_op jit(solution)/shard_map/ppermute | solution.py:884
  247.7 19.0 %norm_up.2 = (f32[512,1024]{1,0:T(8,128)}, bf16[512,1024]{1,0:T(8,128)(2,1)}, f32[512,128]{1,0:T(8,128)}, bf16[512,4096]{1,0:T(8,128)(2,1)}, bf16[512,4096]{1,0:...) custom-call(s32[5]{0:T(128)} %stack.171.refs_0_, ...), custom_call_target="tpu_custom_call", output_to_operand_aliasing={{5}: (3, {}), {6}: (4, {})} | custom-call | flops 7000000000 | bytes 1024 | tf_op jit(solution)/shard_map/norm_up/pallas_call | solution.py:80
  272.7 14.5 %down_norm.2 = (f32[512,1024]{1,0:T(8,128)}, bf16[512,1024]{1,0:T(8,128)(2,1)}, f32[512,128]{1,0:T(8,128)}) custom-call(s32[5]{0:T(128)} %stack.171.refs_0_, bf16[512,4096]{1,0:T(8,128)(2,1)} %get-tuple-element.196.refs_1_.refs_5_.refs_3_, f32[512,1024]{1,0:T(8,128)} %get-tuple-element.197.refs_1_.refs_2_.refs_4_, ...), custom_call_target="tpu_custom_call" | custom-call | flops 7000000000 | bytes 1024 | tf_op jit(solution)/shard_map/down_norm/pallas_call | solution.py:80
  305.8 10.7 %collective-permute-done.40.refs_4_ = bf16[512,1024]{1,0:T(8,128)(2,1)S(1)} collective-permute-done((bf16[512,1024]{1,0:T(8,128)(2,1)}, bf16[512,1024]{1,0:T(8,128)(2,1)S(1)}, u32[]{:S(2)}, u32[]{:S(2)}) %collective-permute-start.40) | collective-permute-done | bytes 1048608 | tf_op jit(solution)/shard_map/ppermute | solution.py:884
  330.7 28.8 %attend_forward.3 = (bf16[4,512,256]{2,1,0:T(8,128)(2,1)}, f32[4,512,256]{2,1,0:T(8,128)}, f32[4,8,512]{2,1,0:T(8,128)}) custom-call(s32[5]{0:T(128)} %stack.171.refs_0_, s32[4]{0:T(128)} %bitcast.284, bf16[2,512,768]{2,1,0:T(8,128)(2,1)} %project_qkv.6.refs_1_.refs_2_.refs_3_, bf16[2,512,768]{2,1,0:T(8,128)(2,1)} %get-tuple-element.209.refs_3_.refs_4_), custom_call_target="tpu_custom_call" | custom-call | flops 14000000000 | bytes 1024 | tf_op jit(solution)/shard_map/attend_forward/pallas_call | solution.py:80
  383.9 20.7 %collective-permute-done.47.refs_2_ = bf16[2,2,128,1024]{3,2,1,0:T(8,128)(2,1)S(1)} collective-permute-done((bf16[2,2,128,1024]{3,2,1,0:T(8,128)(2,1)S(1)}, bf16[2,2,128,1024]{3,2,1,0:T(8,128)(2,1)S(1)}, u32[]{:S(2)}, u32[]{:S(2)}) %collective-permute-start.47) | collective-permute-done | bytes 1048608 | tf_op jit(solution)/shard_map/ppermute | solution.py:884
  414.4 19.0 %norm_up.3 = (f32[512,1024]{1,0:T(8,128)}, bf16[512,1024]{1,0:T(8,128)(2,1)}, f32[512,128]{1,0:T(8,128)}, bf16[512,4096]{1,0:T(8,128)(2,1)}, bf16[512,4096]{1,0:T(8,128)(2,1)}) custom-call(s32[5]{0:T(128)} %stack.171.refs_0_, f32[512,1024]{1,0:T(8,128)} %get-tuple-element.212.refs_1_.refs_6_, bf16[512,1024]{1,0:T(8,128)(2,1)} %get-tuple-element.213.refs_2_, ...), custom_call_target="tpu_custom_call" | custom-call | flops 7000000000 | bytes 1024 | tf_op jit(solution)/shard_map/norm_up/pallas_call | solution.py:80
  433.5 14.3 %down_norm.3 = (f32[512,1024]{1,0:T(8,128)}, bf16[512,1024]{1,0:T(8,128)(2,1)}, f32[512,128]{1,0:T(8,128)}) custom-call(s32[5]{0:T(128)} %stack.171.refs_0_, bf16[512,4096]{1,0:T(8,128)(2,1)} %get-tuple-element.218.refs_1_.refs_3_, f32[512,1024]{1,0:T(8,128)} %get-tuple-element.219.refs_2_.refs_4_, ...), custom_call_target="tpu_custom_call" | custom-call | flops 7000000000 | bytes 1024 | tf_op jit(solution)/shard_map/down_norm/pallas_call | solution.py:80
  449.7 12.7 %units_back.2 = (f32[512,1024]{1,0:T(8,128)}, bf16[512,1024]{1,0:T(8,128)(2,1)}, f32[8,1024]{1,0:T(8,128)}, bf16[512,4096]{1,0:T(8,128)(2,1)}, f32[4,1,1024]{2,1,0:T(1,128)}) custom-call(s32[5]{0:T(128)} %stack.171.refs_0_, bf16[512,1024]{1,0:T(8,128)(2,1)} %copy-done.83, f32[512,1024]{1,0:T(8,128)} %get-tuple-element.221.refs_2_, ...), custom_call_target="tpu_custom_call" | custom-call | flops 15749999616 | bytes 1024 | tf_op jit(solution)/shard_map/units_back/pallas_call | solution.py:80
  462.4 13.5 %collective-permute-done.54.refs_1_ = bf16[512,1024]{1,0:T(8,128)(2,1)S(1)} collective-permute-done((bf16[512,1024]{1,0:T(8,128)(2,1)}, bf16[512,1024]{1,0:T(8,128)(2,1)S(1)}, u32[]{:S(2)}, u32[]{:S(2)}) %collective-permute-start.54) | collective-permute-done | bytes 1048608 | tf_op jit(solution)/shard_map/ppermute | solution.py:888
  476.9 14.9 %up_back.2 = (f32[512,1024]{1,0:T(8,128)}, bf16[512,1024]{1,0:T(8,128)(2,1)}, f32[8,1024]{1,0:T(8,128)}, bf16[512,1024]{1,0:T(8,128)(2,1)}) custom-call(s32[5]{0:T(128)} %stack.171.refs_0_, bf16[512,1024]{1,0:T(8,128)(2,1)} %copy-done.15, bf16[512,4096]{1,0:T(8,128)(2,1)} %get-tuple-element.224.refs_2_.refs_5_, ...), custom_call_target="tpu_custom_call", output_to_operand_aliasing={{3}: (1, {})} | custom-call | flops 7000000000 | bytes 1024 | tf_op jit(solution)/shard_map/up_back/pallas_call | solution.py:80
  492.0 12.7 %grads_theirs.2.refs_1_.refs_2_ = bf16[4,8,128,1024]{3,2,1,0:T(8,128)(2,1)} custom-call(s32[5]{0:T(128)} %stack.171.refs_0_, bf16[512,1024]{1,0:T(8,128)(2,1)} %get-tuple-element.227.refs_1_.refs_10_, bf16[512,1024]{1,0:T(8,128)(2,1)} %get-tuple-element.228.refs_2_, bf16[512,4096]{1,0:T(8,128)(2,1)} %get-tuple-element.218.refs_1_.refs_3_, ...), custom_call_target="tpu_custom_call" | custom-call | flops 70000000 | bytes 1024 | tf_op jit(solution)/shard_map/grads_theirs/pallas_call | solution.py:80
  518.9 28.8 %attend_backward.4.refs_2_.refs_1_.refs_14_ = bf16[4,512,384]{2,1,0:T(8,128)(2,1)} custom-call(s32[5]{0:T(128)} %stack.171.refs_0_, s32[4]{0:T(128)} %gate.16.refs_1_, bf16[2,512,768]{2,1,0:T(8,128)(2,1)} %project_qkv.6.refs_1_.refs_2_.refs_3_, bf16[2,512,768]{2,1,0:T(8,128)(2,1)} %get-tuple-element.209.refs_3_.refs_4_, ...), custom_call_target="tpu_custom_call" | custom-call | flops 10499999744 | bytes 1024 | tf_op jit(solution)/shard_map/attend_backward/pallas_call | solution.py:80
  547.6 29.0 %attend_backward.5.refs_2_.refs_3_.refs_15_ = bf16[4,512,384]{2,1,0:T(8,128)(2,1)} custom-call(s32[5]{0:T(128)} %stack.171.refs_0_, s32[4]{0:T(128)} %gate.16.refs_1_, bf16[4,512,384]{2,1,0:T(8,128)(2,1)} %attend_backward.4.refs_2_.refs_1_.refs_14_, bf16[2,512,768]{2,1,0:T(8,128)(2,1)} %project_qkv.6.refs_1_.refs_2_.refs_3_, ...), custom_call_target="tpu_custom_call" | custom-call | flops 10499999744 | bytes 1024 | tf_op jit(solution)/shard_map/attend_backward/pallas_call | solution.py:80
  592.6 15.8 %grads_mine.2 = (bf16[8,128,1024]{2,1,0:T(8,128)(2,1)}, bf16[8,128,1024]{2,1,0:T(8,128)(2,1)}, bf16[8,128,1024]{2,1,0:T(8,128)(2,1)}, bf16[4,128,1024]{2,1,0:T(8,128)(2,1)}, bf16[4,128,1024]{2,1,0:T(8,128)(2,1)}) custom-call(s32[5]{0:T(128)} %stack.171.refs_0_, bf16[512,1024]{1,0:T(8,128)(2,1)} %copy-done.35, bf16[512,1024]{1,0:T(8,128)(2,1)} %get-tuple-element.228.refs_2_, ...), custom_call_target="tpu_custom_call" | custom-call | flops 70000000 | bytes 1024 | tf_op jit(solution)/shard_map/grads_mine/pallas_call | solution.py:80
  609.0 13.1 %heads_grad.2 = (bf16[2,2,128,1024]{3,2,1,0:T(8,128)(2,1)}, bf16[2,2,128,1024]{3,2,1,0:T(8,128)(2,1)}, f32[1,768]{1,0:T(1,128)}) custom-call(s32[5]{0:T(128)} %stack.171.refs_0_, bf16[8,128,1024]{2,1,0:T(8,128)(2,1)} %get-tuple-element.237.refs_1_.refs_5_, bf16[8,128,1024]{2,1,0:T(8,128)(2,1)} %get-tuple-element.235.refs_2_, ...), custom_call_target="tpu_custom_call" | custom-call | flops 70000000 | bytes 1024 | tf_op jit(solution)/shard_map/heads_grad/pallas_call | solution.py:80
  622.0 14.2 %units_back.3 = (f32[512,1024]{1,0:T(8,128)}, bf16[512,1024]{1,0:T(8,128)(2,1)}, f32[8,1024]{1,0:T(8,128)}, bf16[512,4096]{1,0:T(8,128)(2,1)}, f32[4,1,1024]{2,1,0:T(1,128)}) custom-call(s32[5]{0:T(128)} %stack.171.refs_0_, bf16[2,2,128,1024]{3,2,1,0:T(8,128)(2,1)} %get-tuple-element.240.refs_1_.refs_3_, f32[512,1024]{1,0:T(8,128)} %get-tuple-element.241.refs_2_, ...), custom_call_target="tpu_custom_call" | custom-call | flops 15749999616 | bytes 1024 | tf_op jit(solution)/shard_map/units_back/pallas_call | solution.py:80
  636.3 19.0 %collective-permute-done.61.refs_2_ = bf16[8,128,1024]{2,1,0:T(8,128)(2,1)S(1)} collective-permute-done((bf16[8,128,1024]{2,1,0:T(8,128)(2,1)}, bf16[8,128,1024]{2,1,0:T(8,128)(2,1)S(1)}, u32[]{:S(2)}, u32[]{:S(2)}) %collective-permute-start.61) | collective-permute-done | bytes 2097184 | tf_op jit(solution)/shard_map/ppermute | solution.py:884
  657.3 12.8 %grads_theirs.3 = (bf16[4,8,128,1024]{3,2,1,0:T(8,128)(2,1)}, bf16[2,2,128,1024]{3,2,1,0:T(8,128)(2,1)}) custom-call(s32[5]{0:T(128)} %stack.171.refs_0_, bf16[8,128,1024]{2,1,0:T(8,128)(2,1)} %copy-done.8, bf16[8,128,1024]{2,1,0:T(8,128)(2,1)} %copy-done.17, ...), custom_call_target="tpu_custom_call", output_to_operand_aliasing={{1}: (3, {})} | custom-call | flops 70000000 | bytes 1024 | tf_op jit(solution)/shard_map/grads_theirs/pallas_call | solution.py:80
  677.0 15.1 %up_back.3 = (f32[512,1024]{1,0:T(8,128)}, bf16[512,1024]{1,0:T(8,128)(2,1)}, f32[8,1024]{1,0:T(8,128)}) custom-call(s32[5]{0:T(128)} %stack.171.refs_0_, bf16[4,8,128,1024]{3,2,1,0:T(8,128)(2,1)} %get-tuple-element.248.refs_1_, bf16[512,4096]{1,0:T(8,128)(2,1)} %get-tuple-element.247.refs_7_.refs_2_.refs_5_, f32[512,1024]{1,0:T(8,128)} %get-tuple-element.249.refs_3_, ...), custom_call_target="tpu_custom_call" | custom-call | flops 7000000000 | bytes 1024 | tf_op jit(solution)/shard_map/up_back/pallas_call | solution.py:80
  694.2 15.8 %grads_mine.3 = (bf16[8,128,1024]{2,1,0:T(8,128)(2,1)}, bf16[8,128,1024]{2,1,0:T(8,128)(2,1)}, bf16[8,128,1024]{2,1,0:T(8,128)(2,1)}, bf16[4,128,1024]{2,1,0:T(8,128)(2,1)}, bf16[4,128,1024]{2,1,0:T(8,128)(2,1)}) custom-call(s32[5]{0:T(128)} %stack.171.refs_0_, bf16[512,1024]{1,0:T(8,128)(2,1)} %get-tuple-element.252.refs_1_.refs_8_, ...), custom_call_target="tpu_custom_call" | custom-call | flops 70000000 | bytes 1024 | tf_op jit(solution)/shard_map/grads_mine/pallas_call | solution.py:80
  710.0 10.3 %collective-permute-done.67.refs_3_ = bf16[2,2,128,1024]{3,2,1,0:T(8,128)(2,1)S(1)} collective-permute-done((bf16[2,2,128,1024]{3,2,1,0:T(8,128)(2,1)}, bf16[2,2,128,1024]{3,2,1,0:T(8,128)(2,1)S(1)}, u32[]{:S(2)}, u32[]{:S(2)}) %collective-permute-start.67) | collective-permute-done | bytes 1048608 | tf_op jit(solution)/shard_map/ppermute | solution.py:884
  737.0 29.2 %attend_backward.6 = (bf16[4,512,384]{2,1,0:T(8,128)(2,1)}, bf16[4,128,1024]{2,1,0:T(8,128)(2,1)}, bf16[4,128,1024]{2,1,0:T(8,128)(2,1)}, bf16[2,2,128,1024]{3,2,1,0:T(8,128)(2,1)}, bf16[8,128,1024]{2,1,0:T(8,128)(2,1)}) custom-call(s32[5]{0:T(128)} %stack.171.refs_0_, ...), custom_call_target="tpu_custom_call", output_to_operand_aliasing={{1}: (2, {}), {2}: (3, {}), {3}: (4, {}), {4}: (5, {})} | custom-call | flops 10499999744 | bytes 1024 | tf_op jit(solution)/shard_map/attend_backward/pallas_call | solution.py:80
  777.1 28.8 %attend_backward.7 = (bf16[4,512,384]{2,1,0:T(8,128)(2,1)}, bf16[8,128,1024]{2,1,0:T(8,128)(2,1)}, bf16[2,2,128,1024]{3,2,1,0:T(8,128)(2,1)}) custom-call(s32[5]{0:T(128)} %stack.171.refs_0_, s32[4]{0:T(128)} %gate.16.refs_1_, bf16[4,512,384]{2,1,0:T(8,128)(2,1)} %get-tuple-element.266.refs_2_.refs_5_.refs_12_, ...), custom_call_target="tpu_custom_call", output_to_operand_aliasing={{1}: (6, {}), {2}: (7, {})} | custom-call | flops 10499999744 | bytes 1024 | tf_op jit(solution)/shard_map/attend_backward/pallas_call | solution.py:80
  846.4 12.8 %heads_grad.3 = (bf16[2,2,128,1024]{3,2,1,0:T(8,128)(2,1)}, bf16[2,2,128,1024]{3,2,1,0:T(8,128)(2,1)}, f32[1,768]{1,0:T(1,128)}) custom-call(s32[5]{0:T(128)} %stack.171.refs_0_, bf16[512,1024]{1,0:T(8,128)(2,1)} %copy-done.46, bf16[128,1024]{1,0:T(8,128)(2,1)} %copy-done.71, bf16[128,1024]{1,0:T(8,128)(2,1)} %copy-done.72, ...), custom_call_target="tpu_custom_call" | custom-call | flops 70000000 | bytes 1024 | tf_op jit(solution)/shard_map/heads_grad/pallas_call | solution.py:80
  870.0 13.4 %collective-permute-done.83.refs_3_ = bf16[2,2,128,1024]{3,2,1,0:T(8,128)(2,1)S(1)} collective-permute-done((bf16[2,2,128,1024]{3,2,1,0:T(8,128)(2,1)}, bf16[2,2,128,1024]{3,2,1,0:T(8,128)(2,1)S(1)}, u32[]{:S(2)}, u32[]{:S(2)}) %collective-permute-start.83) | collective-permute-done | bytes 1048608 | tf_op jit(solution)/shard_map/ppermute | solution.py:884
  902.0 10.0 collective-permute-done.85
  912.6 10.5 %collective-permute-done.86.refs_3_ = bf16[4,128,1024]{2,1,0:T(8,128)(2,1)S(1)} collective-permute-done((bf16[4,128,1024]{2,1,0:T(8,128)(2,1)S(1)}, bf16[4,128,1024]{2,1,0:T(8,128)(2,1)S(1)}, u32[]{:S(2)}, u32[]{:S(2)}) %collective-permute-start.86) | collective-permute-done | bytes 1048608 | tf_op jit(solution)/shard_map/ppermute | solution.py:884
  942.0 23.7 %collective-permute-done.88.refs_8_ = bf16[128,1024]{1,0:T(8,128)(2,1)S(1)} collective-permute-done((bf16[128,1024]{1,0:T(8,128)(2,1)S(1)}, bf16[128,1024]{1,0:T(8,128)(2,1)S(1)}, u32[]{:S(2)}, u32[]{:S(2)}) %collective-permute-start.88) | collective-permute-done | bytes 262176 | tf_op jit(solution)/shard_map/ppermute | solution.py:888
  (652 shorter events, 398.6 us)
Async XLA Ops:
  7.2 192.3 %all-gather.2.cloned.1.call-start = ((), (), s32[]{:S(2)}) async-start(), calls=%async_computation | async-start | bytes 2162688 | tf_op jit(solution)/shard_map/all_gather | solution.py:1173
  13.0 42.1 %collective-permute-start.1 = (bf16[800,1024]{1,0:T(8,128)(2,1)S(1)}, bf16[800,1024]{1,0:T(8,128)(2,1)S(1)}, u32[]{:S(2)}, u32[]{:S(2)}) collective-permute-start(bf16[800,1024]{1,0:T(8,128)(2,1)S(1)} %pad_maximum_fusion.1), channel_id=1, source_target_pairs={{0,0},{2,4},{4,2},{6,6},{1,1},{3,5},{5,3},{7,7},{8,8},{10,12},{12,... | collective-permute-start | bytes 4915208 | tf_op jit(solution)/shard_map/ppermute | solution.py:888
  128.4 49.0 %collective-permute-start.11 = (bf16[4,1,128,1024]{3,2,1,0:T(8,128)(2,1)}, bf16[4,1,128,1024]{3,2,1,0:T(8,128)(2,1)S(1)}, u32[]{:S(2)}, u32[]{:S(2)}) collective-permute-start(bf16[4,1,128,1024]{3,2,1,0:T(8,128)(2,1)} %pad_maximum_fusion.6.refs_11_.refs_7_), channel_id=1, source_target_pairs={{0,8},{8,0},{16,24},{24,16},{1,9},{9,1},{17,25},{25,17},{2,10},{10... | collective-permute-start | bytes 3145736 | tf_op jit(solution)/shard_map/ppermute | solution.py:884
  129.6 47.7 %collective-permute-start.12 = (bf16[4,1,128,1024]{3,2,1,0:T(8,128)(2,1)}, bf16[4,1,128,1024]{3,2,1,0:T(8,128)(2,1)S(1)}, u32[]{:S(2)}, u32[]{:S(2)}) collective-permute-start(bf16[4,1,128,1024]{3,2,1,0:T(8,128)(2,1)} %pad_maximum_fusion.6.refs_11_.refs_7_), channel_id=1, source_target_pairs={{0,16},{8,24},{16,0},{24,8},{1,17},{9,25},{17,1},{25,9},{2,18},{10... | collective-permute-start | bytes 3145736 | tf_op jit(solution)/shard_map/ppermute | solution.py:884
  130.8 45.7 %collective-permute-start.13 = (bf16[2,144,1024]{2,1,0:T(8,128)(2,1)S(1)}, bf16[2,144,1024]{2,1,0:T(8,128)(2,1)S(1)}, u32[]{:S(2)}, u32[]{:S(2)}) collective-permute-start(bf16[2,144,1024]{2,1,0:T(8,128)(2,1)S(1)} %copy-done.60), channel_id=1, source_target_pairs={{0,0},{2,4},{4,2},{6,6},{1,1},{3,5},{5,3},{7,7},{8,8},{10,12},{12,... | collective-permute-start | bytes 1769480 | tf_op jit(solution)/shard_map/ppermute | solution.py:888
  136.8 37.6 %collective-permute-start.14 = (bf16[2,128,1024]{2,1,0:T(8,128)(2,1)S(1)}, bf16[2,128,1024]{2,1,0:T(8,128)(2,1)S(1)}, u32[]{:S(2)}, u32[]{:S(2)}) collective-permute-start(bf16[2,128,1024]{2,1,0:T(8,128)(2,1)S(1)} %copy-done.6), channel_id=1, source_target_pairs={{0,2},{2,0},{1,3},{3,1},{4,6},{6,4},{5,7},{7,5},{8,10},{10,8},{9,1... | collective-permute-start | bytes 1572872 | tf_op jit(solution)/shard_map/ppermute | solution.py:884
  136.9 38.5 %collective-permute-start.16 = (bf16[2,1,128,1024]{3,2,1,0:T(8,128)(2,1)S(1)}, bf16[2,1,128,1024]{3,2,1,0:T(8,128)(2,1)S(1)}, u32[]{:S(2)}, u32[]{:S(2)}) collective-permute-start(bf16[2,1,128,1024]{3,2,1,0:T(8,128)(2,1)S(1)} %pad_maximum_fusion.12), channel_id=1, source_target_pairs={{0,1},{1,0},{2,3},{3,2},{4,5},{5,4},{6,7},{7,6},{8,9},{9,8},{10,11... | collective-permute-start | bytes 1572872 | tf_op jit(solution)/shard_map/ppermute | solution.py:884
  201.6 39.0 %collective-permute-start.22 = (bf16[4,1,128,1024]{3,2,1,0:T(8,128)(2,1)}, bf16[4,1,128,1024]{3,2,1,0:T(8,128)(2,1)}, u32[]{:S(2)}, u32[]{:S(2)}) collective-permute-start(bf16[4,1,128,1024]{3,2,1,0:T(8,128)(2,1)} %get-tuple-element.190.refs_4_.refs_10_), channel_id=1, source_target_pairs={{0,8},{8,0},{16,24},{24,16},{1,9},{9,1},{17,25},{25,17},{2,10},{10... | collective-permute-start | bytes 3145736 | tf_op jit(solution)/shard_map/ppermute | solution.py:884
  202.9 38.3 %collective-permute-start.23 = (bf16[4,1,128,1024]{3,2,1,0:T(8,128)(2,1)}, bf16[4,1,128,1024]{3,2,1,0:T(8,128)(2,1)}, u32[]{:S(2)}, u32[]{:S(2)}) collective-permute-start(bf16[4,1,128,1024]{3,2,1,0:T(8,128)(2,1)} %get-tuple-element.190.refs_4_.refs_10_), channel_id=1, source_target_pairs={{0,16},{8,24},{16,0},{24,8},{1,17},{9,25},{17,1},{25,9},{2,18},{10... | collective-permute-start | bytes 3145736 | tf_op jit(solution)/shard_map/ppermute | solution.py:884
  203.2 38.2 %collective-permute-start.24 = (bf16[512,1024]{1,0:T(8,128)(2,1)S(1)}, bf16[512,1024]{1,0:T(8,128)(2,1)}, u32[]{:S(2)}, u32[]{:S(2)}) collective-permute-start(bf16[512,1024]{1,0:T(8,128)(2,1)S(1)} %copy-done.45), channel_id=1, source_target_pairs={{0,1},{1,0},{4,5},{5,4},{2,3},{3,2},{6,7},{7,6},{8,9},{9,8},{12,13... | collective-permute-start | bytes 3145736 | tf_op jit(solution)/shard_map/ppermute | solution.py:884
  205.0 34.2 %collective-permute-start.25 = (bf16[2,1,128,1024]{3,2,1,0:T(8,128)(2,1)}, bf16[2,1,128,1024]{3,2,1,0:T(8,128)(2,1)}, u32[]{:S(2)}, u32[]{:S(2)}) collective-permute-start(bf16[2,1,128,1024]{3,2,1,0:T(8,128)(2,1)} %slice.360), channel_id=1, source_target_pairs={{0,8},{8,0},{16,24},{24,16},{1,9},{9,1},{17,25},{25,17},{2,10},{10... | collective-permute-start | bytes 1572872 | tf_op jit(solution)/shard_map/ppermute | solution.py:884
  206.4 34.2 %collective-permute-start.26 = (bf16[2,1,128,1024]{3,2,1,0:T(8,128)(2,1)S(1)}, bf16[2,1,128,1024]{3,2,1,0:T(8,128)(2,1)}, u32[]{:S(2)}, u32[]{:S(2)}) collective-permute-start(bf16[2,1,128,1024]{3,2,1,0:T(8,128)(2,1)S(1)} %slice.361), channel_id=1, source_target_pairs={{0,16},{8,24},{16,0},{24,8},{1,17},{9,25},{17,1},{25,9},{2,18},{10... | collective-permute-start | bytes 1572872 | tf_op jit(solution)/shard_map/ppermute | solution.py:884
  319.4 47.5 %collective-permute-start.41 = (bf16[4,2,128,1024]{3,2,1,0:T(8,128)(2,1)}, bf16[4,2,128,1024]{3,2,1,0:T(8,128)(2,1)S(1)}, u32[]{:S(2)}, u32[]{:S(2)}) collective-permute-start(bf16[4,2,128,1024]{3,2,1,0:T(8,128)(2,1)} %get-tuple-element.205.refs_7_.refs_4_.refs_6_), channel_id=1, source_target_pairs={{0,8},{8,0},{16,24},{24,16},{1,9},{9,1},{17,25},{25,17},{2,10},{10... | collective-permute-start | bytes 6291464 | tf_op jit(solution)/shard_map/ppermute | solution.py:884
  320.6 47.2 %collective-permute-start.42 = (bf16[4,2,128,1024]{3,2,1,0:T(8,128)(2,1)}, bf16[4,2,128,1024]{3,2,1,0:T(8,128)(2,1)}, u32[]{:S(2)}, u32[]{:S(2)}) collective-permute-start(bf16[4,2,128,1024]{3,2,1,0:T(8,128)(2,1)} %get-tuple-element.205.refs_7_.refs_4_.refs_6_), channel_id=1, source_target_pairs={{0,16},{8,24},{16,0},{24,8},{1,17},{9,25},{17,1},{25,9},{2,18},{10... | collective-permute-start | bytes 6291464 | tf_op jit(solution)/shard_map/ppermute | solution.py:884
  328.7 39.1 %collective-permute-start.44 = (bf16[512,1024]{1,0:T(8,128)(2,1)}, bf16[512,1024]{1,0:T(8,128)(2,1)S(1)}, u32[]{:S(2)}, u32[]{:S(2)}) collective-permute-start(bf16[512,1024]{1,0:T(8,128)(2,1)} %get-tuple-element.208), channel_id=1, source_target_pairs={{0,0},{2,4},{4,2},{6,6},{1,1},{3,5},{5,3},{7,7},{8,8},{10,12},{12,... | collective-permute-start | bytes 3145736 | tf_op jit(solution)/shard_map/ppermute | solution.py:888
  517.7 74.7 %collective-permute-start.59 = (bf16[4,8,128,1024]{3,2,1,0:T(8,128)(2,1)}, bf16[4,8,128,1024]{3,2,1,0:T(8,128)(2,1)}, u32[]{:S(2)}, u32[]{:S(2)}) collective-permute-start(bf16[4,8,128,1024]{3,2,1,0:T(8,128)(2,1)} %get-tuple-element.234), channel_id=1, source_target_pairs={{0,4},{4,0},{1,5},{5,1},{2,6},{6,2},{3,7},{7,3},{8,12},{12,8},{9,1... | collective-permute-start | bytes 25165832 | tf_op jit(solution)/shard_map/ppermute | solution.py:884
  608.4 46.9 %collective-permute-start.61 = (bf16[8,128,1024]{2,1,0:T(8,128)(2,1)}, bf16[8,128,1024]{2,1,0:T(8,128)(2,1)S(1)}, u32[]{:S(2)}, u32[]{:S(2)}) collective-permute-start(bf16[8,128,1024]{2,1,0:T(8,128)(2,1)} %get-tuple-element.236.refs_3_), channel_id=1, source_target_pairs={{0,16},{8,24},{16,0},{24,8},{1,17},{9,25},{17,1},{25,9},{2,18},{10... | collective-permute-start | bytes 6291464 | tf_op jit(solution)/shard_map/ppermute | solution.py:884
  609.0 46.6 %collective-permute-start.60 = (bf16[8,128,1024]{2,1,0:T(8,128)(2,1)}, bf16[8,128,1024]{2,1,0:T(8,128)(2,1)S(1)}, u32[]{:S(2)}, u32[]{:S(2)}) collective-permute-start(bf16[8,128,1024]{2,1,0:T(8,128)(2,1)} %get-tuple-element.235.refs_2_), channel_id=1, source_target_pairs={{0,8},{8,0},{16,24},{24,16},{1,9},{9,1},{17,25},{25,17},{2,10},{10... | collective-permute-start | bytes 6291464 | tf_op jit(solution)/shard_map/ppermute | solution.py:884
  673.2 36.8 %collective-permute-start.65 = (bf16[4,128,1024]{2,1,0:T(8,128)(2,1)S(1)}, bf16[4,128,1024]{2,1,0:T(8,128)(2,1)S(1)}, u32[]{:S(2)}, u32[]{:S(2)}) collective-permute-start(bf16[4,128,1024]{2,1,0:T(8,128)(2,1)S(1)} %add_convert_fusion.5), channel_id=1, source_target_pairs={{0,8},{8,0},{16,24},{24,16},{1,9},{9,1},{17,25},{25,17},{2,10},{10... | collective-permute-start | bytes 3145736 | tf_op jit(solution)/shard_map/ppermute | solution.py:884
  674.7 35.3 %collective-permute-start.66 = (bf16[4,128,1024]{2,1,0:T(8,128)(2,1)}, bf16[4,128,1024]{2,1,0:T(8,128)(2,1)S(1)}, u32[]{:S(2)}, u32[]{:S(2)}) collective-permute-start(bf16[4,128,1024]{2,1,0:T(8,128)(2,1)} %add_convert_fusion.4), channel_id=1, source_target_pairs={{0,16},{8,24},{16,0},{24,8},{1,17},{9,25},{17,1},{25,9},{2,18},{10... | collective-permute-start | bytes 3145736 | tf_op jit(solution)/shard_map/ppermute | solution.py:884
  675.5 44.8 %collective-permute-start.67 = (bf16[2,2,128,1024]{3,2,1,0:T(8,128)(2,1)}, bf16[2,2,128,1024]{3,2,1,0:T(8,128)(2,1)S(1)}, u32[]{:S(2)}, u32[]{:S(2)}) collective-permute-start(bf16[2,2,128,1024]{3,2,1,0:T(8,128)(2,1)} %get-tuple-element.256), channel_id=1, source_target_pairs={{0,8},{8,0},{16,24},{24,16},{1,9},{9,1},{17,25},{25,17},{2,10},{10... | collective-permute-start | bytes 3145736 | tf_op jit(solution)/shard_map/ppermute | solution.py:884
  692.9 35.1 %collective-permute-start.64 = (bf16[512,1024]{1,0:T(8,128)(2,1)}, bf16[512,1024]{1,0:T(8,128)(2,1)}, u32[]{:S(2)}, u32[]{:S(2)}) collective-permute-start(bf16[512,1024]{1,0:T(8,128)(2,1)} %get-tuple-element.252.refs_1_.refs_8_), channel_id=1, source_target_pairs={{0,4},{1,5},{4,0},{5,1},{2,6},{3,7},{6,2},{7,3},{8,12},{9,13},{12,... | collective-permute-start | bytes 3145736 | tf_op jit(solution)/shard_map/ppermute | solution.py:884
  723.5 47.5 %collective-permute-start.70 = (bf16[8,128,1024]{2,1,0:T(8,128)(2,1)}, bf16[8,128,1024]{2,1,0:T(8,128)(2,1)}, u32[]{:S(2)}, u32[]{:S(2)}) collective-permute-start(bf16[8,128,1024]{2,1,0:T(8,128)(2,1)} %get-tuple-element.259.refs_6_), channel_id=1, source_target_pairs={{0,16},{8,24},{16,0},{24,8},{1,17},{9,25},{17,1},{25,9},{2,18},{10... | collective-permute-start | bytes 6291464 | tf_op jit(solution)/shard_map/ppermute | solution.py:884
  724.3 49.3 %collective-permute-start.72 = (bf16[8,128,1024]{2,1,0:T(8,128)(2,1)}, bf16[8,128,1024]{2,1,0:T(8,128)(2,1)}, u32[]{:S(2)}, u32[]{:S(2)}) collective-permute-start(bf16[8,128,1024]{2,1,0:T(8,128)(2,1)} %get-tuple-element.258.refs_5_), channel_id=1, source_target_pairs={{0,8},{8,0},{16,24},{24,16},{1,9},{9,1},{17,25},{25,17},{2,10},{10... | collective-permute-start | bytes 6291464 | tf_op jit(solution)/shard_map/ppermute | solution.py:884
  727.2 39.0 %collective-permute-start.74 = (bf16[4,128,1024]{2,1,0:T(8,128)(2,1)}, bf16[4,128,1024]{2,1,0:T(8,128)(2,1)S(1)}, u32[]{:S(2)}, u32[]{:S(2)}) collective-permute-start(bf16[4,128,1024]{2,1,0:T(8,128)(2,1)} %add_convert_fusion.1), channel_id=1, source_target_pairs={{0,1},{1,0},{2,3},{3,2},{4,5},{5,4},{6,7},{7,6},{8,9},{9,8},{10,11... | collective-permute-start | bytes 3145736 | tf_op jit(solution)/shard_map/ppermute | solution.py:884
  768.8 37.0 %collective-permute-start.75 = (bf16[2,128,1024]{2,1,0:T(8,128)(2,1)}, bf16[2,128,1024]{2,1,0:T(8,128)(2,1)S(1)}, u32[]{:S(2)}, u32[]{:S(2)}) collective-permute-start(bf16[2,128,1024]{2,1,0:T(8,128)(2,1)} %add_convert_fusion.9), channel_id=1, source_target_pairs={{0,2},{2,0},{1,3},{3,1},{4,6},{6,4},{5,7},{7,5},{8,10},{10,8},{9,1... | collective-permute-start | bytes 1572872 | tf_op jit(solution)/shard_map/ppermute | solution.py:884
  772.7 37.0 %collective-permute-start.71 = (bf16[4,128,1024]{2,1,0:T(8,128)(2,1)S(1)}, bf16[4,128,1024]{2,1,0:T(8,128)(2,1)S(1)}, u32[]{:S(2)}, u32[]{:S(2)}) collective-permute-start(bf16[4,128,1024]{2,1,0:T(8,128)(2,1)S(1)} %add_convert_fusion.3), channel_id=1, source_target_pairs={{0,8},{8,0},{16,24},{24,16},{1,9},{9,1},{17,25},{25,17},{2,10},{10... | collective-permute-start | bytes 3145736 | tf_op jit(solution)/shard_map/ppermute | solution.py:884
  775.3 34.5 %collective-permute-start.73 = (bf16[4,128,1024]{2,1,0:T(8,128)(2,1)S(1)}, bf16[4,128,1024]{2,1,0:T(8,128)(2,1)S(1)}, u32[]{:S(2)}, u32[]{:S(2)}) collective-permute-start(bf16[4,128,1024]{2,1,0:T(8,128)(2,1)S(1)} %add_convert_fusion.2), channel_id=1, source_target_pairs={{0,16},{8,24},{16,0},{24,8},{1,17},{9,25},{17,1},{25,9},{2,18},{10... | collective-permute-start | bytes 3145736 | tf_op jit(solution)/shard_map/ppermute | solution.py:884
  776.4 33.4 %collective-permute-start.76 = (bf16[2,128,1024]{2,1,0:T(8,128)(2,1)S(1)}, bf16[2,128,1024]{2,1,0:T(8,128)(2,1)S(1)}, u32[]{:S(2)}, u32[]{:S(2)}) collective-permute-start(bf16[2,128,1024]{2,1,0:T(8,128)(2,1)S(1)} %fusion.9), channel_id=1, source_target_pairs={{0,16},{8,24},{16,0},{24,8},{1,17},{9,25},{17,1},{25,9},{2,18},{10... | collective-permute-start | bytes 1572872 | tf_op jit(solution)/shard_map/ppermute | solution.py:884
  887.9 35.3 %collective-permute-start.86 = (bf16[4,128,1024]{2,1,0:T(8,128)(2,1)S(1)}, bf16[4,128,1024]{2,1,0:T(8,128)(2,1)S(1)}, u32[]{:S(2)}, u32[]{:S(2)}) collective-permute-start(bf16[4,128,1024]{2,1,0:T(8,128)(2,1)S(1)} %add_convert_fusion), channel_id=1, source_target_pairs={{0,1},{1,0},{2,3},{3,2},{4,5},{5,4},{6,7},{7,6},{8,9},{9,8},{10,11... | collective-permute-start | bytes 3145736 | tf_op jit(solution)/shard_map/ppermute | solution.py:884
  898.2 67.5 %collective-permute-start.79 = (bf16[512,1024]{1,0:T(8,128)(2,1)}, bf16[512,1024]{1,0:T(8,128)(2,1)S(1)}, u32[]{:S(2)}, u32[]{:S(2)}) collective-permute-start(bf16[512,1024]{1,0:T(8,128)(2,1)} %fusion.2), channel_id=1, source_target_pairs={{0,0},{2,4},{4,2},{6,6},{1,1},{3,5},{5,3},{7,7},{8,8},{10,12},{12,... | collective-permute-start | bytes 3145736 | tf_op jit(solution)/shard_map/ppermute | solution.py:888
  927.4 38.4 %collective-permute-start.87 = (bf16[2,128,1024]{2,1,0:T(8,128)(2,1)S(1)}, bf16[2,128,1024]{2,1,0:T(8,128)(2,1)S(1)}, u32[]{:S(2)}, u32[]{:S(2)}) collective-permute-start(bf16[2,128,1024]{2,1,0:T(8,128)(2,1)S(1)} %add_convert_fusion.6), channel_id=1, source_target_pairs={{0,2},{2,0},{1,3},{3,1},{4,6},{6,4},{5,7},{7,5},{8,10},{10,8},{9,1... | collective-permute-start | bytes 1572872 | tf_op jit(solution)/shard_map/ppermute | solution.py:884
  (177 other events, 1720.1 us)
Sparse Core Ops, SparseCore 0:
  110.6 70.3 all-gather.1

commit v13 on v11

--- a/solution.py
+++ b/solution.py
@@ -21,7 +21,7 @@
 GROUP = ("c", "zl")
 MODEL = ("zh", "zl")
 ALL = ("zh", "zl", "q", "c")
-VMEM_LIMIT = 56 * 1024 * 1024
+VMEM_LIMIT = 62 * 1024 * 1024
 TIMES = {
     "gate": 0.1, "finish": 0.2, "norm_up": 20.0, "down_norm": 20.0, "units_back": 45.0, "up_back": 20.0, "norm_back": 6.0,
     "sum_norm_back": 20.0, "grads_theirs": 0.2, "grads_mine": 0.2, "project_qkv": 0.2, "project_gc": 0.2,
@@ -1212,13 +1212,15 @@
         first, last = small_slice and l == 0, small_slice and l == 1
         xs = gather_group(x_low)
         w_heads, bias = weights_of[l]
+        if last:
+            flow.hold(top=cotangent[:ROWS])
         qkv_near = project_in(flow, (xs[0], xs[2]), False, w_heads, in_cols, bias, "project_qkv")
         if first:
             up0.shard = flow.free("up0")
             up0.start_far_z()
             flow.wait(up0.other)
         if last:
-            flow.hold(top=cotangent, own=both1.own)
+            flow.hold(top=jnp.concatenate([flow.free("top"), cotangent[ROWS:]]), own=both1.own)
         forward(flow, xs, qkv_near)
         if first:
             twin, down0.shard = flow.free("up0_twin"), flow.free("down0")
@@ -1248,13 +1250,17 @@
             up0.swap("own", "near_x", "near_y")
         if last:
             flow.wait(both1.near_x, both1.near_y, top_grad)
-            both1.corner()
-            both1.swap("near_x", "near_y")
         send = project_out(flow, [ctx], (2, 3), w_heads, out_cols, True, "project_attn")
         flow.wait(send)
         if first:
             pair = with_sibling(flow.free("heads1"))
+        if last:
+            flow.hold(near_x=both1.near_x, near_y=both1.near_y)
         keep = project_out(flow, [ctx], (0, 1), w_heads, out_cols, False, "project_attn")
+        if last:
+            both1.near_x, both1.near_y = flow.free("near_x"), flow.free("near_y")
+            both1.corner()
+            both1.swap("near_x", "near_y")
         attn, passed = sum_group(keep, send)
         if first:
             flow.wait(passed, gathered, pair, *up0.theirs.values())

time: 991 us -> 991 us (level)
  other arithmetic: 54.4 us -> 72.3 us
  local copies, waits for them, and re-layouts: 71 us -> 60.5 us
    unnamed x210 -> x133, local copies, waits for them, and re-layouts: 40.2 us -> 26.5 us
  transfers between devices with their start and end apart: 101 -> 101, of which waited for: 34 -> 32; matrix products, arithmetic and copies ran while one was open for 9% -> 11% of each run, Pallas kernels for 40% -> 40%
where the time goes in v13:
time: 991 us; the launch traced here: 983 us
  Pallas kernels  473 us (48%)
  waiting for transfers between devices  248 us (25%)
  starting transfers between devices  112 us (11%)
  other arithmetic  72.3 us (7%)
  local copies, waits for them, and re-layouts  60.5 us (6%)
  between operations  17.8 us (2%)
    pallas_call x49, Pallas kernels, call(): pl.pallas_call(wrapped, grid_spec=pltpu.PrefetchScalarGridSpec(num_scalar...  473 us
    ppermute x90, waiting for transfers between devices, flip(): lax.ppermute(values_in, axes, [(a, a ^ mask) for a in range(lax.axis_size...  165 us
    ppermute x8, waiting for transfers between devices, turn(): lax.ppermute(values_in, ('c', 'zh'), [(2 * a + b, 2 * b + a) for a in ran...  83.4 us
    ppermute x90, starting transfers between devices, flip(): lax.ppermute(values_in, axes, [(a, a ^ mask) for a in range(lax.axis_size...  79.4 us
    ppermute x8, starting transfers between devices, turn(): lax.ppermute(values_in, ('c', 'zh'), [(2 * a + b, 2 * b + a) for a in ran...  31.9 us
    unnamed x133, local copies, waits for them, and re-layouts  26.5 us
  transfers between devices with their start and end apart: 101, of which 32 were waited for; matrix products, arithmetic and copies ran while one was open for 11% of the time, Pallas kernels for 40%

profile of v13, /device:TPU:1, one launch (start us, length us, event | category | flops | bytes accessed | tf_op | source)
XLA Modules:
  0.0 982.8 jit_solution(5788100180483567294)
XLA Ops:
  18.7 36.3 %collective-permute-done.1 = bf16[800,1024]{1,0:T(8,128)(2,1)S(1)} collective-permute-done((bf16[800,1024]{1,0:T(8,128)(2,1)S(1)}, bf16[800,1024]{1,0:T(8,128)(2,1)S(1)}, u32[]{:S(2)}, u32[]{:S(2)}) %collective-permute-start.1) | collective-permute-done | bytes 1638432 | tf_op jit(solution)/shard_map/ppermute | solution.py:888
  85.0 11.8 %collective-permute-done.7.refs_9_ = bf16[512,1024]{1,0:T(8,128)(2,1)S(1)} collective-permute-done((bf16[512,1024]{1,0:T(8,128)(2,1)}, bf16[512,1024]{1,0:T(8,128)(2,1)S(1)}, u32[]{:S(2)}, u32[]{:S(2)}) %collective-permute-start.7) | collective-permute-done | bytes 1048608 | tf_op jit(solution)/shard_map/ppermute | solution.py:884
  110.2 11.4 %collective-permute-done.12 = s32[1,4]{1,0:T(1,128)S(1)} collective-permute-done((s32[1,4]{1,0:T(1,128)S(1)}, s32[1,4]{1,0:T(1,128)S(1)}, u32[]{:S(2)}, u32[]{:S(2)}) %collective-permute-start.12) | collective-permute-done | bytes 48 | tf_op jit(solution)/shard_map/ppermute | solution.py:888
  138.4 28.1 %attend_forward.2 = (bf16[4,512,256]{2,1,0:T(8,128)(2,1)}, f32[4,512,256]{2,1,0:T(8,128)}, f32[4,8,512]{2,1,0:T(8,128)}, bf16[144,1024]{1,0:T(8,128)(2,1)}) custom-call(s32[5]{0:T(128)} %stack.171.refs_0_, s32[4]{0:T(128)} %bitcast.275, bf16[144,1024]{1,0:T(8,128)(2,1)} %get-tuple-element.177.refs_2_, ...), custom_call_target="tpu_custom_call", output_to_operand_aliasing={{3}: (2, {})} | custom-call | flops 14000000000 | bytes 1024 | tf_op jit(solution)/shard_map/attend_forward/pallas_call | solution.py:80
  199.8 27.2 %collective-permute-done.24.refs_14_.refs_10_ = bf16[2,1,128,1024]{3,2,1,0:T(8,128)(2,1)} collective-permute-done((bf16[2,1,128,1024]{3,2,1,0:T(8,128)(2,1)S(1)}, bf16[2,1,128,1024]{3,2,1,0:T(8,128)(2,1)}, u32[]{:S(2)}, u32[]{:S(2)}) %collective-permute-start.24) | collective-permute-done | bytes 524320 | tf_op jit(solution)/shard_map/ppermute | solution.py:884
  235.9 19.0 %norm_up.2 = (f32[512,1024]{1,0:T(8,128)}, bf16[512,1024]{1,0:T(8,128)(2,1)}, f32[512,128]{1,0:T(8,128)}, bf16[512,4096]{1,0:T(8,128)(2,1)}, bf16[512,4096]{1,0:...) custom-call(s32[5]{0:T(128)} %stack.171.refs_0_, ...), custom_call_target="tpu_custom_call", output_to_operand_aliasing={{5}: (3, {}), {6}: (4, {})} | custom-call | flops 7000000000 | bytes 1024 | tf_op jit(solution)/shard_map/norm_up/pallas_call | solution.py:80
  258.5 15.2 %collective-permute-done.28.refs_1_ = bf16[2,144,1024]{2,1,0:T(8,128)(2,1)S(1)} collective-permute-done((bf16[2,144,1024]{2,1,0:T(8,128)(2,1)}, bf16[2,144,1024]{2,1,0:T(8,128)(2,1)S(1)}, u32[]{:S(2)}, u32[]{:S(2)}) %collective-permute-start.28) | collective-permute-done | bytes 589856 | tf_op jit(solution)/shard_map/ppermute | solution.py:888
  276.3 14.4 %down_norm.2 = (f32[512,1024]{1,0:T(8,128)}, bf16[512,1024]{1,0:T(8,128)(2,1)}, f32[512,128]{1,0:T(8,128)}, bf16[2,144,1024]{2,1,0:T(8,128)(2,1)}) custom-call(s32[5]{0:T(128)} %stack.171.refs_0_, bf16[2,144,1024]{2,1,0:T(8,128)(2,1)} %get-tuple-element.197.refs_1_, ...), custom_call_target="tpu_custom_call", output_to_operand_aliasing={{3}: (1, {})} | custom-call | flops 7000000000 | bytes 1024 | tf_op jit(solution)/shard_map/down_norm/pallas_call | solution.py:80
  298.0 10.1 %collective-permute-done.38.refs_6_.refs_4_.refs_5_ = bf16[2,2,144,1024]{3,2,1,0:T(8,128)(2,1)S(1)} collective-permute-done((bf16[2,2,144,1024]{3,2,1,0:T(8,128)(2,1)S(1)}, bf16[2,2,144,1024]{3,2,1,0:T(8,128)(2,1)S(1)}, u32[]{:S(2)}, u32[]{:S(2)}) %collective-permute-start.38) | collective-permute-done | bytes 1179680 | tf_op jit(solution)/shard_map/ppermute | solution.py:884
  334.0 28.5 %attend_forward.3 = (bf16[4,512,256]{2,1,0:T(8,128)(2,1)}, f32[4,512,256]{2,1,0:T(8,128)}, f32[4,8,512]{2,1,0:T(8,128)}) custom-call(s32[5]{0:T(128)} %stack.171.refs_0_, s32[4]{0:T(128)} %bitcast.276, bf16[2,512,768]{2,1,0:T(8,128)(2,1)} %get-tuple-element.206.refs_1_.refs_2_.refs_3_, bf16[2,512,768]{2,1,0:T(8,128)(2,1)} %get-tuple-element.213.refs_3_.refs_4_), custom_call_target="tpu_custom_call" | custom-call | flops 14000000000 | bytes 1024 | tf_op jit(solution)/shard_map/attend_forward/pallas_call | solution.py:80
  387.7 17.6 %collective-permute-done.47.refs_2_ = bf16[2,2,128,1024]{3,2,1,0:T(8,128)(2,1)S(1)} collective-permute-done((bf16[2,2,128,1024]{3,2,1,0:T(8,128)(2,1)S(1)}, bf16[2,2,128,1024]{3,2,1,0:T(8,128)(2,1)S(1)}, u32[]{:S(2)}, u32[]{:S(2)}) %collective-permute-start.47) | collective-permute-done | bytes 1048608 | tf_op jit(solution)/shard_map/ppermute | solution.py:884
  416.0 19.0 %norm_up.3 = (f32[512,1024]{1,0:T(8,128)}, bf16[512,1024]{1,0:T(8,128)(2,1)}, f32[512,128]{1,0:T(8,128)}, bf16[512,4096]{1,0:T(8,128)(2,1)}, bf16[512,4096]{1,0:T(8,128)(2,1)}) custom-call(s32[5]{0:T(128)} %stack.171.refs_0_, f32[512,1024]{1,0:T(8,128)} %get-tuple-element.216.refs_1_.refs_6_, bf16[512,1024]{1,0:T(8,128)(2,1)} %get-tuple-element.217.refs_2_, ...), custom_call_target="tpu_custom_call" | custom-call | flops 7000000000 | bytes 1024 | tf_op jit(solution)/shard_map/norm_up/pallas_call | solution.py:80
  435.0 14.3 %down_norm.3 = (f32[512,1024]{1,0:T(8,128)}, bf16[512,1024]{1,0:T(8,128)(2,1)}, f32[512,128]{1,0:T(8,128)}) custom-call(s32[5]{0:T(128)} %stack.171.refs_0_, bf16[512,4096]{1,0:T(8,128)(2,1)} %get-tuple-element.222.refs_1_.refs_3_, f32[512,1024]{1,0:T(8,128)} %get-tuple-element.223.refs_2_.refs_4_, ...), custom_call_target="tpu_custom_call" | custom-call | flops 7000000000 | bytes 1024 | tf_op jit(solution)/shard_map/down_norm/pallas_call | solution.py:80
  453.6 12.7 %units_back.2 = (f32[512,1024]{1,0:T(8,128)}, bf16[512,1024]{1,0:T(8,128)(2,1)}, f32[8,1024]{1,0:T(8,128)}, bf16[512,4096]{1,0:T(8,128)(2,1)}, f32[4,1,1024]{2,1,0:T(1,128)}) custom-call(s32[5]{0:T(128)} %stack.171.refs_0_, bf16[512,1024]{1,0:T(8,128)(2,1)} %copy-done.47, f32[512,1024]{1,0:T(8,128)} %get-tuple-element.225.refs_2_, ...), custom_call_target="tpu_custom_call" | custom-call | flops 15749999616 | bytes 1024 | tf_op jit(solution)/shard_map/units_back/pallas_call | solution.py:80
  466.4 11.4 %collective-permute-done.54.refs_1_ = bf16[512,1024]{1,0:T(8,128)(2,1)S(1)} collective-permute-done((bf16[512,1024]{1,0:T(8,128)(2,1)}, bf16[512,1024]{1,0:T(8,128)(2,1)S(1)}, u32[]{:S(2)}, u32[]{:S(2)}) %collective-permute-start.54) | collective-permute-done | bytes 1048608 | tf_op jit(solution)/shard_map/ppermute | solution.py:888
  478.9 15.0 %up_back.2 = (f32[512,1024]{1,0:T(8,128)}, bf16[512,1024]{1,0:T(8,128)(2,1)}, f32[8,1024]{1,0:T(8,128)}, bf16[512,1024]{1,0:T(8,128)(2,1)}) custom-call(s32[5]{0:T(128)} %stack.171.refs_0_, bf16[512,1024]{1,0:T(8,128)(2,1)} %copy-done.10, bf16[512,4096]{1,0:T(8,128)(2,1)} %get-tuple-element.228.refs_2_.refs_5_, ...), custom_call_target="tpu_custom_call", output_to_operand_aliasing={{3}: (1, {})} | custom-call | flops 7000000000 | bytes 1024 | tf_op jit(solution)/shard_map/up_back/pallas_call | solution.py:80
  494.0 12.7 %grads_theirs.2.refs_1_.refs_2_ = bf16[4,8,128,1024]{3,2,1,0:T(8,128)(2,1)} custom-call(s32[5]{0:T(128)} %stack.171.refs_0_, bf16[512,1024]{1,0:T(8,128)(2,1)} %get-tuple-element.231.refs_1_.refs_10_, bf16[512,1024]{1,0:T(8,128)(2,1)} %get-tuple-element.232.refs_2_, bf16[512,4096]{1,0:T(8,128)(2,1)} %get-tuple-element.222.refs_1_.refs_3_, ...), custom_call_target="tpu_custom_call" | custom-call | flops 70000000 | bytes 1024 | tf_op jit(solution)/shard_map/grads_theirs/pallas_call | solution.py:80
  519.8 28.2 %attend_backward.4.refs_2_.refs_1_.refs_14_ = bf16[4,512,384]{2,1,0:T(8,128)(2,1)} custom-call(s32[5]{0:T(128)} %stack.171.refs_0_, s32[4]{0:T(128)} %gate.18.refs_1_, bf16[2,512,768]{2,1,0:T(8,128)(2,1)} %get-tuple-element.206.refs_1_.refs_2_.refs_3_, bf16[2,512,768]{2,1,0:T(8,128)(2,1)} %get-tuple-element.213.refs_3_.refs_4_, ...), custom_call_target="tpu_custom_call" | custom-call | flops 10499999744 | bytes 1024 | tf_op jit(solution)/shard_map/attend_backward/pallas_call | solution.py:80
  548.0 28.4 %attend_backward.5.refs_2_.refs_3_.refs_15_ = bf16[4,512,384]{2,1,0:T(8,128)(2,1)} custom-call(s32[5]{0:T(128)} %stack.171.refs_0_, s32[4]{0:T(128)} %gate.18.refs_1_, bf16[4,512,384]{2,1,0:T(8,128)(2,1)} %attend_backward.4.refs_2_.refs_1_.refs_14_, bf16[2,512,768]{2,1,0:T(8,128)(2,1)} %get-tuple-element.206.refs_1_.refs_2_.refs_3_, ...), custom_call_target="tpu_custom_call" | custom-call | flops 10499999744 | bytes 1024 | tf_op jit(solution)/shard_map/attend_backward/pallas_call | solution.py:80
  592.0 15.8 %grads_mine.2 = (bf16[8,128,1024]{2,1,0:T(8,128)(2,1)}, bf16[8,128,1024]{2,1,0:T(8,128)(2,1)}, bf16[8,128,1024]{2,1,0:T(8,128)(2,1)}, bf16[4,128,1024]{2,1,0:T(8,128)(2,1)}, bf16[4,128,1024]{2,1,0:T(8,128)(2,1)}) custom-call(s32[5]{0:T(128)} %stack.171.refs_0_, bf16[512,1024]{1,0:T(8,128)(2,1)} %copy-done.20, bf16[512,1024]{1,0:T(8,128)(2,1)} %get-tuple-element.232.refs_2_, ...), custom_call_target="tpu_custom_call" | custom-call | flops 70000000 | bytes 1024 | tf_op jit(solution)/shard_map/grads_mine/pallas_call | solution.py:80
  611.1 13.1 %heads_grad.2 = (bf16[2,2,128,1024]{3,2,1,0:T(8,128)(2,1)}, bf16[2,2,128,1024]{3,2,1,0:T(8,128)(2,1)}, f32[1,768]{1,0:T(1,128)}) custom-call(s32[5]{0:T(128)} %stack.171.refs_0_, bf16[8,128,1024]{2,1,0:T(8,128)(2,1)} %get-tuple-element.241.refs_1_.refs_5_, bf16[8,128,1024]{2,1,0:T(8,128)(2,1)} %get-tuple-element.239.refs_2_, ...), custom_call_target="tpu_custom_call" | custom-call | flops 70000000 | bytes 1024 | tf_op jit(solution)/shard_map/heads_grad/pallas_call | solution.py:80
  624.2 14.2 %units_back.3 = (f32[512,1024]{1,0:T(8,128)}, bf16[512,1024]{1,0:T(8,128)(2,1)}, f32[8,1024]{1,0:T(8,128)}, bf16[512,4096]{1,0:T(8,128)(2,1)}, f32[4,1,1024]{2,1,0:T(1,128)}) custom-call(s32[5]{0:T(128)} %stack.171.refs_0_, bf16[2,2,128,1024]{3,2,1,0:T(8,128)(2,1)} %get-tuple-element.244.refs_1_.refs_3_, f32[512,1024]{1,0:T(8,128)} %get-tuple-element.245.refs_2_, ...), custom_call_target="tpu_custom_call" | custom-call | flops 15749999616 | bytes 1024 | tf_op jit(solution)/shard_map/units_back/pallas_call | solution.py:80
  638.4 17.6 %collective-permute-done.61.refs_2_ = bf16[8,128,1024]{2,1,0:T(8,128)(2,1)} collective-permute-done((bf16[8,128,1024]{2,1,0:T(8,128)(2,1)}, bf16[8,128,1024]{2,1,0:T(8,128)(2,1)}, u32[]{:S(2)}, u32[]{:S(2)}) %collective-permute-start.61) | collective-permute-done | bytes 2097184 | tf_op jit(solution)/shard_map/ppermute | solution.py:884
  656.8 12.8 %grads_theirs.3 = (bf16[4,8,128,1024]{3,2,1,0:T(8,128)(2,1)}, bf16[2,2,128,1024]{3,2,1,0:T(8,128)(2,1)}) custom-call(s32[5]{0:T(128)} %stack.171.refs_0_, bf16[8,128,1024]{2,1,0:T(8,128)(2,1)} %collective-permute-done.60.refs_1_.refs_11_, bf16[8,128,1024]{2,1,0:T(8,128)(2,1)} %collective-permute-done.61.refs_2_, ...), custom_call_target="tpu_custom_call", output_to_operand_aliasing={{1}: (3, {})} | custom-call | flops 70000000 | bytes 1024 | tf_op jit(solution)/shard_map/grads_theirs/pallas_call | solution.py:80
  678.0 15.1 %up_back.3 = (f32[512,1024]{1,0:T(8,128)}, bf16[512,1024]{1,0:T(8,128)(2,1)}, f32[8,1024]{1,0:T(8,128)}) custom-call(s32[5]{0:T(128)} %stack.171.refs_0_, bf16[4,8,128,1024]{3,2,1,0:T(8,128)(2,1)} %get-tuple-element.252.refs_1_, bf16[512,4096]{1,0:T(8,128)(2,1)} %get-tuple-element.251.refs_7_.refs_2_.refs_5_, f32[512,1024]{1,0:T(8,128)} %get-tuple-element.253.refs_3_, ...), custom_call_target="tpu_custom_call" | custom-call | flops 7000000000 | bytes 1024 | tf_op jit(solution)/shard_map/up_back/pallas_call | solution.py:80
  695.1 15.8 %grads_mine.3 = (bf16[8,128,1024]{2,1,0:T(8,128)(2,1)}, bf16[8,128,1024]{2,1,0:T(8,128)(2,1)}, bf16[8,128,1024]{2,1,0:T(8,128)(2,1)}, bf16[4,128,1024]{2,1,0:T(8,128)(2,1)}, bf16[4,128,1024]{2,1,0:T(8,128)(2,1)}) custom-call(s32[5]{0:T(128)} %stack.171.refs_0_, bf16[512,1024]{1,0:T(8,128)(2,1)} %get-tuple-element.256.refs_1_.refs_8_, ...), custom_call_target="tpu_custom_call" | custom-call | flops 70000000 | bytes 1024 | tf_op jit(solution)/shard_map/grads_mine/pallas_call | solution.py:80
  711.0 10.4 %collective-permute-done.67.refs_3_ = bf16[2,2,128,1024]{3,2,1,0:T(8,128)(2,1)} collective-permute-done((bf16[2,2,128,1024]{3,2,1,0:T(8,128)(2,1)}, bf16[2,2,128,1024]{3,2,1,0:T(8,128)(2,1)}, u32[]{:S(2)}, u32[]{:S(2)}) %collective-permute-start.67) | collective-permute-done | bytes 1048608 | tf_op jit(solution)/shard_map/ppermute | solution.py:884
  738.4 28.4 %attend_backward.6 = (bf16[4,512,384]{2,1,0:T(8,128)(2,1)}, bf16[4,128,1024]{2,1,0:T(8,128)(2,1)}, bf16[4,128,1024]{2,1,0:T(8,128)(2,1)}, bf16[2,2,128,1024]{3,2,1,0:T(8,128)(2,1)}, bf16[8,128,1024]{2,1,0:T(8,128)(2,1)}) custom-call(s32[5]{0:T(128)} %stack.171.refs_0_, ...), custom_call_target="tpu_custom_call", output_to_operand_aliasing={{1}: (2, {}), {2}: (3, {}), {3}: (4, {}), {4}: (5, {})} | custom-call | flops 10499999744 | bytes 1024 | tf_op jit(solution)/shard_map/attend_backward/pallas_call | solution.py:80
  782.2 28.1 %attend_backward.7 = (bf16[4,512,384]{2,1,0:T(8,128)(2,1)}, bf16[8,128,1024]{2,1,0:T(8,128)(2,1)}, bf16[2,2,128,1024]{3,2,1,0:T(8,128)(2,1)}) custom-call(s32[5]{0:T(128)} %stack.171.refs_0_, s32[4]{0:T(128)} %gate.18.refs_1_, bf16[4,512,384]{2,1,0:T(8,128)(2,1)} %get-tuple-element.266.refs_2_.refs_5_.refs_3_.refs_12_, ...), custom_call_target="tpu_custom_call", output_to_operand_aliasing={{1}: (6, {}), {2}: (7, {})} | custom-call | flops 10499999744 | bytes 1024 | tf_op jit(solution)/shard_map/attend_backward/pallas_call | solution.py:80
  845.5 12.7 %heads_grad.3 = (bf16[2,2,128,1024]{3,2,1,0:T(8,128)(2,1)}, bf16[2,2,128,1024]{3,2,1,0:T(8,128)(2,1)}, f32[1,768]{1,0:T(1,128)}) custom-call(s32[5]{0:T(128)} %stack.171.refs_0_, bf16[512,1024]{1,0:T(8,128)(2,1)} %fusion.refs_1_, bf16[128,1024]{1,0:T(8,128)(2,1)} %copy-done.37, bf16[128,1024]{1,0:T(8,128)(2,1)} %copy-done.38, ...), custom_call_target="tpu_custom_call" | custom-call | flops 70000000 | bytes 1024 | tf_op jit(solution)/shard_map/heads_grad/pallas_call | solution.py:80
  868.3 28.4 %collective-permute-done.78.refs_1_ = bf16[512,1024]{1,0:T(8,128)(2,1)} collective-permute-done((bf16[512,1024]{1,0:T(8,128)(2,1)}, bf16[512,1024]{1,0:T(8,128)(2,1)}, u32[]{:S(2)}, u32[]{:S(2)}) %collective-permute-start.78) | collective-permute-done | bytes 1048608 | tf_op jit(solution)/shard_map/ppermute | solution.py:884
  913.6 9.4 collective-permute-done.90
  (558 shorter events, 381.7 us)
Async XLA Ops:
  7.2 181.9 %all-gather.2.cloned.1.call-start = ((), (), s32[]{:S(2)}) async-start(), calls=%async_computation | async-start | bytes 2162688 | tf_op jit(solution)/shard_map/all_gather | solution.py:1173
  13.1 42.0 %collective-permute-start.1 = (bf16[800,1024]{1,0:T(8,128)(2,1)S(1)}, bf16[800,1024]{1,0:T(8,128)(2,1)S(1)}, u32[]{:S(2)}, u32[]{:S(2)}) collective-permute-start(bf16[800,1024]{1,0:T(8,128)(2,1)S(1)} %pad_maximum_fusion.1), channel_id=1, source_target_pairs={{0,0},{2,4},{4,2},{6,6},{1,1},{3,5},{5,3},{7,7},{8,8},{10,12},{12,... | collective-permute-start | bytes 4915208 | tf_op jit(solution)/shard_map/ppermute | solution.py:888
  131.4 39.5 %collective-permute-start.10 = (bf16[4,1,128,1024]{3,2,1,0:T(8,128)(2,1)}, bf16[4,1,128,1024]{3,2,1,0:T(8,128)(2,1)S(1)}, u32[]{:S(2)}, u32[]{:S(2)}) collective-permute-start(bf16[4,1,128,1024]{3,2,1,0:T(8,128)(2,1)} %pad_maximum_fusion.6.refs_11_.refs_7_), channel_id=1, source_target_pairs={{0,8},{8,0},{16,24},{24,16},{1,9},{9,1},{17,25},{25,17},{2,10},{10... | collective-permute-start | bytes 3145736 | tf_op jit(solution)/shard_map/ppermute | solution.py:884
  132.6 38.3 %collective-permute-start.11 = (bf16[4,1,128,1024]{3,2,1,0:T(8,128)(2,1)}, bf16[4,1,128,1024]{3,2,1,0:T(8,128)(2,1)}, u32[]{:S(2)}, u32[]{:S(2)}) collective-permute-start(bf16[4,1,128,1024]{3,2,1,0:T(8,128)(2,1)} %pad_maximum_fusion.6.refs_11_.refs_7_), channel_id=1, source_target_pairs={{0,16},{8,24},{16,0},{24,8},{1,17},{9,25},{17,1},{25,9},{2,18},{10... | collective-permute-start | bytes 3145736 | tf_op jit(solution)/shard_map/ppermute | solution.py:884
  133.9 32.7 %collective-permute-start.13 = (bf16[2,128,1024]{2,1,0:T(8,128)(2,1)S(1)}, bf16[2,128,1024]{2,1,0:T(8,128)(2,1)}, u32[]{:S(2)}, u32[]{:S(2)}) collective-permute-start(bf16[2,128,1024]{2,1,0:T(8,128)(2,1)S(1)} %copy-done.3), channel_id=1, source_target_pairs={{0,2},{2,0},{1,3},{3,1},{4,6},{6,4},{5,7},{7,5},{8,10},{10,8},{9,1... | collective-permute-start | bytes 1572872 | tf_op jit(solution)/shard_map/ppermute | solution.py:884
  135.7 33.0 %collective-permute-start.15 = (bf16[2,1,128,1024]{3,2,1,0:T(8,128)(2,1)}, bf16[2,1,128,1024]{3,2,1,0:T(8,128)(2,1)}, u32[]{:S(2)}, u32[]{:S(2)}) collective-permute-start(bf16[2,1,128,1024]{3,2,1,0:T(8,128)(2,1)} %pad_maximum_fusion.13), channel_id=1, source_target_pairs={{0,1},{1,0},{2,3},{3,2},{4,5},{5,4},{6,7},{7,6},{8,9},{9,8},{10,11... | collective-permute-start | bytes 1572872 | tf_op jit(solution)/shard_map/ppermute | solution.py:884
  190.7 37.3 %collective-permute-start.21 = (bf16[4,1,128,1024]{3,2,1,0:T(8,128)(2,1)}, bf16[4,1,128,1024]{3,2,1,0:T(8,128)(2,1)}, u32[]{:S(2)}, u32[]{:S(2)}) collective-permute-start(bf16[4,1,128,1024]{3,2,1,0:T(8,128)(2,1)} %get-tuple-element.191.refs_5_.refs_10_), channel_id=1, source_target_pairs={{0,8},{8,0},{16,24},{24,16},{1,9},{9,1},{17,25},{25,17},{2,10},{10... | collective-permute-start | bytes 3145736 | tf_op jit(solution)/shard_map/ppermute | solution.py:884
  190.8 37.8 %collective-permute-start.22 = (bf16[4,1,128,1024]{3,2,1,0:T(8,128)(2,1)}, bf16[4,1,128,1024]{3,2,1,0:T(8,128)(2,1)}, u32[]{:S(2)}, u32[]{:S(2)}) collective-permute-start(bf16[4,1,128,1024]{3,2,1,0:T(8,128)(2,1)} %get-tuple-element.191.refs_5_.refs_10_), channel_id=1, source_target_pairs={{0,16},{8,24},{16,0},{24,8},{1,17},{9,25},{17,1},{25,9},{2,18},{10... | collective-permute-start | bytes 3145736 | tf_op jit(solution)/shard_map/ppermute | solution.py:884
  191.7 37.0 %collective-permute-start.23 = (bf16[512,1024]{1,0:T(8,128)(2,1)}, bf16[512,1024]{1,0:T(8,128)(2,1)}, u32[]{:S(2)}, u32[]{:S(2)}) collective-permute-start(bf16[512,1024]{1,0:T(8,128)(2,1)} %fusion.5.refs_1_), channel_id=1, source_target_pairs={{0,1},{1,0},{4,5},{5,4},{2,3},{3,2},{6,7},{7,6},{8,9},{9,8},{12,13... | collective-permute-start | bytes 3145736 | tf_op jit(solution)/shard_map/ppermute | solution.py:884
  194.5 32.5 %collective-permute-start.24 = (bf16[2,1,128,1024]{3,2,1,0:T(8,128)(2,1)S(1)}, bf16[2,1,128,1024]{3,2,1,0:T(8,128)(2,1)}, u32[]{:S(2)}, u32[]{:S(2)}) collective-permute-start(bf16[2,1,128,1024]{3,2,1,0:T(8,128)(2,1)S(1)} %slice.367), channel_id=1, source_target_pairs={{0,8},{8,0},{16,24},{24,16},{1,9},{9,1},{17,25},{25,17},{2,10},{10... | collective-permute-start | bytes 1572872 | tf_op jit(solution)/shard_map/ppermute | solution.py:884
  320.4 47.5 %collective-permute-start.41 = (bf16[4,2,128,1024]{3,2,1,0:T(8,128)(2,1)}, bf16[4,2,128,1024]{3,2,1,0:T(8,128)(2,1)}, u32[]{:S(2)}, u32[]{:S(2)}) collective-permute-start(bf16[4,2,128,1024]{3,2,1,0:T(8,128)(2,1)} %get-tuple-element.209.refs_7_.refs_4_.refs_6_), channel_id=1, source_target_pairs={{0,8},{8,0},{16,24},{24,16},{1,9},{9,1},{17,25},{25,17},{2,10},{10... | collective-permute-start | bytes 6291464 | tf_op jit(solution)/shard_map/ppermute | solution.py:884
  321.5 47.2 %collective-permute-start.42 = (bf16[4,2,128,1024]{3,2,1,0:T(8,128)(2,1)}, bf16[4,2,128,1024]{3,2,1,0:T(8,128)(2,1)}, u32[]{:S(2)}, u32[]{:S(2)}) collective-permute-start(bf16[4,2,128,1024]{3,2,1,0:T(8,128)(2,1)} %get-tuple-element.209.refs_7_.refs_4_.refs_6_), channel_id=1, source_target_pairs={{0,16},{8,24},{16,0},{24,8},{1,17},{9,25},{17,1},{25,9},{2,18},{10... | collective-permute-start | bytes 6291464 | tf_op jit(solution)/shard_map/ppermute | solution.py:884
  329.8 38.9 %collective-permute-start.44 = (bf16[512,1024]{1,0:T(8,128)(2,1)}, bf16[512,1024]{1,0:T(8,128)(2,1)S(1)}, u32[]{:S(2)}, u32[]{:S(2)}) collective-permute-start(bf16[512,1024]{1,0:T(8,128)(2,1)} %get-tuple-element.212), channel_id=1, source_target_pairs={{0,0},{2,4},{4,2},{6,6},{1,1},{3,5},{5,3},{7,7},{8,8},{10,12},{12,... | collective-permute-start | bytes 3145736 | tf_op jit(solution)/shard_map/ppermute | solution.py:888
  518.6 73.3 %collective-permute-start.59 = (bf16[4,8,128,1024]{3,2,1,0:T(8,128)(2,1)}, bf16[4,8,128,1024]{3,2,1,0:T(8,128)(2,1)}, u32[]{:S(2)}, u32[]{:S(2)}) collective-permute-start(bf16[4,8,128,1024]{3,2,1,0:T(8,128)(2,1)} %get-tuple-element.238), channel_id=1, source_target_pairs={{0,4},{4,0},{1,5},{5,1},{2,6},{6,2},{3,7},{7,3},{8,12},{12,8},{9,1... | collective-permute-start | bytes 25165832 | tf_op jit(solution)/shard_map/ppermute | solution.py:884
  591.1 33.1 %collective-permute-start.62 = (bf16[512,1024]{1,0:T(8,128)(2,1)S(1)}, bf16[512,1024]{1,0:T(8,128)(2,1)}, u32[]{:S(2)}, u32[]{:S(2)}) collective-permute-start(bf16[512,1024]{1,0:T(8,128)(2,1)S(1)} %fusion.3.refs_1_), channel_id=1, source_target_pairs={{0,1},{1,0},{4,5},{5,4},{2,3},{3,2},{6,7},{7,6},{8,9},{9,8},{12,13... | collective-permute-start | bytes 3145736 | tf_op jit(solution)/shard_map/ppermute | solution.py:884
  607.8 48.1 %collective-permute-start.61 = (bf16[8,128,1024]{2,1,0:T(8,128)(2,1)}, bf16[8,128,1024]{2,1,0:T(8,128)(2,1)}, u32[]{:S(2)}, u32[]{:S(2)}) collective-permute-start(bf16[8,128,1024]{2,1,0:T(8,128)(2,1)} %get-tuple-element.240.refs_3_), channel_id=1, source_target_pairs={{0,16},{8,24},{16,0},{24,8},{1,17},{9,25},{17,1},{25,9},{2,18},{10... | collective-permute-start | bytes 6291464 | tf_op jit(solution)/shard_map/ppermute | solution.py:884
  610.1 46.7 %collective-permute-start.60 = (bf16[8,128,1024]{2,1,0:T(8,128)(2,1)}, bf16[8,128,1024]{2,1,0:T(8,128)(2,1)}, u32[]{:S(2)}, u32[]{:S(2)}) collective-permute-start(bf16[8,128,1024]{2,1,0:T(8,128)(2,1)} %get-tuple-element.239.refs_2_), channel_id=1, source_target_pairs={{0,8},{8,0},{16,24},{24,16},{1,9},{9,1},{17,25},{25,17},{2,10},{10... | collective-permute-start | bytes 6291464 | tf_op jit(solution)/shard_map/ppermute | solution.py:884
  673.9 37.1 %collective-permute-start.65 = (bf16[4,128,1024]{2,1,0:T(8,128)(2,1)}, bf16[4,128,1024]{2,1,0:T(8,128)(2,1)}, u32[]{:S(2)}, u32[]{:S(2)}) collective-permute-start(bf16[4,128,1024]{2,1,0:T(8,128)(2,1)} %add_convert_fusion.5), channel_id=1, source_target_pairs={{0,8},{8,0},{16,24},{24,16},{1,9},{9,1},{17,25},{25,17},{2,10},{10... | collective-permute-start | bytes 3145736 | tf_op jit(solution)/shard_map/ppermute | solution.py:884
  677.5 33.5 %collective-permute-start.66 = (bf16[4,128,1024]{2,1,0:T(8,128)(2,1)}, bf16[4,128,1024]{2,1,0:T(8,128)(2,1)}, u32[]{:S(2)}, u32[]{:S(2)}) collective-permute-start(bf16[4,128,1024]{2,1,0:T(8,128)(2,1)} %add_convert_fusion.4), channel_id=1, source_target_pairs={{0,16},{8,24},{16,0},{24,8},{1,17},{9,25},{17,1},{25,9},{2,18},{10... | collective-permute-start | bytes 3145736 | tf_op jit(solution)/shard_map/ppermute | solution.py:884
  677.6 43.7 %collective-permute-start.67 = (bf16[2,2,128,1024]{3,2,1,0:T(8,128)(2,1)}, bf16[2,2,128,1024]{3,2,1,0:T(8,128)(2,1)}, u32[]{:S(2)}, u32[]{:S(2)}) collective-permute-start(bf16[2,2,128,1024]{3,2,1,0:T(8,128)(2,1)} %get-tuple-element.260), channel_id=1, source_target_pairs={{0,8},{8,0},{16,24},{24,16},{1,9},{9,1},{17,25},{25,17},{2,10},{10... | collective-permute-start | bytes 3145736 | tf_op jit(solution)/shard_map/ppermute | solution.py:884
  693.9 35.5 %collective-permute-start.64 = (bf16[512,1024]{1,0:T(8,128)(2,1)}, bf16[512,1024]{1,0:T(8,128)(2,1)}, u32[]{:S(2)}, u32[]{:S(2)}) collective-permute-start(bf16[512,1024]{1,0:T(8,128)(2,1)} %get-tuple-element.256.refs_1_.refs_8_), channel_id=1, source_target_pairs={{0,4},{1,5},{4,0},{5,1},{2,6},{3,7},{6,2},{7,3},{8,12},{9,13},{12,... | collective-permute-start | bytes 3145736 | tf_op jit(solution)/shard_map/ppermute | solution.py:884
  724.0 51.7 %collective-permute-start.71 = (bf16[8,128,1024]{2,1,0:T(8,128)(2,1)}, bf16[8,128,1024]{2,1,0:T(8,128)(2,1)}, u32[]{:S(2)}, u32[]{:S(2)}) collective-permute-start(bf16[8,128,1024]{2,1,0:T(8,128)(2,1)} %get-tuple-element.263.refs_6_), channel_id=1, source_target_pairs={{0,16},{8,24},{16,0},{24,8},{1,17},{9,25},{17,1},{25,9},{2,18},{10... | collective-permute-start | bytes 6291464 | tf_op jit(solution)/shard_map/ppermute | solution.py:884
  724.0 55.2 %collective-permute-start.70 = (bf16[8,128,1024]{2,1,0:T(8,128)(2,1)}, bf16[8,128,1024]{2,1,0:T(8,128)(2,1)}, u32[]{:S(2)}, u32[]{:S(2)}) collective-permute-start(bf16[8,128,1024]{2,1,0:T(8,128)(2,1)} %get-tuple-element.262.refs_5_), channel_id=1, source_target_pairs={{0,8},{8,0},{16,24},{24,16},{1,9},{9,1},{17,25},{25,17},{2,10},{10... | collective-permute-start | bytes 6291464 | tf_op jit(solution)/shard_map/ppermute | solution.py:884
  728.6 38.2 %collective-permute-start.72 = (bf16[4,128,1024]{2,1,0:T(8,128)(2,1)}, bf16[4,128,1024]{2,1,0:T(8,128)(2,1)}, u32[]{:S(2)}, u32[]{:S(2)}) collective-permute-start(bf16[4,128,1024]{2,1,0:T(8,128)(2,1)} %add_convert_fusion.3), channel_id=1, source_target_pairs={{0,1},{1,0},{2,3},{3,2},{4,5},{5,4},{6,7},{7,6},{8,9},{9,8},{10,11... | collective-permute-start | bytes 3145736 | tf_op jit(solution)/shard_map/ppermute | solution.py:884
  769.7 44.2 %collective-permute-start.75 = (bf16[2,128,1024]{2,1,0:T(8,128)(2,1)}, bf16[2,128,1024]{2,1,0:T(8,128)(2,1)S(1)}, u32[]{:S(2)}, u32[]{:S(2)}) collective-permute-start(bf16[2,128,1024]{2,1,0:T(8,128)(2,1)} %add_convert_fusion.9), channel_id=1, source_target_pairs={{0,2},{2,0},{1,3},{3,1},{4,6},{6,4},{5,7},{7,5},{8,10},{10,8},{9,1... | collective-permute-start | bytes 1572872 | tf_op jit(solution)/shard_map/ppermute | solution.py:884
  774.7 39.2 %collective-permute-start.76 = (bf16[2,128,1024]{2,1,0:T(8,128)(2,1)}, bf16[2,128,1024]{2,1,0:T(8,128)(2,1)}, u32[]{:S(2)}, u32[]{:S(2)}) collective-permute-start(bf16[2,128,1024]{2,1,0:T(8,128)(2,1)} %fusion.9), channel_id=1, source_target_pairs={{0,16},{8,24},{16,0},{24,8},{1,17},{9,25},{17,1},{25,9},{2,18},{10... | collective-permute-start | bytes 1572872 | tf_op jit(solution)/shard_map/ppermute | solution.py:884
  781.8 32.1 %collective-permute-start.74 = (bf16[4,128,1024]{2,1,0:T(8,128)(2,1)}, bf16[4,128,1024]{2,1,0:T(8,128)(2,1)S(1)}, u32[]{:S(2)}, u32[]{:S(2)}) collective-permute-start(bf16[4,128,1024]{2,1,0:T(8,128)(2,1)} %add_convert_fusion), channel_id=1, source_target_pairs={{0,16},{8,24},{16,0},{24,8},{1,17},{9,25},{17,1},{25,9},{2,18},{10... | collective-permute-start | bytes 3145736 | tf_op jit(solution)/shard_map/ppermute | solution.py:884
  832.7 32.4 %collective-permute-start.80 = (bf16[4,128,1024]{2,1,0:T(8,128)(2,1)}, bf16[4,128,1024]{2,1,0:T(8,128)(2,1)}, u32[]{:S(2)}, u32[]{:S(2)}) collective-permute-start(bf16[4,128,1024]{2,1,0:T(8,128)(2,1)} %add_convert_fusion.1.refs_1_), channel_id=1, source_target_pairs={{0,1},{1,0},{2,3},{3,2},{4,5},{5,4},{6,7},{7,6},{8,9},{9,8},{10,11... | collective-permute-start | bytes 3145736 | tf_op jit(solution)/shard_map/ppermute | solution.py:884
  843.2 53.5 %collective-permute-start.78 = (bf16[512,1024]{1,0:T(8,128)(2,1)}, bf16[512,1024]{1,0:T(8,128)(2,1)}, u32[]{:S(2)}, u32[]{:S(2)}) collective-permute-start(bf16[512,1024]{1,0:T(8,128)(2,1)} %fusion.refs_1_), channel_id=1, source_target_pairs={{0,1},{1,0},{4,5},{5,4},{2,3},{3,2},{6,7},{7,6},{8,9},{9,8},{12,13... | collective-permute-start | bytes 3145736 | tf_op jit(solution)/shard_map/ppermute | solution.py:884
  859.9 36.8 %collective-permute-start.85 = (bf16[2,2,128,1024]{3,2,1,0:T(8,128)(2,1)}, bf16[2,2,128,1024]{3,2,1,0:T(8,128)(2,1)}, u32[]{:S(2)}, u32[]{:S(2)}) collective-permute-start(bf16[2,2,128,1024]{3,2,1,0:T(8,128)(2,1)} %get-tuple-element.287), channel_id=1, source_target_pairs={{0,8},{8,0},{16,24},{24,16},{1,9},{9,1},{17,25},{25,17},{2,10},{10... | collective-permute-start | bytes 3145736 | tf_op jit(solution)/shard_map/ppermute | solution.py:884
  867.7 43.8 %collective-permute-start.81 = (bf16[2,128,1024]{2,1,0:T(8,128)(2,1)}, bf16[2,128,1024]{2,1,0:T(8,128)(2,1)S(1)}, u32[]{:S(2)}, u32[]{:S(2)}) collective-permute-start(bf16[2,128,1024]{2,1,0:T(8,128)(2,1)} %add_convert_fusion.7), channel_id=1, source_target_pairs={{0,2},{2,0},{1,3},{3,1},{4,6},{6,4},{5,7},{7,5},{8,10},{10,8},{9,1... | collective-permute-start | bytes 1572872 | tf_op jit(solution)/shard_map/ppermute | solution.py:884
  905.6 37.6 %collective-permute-start.79 = (bf16[512,1024]{1,0:T(8,128)(2,1)}, bf16[512,1024]{1,0:T(8,128)(2,1)S(1)}, u32[]{:S(2)}, u32[]{:S(2)}) collective-permute-start(bf16[512,1024]{1,0:T(8,128)(2,1)} %fusion.2), channel_id=1, source_target_pairs={{0,0},{2,4},{4,2},{6,6},{1,1},{3,5},{5,3},{7,7},{8,8},{10,12},{12,... | collective-permute-start | bytes 3145736 | tf_op jit(solution)/shard_map/ppermute | solution.py:888
  (129 other events, 1392.4 us)
Sparse Core Ops, SparseCore 0:
  110.3 71.9 all-gather.1
